TPU v7x, 32 devices: a whole 2x2x4 slice. The times are simulated.
32 devices in a mesh: groups: 2 (over y), seq: 4 (over x, core), head: 4 (over z).
Axes of the slice: x: 2, y: 2, z: 4, core: 2. Of those that a mesh axis runs over, the one named last changes fastest.
Arguments:
- tokens: bfloat16 [2048, 4096], P(('groups', 'seq')), parts along dimension 0, may hold values from -6 to 6
- qkv_weight: bfloat16 [4096, 3, 4096], P('seq', None, 'head'), may hold values from -0.09375 to 0.09375
- rate_weight: bfloat16 [4096, 16], P(None, 'head'), may hold values from -0.09375 to 0.09375
- fast_gate: bfloat16 [16, 256, 512], P('head'), may hold values from -0.375 to 0.375
- fast_up: bfloat16 [16, 256, 512], P('head'), may hold values from -0.375 to 0.375
- fast_down: bfloat16 [16, 256, 512], P('head'), may hold values from -0.25 to 0.25
- out_gain: float32 [4096], P('head'), may hold values from 0.1 to 1.9
- out_weight: bfloat16 [4096, 4096], P('seq', 'head'), may hold values from -0.09375 to 0.09375
Outputs:
- mixed: bfloat16 [2048, 4096], P(('groups', 'seq'), 'head'), parts along dimension 0
There are 2 independent parts, one for each index of `groups`. A program takes and returns all parts, laid end to end along the dimension named above; an argument that names none is the same for every part. Nothing has to cross between parts.
All inputs are finite; a program needn't handle non-finite values.
Results may differ from a plain program's by a relative error of at most 0.014.
Values may be sent and summed in bfloat16 or wider, within the bound.
No kernel may reach another device: no remote copies, remote signals or barrier semaphores. Data moves between devices by JAX's collectives and lax.ppermute only.
A program may use at most 128 MiB of HBM per device.

v0:
```python
import jax
import jax.numpy as jnp
from jax import lax
from jax.sharding import PartitionSpec as P

NSI = 5


quintic_a = 3.4445
quintic_b = -4.775
quintic_c = 2.0315


def rms_scale(values):
    return values * lax.rsqrt(jnp.mean(values * values, axis=-1, keepdims=True) + 1e-06)


def silu_slope(gate):
    sigma = jax.nn.sigmoid(gate)
    return sigma * (1.0 + gate * (1.0 - sigma))


def polish(current, gram):
    highest = lax.Precision.HIGHEST
    poly = quintic_b * gram + quintic_c * jnp.einsum("nij,njk->nik", gram, gram, precision=highest)
    return quintic_a * current + jnp.einsum("nij,njk->nik", poly, current, precision=highest)


def orthogonal(matrix):
    highest = lax.Precision.HIGHEST
    norm = jnp.sqrt(jnp.sum(matrix * matrix, axis=(1, 2), keepdims=True))
    current = matrix / (norm + 1e-07)
    for step in range(NSI):
        gram = jnp.einsum("nik,njk->nij", current, current, precision=highest)
        current = polish(current, gram)
    return current


def on_device(tokens, qkv_weight, rate_weight, fast_gate, fast_up, fast_down, out_gain, out_weight):
    rows = tokens.shape[0]
    local_heads = fast_gate.shape[0]
    head_size = fast_gate.shape[1]
    hidden_units = fast_gate.shape[2]
    columns = tokens
    projected = jnp.einsum(
        "td,dcn->tcn",
        columns,
        lax.all_gather(qkv_weight, "seq", axis=0, tiled=True),
        preferred_element_type=jnp.float32,
    )
    projected = projected.reshape(rows, 3, local_heads, head_size)
    rates = jax.nn.softplus(jnp.dot(tokens, rate_weight, preferred_element_type=jnp.float32))
    queries = rms_scale(projected[:, 0]).astype(jnp.bfloat16)
    keys = rms_scale(projected[:, 1]).astype(jnp.bfloat16)
    values = projected[:, 2].astype(jnp.bfloat16)
    gate = jnp.einsum("thd,hdf->thf", keys, fast_gate, preferred_element_type=jnp.float32)
    up = jnp.einsum("thd,hdf->thf", keys, fast_up, preferred_element_type=jnp.float32)
    active = jax.nn.silu(gate)
    hidden = (active * up).astype(jnp.bfloat16)
    scaled = (rates[:, :, None] * values.astype(jnp.float32)).astype(jnp.bfloat16)
    back = jnp.einsum("thd,hdf->thf", scaled, fast_down, preferred_element_type=jnp.float32)
    dgate = (back * up * silu_slope(gate)).astype(jnp.bfloat16)
    dup = (back * active).astype(jnp.bfloat16)
    first = jnp.einsum("thd,thf->hdf", keys, dgate, preferred_element_type=jnp.float32)
    second = jnp.einsum("thd,thf->hdf", keys, dup, preferred_element_type=jnp.float32)
    third = jnp.einsum("thd,thf->hdf", scaled, hidden, preferred_element_type=jnp.float32)
    partial_sum = jnp.stack([first, second, third], axis=1)
    initial = jnp.stack([fast_gate, fast_up, fast_down], axis=1)
    summed = lax.psum(partial_sum, "seq")
    update = orthogonal(summed.reshape(local_heads * 3, head_size, hidden_units))
    update = update.reshape(local_heads, 3, head_size, hidden_units)
    fresh = (initial.astype(jnp.float32) + update).astype(jnp.bfloat16)
    gate_q = jnp.einsum("thd,hdf->thf", queries, fresh[:, 0], preferred_element_type=jnp.float32)
    up_q = jnp.einsum("thd,hdf->thf", queries, fresh[:, 1], preferred_element_type=jnp.float32)
    hidden_q = (jax.nn.silu(gate_q) * up_q).astype(jnp.bfloat16)
    read = jnp.einsum("thf,hdf->thd", hidden_q, fresh[:, 2], preferred_element_type=jnp.float32)
    normed = (rms_scale(read) * out_gain.reshape(local_heads, head_size)).astype(jnp.bfloat16)
    normed = normed.reshape(rows, local_heads * head_size)
    gathered = lax.all_gather(normed, "head", axis=1, tiled=True)
    columns = gathered
    mixed = jnp.dot(
        columns,
        lax.all_gather(out_weight, "seq", axis=0, tiled=True),
        preferred_element_type=jnp.float32,
    )
    return mixed.astype(jnp.bfloat16)


def solution(mesh):
    placed = (
        P(("groups", "seq"), None),
        P("seq", None, "head"),
        P(None, "head"),
        P("head", None, None),
        P("head", None, None),
        P("head", None, None),
        P("head"),
        P("seq", "head"),
    )
    return jax.shard_map(
        on_device,
        mesh=mesh,
        in_specs=placed,
        out_specs=P(("groups", "seq"), "head"),
        check_vma=False,
    )
```

profile of v0, /device:TPU:0, one launch (start us, length us, event | category | flops | bytes accessed | tf_op | source)
XLA Modules:
  0.0 502.1 jit_solution(11924547051163774938)
XLA Ops:
  6.5 0.7 all-gather.4.cloned.1.call-update
  7.3 0.0 all-reduce.2.cloned.1.call-start
  7.3 0.8 copy-done
  8.1 0.7 compare_select_fusion
  8.8 157.7 %all-gather.4.cloned.1.call-done = bf16[4096,3,1024]{2,0,1:T(8,128)(2,1)} async-done(((bf16[1024,3,1024]{2,0,1:T(8,128)(2,1)}), bf16[4096,3,1024]{2,0,1:T(8,128)(2,1)}) %all-gather.4.cloned.1.call-update) | async-done | bytes 25165840 | tf_op jit(solution)/shard_map/all_gather | solution.py:48
  166.5 13.3 %fusion.43 = f32[256,3,1024]{2,0,1:T(8,128)} fusion(bf16[4096,3,1024]{2,0,1:T(8,128)(2,1)} %all-gather.4.cloned.1.call-done, bf16[256,4096]{1,0:T(8,128)(2,1)S(1)} %copy-done), kind=kOutput, calls=%fused_computation.51 | convolution fusion | flops 6442450944 | bytes 30408704 | tf_op jit(solution)/shard_map/td,dcn->tcn/dot_general | solution.py:45
  179.8 5.1 %reshape.54 = f32[256,3,4,256]{3,2,0,1:T(4,128)} reshape(f32[256,3,1024]{2,0,1:T(8,128)} %fusion.43) | data formatting | bytes 6291456 | tf_op jit(solution)/shard_map/reshape | solution.py:51
  184.9 1.9 fusion.80
  186.8 2.2 slice.26
  189.0 0.4 copy.56
  189.4 0.0 copy-start.4
  189.4 0.1 fusion.59
  189.5 0.1 fusion.60
  189.6 0.0 copy-start.11
  189.6 3.1 fusion.82
  192.8 1.8 fusion.81
  194.6 1.1 copy.57
  195.7 1.7 fusion.64
  197.4 0.1 copy-done.9
  197.5 0.8 convolution_bitcast_fusion.1
  198.3 0.7 copy-done.10
  199.1 1.0 convolution_bitcast_fusion.2
  200.1 0.9 convolution_bitcast_fusion
  201.0 3.3 pad_maximum_fusion
  204.3 0.0 all-reduce.2.cloned.1.call-update
  204.4 0.0 all-gather.8.cloned.1.call-start
  204.4 0.7 all-gather.8.cloned.1.call-update
  205.1 0.0 all-gather.6.cloned.1.call-start
  205.2 0.4 copy-done.3
  205.5 1.3 copy.34
  206.9 1.3 copy.35
  208.2 2.8 copy.36
  211.0 0.2 multiply_reduce_fusion.2
  211.2 112.9 %all-reduce.2.cloned.1.call-done = f32[4,3,256,512]{3,2,0,1:T(8,128)} async-done(((f32[4,3,256,512]{3,2,0,1:T(8,128)}), f32[4,3,256,512]{3,2,0,1:T(8,128)}) %all-reduce.2.cloned.1.call-update) | async-done | bytes 6291472 | tf_op jit(solution)/shard_map/psum | solution.py:69
  324.1 3.4 multiply_reduce_fusion
  327.4 0.1 copy.43
  327.5 0.1 add.90
  327.6 3.5 copy.42
  331.1 0.9 bitcast_divide_fusion
  332.0 6.4 %fusion.83 = f32[12,256,256]{2,1,0:T(8,128)S(1)} fusion(f32[12,256,512]{2,1,0:T(8,128)S(1)} %bitcast_divide_fusion), kind=kOutput, calls=%fused_computation.107 | convolution fusion | flops 4831838208 | bytes 9437184 | tf_op jit(solution)/shard_map/nik,njk->nij/dot_general | solution.py:34
  338.4 3.6 fusion.84
  342.0 8.0 %multiply_add_fusion.4 = f32[12,256,512]{2,1,0:T(8,128)S(1)} fusion(f32[12,256,512]{2,1,0:T(8,128)S(1)} %bitcast_divide_fusion, f32[12,256,256]{2,1,0:T(8,128)S(1)} %fusion.84, f32[12,256,256]{2,1,0:T(8,128)S(1)} %fusion.83), kind=kOutput, calls=%fused_computation.7 | convolution fusion | flops 4837343232 | bytes 18874368 | tf_op jit(solution)/shard_map/nij,njk->nik/dot_general | solution.py:26
  350.0 6.6 %fusion.85 = f32[12,256,256]{2,1,0:T(8,128)S(1)} fusion(f32[12,256,512]{2,1,0:T(8,128)S(1)} %multiply_add_fusion.4), kind=kOutput, calls=%fused_computation.109 | convolution fusion | flops 4831838208 | bytes 9437184 | tf_op jit(solution)/shard_map/nik,njk->nij/dot_general | solution.py:34
  356.6 3.6 fusion.86
  360.3 7.8 %multiply_add_fusion.3 = f32[12,256,512]{2,1,0:T(8,128)S(1)} fusion(f32[12,256,512]{2,1,0:T(8,128)S(1)} %multiply_add_fusion.4, f32[12,256,256]{2,1,0:T(8,128)S(1)} %fusion.86, f32[12,256,256]{2,1,0:T(8,128)S(1)} %fusion.85), kind=kOutput, calls=%fused_computation.6 | convolution fusion | flops 4837343232 | bytes 18874368 | tf_op jit(solution)/shard_map/nij,njk->nik/dot_general | solution.py:26
  368.1 6.8 %fusion.87 = f32[12,256,256]{2,1,0:T(8,128)S(1)} fusion(f32[12,256,512]{2,1,0:T(8,128)S(1)} %multiply_add_fusion.3), kind=kOutput, calls=%fused_computation.111 | convolution fusion | flops 4831838208 | bytes 9437184 | tf_op jit(solution)/shard_map/nik,njk->nij/dot_general | solution.py:34
  374.9 3.6 fusion.88
  378.5 8.0 %multiply_add_fusion.2 = f32[12,256,512]{2,1,0:T(8,128)S(1)} fusion(f32[12,256,512]{2,1,0:T(8,128)S(1)} %multiply_add_fusion.3, f32[12,256,256]{2,1,0:T(8,128)S(1)} %fusion.88, f32[12,256,256]{2,1,0:T(8,128)S(1)} %fusion.87), kind=kOutput, calls=%fused_computation.5 | convolution fusion | flops 4837343232 | bytes 18874368 | tf_op jit(solution)/shard_map/nij,njk->nik/dot_general | solution.py:26
  386.5 6.4 %fusion.89 = f32[12,256,256]{2,1,0:T(8,128)S(1)} fusion(f32[12,256,512]{2,1,0:T(8,128)S(1)} %multiply_add_fusion.2), kind=kOutput, calls=%fused_computation.113 | convolution fusion | flops 4831838208 | bytes 9437184 | tf_op jit(solution)/shard_map/nik,njk->nij/dot_general | solution.py:34
  392.9 3.8 fusion.90
  396.7 7.8 %multiply_add_fusion.1 = f32[12,256,512]{2,1,0:T(8,128)S(1)} fusion(f32[12,256,512]{2,1,0:T(8,128)S(1)} %multiply_add_fusion.2, f32[12,256,256]{2,1,0:T(8,128)S(1)} %fusion.90, f32[12,256,256]{2,1,0:T(8,128)S(1)} %fusion.89), kind=kOutput, calls=%fused_computation.4 | convolution fusion | flops 4837343232 | bytes 18874368 | tf_op jit(solution)/shard_map/nij,njk->nik/dot_general | solution.py:26
  404.5 6.8 %fusion.91 = f32[12,256,256]{2,1,0:T(8,128)S(1)} fusion(f32[12,256,512]{2,1,0:T(8,128)S(1)} %multiply_add_fusion.1), kind=kOutput, calls=%fused_computation.115 | convolution fusion | flops 4831838208 | bytes 9437184 | tf_op jit(solution)/shard_map/nik,njk->nij/dot_general | solution.py:34
  411.4 3.6 fusion.92
  415.0 8.3 %multiply_add_fusion = f32[12,256,512]{2,1,0:T(8,128)} fusion(f32[12,256,512]{2,1,0:T(8,128)S(1)} %multiply_add_fusion.1, f32[12,256,256]{2,1,0:T(8,128)S(1)} %fusion.92, f32[12,256,256]{2,1,0:T(8,128)S(1)} %fusion.91), kind=kOutput, calls=%fused_computation.3 | convolution fusion | flops 4837343232 | bytes 18874368 | tf_op jit(solution)/shard_map/nij,njk->nik/dot_general | solution.py:26
  423.3 6.7 %copy.44 = f32[4,3,256,512]{2,3,0,1:T(8,128)} copy(f32[4,3,256,512]{3,2,1,0:T(8,128)} %bitcast.164) | data formatting | bytes 12582912 | tf_op jit(solution)/shard_map/reshape | solution.py:71
  430.0 3.6 add_convert_fusion
  433.6 1.7 copy-done.2
  435.3 1.9 fusion.57
  437.3 3.4 multiply_reduce_fusion.1
  440.7 1.0 multiply_convert_fusion
  441.7 0.0 all-gather.6.cloned.1.call-update
  441.7 0.0 all-gather.8.cloned.1.call-done
  441.8 46.3 %all-gather.6.cloned.1.call-done = bf16[256,4096]{0,1:T(8,128)(2,1)} async-done(((bf16[256,1024]{0,1:T(8,128)(2,1)}), bf16[256,4096]{0,1:T(8,128)(2,1)}) %all-gather.6.cloned.1.call-update) | async-done | bytes 2097168 | tf_op jit(solution)/shard_map/all_gather | solution.py:79
  488.1 7.3 %convolution_convert_fusion = bf16[256,1024]{1,0:T(8,128)(2,1)} fusion(bf16[256,4096]{0,1:T(8,128)(2,1)} %all-gather.6.cloned.1.call-done, bf16[4096,1024]{1,0:T(8,128)(2,1)} %all-gather.8.cloned.1.call-done), kind=kOutput, calls=%fused_computation.67 | convolution fusion | flops 2147745792 | bytes 11010048 | tf_op jit(solution)/shard_map/dot_general | solution.py:81
  (29 shorter events, 0.1 us)
Async XLA Ops:
  6.5 1.6 copy-start
  6.5 1.6 copy-start.13
  6.5 159.9 %all-gather.4.cloned.1.call-start = ((), (), s32[]{:S(2)}) async-start(), calls=%async_computation | async-start | bytes 31457280 | tf_op jit(solution)/shard_map/all_gather | solution.py:48
  7.3 316.8 %all-reduce.2.cloned.1.call-start = ((), (), s32[]{:S(2)}) async-start(), calls=%async_computation.1 | async-start | bytes 12582912 | tf_op jit(solution)/shard_map/psum | solution.py:69
  189.4 3.4 copy-start.4
  189.6 5.0 copy-start.11
  192.8 3.0 copy-start.8
  195.7 1.7 copy-start.9
  197.5 1.6 copy-start.10
  199.1 1.1 copy-start.12
  204.3 1.2 copy-start.3
  204.3 2.5 copy-start.5
  204.4 237.4 %all-gather.8.cloned.1.call-start = ((), (), s32[]{:S(2)}) async-start(), calls=%async_computation.3 | async-start | bytes 10485760 | tf_op jit(solution)/shard_map/all_gather | solution.py:83
  205.1 5.8 %copy-start.14 = (f32[1024]{0:T(1024)S(1)}, f32[1024]{0:T(1024)}, u32[]{:S(2)}) copy-start(f32[1024]{0:T(1024)} %param.14) | copy-start | bytes 12292
  205.1 282.9 %all-gather.6.cloned.1.call-start = ((), (), s32[]{:S(2)}) async-start(), calls=%async_computation.2 | async-start | bytes 2621440 | tf_op jit(solution)/shard_map/all_gather | solution.py:79
  423.3 6.7 %copy-start.6 = (bf16[4,256,512]{1,2,0:T(8,128)(2,1)S(1)}, bf16[4,256,512]{1,2,0:T(8,128)(2,1)}, u32[]{:S(2)}) copy-start(bf16[4,256,512]{1,2,0:T(8,128)(2,1)} %copy.34) | copy-start | bytes 3145732
  423.3 6.7 %copy-start.7 = (bf16[4,256,512]{1,2,0:T(8,128)(2,1)S(1)}, bf16[4,256,512]{1,2,0:T(8,128)(2,1)}, u32[]{:S(2)}) copy-start(bf16[4,256,512]{1,2,0:T(8,128)(2,1)} %copy.35) | copy-start | bytes 3145732
  433.6 1.7 copy-start.2
  488.1 7.3 %copy-start.1 = (bf16[256,4096]{1,0:T(8,128)(2,1)S(1)}, bf16[256,4096]{1,0:T(8,128)(2,1)}, u32[]{:S(2)}) copy-start(bf16[256,4096]{1,0:T(8,128)(2,1)} %param.8) | copy-start | bytes 6291460
Sparse Core Ops, SparseCore 0:
  8.9 157.4 all-gather.3
  204.5 119.5 all-reduce.1
  325.6 58.4 all-gather.7
  441.9 46.1 all-gather.5
where the time goes:
time: 510 us; the launch traced here: 502 us
  waiting for transfers between devices  318 us (62%)
  matrix products  127 us (25%)
  local copies, waits for them, and re-layouts  30.3 us (6%)
  between operations  13.6 us (3%)
  other arithmetic  12.5 us (2%)
    all_gather x1, waiting for transfers between devices, on_device(): lax.all_gather(qkv_weight, 'seq', axis=0, tiled=True)  158 us
    psum x1, waiting for transfers between devices, on_device(): summed = lax.psum(partial_sum, 'seq')  113 us
    all_gather x1, waiting for transfers between devices, on_device(): gathered = lax.all_gather(normed, 'head', axis=1, tiled=True)  46.3 us
    dot_general x5, matrix products, polish(): jnp.einsum('nij,njk->nik', poly, current, precision=highest)  39.9 us
    dot_general x5, matrix products, orthogonal(): gram = jnp.einsum('nik,njk->nij', current, current, precision=highest)  33 us
    dot_general x5, matrix products, polish(): jnp.einsum('nij,njk->nik', gram, gram, precision=highest)  18.3 us
    dot_general x1, matrix products, on_device(): jnp.einsum('td,dcn->tcn', columns, lax.all_gather(qkv_weight, 'seq', axis...  13.3 us
    unnamed x35, local copies, waits for them, and re-layouts  10.7 us
  transfers between devices with their start and end apart: 4, of which 3 were waited for; matrix products, arithmetic and copies ran while one was open for 24% of the time, Pallas kernels for 0%

commit v1 on v0

--- a/solution.py
+++ b/solution.py
@@ -1,14 +1,21 @@
+import functools
+
 import jax
 import jax.numpy as jnp
 from jax import lax
+from jax.experimental import pallas as pl
+from jax.experimental.pallas import tpu as pltpu
 from jax.sharding import PartitionSpec as P
 
 NSI = 5
-
+VMEM_LIMIT = 56 * 1024 * 1024
 
 quintic_a = 3.4445
 quintic_b = -4.775
 quintic_c = 2.0315
+
+BF16 = jnp.bfloat16
+F32 = jnp.float32
 
 
 def rms_scale(values):
@@ -36,7 +43,7 @@
     return current
 
 
-def on_device(tokens, qkv_weight, rate_weight, fast_gate, fast_up, fast_down, out_gain, out_weight):
+def general_plan(tokens, qkv_weight, rate_weight, fast_gate, fast_up, fast_down, out_gain, out_weight):
     rows = tokens.shape[0]
     local_heads = fast_gate.shape[0]
     head_size = fast_gate.shape[1]
@@ -77,13 +84,316 @@
     normed = (rms_scale(read) * out_gain.reshape(local_heads, head_size)).astype(jnp.bfloat16)
     normed = normed.reshape(rows, local_heads * head_size)
     gathered = lax.all_gather(normed, "head", axis=1, tiled=True)
-    columns = gathered
     mixed = jnp.dot(
-        columns,
+        gathered,
         lax.all_gather(out_weight, "seq", axis=0, tiled=True),
         preferred_element_type=jnp.float32,
     )
     return mixed.astype(jnp.bfloat16)
+
+
+def params():
+    return pltpu.CompilerParams(vmem_limit_bytes=VMEM_LIMIT)
+
+
+def dot(a, b):
+    return jnp.dot(a, b, preferred_element_type=F32)
+
+
+def dot_nt(a, b):
+    return lax.dot_general(a, b, (((1,), (1,)), ((), ())), preferred_element_type=F32)
+
+
+def dot_tn(a, b):
+    return lax.dot_general(a, b, (((0,), (0,)), ((), ())), preferred_element_type=F32)
+
+
+def project_kernel(pairs, index_ref, *refs):
+    token_refs = refs[: 2 * pairs]
+    keep_ref, peer_ref, out_ref = refs[2 * pairs :]
+    rows = token_refs[0].shape[0]
+    for pair in range(pairs):
+        low, high = token_refs[2 * pair][...], token_refs[2 * pair + 1][...]
+        swapped = index_ref[1 + pair] == 1
+        first = jnp.where(swapped, high, low)
+        second = jnp.where(swapped, low, high)
+        total = dot(first, keep_ref[0, 0]) + dot(second, peer_ref[0, 0])
+        out_ref[0, pair * rows : (pair + 1) * rows, :] = total.astype(out_ref.dtype)
+
+
+def project(pairs, flags, head, keep, peer, start, count, dtype):
+    rows, depth = pairs[0][0].shape
+    size = keep.shape[3]
+    number = len(pairs)
+    index = jnp.stack([head] + flags).astype(jnp.int32)
+    weight_spec = pl.BlockSpec((1, 1, depth, size), lambda i, idx: (idx[0], start + i, 0, 0))
+    return pl.pallas_call(
+        functools.partial(project_kernel, number),
+        out_shape=jax.ShapeDtypeStruct((count, number * rows, size), dtype),
+        grid_spec=pltpu.PrefetchScalarGridSpec(
+            num_scalar_prefetch=1,
+            grid=(count,),
+            in_specs=[pl.BlockSpec((rows, depth), lambda i, idx: (0, 0))] * (2 * number) + [weight_spec] * 2,
+            out_specs=pl.BlockSpec((1, number * rows, size), lambda i, idx: (i, 0, 0)),
+        ),
+        compiler_params=params(),
+        cost_estimate=pl.CostEstimate(
+            flops=2 * count * number * rows * 2 * depth * size,
+            bytes_accessed=4 * (number * rows * depth + count * depth * size),
+            transcendentals=0,
+        ),
+    )(index, *[block for pair in pairs for block in pair], keep, peer)
+
+
+def split(value):
+    high = value.astype(BF16)
+    return high, (value - high.astype(F32)).astype(BF16)
+
+
+def update_kernel(index_ref, local_ref, near_ref, far_ref, rate_ref, gate_ref, up_ref, down_ref,
+                  gate_out, up_out, down_out, current):
+    gate_w, up_w, down_w = gate_ref[0], up_ref[0], down_ref[0]
+    rows = local_ref.shape[1] // 4
+    sums = [None] * 3
+    for block in range(4):
+        other = (near_ref if block < 2 else far_ref)
+        here = pl.ds(block * rows, rows)
+        there = pl.ds((block % 2) * rows, rows)
+        keys = local_ref[0, here, :] + other[0, there, :].astype(F32)
+        keys = rms_scale(keys).astype(BF16)
+        values = (local_ref[1, here, :] + other[1, there, :].astype(F32)).astype(BF16)
+        rate = rate_ref[block]
+        scaled = (rate * values.astype(F32)).astype(BF16)
+        gate = dot(keys, gate_w)
+        up = dot(keys, up_w)
+        back = dot(scaled, down_w)
+        sigma = jax.nn.sigmoid(gate)
+        active = gate * sigma
+        hidden = (active * up).astype(BF16)
+        dgate = (back * up * (sigma * (1.0 + gate * (1.0 - sigma)))).astype(BF16)
+        dup = (back * active).astype(BF16)
+        parts = [dot_tn(keys, dgate), dot_tn(keys, dup), dot_tn(scaled, hidden)]
+        for i in range(3):
+            current[i] = parts[i] if block == 0 else current[i] + parts[i]
+    for i in range(3):
+        value = current[i]
+        norm = jnp.sqrt(jnp.sum(value * value))
+        current[i] = value / (norm + 1e-07)
+
+    @pl.loop(0, NSI)
+    def _(step):
+        for i in range(3):
+            value = current[i]
+            high, low = split(value)
+            cross = dot_nt(high, low)
+            gram = dot_nt(high, high) + (cross + dot_nt(low, high))
+            gram_high, gram_low = split(gram)
+            square = dot(gram_high, gram_high) + (dot(gram_high, gram_low) + dot(gram_low, gram_high))
+            poly_high, poly_low = split(quintic_b * gram + quintic_c * square)
+            moved = dot(poly_high, high) + (dot(poly_high, low) + dot(poly_low, high))
+            current[i] = quintic_a * value + moved
+
+    gate_out[...] = (gate_w.astype(F32) + current[0]).astype(BF16)
+    up_out[...] = (up_w.astype(F32) + current[1]).astype(BF16)
+    down_out[...] = (down_w.astype(F32) + current[2]).astype(BF16)
+
+
+def update(head, local, near, far, rates, fast_gate, fast_up, fast_down):
+    size, hidden = fast_gate.shape[1:]
+    total = local.shape[1]
+
+    def whole(array):
+        zeros = (0,) * array.ndim
+        return pl.BlockSpec(array.shape, lambda i, idx: zeros)
+
+    pick = pl.BlockSpec((1, size, hidden), lambda i, idx: (idx[0], 0, 0))
+    out = jax.ShapeDtypeStruct((size, hidden), BF16)
+    return pl.pallas_call(
+        update_kernel,
+        out_shape=[out] * 3,
+        grid_spec=pltpu.PrefetchScalarGridSpec(
+            num_scalar_prefetch=1,
+            grid=(1,),
+            in_specs=[whole(local), whole(near), whole(far), whole(rates), pick, pick, pick],
+            out_specs=[pl.BlockSpec((size, hidden), lambda i, idx: (0, 0))] * 3,
+            scratch_shapes=[pltpu.VMEM((3, size, hidden), F32)],
+        ),
+        compiler_params=params(),
+        cost_estimate=pl.CostEstimate(
+            flops=20 * total * size * hidden + 3 * NSI * 3 * 8 * size * size * hidden,
+            bytes_accessed=total * size * 12 + 12 * size * hidden,
+            transcendentals=total * hidden,
+        ),
+    )(head.reshape(1).astype(jnp.int32), local, near, far, rates, fast_gate, fast_up, fast_down)
+
+
+def read_kernel(index_ref, local_ref, other_ref, gain_ref, gate_ref, up_ref, down_ref, out_ref):
+    queries = rms_scale(local_ref[0] + other_ref[0].astype(F32)).astype(BF16)
+    gate = dot(queries, gate_ref[...])
+    up = dot(queries, up_ref[...])
+    hidden = (gate * jax.nn.sigmoid(gate) * up).astype(BF16)
+    read = dot_nt(hidden, down_ref[...])
+    out_ref[0] = (rms_scale(read) * gain_ref[0]).astype(BF16)
+
+
+def read_out(head, local, other, gain, gate, up, down):
+    size, hidden = gate.shape
+    total = local.shape[1]
+    rows = total // 4
+    weight = pl.BlockSpec((size, hidden), lambda i, idx: (0, 0))
+    return pl.pallas_call(
+        read_kernel,
+        out_shape=jax.ShapeDtypeStruct((4, rows, size), BF16),
+        grid_spec=pltpu.PrefetchScalarGridSpec(
+            num_scalar_prefetch=1,
+            grid=(4,),
+            in_specs=[
+                pl.BlockSpec((1, rows, size), lambda i, idx: (0, i, 0)),
+                pl.BlockSpec((1, rows, size), lambda i, idx: (0, (i + 2) % 4, 0)),
+                pl.BlockSpec((1, 1, size), lambda i, idx: (idx[0], 0, 0)),
+                weight,
+                weight,
+                weight,
+            ],
+            out_specs=pl.BlockSpec((1, rows, size), lambda i, idx: (i, 0, 0)),
+        ),
+        compiler_params=params(),
+        cost_estimate=pl.CostEstimate(
+            flops=6 * total * size * hidden, bytes_accessed=total * size * 8, transcendentals=total * hidden
+        ),
+    )(head.reshape(1).astype(jnp.int32), local, other, gain, gate, up, down)
+
+
+def mix_kernel(index_ref, *refs):
+    blocks = refs[:28]
+    weight_ref, out_ref = refs[28:]
+    total = None
+    for offset in range(4):
+        for piece in range(4):
+            group = blocks[7 * piece : 7 * piece + 7]
+            if offset == 0:
+                block = group[0][...]
+            else:
+                block = jnp.where(index_ref[offset - 1] == 1, group[offset][...], group[3 + 4 - offset][...])
+            part = dot(block, weight_ref[index_ref[7 + offset], index_ref[3 + piece]])
+            total = part if total is None else total + part
+    out_ref[...] = total.astype(BF16)
+
+
+def mix(index, blocks, weight):
+    rows, size = blocks[0].shape
+    columns = weight.shape[3]
+    tile = columns // 2
+    return pl.pallas_call(
+        mix_kernel,
+        out_shape=jax.ShapeDtypeStruct((rows, columns), BF16),
+        grid_spec=pltpu.PrefetchScalarGridSpec(
+            num_scalar_prefetch=1,
+            grid=(2,),
+            in_specs=[pl.BlockSpec((rows, size), lambda i, idx: (0, 0))] * 28
+            + [pl.BlockSpec((4, 4, size, tile), lambda i, idx: (0, 0, 0, i))],
+            out_specs=pl.BlockSpec((rows, tile), lambda i, idx: (0, i)),
+        ),
+        compiler_params=params(),
+        cost_estimate=pl.CostEstimate(
+            flops=32 * rows * size * columns, bytes_accessed=32 * size * columns + 56 * rows * size, transcendentals=0
+        ),
+    )(index, *blocks, weight)
+
+
+def chip_plan(tokens, qkv_weight, rate_weight, fast_gate, fast_up, fast_down, out_gain, out_weight):
+    rows, width = tokens.shape
+    depth = qkv_weight.shape[0]
+    size = fast_gate.shape[1]
+    seq = lax.axis_index("seq")
+    chip, core = seq // 2, seq % 2
+    place = lax.axis_index("head")
+    side = lax.axis_index("groups")
+    odd = place % 2
+    head = 2 * core + chip
+
+    def across(array, bit):
+        return lax.ppermute(array, "seq", [(i, i ^ bit) for i in range(4)])
+
+    def hop(array, links):
+        return lax.ppermute(array, "head", links)
+
+    def token_block(block):
+        return lax.dynamic_slice(tokens, (0, block * depth), (rows, depth))
+
+    direct = across(token_block(2 * (1 - chip) + odd), 2)
+    handed = hop(direct, [(i, i ^ 1) for i in range(4)])
+    own = (token_block(2 * chip), token_block(2 * chip + 1))
+    peer = (across(own[0], 1), across(own[1], 1))
+    direct_peer = across(direct, 1)
+    handed_peer = across(handed, 1)
+    near = [own, peer]
+    far = [(direct, handed), (direct_peer, handed_peer)]
+
+    def heads_of(half):
+        cut = lax.dynamic_slice(qkv_weight, (0, 0, half * 2 * size), (depth, 3, 2 * size))
+        return jnp.transpose(cut.reshape(depth, 3, 2, size), (2, 1, 0, 3))
+
+    given = across(heads_of(1 - core), 1)
+    keep = heads_of(core)
+
+    near_flags = [core, core]
+    far_flags = [core ^ odd, core ^ odd]
+    send_near = project(near, near_flags, 1 - chip, keep, given, 1, 2, BF16)
+    got_far = across(send_near, 2)
+    send_far = project(far, far_flags, 1 - chip, keep, given, 1, 2, BF16)
+    got_near = across(send_far, 2)
+    send_query = project(near + far, near_flags + far_flags, 1 - chip, keep, given, 0, 1, BF16)
+    got_query = across(send_query, 2)
+    local = project(near + far, near_flags + far_flags, chip, keep, given, 0, 3, F32)
+
+    activity = lax.dot_general(rate_weight, tokens, (((0,), (1,)), ((), ())), preferred_element_type=F32)
+    rates_own = jax.nn.softplus(activity)
+    rates = jnp.stack([rates_own, across(rates_own, 1), across(rates_own, 2), across(rates_own, 3)])
+    rates = lax.dynamic_index_in_dim(rates, head, axis=1, keepdims=False)[:, :, None]
+
+    half = out_weight.shape[0] // 2
+    send_query, out_held = lax.optimization_barrier((send_query, out_weight))
+    over_x = across(lax.dynamic_slice(out_held, (side * half, 0), (half, out_held.shape[1])), 2)
+    over_y = lax.ppermute(over_x, "groups", [(0, 1), (1, 0)])
+    low = jnp.where(side == 0, over_x, over_y)
+    high = jnp.where(side == 0, over_y, over_x)
+    beyond = jnp.concatenate([low, high])
+    gathered = jnp.stack([out_weight, across(out_weight, 1), beyond, across(beyond, 1)])
+    gathered = gathered.reshape(4, 4, size, out_weight.shape[1])
+
+    fresh = update(head, local[1:], got_near, got_far, rates, fast_gate, fast_up, fast_down)
+    normed = read_out(head, local[:1], got_query, out_gain.reshape(4, 1, size), *fresh)
+
+    pieces = [normed[0], across(normed[1], 1), across(normed[2], 2), across(normed[3], 3)]
+    ups = [[(i, i + 1) for i in range(first, 3)] for first in range(3)]
+    downs = [[(i + 1, i) for i in range(0, 3 - first)] for first in range(3)]
+    blocks = []
+    for piece in pieces:
+        below, above = [piece], [piece]
+        for step in range(3):
+            below.append(hop(below[-1], ups[step]))
+            above.append(hop(above[-1], downs[step]))
+        blocks += below + above[1:]
+    index = jnp.stack(
+        [place >= 1, place >= 2, place >= 3]
+        + [2 * (core ^ (k & 1)) + (chip ^ (k >> 1)) for k in range(4)]
+        + [seq ^ ((place - k) % 4) for k in range(4)]
+    ).astype(jnp.int32)
+    return mix(index, blocks, gathered)
+
+
+def on_device(axis_sizes, tokens, qkv_weight, rate_weight, fast_gate, fast_up, fast_down, out_gain, out_weight):
+    arguments = (tokens, qkv_weight, rate_weight, fast_gate, fast_up, fast_down, out_gain, out_weight)
+    special = (
+        axis_sizes == {"groups": 2, "seq": 4, "head": 4}
+        and fast_gate.shape[0] == 4
+        and tokens.shape[0] % 16 == 0
+        and out_weight.shape[0] == 4 * fast_gate.shape[1]
+        and fast_gate.shape[1] % 128 == 0
+        and qkv_weight.shape[0] % 128 == 0
+    )
+    return chip_plan(*arguments) if special else general_plan(*arguments)
 
 
 def solution(mesh):
@@ -98,7 +408,7 @@
         P("seq", "head"),
     )
     return jax.shard_map(
-        on_device,
+        functools.partial(on_device, dict(mesh.shape)),
         mesh=mesh,
         in_specs=placed,
         out_specs=P(("groups", "seq"), "head"),

time: 510 us -> 246 us (0.48); the launches traced: 502 us -> 244 us
  waiting for transfers between devices: 318 us -> 80.6 us
  matrix products: 127 us -> 0.66 us
  Pallas kernels: 0 us -> 57.8 us
  starting transfers between devices: 0.12 us -> 56.2 us
  between operations: 13.6 us -> 0.87 us
  local copies, waits for them, and re-layouts: 30.3 us -> 40.1 us
    all_gather x3 -> x0, waiting for transfers between devices: 204 us -> none  [the longest x1 158 us: on_device(): lax.all_gather(qkv_weight, 'seq', axis=0, tiled=True)]
    dot_general x26 -> x1, matrix products: 127 us -> 0.66 us  [chip_plan(): lax.dot_general(rate_weight, tokens, (((0,), (1,)), ((), ())), preferred_...]
    psum x1 -> x0, waiting for transfers between devices: 113 us -> none  [on_device(): summed = lax.psum(partial_sum, 'seq')]
    ppermute x0 -> x44, waiting for transfers between devices: none -> 80.6 us  [the longest x18 50.5 us: across(): return lax.ppermute(array, 'seq', [(i, i ^ bit) for i in range(4)])]
    pallas_call x0 -> x7, Pallas kernels: none -> 57.8 us  [the longest x4 23 us: project(): pl.pallas_call(functools.partial(project_kernel, number), out_shape=jax.S...]
    ppermute x0 -> x44, starting transfers between devices: none -> 56.2 us  [the longest x25 42.3 us: hop(): return lax.ppermute(array, 'head', links)]
    dynamic_slice x0 -> x3, local copies, waits for them, and re-layouts: none -> 10 us  [the longest x1 6.21 us: heads_of(): lax.dynamic_slice(qkv_weight, (0, 0, half * 2 * size), (depth, 3, 2 * size))]
    unnamed x35 -> x58, local copies, waits for them, and re-layouts: 10.7 us -> 13.2 us
  transfers between devices with their start and end apart: 4 -> 44, of which waited for: 3 -> 12; matrix products, arithmetic and copies ran while one was open for 24% -> 12% of each run, Pallas kernels for 0% -> 18%
where the time goes in v1:
time: 246 us; the launch traced here: 244 us
  waiting for transfers between devices  80.6 us (33%)
  Pallas kernels  57.8 us (23%)
  starting transfers between devices  56.2 us (23%)
  local copies, waits for them, and re-layouts  40.1 us (16%)
  other arithmetic  8.25 us (3%)
    ppermute x18, waiting for transfers between devices, across(): return lax.ppermute(array, 'seq', [(i, i ^ bit) for i in range(4)])  50.5 us
    ppermute x25, starting transfers between devices, hop(): return lax.ppermute(array, 'head', links)  42.3 us
    ppermute x25, waiting for transfers between devices, hop(): return lax.ppermute(array, 'head', links)  30.1 us
    pallas_call x4, Pallas kernels, project(): pl.pallas_call(functools.partial(project_kernel, number), out_shape=jax.S...  23 us
    pallas_call x1, Pallas kernels, update(): pl.pallas_call(update_kernel, out_shape=[out] * 3, grid_spec=pltpu.Prefet...  22.5 us
    unnamed x58, local copies, waits for them, and re-layouts  13.2 us
    ppermute x18, starting transfers between devices, across(): return lax.ppermute(array, 'seq', [(i, i ^ bit) for i in range(4)])  12.3 us
    reshape x2, local copies, waits for them, and re-layouts, heads_of(): return jnp.transpose(cut.reshape(depth, 3, 2, size), (2, 1, 0, 3))  7.55 us
  transfers between devices with their start and end apart: 44, of which 12 were waited for; matrix products, arithmetic and copies ran while one was open for 12% of the time, Pallas kernels for 18%

profile of v1, /device:TPU:0, one launch (start us, length us, event | category | flops | bytes accessed | tf_op | source)
XLA Modules:
  0.0 244.4 jit_solution(10769116346578824534)
XLA Ops:
  0.0 6.2 %constant_dynamic-slice_fusion.1 = (bf16[1024,3,512]{2,0,1:T(8,128)(2,1)}, bf16[1024,3,512]{2,0,1:T(8,128)(2,1)}) fusion(bf16[1024,3,1024]{2,0,1:T(8,128)(2,1)} %param.9, s32[]{:T(128)S(6)} %select_n.80, s32[]{:T(128)S(6)} %select_n.79), kind=kLoop, calls=%fused_computation.18 | loop fusion | bytes 12582920 | tf_op jit(solution)/shard_map/dynamic_slice | solution.py:334
  6.2 3.2 %copy.15 = bf16[1024,3,512]{0,2,1:T(8,128)(2,1)S(1)} copy(bf16[1024,3,512]{2,0,1:T(8,128)(2,1)} %get-tuple-element.13) | data formatting | bytes 6291456
  9.4 2.8 %copy.12 = bf16[1024,3,2,256]{3,0,1,2:T(8,128)(2,1)} copy(bf16[1024,3,2,256]{0,3,2,1:T(8,128)(2,1)S(1)} %bitcast.43) | data formatting | bytes 6291456 | tf_op jit(solution)/shard_map/reshape | solution.py:335
  12.7 2.5 %constant_dynamic-slice_fusion.3 = (bf16[256,1024]{1,0:T(8,128)(2,1)S(1)}, bf16[256,1024]{1,0:T(8,128)(2,1)}, bf16[256,1024]{1,0:T(8,128)(2,1)}) fusion(bf16[256,4096]{1,0:T(8,128)(2,1)} %param.8, s32[]{:T(128)S(6)} %select_n.78, s32[]{:T(128)S(6)} %select_n.77, s32[]{:T(128)S(6)} %select_n.76), kind=kLoop, calls=%fused_computation.20 | loop fusion | bytes 3145740 | tf_op jit(solution)/shard_map/dynamic_slice | solution.py:322
  15.1 2.5 %collective-permute-start.2 = (bf16[256,1024]{1,0:T(8,128)(2,1)S(1)}, bf16[256,1024]{1,0:T(8,128)(2,1)}, u32[]{:S(2)}, u32[]{:S(2)}) collective-permute-start(bf16[256,1024]{1,0:T(8,128)(2,1)S(1)} %get-tuple-element.17), channel_id=1, source_target_pairs={{0,8},{4,12},{8,0},{12,4},{1,9},{5,13},{9,1},{13,5},{2,10},{6,14},... | collective-permute-start | bytes 1572872 | tf_op jit(solution)/shard_map/ppermute | solution.py:316
  17.6 12.7 %collective-permute-done.2.refs_4_.refs_0_ = bf16[256,1024]{1,0:T(8,128)(2,1)} collective-permute-done((bf16[256,1024]{1,0:T(8,128)(2,1)S(1)}, bf16[256,1024]{1,0:T(8,128)(2,1)}, u32[]{:S(2)}, u32[]{:S(2)}) %collective-permute-start.2) | collective-permute-done | bytes 524320 | tf_op jit(solution)/shard_map/ppermute | solution.py:316
  30.3 1.8 collective-permute-start.3
  32.7 11.7 %collective-permute-done.3.refs_5_.refs_1_ = bf16[256,1024]{1,0:T(8,128)(2,1)} collective-permute-done((bf16[256,1024]{1,0:T(8,128)(2,1)}, bf16[256,1024]{1,0:T(8,128)(2,1)}, u32[]{:S(2)}, u32[]{:S(2)}) %collective-permute-start.3) | collective-permute-done | bytes 524320 | tf_op jit(solution)/shard_map/ppermute | solution.py:319
  44.4 4.7 %copy.14 = bf16[1024,3,512]{0,2,1:T(8,128)(2,1)} copy(bf16[1024,3,512]{2,0,1:T(8,128)(2,1)} %get-tuple-element.14) | data formatting | bytes 6291456
  49.1 4.7 %copy.10 = bf16[1024,3,2,256]{3,0,1,2:T(8,128)(2,1)} copy(bf16[1024,3,2,256]{0,3,2,1:T(8,128)(2,1)} %bitcast.44) | data formatting | bytes 6291456 | tf_op jit(solution)/shard_map/reshape | solution.py:335
  54.5 1.7 copy-done.2
  56.2 5.3 %shard_map.83 = bf16[1,1024,256]{2,1,0:T(8,128)(2,1)} custom-call(s32[5]{0:T(128)} %stack.131.index_ref, bf16[256,1024]{1,0:T(8,128)(2,1)} %get-tuple-element.19.refs_0_, bf16[256,1024]{1,0:T(8,128)(2,1)} %get-tuple-element.18.refs_1_, bf16[256,1024]{1,0:T(8,128)(2,1)} %collective-permute-done.refs_2_, bf16[256,1024]{1,0:T(8,128)(2,1)} %collective-permute-done.1.refs_3_, ...), custom_call_target="tpu_custom_call" | custom-call | flops 1073741824 | bytes 5242880 | tf_op jit(solution)/shard_map/pallas_call | solution.py:130
  61.5 1.4 constant_dynamic-slice_fusion
  62.9 1.6 collective-permute-start.41
  64.5 24.1 %collective-permute-done.41 = bf16[512,1024]{1,0:T(8,128)(2,1)S(1)} collective-permute-done((bf16[512,1024]{1,0:T(8,128)(2,1)S(1)}, bf16[512,1024]{1,0:T(8,128)(2,1)S(1)}, u32[]{:S(2)}, u32[]{:S(2)}) %collective-permute-start.41) | collective-permute-done | bytes 1048608 | tf_op jit(solution)/shard_map/ppermute | solution.py:316
  88.5 1.6 collective-permute-start.42
  90.8 1.5 collective-permute-start.11
  95.4 1.0 broadcast_in_dim.4.rate_ref
  96.4 1.0 collective-permute-start.7
  97.3 4.7 %shard_map.84 = bf16[2,512,256]{2,1,0:T(8,128)(2,1)} custom-call(s32[3]{0:T(128)} %pad_add_fusion.index_ref, bf16[256,1024]{1,0:T(8,128)(2,1)} %collective-permute-done.2.refs_4_.refs_0_, bf16[256,1024]{1,0:T(8,128)(2,1)} %collective-permute-done.3.refs_5_.refs_1_, bf16[256,1024]{1,0:T(8,128)(2,1)} %collective-permute-done.4.refs_6_.refs_2_, ...), custom_call_target="tpu_custom_call" | custom-call | flops 1073741824 | bytes 4194304 | tf_op jit(solution)/shard_map/pallas_call | solution.py:130
  102.1 1.1 collective-permute-start.8
  103.1 4.7 %shard_map.85 = bf16[2,512,256]{2,1,0:T(8,128)(2,1)} custom-call(s32[3]{0:T(128)} %pad_add_fusion.1.index_ref, bf16[256,1024]{1,0:T(8,128)(2,1)} %get-tuple-element.19.refs_0_, bf16[256,1024]{1,0:T(8,128)(2,1)} %get-tuple-element.18.refs_1_, bf16[256,1024]{1,0:T(8,128)(2,1)} %collective-permute-done.refs_2_, ...), custom_call_target="tpu_custom_call" | custom-call | flops 1073741824 | bytes 4194304 | tf_op jit(solution)/shard_map/pallas_call | solution.py:130
  107.8 1.0 collective-permute-start.9
  108.8 8.2 %shard_map.82 = f32[3,1024,256]{2,1,0:T(8,128)} custom-call(s32[5]{0:T(128)} %stack.129.index_ref, bf16[256,1024]{1,0:T(8,128)(2,1)} %get-tuple-element.19.refs_0_, bf16[256,1024]{1,0:T(8,128)(2,1)} %get-tuple-element.18.refs_1_, bf16[256,1024]{1,0:T(8,128)(2,1)} %collective-permute-done.refs_2_, bf16[256,1024]{1,0:T(8,128)(2,1)} %collective-permute-done.1.refs_3_, ...), custom_call_target="tpu_custom_call" | custom-call | flops 3221225472 | bytes 7340032 | tf_op jit(solution)/shard_map/pallas_call | solution.py:130
  117.1 2.3 slice.24.local_ref
  119.4 3.0 %slice.25.local_ref = f32[2,1024,256]{2,1,0:T(8,128)} slice(f32[3,1024,256]{2,1,0:T(8,128)} %shard_map.82), slice={[1:3], [0:1024], [0:256]} | slice | bytes 4194304 | tf_op jit(solution)/shard_map/slice | solution.py:365
  122.8 10.7 %collective-permute-done.9.far_ref = bf16[2,512,256]{2,1,0:T(8,128)(2,1)S(1)} collective-permute-done((bf16[2,512,256]{2,1,0:T(8,128)(2,1)}, bf16[2,512,256]{2,1,0:T(8,128)(2,1)S(1)}, u32[]{:S(2)}, u32[]{:S(2)}) %collective-permute-start.9) | collective-permute-done | bytes 524320 | tf_op jit(solution)/shard_map/ppermute | solution.py:316
  133.5 0.8 copy-done.27
  134.3 22.5 %shard_map.86 = (bf16[256,512]{1,0:T(8,128)(2,1)}, bf16[256,512]{1,0:T(8,128)(2,1)}, bf16[256,512]{1,0:T(8,128)(2,1)}) custom-call(s32[1]{0:T(128)} %bitcast.3.index_ref, f32[2,1024,256]{2,1,0:T(8,128)} %slice.25.local_ref, bf16[2,512,256]{2,1,0:T(8,128)(2,1)} %copy-done.26, bf16[2,512,256]{2,1,0:T(8,128)(2,1)} %copy-done.27, ...), custom_call_target="tpu_custom_call" | custom-call | flops 14763950080 | bytes 4718592 | tf_op jit(solution)/shard_map/pallas_call | solution.py:211
  156.8 0.8 copy-done.25
  157.6 5.0 %shard_map.87 = bf16[4,256,256]{2,1,0:T(8,128)(2,1)} custom-call(s32[1]{0:T(128)} %bitcast.3.index_ref, f32[1,1024,256]{2,1,0:T(8,128)} %slice.24.local_ref, bf16[1,1024,256]{2,1,0:T(8,128)(2,1)} %copy-done.25, f32[4,1,256]{2,1,0:T(1,128)} %bitcast.50, bf16[256,512]{1,0:T(8,128)(2,1)} %get-tuple-element.9.gate_ref, ...), custom_call_target="tpu_custom_call" | custom-call | flops 805306368 | bytes 2097152 | tf_op jit(solution)/shard_map/pallas_call | solution.py:244
  162.5 1.1 slice_bitcast_fusion
  163.7 1.6 collective-permute-start.26
  165.6 1.3 collective-permute-start.16
  166.9 2.5 %collective-permute-done.33.refs_21_ = bf16[256,256]{1,0:T(8,128)(2,1)S(1)} collective-permute-done((bf16[256,256]{1,0:T(8,128)(2,1)S(1)}, bf16[256,256]{1,0:T(8,128)(2,1)S(1)}, u32[]{:S(2)}, u32[]{:S(2)}) %collective-permute-start.33) | collective-permute-done | bytes 131104 | tf_op jit(solution)/shard_map/ppermute | solution.py:316
  169.4 3.5 %collective-permute-start.13 = (bf16[256,256]{1,0:T(8,128)(2,1)S(1)}, bf16[256,256]{1,0:T(8,128)(2,1)S(1)}, u32[]{:S(2)}, u32[]{:S(2)}) collective-permute-start(bf16[256,256]{1,0:T(8,128)(2,1)S(1)} %get-tuple-element.23.refs_0_), channel_id=1, source_target_pairs={{0,1},{1,2},{2,3},{4,5},{5,6},{6,7},{8,9},{9,10},{10,11},{12,13},{... | collective-permute-start | bytes 393224 | tf_op jit(solution)/shard_map/ppermute | solution.py:319
  172.9 1.3 collective-permute-start.37
  174.2 4.6 %collective-permute-start.34 = (bf16[256,256]{1,0:T(8,128)(2,1)S(1)}, bf16[256,256]{1,0:T(8,128)(2,1)S(1)}, u32[]{:S(2)}, u32[]{:S(2)}) collective-permute-start(bf16[256,256]{1,0:T(8,128)(2,1)S(1)} %collective-permute-done.33.refs_21_), channel_id=1, source_target_pairs={{0,1},{1,2},{2,3},{4,5},{5,6},{6,7},{8,9},{9,10},{10,11},{12,13},{... | collective-permute-start | bytes 393224 | tf_op jit(solution)/shard_map/ppermute | solution.py:319
  178.8 1.3 collective-permute-start.30
  180.1 4.6 %collective-permute-start.27 = (bf16[256,256]{1,0:T(8,128)(2,1)S(1)}, bf16[256,256]{1,0:T(8,128)(2,1)S(1)}, u32[]{:S(2)}, u32[]{:S(2)}) collective-permute-start(bf16[256,256]{1,0:T(8,128)(2,1)S(1)} %collective-permute-done.26.refs_14_), channel_id=1, source_target_pairs={{0,1},{1,2},{2,3},{4,5},{5,6},{6,7},{8,9},{9,10},{10,11},{12,13},{... | collective-permute-start | bytes 393224 | tf_op jit(solution)/shard_map/ppermute | solution.py:319
  184.7 1.3 collective-permute-start.23
  186.0 5.2 %collective-permute-start.20 = (bf16[256,256]{1,0:T(8,128)(2,1)S(1)}, bf16[256,256]{1,0:T(8,128)(2,1)}, u32[]{:S(2)}, u32[]{:S(2)}) collective-permute-start(bf16[256,256]{1,0:T(8,128)(2,1)S(1)} %collective-permute-done.19.refs_7_), channel_id=1, source_target_pairs={{0,1},{1,2},{2,3},{4,5},{5,6},{6,7},{8,9},{9,10},{10,11},{12,13},{... | collective-permute-start | bytes 393224 | tf_op jit(solution)/shard_map/ppermute | solution.py:319
  191.2 1.3 collective-permute-start.17
  192.6 1.3 collective-permute-start.14
  193.9 1.3 collective-permute-start.38
  195.2 0.7 collective-permute-start.35
  195.9 2.3 collective-permute-done.17.refs_5_
  198.2 1.3 collective-permute-start.31
  199.5 0.7 collective-permute-start.28
  200.2 4.1 %collective-permute-done.38.refs_26_ = bf16[256,256]{1,0:T(8,128)(2,1)} collective-permute-done((bf16[256,256]{1,0:T(8,128)(2,1)S(1)}, bf16[256,256]{1,0:T(8,128)(2,1)}, u32[]{:S(2)}, u32[]{:S(2)}) %collective-permute-start.38) | collective-permute-done | bytes 131104 | tf_op jit(solution)/shard_map/ppermute | solution.py:319
  204.3 1.3 collective-permute-start.24
  205.6 1.3 collective-permute-start.21
  206.9 3.8 %collective-permute-done.31.refs_19_ = bf16[256,256]{1,0:T(8,128)(2,1)S(1)} collective-permute-done((bf16[256,256]{1,0:T(8,128)(2,1)S(1)}, bf16[256,256]{1,0:T(8,128)(2,1)S(1)}, u32[]{:S(2)}, u32[]{:S(2)}) %collective-permute-start.31) | collective-permute-done | bytes 131104 | tf_op jit(solution)/shard_map/ppermute | solution.py:319
  210.7 1.3 collective-permute-start.18
  212.0 1.3 collective-permute-start.15
  213.3 3.3 %collective-permute-done.24.refs_12_ = bf16[256,256]{1,0:T(8,128)(2,1)S(1)} collective-permute-done((bf16[256,256]{1,0:T(8,128)(2,1)S(1)}, bf16[256,256]{1,0:T(8,128)(2,1)S(1)}, u32[]{:S(2)}, u32[]{:S(2)}) %collective-permute-start.24) | collective-permute-done | bytes 131104 | tf_op jit(solution)/shard_map/ppermute | solution.py:319
  217.3 1.3 collective-permute-start.39
  219.9 3.4 %collective-permute-done.18.refs_6_ = bf16[256,256]{1,0:T(8,128)(2,1)} collective-permute-done((bf16[256,256]{1,0:T(8,128)(2,1)}, bf16[256,256]{1,0:T(8,128)(2,1)}, u32[]{:S(2)}, u32[]{:S(2)}) %collective-permute-start.18) | collective-permute-done | bytes 131104 | tf_op jit(solution)/shard_map/ppermute | solution.py:319
  223.4 1.3 collective-permute-start.32
  224.6 0.7 collective-permute-start.29
  225.3 1.4 collective-permute-done.39.refs_27_
  226.7 1.3 collective-permute-start.25
  228.7 6.7 %pad_maximum_fusion.refs_28_ = bf16[4,4,256,1024]{3,2,1,0:T(8,128)(2,1)} fusion(bf16[1,4,256,1024]{3,2,1,0:T(8,128)(2,1)} %bitcast.31, bf16[1,4,256,1024]{3,2,1,0:T(8,128)(2,1)S(1)} %bitcast.45, bf16[1,4,256,1024]{3,2,1,0:T(8,128)(2,1)} %bitcast.29, bf16[1,4,256,1024]{3,2,1,0:T(8,128)(2,1)} %bitcast.28), kind=kLoop, calls=%fused_computation | loop fusion | flops 12582912 | bytes 16777216 | tf_op jit(solution)/shard_map/stack | solution.py:362
  236.9 7.3 %shard_map.88 = bf16[256,1024]{1,0:T(8,128)(2,1)} custom-call(s32[11]{0:T(128)} %stack.125.index_ref, bf16[256,256]{1,0:T(8,128)(2,1)} %copy-done.4, bf16[256,256]{1,0:T(8,128)(2,1)} %copy-done.10, bf16[256,256]{1,0:T(8,128)(2,1)} %collective-permute-done.14.refs_2_, bf16[256,256]{1,0:T(8,128)(2,1)} %collective-permute-done.15.refs_3_, ...), custom_call_target="tpu_custom_call" | custom-call | flops 2147483648 | bytes 12058624 | tf_op jit(solution)/shard_map/pallas_call | solution.py:287
  (108 shorter events, 10.2 us)
Async XLA Ops:
  0.0 90.1 %copy-start = (bf16[4096,4]{0,1:T(4,128)(2,1)S(1)}, bf16[4096,4]{0,1:T(4,128)(2,1)}, u32[]{:S(2)}) copy-start(bf16[4096,4]{0,1:T(4,128)(2,1)} %param.10) | copy-start | bytes 98308
  12.2 42.3 %collective-permute-start.6 = (bf16[2,3,1024,256]{3,2,1,0:T(8,128)(2,1)}, bf16[2,3,1024,256]{3,2,1,0:T(8,128)(2,1)S(1)}, u32[]{:S(2)}, u32[]{:S(2)}) collective-permute-start(bf16[2,3,1024,256]{3,2,1,0:T(8,128)(2,1)} %bitcast.46), channel_id=1, source_target_pairs={{0,4},{4,0},{8,12},{12,8},{1,5},{5,1},{9,13},{13,9},{2,6},{6,2},{1... | collective-permute-start | bytes 9437192 | tf_op jit(solution)/shard_map/ppermute | solution.py:316
  15.1 15.2 %collective-permute-start.2 = (bf16[256,1024]{1,0:T(8,128)(2,1)S(1)}, bf16[256,1024]{1,0:T(8,128)(2,1)}, u32[]{:S(2)}, u32[]{:S(2)}) collective-permute-start(bf16[256,1024]{1,0:T(8,128)(2,1)S(1)} %get-tuple-element.17), channel_id=1, source_target_pairs={{0,8},{4,12},{8,0},{12,4},{1,9},{5,13},{9,1},{13,5},{2,10},{6,14},... | collective-permute-start | bytes 1572872 | tf_op jit(solution)/shard_map/ppermute | solution.py:316
  30.3 14.1 %collective-permute-start.3 = (bf16[256,1024]{1,0:T(8,128)(2,1)}, bf16[256,1024]{1,0:T(8,128)(2,1)}, u32[]{:S(2)}, u32[]{:S(2)}) collective-permute-start(bf16[256,1024]{1,0:T(8,128)(2,1)} %collective-permute-done.2.refs_4_.refs_0_), channel_id=1, source_target_pairs={{0,1},{1,0},{2,3},{3,2},{4,5},{5,4},{6,7},{7,6},{8,9},{9,8},{10,11... | collective-permute-start | bytes 1572872 | tf_op jit(solution)/shard_map/ppermute | solution.py:319
  32.2 22.3 %collective-permute-start.1 = (bf16[256,1024]{1,0:T(8,128)(2,1)}, bf16[256,1024]{1,0:T(8,128)(2,1)}, u32[]{:S(2)}, u32[]{:S(2)}) collective-permute-start(bf16[256,1024]{1,0:T(8,128)(2,1)} %get-tuple-element.18.refs_1_), channel_id=1, source_target_pairs={{0,4},{4,0},{8,12},{12,8},{1,5},{5,1},{9,13},{13,9},{2,6},{6,2},{1... | collective-permute-start | bytes 1572872 | tf_op jit(solution)/shard_map/ppermute | solution.py:316
  32.2 22.3 %collective-permute-start = (bf16[256,1024]{1,0:T(8,128)(2,1)}, bf16[256,1024]{1,0:T(8,128)(2,1)}, u32[]{:S(2)}, u32[]{:S(2)}) collective-permute-start(bf16[256,1024]{1,0:T(8,128)(2,1)} %get-tuple-element.19.refs_0_), channel_id=1, source_target_pairs={{0,4},{4,0},{8,12},{12,8},{1,5},{5,1},{9,13},{13,9},{2,6},{6,2},{1... | collective-permute-start | bytes 1572872 | tf_op jit(solution)/shard_map/ppermute | solution.py:316
  32.7 21.8 %collective-permute-start.4 = (bf16[256,1024]{1,0:T(8,128)(2,1)}, bf16[256,1024]{1,0:T(8,128)(2,1)}, u32[]{:S(2)}, u32[]{:S(2)}) collective-permute-start(bf16[256,1024]{1,0:T(8,128)(2,1)} %collective-permute-done.2.refs_4_.refs_0_), channel_id=1, source_target_pairs={{0,4},{4,0},{8,12},{12,8},{1,5},{5,1},{9,13},{13,9},{2,6},{6,2},{1... | collective-permute-start | bytes 1572872 | tf_op jit(solution)/shard_map/ppermute | solution.py:316
  44.4 10.1 %collective-permute-start.5 = (bf16[256,1024]{1,0:T(8,128)(2,1)}, bf16[256,1024]{1,0:T(8,128)(2,1)}, u32[]{:S(2)}, u32[]{:S(2)}) collective-permute-start(bf16[256,1024]{1,0:T(8,128)(2,1)} %collective-permute-done.3.refs_5_.refs_1_), channel_id=1, source_target_pairs={{0,4},{4,0},{8,12},{12,8},{1,5},{5,1},{9,13},{13,9},{2,6},{6,2},{1... | collective-permute-start | bytes 1572872 | tf_op jit(solution)/shard_map/ppermute | solution.py:316
  54.5 1.7 copy-start.2
  56.2 33.9 %copy-start.3 = (bf16[256,4096]{1,0:T(8,128)(2,1)S(1)}, bf16[256,4096]{1,0:T(8,128)(2,1)}, u32[]{:S(2)}) copy-start(bf16[256,4096]{1,0:T(8,128)(2,1)} %param.8) | copy-start | bytes 6291460
  61.5 34.9 %copy-start.5 = (bf16[1,1024,256]{2,1,0:T(8,128)(2,1)S(1)}, bf16[1,1024,256]{2,1,0:T(8,128)(2,1)}, u32[]{:S(2)}) copy-start(bf16[1,1024,256]{2,1,0:T(8,128)(2,1)} %shard_map.83) | copy-start | bytes 1572868
  62.9 25.7 %collective-permute-start.41 = (bf16[512,1024]{1,0:T(8,128)(2,1)S(1)}, bf16[512,1024]{1,0:T(8,128)(2,1)S(1)}, u32[]{:S(2)}, u32[]{:S(2)}) collective-permute-start(bf16[512,1024]{1,0:T(8,128)(2,1)S(1)} %constant_dynamic-slice_fusion), channel_id=1, source_target_pairs={{0,8},{4,12},{8,0},{12,4},{1,9},{5,13},{9,1},{13,5},{2,10},{6,14},... | collective-permute-start | bytes 3145736 | tf_op jit(solution)/shard_map/ppermute | solution.py:316
  88.5 33.9 %collective-permute-start.42 = (bf16[512,1024]{1,0:T(8,128)(2,1)S(1)}, bf16[512,1024]{1,0:T(8,128)(2,1)S(1)}, u32[]{:S(2)}, u32[]{:S(2)}) collective-permute-start(bf16[512,1024]{1,0:T(8,128)(2,1)S(1)} %collective-permute-done.41), channel_id=1, source_target_pairs={{0,16},{16,0},{1,17},{17,1},{2,18},{18,2},{3,19},{19,3},{4,20},{20... | collective-permute-start | bytes 3145736 | tf_op jit(solution)/shard_map/ppermute | solution.py:358
  90.8 4.0 %collective-permute-start.11 = (f32[4,256]{1,0:T(4,128)S(1)}, f32[4,256]{1,0:T(4,128)S(1)}, u32[]{:S(2)}, u32[]{:S(2)}) collective-permute-start(f32[4,256]{1,0:T(4,128)S(1)} %get-tuple-element.25), channel_id=1, source_target_pairs={{0,8},{4,12},{8,0},{12,4},{1,9},{5,13},{9,1},{13,5},{2,10},{6,14},... | collective-permute-start | bytes 12296 | tf_op jit(solution)/shard_map/ppermute | solution.py:316
  92.3 2.5 %collective-permute-start.10 = (f32[4,256]{1,0:T(4,128)S(1)}, f32[4,256]{1,0:T(4,128)S(1)}, u32[]{:S(2)}, u32[]{:S(2)}) collective-permute-start(f32[4,256]{1,0:T(4,128)S(1)} %get-tuple-element.25), channel_id=1, source_target_pairs={{0,4},{4,0},{8,12},{12,8},{1,5},{5,1},{9,13},{13,9},{2,6},{6,2},{1... | collective-permute-start | bytes 12296 | tf_op jit(solution)/shard_map/ppermute | solution.py:316
  92.3 3.0 %collective-permute-start.12 = (f32[4,256]{1,0:T(4,128)S(1)}, f32[4,256]{1,0:T(4,128)S(1)}, u32[]{:S(2)}, u32[]{:S(2)}) collective-permute-start(f32[4,256]{1,0:T(4,128)S(1)} %get-tuple-element.25), channel_id=1, source_target_pairs={{0,12},{4,8},{8,4},{12,0},{1,13},{5,9},{9,5},{13,1},{2,14},{6,10},... | collective-permute-start | bytes 12296 | tf_op jit(solution)/shard_map/ppermute | solution.py:316
  93.0 72.6 %collective-permute-start.40 = (bf16[1024,1024]{1,0:T(8,128)(2,1)}, bf16[1024,1024]{1,0:T(8,128)(2,1)}, u32[]{:S(2)}, u32[]{:S(2)}) collective-permute-start(bf16[1024,1024]{1,0:T(8,128)(2,1)} %param.15), channel_id=1, source_target_pairs={{0,4},{4,0},{8,12},{12,8},{1,5},{5,1},{9,13},{13,9},{2,6},{6,2},{1... | collective-permute-start | bytes 6291464 | tf_op jit(solution)/shard_map/ppermute | solution.py:316
  96.4 60.4 %collective-permute-start.7 = (bf16[1,1024,256]{2,1,0:T(8,128)(2,1)S(1)}, bf16[1,1024,256]{2,1,0:T(8,128)(2,1)S(1)}, u32[]{:S(2)}, u32[]{:S(2)}) collective-permute-start(bf16[1,1024,256]{2,1,0:T(8,128)(2,1)S(1)} %copy-done.5), channel_id=1, source_target_pairs={{0,8},{4,12},{8,0},{12,4},{1,9},{5,13},{9,1},{13,5},{2,10},{6,14},... | collective-permute-start | bytes 1572872 | tf_op jit(solution)/shard_map/ppermute | solution.py:316
  102.1 20.7 %collective-permute-start.8 = (bf16[2,512,256]{2,1,0:T(8,128)(2,1)}, bf16[2,512,256]{2,1,0:T(8,128)(2,1)S(1)}, u32[]{:S(2)}, u32[]{:S(2)}) collective-permute-start(bf16[2,512,256]{2,1,0:T(8,128)(2,1)} %shard_map.84), channel_id=1, source_target_pairs={{0,8},{4,12},{8,0},{12,4},{1,9},{5,13},{9,1},{13,5},{2,10},{6,14},... | collective-permute-start | bytes 1572872 | tf_op jit(solution)/shard_map/ppermute | solution.py:316
  107.8 25.6 %collective-permute-start.9 = (bf16[2,512,256]{2,1,0:T(8,128)(2,1)}, bf16[2,512,256]{2,1,0:T(8,128)(2,1)S(1)}, u32[]{:S(2)}, u32[]{:S(2)}) collective-permute-start(bf16[2,512,256]{2,1,0:T(8,128)(2,1)} %shard_map.85), channel_id=1, source_target_pairs={{0,8},{4,12},{8,0},{12,4},{1,9},{5,13},{9,1},{13,5},{2,10},{6,14},... | collective-permute-start | bytes 1572872 | tf_op jit(solution)/shard_map/ppermute | solution.py:316
  122.7 105.3 %collective-permute-start.43 = (bf16[1024,1024]{1,0:T(8,128)(2,1)S(1)}, bf16[1024,1024]{1,0:T(8,128)(2,1)}, u32[]{:S(2)}, u32[]{:S(2)}) collective-permute-start(bf16[1024,1024]{1,0:T(8,128)(2,1)S(1)} %pad_maximum_fusion.1), channel_id=1, source_target_pairs={{0,4},{4,0},{8,12},{12,8},{1,5},{5,1},{9,13},{13,9},{2,6},{6,2},{1... | collective-permute-start | bytes 6291464 | tf_op jit(solution)/shard_map/ppermute | solution.py:316
  122.8 10.7 %copy-start.26 = (bf16[2,512,256]{2,1,0:T(8,128)(2,1)}, bf16[2,512,256]{2,1,0:T(8,128)(2,1)S(1)}, u32[]{:S(2)}) copy-start(bf16[2,512,256]{2,1,0:T(8,128)(2,1)S(1)} %collective-permute-done.8.near_ref) | copy-start | bytes 1572868
  163.6 71.7 %copy-start.4 = (bf16[256,256]{1,0:T(8,128)(2,1)}, bf16[256,256]{1,0:T(8,128)(2,1)S(1)}, u32[]{:S(2)}) copy-start(bf16[256,256]{1,0:T(8,128)(2,1)S(1)} %get-tuple-element.23.refs_0_) | copy-start | bytes 393220
  163.7 5.7 %collective-permute-start.33 = (bf16[256,256]{1,0:T(8,128)(2,1)S(1)}, bf16[256,256]{1,0:T(8,128)(2,1)S(1)}, u32[]{:S(2)}, u32[]{:S(2)}) collective-permute-start(bf16[256,256]{1,0:T(8,128)(2,1)S(1)} %get-tuple-element.20), channel_id=1, source_target_pairs={{0,12},{4,8},{8,4},{12,0},{1,13},{5,9},{9,5},{13,1},{2,14},{6,10},... | collective-permute-start | bytes 393224 | tf_op jit(solution)/shard_map/ppermute | solution.py:316
  163.7 9.1 %collective-permute-start.26 = (bf16[256,256]{1,0:T(8,128)(2,1)S(1)}, bf16[256,256]{1,0:T(8,128)(2,1)S(1)}, u32[]{:S(2)}, u32[]{:S(2)}) collective-permute-start(bf16[256,256]{1,0:T(8,128)(2,1)S(1)} %get-tuple-element.21), channel_id=1, source_target_pairs={{0,8},{4,12},{8,0},{12,4},{1,9},{5,13},{9,1},{13,5},{2,10},{6,14},... | collective-permute-start | bytes 393224 | tf_op jit(solution)/shard_map/ppermute | solution.py:316
  165.3 8.9 %collective-permute-start.19 = (bf16[256,256]{1,0:T(8,128)(2,1)S(1)}, bf16[256,256]{1,0:T(8,128)(2,1)S(1)}, u32[]{:S(2)}, u32[]{:S(2)}) collective-permute-start(bf16[256,256]{1,0:T(8,128)(2,1)S(1)} %get-tuple-element.22), channel_id=1, source_target_pairs={{0,4},{4,0},{8,12},{12,8},{1,5},{5,1},{9,13},{13,9},{2,6},{6,2},{1... | collective-permute-start | bytes 393224 | tf_op jit(solution)/shard_map/ppermute | solution.py:316
  165.6 13.2 %collective-permute-start.16 = (bf16[256,256]{1,0:T(8,128)(2,1)S(1)}, bf16[256,256]{1,0:T(8,128)(2,1)S(1)}, u32[]{:S(2)}, u32[]{:S(2)}) collective-permute-start(bf16[256,256]{1,0:T(8,128)(2,1)S(1)} %get-tuple-element.23.refs_0_), channel_id=1, source_target_pairs={{1,0},{2,1},{3,2},{5,4},{6,5},{7,6},{9,8},{10,9},{11,10},{13,12},{... | collective-permute-start | bytes 393224 | tf_op jit(solution)/shard_map/ppermute | solution.py:319
  169.4 66.0 %copy-start.6 = (bf16[256,256]{1,0:T(8,128)(2,1)}, bf16[256,256]{1,0:T(8,128)(2,1)S(1)}, u32[]{:S(2)}) copy-start(bf16[256,256]{1,0:T(8,128)(2,1)S(1)} %collective-permute-done.33.refs_21_) | copy-start | bytes 393220
  169.4 10.7 %collective-permute-start.13 = (bf16[256,256]{1,0:T(8,128)(2,1)S(1)}, bf16[256,256]{1,0:T(8,128)(2,1)S(1)}, u32[]{:S(2)}, u32[]{:S(2)}) collective-permute-start(bf16[256,256]{1,0:T(8,128)(2,1)S(1)} %get-tuple-element.23.refs_0_), channel_id=1, source_target_pairs={{0,1},{1,2},{2,3},{4,5},{5,6},{6,7},{8,9},{9,10},{10,11},{12,13},{... | collective-permute-start | bytes 393224 | tf_op jit(solution)/shard_map/ppermute | solution.py:319
  172.9 62.5 %copy-start.7 = (bf16[256,256]{1,0:T(8,128)(2,1)}, bf16[256,256]{1,0:T(8,128)(2,1)S(1)}, u32[]{:S(2)}) copy-start(bf16[256,256]{1,0:T(8,128)(2,1)S(1)} %collective-permute-done.26.refs_14_) | copy-start | bytes 393220
  172.9 11.8 %collective-permute-start.37 = (bf16[256,256]{1,0:T(8,128)(2,1)S(1)}, bf16[256,256]{1,0:T(8,128)(2,1)S(1)}, u32[]{:S(2)}, u32[]{:S(2)}) collective-permute-start(bf16[256,256]{1,0:T(8,128)(2,1)S(1)} %collective-permute-done.33.refs_21_), channel_id=1, source_target_pairs={{1,0},{2,1},{3,2},{5,4},{6,5},{7,6},{9,8},{10,9},{11,10},{13,12},{... | collective-permute-start | bytes 393224 | tf_op jit(solution)/shard_map/ppermute | solution.py:319
  174.2 61.2 %copy-start.8 = (bf16[256,256]{1,0:T(8,128)(2,1)}, bf16[256,256]{1,0:T(8,128)(2,1)S(1)}, u32[]{:S(2)}) copy-start(bf16[256,256]{1,0:T(8,128)(2,1)S(1)} %collective-permute-done.19.refs_7_) | copy-start | bytes 393220
  174.2 11.8 %collective-permute-start.34 = (bf16[256,256]{1,0:T(8,128)(2,1)S(1)}, bf16[256,256]{1,0:T(8,128)(2,1)S(1)}, u32[]{:S(2)}, u32[]{:S(2)}) collective-permute-start(bf16[256,256]{1,0:T(8,128)(2,1)S(1)} %collective-permute-done.33.refs_21_), channel_id=1, source_target_pairs={{0,1},{1,2},{2,3},{4,5},{5,6},{6,7},{8,9},{9,10},{10,11},{12,13},{... | collective-permute-start | bytes 393224 | tf_op jit(solution)/shard_map/ppermute | solution.py:319
  178.8 56.6 %copy-start.9 = (bf16[256,256]{1,0:T(8,128)(2,1)}, bf16[256,256]{1,0:T(8,128)(2,1)S(1)}, u32[]{:S(2)}) copy-start(bf16[256,256]{1,0:T(8,128)(2,1)S(1)} %collective-permute-done.16.refs_4_) | copy-start | bytes 393220
  178.8 12.4 %collective-permute-start.30 = (bf16[256,256]{1,0:T(8,128)(2,1)S(1)}, bf16[256,256]{1,0:T(8,128)(2,1)S(1)}, u32[]{:S(2)}, u32[]{:S(2)}) collective-permute-start(bf16[256,256]{1,0:T(8,128)(2,1)S(1)} %collective-permute-done.26.refs_14_), channel_id=1, source_target_pairs={{1,0},{2,1},{3,2},{5,4},{6,5},{7,6},{9,8},{10,9},{11,10},{13,12},{... | collective-permute-start | bytes 393224 | tf_op jit(solution)/shard_map/ppermute | solution.py:319
  180.1 55.3 %copy-start.10 = (bf16[256,256]{1,0:T(8,128)(2,1)}, bf16[256,256]{1,0:T(8,128)(2,1)S(1)}, u32[]{:S(2)}) copy-start(bf16[256,256]{1,0:T(8,128)(2,1)S(1)} %collective-permute-done.13.refs_1_) | copy-start | bytes 393220
  180.1 12.4 %collective-permute-start.27 = (bf16[256,256]{1,0:T(8,128)(2,1)S(1)}, bf16[256,256]{1,0:T(8,128)(2,1)S(1)}, u32[]{:S(2)}, u32[]{:S(2)}) collective-permute-start(bf16[256,256]{1,0:T(8,128)(2,1)S(1)} %collective-permute-done.26.refs_14_), channel_id=1, source_target_pairs={{0,1},{1,2},{2,3},{4,5},{5,6},{6,7},{8,9},{9,10},{10,11},{12,13},{... | collective-permute-start | bytes 393224 | tf_op jit(solution)/shard_map/ppermute | solution.py:319
  184.7 50.7 %copy-start.11 = (bf16[256,256]{1,0:T(8,128)(2,1)}, bf16[256,256]{1,0:T(8,128)(2,1)S(1)}, u32[]{:S(2)}) copy-start(bf16[256,256]{1,0:T(8,128)(2,1)S(1)} %collective-permute-done.37.refs_25_) | copy-start | bytes 393220
  184.7 9.2 %collective-permute-start.23 = (bf16[256,256]{1,0:T(8,128)(2,1)S(1)}, bf16[256,256]{1,0:T(8,128)(2,1)S(1)}, u32[]{:S(2)}, u32[]{:S(2)}) collective-permute-start(bf16[256,256]{1,0:T(8,128)(2,1)S(1)} %collective-permute-done.19.refs_7_), channel_id=1, source_target_pairs={{1,0},{2,1},{3,2},{5,4},{6,5},{7,6},{9,8},{10,9},{11,10},{13,12},{... | collective-permute-start | bytes 393224 | tf_op jit(solution)/shard_map/ppermute | solution.py:319
  186.0 49.4 %copy-start.12 = (bf16[256,256]{1,0:T(8,128)(2,1)}, bf16[256,256]{1,0:T(8,128)(2,1)S(1)}, u32[]{:S(2)}) copy-start(bf16[256,256]{1,0:T(8,128)(2,1)S(1)} %collective-permute-done.34.refs_22_) | copy-start | bytes 393220
  186.0 9.1 %collective-permute-start.20 = (bf16[256,256]{1,0:T(8,128)(2,1)S(1)}, bf16[256,256]{1,0:T(8,128)(2,1)}, u32[]{:S(2)}, u32[]{:S(2)}) collective-permute-start(bf16[256,256]{1,0:T(8,128)(2,1)S(1)} %collective-permute-done.19.refs_7_), channel_id=1, source_target_pairs={{0,1},{1,2},{2,3},{4,5},{5,6},{6,7},{8,9},{9,10},{10,11},{12,13},{... | collective-permute-start | bytes 393224 | tf_op jit(solution)/shard_map/ppermute | solution.py:319
  191.2 44.2 %copy-start.13 = (bf16[256,256]{1,0:T(8,128)(2,1)}, bf16[256,256]{1,0:T(8,128)(2,1)S(1)}, u32[]{:S(2)}) copy-start(bf16[256,256]{1,0:T(8,128)(2,1)S(1)} %collective-permute-done.30.refs_18_) | copy-start | bytes 393220
  191.2 7.0 %collective-permute-start.17 = (bf16[256,256]{1,0:T(8,128)(2,1)S(1)}, bf16[256,256]{1,0:T(8,128)(2,1)}, u32[]{:S(2)}, u32[]{:S(2)}) collective-permute-start(bf16[256,256]{1,0:T(8,128)(2,1)S(1)} %collective-permute-done.16.refs_4_), channel_id=1, source_target_pairs={{1,0},{2,1},{5,4},{6,5},{9,8},{10,9},{13,12},{14,13},{17,16},{18,1... | collective-permute-start | bytes 393224 | tf_op jit(solution)/shard_map/ppermute | solution.py:319
  192.5 42.9 %copy-start.14 = (bf16[256,256]{1,0:T(8,128)(2,1)}, bf16[256,256]{1,0:T(8,128)(2,1)S(1)}, u32[]{:S(2)}) copy-start(bf16[256,256]{1,0:T(8,128)(2,1)S(1)} %collective-permute-done.27.refs_15_) | copy-start | bytes 393220
  192.6 6.9 %collective-permute-start.14 = (bf16[256,256]{1,0:T(8,128)(2,1)S(1)}, bf16[256,256]{1,0:T(8,128)(2,1)}, u32[]{:S(2)}, u32[]{:S(2)}) collective-permute-start(bf16[256,256]{1,0:T(8,128)(2,1)S(1)} %collective-permute-done.13.refs_1_), channel_id=1, source_target_pairs={{1,2},{2,3},{5,6},{6,7},{9,10},{10,11},{13,14},{14,15},{17,18},{18... | collective-permute-start | bytes 393224 | tf_op jit(solution)/shard_map/ppermute | solution.py:319
  193.9 18.1 %copy-start.15 = (bf16[256,256]{1,0:T(8,128)(2,1)}, bf16[256,256]{1,0:T(8,128)(2,1)S(1)}, u32[]{:S(2)}) copy-start(bf16[256,256]{1,0:T(8,128)(2,1)S(1)} %collective-permute-done.23.refs_11_) | copy-start | bytes 393220
  193.9 10.4 %collective-permute-start.38 = (bf16[256,256]{1,0:T(8,128)(2,1)S(1)}, bf16[256,256]{1,0:T(8,128)(2,1)}, u32[]{:S(2)}, u32[]{:S(2)}) collective-permute-start(bf16[256,256]{1,0:T(8,128)(2,1)S(1)} %collective-permute-done.37.refs_25_), channel_id=1, source_target_pairs={{1,0},{2,1},{5,4},{6,5},{9,8},{10,9},{13,12},{14,13},{17,16},{18,1... | collective-permute-start | bytes 393224 | tf_op jit(solution)/shard_map/ppermute | solution.py:319
  195.2 10.4 %collective-permute-start.35 = (bf16[256,256]{1,0:T(8,128)(2,1)S(1)}, bf16[256,256]{1,0:T(8,128)(2,1)S(1)}, u32[]{:S(2)}, u32[]{:S(2)}) collective-permute-start(bf16[256,256]{1,0:T(8,128)(2,1)S(1)} %collective-permute-done.34.refs_22_), channel_id=1, source_target_pairs={{1,2},{2,3},{5,6},{6,7},{9,10},{10,11},{13,14},{14,15},{17,18},{18... | collective-permute-start | bytes 393224 | tf_op jit(solution)/shard_map/ppermute | solution.py:319
  198.2 12.5 %collective-permute-start.31 = (bf16[256,256]{1,0:T(8,128)(2,1)S(1)}, bf16[256,256]{1,0:T(8,128)(2,1)S(1)}, u32[]{:S(2)}, u32[]{:S(2)}) collective-permute-start(bf16[256,256]{1,0:T(8,128)(2,1)S(1)} %collective-permute-done.30.refs_18_), channel_id=1, source_target_pairs={{1,0},{2,1},{5,4},{6,5},{9,8},{10,9},{13,12},{14,13},{17,16},{18,1... | collective-permute-start | bytes 393224 | tf_op jit(solution)/shard_map/ppermute | solution.py:319
  199.5 12.5 %collective-permute-start.28 = (bf16[256,256]{1,0:T(8,128)(2,1)S(1)}, bf16[256,256]{1,0:T(8,128)(2,1)S(1)}, u32[]{:S(2)}, u32[]{:S(2)}) collective-permute-start(bf16[256,256]{1,0:T(8,128)(2,1)S(1)} %collective-permute-done.27.refs_15_), channel_id=1, source_target_pairs={{1,2},{2,3},{5,6},{6,7},{9,10},{10,11},{13,14},{14,15},{17,18},{18... | collective-permute-start | bytes 393224 | tf_op jit(solution)/shard_map/ppermute | solution.py:319
  204.3 12.3 %collective-permute-start.24 = (bf16[256,256]{1,0:T(8,128)(2,1)S(1)}, bf16[256,256]{1,0:T(8,128)(2,1)S(1)}, u32[]{:S(2)}, u32[]{:S(2)}) collective-permute-start(bf16[256,256]{1,0:T(8,128)(2,1)S(1)} %collective-permute-done.23.refs_11_), channel_id=1, source_target_pairs={{1,0},{2,1},{5,4},{6,5},{9,8},{10,9},{13,12},{14,13},{17,16},{18,1... | collective-permute-start | bytes 393224 | tf_op jit(solution)/shard_map/ppermute | solution.py:319
  205.6 11.0 %copy-start.16 = (bf16[256,256]{1,0:T(8,128)(2,1)}, bf16[256,256]{1,0:T(8,128)(2,1)S(1)}, u32[]{:S(2)}) copy-start(bf16[256,256]{1,0:T(8,128)(2,1)S(1)} %collective-permute-done.35.refs_23_) | copy-start | bytes 393220
  205.6 13.7 %collective-permute-start.21 = (bf16[256,256]{1,0:T(8,128)(2,1)}, bf16[256,256]{1,0:T(8,128)(2,1)}, u32[]{:S(2)}, u32[]{:S(2)}) collective-permute-start(bf16[256,256]{1,0:T(8,128)(2,1)} %collective-permute-done.20.refs_8_), channel_id=1, source_target_pairs={{1,2},{2,3},{5,6},{6,7},{9,10},{10,11},{13,14},{14,15},{17,18},{18... | collective-permute-start | bytes 393224 | tf_op jit(solution)/shard_map/ppermute | solution.py:319
  210.7 5.9 %copy-start.17 = (bf16[256,256]{1,0:T(8,128)(2,1)}, bf16[256,256]{1,0:T(8,128)(2,1)S(1)}, u32[]{:S(2)}) copy-start(bf16[256,256]{1,0:T(8,128)(2,1)S(1)} %collective-permute-done.31.refs_19_) | copy-start | bytes 393220
  210.7 12.6 %collective-permute-start.18 = (bf16[256,256]{1,0:T(8,128)(2,1)}, bf16[256,256]{1,0:T(8,128)(2,1)}, u32[]{:S(2)}, u32[]{:S(2)}) collective-permute-start(bf16[256,256]{1,0:T(8,128)(2,1)} %collective-permute-done.17.refs_5_), channel_id=1, source_target_pairs={{1,0},{5,4},{9,8},{13,12},{17,16},{21,20},{25,24},{29,28}} | collective-permute-start | bytes 393224 | tf_op jit(solution)/shard_map/ppermute | solution.py:319
  212.0 4.6 %copy-start.18 = (bf16[256,256]{1,0:T(8,128)(2,1)}, bf16[256,256]{1,0:T(8,128)(2,1)S(1)}, u32[]{:S(2)}) copy-start(bf16[256,256]{1,0:T(8,128)(2,1)S(1)} %collective-permute-done.28.refs_16_) | copy-start | bytes 393220
  212.0 12.6 %collective-permute-start.15 = (bf16[256,256]{1,0:T(8,128)(2,1)}, bf16[256,256]{1,0:T(8,128)(2,1)}, u32[]{:S(2)}, u32[]{:S(2)}) collective-permute-start(bf16[256,256]{1,0:T(8,128)(2,1)} %collective-permute-done.14.refs_2_), channel_id=1, source_target_pairs={{2,3},{6,7},{10,11},{14,15},{18,19},{22,23},{26,27},{30,31}} | collective-permute-start | bytes 393224 | tf_op jit(solution)/shard_map/ppermute | solution.py:319
  217.3 9.4 %collective-permute-start.39 = (bf16[256,256]{1,0:T(8,128)(2,1)}, bf16[256,256]{1,0:T(8,128)(2,1)}, u32[]{:S(2)}, u32[]{:S(2)}) collective-permute-start(bf16[256,256]{1,0:T(8,128)(2,1)} %collective-permute-done.38.refs_26_), channel_id=1, source_target_pairs={{1,0},{5,4},{9,8},{13,12},{17,16},{21,20},{25,24},{29,28}} | collective-permute-start | bytes 393224 | tf_op jit(solution)/shard_map/ppermute | solution.py:319
  219.3 16.2 %collective-permute-start.36 = (bf16[256,256]{1,0:T(8,128)(2,1)}, bf16[256,256]{1,0:T(8,128)(2,1)S(1)}, u32[]{:S(2)}, u32[]{:S(2)}) collective-permute-start(bf16[256,256]{1,0:T(8,128)(2,1)} %copy-done.16), channel_id=1, source_target_pairs={{2,3},{6,7},{10,11},{14,15},{18,19},{22,23},{26,27},{30,31}} | collective-permute-start | bytes 393224 | tf_op jit(solution)/shard_map/ppermute | solution.py:319
  223.4 12.1 %collective-permute-start.32 = (bf16[256,256]{1,0:T(8,128)(2,1)}, bf16[256,256]{1,0:T(8,128)(2,1)S(1)}, u32[]{:S(2)}, u32[]{:S(2)}) collective-permute-start(bf16[256,256]{1,0:T(8,128)(2,1)} %copy-done.17), channel_id=1, source_target_pairs={{1,0},{5,4},{9,8},{13,12},{17,16},{21,20},{25,24},{29,28}} | collective-permute-start | bytes 393224 | tf_op jit(solution)/shard_map/ppermute | solution.py:319
  224.6 10.8 %collective-permute-start.29 = (bf16[256,256]{1,0:T(8,128)(2,1)}, bf16[256,256]{1,0:T(8,128)(2,1)S(1)}, u32[]{:S(2)}, u32[]{:S(2)}) collective-permute-start(bf16[256,256]{1,0:T(8,128)(2,1)} %copy-done.18), channel_id=1, source_target_pairs={{2,3},{6,7},{10,11},{14,15},{18,19},{22,23},{26,27},{30,31}} | collective-permute-start | bytes 393224 | tf_op jit(solution)/shard_map/ppermute | solution.py:319
  226.7 8.8 %collective-permute-start.25 = (bf16[256,256]{1,0:T(8,128)(2,1)}, bf16[256,256]{1,0:T(8,128)(2,1)S(1)}, u32[]{:S(2)}, u32[]{:S(2)}) collective-permute-start(bf16[256,256]{1,0:T(8,128)(2,1)} %copy-done.19), channel_id=1, source_target_pairs={{1,0},{5,4},{9,8},{13,12},{17,16},{21,20},{25,24},{29,28}} | collective-permute-start | bytes 393224 | tf_op jit(solution)/shard_map/ppermute | solution.py:319
  228.0 7.5 %collective-permute-start.22 = (bf16[256,256]{1,0:T(8,128)(2,1)}, bf16[256,256]{1,0:T(8,128)(2,1)S(1)}, u32[]{:S(2)}, u32[]{:S(2)}) collective-permute-start(bf16[256,256]{1,0:T(8,128)(2,1)} %collective-permute-done.21.refs_9_), channel_id=1, source_target_pairs={{2,3},{6,7},{10,11},{14,15},{18,19},{22,23},{26,27},{30,31}} | collective-permute-start | bytes 393224 | tf_op jit(solution)/shard_map/ppermute | solution.py:319
  236.9 7.3 %copy-start.1 = (bf16[4096,4]{0,1:T(4,128)(2,1)S(1)}, bf16[4096,4]{0,1:T(4,128)(2,1)}, u32[]{:S(2)}) copy-start(bf16[4096,4]{0,1:T(4,128)(2,1)} %param.10) | copy-start | bytes 98308
  (8 other events, 5.7 us)

commit v2 on v1

--- a/solution.py
+++ b/solution.py
@@ -108,32 +108,47 @@
     return lax.dot_general(a, b, (((0,), (0,)), ((), ())), preferred_element_type=F32)
 
 
-def project_kernel(pairs, index_ref, *refs):
-    token_refs = refs[: 2 * pairs]
-    keep_ref, peer_ref, out_ref = refs[2 * pairs :]
-    rows = token_refs[0].shape[0]
+def project_kernel(pairs, whole_pairs, index_ref, *refs):
+    keep_ref, given_ref, out_ref = refs[-3:]
+    depth = keep_ref.shape[1]
+    place = 0
     for pair in range(pairs):
-        low, high = token_refs[2 * pair][...], token_refs[2 * pair + 1][...]
-        swapped = index_ref[1 + pair] == 1
-        first = jnp.where(swapped, high, low)
-        second = jnp.where(swapped, low, high)
-        total = dot(first, keep_ref[0, 0]) + dot(second, peer_ref[0, 0])
+        order = index_ref[3 + pair]
+        if pair < whole_pairs:
+            both = refs[place]
+            place += 1
+            first = both[:, pl.ds(pl.multiple_of(order * depth, depth), depth)]
+            second = both[:, pl.ds(pl.multiple_of((1 - order) * depth, depth), depth)]
+        else:
+            low, high = refs[place][...], refs[place + 1][...]
+            place += 2
+            first = jnp.where(order == 1, high, low)
+            second = jnp.where(order == 1, low, high)
+        rows = first.shape[0]
+        total = dot(first, keep_ref[0]) + dot(second, given_ref[0])
         out_ref[0, pair * rows : (pair + 1) * rows, :] = total.astype(out_ref.dtype)
 
 
-def project(pairs, flags, head, keep, peer, start, count, dtype):
-    rows, depth = pairs[0][0].shape
-    size = keep.shape[3]
-    number = len(pairs)
-    index = jnp.stack([head] + flags).astype(jnp.int32)
-    weight_spec = pl.BlockSpec((1, 1, depth, size), lambda i, idx: (idx[0], start + i, 0, 0))
+def project(index, whole, pairs, weight, given, size, start, count, dtype):
+    rows = whole[0].shape[0] if whole else pairs[0][0].shape[0]
+    depth = weight.shape[1]
+    number = len(whole) + len(pairs)
+    specs = []
+    for place in range(len(whole)):
+        if place == 0:
+            specs.append(pl.BlockSpec((rows, 2 * depth), lambda i, idx: (0, idx[0])))
+        else:
+            specs.append(pl.BlockSpec((rows, 2 * depth), lambda i, idx: (0, 0)))
+    specs += [pl.BlockSpec((rows, depth), lambda i, idx: (0, 0))] * (2 * len(pairs))
+    specs.append(pl.BlockSpec((1, depth, size), lambda i, idx: ((start + i) % 3, 0, idx[1])))
+    specs.append(pl.BlockSpec((1, depth, size), lambda i, idx: ((start + i) % 3, 0, idx[2])))
     return pl.pallas_call(
-        functools.partial(project_kernel, number),
+        functools.partial(project_kernel, number, len(whole)),
         out_shape=jax.ShapeDtypeStruct((count, number * rows, size), dtype),
         grid_spec=pltpu.PrefetchScalarGridSpec(
             num_scalar_prefetch=1,
             grid=(count,),
-            in_specs=[pl.BlockSpec((rows, depth), lambda i, idx: (0, 0))] * (2 * number) + [weight_spec] * 2,
+            in_specs=specs,
             out_specs=pl.BlockSpec((1, number * rows, size), lambda i, idx: (i, 0, 0)),
         ),
         compiler_params=params(),
@@ -142,7 +157,11 @@
             bytes_accessed=4 * (number * rows * depth + count * depth * size),
             transcendentals=0,
         ),
-    )(index, *[block for pair in pairs for block in pair], keep, peer)
+    )(index, *whole, *[block for pair in pairs for block in pair], weight, given)
+
+
+def project_own(index, whole, pairs, weight, given, size):
+    return project(index, whole, pairs, weight, given, size, 1, 3, F32)
 
 
 def split(value):
@@ -162,7 +181,7 @@
         keys = local_ref[0, here, :] + other[0, there, :].astype(F32)
         keys = rms_scale(keys).astype(BF16)
         values = (local_ref[1, here, :] + other[1, there, :].astype(F32)).astype(BF16)
-        rate = rate_ref[block]
+        rate = jnp.broadcast_to(rate_ref[block, pl.ds(index_ref[0], 1), :], (8, rows)).T[:, :1]
         scaled = (rate * values.astype(F32)).astype(BF16)
         gate = dot(keys, gate_w)
         up = dot(keys, up_w)
@@ -214,7 +233,15 @@
         grid_spec=pltpu.PrefetchScalarGridSpec(
             num_scalar_prefetch=1,
             grid=(1,),
-            in_specs=[whole(local), whole(near), whole(far), whole(rates), pick, pick, pick],
+            in_specs=[
+                pl.BlockSpec((2, total, size), lambda i, idx: (0, 0, 0)),
+                whole(near),
+                whole(far),
+                whole(rates),
+                pick,
+                pick,
+                pick,
+            ],
             out_specs=[pl.BlockSpec((size, hidden), lambda i, idx: (0, 0))] * 3,
             scratch_shapes=[pltpu.VMEM((3, size, hidden), F32)],
         ),
@@ -248,7 +275,7 @@
             num_scalar_prefetch=1,
             grid=(4,),
             in_specs=[
-                pl.BlockSpec((1, rows, size), lambda i, idx: (0, i, 0)),
+                pl.BlockSpec((1, rows, size), lambda i, idx: (2, i, 0)),
                 pl.BlockSpec((1, rows, size), lambda i, idx: (0, (i + 2) % 4, 0)),
                 pl.BlockSpec((1, 1, size), lambda i, idx: (idx[0], 0, 0)),
                 weight,
@@ -265,40 +292,63 @@
 
 
 def mix_kernel(index_ref, *refs):
-    blocks = refs[:28]
-    weight_ref, out_ref = refs[28:]
-    total = None
-    for offset in range(4):
-        for piece in range(4):
-            group = blocks[7 * piece : 7 * piece + 7]
-            if offset == 0:
-                block = group[0][...]
-            else:
-                block = jnp.where(index_ref[offset - 1] == 1, group[offset][...], group[3 + 4 - offset][...])
-            part = dot(block, weight_ref[index_ref[7 + offset], index_ref[3 + piece]])
-            total = part if total is None else total + part
-    out_ref[...] = total.astype(BF16)
-
-
-def mix(index, blocks, weight):
-    rows, size = blocks[0].shape
-    columns = weight.shape[3]
+    blocks = refs[:7]
+    own_a, own_b, peer_a, peer_b, x_ref, y_ref, x_peer, y_peer = refs[7:15]
+    place, seq = index_ref[0], index_ref[1]
+    held = refs[-1]
+    size = own_a.shape[0]
+
+    @pl.when(pl.program_id(0) == 0)
+    def _():
+        held[place] = blocks[0][...]
+        for offset in range(1, 4):
+            below = place >= offset
+            held[lax.rem(place - offset + 4, 4)] = jnp.where(below, blocks[offset][...], blocks[7 - offset][...])
+
+    total = refs[15][...] if len(refs) == 18 else None
+    out_ref = refs[-2]
+    for k, pair in enumerate([(own_a, own_b), (peer_a, peer_b), (x_ref, y_ref), (x_peer, y_peer)]):
+        owner = lax.bitwise_xor(seq, k)
+        for part in range(2):
+            column = part * size if k < 2 else pl.multiple_of(index_ref[2 + part] * size, size)
+            block = held[owner, :, pl.ds(column, size)]
+            term = dot(block, pair[part][...])
+            total = term if total is None else total + term
+    out_ref[...] = total.astype(out_ref.dtype)
+
+
+def mix(index, blocks, weights, before, dtype):
+    rows, double = blocks[0].shape
+    size = double // 2
+    own, peer, over_x, over_y, x_peer, y_peer = weights
+    columns = own.shape[1]
     tile = columns // 2
+    first = pl.BlockSpec((size, tile), lambda i, idx: (idx[4], i))
+    second = pl.BlockSpec((size, tile), lambda i, idx: (idx[5], i))
+    halved = pl.BlockSpec((size, tile), lambda i, idx: (idx[6], i))
+    slab = pl.BlockSpec((rows, tile), lambda i, idx: (0, i))
+    more = [] if before is None else [before]
     return pl.pallas_call(
         mix_kernel,
-        out_shape=jax.ShapeDtypeStruct((rows, columns), BF16),
+        out_shape=jax.ShapeDtypeStruct((rows, columns), dtype),
         grid_spec=pltpu.PrefetchScalarGridSpec(
             num_scalar_prefetch=1,
             grid=(2,),
-            in_specs=[pl.BlockSpec((rows, size), lambda i, idx: (0, 0))] * 28
-            + [pl.BlockSpec((4, 4, size, tile), lambda i, idx: (0, 0, 0, i))],
-            out_specs=pl.BlockSpec((rows, tile), lambda i, idx: (0, i)),
+            in_specs=[pl.BlockSpec((rows, double), lambda i, idx: (0, 0))] * 7
+            + [first, second, first, second, halved, halved, halved, halved]
+            + [slab] * len(more),
+            out_specs=slab,
+            scratch_shapes=[pltpu.VMEM((4, rows, double), BF16)],
         ),
         compiler_params=params(),
         cost_estimate=pl.CostEstimate(
-            flops=32 * rows * size * columns, bytes_accessed=32 * size * columns + 56 * rows * size, transcendentals=0
-        ),
-    )(index, *blocks, weight)
+            flops=16 * rows * size * columns, bytes_accessed=16 * size * columns + 28 * rows * size, transcendentals=0
+        ),
+    )(index, *blocks, own, own, peer, peer, over_x, over_y, x_peer, y_peer, *more)
+
+
+def after(value, *others):
+    return lax.optimization_barrier((value,) + others)[0]
 
 
 def chip_plan(tokens, qkv_weight, rate_weight, fast_gate, fast_up, fast_down, out_gain, out_weight):
@@ -306,10 +356,10 @@
     depth = qkv_weight.shape[0]
     size = fast_gate.shape[1]
     seq = lax.axis_index("seq")
-    chip, core = seq // 2, seq % 2
+    chip, core = seq >> 1, seq & 1
     place = lax.axis_index("head")
     side = lax.axis_index("groups")
-    odd = place % 2
+    odd = place & 1
     head = 2 * core + chip
 
     def across(array, bit):
@@ -318,69 +368,73 @@
     def hop(array, links):
         return lax.ppermute(array, "head", links)
 
-    def token_block(block):
-        return lax.dynamic_slice(tokens, (0, block * depth), (rows, depth))
-
-    direct = across(token_block(2 * (1 - chip) + odd), 2)
+    leaving = lax.dynamic_slice(tokens, (0, (2 * (1 - chip) + odd) * depth), (rows, depth))
+    direct = across(leaving, 2)
+    tokens, leaving = lax.optimization_barrier((tokens, leaving))
+    shared = lax.dynamic_slice(tokens, (0, chip * 2 * depth), (rows, 2 * depth))
+    peer = across(shared, 1)
+    weight = jnp.transpose(after(qkv_weight, shared), (1, 0, 2))
+    given = across(lax.dynamic_slice(weight, (0, 0, (1 - core) * 2 * size), (3, depth, 2 * size)), 1)
+
     handed = hop(direct, [(i, i ^ 1) for i in range(4)])
-    own = (token_block(2 * chip), token_block(2 * chip + 1))
-    peer = (across(own[0], 1), across(own[1], 1))
     direct_peer = across(direct, 1)
     handed_peer = across(handed, 1)
-    near = [own, peer]
     far = [(direct, handed), (direct_peer, handed_peer)]
 
-    def heads_of(half):
-        cut = lax.dynamic_slice(qkv_weight, (0, 0, half * 2 * size), (depth, 3, 2 * size))
-        return jnp.transpose(cut.reshape(depth, 3, 2, size), (2, 1, 0, 3))
-
-    given = across(heads_of(1 - core), 1)
-    keep = heads_of(core)
-
-    near_flags = [core, core]
-    far_flags = [core ^ odd, core ^ odd]
-    send_near = project(near, near_flags, 1 - chip, keep, given, 1, 2, BF16)
+    def order(which, *flags):
+        return jnp.stack([chip, 2 * core + which, which] + list(flags)).astype(jnp.int32)
+
+    far_flag = core ^ odd
+    send_near = project(order(1 - chip, core, core), [tokens, peer], [], weight, given, size, 1, 2, BF16)
     got_far = across(send_near, 2)
-    send_far = project(far, far_flags, 1 - chip, keep, given, 1, 2, BF16)
+    far = [tuple(after(block, send_near) for block in pair) for pair in far]
+    send_far = project(order(1 - chip, far_flag, far_flag), [], far, weight, given, size, 1, 2, BF16)
     got_near = across(send_far, 2)
-    send_query = project(near + far, near_flags + far_flags, 1 - chip, keep, given, 0, 1, BF16)
+    given = after(given, send_far)
+    everything = order(1 - chip, core, core, far_flag, far_flag)
+    send_query = project(everything, [tokens, peer], far, weight, given, size, 0, 1, BF16)
     got_query = across(send_query, 2)
-    local = project(near + far, near_flags + far_flags, chip, keep, given, 0, 3, F32)
+
+    half = out_weight.shape[0] // 2
+    out_held = after(out_weight, send_query)
+    out_half = lax.dynamic_slice(out_held, (side * half, 0), (half, out_held.shape[1]))
+    over_x = across(out_half, 2)
+    out_peer = across(out_held, 1)
 
     activity = lax.dot_general(rate_weight, tokens, (((0,), (1,)), ((), ())), preferred_element_type=F32)
     rates_own = jax.nn.softplus(activity)
     rates = jnp.stack([rates_own, across(rates_own, 1), across(rates_own, 2), across(rates_own, 3)])
-    rates = lax.dynamic_index_in_dim(rates, head, axis=1, keepdims=False)[:, :, None]
-
-    half = out_weight.shape[0] // 2
-    send_query, out_held = lax.optimization_barrier((send_query, out_weight))
-    over_x = across(lax.dynamic_slice(out_held, (side * half, 0), (half, out_held.shape[1])), 2)
+
+    given = after(given, out_half)
+    everything = order(chip, core, core, far_flag, far_flag)
+    local = project_own(everything, [tokens, peer], far, weight, given, size)
+
+    fresh = update(head, local, got_near, got_far, rates, fast_gate, fast_up, fast_down)
+    normed = read_out(head, local, got_query, out_gain.reshape(4, 1, size), *fresh)
+
+    over_x, _ = lax.optimization_barrier((over_x, normed))
     over_y = lax.ppermute(over_x, "groups", [(0, 1), (1, 0)])
-    low = jnp.where(side == 0, over_x, over_y)
-    high = jnp.where(side == 0, over_y, over_x)
-    beyond = jnp.concatenate([low, high])
-    gathered = jnp.stack([out_weight, across(out_weight, 1), beyond, across(beyond, 1)])
-    gathered = gathered.reshape(4, 4, size, out_weight.shape[1])
-
-    fresh = update(head, local[1:], got_near, got_far, rates, fast_gate, fast_up, fast_down)
-    normed = read_out(head, local[:1], got_query, out_gain.reshape(4, 1, size), *fresh)
-
-    pieces = [normed[0], across(normed[1], 1), across(normed[2], 2), across(normed[3], 3)]
+    weights = [out_weight, out_peer, over_x, over_y, across(over_x, 1), across(over_y, 1)]
+
     ups = [[(i, i + 1) for i in range(first, 3)] for first in range(3)]
     downs = [[(i + 1, i) for i in range(0, 3 - first)] for first in range(3)]
-    blocks = []
-    for piece in pieces:
+
+    def spread(piece):
         below, above = [piece], [piece]
         for step in range(3):
             below.append(hop(below[-1], ups[step]))
             above.append(hop(above[-1], downs[step]))
-        blocks += below + above[1:]
-    index = jnp.stack(
-        [place >= 1, place >= 2, place >= 3]
-        + [2 * (core ^ (k & 1)) + (chip ^ (k >> 1)) for k in range(4)]
-        + [seq ^ ((place - k) % 4) for k in range(4)]
-    ).astype(jnp.int32)
-    return mix(index, blocks, gathered)
+        return below + above[1:]
+
+    def mix_index(lead):
+        values = [place, seq, side ^ core, (1 - side) ^ core]
+        values += [2 * core + lead, 2 * (1 - core) + lead, lead]
+        return jnp.stack(values).astype(jnp.int32)
+
+    mine = spread(jnp.concatenate([normed[0], across(normed[1], 1)], axis=1))
+    theirs = spread(jnp.concatenate([across(normed[2], 2), across(normed[3], 3)], axis=1))
+    mixed = mix(mix_index(chip), mine, weights, None, F32)
+    return mix(mix_index(1 - chip), theirs, weights, mixed, BF16)
 
 
 def on_device(axis_sizes, tokens, qkv_weight, rate_weight, fast_gate, fast_up, fast_down, out_gain, out_weight):

time: 246 us -> 187 us (0.76)
  local copies, waits for them, and re-layouts: 40.1 us -> 17.8 us
  starting transfers between devices: 56.2 us -> 36 us
  waiting for transfers between devices: 80.6 us -> 69.7 us
  other arithmetic: 8.25 us -> 0.63 us
  Pallas kernels: 57.8 us -> 61.4 us
    ppermute x18, waiting for transfers between devices: 50.5 us -> 29.1 us  [across(): return lax.ppermute(array, 'seq', [(i, i ^ bit) for i in range(4)])]
    ppermute x25 -> x13, starting transfers between devices: 42.3 us -> 21.8 us  [hop(): return lax.ppermute(array, 'head', links)]
    ppermute x25 -> x13, waiting for transfers between devices: 30.1 us -> 39.9 us  [hop(): return lax.ppermute(array, 'head', links)]
    unnamed x58 -> x39, local copies, waits for them, and re-layouts: 13.2 us -> 4.83 us
    reshape x2 -> x0, local copies, waits for them, and re-layouts: 7.55 us -> none  [heads_of(): return jnp.transpose(cut.reshape(depth, 3, 2, size), (2, 1, 0, 3))]
    another operation x3 -> x1, other arithmetic: 7.91 us -> 0.61 us  [chip_plan(): jnp.stack([rates_own, across(rates_own, 1), across(rates_own, 2), across(...]
    slice x2 -> x0, local copies, waits for them, and re-layouts: 5.33 us -> none  [the longest x1 3.03 us: chip_plan(): local[1:]]
    pallas_call x1 -> x2, Pallas kernels: 7.34 us -> 11.2 us  [mix(): pl.pallas_call(mix_kernel, out_shape=jax.ShapeDtypeStruct((rows, columns)...]
  transfers between devices with their start and end apart: 44 -> 32, of which waited for: 12 -> 16; matrix products, arithmetic and copies ran while one was open for 12% -> 3% of each run, Pallas kernels for 18% -> 30%
where the time goes in v2:
time: 187 us; the launch traced here: 186 us
  waiting for transfers between devices  69.7 us (37%)
  Pallas kernels  61.4 us (33%)
  starting transfers between devices  36 us (19%)
  local copies, waits for them, and re-layouts  17.8 us (10%)
    ppermute x13, waiting for transfers between devices, hop(): return lax.ppermute(array, 'head', links)  39.9 us
    ppermute x18, waiting for transfers between devices, across(): return lax.ppermute(array, 'seq', [(i, i ^ bit) for i in range(4)])  29.1 us
    pallas_call x4, Pallas kernels, project(): pl.pallas_call(functools.partial(project_kernel, number, len(whole)), out...  23.1 us
    pallas_call x1, Pallas kernels, update(): pl.pallas_call(update_kernel, out_shape=[out] * 3, grid_spec=pltpu.Prefet...  22.2 us
    ppermute x13, starting transfers between devices, hop(): return lax.ppermute(array, 'head', links)  21.8 us
    ppermute x18, starting transfers between devices, across(): return lax.ppermute(array, 'seq', [(i, i ^ bit) for i in range(4)])  12.6 us
    pallas_call x2, Pallas kernels, mix(): pl.pallas_call(mix_kernel, out_shape=jax.ShapeDtypeStruct((rows, columns)...  11.2 us
    pallas_call x1, Pallas kernels, read_out(): pl.pallas_call(read_kernel, out_shape=jax.ShapeDtypeStruct((4, rows, size...  4.96 us
  transfers between devices with their start and end apart: 32, of which 16 were waited for; matrix products, arithmetic and copies ran while one was open for 3% of the time, Pallas kernels for 30%

profile of v2, /device:TPU:0, one launch (start us, length us, event | category | flops | bytes accessed | tf_op | source)
XLA Modules:
  0.0 186.5 jit_solution(2754572834742366900)
XLA Ops:
  0.0 1.9 %constant_dynamic-slice_fusion.2 = bf16[256,1024]{1,0:T(8,128)(2,1)} fusion(bf16[256,4096]{1,0:T(8,128)(2,1)} %refs_0_.2, s32[]{:T(128)S(6)} %select_n.16), kind=kLoop, calls=%fused_computation.13 | loop fusion | bytes 1048580 | tf_op jit(solution)/shard_map/dynamic_slice | solution.py:371
  1.9 2.3 %constant_dynamic-slice_fusion.1 = bf16[256,2048]{1,0:T(8,128)(2,1)} fusion(bf16[256,4096]{1,0:T(8,128)(2,1)} %refs_0_.2, s32[]{:T(128)S(6)} %select_n.17), kind=kLoop, calls=%fused_computation.12 | loop fusion | bytes 2097156 | tf_op jit(solution)/shard_map/dynamic_slice | solution.py:374
  4.2 3.9 %dynamic-slice_bitcast_fusion = bf16[3,1024,512]{2,1,0:T(8,128)(2,1)} fusion(bf16[1024,3,1024]{2,0,1:T(8,128)(2,1)} %param.9, s32[]{:T(128)S(6)} %select_n.18), kind=kLoop, calls=%fused_computation | loop fusion | bytes 6291460 | tf_op jit(solution)/shard_map/dynamic_slice | solution.py:377
  8.5 2.5 %collective-permute-start.1 = (bf16[256,1024]{1,0:T(8,128)(2,1)S(1)}, bf16[256,1024]{1,0:T(8,128)(2,1)}, u32[]{:S(2)}, u32[]{:S(2)}) collective-permute-start(bf16[256,1024]{1,0:T(8,128)(2,1)S(1)} %copy-done.8), channel_id=1, source_target_pairs={{0,8},{4,12},{8,0},{12,4},{1,9},{5,13},{9,1},{13,5},{2,10},{6,14},... | collective-permute-start | bytes 1572872 | tf_op jit(solution)/shard_map/ppermute | solution.py:366
  11.2 12.5 %collective-permute-done.1.refs_0_.refs_2_ = bf16[256,1024]{1,0:T(8,128)(2,1)} collective-permute-done((bf16[256,1024]{1,0:T(8,128)(2,1)S(1)}, bf16[256,1024]{1,0:T(8,128)(2,1)}, u32[]{:S(2)}, u32[]{:S(2)}) %collective-permute-start.1) | collective-permute-done | bytes 524320 | tf_op jit(solution)/shard_map/ppermute | solution.py:366
  23.7 1.8 collective-permute-start.3
  25.5 12.2 %collective-permute-done.3.refs_1_.refs_3_ = bf16[256,1024]{1,0:T(8,128)(2,1)} collective-permute-done((bf16[256,1024]{1,0:T(8,128)(2,1)}, bf16[256,1024]{1,0:T(8,128)(2,1)}, u32[]{:S(2)}, u32[]{:S(2)}) %collective-permute-start.3) | collective-permute-done | bytes 524320 | tf_op jit(solution)/shard_map/ppermute | solution.py:369
  37.8 0.7 compare_select_fusion
  38.4 1.7 collective-permute-start.11
  40.2 1.4 collective-permute-done.11
  41.5 1.5 collective-permute-start.10
  43.1 2.1 %collective-permute-done.10 = f32[4,256]{1,0:T(4,128)S(1)} collective-permute-done((f32[4,256]{1,0:T(4,128)S(1)}, f32[4,256]{1,0:T(4,128)S(1)}, u32[]{:S(2)}, u32[]{:S(2)}) %collective-permute-start.10) | collective-permute-done | bytes 4128 | tf_op jit(solution)/shard_map/ppermute | solution.py:366
  45.2 0.6 stack.105.index_ref
  45.8 0.6 stack.106.index_ref
  46.4 0.7 stack.107.index_ref
  47.1 0.6 stack.104.index_ref
  47.7 0.6 pad_maximum_fusion.1.rate_ref
  48.3 1.7 copy-done.1
  50.0 4.7 %shard_map.82 = bf16[2,512,256]{2,1,0:T(8,128)(2,1)} custom-call(s32[5]{0:T(128)} %stack.105.index_ref, bf16[256,4096]{1,0:T(8,128)(2,1)} %refs_0_.2, bf16[256,2048]{1,0:T(8,128)(2,1)} %collective-permute-done.refs_1_, bf16[3,1024,1024]{2,1,0:T(8,128)(2,1)} %bitcast.34, bf16[3,1024,512]{2,1,0:T(8,128)(2,1)} %copy-done.1), custom_call_target="tpu_custom_call" | custom-call | flops 1073741824 | bytes 4194304 | tf_op jit(solution)/shard_map/pallas_call | solution.py:145
  54.7 1.5 collective-permute-start.8
  56.3 4.8 %shard_map.83 = bf16[2,512,256]{2,1,0:T(8,128)(2,1)} custom-call(s32[5]{0:T(128)} %stack.106.index_ref, bf16[256,1024]{1,0:T(8,128)(2,1)} %collective-permute-done.1.refs_0_.refs_2_, bf16[256,1024]{1,0:T(8,128)(2,1)} %collective-permute-done.3.refs_1_.refs_3_, bf16[256,1024]{1,0:T(8,128)(2,1)} %collective-permute-done.4.refs_2_.refs_4_, ...), custom_call_target="tpu_custom_call" | custom-call | flops 1073741824 | bytes 4194304 | tf_op jit(solution)/shard_map/pallas_call | solution.py:145
  61.1 0.5 collective-permute-start.7
  61.5 5.3 %shard_map.84 = bf16[1,1024,256]{2,1,0:T(8,128)(2,1)} custom-call(s32[7]{0:T(128)} %stack.107.index_ref, bf16[256,4096]{1,0:T(8,128)(2,1)} %refs_0_.2, bf16[256,2048]{1,0:T(8,128)(2,1)} %collective-permute-done.refs_1_, bf16[256,1024]{1,0:T(8,128)(2,1)} %collective-permute-done.1.refs_0_.refs_2_, bf16[256,1024]{1,0:T(8,128)(2,1)} %collective-permute-done.3.refs_1_.refs_3_, ...), custom_call_target="tpu_custom_call" | custom-call | flops 1073741824 | bytes 5242880 | tf_op jit(solution)/shard_map/pallas_call | solution.py:145
  66.8 1.4 collective-permute-start.6
  68.3 0.7 collective-permute-start.21
  69.0 8.3 %shard_map.85.local_ref = f32[3,1024,256]{2,1,0:T(8,128)} custom-call(s32[7]{0:T(128)} %stack.104.index_ref, bf16[256,4096]{1,0:T(8,128)(2,1)} %refs_0_.2, bf16[256,2048]{1,0:T(8,128)(2,1)} %collective-permute-done.refs_1_, bf16[256,1024]{1,0:T(8,128)(2,1)} %collective-permute-done.1.refs_0_.refs_2_, ...), custom_call_target="tpu_custom_call" | custom-call | flops 3221225472 | bytes 7340032 | tf_op jit(solution)/shard_map/pallas_call | solution.py:145
  77.3 3.6 %collective-permute-done.7.near_ref = bf16[2,512,256]{2,1,0:T(8,128)(2,1)S(1)} collective-permute-done((bf16[2,512,256]{2,1,0:T(8,128)(2,1)}, bf16[2,512,256]{2,1,0:T(8,128)(2,1)S(1)}, u32[]{:S(2)}, u32[]{:S(2)}) %collective-permute-start.7) | collective-permute-done | bytes 524320 | tf_op jit(solution)/shard_map/ppermute | solution.py:366
  80.9 0.8 copy-done.18
  81.7 0.8 copy-done.17
  82.5 22.2 %shard_map.86 = (bf16[256,512]{1,0:T(8,128)(2,1)}, bf16[256,512]{1,0:T(8,128)(2,1)}, bf16[256,512]{1,0:T(8,128)(2,1)}) custom-call(s32[1]{0:T(128)} %bitcast.7.index_ref, f32[3,1024,256]{2,1,0:T(8,128)} %shard_map.85.local_ref, bf16[2,512,256]{2,1,0:T(8,128)(2,1)} %copy-done.18, bf16[2,512,256]{2,1,0:T(8,128)(2,1)} %copy-done.17, ...), custom_call_target="tpu_custom_call" | custom-call | flops 14763950080 | bytes 4718592 | tf_op jit(solution)/shard_map/pallas_call | solution.py:230
  104.7 0.8 copy-done.7
  105.5 5.0 %shard_map.87 = bf16[4,256,256]{2,1,0:T(8,128)(2,1)} custom-call(s32[1]{0:T(128)} %bitcast.7.index_ref, f32[3,1024,256]{2,1,0:T(8,128)} %shard_map.85.local_ref, bf16[1,1024,256]{2,1,0:T(8,128)(2,1)} %copy-done.7, f32[4,1,256]{2,1,0:T(1,128)} %bitcast.42, bf16[256,512]{1,0:T(8,128)(2,1)} %get-tuple-element.27.gate_ref, ...), custom_call_target="tpu_custom_call" | custom-call | flops 805306368 | bytes 2097152 | tf_op jit(solution)/shard_map/pallas_call | solution.py:271
  110.5 3.8 %collective-permute-done.21.refs_11_ = bf16[512,1024]{1,0:T(8,128)(2,1)S(1)} collective-permute-done((bf16[512,1024]{1,0:T(8,128)(2,1)S(1)}, bf16[512,1024]{1,0:T(8,128)(2,1)S(1)}, u32[]{:S(2)}, u32[]{:S(2)}) %collective-permute-start.21) | collective-permute-done | bytes 1048608 | tf_op jit(solution)/shard_map/ppermute | solution.py:366
  114.2 1.6 collective-permute-start.22
  115.8 1.1 slice_bitcast_fusion.1
  116.9 1.6 collective-permute-start.12
  118.5 4.0 %collective-permute-done.12 = bf16[256,256]{1,0:T(8,128)(2,1)S(1)} collective-permute-done((bf16[256,256]{1,0:T(8,128)(2,1)S(1)}, bf16[256,256]{1,0:T(8,128)(2,1)S(1)}, u32[]{:S(2)}, u32[]{:S(2)}) %collective-permute-start.12) | collective-permute-done | bytes 131104 | tf_op jit(solution)/shard_map/ppermute | solution.py:366
  122.5 1.8 collective-permute-done.13
  124.3 3.5 %collective-permute-start.14 = (bf16[256,512]{1,0:T(8,128)(2,1)S(1)}, bf16[256,512]{1,0:T(8,128)(2,1)S(1)}, u32[]{:S(2)}, u32[]{:S(2)}) collective-permute-start(bf16[256,512]{1,0:T(8,128)(2,1)S(1)} %constant_dynamic-update-slice_fusion.refs_0_), channel_id=1, source_target_pairs={{0,1},{1,2},{2,3},{4,5},{5,6},{6,7},{8,9},{9,10},{10,11},{12,13},{... | collective-permute-start | bytes 786440 | tf_op jit(solution)/shard_map/ppermute | solution.py:369
  127.8 0.5 collective-permute-start.25
  128.3 1.3 collective-permute-start.17
  129.6 4.7 %collective-permute-start.26 = (bf16[256,512]{1,0:T(8,128)(2,1)S(1)}, bf16[256,512]{1,0:T(8,128)(2,1)S(1)}, u32[]{:S(2)}, u32[]{:S(2)}) collective-permute-start(bf16[256,512]{1,0:T(8,128)(2,1)S(1)} %pad_maximum_fusion.refs_0_), channel_id=1, source_target_pairs={{0,1},{1,2},{2,3},{4,5},{5,6},{6,7},{8,9},{9,10},{10,11},{12,13},{... | collective-permute-start | bytes 786440 | tf_op jit(solution)/shard_map/ppermute | solution.py:369
  134.4 1.3 collective-permute-start.29
  135.7 2.7 %collective-permute-done.17.refs_4_ = bf16[256,512]{1,0:T(8,128)(2,1)S(1)} collective-permute-done((bf16[256,512]{1,0:T(8,128)(2,1)S(1)}, bf16[256,512]{1,0:T(8,128)(2,1)S(1)}, u32[]{:S(2)}, u32[]{:S(2)}) %collective-permute-start.17) | collective-permute-done | bytes 262176 | tf_op jit(solution)/shard_map/ppermute | solution.py:369
  138.5 0.7 collective-permute-done.22.refs_12_
  139.1 0.7 collective-permute-done.26.refs_1_
  139.9 1.4 collective-permute-start.15
  141.2 3.8 %collective-permute-done.29.refs_4_ = bf16[256,512]{1,0:T(8,128)(2,1)S(1)} collective-permute-done((bf16[256,512]{1,0:T(8,128)(2,1)S(1)}, bf16[256,512]{1,0:T(8,128)(2,1)S(1)}, u32[]{:S(2)}, u32[]{:S(2)}) %collective-permute-start.29) | collective-permute-done | bytes 262176 | tf_op jit(solution)/shard_map/ppermute | solution.py:369
  145.0 1.3 collective-permute-start.18
  146.4 0.7 collective-permute-start.27
  147.0 7.6 %collective-permute-done.18.refs_5_ = bf16[256,512]{1,0:T(8,128)(2,1)} collective-permute-done((bf16[256,512]{1,0:T(8,128)(2,1)S(1)}, bf16[256,512]{1,0:T(8,128)(2,1)}, u32[]{:S(2)}, u32[]{:S(2)}) %collective-permute-start.18) | collective-permute-done | bytes 262176 | tf_op jit(solution)/shard_map/ppermute | solution.py:369
  154.7 1.3 collective-permute-start.30
  156.0 0.7 collective-permute-start.28
  156.7 6.6 %collective-permute-done.30.refs_5_ = bf16[256,512]{1,0:T(8,128)(2,1)S(1)} collective-permute-done((bf16[256,512]{1,0:T(8,128)(2,1)S(1)}, bf16[256,512]{1,0:T(8,128)(2,1)S(1)}, u32[]{:S(2)}, u32[]{:S(2)}) %collective-permute-start.30) | collective-permute-done | bytes 262176 | tf_op jit(solution)/shard_map/ppermute | solution.py:369
  163.3 1.3 collective-permute-start.31
  164.6 1.4 collective-permute-start.16
  166.0 5.6 %collective-permute-done.31.refs_6_ = bf16[256,512]{1,0:T(8,128)(2,1)S(1)} collective-permute-done((bf16[256,512]{1,0:T(8,128)(2,1)S(1)}, bf16[256,512]{1,0:T(8,128)(2,1)S(1)}, u32[]{:S(2)}, u32[]{:S(2)}) %collective-permute-start.31) | collective-permute-done | bytes 262176 | tf_op jit(solution)/shard_map/ppermute | solution.py:369
  171.6 0.7 copy-done.16
  172.3 1.3 collective-permute-start.19
  173.6 0.6 stack.100.index_ref
  174.1 0.6 stack.114.index_ref
  174.8 5.5 %shard_map.88.refs_15_ = f32[256,1024]{1,0:T(8,128)} custom-call(s32[7]{0:T(128)} %stack.114.index_ref, bf16[256,512]{1,0:T(8,128)(2,1)} %copy-done.5, bf16[256,512]{1,0:T(8,128)(2,1)} %copy-done.11, bf16[256,512]{1,0:T(8,128)(2,1)} %copy-done.13, bf16[256,512]{1,0:T(8,128)(2,1)} %copy-done.15, bf16[256,512]{1,0:T(8,128)(2,1)} %copy-done.12, ...), custom_call_target="tpu_custom_call" | custom-call | flops 1073741824 | bytes 6029312 | tf_op jit(solution)/shard_map/pallas_call | solution.py:331
  180.3 0.5 collective-permute-done.19.refs_6_
  180.8 5.6 %shard_map.89 = bf16[256,1024]{1,0:T(8,128)(2,1)} custom-call(s32[7]{0:T(128)} %stack.100.index_ref, bf16[256,512]{1,0:T(8,128)(2,1)} %copy-done.6, bf16[256,512]{1,0:T(8,128)(2,1)} %copy-done.9, bf16[256,512]{1,0:T(8,128)(2,1)} %collective-permute-done.15.refs_2_, bf16[256,512]{1,0:T(8,128)(2,1)} %collective-permute-done.16.refs_3_, ...), custom_call_target="tpu_custom_call" | custom-call | flops 1073741824 | bytes 6029312 | tf_op jit(solution)/shard_map/pallas_call | solution.py:331
  (62 shorter events, 0.9 us)
Async XLA Ops:
  0.0 37.8 %copy-start = (bf16[4096,4]{0,1:T(4,128)(2,1)S(1)}, bf16[4096,4]{0,1:T(4,128)(2,1)}, u32[]{:S(2)}) copy-start(bf16[4096,4]{0,1:T(4,128)(2,1)} %param.10) | copy-start | bytes 98308
  4.2 4.3 %copy-start.8 = (bf16[256,1024]{1,0:T(8,128)(2,1)S(1)}, bf16[256,1024]{1,0:T(8,128)(2,1)}, u32[]{:S(2)}) copy-start(bf16[256,1024]{1,0:T(8,128)(2,1)} %constant_dynamic-slice_fusion.2) | copy-start | bytes 1572868
  4.2 33.6 %copy-start.2 = (bf16[256,4096]{1,0:T(8,128)(2,1)S(1)}, bf16[256,4096]{1,0:T(8,128)(2,1)}, u32[]{:S(2)}) copy-start(bf16[256,4096]{1,0:T(8,128)(2,1)} %refs_0_.2) | copy-start | bytes 6291460
  8.0 40.3 %collective-permute-start.2 = (bf16[3,1024,512]{2,1,0:T(8,128)(2,1)}, bf16[3,1024,512]{2,1,0:T(8,128)(2,1)S(1)}, u32[]{:S(2)}, u32[]{:S(2)}) collective-permute-start(bf16[3,1024,512]{2,1,0:T(8,128)(2,1)} %dynamic-slice_bitcast_fusion), channel_id=1, source_target_pairs={{0,4},{4,0},{8,12},{12,8},{1,5},{5,1},{9,13},{13,9},{2,6},{6,2},{1... | collective-permute-start | bytes 9437192 | tf_op jit(solution)/shard_map/ppermute | solution.py:366
  8.5 15.2 %collective-permute-start.1 = (bf16[256,1024]{1,0:T(8,128)(2,1)S(1)}, bf16[256,1024]{1,0:T(8,128)(2,1)}, u32[]{:S(2)}, u32[]{:S(2)}) collective-permute-start(bf16[256,1024]{1,0:T(8,128)(2,1)S(1)} %copy-done.8), channel_id=1, source_target_pairs={{0,8},{4,12},{8,0},{12,4},{1,9},{5,13},{9,1},{13,5},{2,10},{6,14},... | collective-permute-start | bytes 1572872 | tf_op jit(solution)/shard_map/ppermute | solution.py:366
  11.0 37.3 %collective-permute-start = (bf16[256,2048]{1,0:T(8,128)(2,1)}, bf16[256,2048]{1,0:T(8,128)(2,1)}, u32[]{:S(2)}, u32[]{:S(2)}) collective-permute-start(bf16[256,2048]{1,0:T(8,128)(2,1)} %constant_dynamic-slice_fusion.1), channel_id=1, source_target_pairs={{0,4},{4,0},{8,12},{12,8},{1,5},{5,1},{9,13},{13,9},{2,6},{6,2},{1... | collective-permute-start | bytes 3145736 | tf_op jit(solution)/shard_map/ppermute | solution.py:366
  23.7 14.1 %collective-permute-start.3 = (bf16[256,1024]{1,0:T(8,128)(2,1)}, bf16[256,1024]{1,0:T(8,128)(2,1)}, u32[]{:S(2)}, u32[]{:S(2)}) collective-permute-start(bf16[256,1024]{1,0:T(8,128)(2,1)} %collective-permute-done.1.refs_0_.refs_2_), channel_id=1, source_target_pairs={{0,1},{1,0},{2,3},{3,2},{4,5},{5,4},{6,7},{7,6},{8,9},{9,8},{10,11... | collective-permute-start | bytes 1572872 | tf_op jit(solution)/shard_map/ppermute | solution.py:369
  25.5 30.8 %collective-permute-start.4 = (bf16[256,1024]{1,0:T(8,128)(2,1)}, bf16[256,1024]{1,0:T(8,128)(2,1)}, u32[]{:S(2)}, u32[]{:S(2)}) collective-permute-start(bf16[256,1024]{1,0:T(8,128)(2,1)} %collective-permute-done.1.refs_0_.refs_2_), channel_id=1, source_target_pairs={{0,4},{4,0},{8,12},{12,8},{1,5},{5,1},{9,13},{13,9},{2,6},{6,2},{1... | collective-permute-start | bytes 1572872 | tf_op jit(solution)/shard_map/ppermute | solution.py:366
  37.8 18.5 %collective-permute-start.5 = (bf16[256,1024]{1,0:T(8,128)(2,1)}, bf16[256,1024]{1,0:T(8,128)(2,1)}, u32[]{:S(2)}, u32[]{:S(2)}) collective-permute-start(bf16[256,1024]{1,0:T(8,128)(2,1)} %collective-permute-done.3.refs_1_.refs_3_), channel_id=1, source_target_pairs={{0,4},{4,0},{8,12},{12,8},{1,5},{5,1},{9,13},{13,9},{2,6},{6,2},{1... | collective-permute-start | bytes 1572872 | tf_op jit(solution)/shard_map/ppermute | solution.py:366
  38.4 3.1 %collective-permute-start.11 = (f32[4,256]{1,0:T(4,128)S(1)}, f32[4,256]{1,0:T(4,128)S(1)}, u32[]{:S(2)}, u32[]{:S(2)}) collective-permute-start(f32[4,256]{1,0:T(4,128)S(1)} %compare_select_fusion), channel_id=1, source_target_pairs={{0,12},{4,8},{8,4},{12,0},{1,13},{5,9},{9,5},{13,1},{2,14},{6,10},... | collective-permute-start | bytes 12296 | tf_op jit(solution)/shard_map/ppermute | solution.py:366
  41.5 3.6 %collective-permute-start.10 = (f32[4,256]{1,0:T(4,128)S(1)}, f32[4,256]{1,0:T(4,128)S(1)}, u32[]{:S(2)}, u32[]{:S(2)}) collective-permute-start(f32[4,256]{1,0:T(4,128)S(1)} %compare_select_fusion), channel_id=1, source_target_pairs={{0,8},{4,12},{8,0},{12,4},{1,9},{5,13},{9,1},{13,5},{2,10},{6,14},... | collective-permute-start | bytes 12296 | tf_op jit(solution)/shard_map/ppermute | solution.py:366
  45.2 2.5 %collective-permute-start.9 = (f32[4,256]{1,0:T(4,128)S(1)}, f32[4,256]{1,0:T(4,128)S(1)}, u32[]{:S(2)}, u32[]{:S(2)}) collective-permute-start(f32[4,256]{1,0:T(4,128)S(1)} %compare_select_fusion), channel_id=1, source_target_pairs={{0,4},{4,0},{8,12},{12,8},{1,5},{5,1},{9,13},{13,9},{2,6},{6,2},{1... | collective-permute-start | bytes 12296 | tf_op jit(solution)/shard_map/ppermute | solution.py:366
  48.3 1.7 copy-start.1
  54.7 26.2 %collective-permute-start.8 = (bf16[2,512,256]{2,1,0:T(8,128)(2,1)}, bf16[2,512,256]{2,1,0:T(8,128)(2,1)S(1)}, u32[]{:S(2)}, u32[]{:S(2)}) collective-permute-start(bf16[2,512,256]{2,1,0:T(8,128)(2,1)} %shard_map.82), channel_id=1, source_target_pairs={{0,8},{4,12},{8,0},{12,4},{1,9},{5,13},{9,1},{13,5},{2,10},{6,14},... | collective-permute-start | bytes 1572872 | tf_op jit(solution)/shard_map/ppermute | solution.py:366
  61.1 7.2 %copy-start.3 = (bf16[1024,1024]{1,0:T(8,128)(2,1)S(1)}, bf16[1024,1024]{1,0:T(8,128)(2,1)}, u32[]{:S(2)}) copy-start(bf16[1024,1024]{1,0:T(8,128)(2,1)} %refs_8_.3) | copy-start | bytes 6291460
  61.1 19.8 %collective-permute-start.7 = (bf16[2,512,256]{2,1,0:T(8,128)(2,1)}, bf16[2,512,256]{2,1,0:T(8,128)(2,1)S(1)}, u32[]{:S(2)}, u32[]{:S(2)}) collective-permute-start(bf16[2,512,256]{2,1,0:T(8,128)(2,1)} %shard_map.83), channel_id=1, source_target_pairs={{0,8},{4,12},{8,0},{12,4},{1,9},{5,13},{9,1},{13,5},{2,10},{6,14},... | collective-permute-start | bytes 1572872 | tf_op jit(solution)/shard_map/ppermute | solution.py:366
  66.8 37.9 %collective-permute-start.6 = (bf16[1,1024,256]{2,1,0:T(8,128)(2,1)}, bf16[1,1024,256]{2,1,0:T(8,128)(2,1)S(1)}, u32[]{:S(2)}, u32[]{:S(2)}) collective-permute-start(bf16[1,1024,256]{2,1,0:T(8,128)(2,1)} %shard_map.84), channel_id=1, source_target_pairs={{0,8},{4,12},{8,0},{12,4},{1,9},{5,13},{9,1},{13,5},{2,10},{6,14},... | collective-permute-start | bytes 1572872 | tf_op jit(solution)/shard_map/ppermute | solution.py:366
  68.3 106.5 %collective-permute-start.20 = (bf16[1024,1024]{1,0:T(8,128)(2,1)S(1)}, bf16[1024,1024]{1,0:T(8,128)(2,1)}, u32[]{:S(2)}, u32[]{:S(2)}) collective-permute-start(bf16[1024,1024]{1,0:T(8,128)(2,1)S(1)} %copy-done.3), channel_id=1, source_target_pairs={{0,4},{4,0},{8,12},{12,8},{1,5},{5,1},{9,13},{13,9},{2,6},{6,2},{1... | collective-permute-start | bytes 6291464 | tf_op jit(solution)/shard_map/ppermute | solution.py:366
  68.3 45.9 %collective-permute-start.21 = (bf16[512,1024]{1,0:T(8,128)(2,1)S(1)}, bf16[512,1024]{1,0:T(8,128)(2,1)S(1)}, u32[]{:S(2)}, u32[]{:S(2)}) collective-permute-start(bf16[512,1024]{1,0:T(8,128)(2,1)S(1)} %constant_dynamic-slice_fusion), channel_id=1, source_target_pairs={{0,8},{4,12},{8,0},{12,4},{1,9},{5,13},{9,1},{13,5},{2,10},{6,14},... | collective-permute-start | bytes 3145736 | tf_op jit(solution)/shard_map/ppermute | solution.py:366
  80.9 0.8 copy-start.18
  81.7 0.8 copy-start.17
  104.7 0.8 copy-start.7
  114.2 60.5 %copy-start.4 = (bf16[512,1024]{1,0:T(8,128)(2,1)}, bf16[512,1024]{1,0:T(8,128)(2,1)S(1)}, u32[]{:S(2)}) copy-start(bf16[512,1024]{1,0:T(8,128)(2,1)S(1)} %collective-permute-done.21.refs_11_) | copy-start | bytes 3145732
  114.2 24.9 %collective-permute-start.22 = (bf16[512,1024]{1,0:T(8,128)(2,1)S(1)}, bf16[512,1024]{1,0:T(8,128)(2,1)}, u32[]{:S(2)}, u32[]{:S(2)}) collective-permute-start(bf16[512,1024]{1,0:T(8,128)(2,1)S(1)} %collective-permute-done.21.refs_11_), channel_id=1, source_target_pairs={{0,16},{16,0},{1,17},{17,1},{2,18},{18,2},{3,19},{19,3},{4,20},{20... | collective-permute-start | bytes 3145736 | tf_op jit(solution)/shard_map/ppermute | solution.py:416
  116.9 5.5 %collective-permute-start.12 = (bf16[256,256]{1,0:T(8,128)(2,1)S(1)}, bf16[256,256]{1,0:T(8,128)(2,1)S(1)}, u32[]{:S(2)}, u32[]{:S(2)}) collective-permute-start(bf16[256,256]{1,0:T(8,128)(2,1)S(1)} %get-tuple-element.34), channel_id=1, source_target_pairs={{0,8},{4,12},{8,0},{12,4},{1,9},{5,13},{9,1},{13,5},{2,10},{6,14},... | collective-permute-start | bytes 393224 | tf_op jit(solution)/shard_map/ppermute | solution.py:366
  118.5 5.8 %collective-permute-start.13 = (bf16[256,256]{1,0:T(8,128)(2,1)S(1)}, bf16[256,256]{1,0:T(8,128)(2,1)S(1)}, u32[]{:S(2)}, u32[]{:S(2)}) collective-permute-start(bf16[256,256]{1,0:T(8,128)(2,1)S(1)} %get-tuple-element.33), channel_id=1, source_target_pairs={{0,12},{4,8},{8,4},{12,0},{1,13},{5,9},{9,5},{13,1},{2,14},{6,10},... | collective-permute-start | bytes 393224 | tf_op jit(solution)/shard_map/ppermute | solution.py:366
  124.3 20.8 %copy-start.6 = (bf16[256,512]{1,0:T(8,128)(2,1)}, bf16[256,512]{1,0:T(8,128)(2,1)S(1)}, u32[]{:S(2)}) copy-start(bf16[256,512]{1,0:T(8,128)(2,1)S(1)} %constant_dynamic-update-slice_fusion.refs_0_) | copy-start | bytes 786436
  124.3 10.1 %collective-permute-start.14 = (bf16[256,512]{1,0:T(8,128)(2,1)S(1)}, bf16[256,512]{1,0:T(8,128)(2,1)S(1)}, u32[]{:S(2)}, u32[]{:S(2)}) collective-permute-start(bf16[256,512]{1,0:T(8,128)(2,1)S(1)} %constant_dynamic-update-slice_fusion.refs_0_), channel_id=1, source_target_pairs={{0,1},{1,2},{2,3},{4,5},{5,6},{6,7},{8,9},{9,10},{10,11},{12,13},{... | collective-permute-start | bytes 786440 | tf_op jit(solution)/shard_map/ppermute | solution.py:369
  127.8 1.8 collective-permute-start.25
  128.3 10.2 %collective-permute-start.17 = (bf16[256,512]{1,0:T(8,128)(2,1)S(1)}, bf16[256,512]{1,0:T(8,128)(2,1)S(1)}, u32[]{:S(2)}, u32[]{:S(2)}) collective-permute-start(bf16[256,512]{1,0:T(8,128)(2,1)S(1)} %constant_dynamic-update-slice_fusion.refs_0_), channel_id=1, source_target_pairs={{1,0},{2,1},{3,2},{5,4},{6,5},{7,6},{9,8},{10,9},{11,10},{13,12},{... | collective-permute-start | bytes 786440 | tf_op jit(solution)/shard_map/ppermute | solution.py:369
  129.6 45.1 %copy-start.5 = (bf16[256,512]{1,0:T(8,128)(2,1)}, bf16[256,512]{1,0:T(8,128)(2,1)S(1)}, u32[]{:S(2)}) copy-start(bf16[256,512]{1,0:T(8,128)(2,1)S(1)} %pad_maximum_fusion.refs_0_) | copy-start | bytes 786436
  129.6 10.2 %collective-permute-start.26 = (bf16[256,512]{1,0:T(8,128)(2,1)S(1)}, bf16[256,512]{1,0:T(8,128)(2,1)S(1)}, u32[]{:S(2)}, u32[]{:S(2)}) collective-permute-start(bf16[256,512]{1,0:T(8,128)(2,1)S(1)} %pad_maximum_fusion.refs_0_), channel_id=1, source_target_pairs={{0,1},{1,2},{2,3},{4,5},{5,6},{6,7},{8,9},{9,10},{10,11},{12,13},{... | collective-permute-start | bytes 786440 | tf_op jit(solution)/shard_map/ppermute | solution.py:369
  134.4 11.9 %copy-start.9 = (bf16[256,512]{1,0:T(8,128)(2,1)}, bf16[256,512]{1,0:T(8,128)(2,1)S(1)}, u32[]{:S(2)}) copy-start(bf16[256,512]{1,0:T(8,128)(2,1)S(1)} %collective-permute-done.14.refs_1_) | copy-start | bytes 786436
  134.4 10.6 %collective-permute-start.29 = (bf16[256,512]{1,0:T(8,128)(2,1)S(1)}, bf16[256,512]{1,0:T(8,128)(2,1)S(1)}, u32[]{:S(2)}, u32[]{:S(2)}) collective-permute-start(bf16[256,512]{1,0:T(8,128)(2,1)S(1)} %pad_maximum_fusion.refs_0_), channel_id=1, source_target_pairs={{1,0},{2,1},{3,2},{5,4},{6,5},{7,6},{9,8},{10,9},{11,10},{13,12},{... | collective-permute-start | bytes 786440 | tf_op jit(solution)/shard_map/ppermute | solution.py:369
  138.5 7.9 %copy-start.10 = (bf16[256,512]{1,0:T(8,128)(2,1)}, bf16[256,512]{1,0:T(8,128)(2,1)S(1)}, u32[]{:S(2)}) copy-start(bf16[256,512]{1,0:T(8,128)(2,1)S(1)} %collective-permute-done.17.refs_4_) | copy-start | bytes 786436
  138.5 36.3 %collective-permute-start.23 = (bf16[512,1024]{1,0:T(8,128)(2,1)S(1)}, bf16[512,1024]{1,0:T(8,128)(2,1)}, u32[]{:S(2)}, u32[]{:S(2)}) collective-permute-start(bf16[512,1024]{1,0:T(8,128)(2,1)S(1)} %collective-permute-done.21.refs_11_), channel_id=1, source_target_pairs={{0,4},{4,0},{8,12},{12,8},{1,5},{5,1},{9,13},{13,9},{2,6},{6,2},{1... | collective-permute-start | bytes 3145736 | tf_op jit(solution)/shard_map/ppermute | solution.py:366
  139.1 35.6 %collective-permute-start.24 = (bf16[512,1024]{1,0:T(8,128)(2,1)}, bf16[512,1024]{1,0:T(8,128)(2,1)}, u32[]{:S(2)}, u32[]{:S(2)}) collective-permute-start(bf16[512,1024]{1,0:T(8,128)(2,1)} %collective-permute-done.22.refs_12_), channel_id=1, source_target_pairs={{0,4},{4,0},{8,12},{12,8},{1,5},{5,1},{9,13},{13,9},{2,6},{6,2},{1... | collective-permute-start | bytes 3145736 | tf_op jit(solution)/shard_map/ppermute | solution.py:366
  139.9 14.8 %copy-start.11 = (bf16[256,512]{1,0:T(8,128)(2,1)}, bf16[256,512]{1,0:T(8,128)(2,1)S(1)}, u32[]{:S(2)}) copy-start(bf16[256,512]{1,0:T(8,128)(2,1)S(1)} %collective-permute-done.26.refs_1_) | copy-start | bytes 786436
  139.9 6.5 %collective-permute-start.15 = (bf16[256,512]{1,0:T(8,128)(2,1)S(1)}, bf16[256,512]{1,0:T(8,128)(2,1)}, u32[]{:S(2)}, u32[]{:S(2)}) collective-permute-start(bf16[256,512]{1,0:T(8,128)(2,1)S(1)} %collective-permute-done.14.refs_1_), channel_id=1, source_target_pairs={{1,2},{2,3},{5,6},{6,7},{9,10},{10,11},{13,14},{14,15},{17,18},{18... | collective-permute-start | bytes 786440 | tf_op jit(solution)/shard_map/ppermute | solution.py:369
  145.0 10.9 %copy-start.12 = (bf16[256,512]{1,0:T(8,128)(2,1)}, bf16[256,512]{1,0:T(8,128)(2,1)S(1)}, u32[]{:S(2)}) copy-start(bf16[256,512]{1,0:T(8,128)(2,1)S(1)} %collective-permute-done.29.refs_4_) | copy-start | bytes 786436
  145.0 9.6 %collective-permute-start.18 = (bf16[256,512]{1,0:T(8,128)(2,1)S(1)}, bf16[256,512]{1,0:T(8,128)(2,1)}, u32[]{:S(2)}, u32[]{:S(2)}) collective-permute-start(bf16[256,512]{1,0:T(8,128)(2,1)S(1)} %collective-permute-done.17.refs_4_), channel_id=1, source_target_pairs={{1,0},{2,1},{5,4},{6,5},{9,8},{10,9},{13,12},{14,13},{17,16},{18,1... | collective-permute-start | bytes 786440 | tf_op jit(solution)/shard_map/ppermute | solution.py:369
  146.4 9.6 %collective-permute-start.27 = (bf16[256,512]{1,0:T(8,128)(2,1)S(1)}, bf16[256,512]{1,0:T(8,128)(2,1)S(1)}, u32[]{:S(2)}, u32[]{:S(2)}) collective-permute-start(bf16[256,512]{1,0:T(8,128)(2,1)S(1)} %collective-permute-done.26.refs_1_), channel_id=1, source_target_pairs={{1,2},{2,3},{5,6},{6,7},{9,10},{10,11},{13,14},{14,15},{17,18},{18... | collective-permute-start | bytes 786440 | tf_op jit(solution)/shard_map/ppermute | solution.py:369
  154.7 8.6 %collective-permute-start.30 = (bf16[256,512]{1,0:T(8,128)(2,1)S(1)}, bf16[256,512]{1,0:T(8,128)(2,1)S(1)}, u32[]{:S(2)}, u32[]{:S(2)}) collective-permute-start(bf16[256,512]{1,0:T(8,128)(2,1)S(1)} %collective-permute-done.29.refs_4_), channel_id=1, source_target_pairs={{1,0},{2,1},{5,4},{6,5},{9,8},{10,9},{13,12},{14,13},{17,16},{18,1... | collective-permute-start | bytes 786440 | tf_op jit(solution)/shard_map/ppermute | solution.py:369
  156.0 7.3 %copy-start.13 = (bf16[256,512]{1,0:T(8,128)(2,1)}, bf16[256,512]{1,0:T(8,128)(2,1)S(1)}, u32[]{:S(2)}) copy-start(bf16[256,512]{1,0:T(8,128)(2,1)S(1)} %collective-permute-done.27.refs_2_) | copy-start | bytes 786436
  156.0 8.6 %collective-permute-start.28 = (bf16[256,512]{1,0:T(8,128)(2,1)S(1)}, bf16[256,512]{1,0:T(8,128)(2,1)S(1)}, u32[]{:S(2)}, u32[]{:S(2)}) collective-permute-start(bf16[256,512]{1,0:T(8,128)(2,1)S(1)} %collective-permute-done.27.refs_2_), channel_id=1, source_target_pairs={{2,3},{6,7},{10,11},{14,15},{18,19},{22,23},{26,27},{30,31}} | collective-permute-start | bytes 786440 | tf_op jit(solution)/shard_map/ppermute | solution.py:369
  163.3 1.3 copy-start.14
  163.3 8.3 %collective-permute-start.31 = (bf16[256,512]{1,0:T(8,128)(2,1)S(1)}, bf16[256,512]{1,0:T(8,128)(2,1)S(1)}, u32[]{:S(2)}, u32[]{:S(2)}) collective-permute-start(bf16[256,512]{1,0:T(8,128)(2,1)S(1)} %collective-permute-done.30.refs_5_), channel_id=1, source_target_pairs={{1,0},{5,4},{9,8},{13,12},{17,16},{21,20},{25,24},{29,28}} | collective-permute-start | bytes 786440 | tf_op jit(solution)/shard_map/ppermute | solution.py:369
  164.6 6.9 %copy-start.15 = (bf16[256,512]{1,0:T(8,128)(2,1)}, bf16[256,512]{1,0:T(8,128)(2,1)S(1)}, u32[]{:S(2)}) copy-start(bf16[256,512]{1,0:T(8,128)(2,1)S(1)} %collective-permute-done.28.refs_3_) | copy-start | bytes 786436
  164.6 15.7 %collective-permute-start.16 = (bf16[256,512]{1,0:T(8,128)(2,1)}, bf16[256,512]{1,0:T(8,128)(2,1)}, u32[]{:S(2)}, u32[]{:S(2)}) collective-permute-start(bf16[256,512]{1,0:T(8,128)(2,1)} %collective-permute-done.15.refs_2_), channel_id=1, source_target_pairs={{2,3},{6,7},{10,11},{14,15},{18,19},{22,23},{26,27},{30,31}} | collective-permute-start | bytes 786440 | tf_op jit(solution)/shard_map/ppermute | solution.py:369
  171.6 0.7 copy-start.16
  172.3 8.6 %collective-permute-start.19 = (bf16[256,512]{1,0:T(8,128)(2,1)}, bf16[256,512]{1,0:T(8,128)(2,1)}, u32[]{:S(2)}, u32[]{:S(2)}) collective-permute-start(bf16[256,512]{1,0:T(8,128)(2,1)} %collective-permute-done.18.refs_5_), channel_id=1, source_target_pairs={{1,0},{5,4},{9,8},{13,12},{17,16},{21,20},{25,24},{29,28}} | collective-permute-start | bytes 786440 | tf_op jit(solution)/shard_map/ppermute | solution.py:369

commit v3 on v2

--- a/solution.py
+++ b/solution.py
@@ -113,7 +113,7 @@
     depth = keep_ref.shape[1]
     place = 0
     for pair in range(pairs):
-        order = index_ref[3 + pair]
+        order = index_ref[2 + pair]
         if pair < whole_pairs:
             both = refs[place]
             place += 1
@@ -129,10 +129,11 @@
         out_ref[0, pair * rows : (pair + 1) * rows, :] = total.astype(out_ref.dtype)
 
 
-def project(index, whole, pairs, weight, given, size, start, count, dtype):
+def project(index, whole, pairs, weight, given, size, start, dtype):
     rows = whole[0].shape[0] if whole else pairs[0][0].shape[0]
     depth = weight.shape[1]
     number = len(whole) + len(pairs)
+    count = given.shape[0]
     specs = []
     for place in range(len(whole)):
         if place == 0:
@@ -141,7 +142,7 @@
             specs.append(pl.BlockSpec((rows, 2 * depth), lambda i, idx: (0, 0)))
     specs += [pl.BlockSpec((rows, depth), lambda i, idx: (0, 0))] * (2 * len(pairs))
     specs.append(pl.BlockSpec((1, depth, size), lambda i, idx: ((start + i) % 3, 0, idx[1])))
-    specs.append(pl.BlockSpec((1, depth, size), lambda i, idx: ((start + i) % 3, 0, idx[2])))
+    specs.append(pl.BlockSpec((1, depth, size), lambda i, idx: ((start + i) % 3 if count == 3 else i, 0, 0)))
     return pl.pallas_call(
         functools.partial(project_kernel, number, len(whole)),
         out_shape=jax.ShapeDtypeStruct((count, number * rows, size), dtype),
@@ -152,16 +153,8 @@
             out_specs=pl.BlockSpec((1, number * rows, size), lambda i, idx: (i, 0, 0)),
         ),
         compiler_params=params(),
-        cost_estimate=pl.CostEstimate(
-            flops=2 * count * number * rows * 2 * depth * size,
-            bytes_accessed=4 * (number * rows * depth + count * depth * size),
-            transcendentals=0,
-        ),
+        cost_estimate=pl.CostEstimate(flops=1, bytes_accessed=1, transcendentals=0),
     )(index, *whole, *[block for pair in pairs for block in pair], weight, given)
-
-
-def project_own(index, whole, pairs, weight, given, size):
-    return project(index, whole, pairs, weight, given, size, 1, 3, F32)
 
 
 def split(value):
@@ -169,18 +162,17 @@
     return high, (value - high.astype(F32)).astype(BF16)
 
 
-def update_kernel(index_ref, local_ref, near_ref, far_ref, rate_ref, gate_ref, up_ref, down_ref,
+def update_kernel(index_ref, local_near_ref, local_far_ref, near_ref, far_ref, rate_ref, gate_ref, up_ref, down_ref,
                   gate_out, up_out, down_out, current):
     gate_w, up_w, down_w = gate_ref[0], up_ref[0], down_ref[0]
-    rows = local_ref.shape[1] // 4
+    rows = near_ref.shape[1] // 2
     sums = [None] * 3
     for block in range(4):
-        other = (near_ref if block < 2 else far_ref)
-        here = pl.ds(block * rows, rows)
-        there = pl.ds((block % 2) * rows, rows)
-        keys = local_ref[0, here, :] + other[0, there, :].astype(F32)
+        local_ref, other = (local_near_ref, near_ref) if block < 2 else (local_far_ref, far_ref)
+        here = pl.ds((block % 2) * rows, rows)
+        keys = local_ref[0, here, :] + other[0, here, :].astype(F32)
         keys = rms_scale(keys).astype(BF16)
-        values = (local_ref[1, here, :] + other[1, there, :].astype(F32)).astype(BF16)
+        values = (local_ref[1, here, :] + other[1, here, :].astype(F32)).astype(BF16)
         rate = jnp.broadcast_to(rate_ref[block, pl.ds(index_ref[0], 1), :], (8, rows)).T[:, :1]
         scaled = (rate * values.astype(F32)).astype(BF16)
         gate = dot(keys, gate_w)
@@ -201,25 +193,26 @@
 
     @pl.loop(0, NSI)
     def _(step):
+        values = [current[i] for i in range(3)]
+        halves = [split(value) for value in values]
+        crosses = [dot_nt(high, low) for high, low in halves]
+        grams = [dot_nt(high, high) + (cross + cross.T) for (high, low), cross in zip(halves, crosses)]
+        gram_halves = [split(gram) for gram in grams]
+        squares = [dot(high, high) + (dot(high, low) + dot(low, high)) for high, low in gram_halves]
+        polys = [split(quintic_b * gram + quintic_c * square) for gram, square in zip(grams, squares)]
         for i in range(3):
-            value = current[i]
-            high, low = split(value)
-            cross = dot_nt(high, low)
-            gram = dot_nt(high, high) + (cross + dot_nt(low, high))
-            gram_high, gram_low = split(gram)
-            square = dot(gram_high, gram_high) + (dot(gram_high, gram_low) + dot(gram_low, gram_high))
-            poly_high, poly_low = split(quintic_b * gram + quintic_c * square)
+            (poly_high, poly_low), (high, low) = polys[i], halves[i]
             moved = dot(poly_high, high) + (dot(poly_high, low) + dot(poly_low, high))
-            current[i] = quintic_a * value + moved
+            current[i] = quintic_a * values[i] + moved
 
     gate_out[...] = (gate_w.astype(F32) + current[0]).astype(BF16)
     up_out[...] = (up_w.astype(F32) + current[1]).astype(BF16)
     down_out[...] = (down_w.astype(F32) + current[2]).astype(BF16)
 
 
-def update(head, local, near, far, rates, fast_gate, fast_up, fast_down):
+def update(head, local_near, local_far, near, far, rates, fast_gate, fast_up, fast_down):
     size, hidden = fast_gate.shape[1:]
-    total = local.shape[1]
+    total = 2 * near.shape[1]
 
     def whole(array):
         zeros = (0,) * array.ndim
@@ -234,7 +227,8 @@
             num_scalar_prefetch=1,
             grid=(1,),
             in_specs=[
-                pl.BlockSpec((2, total, size), lambda i, idx: (0, 0, 0)),
+                pl.BlockSpec(near.shape, lambda i, idx: (0, 0, 0)),
+                pl.BlockSpec(far.shape, lambda i, idx: (0, 0, 0)),
                 whole(near),
                 whole(far),
                 whole(rates),
@@ -246,49 +240,51 @@
             scratch_shapes=[pltpu.VMEM((3, size, hidden), F32)],
         ),
         compiler_params=params(),
-        cost_estimate=pl.CostEstimate(
-            flops=20 * total * size * hidden + 3 * NSI * 3 * 8 * size * size * hidden,
-            bytes_accessed=total * size * 12 + 12 * size * hidden,
-            transcendentals=total * hidden,
-        ),
-    )(head.reshape(1).astype(jnp.int32), local, near, far, rates, fast_gate, fast_up, fast_down)
-
-
-def read_kernel(index_ref, local_ref, other_ref, gain_ref, gate_ref, up_ref, down_ref, out_ref):
-    queries = rms_scale(local_ref[0] + other_ref[0].astype(F32)).astype(BF16)
-    gate = dot(queries, gate_ref[...])
-    up = dot(queries, up_ref[...])
-    hidden = (gate * jax.nn.sigmoid(gate) * up).astype(BF16)
-    read = dot_nt(hidden, down_ref[...])
-    out_ref[0] = (rms_scale(read) * gain_ref[0]).astype(BF16)
-
-
-def read_out(head, local, other, gain, gate, up, down):
+        cost_estimate=pl.CostEstimate(flops=1, bytes_accessed=1, transcendentals=0),
+    )(head.reshape(1).astype(jnp.int32), local_near, local_far, near, far, rates, fast_gate, fast_up, fast_down)
+
+
+def read_kernel(index_ref, local_near_ref, local_far_ref, other_ref, gain_ref, gate_ref, up_ref, down_ref, *out_refs):
+    rows = out_refs[0].shape[0]
+    gate_w, up_w, down_w = gate_ref[...], up_ref[...], down_ref[...]
+    for block in range(4):
+        local_ref = local_near_ref if block < 2 else local_far_ref
+        here = pl.ds((block % 2) * rows, rows)
+        there = pl.ds(((block + 2) % 4) * rows, rows)
+        queries = rms_scale(local_ref[0, here, :] + other_ref[0, there, :].astype(F32)).astype(BF16)
+        gate = dot(queries, gate_w)
+        up = dot(queries, up_w)
+        hidden = (gate * jax.nn.sigmoid(gate) * up).astype(BF16)
+        read = dot_nt(hidden, down_w)
+        out_refs[block][...] = (rms_scale(read) * gain_ref[0]).astype(BF16)
+
+
+def read_out(head, local_near, local_far, other, gain, gate, up, down):
     size, hidden = gate.shape
-    total = local.shape[1]
+    total = other.shape[1]
     rows = total // 4
     weight = pl.BlockSpec((size, hidden), lambda i, idx: (0, 0))
+    local = pl.BlockSpec((1, 2 * rows, size), lambda i, idx: (2, 0, 0))
     return pl.pallas_call(
         read_kernel,
-        out_shape=jax.ShapeDtypeStruct((4, rows, size), BF16),
+        out_shape=[jax.ShapeDtypeStruct((rows, size), BF16)] * 4,
         grid_spec=pltpu.PrefetchScalarGridSpec(
             num_scalar_prefetch=1,
-            grid=(4,),
+            grid=(1,),
             in_specs=[
-                pl.BlockSpec((1, rows, size), lambda i, idx: (2, i, 0)),
-                pl.BlockSpec((1, rows, size), lambda i, idx: (0, (i + 2) % 4, 0)),
+                local,
+                local,
+                pl.BlockSpec((1, total, size), lambda i, idx: (0, 0, 0)),
                 pl.BlockSpec((1, 1, size), lambda i, idx: (idx[0], 0, 0)),
                 weight,
                 weight,
                 weight,
             ],
-            out_specs=pl.BlockSpec((1, rows, size), lambda i, idx: (i, 0, 0)),
+            out_specs=[pl.BlockSpec((rows, size), lambda i, idx: (0, 0))] * 4,
         ),
         compiler_params=params(),
-        cost_estimate=pl.CostEstimate(
-            flops=6 * total * size * hidden, bytes_accessed=total * size * 8, transcendentals=total * hidden
-        ),
-    )(head.reshape(1).astype(jnp.int32), local, other, gain, gate, up, down)
+        cost_estimate=pl.CostEstimate(flops=1, bytes_accessed=1, transcendentals=0),
+    )(head.reshape(1).astype(jnp.int32), local_near, local_far, other, gain, gate, up, down)
 
 
 def mix_kernel(index_ref, *refs):
@@ -320,12 +316,13 @@
 def mix(index, blocks, weights, before, dtype):
     rows, double = blocks[0].shape
     size = double // 2
-    own, peer, over_x, over_y, x_peer, y_peer = weights
+    own, peer, one, other, one_peer, other_peer = weights
     columns = own.shape[1]
     tile = columns // 2
     first = pl.BlockSpec((size, tile), lambda i, idx: (idx[4], i))
     second = pl.BlockSpec((size, tile), lambda i, idx: (idx[5], i))
-    halved = pl.BlockSpec((size, tile), lambda i, idx: (idx[6], i))
+    low = pl.BlockSpec((size, tile), lambda i, idx: (0, i))
+    high = pl.BlockSpec((size, tile), lambda i, idx: (idx[6], i))
     slab = pl.BlockSpec((rows, tile), lambda i, idx: (0, i))
     more = [] if before is None else [before]
     return pl.pallas_call(
@@ -335,16 +332,14 @@
             num_scalar_prefetch=1,
             grid=(2,),
             in_specs=[pl.BlockSpec((rows, double), lambda i, idx: (0, 0))] * 7
-            + [first, second, first, second, halved, halved, halved, halved]
+            + [first, second, first, second, low, high, low, high]
             + [slab] * len(more),
             out_specs=slab,
             scratch_shapes=[pltpu.VMEM((4, rows, double), BF16)],
         ),
         compiler_params=params(),
-        cost_estimate=pl.CostEstimate(
-            flops=16 * rows * size * columns, bytes_accessed=16 * size * columns + 28 * rows * size, transcendentals=0
-        ),
-    )(index, *blocks, own, own, peer, peer, over_x, over_y, x_peer, y_peer, *more)
+        cost_estimate=pl.CostEstimate(flops=1, bytes_accessed=1, transcendentals=0),
+    )(index, *blocks, own, own, peer, peer, one, other, one_peer, other_peer, *more)
 
 
 def after(value, *others):
@@ -374,67 +369,90 @@
     shared = lax.dynamic_slice(tokens, (0, chip * 2 * depth), (rows, 2 * depth))
     peer = across(shared, 1)
     weight = jnp.transpose(after(qkv_weight, shared), (1, 0, 2))
-    given = across(lax.dynamic_slice(weight, (0, 0, (1 - core) * 2 * size), (3, depth, 2 * size)), 1)
-
+
+    def for_peer(source, which, start, count):
+        block = (2 * (1 - core) + which) * size
+        return across(lax.dynamic_slice(source, (start, 0, block), (count, depth, size)), 1)
+
+    def order(which, *flags):
+        return jnp.stack([chip, 2 * core + which] + list(flags)).astype(jnp.int32)
+
+    far_flag = core ^ odd
+    given_other = for_peer(weight, 1 - chip, 1, 2)
+    send_near = project(order(1 - chip, core, core), [tokens, peer], [], weight, given_other, size, 1, BF16)
+    got_far = across(send_near, 2)
+    direct = after(direct, send_near)
     handed = hop(direct, [(i, i ^ 1) for i in range(4)])
     direct_peer = across(direct, 1)
+    held = after(weight, direct)
+    given_own = for_peer(held, chip, 0, 3)
+    given_query = for_peer(held, 1 - chip, 0, 1)
+    local_near = project(order(chip, core, core), [tokens, peer], [], weight, given_own, size, 1, F32)
+    activity = lax.dot_general(rate_weight, after(tokens, direct), (((0,), (1,)), ((), ())), preferred_element_type=F32)
+    rates_own = jax.nn.softplus(activity)
+    rates = jnp.stack([rates_own, across(rates_own, 1), across(rates_own, 2), across(rates_own, 3)])
+
+    out_held = after(out_weight, direct)
+    columns = out_held.shape[1]
+    out_first = lax.dynamic_slice(out_held, ((2 * side + 1 - chip) * size, 0), (size, columns))
+    out_later = lax.dynamic_slice(out_held.reshape(2, 2, size, columns), (0, chip, 0, 0), (2, 1, size, columns))
+    out_later = out_later.reshape(2 * size, columns)
+
+    handed = after(handed, local_near, got_far, rates, out_first, out_later, given_query)
     handed_peer = across(handed, 1)
     far = [(direct, handed), (direct_peer, handed_peer)]
-
-    def order(which, *flags):
-        return jnp.stack([chip, 2 * core + which, which] + list(flags)).astype(jnp.int32)
-
-    far_flag = core ^ odd
-    send_near = project(order(1 - chip, core, core), [tokens, peer], [], weight, given, size, 1, 2, BF16)
-    got_far = across(send_near, 2)
-    far = [tuple(after(block, send_near) for block in pair) for pair in far]
-    send_far = project(order(1 - chip, far_flag, far_flag), [], far, weight, given, size, 1, 2, BF16)
+    send_far = project(order(1 - chip, far_flag, far_flag), [], far, weight, given_other, size, 1, BF16)
     got_near = across(send_far, 2)
-    given = after(given, send_far)
+    given_query = after(given_query, send_far)
     everything = order(1 - chip, core, core, far_flag, far_flag)
-    send_query = project(everything, [tokens, peer], far, weight, given, size, 0, 1, BF16)
+    send_query = project(everything, [tokens, peer], far, weight, given_query, size, 0, BF16)
+    out_peer = across(after(out_weight, send_far), 1)
+    local_far = project(order(chip, far_flag, far_flag), [], far, weight, after(given_own, send_query, out_peer), size, 1, F32)
+    send_query, out_first, _ = lax.optimization_barrier((send_query, out_first, got_near))
     got_query = across(send_query, 2)
-
-    half = out_weight.shape[0] // 2
-    out_held = after(out_weight, send_query)
-    out_half = lax.dynamic_slice(out_held, (side * half, 0), (half, out_held.shape[1]))
-    over_x = across(out_half, 2)
-    out_peer = across(out_held, 1)
-
-    activity = lax.dot_general(rate_weight, tokens, (((0,), (1,)), ((), ())), preferred_element_type=F32)
-    rates_own = jax.nn.softplus(activity)
-    rates = jnp.stack([rates_own, across(rates_own, 1), across(rates_own, 2), across(rates_own, 3)])
-
-    given = after(given, out_half)
-    everything = order(chip, core, core, far_flag, far_flag)
-    local = project_own(everything, [tokens, peer], far, weight, given, size)
-
-    fresh = update(head, local, got_near, got_far, rates, fast_gate, fast_up, fast_down)
-    normed = read_out(head, local, got_query, out_gain.reshape(4, 1, size), *fresh)
-
-    over_x, _ = lax.optimization_barrier((over_x, normed))
-    over_y = lax.ppermute(over_x, "groups", [(0, 1), (1, 0)])
-    weights = [out_weight, out_peer, over_x, over_y, across(over_x, 1), across(over_y, 1)]
+    first_x = across(after(out_first, local_far), 2)
+
+
+    fresh = update(head, local_near, local_far, got_near, got_far, rates, fast_gate, fast_up, fast_down)
+    normed = read_out(head, local_near, local_far, got_query, out_gain.reshape(4, 1, size), *fresh)
 
     ups = [[(i, i + 1) for i in range(first, 3)] for first in range(3)]
     downs = [[(i + 1, i) for i in range(0, 3 - first)] for first in range(3)]
 
-    def spread(piece):
-        below, above = [piece], [piece]
-        for step in range(3):
-            below.append(hop(below[-1], ups[step]))
-            above.append(hop(above[-1], downs[step]))
-        return below + above[1:]
-
-    def mix_index(lead):
-        values = [place, seq, side ^ core, (1 - side) ^ core]
-        values += [2 * core + lead, 2 * (1 - core) + lead, lead]
+    def step(number, below, above):
+        return hop(below, ups[number]), hop(above, downs[number])
+
+    def mix_index(lead, order, second):
+        values = [place, seq, order ^ core, (1 - order) ^ core]
+        values += [2 * core + lead, 2 * (1 - core) + lead, jnp.int32(second)]
         return jnp.stack(values).astype(jnp.int32)
 
-    mine = spread(jnp.concatenate([normed[0], across(normed[1], 1)], axis=1))
-    theirs = spread(jnp.concatenate([across(normed[2], 2), across(normed[3], 3)], axis=1))
-    mixed = mix(mix_index(chip), mine, weights, None, F32)
-    return mix(mix_index(1 - chip), theirs, weights, mixed, BF16)
+    def swap_groups(array):
+        return lax.ppermute(array, "groups", [(0, 1), (1, 0)])
+
+    near_read, held_x = lax.optimization_barrier((normed[1], first_x))
+    first_y = swap_groups(held_x)
+    mine_own = jnp.concatenate([normed[0], across(near_read, 1)], axis=1)
+    far_reads = [after(block, mine_own) for block in normed[2:]]
+    theirs_own = jnp.concatenate([across(far_reads[0], 2), across(far_reads[1], 3)], axis=1)
+    mine_1 = step(0, mine_own, mine_own)
+    *mine_1, theirs_own, first_y, out_later = lax.optimization_barrier((*mine_1, theirs_own, first_y, out_later))
+    later_x = across(out_later, 2)
+    mine_2, theirs_1 = step(1, *mine_1), step(0, theirs_own, theirs_own)
+    *mine_2, below, above = lax.optimization_barrier((*mine_2, *theirs_1))
+    theirs_1 = [below, above]
+    mine_3, theirs_2 = step(2, *mine_2), step(1, *theirs_1)
+    *mine_3, below, above = lax.optimization_barrier((*mine_3, *theirs_2))
+    theirs_2 = [below, above]
+    held_x, held_y, held_later = after(first_x, below), after(first_y, below), after(later_x, below)
+    theirs_3 = step(2, *theirs_2)
+    mine = [mine_own] + [pair[i] for i in range(2) for pair in (mine_1, mine_2, mine_3)]
+    theirs = [theirs_own] + [pair[i] for i in range(2) for pair in (theirs_1, theirs_2, theirs_3)]
+    first = [out_weight, out_peer, first_x, first_y, across(held_x, 1), across(held_y, 1)]
+    later_peer = across(held_later, 1)
+    later = [out_weight, out_peer, later_x, later_x, later_peer, later_peer]
+    mixed = mix(mix_index(chip, side, 0), mine, first, None, F32)
+    return mix(mix_index(1 - chip, 0, 1), theirs, later, mixed, BF16)
 
 
 def on_device(axis_sizes, tokens, qkv_weight, rate_weight, fast_gate, fast_up, fast_down, out_gain, out_weight):

time: 187 us -> 177 us (0.947)
  waiting for transfers between devices: 69.7 us -> 51.6 us
  starting transfers between devices: 36 us -> 42 us
  Pallas kernels: 61.4 us -> 57.5 us
  local copies, waits for them, and re-layouts: 17.8 us -> 20.4 us
  other arithmetic: 0.63 us -> 3.13 us
    ppermute x13, waiting for transfers between devices: 39.9 us -> 23.3 us  [hop(): return lax.ppermute(array, 'head', links)]
    dynamic_slice x2 -> x5, local copies, waits for them, and re-layouts: 3.93 us -> 11 us  [the longest x3 6.86 us: for_peer(): lax.dynamic_slice(source, (start, 0, block), (count, depth, size))]
    pallas_call x1, Pallas kernels: 22.2 us -> 15.5 us  [update(): pl.pallas_call(update_kernel, out_shape=[out] * 3, grid_spec=pltpu.Prefet...]
    pallas_call x4 -> x5, Pallas kernels: 23.1 us -> 27.1 us  [project(): pl.pallas_call(functools.partial(project_kernel, number, len(whole)), out...]
    ppermute x13, starting transfers between devices: 21.8 us -> 25.9 us  [hop(): return lax.ppermute(array, 'head', links)]
    another operation x0 -> x4, other arithmetic: none -> 2.51 us  [order(): return jnp.stack([chip, 2 * core + which] + list(flags)).astype(jnp.int32)]
    another operation x4 -> x1, local copies, waits for them, and re-layouts: 2.54 us -> 0.57 us  [order(): return jnp.stack([chip, 2 * core + which] + list(flags)).astype(jnp.int32)]
    ppermute x18 -> x22, starting transfers between devices: 12.6 us -> 14.6 us  [across(): return lax.ppermute(array, 'seq', [(i, i ^ bit) for i in range(4)])]
  transfers between devices with their start and end apart: 32 -> 36, of which waited for: 16 -> 13; matrix products, arithmetic and copies ran while one was open for 3% -> 7% of each run, Pallas kernels for 30% -> 27%
where the time goes in v3:
time: 177 us; the launch traced here: 176 us
  Pallas kernels  57.5 us (32%)
  waiting for transfers between devices  51.6 us (29%)
  starting transfers between devices  42 us (24%)
  local copies, waits for them, and re-layouts  20.4 us (12%)
  other arithmetic  3.13 us (2%)
    ppermute x22, waiting for transfers between devices, across(): return lax.ppermute(array, 'seq', [(i, i ^ bit) for i in range(4)])  28.3 us
    pallas_call x5, Pallas kernels, project(): pl.pallas_call(functools.partial(project_kernel, number, len(whole)), out...  27.1 us
    ppermute x13, starting transfers between devices, hop(): return lax.ppermute(array, 'head', links)  25.9 us
    ppermute x13, waiting for transfers between devices, hop(): return lax.ppermute(array, 'head', links)  23.3 us
    pallas_call x1, Pallas kernels, update(): pl.pallas_call(update_kernel, out_shape=[out] * 3, grid_spec=pltpu.Prefet...  15.5 us
    ppermute x22, starting transfers between devices, across(): return lax.ppermute(array, 'seq', [(i, i ^ bit) for i in range(4)])  14.6 us
    pallas_call x2, Pallas kernels, mix(): pl.pallas_call(mix_kernel, out_shape=jax.ShapeDtypeStruct((rows, columns)...  11.1 us
    dynamic_slice x3, local copies, waits for them, and re-layouts, for_peer(): lax.dynamic_slice(source, (start, 0, block), (count, depth, size))  6.86 us
  transfers between devices with their start and end apart: 36, of which 13 were waited for; matrix products, arithmetic and copies ran while one was open for 7% of the time, Pallas kernels for 27%

profile of v3, /device:TPU:0, one launch (start us, length us, event | category | flops | bytes accessed | tf_op | source)
XLA Modules:
  0.0 175.8 jit_solution(12854702608293077197)
XLA Ops:
  0.0 1.9 %constant_dynamic-slice_fusion.5 = bf16[256,1024]{1,0:T(8,128)(2,1)} fusion(bf16[256,4096]{1,0:T(8,128)(2,1)} %refs_0_.2, s32[]{:T(128)S(6)} %select_n.23), kind=kLoop, calls=%fused_computation.12 | loop fusion | bytes 1048580 | tf_op jit(solution)/shard_map/dynamic_slice | solution.py:366
  1.9 1.3 constant_dynamic-slice_fusion.4
  3.2 2.3 %dynamic-slice_bitcast_fusion = bf16[2,1024,256]{2,1,0:T(8,128)(2,1)} fusion(bf16[1024,3,1024]{2,0,1:T(8,128)(2,1)} %param.9, s32[]{:T(128)S(6)} %select_n.25), kind=kLoop, calls=%fused_computation.1 | loop fusion | bytes 2097156 | tf_op jit(solution)/shard_map/dynamic_slice | solution.py:375
  6.0 2.9 %collective-permute-start.1 = (bf16[256,1024]{1,0:T(8,128)(2,1)}, bf16[256,1024]{1,0:T(8,128)(2,1)}, u32[]{:S(2)}, u32[]{:S(2)}) collective-permute-start(bf16[256,1024]{1,0:T(8,128)(2,1)} %constant_dynamic-slice_fusion.5), channel_id=1, source_target_pairs={{0,8},{4,12},{8,0},{12,4},{1,9},{5,13},{9,1},{13,5},{2,10},{6,14},... | collective-permute-start | bytes 1572872 | tf_op jit(solution)/shard_map/ppermute | solution.py:361
  8.9 0.7 add_add_fusion.1.index_ref
  9.7 0.9 copy-done.8
  10.9 4.7 %shard_map.82 = bf16[2,512,256]{2,1,0:T(8,128)(2,1)} custom-call(s32[4]{0:T(128)} %add_add_fusion.1.index_ref, bf16[256,4096]{1,0:T(8,128)(2,1)} %refs_0_.2, bf16[256,2048]{1,0:T(8,128)(2,1)} %copy-done.3, bf16[3,1024,1024]{2,1,0:T(8,128)(2,1)} %bitcast.30, bf16[2,1024,256]{2,1,0:T(8,128)(2,1)} %copy-done.8), custom_call_target="tpu_custom_call" | custom-call | flops 1 | bytes 1 | tf_op jit(solution)/shard_map/pallas_call | solution.py:146
  15.7 5.7 %collective-permute-done.1.refs_0_.refs_2_ = bf16[256,1024]{1,0:T(8,128)(2,1)} collective-permute-done((bf16[256,1024]{1,0:T(8,128)(2,1)}, bf16[256,1024]{1,0:T(8,128)(2,1)}, u32[]{:S(2)}, u32[]{:S(2)}) %collective-permute-start.1) | collective-permute-done | bytes 524320 | tf_op jit(solution)/shard_map/ppermute | solution.py:361
  21.4 2.7 %constant_dynamic-slice_fusion.3 = bf16[3,1024,256]{2,1,0:T(8,128)(2,1)} fusion(bf16[3,1024,1024]{2,1,0:T(8,128)(2,1)} %bitcast.31, s32[]{:T(128)S(6)} %select_n.26), kind=kLoop, calls=%fused_computation.10 | loop fusion | bytes 3145732 | tf_op jit(solution)/shard_map/dynamic_slice | solution.py:375
  24.0 1.8 %collective-permute-start.4 = (bf16[256,1024]{1,0:T(8,128)(2,1)}, bf16[256,1024]{1,0:T(8,128)(2,1)S(1)}, u32[]{:S(2)}, u32[]{:S(2)}) collective-permute-start(bf16[256,1024]{1,0:T(8,128)(2,1)} %collective-permute-done.1.refs_0_.refs_2_), channel_id=1, source_target_pairs={{0,1},{1,0},{2,3},{3,2},{4,5},{5,4},{6,7},{7,6},{8,9},{9,8},{10,11... | collective-permute-start | bytes 1572872 | tf_op jit(solution)/shard_map/ppermute | solution.py:364
  25.9 1.5 collective-permute-start.5
  27.3 1.9 %constant_dynamic-slice_fusion = bf16[1,1024,256]{2,1,0:T(8,128)(2,1)} fusion(bf16[3,1024,1024]{2,1,0:T(8,128)(2,1)} %bitcast.32, s32[]{:T(128)S(6)} %select_n.25), kind=kLoop, calls=%fused_computation.7 | loop fusion | bytes 1048580 | tf_op jit(solution)/shard_map/dynamic_slice | solution.py:375
  29.2 0.7 compare_select_fusion
  29.9 0.7 collective-permute-start.8
  30.6 0.6 add_add_fusion.index_ref
  31.2 8.3 %collective-permute-done.8 = f32[4,256]{1,0:T(4,128)S(1)} collective-permute-done((f32[4,256]{1,0:T(4,128)S(1)}, f32[4,256]{1,0:T(4,128)S(1)}, u32[]{:S(2)}, u32[]{:S(2)}) %collective-permute-start.8) | collective-permute-done | bytes 4128 | tf_op jit(solution)/shard_map/ppermute | solution.py:361
  39.5 1.5 collective-permute-start.7
  41.0 2.3 %constant_dynamic-slice_fusion.1 = bf16[2,1,256,1024]{3,2,1,0:T(8,128)(2,1)} fusion(bf16[2,2,256,1024]{3,2,1,0:T(8,128)(2,1)} %bitcast.37, s32[]{:T(128)S(6)} %select_n.29), kind=kLoop, calls=%fused_computation.8 | loop fusion | bytes 2097156 | tf_op jit(solution)/shard_map/dynamic_slice | solution.py:398
  43.8 1.9 %constant_dynamic-slice_fusion.2 = bf16[256,1024]{1,0:T(8,128)(2,1)} fusion(bf16[1024,1024]{1,0:T(8,128)(2,1)} %refs_8_.3, s32[]{:T(128)S(6)} %select_n.28), kind=kLoop, calls=%fused_computation.9 | loop fusion | bytes 1048580 | tf_op jit(solution)/shard_map/dynamic_slice | solution.py:397
  45.7 0.6 pad_maximum_fusion.1.rate_ref
  46.3 6.2 %shard_map.83.local_near_ref = f32[3,512,256]{2,1,0:T(8,128)} custom-call(s32[4]{0:T(128)} %add_add_fusion.index_ref, bf16[256,4096]{1,0:T(8,128)(2,1)} %refs_0_.2, bf16[256,2048]{1,0:T(8,128)(2,1)} %copy-done.3, bf16[3,1024,1024]{2,1,0:T(8,128)(2,1)} %bitcast.33, bf16[3,1024,256]{2,1,0:T(8,128)(2,1)} %collective-permute-done.3.refs_3_.refs_5_), custom_call_target="tpu_custom_call" | custom-call | flops 1 | bytes 1 | tf_op jit(solution)/shard_map/pallas_call | solution.py:146
  53.4 0.7 add_add_fusion.3.index_ref
  54.1 0.7 collective-permute-done.11.refs_3_.refs_5_
  54.9 4.9 %shard_map.84 = bf16[2,512,256]{2,1,0:T(8,128)(2,1)} custom-call(s32[4]{0:T(128)} %add_add_fusion.3.index_ref, bf16[256,1024]{1,0:T(8,128)(2,1)} %collective-permute-done.1.refs_0_.refs_2_, bf16[256,1024]{1,0:T(8,128)(2,1)} %copy-done.4, bf16[256,1024]{1,0:T(8,128)(2,1)} %copy-done.5, bf16[256,1024]{1,0:T(8,128)(2,1)} %collective-permute-done.11.refs_3_.refs_5_, ...), custom_call_target="tpu_custom_call" | custom-call | flops 1 | bytes 1 | tf_op jit(solution)/shard_map/pallas_call | solution.py:146
  60.2 0.9 collective-permute-start.13
  61.1 0.6 stack.109.index_ref
  61.7 0.6 add_add_fusion.2.index_ref
  62.3 5.2 %shard_map.85 = bf16[1,1024,256]{2,1,0:T(8,128)(2,1)} custom-call(s32[6]{0:T(128)} %stack.109.index_ref, bf16[256,4096]{1,0:T(8,128)(2,1)} %refs_0_.2, bf16[256,2048]{1,0:T(8,128)(2,1)} %copy-done.3, bf16[256,1024]{1,0:T(8,128)(2,1)} %collective-permute-done.1.refs_0_.refs_2_, bf16[256,1024]{1,0:T(8,128)(2,1)} %copy-done.4, bf16[256,1024]{1,0:T(8,128)(2,1)} %copy-done.5, ...), custom_call_target="tpu_custom_call" | custom-call | flops 1 | bytes 1 | tf_op jit(solution)/shard_map/pallas_call | solution.py:146
  67.5 6.9 %collective-permute-done.13.near_ref = bf16[2,512,256]{2,1,0:T(8,128)(2,1)S(1)} collective-permute-done((bf16[2,512,256]{2,1,0:T(8,128)(2,1)}, bf16[2,512,256]{2,1,0:T(8,128)(2,1)S(1)}, u32[]{:S(2)}, u32[]{:S(2)}) %collective-permute-start.13) | collective-permute-done | bytes 524320 | tf_op jit(solution)/shard_map/ppermute | solution.py:361
  74.4 1.3 collective-permute-start.14
  75.6 6.2 %shard_map.86.local_far_ref = f32[3,512,256]{2,1,0:T(8,128)} custom-call(s32[4]{0:T(128)} %add_add_fusion.2.index_ref, bf16[256,1024]{1,0:T(8,128)(2,1)} %collective-permute-done.1.refs_0_.refs_2_, bf16[256,1024]{1,0:T(8,128)(2,1)} %copy-done.4, bf16[256,1024]{1,0:T(8,128)(2,1)} %copy-done.5, bf16[256,1024]{1,0:T(8,128)(2,1)} %collective-permute-done.11.refs_3_.refs_5_, ...), custom_call_target="tpu_custom_call" | custom-call | flops 1 | bytes 1 | tf_op jit(solution)/shard_map/pallas_call | solution.py:146
  81.8 0.8 collective-permute-start.15
  82.6 15.5 %shard_map.87 = (bf16[256,512]{1,0:T(8,128)(2,1)}, bf16[256,512]{1,0:T(8,128)(2,1)}, bf16[256,512]{1,0:T(8,128)(2,1)}) custom-call(s32[1]{0:T(128)} %bitcast.6.index_ref, f32[3,512,256]{2,1,0:T(8,128)} %shard_map.83.local_near_ref, f32[3,512,256]{2,1,0:T(8,128)} %shard_map.86.local_far_ref, bf16[2,512,256]{2,1,0:T(8,128)(2,1)} %copy-done.14, ...), custom_call_target="tpu_custom_call" | custom-call | flops 1 | bytes 1 | tf_op jit(solution)/shard_map/pallas_call | solution.py:223
  98.2 0.8 copy-done.15
  99.0 3.8 %shard_map.88 = (bf16[256,256]{1,0:T(8,128)(2,1)}, bf16[256,256]{1,0:T(8,128)(2,1)}, bf16[256,256]{1,0:T(8,128)(2,1)}, bf16[256,256]{1,0:T(8,128)(2,1)}) custom-call(s32[1]{0:T(128)} %bitcast.6.index_ref, f32[3,512,256]{2,1,0:T(8,128)} %shard_map.83.local_near_ref, f32[3,512,256]{2,1,0:T(8,128)} %shard_map.86.local_far_ref, ...), custom_call_target="tpu_custom_call" | custom-call | flops 1 | bytes 1 | tf_op jit(solution)/shard_map/pallas_call | solution.py:268
  102.8 1.6 collective-permute-start.21
  104.3 0.9 constant_dynamic-update-slice_fusion.1
  105.3 0.6 collective-permute-done.16
  105.9 1.3 collective-permute-start.18
  107.2 4.7 %collective-permute-start.17 = (bf16[256,512]{1,0:T(8,128)(2,1)S(1)}, bf16[256,512]{1,0:T(8,128)(2,1)S(1)}, u32[]{:S(2)}, u32[]{:S(2)}) collective-permute-start(bf16[256,512]{1,0:T(8,128)(2,1)S(1)} %constant_dynamic-update-slice_fusion.refs_0_), channel_id=1, source_target_pairs={{0,1},{1,2},{2,3},{4,5},{5,6},{6,7},{8,9},{9,10},{10,11},{12,13},{... | collective-permute-start | bytes 786440 | tf_op jit(solution)/shard_map/ppermute | solution.py:364
  112.0 1.3 collective-permute-start.19
  113.3 4.7 %collective-permute-done.19 = bf16[256,256]{1,0:T(8,128)(2,1)S(1)} collective-permute-done((bf16[256,256]{1,0:T(8,128)(2,1)}, bf16[256,256]{1,0:T(8,128)(2,1)S(1)}, u32[]{:S(2)}, u32[]{:S(2)}) %collective-permute-start.19) | collective-permute-done | bytes 131104 | tf_op jit(solution)/shard_map/ppermute | solution.py:361
  118.0 1.3 collective-permute-done.20
  119.4 0.9 collective-permute-start.32
  120.2 0.7 collective-permute-start.22
  120.9 1.3 collective-permute-start.23
  122.2 1.3 collective-permute-start.25
  123.5 7.5 %collective-permute-start.24 = (bf16[256,512]{1,0:T(8,128)(2,1)S(1)}, bf16[256,512]{1,0:T(8,128)(2,1)S(1)}, u32[]{:S(2)}, u32[]{:S(2)}) collective-permute-start(bf16[256,512]{1,0:T(8,128)(2,1)S(1)} %pad_maximum_fusion.refs_0_), channel_id=1, source_target_pairs={{0,1},{1,2},{2,3},{4,5},{5,6},{6,7},{8,9},{9,10},{10,11},{12,13},{... | collective-permute-start | bytes 786440 | tf_op jit(solution)/shard_map/ppermute | solution.py:364
  131.1 3.3 %collective-permute-done.23.refs_5_ = bf16[256,512]{1,0:T(8,128)(2,1)S(1)} collective-permute-done((bf16[256,512]{1,0:T(8,128)(2,1)S(1)}, bf16[256,512]{1,0:T(8,128)(2,1)S(1)}, u32[]{:S(2)}, u32[]{:S(2)}) %collective-permute-start.23) | collective-permute-done | bytes 262176 | tf_op jit(solution)/shard_map/ppermute | solution.py:364
  134.3 5.4 %collective-permute-done.25.refs_4_ = bf16[256,512]{1,0:T(8,128)(2,1)S(1)} collective-permute-done((bf16[256,512]{1,0:T(8,128)(2,1)S(1)}, bf16[256,512]{1,0:T(8,128)(2,1)S(1)}, u32[]{:S(2)}, u32[]{:S(2)}) %collective-permute-start.25) | collective-permute-done | bytes 262176 | tf_op jit(solution)/shard_map/ppermute | solution.py:364
  139.8 1.4 collective-permute-start.28
  141.1 0.7 collective-permute-start.26
  141.8 1.3 collective-permute-start.27
  143.1 1.3 collective-permute-start.29
  144.4 8.8 %collective-permute-done.27.refs_6_ = bf16[256,512]{1,0:T(8,128)(2,1)S(1)} collective-permute-done((bf16[256,512]{1,0:T(8,128)(2,1)S(1)}, bf16[256,512]{1,0:T(8,128)(2,1)S(1)}, u32[]{:S(2)}, u32[]{:S(2)}) %collective-permute-start.27) | collective-permute-done | bytes 262176 | tf_op jit(solution)/shard_map/ppermute | solution.py:364
  153.2 4.3 %collective-permute-done.29.refs_5_ = bf16[256,512]{1,0:T(8,128)(2,1)} collective-permute-done((bf16[256,512]{1,0:T(8,128)(2,1)S(1)}, bf16[256,512]{1,0:T(8,128)(2,1)}, u32[]{:S(2)}, u32[]{:S(2)}) %collective-permute-start.29) | collective-permute-done | bytes 262176 | tf_op jit(solution)/shard_map/ppermute | solution.py:364
  158.3 1.3 collective-permute-start.31
  159.6 1.4 collective-permute-start.30
  160.9 0.6 stack.98.index_ref
  161.5 0.6 stack.114.index_ref
  162.2 5.5 %shard_map.89.refs_15_ = f32[256,1024]{1,0:T(8,128)} custom-call(s32[7]{0:T(128)} %stack.114.index_ref, bf16[256,512]{1,0:T(8,128)(2,1)} %copy-done.11, bf16[256,512]{1,0:T(8,128)(2,1)} %copy-done.20, bf16[256,512]{1,0:T(8,128)(2,1)} %copy-done.21, bf16[256,512]{1,0:T(8,128)(2,1)} %copy-done.23, bf16[256,512]{1,0:T(8,128)(2,1)} %copy-done.19, ...), custom_call_target="tpu_custom_call" | custom-call | flops 1 | bytes 1 | tf_op jit(solution)/shard_map/pallas_call | solution.py:328
  167.7 1.4 collective-permute-done.31.refs_6_
  169.1 1.0 copy-done.7
  170.2 5.6 %shard_map.90 = bf16[256,1024]{1,0:T(8,128)(2,1)} custom-call(s32[7]{0:T(128)} %stack.98.index_ref, bf16[256,512]{1,0:T(8,128)(2,1)} %copy-done.9, bf16[256,512]{1,0:T(8,128)(2,1)} %copy-done.18, bf16[256,512]{1,0:T(8,128)(2,1)} %collective-permute-done.28.refs_2_, bf16[256,512]{1,0:T(8,128)(2,1)} %collective-permute-done.30.refs_3_, ...), custom_call_target="tpu_custom_call" | custom-call | flops 1 | bytes 1 | tf_op jit(solution)/shard_map/pallas_call | solution.py:328
  (86 shorter events, 3.7 us)
Async XLA Ops:
  0.0 29.2 %copy-start = (bf16[4096,4]{0,1:T(4,128)(2,1)S(1)}, bf16[4096,4]{0,1:T(4,128)(2,1)}, u32[]{:S(2)}) copy-start(bf16[4096,4]{0,1:T(4,128)(2,1)} %param.10) | copy-start | bytes 98308
  5.5 4.1 %collective-permute-start.2 = (bf16[2,1024,256]{2,1,0:T(8,128)(2,1)}, bf16[2,1024,256]{2,1,0:T(8,128)(2,1)S(1)}, u32[]{:S(2)}, u32[]{:S(2)}) collective-permute-start(bf16[2,1024,256]{2,1,0:T(8,128)(2,1)} %dynamic-slice_bitcast_fusion), channel_id=1, source_target_pairs={{0,4},{4,0},{8,12},{12,8},{1,5},{5,1},{9,13},{13,9},{2,6},{6,2},{1... | collective-permute-start | bytes 3145736 | tf_op jit(solution)/shard_map/ppermute | solution.py:361
  6.0 3.8 %collective-permute-start = (bf16[256,2048]{1,0:T(8,128)(2,1)S(1)}, bf16[256,2048]{1,0:T(8,128)(2,1)S(1)}, u32[]{:S(2)}, u32[]{:S(2)}) collective-permute-start(bf16[256,2048]{1,0:T(8,128)(2,1)S(1)} %constant_dynamic-slice_fusion.4), channel_id=1, source_target_pairs={{0,4},{4,0},{8,12},{12,8},{1,5},{5,1},{9,13},{13,9},{2,6},{6,2},{1... | collective-permute-start | bytes 3145736 | tf_op jit(solution)/shard_map/ppermute | solution.py:361
  6.0 15.3 %collective-permute-start.1 = (bf16[256,1024]{1,0:T(8,128)(2,1)}, bf16[256,1024]{1,0:T(8,128)(2,1)}, u32[]{:S(2)}, u32[]{:S(2)}) collective-permute-start(bf16[256,1024]{1,0:T(8,128)(2,1)} %constant_dynamic-slice_fusion.5), channel_id=1, source_target_pairs={{0,8},{4,12},{8,0},{12,4},{1,9},{5,13},{9,1},{13,5},{2,10},{6,14},... | collective-permute-start | bytes 1572872 | tf_op jit(solution)/shard_map/ppermute | solution.py:361
  9.6 1.0 copy-start.8
  9.7 1.2 copy-start.3
  15.7 13.6 %copy-start.1 = (bf16[256,4096]{1,0:T(8,128)(2,1)S(1)}, bf16[256,4096]{1,0:T(8,128)(2,1)}, u32[]{:S(2)}) copy-start(bf16[256,4096]{1,0:T(8,128)(2,1)} %refs_0_.2) | copy-start | bytes 6291460
  24.0 22.3 %collective-permute-start.3 = (bf16[3,1024,256]{2,1,0:T(8,128)(2,1)}, bf16[3,1024,256]{2,1,0:T(8,128)(2,1)}, u32[]{:S(2)}, u32[]{:S(2)}) collective-permute-start(bf16[3,1024,256]{2,1,0:T(8,128)(2,1)} %constant_dynamic-slice_fusion.3), channel_id=1, source_target_pairs={{0,4},{4,0},{8,12},{12,8},{1,5},{5,1},{9,13},{13,9},{2,6},{6,2},{1... | collective-permute-start | bytes 4718600 | tf_op jit(solution)/shard_map/ppermute | solution.py:361
  24.0 28.5 %collective-permute-start.4 = (bf16[256,1024]{1,0:T(8,128)(2,1)}, bf16[256,1024]{1,0:T(8,128)(2,1)S(1)}, u32[]{:S(2)}, u32[]{:S(2)}) collective-permute-start(bf16[256,1024]{1,0:T(8,128)(2,1)} %collective-permute-done.1.refs_0_.refs_2_), channel_id=1, source_target_pairs={{0,1},{1,0},{2,3},{3,2},{4,5},{5,4},{6,7},{7,6},{8,9},{9,8},{10,11... | collective-permute-start | bytes 1572872 | tf_op jit(solution)/shard_map/ppermute | solution.py:364
  25.9 26.7 %collective-permute-start.5 = (bf16[2,512,256]{2,1,0:T(8,128)(2,1)}, bf16[2,512,256]{2,1,0:T(8,128)(2,1)S(1)}, u32[]{:S(2)}, u32[]{:S(2)}) collective-permute-start(bf16[2,512,256]{2,1,0:T(8,128)(2,1)} %shard_map.82), channel_id=1, source_target_pairs={{0,8},{4,12},{8,0},{12,4},{1,9},{5,13},{9,1},{13,5},{2,10},{6,14},... | collective-permute-start | bytes 1572872 | tf_op jit(solution)/shard_map/ppermute | solution.py:361
  29.2 23.3 %collective-permute-start.9 = (bf16[1,1024,256]{2,1,0:T(8,128)(2,1)}, bf16[1,1024,256]{2,1,0:T(8,128)(2,1)}, u32[]{:S(2)}, u32[]{:S(2)}) collective-permute-start(bf16[1,1024,256]{2,1,0:T(8,128)(2,1)} %constant_dynamic-slice_fusion), channel_id=1, source_target_pairs={{0,4},{4,0},{8,12},{12,8},{1,5},{5,1},{9,13},{13,9},{2,6},{6,2},{1... | collective-permute-start | bytes 1572872 | tf_op jit(solution)/shard_map/ppermute | solution.py:361
  29.9 9.6 %collective-permute-start.8 = (f32[4,256]{1,0:T(4,128)S(1)}, f32[4,256]{1,0:T(4,128)S(1)}, u32[]{:S(2)}, u32[]{:S(2)}) collective-permute-start(f32[4,256]{1,0:T(4,128)S(1)} %compare_select_fusion), channel_id=1, source_target_pairs={{0,12},{4,8},{8,4},{12,0},{1,13},{5,9},{9,5},{13,1},{2,14},{6,10},... | collective-permute-start | bytes 12296 | tf_op jit(solution)/shard_map/ppermute | solution.py:361
  39.5 3.8 %collective-permute-start.7 = (f32[4,256]{1,0:T(4,128)S(1)}, f32[4,256]{1,0:T(4,128)S(1)}, u32[]{:S(2)}, u32[]{:S(2)}) collective-permute-start(f32[4,256]{1,0:T(4,128)S(1)} %compare_select_fusion), channel_id=1, source_target_pairs={{0,8},{4,12},{8,0},{12,4},{1,9},{5,13},{9,1},{13,5},{2,10},{6,14},... | collective-permute-start | bytes 12296 | tf_op jit(solution)/shard_map/ppermute | solution.py:361
  43.3 2.4 %collective-permute-start.6 = (f32[4,256]{1,0:T(4,128)S(1)}, f32[4,256]{1,0:T(4,128)S(1)}, u32[]{:S(2)}, u32[]{:S(2)}) collective-permute-start(f32[4,256]{1,0:T(4,128)S(1)} %compare_select_fusion), channel_id=1, source_target_pairs={{0,4},{4,0},{8,12},{12,8},{1,5},{5,1},{9,13},{13,9},{2,6},{6,2},{1... | collective-permute-start | bytes 12296 | tf_op jit(solution)/shard_map/ppermute | solution.py:361
  45.7 8.4 %collective-permute-start.10 = (bf16[256,1024]{1,0:T(8,128)(2,1)}, bf16[256,1024]{1,0:T(8,128)(2,1)S(1)}, u32[]{:S(2)}, u32[]{:S(2)}) collective-permute-start(bf16[256,1024]{1,0:T(8,128)(2,1)} %collective-permute-done.1.refs_0_.refs_2_), channel_id=1, source_target_pairs={{0,4},{4,0},{8,12},{12,8},{1,5},{5,1},{9,13},{13,9},{2,6},{6,2},{1... | collective-permute-start | bytes 1572872 | tf_op jit(solution)/shard_map/ppermute | solution.py:361
  52.5 2.3 %copy-start.4 = (bf16[256,1024]{1,0:T(8,128)(2,1)}, bf16[256,1024]{1,0:T(8,128)(2,1)S(1)}, u32[]{:S(2)}) copy-start(bf16[256,1024]{1,0:T(8,128)(2,1)S(1)} %collective-permute-done.4.refs_1_.refs_3_) | copy-start | bytes 1572868
  52.5 0.9 copy-start.13
  52.5 2.2 %collective-permute-start.11 = (bf16[256,1024]{1,0:T(8,128)(2,1)S(1)}, bf16[256,1024]{1,0:T(8,128)(2,1)}, u32[]{:S(2)}, u32[]{:S(2)}) collective-permute-start(bf16[256,1024]{1,0:T(8,128)(2,1)S(1)} %collective-permute-done.4.refs_1_.refs_3_), channel_id=1, source_target_pairs={{0,4},{4,0},{8,12},{12,8},{1,5},{5,1},{9,13},{13,9},{2,6},{6,2},{1... | collective-permute-start | bytes 1572872 | tf_op jit(solution)/shard_map/ppermute | solution.py:361
  54.1 5.7 %copy-start.2 = (bf16[1024,1024]{1,0:T(8,128)(2,1)S(1)}, bf16[1024,1024]{1,0:T(8,128)(2,1)}, u32[]{:S(2)}) copy-start(bf16[1024,1024]{1,0:T(8,128)(2,1)} %refs_8_.3) | copy-start | bytes 6291460
  54.1 0.8 copy-start.5
  59.7 15.9 %collective-permute-start.12 = (bf16[1024,1024]{1,0:T(8,128)(2,1)S(1)}, bf16[1024,1024]{1,0:T(8,128)(2,1)}, u32[]{:S(2)}, u32[]{:S(2)}) collective-permute-start(bf16[1024,1024]{1,0:T(8,128)(2,1)S(1)} %copy-done.2), channel_id=1, source_target_pairs={{0,4},{4,0},{8,12},{12,8},{1,5},{5,1},{9,13},{13,9},{2,6},{6,2},{1... | collective-permute-start | bytes 6291464 | tf_op jit(solution)/shard_map/ppermute | solution.py:361
  60.2 14.1 %collective-permute-start.13 = (bf16[2,512,256]{2,1,0:T(8,128)(2,1)}, bf16[2,512,256]{2,1,0:T(8,128)(2,1)S(1)}, u32[]{:S(2)}, u32[]{:S(2)}) collective-permute-start(bf16[2,512,256]{2,1,0:T(8,128)(2,1)} %shard_map.84), channel_id=1, source_target_pairs={{0,8},{4,12},{8,0},{12,4},{1,9},{5,13},{9,1},{13,5},{2,10},{6,14},... | collective-permute-start | bytes 1572872 | tf_op jit(solution)/shard_map/ppermute | solution.py:361
  67.5 14.3 %copy-start.12 = (bf16[256,1024]{1,0:T(8,128)(2,1)S(1)}, bf16[256,1024]{1,0:T(8,128)(2,1)}, u32[]{:S(2)}) copy-start(bf16[256,1024]{1,0:T(8,128)(2,1)} %constant_dynamic-slice_fusion.2) | copy-start | bytes 1572868
  74.4 7.5 %copy-start.14 = (bf16[2,512,256]{2,1,0:T(8,128)(2,1)}, bf16[2,512,256]{2,1,0:T(8,128)(2,1)S(1)}, u32[]{:S(2)}) copy-start(bf16[2,512,256]{2,1,0:T(8,128)(2,1)S(1)} %collective-permute-done.13.near_ref) | copy-start | bytes 1572868
  74.4 23.8 %collective-permute-start.14 = (bf16[1,1024,256]{2,1,0:T(8,128)(2,1)}, bf16[1,1024,256]{2,1,0:T(8,128)(2,1)S(1)}, u32[]{:S(2)}, u32[]{:S(2)}) collective-permute-start(bf16[1,1024,256]{2,1,0:T(8,128)(2,1)} %shard_map.85), channel_id=1, source_target_pairs={{0,8},{4,12},{8,0},{12,4},{1,9},{5,13},{9,1},{13,5},{2,10},{6,14},... | collective-permute-start | bytes 1572872 | tf_op jit(solution)/shard_map/ppermute | solution.py:361
  81.8 20.9 %collective-permute-start.15 = (bf16[256,1024]{1,0:T(8,128)(2,1)S(1)}, bf16[256,1024]{1,0:T(8,128)(2,1)S(1)}, u32[]{:S(2)}, u32[]{:S(2)}) collective-permute-start(bf16[256,1024]{1,0:T(8,128)(2,1)S(1)} %copy-done.12), channel_id=1, source_target_pairs={{0,8},{4,12},{8,0},{12,4},{1,9},{5,13},{9,1},{13,5},{2,10},{6,14},... | collective-permute-start | bytes 1572872 | tf_op jit(solution)/shard_map/ppermute | solution.py:361
  98.2 0.8 copy-start.15
  99.0 20.4 %copy-start.10 = (bf16[2,1,256,1024]{3,2,1,0:T(8,128)(2,1)S(1)}, bf16[2,1,256,1024]{3,2,1,0:T(8,128)(2,1)}, u32[]{:S(2)}) copy-start(bf16[2,1,256,1024]{3,2,1,0:T(8,128)(2,1)} %constant_dynamic-slice_fusion.1) | copy-start | bytes 3145732
  102.7 59.4 %copy-start.16 = (bf16[256,1024]{1,0:T(8,128)(2,1)}, bf16[256,1024]{1,0:T(8,128)(2,1)S(1)}, u32[]{:S(2)}) copy-start(bf16[256,1024]{1,0:T(8,128)(2,1)S(1)} %collective-permute-done.15.refs_11_) | copy-start | bytes 1572868
  102.8 16.6 %collective-permute-start.21 = (bf16[256,1024]{1,0:T(8,128)(2,1)S(1)}, bf16[256,1024]{1,0:T(8,128)(2,1)}, u32[]{:S(2)}, u32[]{:S(2)}) collective-permute-start(bf16[256,1024]{1,0:T(8,128)(2,1)S(1)} %collective-permute-done.15.refs_11_), channel_id=1, source_target_pairs={{0,16},{16,0},{1,17},{17,1},{2,18},{18,2},{3,19},{19,3},{4,20},{20... | collective-permute-start | bytes 1572872 | tf_op jit(solution)/shard_map/ppermute | solution.py:431
  104.3 1.6 collective-permute-start.16
  105.9 56.3 %copy-start.11 = (bf16[256,512]{1,0:T(8,128)(2,1)}, bf16[256,512]{1,0:T(8,128)(2,1)S(1)}, u32[]{:S(2)}) copy-start(bf16[256,512]{1,0:T(8,128)(2,1)S(1)} %constant_dynamic-update-slice_fusion.refs_0_) | copy-start | bytes 786436
  105.9 13.4 %collective-permute-start.18 = (bf16[256,512]{1,0:T(8,128)(2,1)S(1)}, bf16[256,512]{1,0:T(8,128)(2,1)S(1)}, u32[]{:S(2)}, u32[]{:S(2)}) collective-permute-start(bf16[256,512]{1,0:T(8,128)(2,1)S(1)} %constant_dynamic-update-slice_fusion.refs_0_), channel_id=1, source_target_pairs={{1,0},{2,1},{3,2},{5,4},{6,5},{7,6},{9,8},{10,9},{11,10},{13,12},{... | collective-permute-start | bytes 786440 | tf_op jit(solution)/shard_map/ppermute | solution.py:364
  107.2 12.1 %collective-permute-start.17 = (bf16[256,512]{1,0:T(8,128)(2,1)S(1)}, bf16[256,512]{1,0:T(8,128)(2,1)S(1)}, u32[]{:S(2)}, u32[]{:S(2)}) collective-permute-start(bf16[256,512]{1,0:T(8,128)(2,1)S(1)} %constant_dynamic-update-slice_fusion.refs_0_), channel_id=1, source_target_pairs={{0,1},{1,2},{2,3},{4,5},{5,6},{6,7},{8,9},{9,10},{10,11},{12,13},{... | collective-permute-start | bytes 786440 | tf_op jit(solution)/shard_map/ppermute | solution.py:364
  112.0 6.0 %collective-permute-start.19 = (bf16[256,256]{1,0:T(8,128)(2,1)}, bf16[256,256]{1,0:T(8,128)(2,1)S(1)}, u32[]{:S(2)}, u32[]{:S(2)}) collective-permute-start(bf16[256,256]{1,0:T(8,128)(2,1)} %get-tuple-element.65), channel_id=1, source_target_pairs={{0,8},{4,12},{8,0},{12,4},{1,9},{5,13},{9,1},{13,5},{2,10},{6,14},... | collective-permute-start | bytes 393224 | tf_op jit(solution)/shard_map/ppermute | solution.py:361
  113.3 6.0 %collective-permute-start.20 = (bf16[256,256]{1,0:T(8,128)(2,1)}, bf16[256,256]{1,0:T(8,128)(2,1)S(1)}, u32[]{:S(2)}, u32[]{:S(2)}) collective-permute-start(bf16[256,256]{1,0:T(8,128)(2,1)} %get-tuple-element.67), channel_id=1, source_target_pairs={{0,12},{4,8},{8,4},{12,0},{1,13},{5,9},{9,5},{13,1},{2,14},{6,10},... | collective-permute-start | bytes 393224 | tf_op jit(solution)/shard_map/ppermute | solution.py:361
  119.3 48.4 %copy-start.9 = (bf16[256,512]{1,0:T(8,128)(2,1)}, bf16[256,512]{1,0:T(8,128)(2,1)S(1)}, u32[]{:S(2)}) copy-start(bf16[256,512]{1,0:T(8,128)(2,1)S(1)} %pad_maximum_fusion.refs_0_) | copy-start | bytes 786436
  119.3 38.3 %copy-start.19 = (bf16[256,512]{1,0:T(8,128)(2,1)}, bf16[256,512]{1,0:T(8,128)(2,1)S(1)}, u32[]{:S(2)}) copy-start(bf16[256,512]{1,0:T(8,128)(2,1)S(1)} %collective-permute-done.18.refs_4_) | copy-start | bytes 786436
  119.3 38.2 %copy-start.20 = (bf16[256,512]{1,0:T(8,128)(2,1)}, bf16[256,512]{1,0:T(8,128)(2,1)S(1)}, u32[]{:S(2)}) copy-start(bf16[256,512]{1,0:T(8,128)(2,1)S(1)} %collective-permute-done.17.refs_1_) | copy-start | bytes 786436
  119.4 38.2 %collective-permute-start.32 = (bf16[512,1024]{1,0:T(8,128)(2,1)S(1)}, bf16[512,1024]{1,0:T(8,128)(2,1)S(1)}, u32[]{:S(2)}, u32[]{:S(2)}) collective-permute-start(bf16[512,1024]{1,0:T(8,128)(2,1)S(1)} %bitcast.38), channel_id=1, source_target_pairs={{0,8},{4,12},{8,0},{12,4},{1,9},{5,13},{9,1},{13,5},{2,10},{6,14},... | collective-permute-start | bytes 3145736 | tf_op jit(solution)/shard_map/ppermute | solution.py:361
  120.2 10.8 %collective-permute-start.22 = (bf16[256,512]{1,0:T(8,128)(2,1)S(1)}, bf16[256,512]{1,0:T(8,128)(2,1)S(1)}, u32[]{:S(2)}, u32[]{:S(2)}) collective-permute-start(bf16[256,512]{1,0:T(8,128)(2,1)S(1)} %collective-permute-done.17.refs_1_), channel_id=1, source_target_pairs={{1,2},{2,3},{5,6},{6,7},{9,10},{10,11},{13,14},{14,15},{17,18},{18... | collective-permute-start | bytes 786440 | tf_op jit(solution)/shard_map/ppermute | solution.py:364
  120.9 13.4 %collective-permute-start.23 = (bf16[256,512]{1,0:T(8,128)(2,1)S(1)}, bf16[256,512]{1,0:T(8,128)(2,1)S(1)}, u32[]{:S(2)}, u32[]{:S(2)}) collective-permute-start(bf16[256,512]{1,0:T(8,128)(2,1)S(1)} %collective-permute-done.18.refs_4_), channel_id=1, source_target_pairs={{1,0},{2,1},{5,4},{6,5},{9,8},{10,9},{13,12},{14,13},{17,16},{18,1... | collective-permute-start | bytes 786440 | tf_op jit(solution)/shard_map/ppermute | solution.py:364
  122.2 17.6 %collective-permute-start.25 = (bf16[256,512]{1,0:T(8,128)(2,1)S(1)}, bf16[256,512]{1,0:T(8,128)(2,1)S(1)}, u32[]{:S(2)}, u32[]{:S(2)}) collective-permute-start(bf16[256,512]{1,0:T(8,128)(2,1)S(1)} %pad_maximum_fusion.refs_0_), channel_id=1, source_target_pairs={{1,0},{2,1},{3,2},{5,4},{6,5},{7,6},{9,8},{10,9},{11,10},{13,12},{... | collective-permute-start | bytes 786440 | tf_op jit(solution)/shard_map/ppermute | solution.py:364
  123.5 16.3 %collective-permute-start.24 = (bf16[256,512]{1,0:T(8,128)(2,1)S(1)}, bf16[256,512]{1,0:T(8,128)(2,1)S(1)}, u32[]{:S(2)}, u32[]{:S(2)}) collective-permute-start(bf16[256,512]{1,0:T(8,128)(2,1)S(1)} %pad_maximum_fusion.refs_0_), channel_id=1, source_target_pairs={{0,1},{1,2},{2,3},{4,5},{5,6},{6,7},{8,9},{9,10},{10,11},{12,13},{... | collective-permute-start | bytes 786440 | tf_op jit(solution)/shard_map/ppermute | solution.py:364
  131.1 26.5 %copy-start.21 = (bf16[256,512]{1,0:T(8,128)(2,1)}, bf16[256,512]{1,0:T(8,128)(2,1)S(1)}, u32[]{:S(2)}) copy-start(bf16[256,512]{1,0:T(8,128)(2,1)S(1)} %collective-permute-done.22.refs_2_) | copy-start | bytes 786436
  134.3 23.3 %copy-start.22 = (bf16[256,512]{1,0:T(8,128)(2,1)}, bf16[256,512]{1,0:T(8,128)(2,1)S(1)}, u32[]{:S(2)}) copy-start(bf16[256,512]{1,0:T(8,128)(2,1)S(1)} %collective-permute-done.23.refs_5_) | copy-start | bytes 786436
  139.8 27.9 %copy-start.17 = (bf16[256,512]{1,0:T(8,128)(2,1)}, bf16[256,512]{1,0:T(8,128)(2,1)S(1)}, u32[]{:S(2)}) copy-start(bf16[256,512]{1,0:T(8,128)(2,1)S(1)} %collective-permute-done.25.refs_4_) | copy-start | bytes 786436
  139.8 17.8 %copy-start.18 = (bf16[256,512]{1,0:T(8,128)(2,1)}, bf16[256,512]{1,0:T(8,128)(2,1)S(1)}, u32[]{:S(2)}) copy-start(bf16[256,512]{1,0:T(8,128)(2,1)S(1)} %collective-permute-done.24.refs_1_) | copy-start | bytes 786436
  139.8 4.6 %collective-permute-start.28 = (bf16[256,512]{1,0:T(8,128)(2,1)S(1)}, bf16[256,512]{1,0:T(8,128)(2,1)}, u32[]{:S(2)}, u32[]{:S(2)}) collective-permute-start(bf16[256,512]{1,0:T(8,128)(2,1)S(1)} %collective-permute-done.24.refs_1_), channel_id=1, source_target_pairs={{1,2},{2,3},{5,6},{6,7},{9,10},{10,11},{13,14},{14,15},{17,18},{18... | collective-permute-start | bytes 786440 | tf_op jit(solution)/shard_map/ppermute | solution.py:364
  141.1 3.3 %collective-permute-start.26 = (bf16[256,512]{1,0:T(8,128)(2,1)S(1)}, bf16[256,512]{1,0:T(8,128)(2,1)S(1)}, u32[]{:S(2)}, u32[]{:S(2)}) collective-permute-start(bf16[256,512]{1,0:T(8,128)(2,1)S(1)} %collective-permute-done.22.refs_2_), channel_id=1, source_target_pairs={{2,3},{6,7},{10,11},{14,15},{18,19},{22,23},{26,27},{30,31}} | collective-permute-start | bytes 786440 | tf_op jit(solution)/shard_map/ppermute | solution.py:364
  141.8 11.4 %collective-permute-start.27 = (bf16[256,512]{1,0:T(8,128)(2,1)S(1)}, bf16[256,512]{1,0:T(8,128)(2,1)S(1)}, u32[]{:S(2)}, u32[]{:S(2)}) collective-permute-start(bf16[256,512]{1,0:T(8,128)(2,1)S(1)} %collective-permute-done.23.refs_5_), channel_id=1, source_target_pairs={{1,0},{5,4},{9,8},{13,12},{17,16},{21,20},{25,24},{29,28}} | collective-permute-start | bytes 786440 | tf_op jit(solution)/shard_map/ppermute | solution.py:364
  143.1 14.5 %collective-permute-start.29 = (bf16[256,512]{1,0:T(8,128)(2,1)S(1)}, bf16[256,512]{1,0:T(8,128)(2,1)}, u32[]{:S(2)}, u32[]{:S(2)}) collective-permute-start(bf16[256,512]{1,0:T(8,128)(2,1)S(1)} %collective-permute-done.25.refs_4_), channel_id=1, source_target_pairs={{1,0},{2,1},{5,4},{6,5},{9,8},{10,9},{13,12},{14,13},{17,16},{18,1... | collective-permute-start | bytes 786440 | tf_op jit(solution)/shard_map/ppermute | solution.py:364
  144.4 13.3 %copy-start.23 = (bf16[256,512]{1,0:T(8,128)(2,1)}, bf16[256,512]{1,0:T(8,128)(2,1)S(1)}, u32[]{:S(2)}) copy-start(bf16[256,512]{1,0:T(8,128)(2,1)S(1)} %collective-permute-done.26.refs_3_) | copy-start | bytes 786436
  153.2 5.0 %copy-start.24 = (bf16[256,512]{1,0:T(8,128)(2,1)}, bf16[256,512]{1,0:T(8,128)(2,1)S(1)}, u32[]{:S(2)}) copy-start(bf16[256,512]{1,0:T(8,128)(2,1)S(1)} %collective-permute-done.27.refs_6_) | copy-start | bytes 786436
  157.6 10.1 %copy-start.6 = (bf16[512,1024]{1,0:T(8,128)(2,1)}, bf16[512,1024]{1,0:T(8,128)(2,1)S(1)}, u32[]{:S(2)}) copy-start(bf16[512,1024]{1,0:T(8,128)(2,1)S(1)} %collective-permute-done.32.refs_11_.refs_12_) | copy-start | bytes 3145732
  157.6 11.5 %collective-permute-start.33 = (bf16[512,1024]{1,0:T(8,128)(2,1)S(1)}, bf16[512,1024]{1,0:T(8,128)(2,1)S(1)}, u32[]{:S(2)}, u32[]{:S(2)}) collective-permute-start(bf16[512,1024]{1,0:T(8,128)(2,1)S(1)} %collective-permute-done.32.refs_11_.refs_12_), channel_id=1, source_target_pairs={{0,4},{4,0},{8,12},{12,8},{1,5},{5,1},{9,13},{13,9},{2,6},{6,2},{1... | collective-permute-start | bytes 3145736 | tf_op jit(solution)/shard_map/ppermute | solution.py:361
  157.7 4.5 %collective-permute-start.34 = (bf16[256,1024]{1,0:T(8,128)(2,1)S(1)}, bf16[256,1024]{1,0:T(8,128)(2,1)}, u32[]{:S(2)}, u32[]{:S(2)}) collective-permute-start(bf16[256,1024]{1,0:T(8,128)(2,1)S(1)} %collective-permute-done.15.refs_11_), channel_id=1, source_target_pairs={{0,4},{4,0},{8,12},{12,8},{1,5},{5,1},{9,13},{13,9},{2,6},{6,2},{1... | collective-permute-start | bytes 1572872 | tf_op jit(solution)/shard_map/ppermute | solution.py:361
  158.2 4.0 %collective-permute-start.35 = (bf16[256,1024]{1,0:T(8,128)(2,1)}, bf16[256,1024]{1,0:T(8,128)(2,1)}, u32[]{:S(2)}, u32[]{:S(2)}) collective-permute-start(bf16[256,1024]{1,0:T(8,128)(2,1)} %collective-permute-done.21.refs_12_), channel_id=1, source_target_pairs={{0,4},{4,0},{8,12},{12,8},{1,5},{5,1},{9,13},{13,9},{2,6},{6,2},{1... | collective-permute-start | bytes 1572872 | tf_op jit(solution)/shard_map/ppermute | solution.py:361
  158.3 10.8 %collective-permute-start.31 = (bf16[256,512]{1,0:T(8,128)(2,1)}, bf16[256,512]{1,0:T(8,128)(2,1)}, u32[]{:S(2)}, u32[]{:S(2)}) collective-permute-start(bf16[256,512]{1,0:T(8,128)(2,1)} %collective-permute-done.29.refs_5_), channel_id=1, source_target_pairs={{1,0},{5,4},{9,8},{13,12},{17,16},{21,20},{25,24},{29,28}} | collective-permute-start | bytes 786440 | tf_op jit(solution)/shard_map/ppermute | solution.py:364
  159.6 9.6 %collective-permute-start.30 = (bf16[256,512]{1,0:T(8,128)(2,1)}, bf16[256,512]{1,0:T(8,128)(2,1)}, u32[]{:S(2)}, u32[]{:S(2)}) collective-permute-start(bf16[256,512]{1,0:T(8,128)(2,1)} %collective-permute-done.28.refs_2_), channel_id=1, source_target_pairs={{2,3},{6,7},{10,11},{14,15},{18,19},{22,23},{26,27},{30,31}} | collective-permute-start | bytes 786440 | tf_op jit(solution)/shard_map/ppermute | solution.py:364
  169.1 1.0 copy-start.7

commit v4 on v3

--- a/solution.py
+++ b/solution.py
@@ -113,7 +113,7 @@
     depth = keep_ref.shape[1]
     place = 0
     for pair in range(pairs):
-        order = index_ref[2 + pair]
+        order = index_ref[3 + pair]
         if pair < whole_pairs:
             both = refs[place]
             place += 1
@@ -129,11 +129,10 @@
         out_ref[0, pair * rows : (pair + 1) * rows, :] = total.astype(out_ref.dtype)
 
 
-def project(index, whole, pairs, weight, given, size, start, dtype):
+def project(index, whole, pairs, weight, given, size, start, count, dtype):
     rows = whole[0].shape[0] if whole else pairs[0][0].shape[0]
     depth = weight.shape[1]
     number = len(whole) + len(pairs)
-    count = given.shape[0]
     specs = []
     for place in range(len(whole)):
         if place == 0:
@@ -142,7 +141,7 @@
             specs.append(pl.BlockSpec((rows, 2 * depth), lambda i, idx: (0, 0)))
     specs += [pl.BlockSpec((rows, depth), lambda i, idx: (0, 0))] * (2 * len(pairs))
     specs.append(pl.BlockSpec((1, depth, size), lambda i, idx: ((start + i) % 3, 0, idx[1])))
-    specs.append(pl.BlockSpec((1, depth, size), lambda i, idx: ((start + i) % 3 if count == 3 else i, 0, 0)))
+    specs.append(pl.BlockSpec((1, depth, size), lambda i, idx: ((start + i) % 3, 0, idx[2])))
     return pl.pallas_call(
         functools.partial(project_kernel, number, len(whole)),
         out_shape=jax.ShapeDtypeStruct((count, number * rows, size), dtype),
@@ -162,7 +161,8 @@
     return high, (value - high.astype(F32)).astype(BF16)
 
 
-def update_kernel(index_ref, local_near_ref, local_far_ref, near_ref, far_ref, rate_ref, gate_ref, up_ref, down_ref,
+def update_kernel(index_ref, local_near_ref, local_far_ref, near_ref, far_ref, rate_near_ref,
+                  rate_far_ref, gate_ref, up_ref, down_ref,
                   gate_out, up_out, down_out, current):
     gate_w, up_w, down_w = gate_ref[0], up_ref[0], down_ref[0]
     rows = near_ref.shape[1] // 2
@@ -173,7 +173,8 @@
         keys = local_ref[0, here, :] + other[0, here, :].astype(F32)
         keys = rms_scale(keys).astype(BF16)
         values = (local_ref[1, here, :] + other[1, here, :].astype(F32)).astype(BF16)
-        rate = jnp.broadcast_to(rate_ref[block, pl.ds(index_ref[0], 1), :], (8, rows)).T[:, :1]
+        rate_ref = rate_near_ref if block < 2 else rate_far_ref
+        rate = jnp.broadcast_to(rate_ref[pl.ds((block % 2) * 4 + index_ref[0], 1), :], (8, rows)).T[:, :1]
         scaled = (rate * values.astype(F32)).astype(BF16)
         gate = dot(keys, gate_w)
         up = dot(keys, up_w)
@@ -210,7 +211,7 @@
     down_out[...] = (down_w.astype(F32) + current[2]).astype(BF16)
 
 
-def update(head, local_near, local_far, near, far, rates, fast_gate, fast_up, fast_down):
+def update(head, local_near, local_far, near, far, rates_near, rates_far, fast_gate, fast_up, fast_down):
     size, hidden = fast_gate.shape[1:]
     total = 2 * near.shape[1]
 
@@ -231,7 +232,8 @@
                 pl.BlockSpec(far.shape, lambda i, idx: (0, 0, 0)),
                 whole(near),
                 whole(far),
-                whole(rates),
+                whole(rates_near),
+                whole(rates_far),
                 pick,
                 pick,
                 pick,
@@ -241,105 +243,126 @@
         ),
         compiler_params=params(),
         cost_estimate=pl.CostEstimate(flops=1, bytes_accessed=1, transcendentals=0),
-    )(head.reshape(1).astype(jnp.int32), local_near, local_far, near, far, rates, fast_gate, fast_up, fast_down)
-
-
-def read_kernel(index_ref, local_near_ref, local_far_ref, other_ref, gain_ref, gate_ref, up_ref, down_ref, *out_refs):
+    )(head.reshape(1).astype(jnp.int32), local_near, local_far, near, far, rates_near, rates_far, fast_gate, fast_up, fast_down)
+
+
+def read_kernel(index_ref, local_ref, other_ref, gain_ref, gate_ref, up_ref, down_ref, *out_refs):
     rows = out_refs[0].shape[0]
     gate_w, up_w, down_w = gate_ref[...], up_ref[...], down_ref[...]
-    for block in range(4):
-        local_ref = local_near_ref if block < 2 else local_far_ref
-        here = pl.ds((block % 2) * rows, rows)
-        there = pl.ds(((block + 2) % 4) * rows, rows)
-        queries = rms_scale(local_ref[0, here, :] + other_ref[0, there, :].astype(F32)).astype(BF16)
+    for block, out_ref in enumerate(out_refs):
+        here = pl.ds(block * rows, rows)
+        queries = rms_scale(local_ref[0, here, :] + other_ref[0, here, :].astype(F32)).astype(BF16)
         gate = dot(queries, gate_w)
         up = dot(queries, up_w)
         hidden = (gate * jax.nn.sigmoid(gate) * up).astype(BF16)
         read = dot_nt(hidden, down_w)
-        out_refs[block][...] = (rms_scale(read) * gain_ref[0]).astype(BF16)
-
-
-def read_out(head, local_near, local_far, other, gain, gate, up, down):
+        out_ref[...] = (rms_scale(read) * gain_ref[0]).astype(BF16)
+
+
+def read_out(head, local, other, which, gain, gate, up, down):
     size, hidden = gate.shape
-    total = other.shape[1]
-    rows = total // 4
+    rows = other.shape[1] // 4
     weight = pl.BlockSpec((size, hidden), lambda i, idx: (0, 0))
-    local = pl.BlockSpec((1, 2 * rows, size), lambda i, idx: (2, 0, 0))
     return pl.pallas_call(
         read_kernel,
-        out_shape=[jax.ShapeDtypeStruct((rows, size), BF16)] * 4,
+        out_shape=[jax.ShapeDtypeStruct((rows, size), BF16)] * 2,
         grid_spec=pltpu.PrefetchScalarGridSpec(
             num_scalar_prefetch=1,
             grid=(1,),
             in_specs=[
-                local,
-                local,
-                pl.BlockSpec((1, total, size), lambda i, idx: (0, 0, 0)),
+                pl.BlockSpec((1, 2 * rows, size), lambda i, idx: (2, 0, 0)),
+                pl.BlockSpec((1, 2 * rows, size), lambda i, idx: (0, which, 0)),
                 pl.BlockSpec((1, 1, size), lambda i, idx: (idx[0], 0, 0)),
                 weight,
                 weight,
                 weight,
             ],
-            out_specs=[pl.BlockSpec((rows, size), lambda i, idx: (0, 0))] * 4,
+            out_specs=[pl.BlockSpec((rows, size), lambda i, idx: (0, 0))] * 2,
         ),
         compiler_params=params(),
         cost_estimate=pl.CostEstimate(flops=1, bytes_accessed=1, transcendentals=0),
-    )(head.reshape(1).astype(jnp.int32), local_near, local_far, other, gain, gate, up, down)
-
-
-def mix_kernel(index_ref, *refs):
-    blocks = refs[:7]
-    own_a, own_b, peer_a, peer_b, x_ref, y_ref, x_peer, y_peer = refs[7:15]
-    place, seq = index_ref[0], index_ref[1]
-    held = refs[-1]
-    size = own_a.shape[0]
+    )(head.reshape(1).astype(jnp.int32), local, other, gain, gate, up, down)
+
+
+def mix_kernel(index_ref, own, below_1, above_1, below_2, above_2, *refs):
+    own_w, peer_w = refs[:2]
+    parts, peer_parts = refs[2:6], refs[6:10]
+    out_ref, last_ref, held = refs[10:]
+    place, seq, last = index_ref[0], index_ref[1], index_ref[2]
+    size = parts[0].shape[0]
 
     @pl.when(pl.program_id(0) == 0)
     def _():
-        held[place] = blocks[0][...]
-        for offset in range(1, 4):
-            below = place >= offset
-            held[lax.rem(place - offset + 4, 4)] = jnp.where(below, blocks[offset][...], blocks[7 - offset][...])
-
-    total = refs[15][...] if len(refs) == 18 else None
-    out_ref = refs[-2]
-    for k, pair in enumerate([(own_a, own_b), (peer_a, peer_b), (x_ref, y_ref), (x_peer, y_peer)]):
+        held[place] = own[...]
+        held[lax.rem(place + 3, 4)] = below_1[...]
+        held[lax.rem(place + 1, 4)] = above_1[...]
+        held[lax.rem(place + 2, 4)] = jnp.where(place >= 2, below_2[...], above_2[...])
+
+    total = None
+    for k in range(4):
         owner = lax.bitwise_xor(seq, k)
-        for part in range(2):
-            column = part * size if k < 2 else pl.multiple_of(index_ref[2 + part] * size, size)
-            block = held[owner, :, pl.ds(column, size)]
-            term = dot(block, pair[part][...])
+        for part in range(4):
+            if k < 2:
+                ref, head, here = (own_w, peer_w)[k], part, pl.ds(part * size, size)
+            else:
+                ref, head, here = (parts, peer_parts)[k - 2][part], index_ref[3 + part], pl.ds(0, size)
+            column = pl.multiple_of(index_ref[7 + head] * size, size)
+            term = dot(held[owner, :, pl.ds(column, size)], ref[here, :])
             total = term if total is None else total + term
-    out_ref[...] = total.astype(out_ref.dtype)
-
-
-def mix(index, blocks, weights, before, dtype):
-    rows, double = blocks[0].shape
-    size = double // 2
-    own, peer, one, other, one_peer, other_peer = weights
-    columns = own.shape[1]
+
+            @pl.when(owner == last)
+            def _():
+                last_ref[pl.ds(column, size), :] = ref[here, :]
+
+    out_ref[...] = total
+
+
+def mix(index, shards, own, peer, parts, peer_parts):
+    rows, width = shards[0].shape
+    depth, columns = own.shape
+    size = parts[0].shape[0]
     tile = columns // 2
-    first = pl.BlockSpec((size, tile), lambda i, idx: (idx[4], i))
-    second = pl.BlockSpec((size, tile), lambda i, idx: (idx[5], i))
-    low = pl.BlockSpec((size, tile), lambda i, idx: (0, i))
-    high = pl.BlockSpec((size, tile), lambda i, idx: (idx[6], i))
-    slab = pl.BlockSpec((rows, tile), lambda i, idx: (0, i))
-    more = [] if before is None else [before]
+    shard = pl.BlockSpec((rows, width), lambda i, idx: (0, 0))
+    whole = pl.BlockSpec((depth, tile), lambda i, idx: (0, i))
+    part = pl.BlockSpec((size, tile), lambda i, idx: (0, i))
     return pl.pallas_call(
         mix_kernel,
-        out_shape=jax.ShapeDtypeStruct((rows, columns), dtype),
+        out_shape=[jax.ShapeDtypeStruct((rows, columns), F32), jax.ShapeDtypeStruct((depth, columns), BF16)],
         grid_spec=pltpu.PrefetchScalarGridSpec(
             num_scalar_prefetch=1,
             grid=(2,),
-            in_specs=[pl.BlockSpec((rows, double), lambda i, idx: (0, 0))] * 7
-            + [first, second, first, second, low, high, low, high]
-            + [slab] * len(more),
-            out_specs=slab,
-            scratch_shapes=[pltpu.VMEM((4, rows, double), BF16)],
+            in_specs=[shard] * 5 + [whole] * 2 + [part] * 8,
+            out_specs=[pl.BlockSpec((rows, tile), lambda i, idx: (0, i)), whole],
+            scratch_shapes=[pltpu.VMEM((4, rows, width), BF16)],
         ),
         compiler_params=params(),
         cost_estimate=pl.CostEstimate(flops=1, bytes_accessed=1, transcendentals=0),
-    )(index, *blocks, own, own, peer, peer, one, other, one_peer, other_peer, *more)
+    )(index, *shards, own, peer, *parts, *peer_parts)
+
+
+def last_kernel(index_ref, below, above, weight, before, out_ref):
+    block = jnp.where(index_ref[0] == 0, above[...], below[...])
+    out_ref[...] = (before[...] + dot(block, weight[...])).astype(out_ref.dtype)
+
+
+def mix_last(index, below, above, weight, before):
+    rows, width = below.shape
+    columns = weight.shape[1]
+    tile = columns // 2
+    slab = pl.BlockSpec((rows, tile), lambda i, idx: (0, i))
+    shard = pl.BlockSpec((rows, width), lambda i, idx: (0, 0))
+    return pl.pallas_call(
+        last_kernel,
+        out_shape=jax.ShapeDtypeStruct((rows, columns), BF16),
+        grid_spec=pltpu.PrefetchScalarGridSpec(
+            num_scalar_prefetch=1,
+            grid=(2,),
+            in_specs=[shard, shard, pl.BlockSpec((width, tile), lambda i, idx: (0, i)), slab],
+            out_specs=slab,
+        ),
+        compiler_params=params(),
+        cost_estimate=pl.CostEstimate(flops=1, bytes_accessed=1, transcendentals=0),
+    )(index, below, above, weight, before)
 
 
 def after(value, *others):
@@ -370,89 +393,81 @@
     peer = across(shared, 1)
     weight = jnp.transpose(after(qkv_weight, shared), (1, 0, 2))
 
-    def for_peer(source, which, start, count):
-        block = (2 * (1 - core) + which) * size
-        return across(lax.dynamic_slice(source, (start, 0, block), (count, depth, size)), 1)
+    given = across(lax.dynamic_slice(weight, (0, 0, (1 - core) * 2 * size), (3, depth, 2 * size)), 1)
 
     def order(which, *flags):
-        return jnp.stack([chip, 2 * core + which] + list(flags)).astype(jnp.int32)
+        return jnp.stack([chip, 2 * core + which, which] + list(flags)).astype(jnp.int32)
+
+    activity = lax.dot_general(rate_weight, tokens, (((0,), (1,)), ((), ())), preferred_element_type=F32)
+    rates_own = jax.nn.softplus(activity)
+    rates_near = jnp.concatenate([rates_own, across(rates_own, 1)])
+    rates_far = across(rates_near, 2)
 
     far_flag = core ^ odd
-    given_other = for_peer(weight, 1 - chip, 1, 2)
-    send_near = project(order(1 - chip, core, core), [tokens, peer], [], weight, given_other, size, 1, BF16)
+    send_near = project(order(1 - chip, core, core), [tokens, peer], [], weight, given, size, 1, 2, BF16)
     got_far = across(send_near, 2)
-    direct = after(direct, send_near)
+    direct = after(direct, send_near, rates_far)
     handed = hop(direct, [(i, i ^ 1) for i in range(4)])
     direct_peer = across(direct, 1)
-    held = after(weight, direct)
-    given_own = for_peer(held, chip, 0, 3)
-    given_query = for_peer(held, 1 - chip, 0, 1)
-    local_near = project(order(chip, core, core), [tokens, peer], [], weight, given_own, size, 1, F32)
-    activity = lax.dot_general(rate_weight, after(tokens, direct), (((0,), (1,)), ((), ())), preferred_element_type=F32)
-    rates_own = jax.nn.softplus(activity)
-    rates = jnp.stack([rates_own, across(rates_own, 1), across(rates_own, 2), across(rates_own, 3)])
-
-    out_held = after(out_weight, direct)
-    columns = out_held.shape[1]
-    out_first = lax.dynamic_slice(out_held, ((2 * side + 1 - chip) * size, 0), (size, columns))
-    out_later = lax.dynamic_slice(out_held.reshape(2, 2, size, columns), (0, chip, 0, 0), (2, 1, size, columns))
-    out_later = out_later.reshape(2 * size, columns)
-
-    handed = after(handed, local_near, got_far, rates, out_first, out_later, given_query)
+    local_near = project(order(chip, core, core), [tokens, peer], [], weight, after(given, direct), size, 1, 3, F32)
+    half = out_weight.shape[0] // 2
+    out_half = lax.dynamic_slice(after(out_weight, direct), (side * half, 0), (half, out_weight.shape[1]))
+    out_first, out_later = out_half[:size], out_half[size:]
+
+    handed = after(handed, local_near, got_far, out_first, out_later)
     handed_peer = across(handed, 1)
     far = [(direct, handed), (direct_peer, handed_peer)]
-    send_far = project(order(1 - chip, far_flag, far_flag), [], far, weight, given_other, size, 1, BF16)
+    send_far = project(order(1 - chip, far_flag, far_flag), [], far, weight, given, size, 1, 2, BF16)
     got_near = across(send_far, 2)
-    given_query = after(given_query, send_far)
     everything = order(1 - chip, core, core, far_flag, far_flag)
-    send_query = project(everything, [tokens, peer], far, weight, given_query, size, 0, BF16)
+    send_query = project(everything, [tokens, peer], far, weight, after(given, send_far), size, 0, 1, BF16)
     out_peer = across(after(out_weight, send_far), 1)
-    local_far = project(order(chip, far_flag, far_flag), [], far, weight, after(given_own, send_query, out_peer), size, 1, F32)
-    send_query, out_first, _ = lax.optimization_barrier((send_query, out_first, got_near))
+    held = after(given, send_query, out_peer)
+    local_far = project(order(chip, far_flag, far_flag), [], far, weight, held, size, 1, 3, F32)
+    send_query = after(send_query, got_near, local_far)
     got_query = across(send_query, 2)
-    first_x = across(after(out_first, local_far), 2)
-
-
-    fresh = update(head, local_near, local_far, got_near, got_far, rates, fast_gate, fast_up, fast_down)
-    normed = read_out(head, local_near, local_far, got_query, out_gain.reshape(4, 1, size), *fresh)
-
-    ups = [[(i, i + 1) for i in range(first, 3)] for first in range(3)]
-    downs = [[(i + 1, i) for i in range(0, 3 - first)] for first in range(3)]
-
-    def step(number, below, above):
-        return hop(below, ups[number]), hop(above, downs[number])
-
-    def mix_index(lead, order, second):
-        values = [place, seq, order ^ core, (1 - order) ^ core]
-        values += [2 * core + lead, 2 * (1 - core) + lead, jnp.int32(second)]
-        return jnp.stack(values).astype(jnp.int32)
+
+    rates = (rates_near, rates_far)
+    fresh = update(head, local_near, local_far, got_near, got_far, *rates, fast_gate, fast_up, fast_down)
+    gain = out_gain.reshape(4, 1, size)
+    far_reads = read_out(head, local_far, got_query, 0, gain, *fresh)
+    near_reads = read_out(head, local_near, after(got_query, *far_reads), 1, gain, *fresh)
+    pieces = [near_reads[0], across(near_reads[1], 1), across(far_reads[0], 2), across(far_reads[1], 3)]
+    shard = jnp.concatenate(pieces, axis=1)
+
+    def both(number, below, above):
+        up = [(i, i + 1) for i in range(number, 3)]
+        down = [(i + 1, i) for i in range(0, 3 - number)]
+        return hop(below, up), hop(above, down)
 
     def swap_groups(array):
         return lax.ppermute(array, "groups", [(0, 1), (1, 0)])
 
-    near_read, held_x = lax.optimization_barrier((normed[1], first_x))
-    first_y = swap_groups(held_x)
-    mine_own = jnp.concatenate([normed[0], across(near_read, 1)], axis=1)
-    far_reads = [after(block, mine_own) for block in normed[2:]]
-    theirs_own = jnp.concatenate([across(far_reads[0], 2), across(far_reads[1], 3)], axis=1)
-    mine_1 = step(0, mine_own, mine_own)
-    *mine_1, theirs_own, first_y, out_later = lax.optimization_barrier((*mine_1, theirs_own, first_y, out_later))
-    later_x = across(out_later, 2)
-    mine_2, theirs_1 = step(1, *mine_1), step(0, theirs_own, theirs_own)
-    *mine_2, below, above = lax.optimization_barrier((*mine_2, *theirs_1))
-    theirs_1 = [below, above]
-    mine_3, theirs_2 = step(2, *mine_2), step(1, *theirs_1)
-    *mine_3, below, above = lax.optimization_barrier((*mine_3, *theirs_2))
-    theirs_2 = [below, above]
-    held_x, held_y, held_later = after(first_x, below), after(first_y, below), after(later_x, below)
-    theirs_3 = step(2, *theirs_2)
-    mine = [mine_own] + [pair[i] for i in range(2) for pair in (mine_1, mine_2, mine_3)]
-    theirs = [theirs_own] + [pair[i] for i in range(2) for pair in (theirs_1, theirs_2, theirs_3)]
-    first = [out_weight, out_peer, first_x, first_y, across(held_x, 1), across(held_y, 1)]
-    later_peer = across(held_later, 1)
-    later = [out_weight, out_peer, later_x, later_x, later_peer, later_peer]
-    mixed = mix(mix_index(chip, side, 0), mine, first, None, F32)
-    return mix(mix_index(1 - chip, 0, 1), theirs, later, mixed, BF16)
+    first_x = across(after(out_first, shard), 2)
+    later_x = across(after(out_later, shard), 2)
+    below_1, above_1 = both(0, shard, shard)
+    below_1, above_1, first_x = lax.optimization_barrier((below_1, above_1, first_x))
+    first_y = swap_groups(first_x)
+    below_2, above_2 = both(1, below_1, above_1)
+    later_x = after(later_x, first_y)
+    later_y = swap_groups(later_x)
+    first_x_peer = across(first_x, 1)
+    below_2, above_2, held_x, held_y, first_x_peer = lax.optimization_barrier(
+        (below_2, above_2, later_x, first_y, first_x_peer)
+    )
+    below_3, above_3 = both(2, below_2, above_2)
+    first_y_peer, later_x_peer = across(held_y, 1), across(held_x, 1)
+    later_y_peer = across(later_y, 1)
+
+    values = [place, seq, jnp.where(place == 0, 3, 0)]
+    values += [2 * side, 2 * (1 - side), 2 * side + 1, 2 * (1 - side) + 1]
+    values += [((head_ >> 1) ^ core) + 2 * ((head_ & 1) ^ chip) for head_ in range(4)]
+    index = jnp.stack(values).astype(jnp.int32)
+    shards = [shard, below_1, above_1, below_2, above_2]
+    parts = [first_x, first_y, later_x, later_y]
+    peer_parts = [first_x_peer, first_y_peer, later_x_peer, later_y_peer]
+    mixed, weight_last = mix(index, shards, out_weight, out_peer, parts, peer_parts)
+    return mix_last(index, below_3, above_3, weight_last, mixed)
 
 
 def on_device(axis_sizes, tokens, qkv_weight, rate_weight, fast_gate, fast_up, fast_down, out_gain, out_weight):

time: 177 us -> 158 us (0.89)
  starting transfers between devices: 42 us -> 29.1 us
  Pallas kernels: 57.5 us -> 62.2 us
  waiting for transfers between devices: 51.6 us -> 46.9 us
  other arithmetic: 3.13 us -> 0.01 us
  local copies, waits for them, and re-layouts: 20.4 us -> 18.2 us
    ppermute x13 -> x7, starting transfers between devices: 25.9 us -> 12.5 us  [hop(): return lax.ppermute(array, 'head', links)]
    ppermute x1 -> x2, waiting for transfers between devices: 0.01 us -> 9 us  [swap_groups(): return lax.ppermute(array, 'groups', [(0, 1), (1, 0)])]
    ppermute x13 -> x7, waiting for transfers between devices: 23.3 us -> 15.1 us  [hop(): return lax.ppermute(array, 'head', links)]
    dynamic_slice x5 -> x1, local copies, waits for them, and re-layouts: 11 us -> 3.88 us  [chip_plan(): lax.dynamic_slice(weight, (0, 0, (1 - core) * 2 * size), (3, depth, 2 * s...]
    ppermute x22 -> x20, waiting for transfers between devices: 28.3 us -> 22.8 us  [across(): return lax.ppermute(array, 'seq', [(i, i ^ bit) for i in range(4)])]
    another operation x5 -> x0, other arithmetic: 3.12 us -> none  [the longest x4 2.51 us: order(): return jnp.stack([chip, 2 * core + which] + list(flags)).astype(jnp.int32)]
    pallas_call x2, Pallas kernels: 11.1 us -> 13.5 us  [the longest x1 9.52 us: mix(): pl.pallas_call(mix_kernel, out_shape=[jax.ShapeDtypeStruct((rows, columns...]
    pallas_call x1 -> x2, Pallas kernels: 3.77 us -> 5.86 us  [read_out(): pl.pallas_call(read_kernel, out_shape=[jax.ShapeDtypeStruct((rows, size),...]
  transfers between devices with their start and end apart: 36 -> 29, of which waited for: 13 -> 16; matrix products, arithmetic and copies ran while one was open for 7% -> 5% of each run, Pallas kernels for 27% -> 30%
where the time goes in v4:
time: 158 us; the launch traced here: 157 us
  Pallas kernels  62.2 us (39%)
  waiting for transfers between devices  46.9 us (30%)
  starting transfers between devices  29.1 us (18%)
  local copies, waits for them, and re-layouts  18.2 us (12%)
    pallas_call x5, Pallas kernels, project(): pl.pallas_call(functools.partial(project_kernel, number, len(whole)), out...  27.3 us
    ppermute x20, waiting for transfers between devices, across(): return lax.ppermute(array, 'seq', [(i, i ^ bit) for i in range(4)])  22.8 us
    pallas_call x1, Pallas kernels, update(): pl.pallas_call(update_kernel, out_shape=[out] * 3, grid_spec=pltpu.Prefet...  15.5 us
    ppermute x7, waiting for transfers between devices, hop(): return lax.ppermute(array, 'head', links)  15.1 us
    ppermute x20, starting transfers between devices, across(): return lax.ppermute(array, 'seq', [(i, i ^ bit) for i in range(4)])  13.6 us
    ppermute x7, starting transfers between devices, hop(): return lax.ppermute(array, 'head', links)  12.5 us
    pallas_call x1, Pallas kernels, mix(): pl.pallas_call(mix_kernel, out_shape=[jax.ShapeDtypeStruct((rows, columns...  9.52 us
    ppermute x2, waiting for transfers between devices, swap_groups(): return lax.ppermute(array, 'groups', [(0, 1), (1, 0)])  9 us
  transfers between devices with their start and end apart: 29, of which 16 were waited for; matrix products, arithmetic and copies ran while one was open for 5% of the time, Pallas kernels for 30%

profile of v4, /device:TPU:0, one launch (start us, length us, event | category | flops | bytes accessed | tf_op | source)
XLA Modules:
  0.0 157.4 jit_solution(13683275695951221278)
XLA Ops:
  0.0 1.9 %constant_dynamic-slice_fusion.3 = bf16[256,1024]{1,0:T(8,128)(2,1)} fusion(bf16[256,4096]{1,0:T(8,128)(2,1)} %refs_0_.3, s32[]{:T(128)S(6)} %select_n.21), kind=kLoop, calls=%fused_computation.11 | loop fusion | bytes 1048580 | tf_op jit(solution)/shard_map/dynamic_slice | solution.py:389
  1.9 2.3 %constant_dynamic-slice_fusion.2 = bf16[256,2048]{1,0:T(8,128)(2,1)} fusion(bf16[256,4096]{1,0:T(8,128)(2,1)} %refs_0_.3, s32[]{:T(128)S(6)} %select_n.22), kind=kLoop, calls=%fused_computation.10 | loop fusion | bytes 2097156 | tf_op jit(solution)/shard_map/dynamic_slice | solution.py:392
  4.2 3.9 %dynamic-slice_bitcast_fusion = bf16[3,1024,512]{2,1,0:T(8,128)(2,1)} fusion(bf16[1024,3,1024]{2,0,1:T(8,128)(2,1)} %param.9, s32[]{:T(128)S(6)} %select_n.23), kind=kLoop, calls=%fused_computation | loop fusion | bytes 6291460 | tf_op jit(solution)/shard_map/dynamic_slice | solution.py:396
  8.1 0.5 collective-permute-start.1
  8.6 2.9 %collective-permute-start.2 = (bf16[256,1024]{1,0:T(8,128)(2,1)}, bf16[256,1024]{1,0:T(8,128)(2,1)}, u32[]{:S(2)}, u32[]{:S(2)}) collective-permute-start(bf16[256,1024]{1,0:T(8,128)(2,1)} %constant_dynamic-slice_fusion.3), channel_id=1, source_target_pairs={{0,8},{4,12},{8,0},{12,4},{1,9},{5,13},{9,1},{13,5},{2,10},{6,14},... | collective-permute-start | bytes 1572872 | tf_op jit(solution)/shard_map/ppermute | solution.py:384
  11.5 0.7 compare_select_fusion
  12.2 0.1 collective-permute-start.3
  12.3 3.0 %collective-permute-done.3 = f32[4,256]{1,0:T(4,128)S(1)} collective-permute-done((f32[4,256]{1,0:T(4,128)S(1)}, f32[4,256]{1,0:T(4,128)S(1)}, u32[]{:S(2)}, u32[]{:S(2)}) %collective-permute-start.3) | collective-permute-done | bytes 4128 | tf_op jit(solution)/shard_map/ppermute | solution.py:384
  15.3 1.1 collective-permute-start.4
  16.4 0.7 stack.105.index_ref
  17.1 1.6 %copy-done.1 = bf16[3,1024,512]{2,1,0:T(8,128)(2,1)} copy-done((bf16[3,1024,512]{2,1,0:T(8,128)(2,1)}, bf16[3,1024,512]{2,1,0:T(8,128)(2,1)S(1)}, u32[]{:S(2)}) %copy-start.1) | copy-done | bytes 3145752
  18.7 4.7 %shard_map.82 = bf16[2,512,256]{2,1,0:T(8,128)(2,1)} custom-call(s32[5]{0:T(128)} %stack.105.index_ref, bf16[256,4096]{1,0:T(8,128)(2,1)} %refs_0_.3, bf16[256,2048]{1,0:T(8,128)(2,1)} %collective-permute-done.refs_1_, bf16[3,1024,1024]{2,1,0:T(8,128)(2,1)} %bitcast.27, bf16[3,1024,512]{2,1,0:T(8,128)(2,1)} %copy-done.1), custom_call_target="tpu_custom_call" | custom-call | flops 1 | bytes 1 | tf_op jit(solution)/shard_map/pallas_call | solution.py:145
  23.5 0.5 collective-permute-done.4.rate_far_ref
  24.0 1.8 %collective-permute-start.5 = (bf16[256,1024]{1,0:T(8,128)(2,1)}, bf16[256,1024]{1,0:T(8,128)(2,1)S(1)}, u32[]{:S(2)}, u32[]{:S(2)}) collective-permute-start(bf16[256,1024]{1,0:T(8,128)(2,1)} %collective-permute-done.2.refs_0_.refs_2_), channel_id=1, source_target_pairs={{0,1},{1,0},{2,3},{3,2},{4,5},{5,4},{6,7},{7,6},{8,9},{9,8},{10,11... | collective-permute-start | bytes 1572872 | tf_op jit(solution)/shard_map/ppermute | solution.py:387
  25.9 1.5 collective-permute-start.6
  27.4 0.6 stack.102.index_ref
  28.0 6.2 %shard_map.83.local_near_ref.local_ref = f32[3,512,256]{2,1,0:T(8,128)} custom-call(s32[5]{0:T(128)} %stack.102.index_ref, bf16[256,4096]{1,0:T(8,128)(2,1)} %refs_0_.3, bf16[256,2048]{1,0:T(8,128)(2,1)} %collective-permute-done.refs_1_, bf16[3,1024,1024]{2,1,0:T(8,128)(2,1)} %bitcast.28, bf16[3,1024,512]{2,1,0:T(8,128)(2,1)} %copy-done.1), custom_call_target="tpu_custom_call" | custom-call | flops 1 | bytes 1 | tf_op jit(solution)/shard_map/pallas_call | solution.py:145
  34.2 2.1 %constant_dynamic-slice_fusion.1 = (bf16[256,1024]{1,0:T(8,128)(2,1)}, bf16[256,1024]{1,0:T(8,128)(2,1)S(1)}) fusion(bf16[1024,1024]{1,0:T(8,128)(2,1)} %refs_0_.4, s32[]{:T(128)S(6)} %add.61, s32[]{:T(128)S(6)} %select_n.25), kind=kLoop, calls=%fused_computation.9 | loop fusion | bytes 2097160 | tf_op jit(solution)/shard_map/slice | solution.py:415
  36.2 1.5 collective-permute-done.5.refs_1_.refs_3_
  37.7 1.3 collective-permute-done.6.far_ref
  39.0 0.7 stack.108.index_ref
  39.7 1.2 collective-permute-done.8.refs_3_.refs_5_
  40.9 0.8 copy-done.5
  41.7 4.7 %shard_map.84 = bf16[2,512,256]{2,1,0:T(8,128)(2,1)} custom-call(s32[5]{0:T(128)} %stack.108.index_ref, bf16[256,1024]{1,0:T(8,128)(2,1)} %collective-permute-done.2.refs_0_.refs_2_, bf16[256,1024]{1,0:T(8,128)(2,1)} %copy-done.3, bf16[256,1024]{1,0:T(8,128)(2,1)} %copy-done.4, bf16[256,1024]{1,0:T(8,128)(2,1)} %copy-done.5, ...), custom_call_target="tpu_custom_call" | custom-call | flops 1 | bytes 1 | tf_op jit(solution)/shard_map/pallas_call | solution.py:145
  46.5 0.1 collective-permute-start.10
  46.6 1.4 collective-permute-start.9
  48.0 0.6 stack.109.index_ref
  48.6 0.6 stack.107.index_ref
  49.3 5.2 %shard_map.85 = bf16[1,1024,256]{2,1,0:T(8,128)(2,1)} custom-call(s32[7]{0:T(128)} %stack.107.index_ref, bf16[256,4096]{1,0:T(8,128)(2,1)} %refs_0_.3, bf16[256,2048]{1,0:T(8,128)(2,1)} %collective-permute-done.refs_1_, bf16[256,1024]{1,0:T(8,128)(2,1)} %collective-permute-done.2.refs_0_.refs_2_, bf16[256,1024]{1,0:T(8,128)(2,1)} %copy-done.3, ...), custom_call_target="tpu_custom_call" | custom-call | flops 1 | bytes 1 | tf_op jit(solution)/shard_map/pallas_call | solution.py:145
  54.5 6.4 %shard_map.86.local_far_ref.local_ref = f32[3,512,256]{2,1,0:T(8,128)} custom-call(s32[5]{0:T(128)} %stack.109.index_ref, bf16[256,1024]{1,0:T(8,128)(2,1)} %collective-permute-done.2.refs_0_.refs_2_, bf16[256,1024]{1,0:T(8,128)(2,1)} %copy-done.3, bf16[256,1024]{1,0:T(8,128)(2,1)} %copy-done.4, bf16[256,1024]{1,0:T(8,128)(2,1)} %copy-done.5, ...), custom_call_target="tpu_custom_call" | custom-call | flops 1 | bytes 1 | tf_op jit(solution)/shard_map/pallas_call | solution.py:145
  60.9 0.2 collective-permute-done.9.near_ref
  61.1 1.4 collective-permute-start.11
  62.5 15.5 %shard_map.87 = (bf16[256,512]{1,0:T(8,128)(2,1)}, bf16[256,512]{1,0:T(8,128)(2,1)}, bf16[256,512]{1,0:T(8,128)(2,1)}) custom-call(s32[1]{0:T(128)} %bitcast.11.index_ref, f32[3,512,256]{2,1,0:T(8,128)} %shard_map.83.local_near_ref.local_ref, f32[3,512,256]{2,1,0:T(8,128)} %shard_map.86.local_far_ref.local_ref, ...), custom_call_target="tpu_custom_call" | custom-call | flops 1 | bytes 1 | tf_op jit(solution)/shard_map/pallas_call | solution.py:224
  78.1 0.8 copy-done.6
  78.8 2.9 %shard_map.88 = (bf16[256,256]{1,0:T(8,128)(2,1)}, bf16[256,256]{1,0:T(8,128)(2,1)}) custom-call(s32[1]{0:T(128)} %bitcast.11.index_ref, f32[3,512,256]{2,1,0:T(8,128)} %shard_map.86.local_far_ref.local_ref, bf16[1,1024,256]{2,1,0:T(8,128)(2,1)} %copy-done.6, f32[4,1,256]{2,1,0:T(1,128)} %bitcast.32, bf16[256,512]{1,0:T(8,128)(2,1)} %get-tuple-element.46.gate_ref, ...), custom_call_target="tpu_custom_call" | custom-call | flops 1 | bytes 1 | tf_op jit(solution)/shard_map/pallas_call | solution.py:266
  81.8 2.9 %shard_map.89 = (bf16[256,256]{1,0:T(8,128)(2,1)}, bf16[256,256]{1,0:T(8,128)(2,1)}) custom-call(s32[1]{0:T(128)} %bitcast.11.index_ref, f32[3,512,256]{2,1,0:T(8,128)} %shard_map.83.local_near_ref.local_ref, bf16[1,1024,256]{2,1,0:T(8,128)(2,1)} %copy-done.6, f32[4,1,256]{2,1,0:T(1,128)} %bitcast.33, bf16[256,512]{1,0:T(8,128)(2,1)} %get-tuple-element.46.gate_ref, ...), custom_call_target="tpu_custom_call" | custom-call | flops 1 | bytes 1 | tf_op jit(solution)/shard_map/pallas_call | solution.py:266
  84.7 0.7 collective-permute-start.13
  85.4 1.2 collective-permute-start.14
  86.6 0.9 constant_dynamic-update-slice_fusion.3
  87.5 3.6 %collective-permute-done.13 = bf16[256,256]{1,0:T(8,128)(2,1)S(1)} collective-permute-done((bf16[256,256]{1,0:T(8,128)(2,1)S(1)}, bf16[256,256]{1,0:T(8,128)(2,1)S(1)}, u32[]{:S(2)}, u32[]{:S(2)}) %collective-permute-start.13) | collective-permute-done | bytes 131104 | tf_op jit(solution)/shard_map/ppermute | solution.py:384
  91.1 1.9 %collective-permute-done.14 = bf16[256,256]{1,0:T(8,128)(2,1)S(1)} collective-permute-done((bf16[256,256]{1,0:T(8,128)(2,1)S(1)}, bf16[256,256]{1,0:T(8,128)(2,1)S(1)}, u32[]{:S(2)}, u32[]{:S(2)}) %collective-permute-start.14) | collective-permute-done | bytes 131104 | tf_op jit(solution)/shard_map/ppermute | solution.py:384
  93.0 0.7 collective-permute-start.17
  93.7 1.3 collective-permute-start.16
  95.0 4.6 %collective-permute-start.15 = (bf16[256,1024]{1,0:T(8,128)(2,1)S(1)}, bf16[256,1024]{1,0:T(8,128)(2,1)S(1)}, u32[]{:S(2)}, u32[]{:S(2)}) collective-permute-start(bf16[256,1024]{1,0:T(8,128)(2,1)S(1)} %constant_dynamic-update-slice_fusion.own), channel_id=1, source_target_pairs={{0,1},{1,2},{2,3},{4,5},{5,6},{6,7},{8,9},{9,10},{10,11},{12,13},{... | collective-permute-start | bytes 1572872 | tf_op jit(solution)/shard_map/ppermute | solution.py:387
  99.6 1.5 collective-permute-start.20
  101.0 6.8 %collective-permute-done.17.refs_2_ = bf16[256,1024]{1,0:T(8,128)(2,1)S(1)} collective-permute-done((bf16[256,1024]{1,0:T(8,128)(2,1)S(1)}, bf16[256,1024]{1,0:T(8,128)(2,1)S(1)}, u32[]{:S(2)}, u32[]{:S(2)}) %collective-permute-start.17) | collective-permute-done | bytes 524320 | tf_op jit(solution)/shard_map/ppermute | solution.py:384
  107.8 1.6 %collective-permute-done.16.above_1 = bf16[256,1024]{1,0:T(8,128)(2,1)S(1)} collective-permute-done((bf16[256,1024]{1,0:T(8,128)(2,1)S(1)}, bf16[256,1024]{1,0:T(8,128)(2,1)S(1)}, u32[]{:S(2)}, u32[]{:S(2)}) %collective-permute-start.16) | collective-permute-done | bytes 524320 | tf_op jit(solution)/shard_map/ppermute | solution.py:387
  109.4 1.2 collective-permute-done.15.below_1
  110.6 1.5 collective-permute-start.21
  112.1 0.7 collective-permute-start.18
  112.8 1.3 collective-permute-start.19
  114.1 0.1 collective-permute-start.22
  114.2 4.2 %collective-permute-done.20.refs_4_ = bf16[256,1024]{1,0:T(8,128)(2,1)S(1)} collective-permute-done((bf16[256,1024]{1,0:T(8,128)(2,1)}, bf16[256,1024]{1,0:T(8,128)(2,1)S(1)}, u32[]{:S(2)}, u32[]{:S(2)}) %collective-permute-start.20) | collective-permute-done | bytes 524320 | tf_op jit(solution)/shard_map/ppermute | solution.py:384
  118.4 4.9 %collective-permute-done.21.refs_3_ = bf16[256,1024]{1,0:T(8,128)(2,1)} collective-permute-done((bf16[256,1024]{1,0:T(8,128)(2,1)S(1)}, bf16[256,1024]{1,0:T(8,128)(2,1)}, u32[]{:S(2)}, u32[]{:S(2)}) %collective-permute-start.21) | collective-permute-done | bytes 524320 | tf_op jit(solution)/shard_map/ppermute | solution.py:444
  123.4 1.5 collective-permute-start.25
  124.9 5.7 %collective-permute-done.19.above_2 = bf16[256,1024]{1,0:T(8,128)(2,1)} collective-permute-done((bf16[256,1024]{1,0:T(8,128)(2,1)S(1)}, bf16[256,1024]{1,0:T(8,128)(2,1)}, u32[]{:S(2)}, u32[]{:S(2)}) %collective-permute-start.19) | collective-permute-done | bytes 524320 | tf_op jit(solution)/shard_map/ppermute | solution.py:387
  130.6 0.5 collective-permute-start.27
  131.1 4.1 %collective-permute-done.25.refs_5_ = bf16[256,1024]{1,0:T(8,128)(2,1)} collective-permute-done((bf16[256,1024]{1,0:T(8,128)(2,1)S(1)}, bf16[256,1024]{1,0:T(8,128)(2,1)}, u32[]{:S(2)}, u32[]{:S(2)}) %collective-permute-start.25) | collective-permute-done | bytes 524320 | tf_op jit(solution)/shard_map/ppermute | solution.py:444
  135.2 1.5 collective-permute-start.23
  136.7 1.3 collective-permute-start.24
  138.0 0.6 stack.99.index_ref
  138.7 9.5 %shard_map.90 = (f32[256,1024]{1,0:T(8,128)}, bf16[1024,1024]{1,0:T(8,128)(2,1)}) custom-call(s32[11]{0:T(128)} %stack.99.index_ref, bf16[256,1024]{1,0:T(8,128)(2,1)} %copy-done.8, bf16[256,1024]{1,0:T(8,128)(2,1)} %copy-done.11, bf16[256,1024]{1,0:T(8,128)(2,1)} %copy-done.10, bf16[256,1024]{1,0:T(8,128)(2,1)} %copy-done.13, ...), custom_call_target="tpu_custom_call" | custom-call | flops 1 | bytes 1 | tf_op jit(solution)/shard_map/pallas_call | solution.py:328
  148.3 5.1 %collective-permute-done.24.above = bf16[256,1024]{1,0:T(8,128)(2,1)} collective-permute-done((bf16[256,1024]{1,0:T(8,128)(2,1)}, bf16[256,1024]{1,0:T(8,128)(2,1)}, u32[]{:S(2)}, u32[]{:S(2)}) %collective-permute-start.24) | collective-permute-done | bytes 524320 | tf_op jit(solution)/shard_map/ppermute | solution.py:387
  153.4 4.0 %shard_map.91 = bf16[256,1024]{1,0:T(8,128)(2,1)} custom-call(s32[11]{0:T(128)} %stack.99.index_ref, bf16[256,1024]{1,0:T(8,128)(2,1)} %collective-permute-done.23.below, bf16[256,1024]{1,0:T(8,128)(2,1)} %collective-permute-done.24.above, bf16[1024,1024]{1,0:T(8,128)(2,1)} %get-tuple-element.65.weight, f32[256,1024]{1,0:T(8,128)} %get-tuple-element.66.before), custom_call_target="tpu_custom_call" | custom-call | flops 1 | bytes 1 | tf_op jit(solution)/shard_map/pallas_call | solution.py:354
  (62 shorter events, 0.2 us)
Async XLA Ops:
  0.0 11.5 %copy-start = (bf16[4096,4]{0,1:T(4,128)(2,1)S(1)}, bf16[4096,4]{0,1:T(4,128)(2,1)}, u32[]{:S(2)}) copy-start(bf16[4096,4]{0,1:T(4,128)(2,1)} %param.10) | copy-start | bytes 98308
  4.2 7.3 %copy-start.2 = (bf16[256,4096]{1,0:T(8,128)(2,1)S(1)}, bf16[256,4096]{1,0:T(8,128)(2,1)}, u32[]{:S(2)}) copy-start(bf16[256,4096]{1,0:T(8,128)(2,1)} %refs_0_.3) | copy-start | bytes 6291460
  8.1 9.0 %collective-permute-start.1 = (bf16[3,1024,512]{2,1,0:T(8,128)(2,1)}, bf16[3,1024,512]{2,1,0:T(8,128)(2,1)S(1)}, u32[]{:S(2)}, u32[]{:S(2)}) collective-permute-start(bf16[3,1024,512]{2,1,0:T(8,128)(2,1)} %dynamic-slice_bitcast_fusion), channel_id=1, source_target_pairs={{0,4},{4,0},{8,12},{12,8},{1,5},{5,1},{9,13},{13,9},{2,6},{6,2},{1... | collective-permute-start | bytes 9437192 | tf_op jit(solution)/shard_map/ppermute | solution.py:384
  8.5 8.6 %collective-permute-start = (bf16[256,2048]{1,0:T(8,128)(2,1)}, bf16[256,2048]{1,0:T(8,128)(2,1)}, u32[]{:S(2)}, u32[]{:S(2)}) collective-permute-start(bf16[256,2048]{1,0:T(8,128)(2,1)} %constant_dynamic-slice_fusion.2), channel_id=1, source_target_pairs={{0,4},{4,0},{8,12},{12,8},{1,5},{5,1},{9,13},{13,9},{2,6},{6,2},{1... | collective-permute-start | bytes 3145736 | tf_op jit(solution)/shard_map/ppermute | solution.py:384
  8.6 15.4 %collective-permute-start.2 = (bf16[256,1024]{1,0:T(8,128)(2,1)}, bf16[256,1024]{1,0:T(8,128)(2,1)}, u32[]{:S(2)}, u32[]{:S(2)}) collective-permute-start(bf16[256,1024]{1,0:T(8,128)(2,1)} %constant_dynamic-slice_fusion.3), channel_id=1, source_target_pairs={{0,8},{4,12},{8,0},{12,4},{1,9},{5,13},{9,1},{13,5},{2,10},{6,14},... | collective-permute-start | bytes 1572872 | tf_op jit(solution)/shard_map/ppermute | solution.py:384
  12.2 3.1 %collective-permute-start.3 = (f32[4,256]{1,0:T(4,128)S(1)}, f32[4,256]{1,0:T(4,128)S(1)}, u32[]{:S(2)}, u32[]{:S(2)}) collective-permute-start(f32[4,256]{1,0:T(4,128)S(1)} %compare_select_fusion), channel_id=1, source_target_pairs={{0,4},{4,0},{8,12},{12,8},{1,5},{5,1},{9,13},{13,9},{2,6},{6,2},{1... | collective-permute-start | bytes 12296 | tf_op jit(solution)/shard_map/ppermute | solution.py:384
  15.3 8.1 %copy-start.17 = (f32[8,256]{1,0:T(8,128)}, f32[8,256]{1,0:T(8,128)S(1)}, u32[]{:S(2)}) copy-start(f32[8,256]{1,0:T(8,128)S(1)} %pad_maximum_fusion.rate_near_ref) | copy-start | bytes 24580
  15.3 8.7 %collective-permute-start.4 = (f32[8,256]{1,0:T(8,128)S(1)}, f32[8,256]{1,0:T(8,128)S(1)}, u32[]{:S(2)}, u32[]{:S(2)}) collective-permute-start(f32[8,256]{1,0:T(8,128)S(1)} %pad_maximum_fusion.rate_near_ref), channel_id=1, source_target_pairs={{0,8},{4,12},{8,0},{12,4},{1,9},{5,13},{9,1},{13,5},{2,10},{6,14},... | collective-permute-start | bytes 24584 | tf_op jit(solution)/shard_map/ppermute | solution.py:384
  17.1 1.6 %copy-start.1 = (bf16[3,1024,512]{2,1,0:T(8,128)(2,1)}, bf16[3,1024,512]{2,1,0:T(8,128)(2,1)S(1)}, u32[]{:S(2)}) copy-start(bf16[3,1024,512]{2,1,0:T(8,128)(2,1)S(1)} %collective-permute-done.1.refs_3_.refs_5_.refs_7_) | copy-start | bytes 9437188
  24.0 10.1 %copy-start.18 = (f32[8,256]{1,0:T(8,128)}, f32[8,256]{1,0:T(8,128)S(1)}, u32[]{:S(2)}) copy-start(f32[8,256]{1,0:T(8,128)S(1)} %collective-permute-done.4.rate_far_ref) | copy-start | bytes 24580
  24.0 13.7 %collective-permute-start.5 = (bf16[256,1024]{1,0:T(8,128)(2,1)}, bf16[256,1024]{1,0:T(8,128)(2,1)S(1)}, u32[]{:S(2)}, u32[]{:S(2)}) collective-permute-start(bf16[256,1024]{1,0:T(8,128)(2,1)} %collective-permute-done.2.refs_0_.refs_2_), channel_id=1, source_target_pairs={{0,1},{1,0},{2,3},{3,2},{4,5},{5,4},{6,7},{7,6},{8,9},{9,8},{10,11... | collective-permute-start | bytes 1572872 | tf_op jit(solution)/shard_map/ppermute | solution.py:387
  25.9 13.1 %collective-permute-start.6 = (bf16[2,512,256]{2,1,0:T(8,128)(2,1)}, bf16[2,512,256]{2,1,0:T(8,128)(2,1)S(1)}, u32[]{:S(2)}, u32[]{:S(2)}) collective-permute-start(bf16[2,512,256]{2,1,0:T(8,128)(2,1)} %shard_map.82), channel_id=1, source_target_pairs={{0,8},{4,12},{8,0},{12,4},{1,9},{5,13},{9,1},{13,5},{2,10},{6,14},... | collective-permute-start | bytes 1572872 | tf_op jit(solution)/shard_map/ppermute | solution.py:384
  28.0 11.7 %collective-permute-start.7 = (bf16[256,1024]{1,0:T(8,128)(2,1)}, bf16[256,1024]{1,0:T(8,128)(2,1)S(1)}, u32[]{:S(2)}, u32[]{:S(2)}) collective-permute-start(bf16[256,1024]{1,0:T(8,128)(2,1)} %collective-permute-done.2.refs_0_.refs_2_), channel_id=1, source_target_pairs={{0,4},{4,0},{8,12},{12,8},{1,5},{5,1},{9,13},{13,9},{2,6},{6,2},{1... | collective-permute-start | bytes 1572872 | tf_op jit(solution)/shard_map/ppermute | solution.py:384
  37.7 3.2 %copy-start.3 = (bf16[256,1024]{1,0:T(8,128)(2,1)}, bf16[256,1024]{1,0:T(8,128)(2,1)S(1)}, u32[]{:S(2)}) copy-start(bf16[256,1024]{1,0:T(8,128)(2,1)S(1)} %collective-permute-done.5.refs_1_.refs_3_) | copy-start | bytes 1572868
  39.0 15.5 %copy-start.16 = (bf16[2,512,256]{2,1,0:T(8,128)(2,1)}, bf16[2,512,256]{2,1,0:T(8,128)(2,1)S(1)}, u32[]{:S(2)}) copy-start(bf16[2,512,256]{2,1,0:T(8,128)(2,1)S(1)} %collective-permute-done.6.far_ref) | copy-start | bytes 1572868
  39.0 1.9 %collective-permute-start.8 = (bf16[256,1024]{1,0:T(8,128)(2,1)S(1)}, bf16[256,1024]{1,0:T(8,128)(2,1)S(1)}, u32[]{:S(2)}, u32[]{:S(2)}) collective-permute-start(bf16[256,1024]{1,0:T(8,128)(2,1)S(1)} %collective-permute-done.5.refs_1_.refs_3_), channel_id=1, source_target_pairs={{0,4},{4,0},{8,12},{12,8},{1,5},{5,1},{9,13},{13,9},{2,6},{6,2},{1... | collective-permute-start | bytes 1572872 | tf_op jit(solution)/shard_map/ppermute | solution.py:384
  39.7 1.2 copy-start.4
  40.9 0.8 copy-start.5
  46.5 8.0 %collective-permute-start.10 = (bf16[1024,1024]{1,0:T(8,128)(2,1)}, bf16[1024,1024]{1,0:T(8,128)(2,1)S(1)}, u32[]{:S(2)}, u32[]{:S(2)}) collective-permute-start(bf16[1024,1024]{1,0:T(8,128)(2,1)} %refs_0_.4), channel_id=1, source_target_pairs={{0,4},{4,0},{8,12},{12,8},{1,5},{5,1},{9,13},{13,9},{2,6},{6,2},{1... | collective-permute-start | bytes 6291464 | tf_op jit(solution)/shard_map/ppermute | solution.py:384
  46.6 14.5 %collective-permute-start.9 = (bf16[2,512,256]{2,1,0:T(8,128)(2,1)}, bf16[2,512,256]{2,1,0:T(8,128)(2,1)}, u32[]{:S(2)}, u32[]{:S(2)}) collective-permute-start(bf16[2,512,256]{2,1,0:T(8,128)(2,1)} %shard_map.84), channel_id=1, source_target_pairs={{0,8},{4,12},{8,0},{12,4},{1,9},{5,13},{9,1},{13,5},{2,10},{6,14},... | collective-permute-start | bytes 1572872 | tf_op jit(solution)/shard_map/ppermute | solution.py:384
  54.5 6.6 %copy-start.15 = (bf16[1,1024,256]{2,1,0:T(8,128)(2,1)S(1)}, bf16[1,1024,256]{2,1,0:T(8,128)(2,1)}, u32[]{:S(2)}) copy-start(bf16[1,1024,256]{2,1,0:T(8,128)(2,1)} %shard_map.85) | copy-start | bytes 1572868
  54.5 6.4 %copy-start.7 = (bf16[1024,1024]{1,0:T(8,128)(2,1)}, bf16[1024,1024]{1,0:T(8,128)(2,1)S(1)}, u32[]{:S(2)}) copy-start(bf16[1024,1024]{1,0:T(8,128)(2,1)S(1)} %collective-permute-done.10.refs_1_) | copy-start | bytes 6291460
  61.1 16.9 %collective-permute-start.11 = (bf16[1,1024,256]{2,1,0:T(8,128)(2,1)S(1)}, bf16[1,1024,256]{2,1,0:T(8,128)(2,1)S(1)}, u32[]{:S(2)}, u32[]{:S(2)}) collective-permute-start(bf16[1,1024,256]{2,1,0:T(8,128)(2,1)S(1)} %copy-done.15), channel_id=1, source_target_pairs={{0,8},{4,12},{8,0},{12,4},{1,9},{5,13},{9,1},{13,5},{2,10},{6,14},... | collective-permute-start | bytes 1572872 | tf_op jit(solution)/shard_map/ppermute | solution.py:384
  78.1 0.8 copy-start.6
  81.8 3.0 %copy-start.20 = (bf16[256,256]{1,0:T(8,128)(2,1)S(1)}, bf16[256,256]{1,0:T(8,128)(2,1)}, u32[]{:S(2)}) copy-start(bf16[256,256]{1,0:T(8,128)(2,1)} %get-tuple-element.49) | copy-start | bytes 393220
  81.8 3.6 %copy-start.19 = (bf16[256,256]{1,0:T(8,128)(2,1)S(1)}, bf16[256,256]{1,0:T(8,128)(2,1)}, u32[]{:S(2)}) copy-start(bf16[256,256]{1,0:T(8,128)(2,1)} %get-tuple-element.50) | copy-start | bytes 393220
  84.7 2.8 %collective-permute-start.12 = (bf16[256,256]{1,0:T(8,128)(2,1)}, bf16[256,256]{1,0:T(8,128)(2,1)S(1)}, u32[]{:S(2)}, u32[]{:S(2)}) collective-permute-start(bf16[256,256]{1,0:T(8,128)(2,1)} %get-tuple-element.53), channel_id=1, source_target_pairs={{0,4},{4,0},{8,12},{12,8},{1,5},{5,1},{9,13},{13,9},{2,6},{6,2},{1... | collective-permute-start | bytes 393224 | tf_op jit(solution)/shard_map/ppermute | solution.py:384
  84.7 6.4 %collective-permute-start.13 = (bf16[256,256]{1,0:T(8,128)(2,1)S(1)}, bf16[256,256]{1,0:T(8,128)(2,1)S(1)}, u32[]{:S(2)}, u32[]{:S(2)}) collective-permute-start(bf16[256,256]{1,0:T(8,128)(2,1)S(1)} %copy-done.20), channel_id=1, source_target_pairs={{0,8},{4,12},{8,0},{12,4},{1,9},{5,13},{9,1},{13,5},{2,10},{6,14},... | collective-permute-start | bytes 393224 | tf_op jit(solution)/shard_map/ppermute | solution.py:384
  85.4 7.6 %collective-permute-start.14 = (bf16[256,256]{1,0:T(8,128)(2,1)S(1)}, bf16[256,256]{1,0:T(8,128)(2,1)S(1)}, u32[]{:S(2)}, u32[]{:S(2)}) collective-permute-start(bf16[256,256]{1,0:T(8,128)(2,1)S(1)} %copy-done.19), channel_id=1, source_target_pairs={{0,12},{4,8},{8,4},{12,0},{1,13},{5,9},{9,5},{13,1},{2,14},{6,10},... | collective-permute-start | bytes 393224 | tf_op jit(solution)/shard_map/ppermute | solution.py:384
  93.0 45.7 %copy-start.8 = (bf16[256,1024]{1,0:T(8,128)(2,1)}, bf16[256,1024]{1,0:T(8,128)(2,1)S(1)}, u32[]{:S(2)}) copy-start(bf16[256,1024]{1,0:T(8,128)(2,1)S(1)} %constant_dynamic-update-slice_fusion.own) | copy-start | bytes 1572868
  93.0 14.8 %collective-permute-start.17 = (bf16[256,1024]{1,0:T(8,128)(2,1)S(1)}, bf16[256,1024]{1,0:T(8,128)(2,1)S(1)}, u32[]{:S(2)}, u32[]{:S(2)}) collective-permute-start(bf16[256,1024]{1,0:T(8,128)(2,1)S(1)} %get-tuple-element.54), channel_id=1, source_target_pairs={{0,8},{4,12},{8,0},{12,4},{1,9},{5,13},{9,1},{13,5},{2,10},{6,14},... | collective-permute-start | bytes 1572872 | tf_op jit(solution)/shard_map/ppermute | solution.py:384
  93.7 15.7 %collective-permute-start.16 = (bf16[256,1024]{1,0:T(8,128)(2,1)S(1)}, bf16[256,1024]{1,0:T(8,128)(2,1)S(1)}, u32[]{:S(2)}, u32[]{:S(2)}) collective-permute-start(bf16[256,1024]{1,0:T(8,128)(2,1)S(1)} %constant_dynamic-update-slice_fusion.own), channel_id=1, source_target_pairs={{1,0},{2,1},{3,2},{5,4},{6,5},{7,6},{9,8},{10,9},{11,10},{13,12},{... | collective-permute-start | bytes 1572872 | tf_op jit(solution)/shard_map/ppermute | solution.py:387
  95.0 15.6 %collective-permute-start.15 = (bf16[256,1024]{1,0:T(8,128)(2,1)S(1)}, bf16[256,1024]{1,0:T(8,128)(2,1)S(1)}, u32[]{:S(2)}, u32[]{:S(2)}) collective-permute-start(bf16[256,1024]{1,0:T(8,128)(2,1)S(1)} %constant_dynamic-update-slice_fusion.own), channel_id=1, source_target_pairs={{0,1},{1,2},{2,3},{4,5},{5,6},{6,7},{8,9},{9,10},{10,11},{12,13},{... | collective-permute-start | bytes 1572872 | tf_op jit(solution)/shard_map/ppermute | solution.py:387
  99.6 18.9 %collective-permute-start.20 = (bf16[256,1024]{1,0:T(8,128)(2,1)}, bf16[256,1024]{1,0:T(8,128)(2,1)S(1)}, u32[]{:S(2)}, u32[]{:S(2)}) collective-permute-start(bf16[256,1024]{1,0:T(8,128)(2,1)} %get-tuple-element.57), channel_id=1, source_target_pairs={{0,8},{4,12},{8,0},{12,4},{1,9},{5,13},{9,1},{13,5},{2,10},{6,14},... | collective-permute-start | bytes 1572872 | tf_op jit(solution)/shard_map/ppermute | solution.py:384
  107.8 30.9 %copy-start.9 = (bf16[256,1024]{1,0:T(8,128)(2,1)}, bf16[256,1024]{1,0:T(8,128)(2,1)S(1)}, u32[]{:S(2)}) copy-start(bf16[256,1024]{1,0:T(8,128)(2,1)S(1)} %collective-permute-done.17.refs_2_) | copy-start | bytes 1572868
  109.4 29.3 %copy-start.10 = (bf16[256,1024]{1,0:T(8,128)(2,1)}, bf16[256,1024]{1,0:T(8,128)(2,1)S(1)}, u32[]{:S(2)}) copy-start(bf16[256,1024]{1,0:T(8,128)(2,1)S(1)} %collective-permute-done.16.above_1) | copy-start | bytes 1572868
  110.6 28.1 %copy-start.11 = (bf16[256,1024]{1,0:T(8,128)(2,1)}, bf16[256,1024]{1,0:T(8,128)(2,1)S(1)}, u32[]{:S(2)}) copy-start(bf16[256,1024]{1,0:T(8,128)(2,1)S(1)} %collective-permute-done.15.below_1) | copy-start | bytes 1572868
  110.6 12.8 %collective-permute-start.21 = (bf16[256,1024]{1,0:T(8,128)(2,1)S(1)}, bf16[256,1024]{1,0:T(8,128)(2,1)}, u32[]{:S(2)}, u32[]{:S(2)}) collective-permute-start(bf16[256,1024]{1,0:T(8,128)(2,1)S(1)} %collective-permute-done.17.refs_2_), channel_id=1, source_target_pairs={{0,16},{16,0},{1,17},{17,1},{2,18},{18,2},{3,19},{19,3},{4,20},{20... | collective-permute-start | bytes 1572872 | tf_op jit(solution)/shard_map/ppermute | solution.py:444
  112.1 12.8 %collective-permute-start.18 = (bf16[256,1024]{1,0:T(8,128)(2,1)S(1)}, bf16[256,1024]{1,0:T(8,128)(2,1)S(1)}, u32[]{:S(2)}, u32[]{:S(2)}) collective-permute-start(bf16[256,1024]{1,0:T(8,128)(2,1)S(1)} %collective-permute-done.15.below_1), channel_id=1, source_target_pairs={{1,2},{2,3},{5,6},{6,7},{9,10},{10,11},{13,14},{14,15},{17,18},{18... | collective-permute-start | bytes 1572872 | tf_op jit(solution)/shard_map/ppermute | solution.py:387
  112.8 17.8 %collective-permute-start.19 = (bf16[256,1024]{1,0:T(8,128)(2,1)S(1)}, bf16[256,1024]{1,0:T(8,128)(2,1)}, u32[]{:S(2)}, u32[]{:S(2)}) collective-permute-start(bf16[256,1024]{1,0:T(8,128)(2,1)S(1)} %collective-permute-done.16.above_1), channel_id=1, source_target_pairs={{1,0},{2,1},{5,4},{6,5},{9,8},{10,9},{13,12},{14,13},{17,16},{18,1... | collective-permute-start | bytes 1572872 | tf_op jit(solution)/shard_map/ppermute | solution.py:387
  114.1 16.5 %collective-permute-start.22 = (bf16[256,1024]{1,0:T(8,128)(2,1)S(1)}, bf16[256,1024]{1,0:T(8,128)(2,1)S(1)}, u32[]{:S(2)}, u32[]{:S(2)}) collective-permute-start(bf16[256,1024]{1,0:T(8,128)(2,1)S(1)} %collective-permute-done.17.refs_2_), channel_id=1, source_target_pairs={{0,4},{4,0},{8,12},{12,8},{1,5},{5,1},{9,13},{13,9},{2,6},{6,2},{1... | collective-permute-start | bytes 1572872 | tf_op jit(solution)/shard_map/ppermute | solution.py:384
  118.4 20.3 %copy-start.12 = (bf16[256,1024]{1,0:T(8,128)(2,1)}, bf16[256,1024]{1,0:T(8,128)(2,1)S(1)}, u32[]{:S(2)}) copy-start(bf16[256,1024]{1,0:T(8,128)(2,1)S(1)} %collective-permute-done.20.refs_4_) | copy-start | bytes 1572868
  123.4 11.8 %collective-permute-start.25 = (bf16[256,1024]{1,0:T(8,128)(2,1)S(1)}, bf16[256,1024]{1,0:T(8,128)(2,1)}, u32[]{:S(2)}, u32[]{:S(2)}) collective-permute-start(bf16[256,1024]{1,0:T(8,128)(2,1)S(1)} %collective-permute-done.20.refs_4_), channel_id=1, source_target_pairs={{0,16},{16,0},{1,17},{17,1},{2,18},{18,2},{3,19},{19,3},{4,20},{20... | collective-permute-start | bytes 1572872 | tf_op jit(solution)/shard_map/ppermute | solution.py:444
  124.9 13.8 %copy-start.13 = (bf16[256,1024]{1,0:T(8,128)(2,1)}, bf16[256,1024]{1,0:T(8,128)(2,1)S(1)}, u32[]{:S(2)}) copy-start(bf16[256,1024]{1,0:T(8,128)(2,1)S(1)} %collective-permute-done.18.below_2) | copy-start | bytes 1572868
  130.6 4.6 %copy-start.14 = (bf16[256,1024]{1,0:T(8,128)(2,1)}, bf16[256,1024]{1,0:T(8,128)(2,1)S(1)}, u32[]{:S(2)}) copy-start(bf16[256,1024]{1,0:T(8,128)(2,1)S(1)} %collective-permute-done.22.refs_6_) | copy-start | bytes 1572868
  130.6 8.0 %collective-permute-start.26 = (bf16[256,1024]{1,0:T(8,128)(2,1)}, bf16[256,1024]{1,0:T(8,128)(2,1)}, u32[]{:S(2)}, u32[]{:S(2)}) collective-permute-start(bf16[256,1024]{1,0:T(8,128)(2,1)} %collective-permute-done.21.refs_3_), channel_id=1, source_target_pairs={{0,4},{4,0},{8,12},{12,8},{1,5},{5,1},{9,13},{13,9},{2,6},{6,2},{1... | collective-permute-start | bytes 1572872 | tf_op jit(solution)/shard_map/ppermute | solution.py:384
  130.6 8.0 %collective-permute-start.27 = (bf16[256,1024]{1,0:T(8,128)(2,1)S(1)}, bf16[256,1024]{1,0:T(8,128)(2,1)}, u32[]{:S(2)}, u32[]{:S(2)}) collective-permute-start(bf16[256,1024]{1,0:T(8,128)(2,1)S(1)} %collective-permute-done.20.refs_4_), channel_id=1, source_target_pairs={{0,4},{4,0},{8,12},{12,8},{1,5},{5,1},{9,13},{13,9},{2,6},{6,2},{1... | collective-permute-start | bytes 1572872 | tf_op jit(solution)/shard_map/ppermute | solution.py:384
  135.2 3.4 %collective-permute-start.28 = (bf16[256,1024]{1,0:T(8,128)(2,1)}, bf16[256,1024]{1,0:T(8,128)(2,1)}, u32[]{:S(2)}, u32[]{:S(2)}) collective-permute-start(bf16[256,1024]{1,0:T(8,128)(2,1)} %collective-permute-done.25.refs_5_), channel_id=1, source_target_pairs={{0,4},{4,0},{8,12},{12,8},{1,5},{5,1},{9,13},{13,9},{2,6},{6,2},{1... | collective-permute-start | bytes 1572872 | tf_op jit(solution)/shard_map/ppermute | solution.py:384
  135.2 13.0 %collective-permute-start.23 = (bf16[256,1024]{1,0:T(8,128)(2,1)S(1)}, bf16[256,1024]{1,0:T(8,128)(2,1)}, u32[]{:S(2)}, u32[]{:S(2)}) collective-permute-start(bf16[256,1024]{1,0:T(8,128)(2,1)S(1)} %collective-permute-done.18.below_2), channel_id=1, source_target_pairs={{2,3},{6,7},{10,11},{14,15},{18,19},{22,23},{26,27},{30,31}} | collective-permute-start | bytes 1572872 | tf_op jit(solution)/shard_map/ppermute | solution.py:387
  136.7 16.7 %collective-permute-start.24 = (bf16[256,1024]{1,0:T(8,128)(2,1)}, bf16[256,1024]{1,0:T(8,128)(2,1)}, u32[]{:S(2)}, u32[]{:S(2)}) collective-permute-start(bf16[256,1024]{1,0:T(8,128)(2,1)} %collective-permute-done.19.above_2), channel_id=1, source_target_pairs={{1,0},{5,4},{9,8},{13,12},{17,16},{21,20},{25,24},{29,28}} | collective-permute-start | bytes 1572872 | tf_op jit(solution)/shard_map/ppermute | solution.py:387

commit v5 on v4

--- a/solution.py
+++ b/solution.py
@@ -108,47 +108,53 @@
     return lax.dot_general(a, b, (((0,), (0,)), ((), ())), preferred_element_type=F32)
 
 
-def project_kernel(pairs, whole_pairs, index_ref, *refs):
+CHIP, CORE, HEAD, PLACE, SEQ, LAST, PARTS, BLOCKS, ORDER = 0, 1, 2, 3, 4, 5, 6, 10, 14
+
+
+def project_kernel(wholes, pairs, index_ref, *refs):
     keep_ref, given_ref, out_ref = refs[-3:]
     depth = keep_ref.shape[1]
-    place = 0
-    for pair in range(pairs):
-        order = index_ref[3 + pair]
-        if pair < whole_pairs:
-            both = refs[place]
-            place += 1
-            first = both[:, pl.ds(pl.multiple_of(order * depth, depth), depth)]
-            second = both[:, pl.ds(pl.multiple_of((1 - order) * depth, depth), depth)]
-        else:
-            low, high = refs[place][...], refs[place + 1][...]
-            place += 2
-            first = jnp.where(order == 1, high, low)
-            second = jnp.where(order == 1, low, high)
-        rows = first.shape[0]
-        total = dot(first, keep_ref[0]) + dot(second, given_ref[0])
-        out_ref[0, pair * rows : (pair + 1) * rows, :] = total.astype(out_ref.dtype)
-
-
-def project(index, whole, pairs, weight, given, size, start, count, dtype):
-    rows = whole[0].shape[0] if whole else pairs[0][0].shape[0]
+    core = index_ref[CORE]
+    mine = pl.ds(pl.multiple_of(core * depth, depth), depth)
+    others = pl.ds(pl.multiple_of((1 - core) * depth, depth), depth)
+    rows = refs[0].shape[0]
+
+    def store(block, total):
+        out_ref[0, block * rows : (block + 1) * rows, :] = total.astype(out_ref.dtype)
+
+    for block in range(wholes):
+        ref = refs[block]
+        store(block, dot(ref[:, mine], keep_ref[0]) + dot(ref[:, others], given_ref[0]))
+    for swapped in range(2 if pairs else 0):
+
+        @pl.when(index_ref[ORDER] == swapped)
+        def _():
+            for pair in range(pairs):
+                first = refs[wholes + 2 * pair + swapped]
+                second = refs[wholes + 2 * pair + 1 - swapped]
+                store(wholes + pair, dot(first[...], keep_ref[0]) + dot(second[...], given_ref[0]))
+
+
+def project(index, whole, pairs, weight, given, size, own, start, count, dtype):
+    rows = (whole + [block for pair in pairs for block in pair])[0].shape[0]
     depth = weight.shape[1]
     number = len(whole) + len(pairs)
-    specs = []
-    for place in range(len(whole)):
-        if place == 0:
-            specs.append(pl.BlockSpec((rows, 2 * depth), lambda i, idx: (0, idx[0])))
-        else:
-            specs.append(pl.BlockSpec((rows, 2 * depth), lambda i, idx: (0, 0)))
-    specs += [pl.BlockSpec((rows, depth), lambda i, idx: (0, 0))] * (2 * len(pairs))
-    specs.append(pl.BlockSpec((1, depth, size), lambda i, idx: ((start + i) % 3, 0, idx[1])))
-    specs.append(pl.BlockSpec((1, depth, size), lambda i, idx: ((start + i) % 3, 0, idx[2])))
+
+    def which(idx):
+        return idx[CHIP] if own else 1 - idx[CHIP]
+
     return pl.pallas_call(
-        functools.partial(project_kernel, number, len(whole)),
+        functools.partial(project_kernel, len(whole), len(pairs)),
         out_shape=jax.ShapeDtypeStruct((count, number * rows, size), dtype),
         grid_spec=pltpu.PrefetchScalarGridSpec(
             num_scalar_prefetch=1,
             grid=(count,),
-            in_specs=specs,
+            in_specs=[pl.BlockSpec((rows, 2 * depth), lambda i, idx: (0, idx[CHIP]))] * len(whole)
+            + [pl.BlockSpec((rows, depth), lambda i, idx: (0, 0))] * (2 * len(pairs))
+            + [
+                pl.BlockSpec((1, depth, size), lambda i, idx: ((start + i) % 3, 0, 2 * idx[CORE] + which(idx))),
+                pl.BlockSpec((1, depth, size), lambda i, idx: ((start + i) % 3, 0, which(idx))),
+            ],
             out_specs=pl.BlockSpec((1, number * rows, size), lambda i, idx: (i, 0, 0)),
         ),
         compiler_params=params(),
@@ -174,7 +180,7 @@
         keys = rms_scale(keys).astype(BF16)
         values = (local_ref[1, here, :] + other[1, here, :].astype(F32)).astype(BF16)
         rate_ref = rate_near_ref if block < 2 else rate_far_ref
-        rate = jnp.broadcast_to(rate_ref[pl.ds((block % 2) * 4 + index_ref[0], 1), :], (8, rows)).T[:, :1]
+        rate = jnp.broadcast_to(rate_ref[pl.ds((block % 2) * 4 + index_ref[HEAD], 1), :], (8, rows)).T[:, :1]
         scaled = (rate * values.astype(F32)).astype(BF16)
         gate = dot(keys, gate_w)
         up = dot(keys, up_w)
@@ -211,7 +217,7 @@
     down_out[...] = (down_w.astype(F32) + current[2]).astype(BF16)
 
 
-def update(head, local_near, local_far, near, far, rates_near, rates_far, fast_gate, fast_up, fast_down):
+def update(index, local_near, local_far, near, far, rates_near, rates_far, fast_gate, fast_up, fast_down):
     size, hidden = fast_gate.shape[1:]
     total = 2 * near.shape[1]
 
@@ -219,7 +225,7 @@
         zeros = (0,) * array.ndim
         return pl.BlockSpec(array.shape, lambda i, idx: zeros)
 
-    pick = pl.BlockSpec((1, size, hidden), lambda i, idx: (idx[0], 0, 0))
+    pick = pl.BlockSpec((1, size, hidden), lambda i, idx: (idx[HEAD], 0, 0))
     out = jax.ShapeDtypeStruct((size, hidden), BF16)
     return pl.pallas_call(
         update_kernel,
@@ -243,7 +249,7 @@
         ),
         compiler_params=params(),
         cost_estimate=pl.CostEstimate(flops=1, bytes_accessed=1, transcendentals=0),
-    )(head.reshape(1).astype(jnp.int32), local_near, local_far, near, far, rates_near, rates_far, fast_gate, fast_up, fast_down)
+    )(index, local_near, local_far, near, far, rates_near, rates_far, fast_gate, fast_up, fast_down)
 
 
 def read_kernel(index_ref, local_ref, other_ref, gain_ref, gate_ref, up_ref, down_ref, *out_refs):
@@ -259,7 +265,7 @@
         out_ref[...] = (rms_scale(read) * gain_ref[0]).astype(BF16)
 
 
-def read_out(head, local, other, which, gain, gate, up, down):
+def read_out(index, local, other, which, gain, gate, up, down):
     size, hidden = gate.shape
     rows = other.shape[1] // 4
     weight = pl.BlockSpec((size, hidden), lambda i, idx: (0, 0))
@@ -272,7 +278,7 @@
             in_specs=[
                 pl.BlockSpec((1, 2 * rows, size), lambda i, idx: (2, 0, 0)),
                 pl.BlockSpec((1, 2 * rows, size), lambda i, idx: (0, which, 0)),
-                pl.BlockSpec((1, 1, size), lambda i, idx: (idx[0], 0, 0)),
+                pl.BlockSpec((1, 1, size), lambda i, idx: (idx[HEAD], 0, 0)),
                 weight,
                 weight,
                 weight,
@@ -281,14 +287,14 @@
         ),
         compiler_params=params(),
         cost_estimate=pl.CostEstimate(flops=1, bytes_accessed=1, transcendentals=0),
-    )(head.reshape(1).astype(jnp.int32), local, other, gain, gate, up, down)
+    )(index, local, other, gain, gate, up, down)
 
 
 def mix_kernel(index_ref, own, below_1, above_1, below_2, above_2, *refs):
     own_w, peer_w = refs[:2]
     parts, peer_parts = refs[2:6], refs[6:10]
     out_ref, last_ref, held = refs[10:]
-    place, seq, last = index_ref[0], index_ref[1], index_ref[2]
+    place, seq, last = index_ref[PLACE], index_ref[SEQ], index_ref[LAST]
     size = parts[0].shape[0]
 
     @pl.when(pl.program_id(0) == 0)
@@ -305,8 +311,8 @@
             if k < 2:
                 ref, head, here = (own_w, peer_w)[k], part, pl.ds(part * size, size)
             else:
-                ref, head, here = (parts, peer_parts)[k - 2][part], index_ref[3 + part], pl.ds(0, size)
-            column = pl.multiple_of(index_ref[7 + head] * size, size)
+                ref, head, here = (parts, peer_parts)[k - 2][part], index_ref[PARTS + part], pl.ds(0, size)
+            column = pl.multiple_of(index_ref[BLOCKS + head] * size, size)
             term = dot(held[owner, :, pl.ds(column, size)], ref[here, :])
             total = term if total is None else total + term
 
@@ -341,7 +347,7 @@
 
 
 def last_kernel(index_ref, below, above, weight, before, out_ref):
-    block = jnp.where(index_ref[0] == 0, above[...], below[...])
+    block = jnp.where(index_ref[PLACE] == 0, above[...], below[...])
     out_ref[...] = (before[...] + dot(block, weight[...])).astype(out_ref.dtype)
 
 
@@ -377,7 +383,6 @@
     chip, core = seq >> 1, seq & 1
     place = lax.axis_index("head")
     side = lax.axis_index("groups")
-    odd = place & 1
     head = 2 * core + chip
 
     def across(array, bit):
@@ -386,53 +391,54 @@
     def hop(array, links):
         return lax.ppermute(array, "head", links)
 
+    values = [chip, core, head, place, seq, jnp.where(place == 0, 3, 0)]
+    values += [2 * side, 2 * (1 - side), 2 * side + 1, 2 * (1 - side) + 1]
+    values += [((other >> 1) ^ core) + 2 * ((other & 1) ^ chip) for other in range(4)]
+    odd = place & 1
+    values += [core ^ odd]
+    index = jnp.stack(values).astype(jnp.int32)
+
     leaving = lax.dynamic_slice(tokens, (0, (2 * (1 - chip) + odd) * depth), (rows, depth))
     direct = across(leaving, 2)
-    tokens, leaving = lax.optimization_barrier((tokens, leaving))
-    shared = lax.dynamic_slice(tokens, (0, chip * 2 * depth), (rows, 2 * depth))
-    peer = across(shared, 1)
-    weight = jnp.transpose(after(qkv_weight, shared), (1, 0, 2))
-
+    peer = across(tokens, 1)
+    weight = jnp.transpose(after(qkv_weight, leaving), (1, 0, 2))
     given = across(lax.dynamic_slice(weight, (0, 0, (1 - core) * 2 * size), (3, depth, 2 * size)), 1)
-
-    def order(which, *flags):
-        return jnp.stack([chip, 2 * core + which, which] + list(flags)).astype(jnp.int32)
+    near = [tokens, peer]
+    half = out_weight.shape[0] // 2
+    out_half = lax.dynamic_slice(after(out_weight, leaving), (side * half, 0), (half, out_weight.shape[1]))
+    out_first, out_later = out_half[:size], out_half[size:]
 
     activity = lax.dot_general(rate_weight, tokens, (((0,), (1,)), ((), ())), preferred_element_type=F32)
     rates_own = jax.nn.softplus(activity)
     rates_near = jnp.concatenate([rates_own, across(rates_own, 1)])
     rates_far = across(rates_near, 2)
 
-    far_flag = core ^ odd
-    send_near = project(order(1 - chip, core, core), [tokens, peer], [], weight, given, size, 1, 2, BF16)
+    given = after(given, out_first, out_later, rates_near)
+    send_near = project(index, near, [], weight, given, size, False, 1, 2, BF16)
     got_far = across(send_near, 2)
     direct = after(direct, send_near, rates_far)
     handed = hop(direct, [(i, i ^ 1) for i in range(4)])
     direct_peer = across(direct, 1)
-    local_near = project(order(chip, core, core), [tokens, peer], [], weight, after(given, direct), size, 1, 3, F32)
-    half = out_weight.shape[0] // 2
-    out_half = lax.dynamic_slice(after(out_weight, direct), (side * half, 0), (half, out_weight.shape[1]))
-    out_first, out_later = out_half[:size], out_half[size:]
-
-    handed = after(handed, local_near, got_far, out_first, out_later)
-    handed_peer = across(handed, 1)
-    far = [(direct, handed), (direct_peer, handed_peer)]
-    send_far = project(order(1 - chip, far_flag, far_flag), [], far, weight, given, size, 1, 2, BF16)
+    local_near = project(index, near, [], weight, after(given, direct), size, True, 1, 3, F32)
+    handed = after(handed, local_near, got_far)
+    far = [(direct, handed), (direct_peer, across(handed, 1))]
+    send_far = project(index, [], far, weight, given, size, False, 1, 2, BF16)
     got_near = across(send_far, 2)
-    everything = order(1 - chip, core, core, far_flag, far_flag)
-    send_query = project(everything, [tokens, peer], far, weight, after(given, send_far), size, 0, 1, BF16)
+    send_query = project(index, near, far, weight, after(given, send_far), size, False, 0, 1, BF16)
     out_peer = across(after(out_weight, send_far), 1)
     held = after(given, send_query, out_peer)
-    local_far = project(order(chip, far_flag, far_flag), [], far, weight, held, size, 1, 3, F32)
-    send_query = after(send_query, got_near, local_far)
+    local_far = project(index, [], far, weight, held, size, True, 1, 3, F32)
+    send_query, out_first, _, _ = lax.optimization_barrier((send_query, out_first, got_near, local_far))
     got_query = across(send_query, 2)
+    first_x = across(out_first, 2)
 
     rates = (rates_near, rates_far)
-    fresh = update(head, local_near, local_far, got_near, got_far, *rates, fast_gate, fast_up, fast_down)
+    fresh = update(index, local_near, local_far, got_near, got_far, *rates, fast_gate, fast_up, fast_down)
     gain = out_gain.reshape(4, 1, size)
-    far_reads = read_out(head, local_far, got_query, 0, gain, *fresh)
-    near_reads = read_out(head, local_near, after(got_query, *far_reads), 1, gain, *fresh)
-    pieces = [near_reads[0], across(near_reads[1], 1), across(far_reads[0], 2), across(far_reads[1], 3)]
+    far_reads = read_out(index, local_far, got_query, 0, gain, *fresh)
+    near_reads = read_out(index, local_near, after(got_query, *far_reads), 1, gain, *fresh)
+    *far_reads, near_read, first_x = lax.optimization_barrier((*far_reads, near_reads[1], first_x))
+    pieces = [near_reads[0], across(near_read, 1), across(far_reads[0], 2), across(far_reads[1], 3)]
     shard = jnp.concatenate(pieces, axis=1)
 
     def both(number, below, above):
@@ -443,26 +449,17 @@
     def swap_groups(array):
         return lax.ppermute(array, "groups", [(0, 1), (1, 0)])
 
-    first_x = across(after(out_first, shard), 2)
     later_x = across(after(out_later, shard), 2)
+    first_y = swap_groups(after(first_x, shard))
     below_1, above_1 = both(0, shard, shard)
-    below_1, above_1, first_x = lax.optimization_barrier((below_1, above_1, first_x))
-    first_y = swap_groups(first_x)
+    below_1, above_1, later_x, first_y = lax.optimization_barrier((below_1, above_1, later_x, first_y))
+    later_y = swap_groups(later_x)
+    first_y_peer, later_x_peer = across(first_y, 1), across(later_x, 1)
     below_2, above_2 = both(1, below_1, above_1)
-    later_x = after(later_x, first_y)
-    later_y = swap_groups(later_x)
-    first_x_peer = across(first_x, 1)
-    below_2, above_2, held_x, held_y, first_x_peer = lax.optimization_barrier(
-        (below_2, above_2, later_x, first_y, first_x_peer)
-    )
+    below_2, above_2, later_y, first_x = lax.optimization_barrier((below_2, above_2, later_y, first_x))
     below_3, above_3 = both(2, below_2, above_2)
-    first_y_peer, later_x_peer = across(held_y, 1), across(held_x, 1)
-    later_y_peer = across(later_y, 1)
-
-    values = [place, seq, jnp.where(place == 0, 3, 0)]
-    values += [2 * side, 2 * (1 - side), 2 * side + 1, 2 * (1 - side) + 1]
-    values += [((head_ >> 1) ^ core) + 2 * ((head_ & 1) ^ chip) for head_ in range(4)]
-    index = jnp.stack(values).astype(jnp.int32)
+    first_x_peer, later_y_peer = across(first_x, 1), across(later_y, 1)
+
     shards = [shard, below_1, above_1, below_2, above_2]
     parts = [first_x, first_y, later_x, later_y]
     peer_parts = [first_x_peer, first_y_peer, later_x_peer, later_y_peer]

time: 158 us -> 156 us (0.987)
  local copies, waits for them, and re-layouts: 18.2 us -> 14.3 us
  starting transfers between devices: 29.1 us -> 25.7 us
  Pallas kernels: 62.2 us -> 64.7 us
  waiting for transfers between devices: 46.9 us -> 48.5 us
  matrix products: 0.66 us -> 2.25 us
    ppermute x7, waiting for transfers between devices: 15.1 us -> 28.2 us  [hop(): return lax.ppermute(array, 'head', links)]
    ppermute x2, waiting for transfers between devices: 9 us -> 0.26 us  [swap_groups(): return lax.ppermute(array, 'groups', [(0, 1), (1, 0)])]
    another operation x5 -> x0, local copies, waits for them, and re-layouts: 3.17 us -> none  [order(): jnp.stack([chip, 2 * core + which, which] + list(flags)).astype(jnp.int32)]
    ppermute x20, waiting for transfers between devices: 22.8 us -> 20 us  [across(): return lax.ppermute(array, 'seq', [(i, i ^ bit) for i in range(4)])]
    dynamic_slice x1 -> x0, local copies, waits for them, and re-layouts: 2.32 us -> none  [chip_plan(): shared = lax.dynamic_slice(tokens, (0, chip * 2 * depth), (rows, 2 * depth))]
    unnamed x45 -> x67, local copies, waits for them, and re-layouts: 4.26 us -> 5.91 us
    dot_general x1, matrix products: 0.66 us -> 2.25 us  [chip_plan(): lax.dot_general(rate_weight, tokens, (((0,), (1,)), ((), ())), preferred_...]
  transfers between devices with their start and end apart: 29 -> 29, of which waited for: 16 -> 15; matrix products, arithmetic and copies ran while one was open for 5% -> 4% of each run, Pallas kernels for 30% -> 36%
where the time goes in v5:
time: 156 us
  Pallas kernels  64.7 us (41%)
  waiting for transfers between devices  48.5 us (31%)
  starting transfers between devices  25.7 us (16%)
  local copies, waits for them, and re-layouts  14.3 us (9%)
  matrix products  2.25 us (1%)
    ppermute x7, waiting for transfers between devices, hop(): return lax.ppermute(array, 'head', links)  28.2 us
    pallas_call x5, Pallas kernels, project(): pl.pallas_call(functools.partial(project_kernel, len(whole), len(pairs)),...  27.8 us
    ppermute x20, waiting for transfers between devices, across(): return lax.ppermute(array, 'seq', [(i, i ^ bit) for i in range(4)])  20 us
    pallas_call x1, Pallas kernels, update(): pl.pallas_call(update_kernel, out_shape=[out] * 3, grid_spec=pltpu.Prefet...  16.2 us
    ppermute x20, starting transfers between devices, across(): return lax.ppermute(array, 'seq', [(i, i ^ bit) for i in range(4)])  12.1 us
    ppermute x7, starting transfers between devices, hop(): return lax.ppermute(array, 'head', links)  11.4 us
    pallas_call x1, Pallas kernels, mix(): pl.pallas_call(mix_kernel, out_shape=[jax.ShapeDtypeStruct((rows, columns...  9.48 us
    pallas_call x2, Pallas kernels, read_out(): pl.pallas_call(read_kernel, out_shape=[jax.ShapeDtypeStruct((rows, size),...  7.28 us
  transfers between devices with their start and end apart: 29, of which 15 were waited for; matrix products, arithmetic and copies ran while one was open for 4% of the time, Pallas kernels for 36%

profile of v5, /device:TPU:0, one launch (start us, length us, event | category | flops | bytes accessed | tf_op | source)
XLA Modules:
  0.0 155.8 jit_solution(16546482889158646061)
XLA Ops:
  0.0 1.9 %constant_dynamic-slice_fusion.2 = bf16[256,1024]{1,0:T(8,128)(2,1)} fusion(bf16[256,4096]{1,0:T(8,128)(2,1)} %refs_0_.6, s32[]{:T(128)S(6)} %select_n.18), kind=kLoop, calls=%fused_computation.9 | loop fusion | bytes 1048580 | tf_op jit(solution)/shard_map/dynamic_slice | solution.py:401
  1.9 3.7 %dynamic-slice_bitcast_fusion = bf16[3,1024,512]{2,1,0:T(8,128)(2,1)} fusion(bf16[1024,3,1024]{2,0,1:T(8,128)(2,1)} %param.9, s32[]{:T(128)S(6)} %select_n.19), kind=kLoop, calls=%fused_computation | loop fusion | bytes 6291460 | tf_op jit(solution)/shard_map/dynamic_slice | solution.py:405
  5.6 0.5 collective-permute-start.1
  6.0 0.1 collective-permute-start
  6.1 2.9 %collective-permute-start.3 = (bf16[256,1024]{1,0:T(8,128)(2,1)}, bf16[256,1024]{1,0:T(8,128)(2,1)}, u32[]{:S(2)}, u32[]{:S(2)}) collective-permute-start(bf16[256,1024]{1,0:T(8,128)(2,1)} %constant_dynamic-slice_fusion.2), channel_id=1, source_target_pairs={{0,8},{4,12},{8,0},{12,4},{1,9},{5,13},{9,1},{13,5},{2,10},{6,14},... | collective-permute-start | bytes 1572872 | tf_op jit(solution)/shard_map/ppermute | solution.py:389
  9.0 2.3 %compare_select_fusion = f32[4,256]{1,0:T(4,128)S(1)} fusion(bf16[4096,4]{0,1:T(4,128)(2,1)S(1)} %copy-done, bf16[256,4096]{1,0:T(8,128)(2,1)} %refs_0_.6), kind=kOutput, calls=%fused_computation.1 | convolution fusion | flops 8394752 | bytes 2134016 | tf_op jit(solution)/shard_map/dot_general | solution.py:411
  11.3 0.1 collective-permute-start.2
  11.4 2.9 %collective-permute-done.2 = f32[4,256]{1,0:T(4,128)S(1)} collective-permute-done((f32[4,256]{1,0:T(4,128)S(1)}, f32[4,256]{1,0:T(4,128)S(1)}, u32[]{:S(2)}, u32[]{:S(2)}) %collective-permute-start.2) | collective-permute-done | bytes 4128 | tf_op jit(solution)/shard_map/ppermute | solution.py:389
  14.3 1.5 collective-permute-start.4
  15.8 2.2 %constant_dynamic-slice_fusion.1 = (bf16[256,1024]{1,0:T(8,128)(2,1)}, bf16[256,1024]{1,0:T(8,128)(2,1)}) fusion(bf16[1024,1024]{1,0:T(8,128)(2,1)} %refs_0_.7, s32[]{:T(128)S(6)} %add.49, s32[]{:T(128)S(6)} %select_n.20), kind=kLoop, calls=%fused_computation.8 | loop fusion | bytes 2097160 | tf_op jit(solution)/shard_map/slice | solution.py:409
  18.0 0.6 stack.63.index_ref
  18.6 1.6 %copy-done.1 = bf16[3,1024,512]{2,1,0:T(8,128)(2,1)} copy-done((bf16[3,1024,512]{2,1,0:T(8,128)(2,1)}, bf16[3,1024,512]{2,1,0:T(8,128)(2,1)S(1)}, u32[]{:S(2)}) %copy-start.1) | copy-done | bytes 3145752
  20.2 4.8 %shard_map.82 = bf16[2,512,256]{2,1,0:T(8,128)(2,1)} custom-call(s32[15]{0:T(128)} %stack.63.index_ref, bf16[256,4096]{1,0:T(8,128)(2,1)} %refs_0_.6, bf16[256,4096]{1,0:T(8,128)(2,1)} %collective-permute-done.refs_1_, bf16[3,1024,1024]{2,1,0:T(8,128)(2,1)} %bitcast.21, bf16[3,1024,512]{2,1,0:T(8,128)(2,1)} %copy-done.1), custom_call_target="tpu_custom_call" | custom-call | flops 1 | bytes 1 | tf_op jit(solution)/shard_map/pallas_call | solution.py:146
  25.0 1.6 %collective-permute-start.5 = (bf16[256,1024]{1,0:T(8,128)(2,1)}, bf16[256,1024]{1,0:T(8,128)(2,1)S(1)}, u32[]{:S(2)}, u32[]{:S(2)}) collective-permute-start(bf16[256,1024]{1,0:T(8,128)(2,1)} %collective-permute-done.3.refs_0_.refs_2_), channel_id=1, source_target_pairs={{0,1},{1,0},{2,3},{3,2},{4,5},{5,4},{6,7},{7,6},{8,9},{9,8},{10,11... | collective-permute-start | bytes 1572872 | tf_op jit(solution)/shard_map/ppermute | solution.py:392
  26.7 0.5 collective-permute-start.6
  27.2 6.2 %shard_map.83.local_near_ref.local_ref = f32[3,512,256]{2,1,0:T(8,128)} custom-call(s32[15]{0:T(128)} %stack.63.index_ref, bf16[256,4096]{1,0:T(8,128)(2,1)} %refs_0_.6, bf16[256,4096]{1,0:T(8,128)(2,1)} %collective-permute-done.refs_1_, bf16[3,1024,1024]{2,1,0:T(8,128)(2,1)} %bitcast.22, bf16[3,1024,512]{2,1,0:T(8,128)(2,1)} %copy-done.1), custom_call_target="tpu_custom_call" | custom-call | flops 1 | bytes 1 | tf_op jit(solution)/shard_map/pallas_call | solution.py:146
  33.4 5.6 %collective-permute-done.5.refs_1_.refs_3_ = bf16[256,1024]{1,0:T(8,128)(2,1)S(1)} collective-permute-done((bf16[256,1024]{1,0:T(8,128)(2,1)}, bf16[256,1024]{1,0:T(8,128)(2,1)S(1)}, u32[]{:S(2)}, u32[]{:S(2)}) %collective-permute-start.5) | collective-permute-done | bytes 524320 | tf_op jit(solution)/shard_map/ppermute | solution.py:392
  39.0 1.3 collective-permute-done.6.far_ref
  40.3 1.9 %collective-permute-done.8.refs_3_.refs_5_ = bf16[256,1024]{1,0:T(8,128)(2,1)S(1)} collective-permute-done((bf16[256,1024]{1,0:T(8,128)(2,1)S(1)}, bf16[256,1024]{1,0:T(8,128)(2,1)S(1)}, u32[]{:S(2)}, u32[]{:S(2)}) %collective-permute-start.8) | collective-permute-done | bytes 524320 | tf_op jit(solution)/shard_map/ppermute | solution.py:389
  42.2 0.8 copy-done.4
  43.0 4.7 %shard_map.84 = bf16[2,512,256]{2,1,0:T(8,128)(2,1)} custom-call(s32[15]{0:T(128)} %stack.63.index_ref, bf16[256,1024]{1,0:T(8,128)(2,1)} %collective-permute-done.3.refs_0_.refs_2_, bf16[256,1024]{1,0:T(8,128)(2,1)} %copy-done.2, bf16[256,1024]{1,0:T(8,128)(2,1)} %copy-done.3, bf16[256,1024]{1,0:T(8,128)(2,1)} %copy-done.4, ...), custom_call_target="tpu_custom_call" | custom-call | flops 1 | bytes 1 | tf_op jit(solution)/shard_map/pallas_call | solution.py:146
  47.8 0.1 collective-permute-start.10
  47.9 0.5 collective-permute-start.9
  48.4 5.5 %shard_map.85 = bf16[1,1024,256]{2,1,0:T(8,128)(2,1)} custom-call(s32[15]{0:T(128)} %stack.63.index_ref, bf16[256,4096]{1,0:T(8,128)(2,1)} %refs_0_.6, bf16[256,4096]{1,0:T(8,128)(2,1)} %collective-permute-done.refs_1_, bf16[256,1024]{1,0:T(8,128)(2,1)} %collective-permute-done.3.refs_0_.refs_2_, bf16[256,1024]{1,0:T(8,128)(2,1)} %copy-done.2, ...), custom_call_target="tpu_custom_call" | custom-call | flops 1 | bytes 1 | tf_op jit(solution)/shard_map/pallas_call | solution.py:146
  54.0 6.6 %shard_map.86.local_far_ref.local_ref = f32[3,512,256]{2,1,0:T(8,128)} custom-call(s32[15]{0:T(128)} %stack.63.index_ref, bf16[256,1024]{1,0:T(8,128)(2,1)} %collective-permute-done.3.refs_0_.refs_2_, bf16[256,1024]{1,0:T(8,128)(2,1)} %copy-done.2, bf16[256,1024]{1,0:T(8,128)(2,1)} %copy-done.3, bf16[256,1024]{1,0:T(8,128)(2,1)} %copy-done.4, ...), custom_call_target="tpu_custom_call" | custom-call | flops 1 | bytes 1 | tf_op jit(solution)/shard_map/pallas_call | solution.py:146
  60.6 1.7 %collective-permute-done.9.near_ref = bf16[2,512,256]{2,1,0:T(8,128)(2,1)S(1)} collective-permute-done((bf16[2,512,256]{2,1,0:T(8,128)(2,1)}, bf16[2,512,256]{2,1,0:T(8,128)(2,1)S(1)}, u32[]{:S(2)}, u32[]{:S(2)}) %collective-permute-start.9) | collective-permute-done | bytes 524320 | tf_op jit(solution)/shard_map/ppermute | solution.py:389
  62.3 0.5 collective-permute-start.11
  62.8 1.5 collective-permute-start.12
  64.3 16.2 %shard_map.87 = (bf16[256,512]{1,0:T(8,128)(2,1)}, bf16[256,512]{1,0:T(8,128)(2,1)}, bf16[256,512]{1,0:T(8,128)(2,1)}) custom-call(s32[15]{0:T(128)} %stack.63.index_ref, f32[3,512,256]{2,1,0:T(8,128)} %shard_map.83.local_near_ref.local_ref, f32[3,512,256]{2,1,0:T(8,128)} %shard_map.86.local_far_ref.local_ref, bf16[2,512,256]{2,1,0:T(8,128)(2,1)} %copy-done.27, ...), custom_call_target="tpu_custom_call" | custom-call | flops 1 | bytes 1 | tf_op jit(solution)/shard_map/pallas_call | solution.py:230
  80.5 0.8 copy-done.6
  81.3 3.6 %shard_map.88 = (bf16[256,256]{1,0:T(8,128)(2,1)}, bf16[256,256]{1,0:T(8,128)(2,1)}) custom-call(s32[15]{0:T(128)} %stack.63.index_ref, f32[3,512,256]{2,1,0:T(8,128)} %shard_map.86.local_far_ref.local_ref, bf16[1,1024,256]{2,1,0:T(8,128)(2,1)} %copy-done.6, f32[4,1,256]{2,1,0:T(1,128)} %bitcast.26, bf16[256,512]{1,0:T(8,128)(2,1)} %get-tuple-element.50.gate_ref, ...), custom_call_target="tpu_custom_call" | custom-call | flops 1 | bytes 1 | tf_op jit(solution)/shard_map/pallas_call | solution.py:272
  84.9 3.7 %shard_map.89 = (bf16[256,256]{1,0:T(8,128)(2,1)}, bf16[256,256]{1,0:T(8,128)(2,1)}) custom-call(s32[15]{0:T(128)} %stack.63.index_ref, f32[3,512,256]{2,1,0:T(8,128)} %shard_map.83.local_near_ref.local_ref, bf16[1,1024,256]{2,1,0:T(8,128)(2,1)} %copy-done.6, f32[4,1,256]{2,1,0:T(1,128)} %bitcast.27, bf16[256,512]{1,0:T(8,128)(2,1)} %get-tuple-element.50.gate_ref, ...), custom_call_target="tpu_custom_call" | custom-call | flops 1 | bytes 1 | tf_op jit(solution)/shard_map/pallas_call | solution.py:272
  88.6 0.1 collective-permute-start.13
  88.7 0.6 collective-permute-start.14
  89.3 0.9 constant_dynamic-update-slice_fusion.3
  90.2 1.3 collective-permute-start.15
  91.6 3.5 %collective-permute-done.14 = bf16[256,256]{1,0:T(8,128)(2,1)S(1)} collective-permute-done((bf16[256,256]{1,0:T(8,128)(2,1)S(1)}, bf16[256,256]{1,0:T(8,128)(2,1)S(1)}, u32[]{:S(2)}, u32[]{:S(2)}) %collective-permute-start.14) | collective-permute-done | bytes 131104 | tf_op jit(solution)/shard_map/ppermute | solution.py:389
  95.1 1.9 %collective-permute-done.15 = bf16[256,256]{1,0:T(8,128)(2,1)S(1)} collective-permute-done((bf16[256,256]{1,0:T(8,128)(2,1)S(1)}, bf16[256,256]{1,0:T(8,128)(2,1)S(1)}, u32[]{:S(2)}, u32[]{:S(2)}) %collective-permute-start.15) | collective-permute-done | bytes 131104 | tf_op jit(solution)/shard_map/ppermute | solution.py:389
  97.0 0.0 copy-start.8
  97.0 0.8 collective-permute-start.18
  97.7 1.5 collective-permute-start.19
  99.3 1.3 collective-permute-start.17
  100.5 4.6 %collective-permute-start.16 = (bf16[256,1024]{1,0:T(8,128)(2,1)S(1)}, bf16[256,1024]{1,0:T(8,128)(2,1)S(1)}, u32[]{:S(2)}, u32[]{:S(2)}) collective-permute-start(bf16[256,1024]{1,0:T(8,128)(2,1)S(1)} %constant_dynamic-update-slice_fusion.own), channel_id=1, source_target_pairs={{0,1},{1,2},{2,3},{4,5},{5,6},{6,7},{8,9},{9,10},{10,11},{12,13},{... | collective-permute-start | bytes 1572872 | tf_op jit(solution)/shard_map/ppermute | solution.py:392
  105.1 6.0 %collective-permute-done.18.refs_4_ = bf16[256,1024]{1,0:T(8,128)(2,1)S(1)} collective-permute-done((bf16[256,1024]{1,0:T(8,128)(2,1)S(1)}, bf16[256,1024]{1,0:T(8,128)(2,1)S(1)}, u32[]{:S(2)}, u32[]{:S(2)}) %collective-permute-start.18) | collective-permute-done | bytes 524320 | tf_op jit(solution)/shard_map/ppermute | solution.py:389
  111.2 0.3 collective-permute-done.19.refs_3_
  111.4 3.1 %collective-permute-done.17.above_1 = bf16[256,1024]{1,0:T(8,128)(2,1)S(1)} collective-permute-done((bf16[256,1024]{1,0:T(8,128)(2,1)S(1)}, bf16[256,1024]{1,0:T(8,128)(2,1)S(1)}, u32[]{:S(2)}, u32[]{:S(2)}) %collective-permute-start.17) | collective-permute-done | bytes 524320 | tf_op jit(solution)/shard_map/ppermute | solution.py:392
  114.5 1.2 collective-permute-done.16.below_1
  115.7 0.7 collective-permute-start.20
  116.4 1.3 collective-permute-start.21
  117.7 0.6 collective-permute-start.22
  118.3 0.5 collective-permute-start.27
  118.8 15.1 %collective-permute-done.21.above_2 = bf16[256,1024]{1,0:T(8,128)(2,1)S(1)} collective-permute-done((bf16[256,1024]{1,0:T(8,128)(2,1)S(1)}, bf16[256,1024]{1,0:T(8,128)(2,1)S(1)}, u32[]{:S(2)}, u32[]{:S(2)}) %collective-permute-start.21) | collective-permute-done | bytes 524320 | tf_op jit(solution)/shard_map/ppermute | solution.py:392
  133.9 0.7 collective-permute-start.23
  134.6 0.1 collective-permute-start.25
  134.7 0.5 collective-permute-start.28
  135.2 1.3 collective-permute-start.24
  136.5 0.1 collective-permute-done.25.refs_6_
  136.6 0.7 collective-permute-done.28.refs_9_
  137.4 0.1 copy-done.21
  137.5 0.8 copy-done.23
  138.3 9.5 %shard_map.90 = (f32[256,1024]{1,0:T(8,128)}, bf16[1024,1024]{1,0:T(8,128)(2,1)}) custom-call(s32[15]{0:T(128)} %stack.63.index_ref, bf16[256,1024]{1,0:T(8,128)(2,1)} %copy-done.8, bf16[256,1024]{1,0:T(8,128)(2,1)} %copy-done.13, bf16[256,1024]{1,0:T(8,128)(2,1)} %copy-done.12, bf16[256,1024]{1,0:T(8,128)(2,1)} %copy-done.14, bf16[256,1024]{1,0:T(8,128)(2,1)} %copy-done.15, ...), custom_call_target="tpu_custom_call" | custom-call | flops 1 | bytes 1 | tf_op jit(solution)/shard_map/pallas_call | solution.py:334
  147.8 3.2 %collective-permute-done.24.above = bf16[256,1024]{1,0:T(8,128)(2,1)S(1)} collective-permute-done((bf16[256,1024]{1,0:T(8,128)(2,1)S(1)}, bf16[256,1024]{1,0:T(8,128)(2,1)S(1)}, u32[]{:S(2)}, u32[]{:S(2)}) %collective-permute-start.24) | collective-permute-done | bytes 524320 | tf_op jit(solution)/shard_map/ppermute | solution.py:392
  151.0 0.8 copy-done.20
  151.8 4.0 %shard_map.91 = bf16[256,1024]{1,0:T(8,128)(2,1)} custom-call(s32[15]{0:T(128)} %stack.63.index_ref, bf16[256,1024]{1,0:T(8,128)(2,1)} %copy-done.18, bf16[256,1024]{1,0:T(8,128)(2,1)} %copy-done.20, bf16[1024,1024]{1,0:T(8,128)(2,1)} %get-tuple-element.73.weight, f32[256,1024]{1,0:T(8,128)} %get-tuple-element.74.before), custom_call_target="tpu_custom_call" | custom-call | flops 1 | bytes 1 | tf_op jit(solution)/shard_map/pallas_call | solution.py:360
  (78 shorter events, 0.2 us)
Async XLA Ops:
  0.0 9.0 %copy-start = (bf16[4096,4]{0,1:T(4,128)(2,1)S(1)}, bf16[4096,4]{0,1:T(4,128)(2,1)}, u32[]{:S(2)}) copy-start(bf16[4096,4]{0,1:T(4,128)(2,1)} %param.10) | copy-start | bytes 98308
  5.6 13.0 %collective-permute-start.1 = (bf16[3,1024,512]{2,1,0:T(8,128)(2,1)}, bf16[3,1024,512]{2,1,0:T(8,128)(2,1)S(1)}, u32[]{:S(2)}, u32[]{:S(2)}) collective-permute-start(bf16[3,1024,512]{2,1,0:T(8,128)(2,1)} %dynamic-slice_bitcast_fusion), channel_id=1, source_target_pairs={{0,4},{4,0},{8,12},{12,8},{1,5},{5,1},{9,13},{13,9},{2,6},{6,2},{1... | collective-permute-start | bytes 9437192 | tf_op jit(solution)/shard_map/ppermute | solution.py:389
  6.0 12.6 %collective-permute-start = (bf16[256,4096]{1,0:T(8,128)(2,1)}, bf16[256,4096]{1,0:T(8,128)(2,1)}, u32[]{:S(2)}, u32[]{:S(2)}) collective-permute-start(bf16[256,4096]{1,0:T(8,128)(2,1)} %refs_0_.6), channel_id=1, source_target_pairs={{0,4},{4,0},{8,12},{12,8},{1,5},{5,1},{9,13},{13,9},{2,6},{6,2},{1... | collective-permute-start | bytes 6291464 | tf_op jit(solution)/shard_map/ppermute | solution.py:389
  6.1 18.9 %collective-permute-start.3 = (bf16[256,1024]{1,0:T(8,128)(2,1)}, bf16[256,1024]{1,0:T(8,128)(2,1)}, u32[]{:S(2)}, u32[]{:S(2)}) collective-permute-start(bf16[256,1024]{1,0:T(8,128)(2,1)} %constant_dynamic-slice_fusion.2), channel_id=1, source_target_pairs={{0,8},{4,12},{8,0},{12,4},{1,9},{5,13},{9,1},{13,5},{2,10},{6,14},... | collective-permute-start | bytes 1572872 | tf_op jit(solution)/shard_map/ppermute | solution.py:389
  11.3 3.0 %collective-permute-start.2 = (f32[4,256]{1,0:T(4,128)S(1)}, f32[4,256]{1,0:T(4,128)S(1)}, u32[]{:S(2)}, u32[]{:S(2)}) collective-permute-start(f32[4,256]{1,0:T(4,128)S(1)} %compare_select_fusion), channel_id=1, source_target_pairs={{0,4},{4,0},{8,12},{12,8},{1,5},{5,1},{9,13},{13,9},{2,6},{6,2},{1... | collective-permute-start | bytes 12296 | tf_op jit(solution)/shard_map/ppermute | solution.py:389
  14.3 10.7 %copy-start.28 = (f32[8,256]{1,0:T(8,128)}, f32[8,256]{1,0:T(8,128)S(1)}, u32[]{:S(2)}) copy-start(f32[8,256]{1,0:T(8,128)S(1)} %pad_maximum_fusion.rate_near_ref) | copy-start | bytes 24580
  14.3 10.7 %collective-permute-start.4 = (f32[8,256]{1,0:T(8,128)S(1)}, f32[8,256]{1,0:T(8,128)S(1)}, u32[]{:S(2)}, u32[]{:S(2)}) collective-permute-start(f32[8,256]{1,0:T(8,128)S(1)} %pad_maximum_fusion.rate_near_ref), channel_id=1, source_target_pairs={{0,8},{4,12},{8,0},{12,4},{1,9},{5,13},{9,1},{13,5},{2,10},{6,14},... | collective-permute-start | bytes 24584 | tf_op jit(solution)/shard_map/ppermute | solution.py:389
  18.6 1.6 %copy-start.1 = (bf16[3,1024,512]{2,1,0:T(8,128)(2,1)}, bf16[3,1024,512]{2,1,0:T(8,128)(2,1)S(1)}, u32[]{:S(2)}) copy-start(bf16[3,1024,512]{2,1,0:T(8,128)(2,1)S(1)} %collective-permute-done.1.refs_3_.refs_5_.refs_7_) | copy-start | bytes 9437188
  25.0 8.4 %copy-start.29 = (f32[8,256]{1,0:T(8,128)}, f32[8,256]{1,0:T(8,128)S(1)}, u32[]{:S(2)}) copy-start(f32[8,256]{1,0:T(8,128)S(1)} %collective-permute-done.4.rate_far_ref) | copy-start | bytes 24580
  25.0 14.0 %collective-permute-start.5 = (bf16[256,1024]{1,0:T(8,128)(2,1)}, bf16[256,1024]{1,0:T(8,128)(2,1)S(1)}, u32[]{:S(2)}, u32[]{:S(2)}) collective-permute-start(bf16[256,1024]{1,0:T(8,128)(2,1)} %collective-permute-done.3.refs_0_.refs_2_), channel_id=1, source_target_pairs={{0,1},{1,0},{2,3},{3,2},{4,5},{5,4},{6,7},{7,6},{8,9},{9,8},{10,11... | collective-permute-start | bytes 1572872 | tf_op jit(solution)/shard_map/ppermute | solution.py:392
  26.7 13.6 %collective-permute-start.6 = (bf16[2,512,256]{2,1,0:T(8,128)(2,1)}, bf16[2,512,256]{2,1,0:T(8,128)(2,1)S(1)}, u32[]{:S(2)}, u32[]{:S(2)}) collective-permute-start(bf16[2,512,256]{2,1,0:T(8,128)(2,1)} %shard_map.82), channel_id=1, source_target_pairs={{0,8},{4,12},{8,0},{12,4},{1,9},{5,13},{9,1},{13,5},{2,10},{6,14},... | collective-permute-start | bytes 1572872 | tf_op jit(solution)/shard_map/ppermute | solution.py:389
  27.2 13.1 %collective-permute-start.7 = (bf16[256,1024]{1,0:T(8,128)(2,1)}, bf16[256,1024]{1,0:T(8,128)(2,1)S(1)}, u32[]{:S(2)}, u32[]{:S(2)}) collective-permute-start(bf16[256,1024]{1,0:T(8,128)(2,1)} %collective-permute-done.3.refs_0_.refs_2_), channel_id=1, source_target_pairs={{0,4},{4,0},{8,12},{12,8},{1,5},{5,1},{9,13},{13,9},{2,6},{6,2},{1... | collective-permute-start | bytes 1572872 | tf_op jit(solution)/shard_map/ppermute | solution.py:389
  33.4 14.4 %copy-start.5 = (bf16[1024,1024]{1,0:T(8,128)(2,1)S(1)}, bf16[1024,1024]{1,0:T(8,128)(2,1)}, u32[]{:S(2)}) copy-start(bf16[1024,1024]{1,0:T(8,128)(2,1)} %refs_0_.7) | copy-start | bytes 6291460
  39.0 3.2 %copy-start.2 = (bf16[256,1024]{1,0:T(8,128)(2,1)}, bf16[256,1024]{1,0:T(8,128)(2,1)S(1)}, u32[]{:S(2)}) copy-start(bf16[256,1024]{1,0:T(8,128)(2,1)S(1)} %collective-permute-done.5.refs_1_.refs_3_) | copy-start | bytes 1572868
  40.3 13.7 %copy-start.26 = (bf16[2,512,256]{2,1,0:T(8,128)(2,1)}, bf16[2,512,256]{2,1,0:T(8,128)(2,1)S(1)}, u32[]{:S(2)}) copy-start(bf16[2,512,256]{2,1,0:T(8,128)(2,1)S(1)} %collective-permute-done.6.far_ref) | copy-start | bytes 1572868
  40.3 1.9 %collective-permute-start.8 = (bf16[256,1024]{1,0:T(8,128)(2,1)S(1)}, bf16[256,1024]{1,0:T(8,128)(2,1)S(1)}, u32[]{:S(2)}, u32[]{:S(2)}) collective-permute-start(bf16[256,1024]{1,0:T(8,128)(2,1)S(1)} %collective-permute-done.5.refs_1_.refs_3_), channel_id=1, source_target_pairs={{0,4},{4,0},{8,12},{12,8},{1,5},{5,1},{9,13},{13,9},{2,6},{6,2},{1... | collective-permute-start | bytes 1572872 | tf_op jit(solution)/shard_map/ppermute | solution.py:389
  40.3 1.9 %copy-start.3 = (bf16[256,1024]{1,0:T(8,128)(2,1)}, bf16[256,1024]{1,0:T(8,128)(2,1)S(1)}, u32[]{:S(2)}) copy-start(bf16[256,1024]{1,0:T(8,128)(2,1)S(1)} %collective-permute-done.7.refs_2_.refs_4_) | copy-start | bytes 1572868
  42.2 0.8 copy-start.4
  47.8 6.2 %collective-permute-start.10 = (bf16[1024,1024]{1,0:T(8,128)(2,1)S(1)}, bf16[1024,1024]{1,0:T(8,128)(2,1)S(1)}, u32[]{:S(2)}, u32[]{:S(2)}) collective-permute-start(bf16[1024,1024]{1,0:T(8,128)(2,1)S(1)} %copy-done.5), channel_id=1, source_target_pairs={{0,4},{4,0},{8,12},{12,8},{1,5},{5,1},{9,13},{13,9},{2,6},{6,2},{1... | collective-permute-start | bytes 6291464 | tf_op jit(solution)/shard_map/ppermute | solution.py:389
  47.9 14.4 %collective-permute-start.9 = (bf16[2,512,256]{2,1,0:T(8,128)(2,1)}, bf16[2,512,256]{2,1,0:T(8,128)(2,1)S(1)}, u32[]{:S(2)}, u32[]{:S(2)}) collective-permute-start(bf16[2,512,256]{2,1,0:T(8,128)(2,1)} %shard_map.84), channel_id=1, source_target_pairs={{0,8},{4,12},{8,0},{12,4},{1,9},{5,13},{9,1},{13,5},{2,10},{6,14},... | collective-permute-start | bytes 1572872 | tf_op jit(solution)/shard_map/ppermute | solution.py:389
  54.0 8.3 %copy-start.22 = (bf16[1,1024,256]{2,1,0:T(8,128)(2,1)S(1)}, bf16[1,1024,256]{2,1,0:T(8,128)(2,1)}, u32[]{:S(2)}) copy-start(bf16[1,1024,256]{2,1,0:T(8,128)(2,1)} %shard_map.85) | copy-start | bytes 1572868
  54.0 8.9 %copy-start.25 = (bf16[256,1024]{1,0:T(8,128)(2,1)S(1)}, bf16[256,1024]{1,0:T(8,128)(2,1)}, u32[]{:S(2)}) copy-start(bf16[256,1024]{1,0:T(8,128)(2,1)} %get-tuple-element.58) | copy-start | bytes 1572868
  54.0 6.6 %copy-start.7 = (bf16[1024,1024]{1,0:T(8,128)(2,1)}, bf16[1024,1024]{1,0:T(8,128)(2,1)S(1)}, u32[]{:S(2)}) copy-start(bf16[1024,1024]{1,0:T(8,128)(2,1)S(1)} %collective-permute-done.10.refs_1_) | copy-start | bytes 6291460
  62.3 2.0 %copy-start.27 = (bf16[2,512,256]{2,1,0:T(8,128)(2,1)}, bf16[2,512,256]{2,1,0:T(8,128)(2,1)S(1)}, u32[]{:S(2)}) copy-start(bf16[2,512,256]{2,1,0:T(8,128)(2,1)S(1)} %collective-permute-done.9.near_ref) | copy-start | bytes 1572868
  62.3 18.2 %collective-permute-start.11 = (bf16[1,1024,256]{2,1,0:T(8,128)(2,1)S(1)}, bf16[1,1024,256]{2,1,0:T(8,128)(2,1)S(1)}, u32[]{:S(2)}, u32[]{:S(2)}) collective-permute-start(bf16[1,1024,256]{2,1,0:T(8,128)(2,1)S(1)} %copy-done.22), channel_id=1, source_target_pairs={{0,8},{4,12},{8,0},{12,4},{1,9},{5,13},{9,1},{13,5},{2,10},{6,14},... | collective-permute-start | bytes 1572872 | tf_op jit(solution)/shard_map/ppermute | solution.py:389
  62.8 25.8 %collective-permute-start.12 = (bf16[256,1024]{1,0:T(8,128)(2,1)S(1)}, bf16[256,1024]{1,0:T(8,128)(2,1)S(1)}, u32[]{:S(2)}, u32[]{:S(2)}) collective-permute-start(bf16[256,1024]{1,0:T(8,128)(2,1)S(1)} %copy-done.25), channel_id=1, source_target_pairs={{0,8},{4,12},{8,0},{12,4},{1,9},{5,13},{9,1},{13,5},{2,10},{6,14},... | collective-permute-start | bytes 1572872 | tf_op jit(solution)/shard_map/ppermute | solution.py:389
  80.5 0.8 copy-start.6
  84.9 3.8 %copy-start.31 = (bf16[256,256]{1,0:T(8,128)(2,1)S(1)}, bf16[256,256]{1,0:T(8,128)(2,1)}, u32[]{:S(2)}) copy-start(bf16[256,256]{1,0:T(8,128)(2,1)} %get-tuple-element.60) | copy-start | bytes 393220
  84.9 5.3 %copy-start.30 = (bf16[256,256]{1,0:T(8,128)(2,1)S(1)}, bf16[256,256]{1,0:T(8,128)(2,1)}, u32[]{:S(2)}) copy-start(bf16[256,256]{1,0:T(8,128)(2,1)} %get-tuple-element.61) | copy-start | bytes 393220
  84.9 12.1 %copy-start.24 = (bf16[256,1024]{1,0:T(8,128)(2,1)S(1)}, bf16[256,1024]{1,0:T(8,128)(2,1)}, u32[]{:S(2)}) copy-start(bf16[256,1024]{1,0:T(8,128)(2,1)} %get-tuple-element.62) | copy-start | bytes 1572868
  88.6 48.7 %copy-start.9 = (bf16[256,1024]{1,0:T(8,128)(2,1)}, bf16[256,1024]{1,0:T(8,128)(2,1)S(1)}, u32[]{:S(2)}) copy-start(bf16[256,1024]{1,0:T(8,128)(2,1)S(1)} %collective-permute-done.12.refs_2_) | copy-start | bytes 1572868
  88.6 2.9 %collective-permute-start.13 = (bf16[256,256]{1,0:T(8,128)(2,1)}, bf16[256,256]{1,0:T(8,128)(2,1)S(1)}, u32[]{:S(2)}, u32[]{:S(2)}) collective-permute-start(bf16[256,256]{1,0:T(8,128)(2,1)} %get-tuple-element.59), channel_id=1, source_target_pairs={{0,4},{4,0},{8,12},{12,8},{1,5},{5,1},{9,13},{13,9},{2,6},{6,2},{1... | collective-permute-start | bytes 393224 | tf_op jit(solution)/shard_map/ppermute | solution.py:389
  88.7 6.4 %collective-permute-start.14 = (bf16[256,256]{1,0:T(8,128)(2,1)S(1)}, bf16[256,256]{1,0:T(8,128)(2,1)S(1)}, u32[]{:S(2)}, u32[]{:S(2)}) collective-permute-start(bf16[256,256]{1,0:T(8,128)(2,1)S(1)} %copy-done.31), channel_id=1, source_target_pairs={{0,8},{4,12},{8,0},{12,4},{1,9},{5,13},{9,1},{13,5},{2,10},{6,14},... | collective-permute-start | bytes 393224 | tf_op jit(solution)/shard_map/ppermute | solution.py:389
  90.2 6.7 %collective-permute-start.15 = (bf16[256,256]{1,0:T(8,128)(2,1)S(1)}, bf16[256,256]{1,0:T(8,128)(2,1)S(1)}, u32[]{:S(2)}, u32[]{:S(2)}) collective-permute-start(bf16[256,256]{1,0:T(8,128)(2,1)S(1)} %copy-done.30), channel_id=1, source_target_pairs={{0,12},{4,8},{8,4},{12,0},{1,13},{5,9},{9,5},{13,1},{2,14},{6,10},... | collective-permute-start | bytes 393224 | tf_op jit(solution)/shard_map/ppermute | solution.py:389
  97.0 40.4 %copy-start.8 = (bf16[256,1024]{1,0:T(8,128)(2,1)}, bf16[256,1024]{1,0:T(8,128)(2,1)S(1)}, u32[]{:S(2)}) copy-start(bf16[256,1024]{1,0:T(8,128)(2,1)S(1)} %constant_dynamic-update-slice_fusion.own) | copy-start | bytes 1572868
  97.0 14.2 %collective-permute-start.18 = (bf16[256,1024]{1,0:T(8,128)(2,1)S(1)}, bf16[256,1024]{1,0:T(8,128)(2,1)S(1)}, u32[]{:S(2)}, u32[]{:S(2)}) collective-permute-start(bf16[256,1024]{1,0:T(8,128)(2,1)S(1)} %copy-done.24), channel_id=1, source_target_pairs={{0,8},{4,12},{8,0},{12,4},{1,9},{5,13},{9,1},{13,5},{2,10},{6,14},... | collective-permute-start | bytes 1572872 | tf_op jit(solution)/shard_map/ppermute | solution.py:389
  97.7 13.7 %collective-permute-start.19 = (bf16[256,1024]{1,0:T(8,128)(2,1)S(1)}, bf16[256,1024]{1,0:T(8,128)(2,1)S(1)}, u32[]{:S(2)}, u32[]{:S(2)}) collective-permute-start(bf16[256,1024]{1,0:T(8,128)(2,1)S(1)} %collective-permute-done.12.refs_2_), channel_id=1, source_target_pairs={{0,16},{16,0},{1,17},{17,1},{2,18},{18,2},{3,19},{19,3},{4,20},{20... | collective-permute-start | bytes 1572872 | tf_op jit(solution)/shard_map/ppermute | solution.py:450
  99.3 15.3 %collective-permute-start.17 = (bf16[256,1024]{1,0:T(8,128)(2,1)S(1)}, bf16[256,1024]{1,0:T(8,128)(2,1)S(1)}, u32[]{:S(2)}, u32[]{:S(2)}) collective-permute-start(bf16[256,1024]{1,0:T(8,128)(2,1)S(1)} %constant_dynamic-update-slice_fusion.own), channel_id=1, source_target_pairs={{1,0},{2,1},{3,2},{5,4},{6,5},{7,6},{9,8},{10,9},{11,10},{13,12},{... | collective-permute-start | bytes 1572872 | tf_op jit(solution)/shard_map/ppermute | solution.py:392
  100.5 15.2 %collective-permute-start.16 = (bf16[256,1024]{1,0:T(8,128)(2,1)S(1)}, bf16[256,1024]{1,0:T(8,128)(2,1)S(1)}, u32[]{:S(2)}, u32[]{:S(2)}) collective-permute-start(bf16[256,1024]{1,0:T(8,128)(2,1)S(1)} %constant_dynamic-update-slice_fusion.own), channel_id=1, source_target_pairs={{0,1},{1,2},{2,3},{4,5},{5,6},{6,7},{8,9},{9,10},{10,11},{12,13},{... | collective-permute-start | bytes 1572872 | tf_op jit(solution)/shard_map/ppermute | solution.py:392
  111.2 26.2 %copy-start.10 = (bf16[256,1024]{1,0:T(8,128)(2,1)}, bf16[256,1024]{1,0:T(8,128)(2,1)S(1)}, u32[]{:S(2)}) copy-start(bf16[256,1024]{1,0:T(8,128)(2,1)S(1)} %collective-permute-done.18.refs_4_) | copy-start | bytes 1572868
  111.4 25.9 %copy-start.11 = (bf16[256,1024]{1,0:T(8,128)(2,1)}, bf16[256,1024]{1,0:T(8,128)(2,1)S(1)}, u32[]{:S(2)}) copy-start(bf16[256,1024]{1,0:T(8,128)(2,1)S(1)} %collective-permute-done.19.refs_3_) | copy-start | bytes 1572868
  114.5 22.8 %copy-start.12 = (bf16[256,1024]{1,0:T(8,128)(2,1)}, bf16[256,1024]{1,0:T(8,128)(2,1)S(1)}, u32[]{:S(2)}) copy-start(bf16[256,1024]{1,0:T(8,128)(2,1)S(1)} %collective-permute-done.17.above_1) | copy-start | bytes 1572868
  115.7 21.7 %copy-start.13 = (bf16[256,1024]{1,0:T(8,128)(2,1)}, bf16[256,1024]{1,0:T(8,128)(2,1)S(1)}, u32[]{:S(2)}) copy-start(bf16[256,1024]{1,0:T(8,128)(2,1)S(1)} %collective-permute-done.16.below_1) | copy-start | bytes 1572868
  115.7 3.1 %collective-permute-start.20 = (bf16[256,1024]{1,0:T(8,128)(2,1)S(1)}, bf16[256,1024]{1,0:T(8,128)(2,1)S(1)}, u32[]{:S(2)}, u32[]{:S(2)}) collective-permute-start(bf16[256,1024]{1,0:T(8,128)(2,1)S(1)} %collective-permute-done.16.below_1), channel_id=1, source_target_pairs={{1,2},{2,3},{5,6},{6,7},{9,10},{10,11},{13,14},{14,15},{17,18},{18... | collective-permute-start | bytes 1572872 | tf_op jit(solution)/shard_map/ppermute | solution.py:392
  116.4 17.5 %collective-permute-start.21 = (bf16[256,1024]{1,0:T(8,128)(2,1)S(1)}, bf16[256,1024]{1,0:T(8,128)(2,1)S(1)}, u32[]{:S(2)}, u32[]{:S(2)}) collective-permute-start(bf16[256,1024]{1,0:T(8,128)(2,1)S(1)} %collective-permute-done.17.above_1), channel_id=1, source_target_pairs={{1,0},{2,1},{5,4},{6,5},{9,8},{10,9},{13,12},{14,13},{17,16},{18,1... | collective-permute-start | bytes 1572872 | tf_op jit(solution)/shard_map/ppermute | solution.py:392
  117.7 16.2 %collective-permute-start.22 = (bf16[256,1024]{1,0:T(8,128)(2,1)S(1)}, bf16[256,1024]{1,0:T(8,128)(2,1)S(1)}, u32[]{:S(2)}, u32[]{:S(2)}) collective-permute-start(bf16[256,1024]{1,0:T(8,128)(2,1)S(1)} %collective-permute-done.18.refs_4_), channel_id=1, source_target_pairs={{0,16},{16,0},{1,17},{17,1},{2,18},{18,2},{3,19},{19,3},{4,20},{20... | collective-permute-start | bytes 1572872 | tf_op jit(solution)/shard_map/ppermute | solution.py:450
  118.3 16.9 %collective-permute-start.26 = (bf16[256,1024]{1,0:T(8,128)(2,1)S(1)}, bf16[256,1024]{1,0:T(8,128)(2,1)S(1)}, u32[]{:S(2)}, u32[]{:S(2)}) collective-permute-start(bf16[256,1024]{1,0:T(8,128)(2,1)S(1)} %collective-permute-done.19.refs_3_), channel_id=1, source_target_pairs={{0,4},{4,0},{8,12},{12,8},{1,5},{5,1},{9,13},{13,9},{2,6},{6,2},{1... | collective-permute-start | bytes 1572872 | tf_op jit(solution)/shard_map/ppermute | solution.py:389
  118.3 18.2 %collective-permute-start.27 = (bf16[256,1024]{1,0:T(8,128)(2,1)S(1)}, bf16[256,1024]{1,0:T(8,128)(2,1)S(1)}, u32[]{:S(2)}, u32[]{:S(2)}) collective-permute-start(bf16[256,1024]{1,0:T(8,128)(2,1)S(1)} %collective-permute-done.18.refs_4_), channel_id=1, source_target_pairs={{0,4},{4,0},{8,12},{12,8},{1,5},{5,1},{9,13},{13,9},{2,6},{6,2},{1... | collective-permute-start | bytes 1572872 | tf_op jit(solution)/shard_map/ppermute | solution.py:389
  118.8 18.6 %copy-start.14 = (bf16[256,1024]{1,0:T(8,128)(2,1)}, bf16[256,1024]{1,0:T(8,128)(2,1)S(1)}, u32[]{:S(2)}) copy-start(bf16[256,1024]{1,0:T(8,128)(2,1)S(1)} %collective-permute-done.20.below_2) | copy-start | bytes 1572868
  133.9 3.5 %copy-start.15 = (bf16[256,1024]{1,0:T(8,128)(2,1)}, bf16[256,1024]{1,0:T(8,128)(2,1)S(1)}, u32[]{:S(2)}) copy-start(bf16[256,1024]{1,0:T(8,128)(2,1)S(1)} %collective-permute-done.21.above_2) | copy-start | bytes 1572868
  133.9 3.5 %copy-start.16 = (bf16[256,1024]{1,0:T(8,128)(2,1)}, bf16[256,1024]{1,0:T(8,128)(2,1)S(1)}, u32[]{:S(2)}) copy-start(bf16[256,1024]{1,0:T(8,128)(2,1)S(1)} %collective-permute-done.22.refs_5_) | copy-start | bytes 1572868
  133.9 13.9 %collective-permute-start.23 = (bf16[256,1024]{1,0:T(8,128)(2,1)S(1)}, bf16[256,1024]{1,0:T(8,128)(2,1)S(1)}, u32[]{:S(2)}, u32[]{:S(2)}) collective-permute-start(bf16[256,1024]{1,0:T(8,128)(2,1)S(1)} %collective-permute-done.20.below_2), channel_id=1, source_target_pairs={{2,3},{6,7},{10,11},{14,15},{18,19},{22,23},{26,27},{30,31}} | collective-permute-start | bytes 1572872 | tf_op jit(solution)/shard_map/ppermute | solution.py:392
  134.6 2.0 %collective-permute-start.25 = (bf16[256,1024]{1,0:T(8,128)(2,1)S(1)}, bf16[256,1024]{1,0:T(8,128)(2,1)S(1)}, u32[]{:S(2)}, u32[]{:S(2)}) collective-permute-start(bf16[256,1024]{1,0:T(8,128)(2,1)S(1)} %collective-permute-done.12.refs_2_), channel_id=1, source_target_pairs={{0,4},{4,0},{8,12},{12,8},{1,5},{5,1},{9,13},{13,9},{2,6},{6,2},{1... | collective-permute-start | bytes 1572872 | tf_op jit(solution)/shard_map/ppermute | solution.py:389
  134.7 2.6 %collective-permute-start.28 = (bf16[256,1024]{1,0:T(8,128)(2,1)S(1)}, bf16[256,1024]{1,0:T(8,128)(2,1)S(1)}, u32[]{:S(2)}, u32[]{:S(2)}) collective-permute-start(bf16[256,1024]{1,0:T(8,128)(2,1)S(1)} %collective-permute-done.22.refs_5_), channel_id=1, source_target_pairs={{0,4},{4,0},{8,12},{12,8},{1,5},{5,1},{9,13},{13,9},{2,6},{6,2},{1... | collective-permute-start | bytes 1572872 | tf_op jit(solution)/shard_map/ppermute | solution.py:389
  135.2 2.2 %copy-start.17 = (bf16[256,1024]{1,0:T(8,128)(2,1)}, bf16[256,1024]{1,0:T(8,128)(2,1)S(1)}, u32[]{:S(2)}) copy-start(bf16[256,1024]{1,0:T(8,128)(2,1)S(1)} %collective-permute-done.26.refs_7_) | copy-start | bytes 1572868
  135.2 15.8 %collective-permute-start.24 = (bf16[256,1024]{1,0:T(8,128)(2,1)S(1)}, bf16[256,1024]{1,0:T(8,128)(2,1)S(1)}, u32[]{:S(2)}, u32[]{:S(2)}) collective-permute-start(bf16[256,1024]{1,0:T(8,128)(2,1)S(1)} %collective-permute-done.21.above_2), channel_id=1, source_target_pairs={{1,0},{5,4},{9,8},{13,12},{17,16},{21,20},{25,24},{29,28}} | collective-permute-start | bytes 1572872 | tf_op jit(solution)/shard_map/ppermute | solution.py:392
  136.5 0.9 copy-start.19
  136.6 0.9 copy-start.21
  137.5 0.8 copy-start.23
  147.8 3.2 %copy-start.18 = (bf16[256,1024]{1,0:T(8,128)(2,1)}, bf16[256,1024]{1,0:T(8,128)(2,1)S(1)}, u32[]{:S(2)}) copy-start(bf16[256,1024]{1,0:T(8,128)(2,1)S(1)} %collective-permute-done.23.below) | copy-start | bytes 1572868
  151.0 0.8 copy-start.20

commit v6 on v5

--- a/solution.py
+++ b/solution.py
@@ -8,7 +8,7 @@
 from jax.sharding import PartitionSpec as P
 
 NSI = 5
-VMEM_LIMIT = 56 * 1024 * 1024
+VMEM_LIMIT = 28 * 1024 * 1024
 
 quintic_a = 3.4445
 quintic_b = -4.775
@@ -252,12 +252,14 @@
     )(index, local_near, local_far, near, far, rates_near, rates_far, fast_gate, fast_up, fast_down)
 
 
-def read_kernel(index_ref, local_ref, other_ref, gain_ref, gate_ref, up_ref, down_ref, *out_refs):
+def read_kernel(index_ref, local_near_ref, local_far_ref, other_ref, gain_ref, gate_ref, up_ref, down_ref, *out_refs):
     rows = out_refs[0].shape[0]
     gate_w, up_w, down_w = gate_ref[...], up_ref[...], down_ref[...]
     for block, out_ref in enumerate(out_refs):
-        here = pl.ds(block * rows, rows)
-        queries = rms_scale(local_ref[0, here, :] + other_ref[0, here, :].astype(F32)).astype(BF16)
+        local_ref = local_near_ref if block < 2 else local_far_ref
+        here = pl.ds((block % 2) * rows, rows)
+        there = pl.ds(((block + 2) % 4) * rows, rows)
+        queries = rms_scale(local_ref[0, here, :] + other_ref[0, there, :].astype(F32)).astype(BF16)
         gate = dot(queries, gate_w)
         up = dot(queries, up_w)
         hidden = (gate * jax.nn.sigmoid(gate) * up).astype(BF16)
@@ -265,29 +267,32 @@
         out_ref[...] = (rms_scale(read) * gain_ref[0]).astype(BF16)
 
 
-def read_out(index, local, other, which, gain, gate, up, down):
+def read_out(index, local_near, local_far, other, gain, gate, up, down):
     size, hidden = gate.shape
-    rows = other.shape[1] // 4
+    total = other.shape[1]
+    rows = total // 4
     weight = pl.BlockSpec((size, hidden), lambda i, idx: (0, 0))
+    local = pl.BlockSpec((1, 2 * rows, size), lambda i, idx: (2, 0, 0))
     return pl.pallas_call(
         read_kernel,
-        out_shape=[jax.ShapeDtypeStruct((rows, size), BF16)] * 2,
+        out_shape=[jax.ShapeDtypeStruct((rows, size), BF16)] * 4,
         grid_spec=pltpu.PrefetchScalarGridSpec(
             num_scalar_prefetch=1,
             grid=(1,),
             in_specs=[
-                pl.BlockSpec((1, 2 * rows, size), lambda i, idx: (2, 0, 0)),
-                pl.BlockSpec((1, 2 * rows, size), lambda i, idx: (0, which, 0)),
+                local,
+                local,
+                pl.BlockSpec((1, total, size), lambda i, idx: (0, 0, 0)),
                 pl.BlockSpec((1, 1, size), lambda i, idx: (idx[HEAD], 0, 0)),
                 weight,
                 weight,
                 weight,
             ],
-            out_specs=[pl.BlockSpec((rows, size), lambda i, idx: (0, 0))] * 2,
+            out_specs=[pl.BlockSpec((rows, size), lambda i, idx: (0, 0))] * 4,
         ),
         compiler_params=params(),
         cost_estimate=pl.CostEstimate(flops=1, bytes_accessed=1, transcendentals=0),
-    )(index, local, other, gain, gate, up, down)
+    )(index, local_near, local_far, other, gain, gate, up, down)
 
 
 def mix_kernel(index_ref, own, below_1, above_1, below_2, above_2, *refs):
@@ -404,23 +409,22 @@
     weight = jnp.transpose(after(qkv_weight, leaving), (1, 0, 2))
     given = across(lax.dynamic_slice(weight, (0, 0, (1 - core) * 2 * size), (3, depth, 2 * size)), 1)
     near = [tokens, peer]
+    send_near = project(index, near, [], weight, given, size, False, 1, 2, BF16)
+    got_far = across(send_near, 2)
+    direct = after(direct, send_near)
+    handed = hop(direct, [(i, i ^ 1) for i in range(4)])
+    direct_peer = across(direct, 1)
+    local_near = project(index, near, [], weight, after(given, direct), size, True, 1, 3, F32)
     half = out_weight.shape[0] // 2
-    out_half = lax.dynamic_slice(after(out_weight, leaving), (side * half, 0), (half, out_weight.shape[1]))
+    out_half = lax.dynamic_slice(after(out_weight, direct), (side * half, 0), (half, out_weight.shape[1]))
     out_first, out_later = out_half[:size], out_half[size:]
 
-    activity = lax.dot_general(rate_weight, tokens, (((0,), (1,)), ((), ())), preferred_element_type=F32)
+    activity = lax.dot_general(rate_weight, after(tokens, direct), (((0,), (1,)), ((), ())), preferred_element_type=F32)
     rates_own = jax.nn.softplus(activity)
     rates_near = jnp.concatenate([rates_own, across(rates_own, 1)])
     rates_far = across(rates_near, 2)
 
-    given = after(given, out_first, out_later, rates_near)
-    send_near = project(index, near, [], weight, given, size, False, 1, 2, BF16)
-    got_far = across(send_near, 2)
-    direct = after(direct, send_near, rates_far)
-    handed = hop(direct, [(i, i ^ 1) for i in range(4)])
-    direct_peer = across(direct, 1)
-    local_near = project(index, near, [], weight, after(given, direct), size, True, 1, 3, F32)
-    handed = after(handed, local_near, got_far)
+    handed = after(handed, local_near, got_far, rates_far, out_first, out_later)
     far = [(direct, handed), (direct_peer, across(handed, 1))]
     send_far = project(index, [], far, weight, given, size, False, 1, 2, BF16)
     got_near = across(send_far, 2)
@@ -434,11 +438,9 @@
 
     rates = (rates_near, rates_far)
     fresh = update(index, local_near, local_far, got_near, got_far, *rates, fast_gate, fast_up, fast_down)
-    gain = out_gain.reshape(4, 1, size)
-    far_reads = read_out(index, local_far, got_query, 0, gain, *fresh)
-    near_reads = read_out(index, local_near, after(got_query, *far_reads), 1, gain, *fresh)
-    *far_reads, near_read, first_x = lax.optimization_barrier((*far_reads, near_reads[1], first_x))
-    pieces = [near_reads[0], across(near_read, 1), across(far_reads[0], 2), across(far_reads[1], 3)]
+    normed = read_out(index, local_near, local_far, got_query, out_gain.reshape(4, 1, size), *fresh)
+    *normed, first_x = lax.optimization_barrier((*normed, first_x))
+    pieces = [normed[0], across(normed[1], 1), across(normed[2], 2), across(normed[3], 3)]
     shard = jnp.concatenate(pieces, axis=1)
 
     def both(number, below, above):
@@ -452,13 +454,14 @@
     later_x = across(after(out_later, shard), 2)
     first_y = swap_groups(after(first_x, shard))
     below_1, above_1 = both(0, shard, shard)
-    below_1, above_1, later_x, first_y = lax.optimization_barrier((below_1, above_1, later_x, first_y))
+    below_2, above_2 = both(1, below_1, above_1)
+    later_x, first_y = lax.optimization_barrier((later_x, first_y, below_1))[:2]
     later_y = swap_groups(later_x)
-    first_y_peer, later_x_peer = across(first_y, 1), across(later_x, 1)
-    below_2, above_2 = both(1, below_1, above_1)
-    below_2, above_2, later_y, first_x = lax.optimization_barrier((below_2, above_2, later_y, first_x))
     below_3, above_3 = both(2, below_2, above_2)
-    first_x_peer, later_y_peer = across(first_x, 1), across(later_y, 1)
+    first_y_peer, later_x_peer, first_x_peer = (
+        across(after(array, below_2), 1) for array in (first_y, later_x, first_x)
+    )
+    later_y_peer = across(later_y, 1)
 
     shards = [shard, below_1, above_1, below_2, above_2]
     parts = [first_x, first_y, later_x, later_y]

time: 156 us -> 144 us (0.923)
  Pallas kernels: 64.7 us -> 44.9 us
  waiting for transfers between devices: 48.5 us -> 56.9 us
  local copies, waits for them, and re-layouts: 14.3 us -> 12.6 us
    ppermute x20, waiting for transfers between devices: 20 us -> 32.6 us  [across(): return lax.ppermute(array, 'seq', [(i, i ^ bit) for i in range(4)])]
    ppermute x7, waiting for transfers between devices: 28.2 us -> 16.9 us  [hop(): return lax.ppermute(array, 'head', links)]
    ppermute x2, waiting for transfers between devices: 0.26 us -> 7.39 us  [swap_groups(): return lax.ppermute(array, 'groups', [(0, 1), (1, 0)])]
    pallas_call x5, Pallas kernels: 27.8 us -> 20.7 us  [project(): pl.pallas_call(functools.partial(project_kernel, len(whole), len(pairs)),...]
    pallas_call x2 -> x1, Pallas kernels: 7.28 us -> 2 us  [read_out(): pl.pallas_call(read_kernel, out_shape=[jax.ShapeDtypeStruct((rows, size),...]
    pallas_call x1, Pallas kernels: 9.48 us -> 5.54 us  [mix(): pl.pallas_call(mix_kernel, out_shape=[jax.ShapeDtypeStruct((rows, columns...]
    ppermute x20, starting transfers between devices: 12.1 us -> 14.3 us  [across(): return lax.ppermute(array, 'seq', [(i, i ^ bit) for i in range(4)])]
    pallas_call x1, Pallas kernels: 16.2 us -> 14.2 us  [update(): pl.pallas_call(update_kernel, out_shape=[out] * 3, grid_spec=pltpu.Prefet...]
  transfers between devices with their start and end apart: 29 -> 29, of which waited for: 15 -> 14; matrix products, arithmetic and copies ran while one was open for 4% -> 3% of each run, Pallas kernels for 36% -> 27%
where the time goes in v6:
time: 144 us
  waiting for transfers between devices  56.9 us (40%)
  Pallas kernels  44.9 us (31%)
  starting transfers between devices  26.8 us (19%)
  local copies, waits for them, and re-layouts  12.6 us (9%)
  matrix products  2.25 us (2%)
    ppermute x20, waiting for transfers between devices, across(): return lax.ppermute(array, 'seq', [(i, i ^ bit) for i in range(4)])  32.6 us
    pallas_call x5, Pallas kernels, project(): pl.pallas_call(functools.partial(project_kernel, len(whole), len(pairs)),...  20.7 us
    ppermute x7, waiting for transfers between devices, hop(): return lax.ppermute(array, 'head', links)  16.9 us
    ppermute x20, starting transfers between devices, across(): return lax.ppermute(array, 'seq', [(i, i ^ bit) for i in range(4)])  14.3 us
    pallas_call x1, Pallas kernels, update(): pl.pallas_call(update_kernel, out_shape=[out] * 3, grid_spec=pltpu.Prefet...  14.2 us
    ppermute x7, starting transfers between devices, hop(): return lax.ppermute(array, 'head', links)  10.5 us
    ppermute x2, waiting for transfers between devices, swap_groups(): return lax.ppermute(array, 'groups', [(0, 1), (1, 0)])  7.39 us
    unnamed x19, local copies, waits for them, and re-layouts  5.63 us
  transfers between devices with their start and end apart: 29, of which 14 were waited for; matrix products, arithmetic and copies ran while one was open for 3% of the time, Pallas kernels for 27%

profile of v6, /device:TPU:0, one launch (start us, length us, event | category | flops | bytes accessed | tf_op | source)
XLA Modules:
  0.0 143.7 jit_solution(4391353152493952643)
XLA Ops:
  0.0 1.9 %constant_dynamic-slice_fusion.2 = bf16[256,1024]{1,0:T(8,128)(2,1)} fusion(bf16[256,4096]{1,0:T(8,128)(2,1)} %refs_0_.6, s32[]{:T(128)S(6)} %select_n.18), kind=kLoop, calls=%fused_computation.10 | loop fusion | bytes 1048580 | tf_op jit(solution)/shard_map/dynamic_slice | solution.py:406
  1.9 3.7 %dynamic-slice_bitcast_fusion = bf16[3,1024,512]{2,1,0:T(8,128)(2,1)} fusion(bf16[1024,3,1024]{2,0,1:T(8,128)(2,1)} %param.9, s32[]{:T(128)S(6)} %select_n.19), kind=kLoop, calls=%fused_computation | loop fusion | bytes 6291460 | tf_op jit(solution)/shard_map/dynamic_slice | solution.py:410
  5.6 0.5 collective-permute-start.1
  6.1 0.1 collective-permute-start
  6.1 2.9 %collective-permute-start.2 = (bf16[256,1024]{1,0:T(8,128)(2,1)}, bf16[256,1024]{1,0:T(8,128)(2,1)}, u32[]{:S(2)}, u32[]{:S(2)}) collective-permute-start(bf16[256,1024]{1,0:T(8,128)(2,1)} %constant_dynamic-slice_fusion.2), channel_id=1, source_target_pairs={{0,8},{4,12},{8,0},{12,4},{1,9},{5,13},{9,1},{13,5},{2,10},{6,14},... | collective-permute-start | bytes 1572872 | tf_op jit(solution)/shard_map/ppermute | solution.py:394
  9.0 0.1 stack.63.index_ref
  9.1 5.5 %collective-permute-done.refs_1_ = bf16[256,4096]{1,0:T(8,128)(2,1)} collective-permute-done((bf16[256,4096]{1,0:T(8,128)(2,1)}, bf16[256,4096]{1,0:T(8,128)(2,1)}, u32[]{:S(2)}, u32[]{:S(2)}) %collective-permute-start) | collective-permute-done | bytes 2097184 | tf_op jit(solution)/shard_map/ppermute | solution.py:394
  14.6 2.8 %copy-done.1 = bf16[1024,3,1024]{2,0,1:T(8,128)(2,1)S(1)} copy-done((bf16[1024,3,1024]{2,0,1:T(8,128)(2,1)S(1)}, bf16[1024,3,1024]{2,0,1:T(8,128)(2,1)}, u32[]{:S(2)}) %copy-start.1) | copy-done | bytes 6291480
  17.4 4.4 %shard_map.82 = bf16[2,512,256]{2,1,0:T(8,128)(2,1)} custom-call(s32[15]{0:T(128)S(1)} %stack.63.index_ref, bf16[256,4096]{1,0:T(8,128)(2,1)} %refs_0_.6, bf16[256,4096]{1,0:T(8,128)(2,1)} %collective-permute-done.refs_1_, bf16[3,1024,1024]{2,1,0:T(8,128)(2,1)S(1)} %bitcast.25, bf16[3,1024,512]{2,1,0:T(8,128)(2,1)S(1)} %collective-permute-done.1.refs_3_.refs_5_.refs_7_), custom_call_target="tpu_custom_call" | custom-call | flops 1 | bytes 1 | tf_op jit(solution)/shard_map/pallas_call | solution.py:146
  21.8 2.9 %collective-permute-start.3 = (bf16[256,1024]{1,0:T(8,128)(2,1)}, bf16[256,1024]{1,0:T(8,128)(2,1)}, u32[]{:S(2)}, u32[]{:S(2)}) collective-permute-start(bf16[256,1024]{1,0:T(8,128)(2,1)} %collective-permute-done.2.refs_0_.refs_2_), channel_id=1, source_target_pairs={{0,1},{1,0},{2,3},{3,2},{4,5},{5,4},{6,7},{7,6},{8,9},{9,8},{10,11... | collective-permute-start | bytes 1572872 | tf_op jit(solution)/shard_map/ppermute | solution.py:397
  24.7 1.5 %collective-permute-start.4 = (bf16[2,512,256]{2,1,0:T(8,128)(2,1)}, bf16[2,512,256]{2,1,0:T(8,128)(2,1)}, u32[]{:S(2)}, u32[]{:S(2)}) collective-permute-start(bf16[2,512,256]{2,1,0:T(8,128)(2,1)} %shard_map.82), channel_id=1, source_target_pairs={{0,8},{4,12},{8,0},{12,4},{1,9},{5,13},{9,1},{13,5},{2,10},{6,14},... | collective-permute-start | bytes 1572872 | tf_op jit(solution)/shard_map/ppermute | solution.py:394
  26.2 2.3 %compare_select_fusion = f32[4,256]{1,0:T(4,128)S(1)} fusion(bf16[256,4096]{1,0:T(8,128)(2,1)} %refs_0_.6, bf16[4096,4]{0,1:T(4,128)(2,1)S(1)} %copy-done), kind=kOutput, calls=%fused_computation.2 | convolution fusion | flops 8394752 | bytes 2134016 | tf_op jit(solution)/shard_map/dot_general | solution.py:422
  28.5 0.1 collective-permute-start.5
  28.5 0.5 collective-permute-start.7
  29.0 0.7 collective-permute-done.5
  29.7 0.5 collective-permute-start.6
  30.2 1.3 constant_dynamic-slice_fusion.1
  31.5 0.0 copy-start.2
  31.5 2.8 %copy-done.2 = bf16[1024,3,1024]{2,0,1:T(8,128)(2,1)S(1)} copy-done((bf16[1024,3,1024]{2,0,1:T(8,128)(2,1)S(1)}, bf16[1024,3,1024]{2,0,1:T(8,128)(2,1)}, u32[]{:S(2)}) %copy-start.2) | copy-done | bytes 6291480
  34.3 4.6 %shard_map.83.local_near_ref = f32[3,512,256]{2,1,0:T(8,128)S(1)} custom-call(s32[15]{0:T(128)S(1)} %stack.63.index_ref, bf16[256,4096]{1,0:T(8,128)(2,1)} %refs_0_.6, bf16[256,4096]{1,0:T(8,128)(2,1)} %collective-permute-done.refs_1_, bf16[3,1024,1024]{2,1,0:T(8,128)(2,1)S(1)} %bitcast.26, ...), custom_call_target="tpu_custom_call" | custom-call | flops 1 | bytes 1 | tf_op jit(solution)/shard_map/pallas_call | solution.py:146
  38.9 0.0 collective-permute-done.6.rate_far_ref
  38.9 0.0 copy-start.3
  38.9 0.1 collective-permute-start.8
  39.0 2.1 %collective-permute-done.8.refs_3_.refs_5_ = bf16[256,1024]{1,0:T(8,128)(2,1)S(1)} collective-permute-done((bf16[256,1024]{1,0:T(8,128)(2,1)}, bf16[256,1024]{1,0:T(8,128)(2,1)S(1)}, u32[]{:S(2)}, u32[]{:S(2)}) %collective-permute-start.8) | collective-permute-done | bytes 524320 | tf_op jit(solution)/shard_map/ppermute | solution.py:394
  41.1 3.4 %shard_map.84 = bf16[2,512,256]{2,1,0:T(8,128)(2,1)S(1)} custom-call(s32[15]{0:T(128)S(1)} %stack.63.index_ref, bf16[256,1024]{1,0:T(8,128)(2,1)} %collective-permute-done.2.refs_0_.refs_2_, bf16[256,1024]{1,0:T(8,128)(2,1)} %collective-permute-done.3.refs_1_.refs_3_, bf16[256,1024]{1,0:T(8,128)(2,1)S(1)} %collective-permute-done.7.refs_2_.refs_4_, ...), custom_call_target="tpu_custom_call" | custom-call | flops 1 | bytes 1 | tf_op jit(solution)/shard_map/pallas_call | solution.py:146
  44.5 0.2 collective-permute-start.9
  44.7 1.5 %collective-permute-start.10 = (bf16[2,512,256]{2,1,0:T(8,128)(2,1)S(1)}, bf16[2,512,256]{2,1,0:T(8,128)(2,1)S(1)}, u32[]{:S(2)}, u32[]{:S(2)}) collective-permute-start(bf16[2,512,256]{2,1,0:T(8,128)(2,1)S(1)} %shard_map.84), channel_id=1, source_target_pairs={{0,8},{4,12},{8,0},{12,4},{1,9},{5,13},{9,1},{13,5},{2,10},{6,14},... | collective-permute-start | bytes 1572872 | tf_op jit(solution)/shard_map/ppermute | solution.py:394
  46.2 3.9 %shard_map.85 = bf16[1,1024,256]{2,1,0:T(8,128)(2,1)S(1)} custom-call(s32[15]{0:T(128)S(1)} %stack.63.index_ref, bf16[256,4096]{1,0:T(8,128)(2,1)} %refs_0_.6, bf16[256,4096]{1,0:T(8,128)(2,1)} %collective-permute-done.refs_1_, bf16[256,1024]{1,0:T(8,128)(2,1)} %collective-permute-done.2.refs_0_.refs_2_, ...), custom_call_target="tpu_custom_call" | custom-call | flops 1 | bytes 1 | tf_op jit(solution)/shard_map/pallas_call | solution.py:146
  50.1 0.0 copy-start.4
  50.2 0.0 copy-start.5
  50.2 0.0 copy-start.6
  50.2 4.4 %shard_map.86.local_far_ref = f32[3,512,256]{2,1,0:T(8,128)S(1)} custom-call(s32[15]{0:T(128)S(1)} %stack.63.index_ref, bf16[256,1024]{1,0:T(8,128)(2,1)} %collective-permute-done.2.refs_0_.refs_2_, bf16[256,1024]{1,0:T(8,128)(2,1)} %collective-permute-done.3.refs_1_.refs_3_, bf16[256,1024]{1,0:T(8,128)(2,1)S(1)} %collective-permute-done.7.refs_2_.refs_4_, ...), custom_call_target="tpu_custom_call" | custom-call | flops 1 | bytes 1 | tf_op jit(solution)/shard_map/pallas_call | solution.py:146
  54.6 0.0 copy-start.7
  54.6 4.2 %collective-permute-done.10.near_ref = bf16[2,512,256]{2,1,0:T(8,128)(2,1)S(1)} collective-permute-done((bf16[2,512,256]{2,1,0:T(8,128)(2,1)S(1)}, bf16[2,512,256]{2,1,0:T(8,128)(2,1)S(1)}, u32[]{:S(2)}, u32[]{:S(2)}) %collective-permute-start.10) | collective-permute-done | bytes 524320 | tf_op jit(solution)/shard_map/ppermute | solution.py:394
  58.9 1.5 %collective-permute-start.11 = (bf16[1,1024,256]{2,1,0:T(8,128)(2,1)S(1)}, bf16[1,1024,256]{2,1,0:T(8,128)(2,1)S(1)}, u32[]{:S(2)}, u32[]{:S(2)}) collective-permute-start(bf16[1,1024,256]{2,1,0:T(8,128)(2,1)S(1)} %shard_map.85), channel_id=1, source_target_pairs={{0,8},{4,12},{8,0},{12,4},{1,9},{5,13},{9,1},{13,5},{2,10},{6,14},... | collective-permute-start | bytes 1572872 | tf_op jit(solution)/shard_map/ppermute | solution.py:394
  60.4 0.5 collective-permute-start.12
  60.9 14.2 %shard_map.87 = (bf16[256,512]{1,0:T(8,128)(2,1)S(1)}, bf16[256,512]{1,0:T(8,128)(2,1)S(1)}, bf16[256,512]{1,0:T(8,128)(2,1)S(1)}) custom-call(s32[15]{0:T(128)S(1)} %stack.63.index_ref, f32[3,512,256]{2,1,0:T(8,128)S(1)} %shard_map.83.local_near_ref, f32[3,512,256]{2,1,0:T(8,128)S(1)} %shard_map.86.local_far_ref, ...), custom_call_target="tpu_custom_call" | custom-call | flops 1 | bytes 1 | tf_op jit(solution)/shard_map/pallas_call | solution.py:230
  75.2 2.0 %shard_map.88 = (bf16[256,256]{1,0:T(8,128)(2,1)S(1)}, bf16[256,256]{1,0:T(8,128)(2,1)S(1)}, bf16[256,256]{1,0:T(8,128)(2,1)S(1)}, bf16[256,256]{1,0:T(8,128)(2,1)S(1)}) custom-call(s32[15]{0:T(128)S(1)} %stack.63.index_ref, f32[3,512,256]{2,1,0:T(8,128)S(1)} %shard_map.83.local_near_ref, f32[3,512,256]{2,1,0:T(8,128)S(1)} %shard_map.86.local_far_ref, ...), custom_call_target="tpu_custom_call" | custom-call | flops 1 | bytes 1 | tf_op jit(solution)/shard_map/pallas_call | solution.py:276
  77.2 6.3 %collective-permute-done.12.refs_2_ = bf16[256,1024]{1,0:T(8,128)(2,1)S(1)} collective-permute-done((bf16[256,1024]{1,0:T(8,128)(2,1)S(1)}, bf16[256,1024]{1,0:T(8,128)(2,1)S(1)}, u32[]{:S(2)}, u32[]{:S(2)}) %collective-permute-start.12) | collective-permute-done | bytes 524320 | tf_op jit(solution)/shard_map/ppermute | solution.py:394
  83.5 1.5 %collective-permute-start.14 = (bf16[256,256]{1,0:T(8,128)(2,1)S(1)}, bf16[256,256]{1,0:T(8,128)(2,1)S(1)}, u32[]{:S(2)}, u32[]{:S(2)}) collective-permute-start(bf16[256,256]{1,0:T(8,128)(2,1)S(1)} %get-tuple-element.57), channel_id=1, source_target_pairs={{0,8},{4,12},{8,0},{12,4},{1,9},{5,13},{9,1},{13,5},{2,10},{6,14},... | collective-permute-start | bytes 393224 | tf_op jit(solution)/shard_map/ppermute | solution.py:394
  85.0 0.4 collective-permute-start.15
  85.4 4.4 %collective-permute-done.14 = bf16[256,256]{1,0:T(8,128)(2,1)S(1)} collective-permute-done((bf16[256,256]{1,0:T(8,128)(2,1)S(1)}, bf16[256,256]{1,0:T(8,128)(2,1)S(1)}, u32[]{:S(2)}, u32[]{:S(2)}) %collective-permute-start.14) | collective-permute-done | bytes 131104 | tf_op jit(solution)/shard_map/ppermute | solution.py:394
  89.8 2.0 %collective-permute-done.15 = bf16[256,256]{1,0:T(8,128)(2,1)S(1)} collective-permute-done((bf16[256,256]{1,0:T(8,128)(2,1)S(1)}, bf16[256,256]{1,0:T(8,128)(2,1)S(1)}, u32[]{:S(2)}, u32[]{:S(2)}) %collective-permute-start.15) | collective-permute-done | bytes 131104 | tf_op jit(solution)/shard_map/ppermute | solution.py:394
  91.9 1.6 %collective-permute-start.22 = (bf16[256,1024]{1,0:T(8,128)(2,1)S(1)}, bf16[256,1024]{1,0:T(8,128)(2,1)S(1)}, u32[]{:S(2)}, u32[]{:S(2)}) collective-permute-start(bf16[256,1024]{1,0:T(8,128)(2,1)S(1)} %get-tuple-element.60), channel_id=1, source_target_pairs={{0,8},{4,12},{8,0},{12,4},{1,9},{5,13},{9,1},{13,5},{2,10},{6,14},... | collective-permute-start | bytes 1572872 | tf_op jit(solution)/shard_map/ppermute | solution.py:394
  93.4 1.5 %collective-permute-start.23 = (bf16[256,1024]{1,0:T(8,128)(2,1)S(1)}, bf16[256,1024]{1,0:T(8,128)(2,1)S(1)}, u32[]{:S(2)}, u32[]{:S(2)}) collective-permute-start(bf16[256,1024]{1,0:T(8,128)(2,1)S(1)} %collective-permute-done.12.refs_2_), channel_id=1, source_target_pairs={{0,16},{16,0},{1,17},{17,1},{2,18},{18,2},{3,19},{19,3},{4,20},{20... | collective-permute-start | bytes 1572872 | tf_op jit(solution)/shard_map/ppermute | solution.py:452
  94.9 2.4 %collective-permute-start.16 = (bf16[256,1024]{1,0:T(8,128)(2,1)S(1)}, bf16[256,1024]{1,0:T(8,128)(2,1)S(1)}, u32[]{:S(2)}, u32[]{:S(2)}) collective-permute-start(bf16[256,1024]{1,0:T(8,128)(2,1)S(1)} %constant_dynamic-update-slice_fusion.own), channel_id=1, source_target_pairs={{0,1},{1,2},{2,3},{4,5},{5,6},{6,7},{8,9},{9,10},{10,11},{12,13},{... | collective-permute-start | bytes 1572872 | tf_op jit(solution)/shard_map/ppermute | solution.py:397
  97.3 1.3 collective-permute-start.19
  98.6 7.4 %collective-permute-done.22.refs_4_ = bf16[256,1024]{1,0:T(8,128)(2,1)S(1)} collective-permute-done((bf16[256,1024]{1,0:T(8,128)(2,1)S(1)}, bf16[256,1024]{1,0:T(8,128)(2,1)S(1)}, u32[]{:S(2)}, u32[]{:S(2)}) %collective-permute-start.22) | collective-permute-done | bytes 524320 | tf_op jit(solution)/shard_map/ppermute | solution.py:394
  106.0 1.2 collective-permute-done.23.refs_3_
  107.2 1.1 collective-permute-done.16.below_1
  108.3 0.5 collective-permute-start.24
  108.8 0.7 collective-permute-start.17
  109.4 3.9 %collective-permute-done.19.above_1 = bf16[256,1024]{1,0:T(8,128)(2,1)S(1)} collective-permute-done((bf16[256,1024]{1,0:T(8,128)(2,1)S(1)}, bf16[256,1024]{1,0:T(8,128)(2,1)S(1)}, u32[]{:S(2)}, u32[]{:S(2)}) %collective-permute-start.19) | collective-permute-done | bytes 524320 | tf_op jit(solution)/shard_map/ppermute | solution.py:397
  113.4 1.3 collective-permute-start.20
  114.6 6.2 %collective-permute-done.24.refs_5_ = bf16[256,1024]{1,0:T(8,128)(2,1)S(1)} collective-permute-done((bf16[256,1024]{1,0:T(8,128)(2,1)S(1)}, bf16[256,1024]{1,0:T(8,128)(2,1)S(1)}, u32[]{:S(2)}, u32[]{:S(2)}) %collective-permute-start.24) | collective-permute-done | bytes 524320 | tf_op jit(solution)/shard_map/ppermute | solution.py:452
  120.8 0.5 collective-permute-start.25
  121.3 0.0 collective-permute-start.26
  121.4 0.5 collective-permute-start.27
  121.9 6.2 %collective-permute-done.20.above_2 = bf16[256,1024]{1,0:T(8,128)(2,1)S(1)} collective-permute-done((bf16[256,1024]{1,0:T(8,128)(2,1)S(1)}, bf16[256,1024]{1,0:T(8,128)(2,1)S(1)}, u32[]{:S(2)}, u32[]{:S(2)}) %collective-permute-start.20) | collective-permute-done | bytes 524320 | tf_op jit(solution)/shard_map/ppermute | solution.py:397
  128.1 1.3 collective-permute-start.21
  129.4 0.7 collective-permute-start.18
  130.1 5.5 %shard_map.89 = (f32[256,1024]{1,0:T(8,128)S(1)}, bf16[1024,1024]{1,0:T(8,128)(2,1)S(1)}) custom-call(s32[15]{0:T(128)S(1)} %stack.63.index_ref, bf16[256,1024]{1,0:T(8,128)(2,1)S(1)} %constant_dynamic-update-slice_fusion.own, bf16[256,1024]{1,0:T(8,128)(2,1)S(1)} %collective-permute-done.16.below_1, bf16[256,1024]{1,0:T(8,128)(2,1)S(1)} %collective-permute-done.19.above_1, ...), custom_call_target="tpu_custom_call" | custom-call | flops 1 | bytes 1 | tf_op jit(solution)/shard_map/pallas_call | solution.py:339
  135.7 5.7 %collective-permute-done.21.above = bf16[256,1024]{1,0:T(8,128)(2,1)S(1)} collective-permute-done((bf16[256,1024]{1,0:T(8,128)(2,1)S(1)}, bf16[256,1024]{1,0:T(8,128)(2,1)S(1)}, u32[]{:S(2)}, u32[]{:S(2)}) %collective-permute-start.21) | collective-permute-done | bytes 524320 | tf_op jit(solution)/shard_map/ppermute | solution.py:397
  141.3 2.4 %shard_map.90 = bf16[256,1024]{1,0:T(8,128)(2,1)} custom-call(s32[15]{0:T(128)S(1)} %stack.63.index_ref, bf16[256,1024]{1,0:T(8,128)(2,1)S(1)} %collective-permute-done.18.below, bf16[256,1024]{1,0:T(8,128)(2,1)S(1)} %collective-permute-done.21.above, bf16[1024,1024]{1,0:T(8,128)(2,1)S(1)} %get-tuple-element.67.weight, f32[256,1024]{1,0:T(8,128)S(1)} %get-tuple-element.68.before), custom_call_target="tpu_custom_call" | custom-call | flops 1 | bytes 1 | tf_op jit(solution)/shard_map/pallas_call | solution.py:365
  (29 shorter events, 0.1 us)
Async XLA Ops:
  0.0 26.2 %copy-start = (bf16[4096,4]{0,1:T(4,128)(2,1)S(1)}, bf16[4096,4]{0,1:T(4,128)(2,1)}, u32[]{:S(2)}) copy-start(bf16[4096,4]{0,1:T(4,128)(2,1)} %param.10) | copy-start | bytes 98308
  5.6 9.0 %collective-permute-start.1 = (bf16[3,1024,512]{2,1,0:T(8,128)(2,1)}, bf16[3,1024,512]{2,1,0:T(8,128)(2,1)S(1)}, u32[]{:S(2)}, u32[]{:S(2)}) collective-permute-start(bf16[3,1024,512]{2,1,0:T(8,128)(2,1)} %dynamic-slice_bitcast_fusion), channel_id=1, source_target_pairs={{0,4},{4,0},{8,12},{12,8},{1,5},{5,1},{9,13},{13,9},{2,6},{6,2},{1... | collective-permute-start | bytes 9437192 | tf_op jit(solution)/shard_map/ppermute | solution.py:394
  6.1 8.5 %collective-permute-start = (bf16[256,4096]{1,0:T(8,128)(2,1)}, bf16[256,4096]{1,0:T(8,128)(2,1)}, u32[]{:S(2)}, u32[]{:S(2)}) collective-permute-start(bf16[256,4096]{1,0:T(8,128)(2,1)} %refs_0_.6), channel_id=1, source_target_pairs={{0,4},{4,0},{8,12},{12,8},{1,5},{5,1},{9,13},{13,9},{2,6},{6,2},{1... | collective-permute-start | bytes 6291464 | tf_op jit(solution)/shard_map/ppermute | solution.py:394
  6.1 15.7 %collective-permute-start.2 = (bf16[256,1024]{1,0:T(8,128)(2,1)}, bf16[256,1024]{1,0:T(8,128)(2,1)}, u32[]{:S(2)}, u32[]{:S(2)}) collective-permute-start(bf16[256,1024]{1,0:T(8,128)(2,1)} %constant_dynamic-slice_fusion.2), channel_id=1, source_target_pairs={{0,8},{4,12},{8,0},{12,4},{1,9},{5,13},{9,1},{13,5},{2,10},{6,14},... | collective-permute-start | bytes 1572872 | tf_op jit(solution)/shard_map/ppermute | solution.py:394
  14.6 2.8 %copy-start.1 = (bf16[1024,3,1024]{2,0,1:T(8,128)(2,1)S(1)}, bf16[1024,3,1024]{2,0,1:T(8,128)(2,1)}, u32[]{:S(2)}) copy-start(bf16[1024,3,1024]{2,0,1:T(8,128)(2,1)} %param.9) | copy-start | bytes 18874372
  21.8 17.1 %collective-permute-start.3 = (bf16[256,1024]{1,0:T(8,128)(2,1)}, bf16[256,1024]{1,0:T(8,128)(2,1)}, u32[]{:S(2)}, u32[]{:S(2)}) collective-permute-start(bf16[256,1024]{1,0:T(8,128)(2,1)} %collective-permute-done.2.refs_0_.refs_2_), channel_id=1, source_target_pairs={{0,1},{1,0},{2,3},{3,2},{4,5},{5,4},{6,7},{7,6},{8,9},{9,8},{10,11... | collective-permute-start | bytes 1572872 | tf_op jit(solution)/shard_map/ppermute | solution.py:397
  24.7 14.2 %collective-permute-start.4 = (bf16[2,512,256]{2,1,0:T(8,128)(2,1)}, bf16[2,512,256]{2,1,0:T(8,128)(2,1)}, u32[]{:S(2)}, u32[]{:S(2)}) collective-permute-start(bf16[2,512,256]{2,1,0:T(8,128)(2,1)} %shard_map.82), channel_id=1, source_target_pairs={{0,8},{4,12},{8,0},{12,4},{1,9},{5,13},{9,1},{13,5},{2,10},{6,14},... | collective-permute-start | bytes 1572872 | tf_op jit(solution)/shard_map/ppermute | solution.py:394
  28.5 1.2 collective-permute-start.5
  28.5 10.4 %collective-permute-start.7 = (bf16[256,1024]{1,0:T(8,128)(2,1)}, bf16[256,1024]{1,0:T(8,128)(2,1)S(1)}, u32[]{:S(2)}, u32[]{:S(2)}) collective-permute-start(bf16[256,1024]{1,0:T(8,128)(2,1)} %collective-permute-done.2.refs_0_.refs_2_), channel_id=1, source_target_pairs={{0,4},{4,0},{8,12},{12,8},{1,5},{5,1},{9,13},{13,9},{2,6},{6,2},{1... | collective-permute-start | bytes 1572872 | tf_op jit(solution)/shard_map/ppermute | solution.py:394
  29.7 9.2 %collective-permute-start.6 = (f32[8,256]{1,0:T(8,128)S(1)}, f32[8,256]{1,0:T(8,128)S(1)}, u32[]{:S(2)}, u32[]{:S(2)}) collective-permute-start(f32[8,256]{1,0:T(8,128)S(1)} %pad_maximum_fusion.rate_near_ref), channel_id=1, source_target_pairs={{0,8},{4,12},{8,0},{12,4},{1,9},{5,13},{9,1},{13,5},{2,10},{6,14},... | collective-permute-start | bytes 24584 | tf_op jit(solution)/shard_map/ppermute | solution.py:394
  31.5 2.8 %copy-start.2 = (bf16[1024,3,1024]{2,0,1:T(8,128)(2,1)S(1)}, bf16[1024,3,1024]{2,0,1:T(8,128)(2,1)}, u32[]{:S(2)}) copy-start(bf16[1024,3,1024]{2,0,1:T(8,128)(2,1)} %param.9) | copy-start | bytes 18874372
  38.9 5.6 %copy-start.3 = (bf16[1024,1024]{1,0:T(8,128)(2,1)S(1)}, bf16[1024,1024]{1,0:T(8,128)(2,1)}, u32[]{:S(2)}) copy-start(bf16[1024,1024]{1,0:T(8,128)(2,1)} %refs_0_.7) | copy-start | bytes 6291460
  38.9 2.2 %collective-permute-start.8 = (bf16[256,1024]{1,0:T(8,128)(2,1)}, bf16[256,1024]{1,0:T(8,128)(2,1)S(1)}, u32[]{:S(2)}, u32[]{:S(2)}) collective-permute-start(bf16[256,1024]{1,0:T(8,128)(2,1)} %collective-permute-done.3.refs_1_.refs_3_), channel_id=1, source_target_pairs={{0,4},{4,0},{8,12},{12,8},{1,5},{5,1},{9,13},{13,9},{2,6},{6,2},{1... | collective-permute-start | bytes 1572872 | tf_op jit(solution)/shard_map/ppermute | solution.py:394
  44.5 5.7 %collective-permute-start.9 = (bf16[1024,1024]{1,0:T(8,128)(2,1)S(1)}, bf16[1024,1024]{1,0:T(8,128)(2,1)S(1)}, u32[]{:S(2)}, u32[]{:S(2)}) collective-permute-start(bf16[1024,1024]{1,0:T(8,128)(2,1)S(1)} %copy-done.3), channel_id=1, source_target_pairs={{0,4},{4,0},{8,12},{12,8},{1,5},{5,1},{9,13},{13,9},{2,6},{6,2},{1... | collective-permute-start | bytes 6291464 | tf_op jit(solution)/shard_map/ppermute | solution.py:394
  44.7 14.2 %collective-permute-start.10 = (bf16[2,512,256]{2,1,0:T(8,128)(2,1)S(1)}, bf16[2,512,256]{2,1,0:T(8,128)(2,1)S(1)}, u32[]{:S(2)}, u32[]{:S(2)}) collective-permute-start(bf16[2,512,256]{2,1,0:T(8,128)(2,1)S(1)} %shard_map.84), channel_id=1, source_target_pairs={{0,8},{4,12},{8,0},{12,4},{1,9},{5,13},{9,1},{13,5},{2,10},{6,14},... | collective-permute-start | bytes 1572872 | tf_op jit(solution)/shard_map/ppermute | solution.py:394
  50.1 10.8 %copy-start.4 = (bf16[4,256,512]{2,1,0:T(8,128)(2,1)S(1)}, bf16[4,256,512]{2,1,0:T(8,128)(2,1)}, u32[]{:S(2)}) copy-start(bf16[4,256,512]{2,1,0:T(8,128)(2,1)} %gate_ref.1) | copy-start | bytes 3145732
  50.2 10.8 %copy-start.5 = (bf16[4,256,512]{2,1,0:T(8,128)(2,1)S(1)}, bf16[4,256,512]{2,1,0:T(8,128)(2,1)}, u32[]{:S(2)}) copy-start(bf16[4,256,512]{2,1,0:T(8,128)(2,1)} %up_ref.1) | copy-start | bytes 3145732
  50.2 10.8 %copy-start.6 = (bf16[4,256,512]{2,1,0:T(8,128)(2,1)S(1)}, bf16[4,256,512]{2,1,0:T(8,128)(2,1)}, u32[]{:S(2)}) copy-start(bf16[4,256,512]{2,1,0:T(8,128)(2,1)} %down_ref.1) | copy-start | bytes 3145732
  54.6 20.5 %copy-start.7 = (f32[1024]{0:T(1024)S(1)}, f32[1024]{0:T(1024)}, u32[]{:S(2)}) copy-start(f32[1024]{0:T(1024)} %param.14) | copy-start | bytes 12292
  58.9 16.3 %collective-permute-start.11 = (bf16[1,1024,256]{2,1,0:T(8,128)(2,1)S(1)}, bf16[1,1024,256]{2,1,0:T(8,128)(2,1)S(1)}, u32[]{:S(2)}, u32[]{:S(2)}) collective-permute-start(bf16[1,1024,256]{2,1,0:T(8,128)(2,1)S(1)} %shard_map.85), channel_id=1, source_target_pairs={{0,8},{4,12},{8,0},{12,4},{1,9},{5,13},{9,1},{13,5},{2,10},{6,14},... | collective-permute-start | bytes 1572872 | tf_op jit(solution)/shard_map/ppermute | solution.py:394
  60.4 23.1 %collective-permute-start.12 = (bf16[256,1024]{1,0:T(8,128)(2,1)S(1)}, bf16[256,1024]{1,0:T(8,128)(2,1)S(1)}, u32[]{:S(2)}, u32[]{:S(2)}) collective-permute-start(bf16[256,1024]{1,0:T(8,128)(2,1)S(1)} %get-tuple-element.54), channel_id=1, source_target_pairs={{0,8},{4,12},{8,0},{12,4},{1,9},{5,13},{9,1},{13,5},{2,10},{6,14},... | collective-permute-start | bytes 1572872 | tf_op jit(solution)/shard_map/ppermute | solution.py:394
  83.5 1.9 %collective-permute-start.13 = (bf16[256,256]{1,0:T(8,128)(2,1)S(1)}, bf16[256,256]{1,0:T(8,128)(2,1)S(1)}, u32[]{:S(2)}, u32[]{:S(2)}) collective-permute-start(bf16[256,256]{1,0:T(8,128)(2,1)S(1)} %get-tuple-element.56), channel_id=1, source_target_pairs={{0,4},{4,0},{8,12},{12,8},{1,5},{5,1},{9,13},{13,9},{2,6},{6,2},{1... | collective-permute-start | bytes 393224 | tf_op jit(solution)/shard_map/ppermute | solution.py:394
  83.5 6.3 %collective-permute-start.14 = (bf16[256,256]{1,0:T(8,128)(2,1)S(1)}, bf16[256,256]{1,0:T(8,128)(2,1)S(1)}, u32[]{:S(2)}, u32[]{:S(2)}) collective-permute-start(bf16[256,256]{1,0:T(8,128)(2,1)S(1)} %get-tuple-element.57), channel_id=1, source_target_pairs={{0,8},{4,12},{8,0},{12,4},{1,9},{5,13},{9,1},{13,5},{2,10},{6,14},... | collective-permute-start | bytes 393224 | tf_op jit(solution)/shard_map/ppermute | solution.py:394
  85.0 6.8 %collective-permute-start.15 = (bf16[256,256]{1,0:T(8,128)(2,1)S(1)}, bf16[256,256]{1,0:T(8,128)(2,1)S(1)}, u32[]{:S(2)}, u32[]{:S(2)}) collective-permute-start(bf16[256,256]{1,0:T(8,128)(2,1)S(1)} %get-tuple-element.58), channel_id=1, source_target_pairs={{0,12},{4,8},{8,4},{12,0},{1,13},{5,9},{9,5},{13,1},{2,14},{6,10},... | collective-permute-start | bytes 393224 | tf_op jit(solution)/shard_map/ppermute | solution.py:394
  91.9 14.1 %collective-permute-start.22 = (bf16[256,1024]{1,0:T(8,128)(2,1)S(1)}, bf16[256,1024]{1,0:T(8,128)(2,1)S(1)}, u32[]{:S(2)}, u32[]{:S(2)}) collective-permute-start(bf16[256,1024]{1,0:T(8,128)(2,1)S(1)} %get-tuple-element.60), channel_id=1, source_target_pairs={{0,8},{4,12},{8,0},{12,4},{1,9},{5,13},{9,1},{13,5},{2,10},{6,14},... | collective-permute-start | bytes 1572872 | tf_op jit(solution)/shard_map/ppermute | solution.py:394
  93.4 13.8 %collective-permute-start.23 = (bf16[256,1024]{1,0:T(8,128)(2,1)S(1)}, bf16[256,1024]{1,0:T(8,128)(2,1)S(1)}, u32[]{:S(2)}, u32[]{:S(2)}) collective-permute-start(bf16[256,1024]{1,0:T(8,128)(2,1)S(1)} %collective-permute-done.12.refs_2_), channel_id=1, source_target_pairs={{0,16},{16,0},{1,17},{17,1},{2,18},{18,2},{3,19},{19,3},{4,20},{20... | collective-permute-start | bytes 1572872 | tf_op jit(solution)/shard_map/ppermute | solution.py:452
  94.9 13.3 %collective-permute-start.16 = (bf16[256,1024]{1,0:T(8,128)(2,1)S(1)}, bf16[256,1024]{1,0:T(8,128)(2,1)S(1)}, u32[]{:S(2)}, u32[]{:S(2)}) collective-permute-start(bf16[256,1024]{1,0:T(8,128)(2,1)S(1)} %constant_dynamic-update-slice_fusion.own), channel_id=1, source_target_pairs={{0,1},{1,2},{2,3},{4,5},{5,6},{6,7},{8,9},{9,10},{10,11},{12,13},{... | collective-permute-start | bytes 1572872 | tf_op jit(solution)/shard_map/ppermute | solution.py:397
  97.3 16.1 %collective-permute-start.19 = (bf16[256,1024]{1,0:T(8,128)(2,1)S(1)}, bf16[256,1024]{1,0:T(8,128)(2,1)S(1)}, u32[]{:S(2)}, u32[]{:S(2)}) collective-permute-start(bf16[256,1024]{1,0:T(8,128)(2,1)S(1)} %constant_dynamic-update-slice_fusion.own), channel_id=1, source_target_pairs={{1,0},{2,1},{3,2},{5,4},{6,5},{7,6},{9,8},{10,9},{11,10},{13,12},{... | collective-permute-start | bytes 1572872 | tf_op jit(solution)/shard_map/ppermute | solution.py:397
  108.3 12.6 %collective-permute-start.24 = (bf16[256,1024]{1,0:T(8,128)(2,1)S(1)}, bf16[256,1024]{1,0:T(8,128)(2,1)S(1)}, u32[]{:S(2)}, u32[]{:S(2)}) collective-permute-start(bf16[256,1024]{1,0:T(8,128)(2,1)S(1)} %collective-permute-done.22.refs_4_), channel_id=1, source_target_pairs={{0,16},{16,0},{1,17},{17,1},{2,18},{18,2},{3,19},{19,3},{4,20},{20... | collective-permute-start | bytes 1572872 | tf_op jit(solution)/shard_map/ppermute | solution.py:452
  108.8 12.1 %collective-permute-start.17 = (bf16[256,1024]{1,0:T(8,128)(2,1)S(1)}, bf16[256,1024]{1,0:T(8,128)(2,1)S(1)}, u32[]{:S(2)}, u32[]{:S(2)}) collective-permute-start(bf16[256,1024]{1,0:T(8,128)(2,1)S(1)} %collective-permute-done.16.below_1), channel_id=1, source_target_pairs={{1,2},{2,3},{5,6},{6,7},{9,10},{10,11},{13,14},{14,15},{17,18},{18... | collective-permute-start | bytes 1572872 | tf_op jit(solution)/shard_map/ppermute | solution.py:397
  113.4 14.7 %collective-permute-start.20 = (bf16[256,1024]{1,0:T(8,128)(2,1)S(1)}, bf16[256,1024]{1,0:T(8,128)(2,1)S(1)}, u32[]{:S(2)}, u32[]{:S(2)}) collective-permute-start(bf16[256,1024]{1,0:T(8,128)(2,1)S(1)} %collective-permute-done.19.above_1), channel_id=1, source_target_pairs={{1,0},{2,1},{5,4},{6,5},{9,8},{10,9},{13,12},{14,13},{17,16},{18,1... | collective-permute-start | bytes 1572872 | tf_op jit(solution)/shard_map/ppermute | solution.py:397
  120.8 8.5 %collective-permute-start.28 = (bf16[256,1024]{1,0:T(8,128)(2,1)S(1)}, bf16[256,1024]{1,0:T(8,128)(2,1)S(1)}, u32[]{:S(2)}, u32[]{:S(2)}) collective-permute-start(bf16[256,1024]{1,0:T(8,128)(2,1)S(1)} %collective-permute-done.24.refs_5_), channel_id=1, source_target_pairs={{0,4},{4,0},{8,12},{12,8},{1,5},{5,1},{9,13},{13,9},{2,6},{6,2},{1... | collective-permute-start | bytes 1572872 | tf_op jit(solution)/shard_map/ppermute | solution.py:394
  120.8 9.3 %collective-permute-start.25 = (bf16[256,1024]{1,0:T(8,128)(2,1)S(1)}, bf16[256,1024]{1,0:T(8,128)(2,1)S(1)}, u32[]{:S(2)}, u32[]{:S(2)}) collective-permute-start(bf16[256,1024]{1,0:T(8,128)(2,1)S(1)} %collective-permute-done.12.refs_2_), channel_id=1, source_target_pairs={{0,4},{4,0},{8,12},{12,8},{1,5},{5,1},{9,13},{13,9},{2,6},{6,2},{1... | collective-permute-start | bytes 1572872 | tf_op jit(solution)/shard_map/ppermute | solution.py:394
  121.3 8.8 %collective-permute-start.26 = (bf16[256,1024]{1,0:T(8,128)(2,1)S(1)}, bf16[256,1024]{1,0:T(8,128)(2,1)S(1)}, u32[]{:S(2)}, u32[]{:S(2)}) collective-permute-start(bf16[256,1024]{1,0:T(8,128)(2,1)S(1)} %collective-permute-done.23.refs_3_), channel_id=1, source_target_pairs={{0,4},{4,0},{8,12},{12,8},{1,5},{5,1},{9,13},{13,9},{2,6},{6,2},{1... | collective-permute-start | bytes 1572872 | tf_op jit(solution)/shard_map/ppermute | solution.py:394
  121.4 8.8 %collective-permute-start.27 = (bf16[256,1024]{1,0:T(8,128)(2,1)S(1)}, bf16[256,1024]{1,0:T(8,128)(2,1)S(1)}, u32[]{:S(2)}, u32[]{:S(2)}) collective-permute-start(bf16[256,1024]{1,0:T(8,128)(2,1)S(1)} %collective-permute-done.22.refs_4_), channel_id=1, source_target_pairs={{0,4},{4,0},{8,12},{12,8},{1,5},{5,1},{9,13},{13,9},{2,6},{6,2},{1... | collective-permute-start | bytes 1572872 | tf_op jit(solution)/shard_map/ppermute | solution.py:394
  128.1 13.3 %collective-permute-start.21 = (bf16[256,1024]{1,0:T(8,128)(2,1)S(1)}, bf16[256,1024]{1,0:T(8,128)(2,1)S(1)}, u32[]{:S(2)}, u32[]{:S(2)}) collective-permute-start(bf16[256,1024]{1,0:T(8,128)(2,1)S(1)} %collective-permute-done.20.above_2), channel_id=1, source_target_pairs={{1,0},{5,4},{9,8},{13,12},{17,16},{21,20},{25,24},{29,28}} | collective-permute-start | bytes 1572872 | tf_op jit(solution)/shard_map/ppermute | solution.py:397
  129.4 12.0 %collective-permute-start.18 = (bf16[256,1024]{1,0:T(8,128)(2,1)S(1)}, bf16[256,1024]{1,0:T(8,128)(2,1)S(1)}, u32[]{:S(2)}, u32[]{:S(2)}) collective-permute-start(bf16[256,1024]{1,0:T(8,128)(2,1)S(1)} %collective-permute-done.17.below_2), channel_id=1, source_target_pairs={{2,3},{6,7},{10,11},{14,15},{18,19},{22,23},{26,27},{30,31}} | collective-permute-start | bytes 1572872 | tf_op jit(solution)/shard_map/ppermute | solution.py:397

commit v7 on v6

--- a/solution.py
+++ b/solution.py
@@ -295,12 +295,10 @@
     )(index, local_near, local_far, other, gain, gate, up, down)
 
 
-def mix_kernel(index_ref, own, below_1, above_1, below_2, above_2, *refs):
-    own_w, peer_w = refs[:2]
-    parts, peer_parts = refs[2:6], refs[6:10]
-    out_ref, last_ref, held = refs[10:]
+def mix_kernel(index_ref, own, below_1, above_1, below_2, above_2, own_w, peer_w, one, other, one_peer, other_peer,
+               out_ref, rest_ref, last_ref, held):
     place, seq, last = index_ref[PLACE], index_ref[SEQ], index_ref[LAST]
-    size = parts[0].shape[0]
+    size = one.shape[0]
 
     @pl.when(pl.program_id(0) == 0)
     def _():
@@ -309,15 +307,21 @@
         held[lax.rem(place + 1, 4)] = above_1[...]
         held[lax.rem(place + 2, 4)] = jnp.where(place >= 2, below_2[...], above_2[...])
 
+    last_ref[...] = jnp.zeros_like(last_ref)
     total = None
     for k in range(4):
         owner = lax.bitwise_xor(seq, k)
         for part in range(4):
+            head = part if k < 2 else index_ref[PARTS + part]
+            column = pl.multiple_of(index_ref[BLOCKS + head] * size, size)
+            if k >= 2 and part >= 2:
+                place_in_rest = (2 * (k - 2) + part - 2) * size
+                rest_ref[:, place_in_rest : place_in_rest + size] = held[owner, :, pl.ds(column, size)]
+                continue
             if k < 2:
-                ref, head, here = (own_w, peer_w)[k], part, pl.ds(part * size, size)
+                ref, here = (own_w, peer_w)[k], pl.ds(part * size, size)
             else:
-                ref, head, here = (parts, peer_parts)[k - 2][part], index_ref[PARTS + part], pl.ds(0, size)
-            column = pl.multiple_of(index_ref[BLOCKS + head] * size, size)
+                ref, here = ((one, other), (one_peer, other_peer))[k - 2][part], pl.ds(0, size)
             term = dot(held[owner, :, pl.ds(column, size)], ref[here, :])
             total = term if total is None else total + term
 
@@ -328,52 +332,71 @@
     out_ref[...] = total
 
 
-def mix(index, shards, own, peer, parts, peer_parts):
+def mix(index, shards, own, peer, firsts):
     rows, width = shards[0].shape
     depth, columns = own.shape
-    size = parts[0].shape[0]
+    size = firsts[0].shape[0]
     tile = columns // 2
     shard = pl.BlockSpec((rows, width), lambda i, idx: (0, 0))
     whole = pl.BlockSpec((depth, tile), lambda i, idx: (0, i))
     part = pl.BlockSpec((size, tile), lambda i, idx: (0, i))
     return pl.pallas_call(
         mix_kernel,
-        out_shape=[jax.ShapeDtypeStruct((rows, columns), F32), jax.ShapeDtypeStruct((depth, columns), BF16)],
+        out_shape=[
+            jax.ShapeDtypeStruct((rows, columns), F32),
+            jax.ShapeDtypeStruct((rows, 4 * size), BF16),
+            jax.ShapeDtypeStruct((depth, columns), BF16),
+        ],
         grid_spec=pltpu.PrefetchScalarGridSpec(
             num_scalar_prefetch=1,
             grid=(2,),
-            in_specs=[shard] * 5 + [whole] * 2 + [part] * 8,
-            out_specs=[pl.BlockSpec((rows, tile), lambda i, idx: (0, i)), whole],
+            in_specs=[shard] * 5 + [whole] * 2 + [part] * 4,
+            out_specs=[
+                pl.BlockSpec((rows, tile), lambda i, idx: (0, i)),
+                pl.BlockSpec((rows, 4 * size), lambda i, idx: (0, 0)),
+                whole,
+            ],
             scratch_shapes=[pltpu.VMEM((4, rows, width), BF16)],
         ),
         compiler_params=params(),
         cost_estimate=pl.CostEstimate(flops=1, bytes_accessed=1, transcendentals=0),
-    )(index, *shards, own, peer, *parts, *peer_parts)
-
-
-def last_kernel(index_ref, below, above, weight, before, out_ref):
-    block = jnp.where(index_ref[PLACE] == 0, above[...], below[...])
-    out_ref[...] = (before[...] + dot(block, weight[...])).astype(out_ref.dtype)
-
-
-def mix_last(index, below, above, weight, before):
+    )(index, *shards, own, peer, *firsts)
+
+
+def last_kernel(index_ref, below, above, weight, rest, one, other, one_peer, other_peer, before, out_ref, held):
+    size = one.shape[0]
+    held[...] = jnp.where(index_ref[PLACE] == 0, above[...], below[...])
+    total = before[...] + dot(held[...], weight[...])
+    for i, ref in enumerate((one, other, one_peer, other_peer)):
+        owner = lax.bitwise_xor(index_ref[SEQ], 2 + i // 2)
+        column = pl.multiple_of(index_ref[BLOCKS + index_ref[PARTS + 2 + i % 2]] * size, size)
+        kept = rest[:, i * size : (i + 1) * size]
+        block = jnp.where(owner == index_ref[LAST], held[:, pl.ds(column, size)], kept)
+        total += dot(block, ref[...])
+    out_ref[...] = total.astype(out_ref.dtype)
+
+
+def mix_last(index, below, above, weight, rest, laters, before):
     rows, width = below.shape
     columns = weight.shape[1]
+    size = laters[0].shape[0]
     tile = columns // 2
     slab = pl.BlockSpec((rows, tile), lambda i, idx: (0, i))
     shard = pl.BlockSpec((rows, width), lambda i, idx: (0, 0))
+    part = pl.BlockSpec((size, tile), lambda i, idx: (0, i))
     return pl.pallas_call(
         last_kernel,
         out_shape=jax.ShapeDtypeStruct((rows, columns), BF16),
         grid_spec=pltpu.PrefetchScalarGridSpec(
             num_scalar_prefetch=1,
             grid=(2,),
-            in_specs=[shard, shard, pl.BlockSpec((width, tile), lambda i, idx: (0, i)), slab],
+            in_specs=[shard, shard, pl.BlockSpec((width, tile), lambda i, idx: (0, i)), shard] + [part] * 4 + [slab],
             out_specs=slab,
+            scratch_shapes=[pltpu.VMEM((rows, width), BF16)],
         ),
         compiler_params=params(),
         cost_estimate=pl.CostEstimate(flops=1, bytes_accessed=1, transcendentals=0),
-    )(index, below, above, weight, before)
+    )(index, below, above, weight, rest, *laters, before)
 
 
 def after(value, *others):
@@ -396,7 +419,7 @@
     def hop(array, links):
         return lax.ppermute(array, "head", links)
 
-    values = [chip, core, head, place, seq, jnp.where(place == 0, 3, 0)]
+    values = [chip, core, head, place, seq, jnp.where(place == 0, 3, jnp.where(place == 3, 0, -1))]
     values += [2 * side, 2 * (1 - side), 2 * side + 1, 2 * (1 - side) + 1]
     values += [((other >> 1) ^ core) + 2 * ((other & 1) ^ chip) for other in range(4)]
     odd = place & 1
@@ -432,14 +455,12 @@
     out_peer = across(after(out_weight, send_far), 1)
     held = after(given, send_query, out_peer)
     local_far = project(index, [], far, weight, held, size, True, 1, 3, F32)
-    send_query, out_first, _, _ = lax.optimization_barrier((send_query, out_first, got_near, local_far))
+    send_query = after(send_query, got_near, local_far)
     got_query = across(send_query, 2)
-    first_x = across(out_first, 2)
 
     rates = (rates_near, rates_far)
     fresh = update(index, local_near, local_far, got_near, got_far, *rates, fast_gate, fast_up, fast_down)
     normed = read_out(index, local_near, local_far, got_query, out_gain.reshape(4, 1, size), *fresh)
-    *normed, first_x = lax.optimization_barrier((*normed, first_x))
     pieces = [normed[0], across(normed[1], 1), across(normed[2], 2), across(normed[3], 3)]
     shard = jnp.concatenate(pieces, axis=1)
 
@@ -451,23 +472,23 @@
     def swap_groups(array):
         return lax.ppermute(array, "groups", [(0, 1), (1, 0)])
 
-    later_x = across(after(out_later, shard), 2)
-    first_y = swap_groups(after(first_x, shard))
+    first_x = across(after(out_first, shard), 2)
     below_1, above_1 = both(0, shard, shard)
+    first_x, out_later = lax.optimization_barrier((first_x, out_later, below_1, above_1))[:2]
+    first_y = swap_groups(first_x)
+    later_x = across(out_later, 2)
     below_2, above_2 = both(1, below_1, above_1)
-    later_x, first_y = lax.optimization_barrier((later_x, first_y, below_1))[:2]
+    first_x_peer, first_y_peer, later_x = (after(array, below_2, above_2) for array in (first_x, first_y, later_x))
+    first_x_peer, first_y_peer = across(first_x_peer, 1), across(first_y_peer, 1)
     later_y = swap_groups(later_x)
     below_3, above_3 = both(2, below_2, above_2)
-    first_y_peer, later_x_peer, first_x_peer = (
-        across(after(array, below_2), 1) for array in (first_y, later_x, first_x)
-    )
-    later_y_peer = across(later_y, 1)
 
     shards = [shard, below_1, above_1, below_2, above_2]
-    parts = [first_x, first_y, later_x, later_y]
-    peer_parts = [first_x_peer, first_y_peer, later_x_peer, later_y_peer]
-    mixed, weight_last = mix(index, shards, out_weight, out_peer, parts, peer_parts)
-    return mix_last(index, below_3, above_3, weight_last, mixed)
+    firsts = [first_x, first_y, first_x_peer, first_y_peer]
+    mixed, rest, weight_last = mix(index, shards, out_weight, out_peer, firsts)
+    later_x, later_y, mixed = lax.optimization_barrier((later_x, later_y, mixed))
+    laters = [later_x, later_y, across(later_x, 1), across(later_y, 1)]
+    return mix_last(index, below_3, above_3, weight_last, rest, laters, mixed)
 
 
 def on_device(axis_sizes, tokens, qkv_weight, rate_weight, fast_gate, fast_up, fast_down, out_gain, out_weight):

time: 144 us -> 143 us (level)
  waiting for transfers between devices: 56.9 us -> 52.4 us
  starting transfers between devices: 26.8 us -> 30.2 us
    ppermute x20, waiting for transfers between devices: 32.6 us -> 26.5 us  [across(): return lax.ppermute(array, 'seq', [(i, i ^ bit) for i in range(4)])]
    ppermute x7, waiting for transfers between devices: 16.9 us -> 19.6 us  [hop(): return lax.ppermute(array, 'head', links)]
    ppermute x7, starting transfers between devices: 10.5 us -> 12.7 us  [hop(): return lax.ppermute(array, 'head', links)]
  transfers between devices with their start and end apart: 29 -> 29, of which waited for: 14 -> 13; matrix products, arithmetic and copies ran while one was open for 3% -> 3% of each run, Pallas kernels for 27% -> 25%
where the time goes in v7:
time: 143 us
  waiting for transfers between devices  52.4 us (37%)
  Pallas kernels  44.8 us (31%)
  starting transfers between devices  30.2 us (21%)
  local copies, waits for them, and re-layouts  12.6 us (9%)
  matrix products  2.25 us (2%)
    ppermute x20, waiting for transfers between devices, across(): return lax.ppermute(array, 'seq', [(i, i ^ bit) for i in range(4)])  26.5 us
    pallas_call x5, Pallas kernels, project(): pl.pallas_call(functools.partial(project_kernel, len(whole), len(pairs)),...  20.7 us
    ppermute x7, waiting for transfers between devices, hop(): return lax.ppermute(array, 'head', links)  19.6 us
    ppermute x20, starting transfers between devices, across(): return lax.ppermute(array, 'seq', [(i, i ^ bit) for i in range(4)])  14.4 us
    pallas_call x1, Pallas kernels, update(): pl.pallas_call(update_kernel, out_shape=[out] * 3, grid_spec=pltpu.Prefet...  14.2 us
    ppermute x7, starting transfers between devices, hop(): return lax.ppermute(array, 'head', links)  12.7 us
    ppermute x2, waiting for transfers between devices, swap_groups(): return lax.ppermute(array, 'groups', [(0, 1), (1, 0)])  6.24 us
    unnamed x19, local copies, waits for them, and re-layouts  5.63 us
  transfers between devices with their start and end apart: 29, of which 13 were waited for; matrix products, arithmetic and copies ran while one was open for 3% of the time, Pallas kernels for 25%

profile of v7, /device:TPU:0, one launch (start us, length us, event | category | flops | bytes accessed | tf_op | source)
XLA Modules:
  0.0 142.5 jit_solution(16943057479316409400)
XLA Ops:
  0.0 1.9 %constant_dynamic-slice_fusion.2 = bf16[256,1024]{1,0:T(8,128)(2,1)} fusion(bf16[256,4096]{1,0:T(8,128)(2,1)} %refs_0_.5, s32[]{:T(128)S(6)} %select_n.23), kind=kLoop, calls=%fused_computation.10 | loop fusion | bytes 1048580 | tf_op jit(solution)/shard_map/dynamic_slice | solution.py:429
  1.9 3.7 %dynamic-slice_bitcast_fusion = bf16[3,1024,512]{2,1,0:T(8,128)(2,1)} fusion(bf16[1024,3,1024]{2,0,1:T(8,128)(2,1)} %param.9, s32[]{:T(128)S(6)} %select_n.24), kind=kLoop, calls=%fused_computation | loop fusion | bytes 6291460 | tf_op jit(solution)/shard_map/dynamic_slice | solution.py:433
  5.6 0.5 collective-permute-start.1
  6.1 0.1 collective-permute-start
  6.1 2.9 %collective-permute-start.2 = (bf16[256,1024]{1,0:T(8,128)(2,1)}, bf16[256,1024]{1,0:T(8,128)(2,1)}, u32[]{:S(2)}, u32[]{:S(2)}) collective-permute-start(bf16[256,1024]{1,0:T(8,128)(2,1)} %constant_dynamic-slice_fusion.2), channel_id=1, source_target_pairs={{0,8},{4,12},{8,0},{12,4},{1,9},{5,13},{9,1},{13,5},{2,10},{6,14},... | collective-permute-start | bytes 1572872 | tf_op jit(solution)/shard_map/ppermute | solution.py:417
  9.0 0.1 stack.63.index_ref
  9.1 5.5 %collective-permute-done.refs_1_ = bf16[256,4096]{1,0:T(8,128)(2,1)} collective-permute-done((bf16[256,4096]{1,0:T(8,128)(2,1)}, bf16[256,4096]{1,0:T(8,128)(2,1)}, u32[]{:S(2)}, u32[]{:S(2)}) %collective-permute-start) | collective-permute-done | bytes 2097184 | tf_op jit(solution)/shard_map/ppermute | solution.py:417
  14.6 2.8 %copy-done.1 = bf16[1024,3,1024]{2,0,1:T(8,128)(2,1)S(1)} copy-done((bf16[1024,3,1024]{2,0,1:T(8,128)(2,1)S(1)}, bf16[1024,3,1024]{2,0,1:T(8,128)(2,1)}, u32[]{:S(2)}) %copy-start.1) | copy-done | bytes 6291480
  17.4 4.4 %shard_map.82 = bf16[2,512,256]{2,1,0:T(8,128)(2,1)} custom-call(s32[15]{0:T(128)S(1)} %stack.63.index_ref, bf16[256,4096]{1,0:T(8,128)(2,1)} %refs_0_.5, bf16[256,4096]{1,0:T(8,128)(2,1)} %collective-permute-done.refs_1_, bf16[3,1024,1024]{2,1,0:T(8,128)(2,1)S(1)} %bitcast.25, bf16[3,1024,512]{2,1,0:T(8,128)(2,1)S(1)} %collective-permute-done.1.refs_3_.refs_5_.refs_7_), custom_call_target="tpu_custom_call" | custom-call | flops 1 | bytes 1 | tf_op jit(solution)/shard_map/pallas_call | solution.py:146
  21.8 2.9 %collective-permute-start.3 = (bf16[256,1024]{1,0:T(8,128)(2,1)}, bf16[256,1024]{1,0:T(8,128)(2,1)}, u32[]{:S(2)}, u32[]{:S(2)}) collective-permute-start(bf16[256,1024]{1,0:T(8,128)(2,1)} %collective-permute-done.2.refs_0_.refs_2_), channel_id=1, source_target_pairs={{0,1},{1,0},{2,3},{3,2},{4,5},{5,4},{6,7},{7,6},{8,9},{9,8},{10,11... | collective-permute-start | bytes 1572872 | tf_op jit(solution)/shard_map/ppermute | solution.py:420
  24.7 1.5 %collective-permute-start.4 = (bf16[2,512,256]{2,1,0:T(8,128)(2,1)}, bf16[2,512,256]{2,1,0:T(8,128)(2,1)}, u32[]{:S(2)}, u32[]{:S(2)}) collective-permute-start(bf16[2,512,256]{2,1,0:T(8,128)(2,1)} %shard_map.82), channel_id=1, source_target_pairs={{0,8},{4,12},{8,0},{12,4},{1,9},{5,13},{9,1},{13,5},{2,10},{6,14},... | collective-permute-start | bytes 1572872 | tf_op jit(solution)/shard_map/ppermute | solution.py:417
  26.2 2.3 %compare_select_fusion = f32[4,256]{1,0:T(4,128)S(1)} fusion(bf16[256,4096]{1,0:T(8,128)(2,1)} %refs_0_.5, bf16[4096,4]{0,1:T(4,128)(2,1)S(1)} %copy-done), kind=kOutput, calls=%fused_computation.2 | convolution fusion | flops 8394752 | bytes 2134016 | tf_op jit(solution)/shard_map/dot_general | solution.py:445
  28.5 0.1 collective-permute-start.5
  28.5 0.5 collective-permute-start.7
  29.0 0.7 collective-permute-done.5
  29.7 0.5 collective-permute-start.6
  30.2 1.3 constant_dynamic-slice_fusion.1
  31.5 0.0 copy-start.2
  31.5 2.8 %copy-done.2 = bf16[1024,3,1024]{2,0,1:T(8,128)(2,1)S(1)} copy-done((bf16[1024,3,1024]{2,0,1:T(8,128)(2,1)S(1)}, bf16[1024,3,1024]{2,0,1:T(8,128)(2,1)}, u32[]{:S(2)}) %copy-start.2) | copy-done | bytes 6291480
  34.3 4.6 %shard_map.83.local_near_ref = f32[3,512,256]{2,1,0:T(8,128)S(1)} custom-call(s32[15]{0:T(128)S(1)} %stack.63.index_ref, bf16[256,4096]{1,0:T(8,128)(2,1)} %refs_0_.5, bf16[256,4096]{1,0:T(8,128)(2,1)} %collective-permute-done.refs_1_, bf16[3,1024,1024]{2,1,0:T(8,128)(2,1)S(1)} %bitcast.26, ...), custom_call_target="tpu_custom_call" | custom-call | flops 1 | bytes 1 | tf_op jit(solution)/shard_map/pallas_call | solution.py:146
  38.9 0.0 collective-permute-done.4.far_ref
  38.9 0.0 copy-start.3
  38.9 0.1 collective-permute-start.8
  39.0 2.1 %collective-permute-done.8.refs_3_.refs_5_ = bf16[256,1024]{1,0:T(8,128)(2,1)S(1)} collective-permute-done((bf16[256,1024]{1,0:T(8,128)(2,1)}, bf16[256,1024]{1,0:T(8,128)(2,1)S(1)}, u32[]{:S(2)}, u32[]{:S(2)}) %collective-permute-start.8) | collective-permute-done | bytes 524320 | tf_op jit(solution)/shard_map/ppermute | solution.py:417
  41.1 3.4 %shard_map.84 = bf16[2,512,256]{2,1,0:T(8,128)(2,1)S(1)} custom-call(s32[15]{0:T(128)S(1)} %stack.63.index_ref, bf16[256,1024]{1,0:T(8,128)(2,1)} %collective-permute-done.2.refs_0_.refs_2_, bf16[256,1024]{1,0:T(8,128)(2,1)} %collective-permute-done.3.refs_1_.refs_3_, bf16[256,1024]{1,0:T(8,128)(2,1)S(1)} %collective-permute-done.7.refs_2_.refs_4_, ...), custom_call_target="tpu_custom_call" | custom-call | flops 1 | bytes 1 | tf_op jit(solution)/shard_map/pallas_call | solution.py:146
  44.5 0.2 collective-permute-start.9
  44.7 1.5 %collective-permute-start.10 = (bf16[2,512,256]{2,1,0:T(8,128)(2,1)S(1)}, bf16[2,512,256]{2,1,0:T(8,128)(2,1)S(1)}, u32[]{:S(2)}, u32[]{:S(2)}) collective-permute-start(bf16[2,512,256]{2,1,0:T(8,128)(2,1)S(1)} %shard_map.84), channel_id=1, source_target_pairs={{0,8},{4,12},{8,0},{12,4},{1,9},{5,13},{9,1},{13,5},{2,10},{6,14},... | collective-permute-start | bytes 1572872 | tf_op jit(solution)/shard_map/ppermute | solution.py:417
  46.2 3.9 %shard_map.85 = bf16[1,1024,256]{2,1,0:T(8,128)(2,1)S(1)} custom-call(s32[15]{0:T(128)S(1)} %stack.63.index_ref, bf16[256,4096]{1,0:T(8,128)(2,1)} %refs_0_.5, bf16[256,4096]{1,0:T(8,128)(2,1)} %collective-permute-done.refs_1_, bf16[256,1024]{1,0:T(8,128)(2,1)} %collective-permute-done.2.refs_0_.refs_2_, ...), custom_call_target="tpu_custom_call" | custom-call | flops 1 | bytes 1 | tf_op jit(solution)/shard_map/pallas_call | solution.py:146
  50.1 0.0 copy-start.4
  50.2 0.0 copy-start.5
  50.2 0.0 copy-start.6
  50.2 4.4 %shard_map.86.local_far_ref = f32[3,512,256]{2,1,0:T(8,128)S(1)} custom-call(s32[15]{0:T(128)S(1)} %stack.63.index_ref, bf16[256,1024]{1,0:T(8,128)(2,1)} %collective-permute-done.2.refs_0_.refs_2_, bf16[256,1024]{1,0:T(8,128)(2,1)} %collective-permute-done.3.refs_1_.refs_3_, bf16[256,1024]{1,0:T(8,128)(2,1)S(1)} %collective-permute-done.7.refs_2_.refs_4_, ...), custom_call_target="tpu_custom_call" | custom-call | flops 1 | bytes 1 | tf_op jit(solution)/shard_map/pallas_call | solution.py:146
  54.6 0.0 copy-start.7
  54.6 4.2 %collective-permute-done.10.near_ref = bf16[2,512,256]{2,1,0:T(8,128)(2,1)S(1)} collective-permute-done((bf16[2,512,256]{2,1,0:T(8,128)(2,1)S(1)}, bf16[2,512,256]{2,1,0:T(8,128)(2,1)S(1)}, u32[]{:S(2)}, u32[]{:S(2)}) %collective-permute-start.10) | collective-permute-done | bytes 524320 | tf_op jit(solution)/shard_map/ppermute | solution.py:417
  58.9 1.5 %collective-permute-start.11 = (bf16[1,1024,256]{2,1,0:T(8,128)(2,1)S(1)}, bf16[1,1024,256]{2,1,0:T(8,128)(2,1)S(1)}, u32[]{:S(2)}, u32[]{:S(2)}) collective-permute-start(bf16[1,1024,256]{2,1,0:T(8,128)(2,1)S(1)} %shard_map.85), channel_id=1, source_target_pairs={{0,8},{4,12},{8,0},{12,4},{1,9},{5,13},{9,1},{13,5},{2,10},{6,14},... | collective-permute-start | bytes 1572872 | tf_op jit(solution)/shard_map/ppermute | solution.py:417
  60.4 14.2 %shard_map.87 = (bf16[256,512]{1,0:T(8,128)(2,1)S(1)}, bf16[256,512]{1,0:T(8,128)(2,1)S(1)}, bf16[256,512]{1,0:T(8,128)(2,1)S(1)}) custom-call(s32[15]{0:T(128)S(1)} %stack.63.index_ref, f32[3,512,256]{2,1,0:T(8,128)S(1)} %shard_map.83.local_near_ref, f32[3,512,256]{2,1,0:T(8,128)S(1)} %shard_map.86.local_far_ref, ...), custom_call_target="tpu_custom_call" | custom-call | flops 1 | bytes 1 | tf_op jit(solution)/shard_map/pallas_call | solution.py:230
  74.6 0.0 collective-permute-done.11.other_ref
  74.6 2.0 %shard_map.88 = (bf16[256,256]{1,0:T(8,128)(2,1)S(1)}, bf16[256,256]{1,0:T(8,128)(2,1)S(1)}, bf16[256,256]{1,0:T(8,128)(2,1)S(1)}, bf16[256,256]{1,0:T(8,128)(2,1)S(1)}) custom-call(s32[15]{0:T(128)S(1)} %stack.63.index_ref, f32[3,512,256]{2,1,0:T(8,128)S(1)} %shard_map.83.local_near_ref, f32[3,512,256]{2,1,0:T(8,128)S(1)} %shard_map.86.local_far_ref, ...), custom_call_target="tpu_custom_call" | custom-call | flops 1 | bytes 1 | tf_op jit(solution)/shard_map/pallas_call | solution.py:276
  76.6 0.1 collective-permute-start.12
  76.7 0.6 collective-permute-start.13
  77.3 1.2 collective-permute-start.14
  78.6 4.5 %collective-permute-done.13 = bf16[256,256]{1,0:T(8,128)(2,1)S(1)} collective-permute-done((bf16[256,256]{1,0:T(8,128)(2,1)S(1)}, bf16[256,256]{1,0:T(8,128)(2,1)S(1)}, u32[]{:S(2)}, u32[]{:S(2)}) %collective-permute-start.13) | collective-permute-done | bytes 131104 | tf_op jit(solution)/shard_map/ppermute | solution.py:417
  83.1 1.9 %collective-permute-done.14 = bf16[256,256]{1,0:T(8,128)(2,1)S(1)} collective-permute-done((bf16[256,256]{1,0:T(8,128)(2,1)S(1)}, bf16[256,256]{1,0:T(8,128)(2,1)S(1)}, u32[]{:S(2)}, u32[]{:S(2)}) %collective-permute-start.14) | collective-permute-done | bytes 131104 | tf_op jit(solution)/shard_map/ppermute | solution.py:417
  85.0 0.6 collective-permute-start.21
  85.6 1.3 collective-permute-start.18
  86.9 4.6 %collective-permute-start.15 = (bf16[256,1024]{1,0:T(8,128)(2,1)S(1)}, bf16[256,1024]{1,0:T(8,128)(2,1)S(1)}, u32[]{:S(2)}, u32[]{:S(2)}) collective-permute-start(bf16[256,1024]{1,0:T(8,128)(2,1)S(1)} %constant_dynamic-update-slice_fusion.own), channel_id=1, source_target_pairs={{0,1},{1,2},{2,3},{4,5},{5,6},{6,7},{8,9},{9,10},{10,11},{12,13},{... | collective-permute-start | bytes 1572872 | tf_op jit(solution)/shard_map/ppermute | solution.py:420
  91.5 7.7 %collective-permute-done.21.one = bf16[256,1024]{1,0:T(8,128)(2,1)S(1)} collective-permute-done((bf16[256,1024]{1,0:T(8,128)(2,1)S(1)}, bf16[256,1024]{1,0:T(8,128)(2,1)S(1)}, u32[]{:S(2)}, u32[]{:S(2)}) %collective-permute-start.21) | collective-permute-done | bytes 524320 | tf_op jit(solution)/shard_map/ppermute | solution.py:417
  99.2 2.1 %collective-permute-done.18.above_1 = bf16[256,1024]{1,0:T(8,128)(2,1)S(1)} collective-permute-done((bf16[256,1024]{1,0:T(8,128)(2,1)S(1)}, bf16[256,1024]{1,0:T(8,128)(2,1)S(1)}, u32[]{:S(2)}, u32[]{:S(2)}) %collective-permute-start.18) | collective-permute-done | bytes 524320 | tf_op jit(solution)/shard_map/ppermute | solution.py:420
  101.3 1.2 collective-permute-done.15.below_1
  102.5 1.3 collective-permute-start.19
  103.8 1.5 %collective-permute-start.25 = (bf16[256,1024]{1,0:T(8,128)(2,1)S(1)}, bf16[256,1024]{1,0:T(8,128)(2,1)S(1)}, u32[]{:S(2)}, u32[]{:S(2)}) collective-permute-start(bf16[256,1024]{1,0:T(8,128)(2,1)S(1)} %get-tuple-element.57), channel_id=1, source_target_pairs={{0,8},{4,12},{8,0},{12,4},{1,9},{5,13},{9,1},{13,5},{2,10},{6,14},... | collective-permute-start | bytes 1572872 | tf_op jit(solution)/shard_map/ppermute | solution.py:417
  105.3 0.7 collective-permute-start.16
  106.0 1.6 %collective-permute-start.22 = (bf16[256,1024]{1,0:T(8,128)(2,1)S(1)}, bf16[256,1024]{1,0:T(8,128)(2,1)S(1)}, u32[]{:S(2)}, u32[]{:S(2)}) collective-permute-start(bf16[256,1024]{1,0:T(8,128)(2,1)S(1)} %collective-permute-done.21.one), channel_id=1, source_target_pairs={{0,16},{16,0},{1,17},{17,1},{2,18},{18,2},{3,19},{19,3},{4,20},{20... | collective-permute-start | bytes 1572872 | tf_op jit(solution)/shard_map/ppermute | solution.py:473
  107.6 10.2 %collective-permute-done.19.above_2 = bf16[256,1024]{1,0:T(8,128)(2,1)S(1)} collective-permute-done((bf16[256,1024]{1,0:T(8,128)(2,1)S(1)}, bf16[256,1024]{1,0:T(8,128)(2,1)S(1)}, u32[]{:S(2)}, u32[]{:S(2)}) %collective-permute-start.19) | collective-permute-done | bytes 524320 | tf_op jit(solution)/shard_map/ppermute | solution.py:420
  117.8 0.7 collective-permute-done.22.other
  118.5 0.5 collective-permute-start.24
  119.0 1.5 %collective-permute-start.26 = (bf16[256,1024]{1,0:T(8,128)(2,1)S(1)}, bf16[256,1024]{1,0:T(8,128)(2,1)S(1)}, u32[]{:S(2)}, u32[]{:S(2)}) collective-permute-start(bf16[256,1024]{1,0:T(8,128)(2,1)S(1)} %collective-permute-done.25.one), channel_id=1, source_target_pairs={{0,16},{16,0},{1,17},{17,1},{2,18},{18,2},{3,19},{19,3},{4,20},{20... | collective-permute-start | bytes 1572872 | tf_op jit(solution)/shard_map/ppermute | solution.py:473
  120.5 1.3 collective-permute-start.20
  121.8 0.7 collective-permute-start.17
  122.5 4.7 %shard_map.89 = (f32[256,1024]{1,0:T(8,128)S(1)}, bf16[256,1024]{1,0:T(8,128)(2,1)S(1)}, bf16[1024,1024]{1,0:T(8,128)(2,1)S(1)}) custom-call(s32[15]{0:T(128)S(1)} %stack.63.index_ref, bf16[256,1024]{1,0:T(8,128)(2,1)S(1)} %constant_dynamic-update-slice_fusion.own, bf16[256,1024]{1,0:T(8,128)(2,1)S(1)} %collective-permute-done.15.below_1, ...), custom_call_target="tpu_custom_call" | custom-call | flops 1 | bytes 1 | tf_op jit(solution)/shard_map/pallas_call | solution.py:343
  127.2 5.6 %collective-permute-done.26.other = bf16[256,1024]{1,0:T(8,128)(2,1)S(1)} collective-permute-done((bf16[256,1024]{1,0:T(8,128)(2,1)S(1)}, bf16[256,1024]{1,0:T(8,128)(2,1)S(1)}, u32[]{:S(2)}, u32[]{:S(2)}) %collective-permute-start.26) | collective-permute-done | bytes 524320 | tf_op jit(solution)/shard_map/ppermute | solution.py:473
  132.8 0.5 collective-permute-start.28
  133.3 6.1 %collective-permute-done.20.above = bf16[256,1024]{1,0:T(8,128)(2,1)S(1)} collective-permute-done((bf16[256,1024]{1,0:T(8,128)(2,1)S(1)}, bf16[256,1024]{1,0:T(8,128)(2,1)S(1)}, u32[]{:S(2)}, u32[]{:S(2)}) %collective-permute-start.20) | collective-permute-done | bytes 524320 | tf_op jit(solution)/shard_map/ppermute | solution.py:420
  139.4 3.1 %shard_map.90 = bf16[256,1024]{1,0:T(8,128)(2,1)} custom-call(s32[15]{0:T(128)S(1)} %stack.63.index_ref, bf16[256,1024]{1,0:T(8,128)(2,1)S(1)} %collective-permute-done.17.below, bf16[256,1024]{1,0:T(8,128)(2,1)S(1)} %collective-permute-done.20.above, bf16[1024,1024]{1,0:T(8,128)(2,1)S(1)} %get-tuple-element.55.weight, ...), custom_call_target="tpu_custom_call" | custom-call | flops 1 | bytes 1 | tf_op jit(solution)/shard_map/pallas_call | solution.py:387
  (29 shorter events, 0.1 us)
Async XLA Ops:
  0.0 26.2 %copy-start = (bf16[4096,4]{0,1:T(4,128)(2,1)S(1)}, bf16[4096,4]{0,1:T(4,128)(2,1)}, u32[]{:S(2)}) copy-start(bf16[4096,4]{0,1:T(4,128)(2,1)} %param.10) | copy-start | bytes 98308
  5.6 9.0 %collective-permute-start.1 = (bf16[3,1024,512]{2,1,0:T(8,128)(2,1)}, bf16[3,1024,512]{2,1,0:T(8,128)(2,1)S(1)}, u32[]{:S(2)}, u32[]{:S(2)}) collective-permute-start(bf16[3,1024,512]{2,1,0:T(8,128)(2,1)} %dynamic-slice_bitcast_fusion), channel_id=1, source_target_pairs={{0,4},{4,0},{8,12},{12,8},{1,5},{5,1},{9,13},{13,9},{2,6},{6,2},{1... | collective-permute-start | bytes 9437192 | tf_op jit(solution)/shard_map/ppermute | solution.py:417
  6.1 8.5 %collective-permute-start = (bf16[256,4096]{1,0:T(8,128)(2,1)}, bf16[256,4096]{1,0:T(8,128)(2,1)}, u32[]{:S(2)}, u32[]{:S(2)}) collective-permute-start(bf16[256,4096]{1,0:T(8,128)(2,1)} %refs_0_.5), channel_id=1, source_target_pairs={{0,4},{4,0},{8,12},{12,8},{1,5},{5,1},{9,13},{13,9},{2,6},{6,2},{1... | collective-permute-start | bytes 6291464 | tf_op jit(solution)/shard_map/ppermute | solution.py:417
  6.1 15.7 %collective-permute-start.2 = (bf16[256,1024]{1,0:T(8,128)(2,1)}, bf16[256,1024]{1,0:T(8,128)(2,1)}, u32[]{:S(2)}, u32[]{:S(2)}) collective-permute-start(bf16[256,1024]{1,0:T(8,128)(2,1)} %constant_dynamic-slice_fusion.2), channel_id=1, source_target_pairs={{0,8},{4,12},{8,0},{12,4},{1,9},{5,13},{9,1},{13,5},{2,10},{6,14},... | collective-permute-start | bytes 1572872 | tf_op jit(solution)/shard_map/ppermute | solution.py:417
  14.6 2.8 %copy-start.1 = (bf16[1024,3,1024]{2,0,1:T(8,128)(2,1)S(1)}, bf16[1024,3,1024]{2,0,1:T(8,128)(2,1)}, u32[]{:S(2)}) copy-start(bf16[1024,3,1024]{2,0,1:T(8,128)(2,1)} %param.9) | copy-start | bytes 18874372
  21.8 17.1 %collective-permute-start.3 = (bf16[256,1024]{1,0:T(8,128)(2,1)}, bf16[256,1024]{1,0:T(8,128)(2,1)}, u32[]{:S(2)}, u32[]{:S(2)}) collective-permute-start(bf16[256,1024]{1,0:T(8,128)(2,1)} %collective-permute-done.2.refs_0_.refs_2_), channel_id=1, source_target_pairs={{0,1},{1,0},{2,3},{3,2},{4,5},{5,4},{6,7},{7,6},{8,9},{9,8},{10,11... | collective-permute-start | bytes 1572872 | tf_op jit(solution)/shard_map/ppermute | solution.py:420
  24.7 14.2 %collective-permute-start.4 = (bf16[2,512,256]{2,1,0:T(8,128)(2,1)}, bf16[2,512,256]{2,1,0:T(8,128)(2,1)}, u32[]{:S(2)}, u32[]{:S(2)}) collective-permute-start(bf16[2,512,256]{2,1,0:T(8,128)(2,1)} %shard_map.82), channel_id=1, source_target_pairs={{0,8},{4,12},{8,0},{12,4},{1,9},{5,13},{9,1},{13,5},{2,10},{6,14},... | collective-permute-start | bytes 1572872 | tf_op jit(solution)/shard_map/ppermute | solution.py:417
  28.5 1.2 collective-permute-start.5
  28.5 10.4 %collective-permute-start.7 = (bf16[256,1024]{1,0:T(8,128)(2,1)}, bf16[256,1024]{1,0:T(8,128)(2,1)S(1)}, u32[]{:S(2)}, u32[]{:S(2)}) collective-permute-start(bf16[256,1024]{1,0:T(8,128)(2,1)} %collective-permute-done.2.refs_0_.refs_2_), channel_id=1, source_target_pairs={{0,4},{4,0},{8,12},{12,8},{1,5},{5,1},{9,13},{13,9},{2,6},{6,2},{1... | collective-permute-start | bytes 1572872 | tf_op jit(solution)/shard_map/ppermute | solution.py:417
  29.7 9.2 %collective-permute-start.6 = (f32[8,256]{1,0:T(8,128)S(1)}, f32[8,256]{1,0:T(8,128)S(1)}, u32[]{:S(2)}, u32[]{:S(2)}) collective-permute-start(f32[8,256]{1,0:T(8,128)S(1)} %pad_maximum_fusion.rate_near_ref), channel_id=1, source_target_pairs={{0,8},{4,12},{8,0},{12,4},{1,9},{5,13},{9,1},{13,5},{2,10},{6,14},... | collective-permute-start | bytes 24584 | tf_op jit(solution)/shard_map/ppermute | solution.py:417
  31.5 2.8 %copy-start.2 = (bf16[1024,3,1024]{2,0,1:T(8,128)(2,1)S(1)}, bf16[1024,3,1024]{2,0,1:T(8,128)(2,1)}, u32[]{:S(2)}) copy-start(bf16[1024,3,1024]{2,0,1:T(8,128)(2,1)} %param.9) | copy-start | bytes 18874372
  38.9 5.6 %copy-start.3 = (bf16[1024,1024]{1,0:T(8,128)(2,1)S(1)}, bf16[1024,1024]{1,0:T(8,128)(2,1)}, u32[]{:S(2)}) copy-start(bf16[1024,1024]{1,0:T(8,128)(2,1)} %own_w.1) | copy-start | bytes 6291460
  38.9 2.2 %collective-permute-start.8 = (bf16[256,1024]{1,0:T(8,128)(2,1)}, bf16[256,1024]{1,0:T(8,128)(2,1)S(1)}, u32[]{:S(2)}, u32[]{:S(2)}) collective-permute-start(bf16[256,1024]{1,0:T(8,128)(2,1)} %collective-permute-done.3.refs_1_.refs_3_), channel_id=1, source_target_pairs={{0,4},{4,0},{8,12},{12,8},{1,5},{5,1},{9,13},{13,9},{2,6},{6,2},{1... | collective-permute-start | bytes 1572872 | tf_op jit(solution)/shard_map/ppermute | solution.py:417
  44.5 5.7 %collective-permute-start.9 = (bf16[1024,1024]{1,0:T(8,128)(2,1)S(1)}, bf16[1024,1024]{1,0:T(8,128)(2,1)S(1)}, u32[]{:S(2)}, u32[]{:S(2)}) collective-permute-start(bf16[1024,1024]{1,0:T(8,128)(2,1)S(1)} %copy-done.3), channel_id=1, source_target_pairs={{0,4},{4,0},{8,12},{12,8},{1,5},{5,1},{9,13},{13,9},{2,6},{6,2},{1... | collective-permute-start | bytes 6291464 | tf_op jit(solution)/shard_map/ppermute | solution.py:417
  44.7 14.2 %collective-permute-start.10 = (bf16[2,512,256]{2,1,0:T(8,128)(2,1)S(1)}, bf16[2,512,256]{2,1,0:T(8,128)(2,1)S(1)}, u32[]{:S(2)}, u32[]{:S(2)}) collective-permute-start(bf16[2,512,256]{2,1,0:T(8,128)(2,1)S(1)} %shard_map.84), channel_id=1, source_target_pairs={{0,8},{4,12},{8,0},{12,4},{1,9},{5,13},{9,1},{13,5},{2,10},{6,14},... | collective-permute-start | bytes 1572872 | tf_op jit(solution)/shard_map/ppermute | solution.py:417
  50.1 10.2 %copy-start.4 = (bf16[4,256,512]{2,1,0:T(8,128)(2,1)S(1)}, bf16[4,256,512]{2,1,0:T(8,128)(2,1)}, u32[]{:S(2)}) copy-start(bf16[4,256,512]{2,1,0:T(8,128)(2,1)} %gate_ref.1) | copy-start | bytes 3145732
  50.2 10.2 %copy-start.5 = (bf16[4,256,512]{2,1,0:T(8,128)(2,1)S(1)}, bf16[4,256,512]{2,1,0:T(8,128)(2,1)}, u32[]{:S(2)}) copy-start(bf16[4,256,512]{2,1,0:T(8,128)(2,1)} %up_ref.1) | copy-start | bytes 3145732
  50.2 10.2 %copy-start.6 = (bf16[4,256,512]{2,1,0:T(8,128)(2,1)S(1)}, bf16[4,256,512]{2,1,0:T(8,128)(2,1)}, u32[]{:S(2)}) copy-start(bf16[4,256,512]{2,1,0:T(8,128)(2,1)} %down_ref.1) | copy-start | bytes 3145732
  54.6 20.0 %copy-start.7 = (f32[1024]{0:T(1024)S(1)}, f32[1024]{0:T(1024)}, u32[]{:S(2)}) copy-start(f32[1024]{0:T(1024)} %param.14) | copy-start | bytes 12292
  58.9 15.7 %collective-permute-start.11 = (bf16[1,1024,256]{2,1,0:T(8,128)(2,1)S(1)}, bf16[1,1024,256]{2,1,0:T(8,128)(2,1)S(1)}, u32[]{:S(2)}, u32[]{:S(2)}) collective-permute-start(bf16[1,1024,256]{2,1,0:T(8,128)(2,1)S(1)} %shard_map.85), channel_id=1, source_target_pairs={{0,8},{4,12},{8,0},{12,4},{1,9},{5,13},{9,1},{13,5},{2,10},{6,14},... | collective-permute-start | bytes 1572872 | tf_op jit(solution)/shard_map/ppermute | solution.py:417
  76.6 2.0 %collective-permute-start.12 = (bf16[256,256]{1,0:T(8,128)(2,1)S(1)}, bf16[256,256]{1,0:T(8,128)(2,1)S(1)}, u32[]{:S(2)}, u32[]{:S(2)}) collective-permute-start(bf16[256,256]{1,0:T(8,128)(2,1)S(1)} %get-tuple-element.48), channel_id=1, source_target_pairs={{0,4},{4,0},{8,12},{12,8},{1,5},{5,1},{9,13},{13,9},{2,6},{6,2},{1... | collective-permute-start | bytes 393224 | tf_op jit(solution)/shard_map/ppermute | solution.py:417
  76.7 6.4 %collective-permute-start.13 = (bf16[256,256]{1,0:T(8,128)(2,1)S(1)}, bf16[256,256]{1,0:T(8,128)(2,1)S(1)}, u32[]{:S(2)}, u32[]{:S(2)}) collective-permute-start(bf16[256,256]{1,0:T(8,128)(2,1)S(1)} %get-tuple-element.49), channel_id=1, source_target_pairs={{0,8},{4,12},{8,0},{12,4},{1,9},{5,13},{9,1},{13,5},{2,10},{6,14},... | collective-permute-start | bytes 393224 | tf_op jit(solution)/shard_map/ppermute | solution.py:417
  77.3 7.7 %collective-permute-start.14 = (bf16[256,256]{1,0:T(8,128)(2,1)S(1)}, bf16[256,256]{1,0:T(8,128)(2,1)S(1)}, u32[]{:S(2)}, u32[]{:S(2)}) collective-permute-start(bf16[256,256]{1,0:T(8,128)(2,1)S(1)} %get-tuple-element.50), channel_id=1, source_target_pairs={{0,12},{4,8},{8,4},{12,0},{1,13},{5,9},{9,5},{13,1},{2,14},{6,10},... | collective-permute-start | bytes 393224 | tf_op jit(solution)/shard_map/ppermute | solution.py:417
  85.0 14.2 %collective-permute-start.21 = (bf16[256,1024]{1,0:T(8,128)(2,1)S(1)}, bf16[256,1024]{1,0:T(8,128)(2,1)S(1)}, u32[]{:S(2)}, u32[]{:S(2)}) collective-permute-start(bf16[256,1024]{1,0:T(8,128)(2,1)S(1)} %get-tuple-element.51), channel_id=1, source_target_pairs={{0,8},{4,12},{8,0},{12,4},{1,9},{5,13},{9,1},{13,5},{2,10},{6,14},... | collective-permute-start | bytes 1572872 | tf_op jit(solution)/shard_map/ppermute | solution.py:417
  85.6 15.7 %collective-permute-start.18 = (bf16[256,1024]{1,0:T(8,128)(2,1)S(1)}, bf16[256,1024]{1,0:T(8,128)(2,1)S(1)}, u32[]{:S(2)}, u32[]{:S(2)}) collective-permute-start(bf16[256,1024]{1,0:T(8,128)(2,1)S(1)} %constant_dynamic-update-slice_fusion.own), channel_id=1, source_target_pairs={{1,0},{2,1},{3,2},{5,4},{6,5},{7,6},{9,8},{10,9},{11,10},{13,12},{... | collective-permute-start | bytes 1572872 | tf_op jit(solution)/shard_map/ppermute | solution.py:420
  86.9 15.6 %collective-permute-start.15 = (bf16[256,1024]{1,0:T(8,128)(2,1)S(1)}, bf16[256,1024]{1,0:T(8,128)(2,1)S(1)}, u32[]{:S(2)}, u32[]{:S(2)}) collective-permute-start(bf16[256,1024]{1,0:T(8,128)(2,1)S(1)} %constant_dynamic-update-slice_fusion.own), channel_id=1, source_target_pairs={{0,1},{1,2},{2,3},{4,5},{5,6},{6,7},{8,9},{9,10},{10,11},{12,13},{... | collective-permute-start | bytes 1572872 | tf_op jit(solution)/shard_map/ppermute | solution.py:420
  102.5 15.3 %collective-permute-start.19 = (bf16[256,1024]{1,0:T(8,128)(2,1)S(1)}, bf16[256,1024]{1,0:T(8,128)(2,1)S(1)}, u32[]{:S(2)}, u32[]{:S(2)}) collective-permute-start(bf16[256,1024]{1,0:T(8,128)(2,1)S(1)} %collective-permute-done.18.above_1), channel_id=1, source_target_pairs={{1,0},{2,1},{5,4},{6,5},{9,8},{10,9},{13,12},{14,13},{17,16},{18,1... | collective-permute-start | bytes 1572872 | tf_op jit(solution)/shard_map/ppermute | solution.py:420
  103.8 14.0 %collective-permute-start.25 = (bf16[256,1024]{1,0:T(8,128)(2,1)S(1)}, bf16[256,1024]{1,0:T(8,128)(2,1)S(1)}, u32[]{:S(2)}, u32[]{:S(2)}) collective-permute-start(bf16[256,1024]{1,0:T(8,128)(2,1)S(1)} %get-tuple-element.57), channel_id=1, source_target_pairs={{0,8},{4,12},{8,0},{12,4},{1,9},{5,13},{9,1},{13,5},{2,10},{6,14},... | collective-permute-start | bytes 1572872 | tf_op jit(solution)/shard_map/ppermute | solution.py:417
  105.3 12.5 %collective-permute-start.16 = (bf16[256,1024]{1,0:T(8,128)(2,1)S(1)}, bf16[256,1024]{1,0:T(8,128)(2,1)S(1)}, u32[]{:S(2)}, u32[]{:S(2)}) collective-permute-start(bf16[256,1024]{1,0:T(8,128)(2,1)S(1)} %collective-permute-done.15.below_1), channel_id=1, source_target_pairs={{1,2},{2,3},{5,6},{6,7},{9,10},{10,11},{13,14},{14,15},{17,18},{18... | collective-permute-start | bytes 1572872 | tf_op jit(solution)/shard_map/ppermute | solution.py:420
  106.0 12.4 %collective-permute-start.22 = (bf16[256,1024]{1,0:T(8,128)(2,1)S(1)}, bf16[256,1024]{1,0:T(8,128)(2,1)S(1)}, u32[]{:S(2)}, u32[]{:S(2)}) collective-permute-start(bf16[256,1024]{1,0:T(8,128)(2,1)S(1)} %collective-permute-done.21.one), channel_id=1, source_target_pairs={{0,16},{16,0},{1,17},{17,1},{2,18},{18,2},{3,19},{19,3},{4,20},{20... | collective-permute-start | bytes 1572872 | tf_op jit(solution)/shard_map/ppermute | solution.py:473
  118.5 4.0 %collective-permute-start.23 = (bf16[256,1024]{1,0:T(8,128)(2,1)S(1)}, bf16[256,1024]{1,0:T(8,128)(2,1)S(1)}, u32[]{:S(2)}, u32[]{:S(2)}) collective-permute-start(bf16[256,1024]{1,0:T(8,128)(2,1)S(1)} %collective-permute-done.21.one), channel_id=1, source_target_pairs={{0,4},{4,0},{8,12},{12,8},{1,5},{5,1},{9,13},{13,9},{2,6},{6,2},{1... | collective-permute-start | bytes 1572872 | tf_op jit(solution)/shard_map/ppermute | solution.py:417
  118.5 4.0 %collective-permute-start.24 = (bf16[256,1024]{1,0:T(8,128)(2,1)S(1)}, bf16[256,1024]{1,0:T(8,128)(2,1)S(1)}, u32[]{:S(2)}, u32[]{:S(2)}) collective-permute-start(bf16[256,1024]{1,0:T(8,128)(2,1)S(1)} %collective-permute-done.22.other), channel_id=1, source_target_pairs={{0,4},{4,0},{8,12},{12,8},{1,5},{5,1},{9,13},{13,9},{2,6},{6,2},{1... | collective-permute-start | bytes 1572872 | tf_op jit(solution)/shard_map/ppermute | solution.py:417
  119.0 13.8 %collective-permute-start.26 = (bf16[256,1024]{1,0:T(8,128)(2,1)S(1)}, bf16[256,1024]{1,0:T(8,128)(2,1)S(1)}, u32[]{:S(2)}, u32[]{:S(2)}) collective-permute-start(bf16[256,1024]{1,0:T(8,128)(2,1)S(1)} %collective-permute-done.25.one), channel_id=1, source_target_pairs={{0,16},{16,0},{1,17},{17,1},{2,18},{18,2},{3,19},{19,3},{4,20},{20... | collective-permute-start | bytes 1572872 | tf_op jit(solution)/shard_map/ppermute | solution.py:473
  120.5 18.9 %collective-permute-start.20 = (bf16[256,1024]{1,0:T(8,128)(2,1)S(1)}, bf16[256,1024]{1,0:T(8,128)(2,1)S(1)}, u32[]{:S(2)}, u32[]{:S(2)}) collective-permute-start(bf16[256,1024]{1,0:T(8,128)(2,1)S(1)} %collective-permute-done.19.above_2), channel_id=1, source_target_pairs={{1,0},{5,4},{9,8},{13,12},{17,16},{21,20},{25,24},{29,28}} | collective-permute-start | bytes 1572872 | tf_op jit(solution)/shard_map/ppermute | solution.py:420
  121.8 17.6 %collective-permute-start.17 = (bf16[256,1024]{1,0:T(8,128)(2,1)S(1)}, bf16[256,1024]{1,0:T(8,128)(2,1)S(1)}, u32[]{:S(2)}, u32[]{:S(2)}) collective-permute-start(bf16[256,1024]{1,0:T(8,128)(2,1)S(1)} %collective-permute-done.16.below_2), channel_id=1, source_target_pairs={{2,3},{6,7},{10,11},{14,15},{18,19},{22,23},{26,27},{30,31}} | collective-permute-start | bytes 1572872 | tf_op jit(solution)/shard_map/ppermute | solution.py:420
  132.8 6.6 %collective-permute-start.27 = (bf16[256,1024]{1,0:T(8,128)(2,1)S(1)}, bf16[256,1024]{1,0:T(8,128)(2,1)S(1)}, u32[]{:S(2)}, u32[]{:S(2)}) collective-permute-start(bf16[256,1024]{1,0:T(8,128)(2,1)S(1)} %collective-permute-done.25.one), channel_id=1, source_target_pairs={{0,4},{4,0},{8,12},{12,8},{1,5},{5,1},{9,13},{13,9},{2,6},{6,2},{1... | collective-permute-start | bytes 1572872 | tf_op jit(solution)/shard_map/ppermute | solution.py:417
  132.8 6.6 %collective-permute-start.28 = (bf16[256,1024]{1,0:T(8,128)(2,1)S(1)}, bf16[256,1024]{1,0:T(8,128)(2,1)S(1)}, u32[]{:S(2)}, u32[]{:S(2)}) collective-permute-start(bf16[256,1024]{1,0:T(8,128)(2,1)S(1)} %collective-permute-done.26.other), channel_id=1, source_target_pairs={{0,4},{4,0},{8,12},{12,8},{1,5},{5,1},{9,13},{13,9},{2,6},{6,2},{1... | collective-permute-start | bytes 1572872 | tf_op jit(solution)/shard_map/ppermute | solution.py:417

commit v8 on v7

--- a/solution.py
+++ b/solution.py
@@ -461,8 +461,9 @@
     rates = (rates_near, rates_far)
     fresh = update(index, local_near, local_far, got_near, got_far, *rates, fast_gate, fast_up, fast_down)
     normed = read_out(index, local_near, local_far, got_query, out_gain.reshape(4, 1, size), *fresh)
-    pieces = [normed[0], across(normed[1], 1), across(normed[2], 2), across(normed[3], 3)]
-    shard = jnp.concatenate(pieces, axis=1)
+    mine = jnp.concatenate([normed[0], across(normed[1], 1)], axis=1)
+    theirs = jnp.concatenate([across(normed[2], 2), across(normed[3], 3)], axis=1)
+    shard = jnp.concatenate([mine, theirs], axis=1)
 
     def both(number, below, above):
         up = [(i, i + 1) for i in range(number, 3)]
@@ -472,8 +473,12 @@
     def swap_groups(array):
         return lax.ppermute(array, "groups", [(0, 1), (1, 0)])
 
-    first_x = across(after(out_first, shard), 2)
-    below_1, above_1 = both(0, shard, shard)
+    first_x = across(after(out_first, theirs), 2)
+    below_mine, above_mine = both(0, mine, mine)
+    theirs, below_mine, above_mine = lax.optimization_barrier((theirs, below_mine, above_mine))
+    below_theirs, above_theirs = both(0, theirs, theirs)
+    below_1 = jnp.concatenate([below_mine, below_theirs], axis=1)
+    above_1 = jnp.concatenate([above_mine, above_theirs], axis=1)
     first_x, out_later = lax.optimization_barrier((first_x, out_later, below_1, above_1))[:2]
     first_y = swap_groups(first_x)
     later_x = across(out_later, 2)

time: 143 us -> 139 us (0.972)
  waiting for transfers between devices: 52.4 us -> 43 us
  starting transfers between devices: 30.2 us -> 35.1 us
    ppermute x20, waiting for transfers between devices: 26.5 us -> 13.2 us  [across(): return lax.ppermute(array, 'seq', [(i, i ^ bit) for i in range(4)])]
    ppermute x7 -> x9, starting transfers between devices: 12.7 us -> 19 us  [hop(): return lax.ppermute(array, 'head', links)]
    ppermute x7 -> x9, waiting for transfers between devices: 19.6 us -> 23.6 us  [hop(): return lax.ppermute(array, 'head', links)]
    unnamed x19 -> x20, local copies, waits for them, and re-layouts: 5.63 us -> 5.67 us
  transfers between devices with their start and end apart: 29 -> 31, of which waited for: 13 -> 13; matrix products, arithmetic and copies ran while one was open for 3% -> 3% of each run, Pallas kernels for 25% -> 26%
where the time goes in v8:
time: 139 us; the launch traced here: 138 us
  Pallas kernels  44.8 us (32%)
  waiting for transfers between devices  43 us (31%)
  starting transfers between devices  35.1 us (25%)
  local copies, waits for them, and re-layouts  12.7 us (9%)
  matrix products  2.25 us (2%)
    ppermute x9, waiting for transfers between devices, hop(): return lax.ppermute(array, 'head', links)  23.6 us
    pallas_call x5, Pallas kernels, project(): pl.pallas_call(functools.partial(project_kernel, len(whole), len(pairs)),...  20.7 us
    ppermute x9, starting transfers between devices, hop(): return lax.ppermute(array, 'head', links)  19 us
    pallas_call x1, Pallas kernels, update(): pl.pallas_call(update_kernel, out_shape=[out] * 3, grid_spec=pltpu.Prefet...  14.2 us
    ppermute x20, waiting for transfers between devices, across(): return lax.ppermute(array, 'seq', [(i, i ^ bit) for i in range(4)])  13.2 us
    ppermute x20, starting transfers between devices, across(): return lax.ppermute(array, 'seq', [(i, i ^ bit) for i in range(4)])  13 us
    ppermute x2, waiting for transfers between devices, swap_groups(): return lax.ppermute(array, 'groups', [(0, 1), (1, 0)])  6.19 us
    unnamed x20, local copies, waits for them, and re-layouts  5.67 us
  transfers between devices with their start and end apart: 31, of which 13 were waited for; matrix products, arithmetic and copies ran while one was open for 3% of the time, Pallas kernels for 26%

profile of v8, /device:TPU:0, one launch (start us, length us, event | category | flops | bytes accessed | tf_op | source)
XLA Modules:
  0.0 138.3 jit_solution(2809144448054274236)
XLA Ops:
  0.0 1.9 %constant_dynamic-slice_fusion.2 = bf16[256,1024]{1,0:T(8,128)(2,1)} fusion(bf16[256,4096]{1,0:T(8,128)(2,1)} %refs_0_.5, s32[]{:T(128)S(6)} %select_n.23), kind=kLoop, calls=%fused_computation.15 | loop fusion | bytes 1048580 | tf_op jit(solution)/shard_map/dynamic_slice | solution.py:429
  1.9 3.7 %dynamic-slice_bitcast_fusion = bf16[3,1024,512]{2,1,0:T(8,128)(2,1)} fusion(bf16[1024,3,1024]{2,0,1:T(8,128)(2,1)} %param.9, s32[]{:T(128)S(6)} %select_n.24), kind=kLoop, calls=%fused_computation | loop fusion | bytes 6291460 | tf_op jit(solution)/shard_map/dynamic_slice | solution.py:433
  5.6 0.5 collective-permute-start.1
  6.1 0.1 collective-permute-start
  6.1 2.9 %collective-permute-start.2 = (bf16[256,1024]{1,0:T(8,128)(2,1)}, bf16[256,1024]{1,0:T(8,128)(2,1)}, u32[]{:S(2)}, u32[]{:S(2)}) collective-permute-start(bf16[256,1024]{1,0:T(8,128)(2,1)} %constant_dynamic-slice_fusion.2), channel_id=1, source_target_pairs={{0,8},{4,12},{8,0},{12,4},{1,9},{5,13},{9,1},{13,5},{2,10},{6,14},... | collective-permute-start | bytes 1572872 | tf_op jit(solution)/shard_map/ppermute | solution.py:417
  9.1 0.1 stack.63.index_ref
  9.2 5.5 %collective-permute-done.refs_1_ = bf16[256,4096]{1,0:T(8,128)(2,1)} collective-permute-done((bf16[256,4096]{1,0:T(8,128)(2,1)}, bf16[256,4096]{1,0:T(8,128)(2,1)}, u32[]{:S(2)}, u32[]{:S(2)}) %collective-permute-start) | collective-permute-done | bytes 2097184 | tf_op jit(solution)/shard_map/ppermute | solution.py:417
  14.6 2.8 %copy-done.1 = bf16[1024,3,1024]{2,0,1:T(8,128)(2,1)S(1)} copy-done((bf16[1024,3,1024]{2,0,1:T(8,128)(2,1)S(1)}, bf16[1024,3,1024]{2,0,1:T(8,128)(2,1)}, u32[]{:S(2)}) %copy-start.1) | copy-done | bytes 6291480
  17.4 4.4 %shard_map.82 = bf16[2,512,256]{2,1,0:T(8,128)(2,1)} custom-call(s32[15]{0:T(128)S(1)} %stack.63.index_ref, bf16[256,4096]{1,0:T(8,128)(2,1)} %refs_0_.5, bf16[256,4096]{1,0:T(8,128)(2,1)} %collective-permute-done.refs_1_, bf16[3,1024,1024]{2,1,0:T(8,128)(2,1)S(1)} %bitcast.25, bf16[3,1024,512]{2,1,0:T(8,128)(2,1)S(1)} %collective-permute-done.1.refs_3_.refs_5_.refs_7_), custom_call_target="tpu_custom_call" | custom-call | flops 1 | bytes 1 | tf_op jit(solution)/shard_map/pallas_call | solution.py:146
  21.8 2.9 %collective-permute-start.3 = (bf16[256,1024]{1,0:T(8,128)(2,1)}, bf16[256,1024]{1,0:T(8,128)(2,1)}, u32[]{:S(2)}, u32[]{:S(2)}) collective-permute-start(bf16[256,1024]{1,0:T(8,128)(2,1)} %collective-permute-done.2.refs_0_.refs_2_), channel_id=1, source_target_pairs={{0,1},{1,0},{2,3},{3,2},{4,5},{5,4},{6,7},{7,6},{8,9},{9,8},{10,11... | collective-permute-start | bytes 1572872 | tf_op jit(solution)/shard_map/ppermute | solution.py:420
  24.7 1.5 %collective-permute-start.4 = (bf16[2,512,256]{2,1,0:T(8,128)(2,1)}, bf16[2,512,256]{2,1,0:T(8,128)(2,1)}, u32[]{:S(2)}, u32[]{:S(2)}) collective-permute-start(bf16[2,512,256]{2,1,0:T(8,128)(2,1)} %shard_map.82), channel_id=1, source_target_pairs={{0,8},{4,12},{8,0},{12,4},{1,9},{5,13},{9,1},{13,5},{2,10},{6,14},... | collective-permute-start | bytes 1572872 | tf_op jit(solution)/shard_map/ppermute | solution.py:417
  26.2 2.3 %compare_select_fusion = f32[4,256]{1,0:T(4,128)S(1)} fusion(bf16[256,4096]{1,0:T(8,128)(2,1)} %refs_0_.5, bf16[4096,4]{0,1:T(4,128)(2,1)S(1)} %copy-done), kind=kOutput, calls=%fused_computation.11 | convolution fusion | flops 8394752 | bytes 2134016 | tf_op jit(solution)/shard_map/dot_general | solution.py:445
  28.5 0.1 collective-permute-start.5
  28.6 0.5 collective-permute-start.7
  29.1 0.7 collective-permute-done.5
  29.7 0.5 collective-permute-start.6
  30.3 1.3 constant_dynamic-slice_fusion.1
  31.5 0.0 copy-start.2
  31.5 2.8 %copy-done.2 = bf16[1024,3,1024]{2,0,1:T(8,128)(2,1)S(1)} copy-done((bf16[1024,3,1024]{2,0,1:T(8,128)(2,1)S(1)}, bf16[1024,3,1024]{2,0,1:T(8,128)(2,1)}, u32[]{:S(2)}) %copy-start.2) | copy-done | bytes 6291480
  34.3 4.6 %shard_map.83.local_near_ref = f32[3,512,256]{2,1,0:T(8,128)S(1)} custom-call(s32[15]{0:T(128)S(1)} %stack.63.index_ref, bf16[256,4096]{1,0:T(8,128)(2,1)} %refs_0_.5, bf16[256,4096]{1,0:T(8,128)(2,1)} %collective-permute-done.refs_1_, bf16[3,1024,1024]{2,1,0:T(8,128)(2,1)S(1)} %bitcast.26, ...), custom_call_target="tpu_custom_call" | custom-call | flops 1 | bytes 1 | tf_op jit(solution)/shard_map/pallas_call | solution.py:146
  38.9 0.0 copy-start.3
  38.9 0.1 collective-permute-start.8
  39.0 2.1 %collective-permute-done.8.refs_3_.refs_5_ = bf16[256,1024]{1,0:T(8,128)(2,1)S(1)} collective-permute-done((bf16[256,1024]{1,0:T(8,128)(2,1)}, bf16[256,1024]{1,0:T(8,128)(2,1)S(1)}, u32[]{:S(2)}, u32[]{:S(2)}) %collective-permute-start.8) | collective-permute-done | bytes 524320 | tf_op jit(solution)/shard_map/ppermute | solution.py:417
  41.1 3.4 %shard_map.84 = bf16[2,512,256]{2,1,0:T(8,128)(2,1)S(1)} custom-call(s32[15]{0:T(128)S(1)} %stack.63.index_ref, bf16[256,1024]{1,0:T(8,128)(2,1)} %collective-permute-done.2.refs_0_.refs_2_, bf16[256,1024]{1,0:T(8,128)(2,1)} %collective-permute-done.3.refs_1_.refs_3_, bf16[256,1024]{1,0:T(8,128)(2,1)S(1)} %collective-permute-done.7.refs_2_.refs_4_, ...), custom_call_target="tpu_custom_call" | custom-call | flops 1 | bytes 1 | tf_op jit(solution)/shard_map/pallas_call | solution.py:146
  44.5 0.2 collective-permute-start.9
  44.7 1.5 %collective-permute-start.10 = (bf16[2,512,256]{2,1,0:T(8,128)(2,1)S(1)}, bf16[2,512,256]{2,1,0:T(8,128)(2,1)S(1)}, u32[]{:S(2)}, u32[]{:S(2)}) collective-permute-start(bf16[2,512,256]{2,1,0:T(8,128)(2,1)S(1)} %shard_map.84), channel_id=1, source_target_pairs={{0,8},{4,12},{8,0},{12,4},{1,9},{5,13},{9,1},{13,5},{2,10},{6,14},... | collective-permute-start | bytes 1572872 | tf_op jit(solution)/shard_map/ppermute | solution.py:417
  46.2 3.9 %shard_map.85 = bf16[1,1024,256]{2,1,0:T(8,128)(2,1)S(1)} custom-call(s32[15]{0:T(128)S(1)} %stack.63.index_ref, bf16[256,4096]{1,0:T(8,128)(2,1)} %refs_0_.5, bf16[256,4096]{1,0:T(8,128)(2,1)} %collective-permute-done.refs_1_, bf16[256,1024]{1,0:T(8,128)(2,1)} %collective-permute-done.2.refs_0_.refs_2_, ...), custom_call_target="tpu_custom_call" | custom-call | flops 1 | bytes 1 | tf_op jit(solution)/shard_map/pallas_call | solution.py:146
  50.2 0.0 copy-start.4
  50.2 0.0 copy-start.6
  50.2 4.4 %shard_map.86.local_far_ref = f32[3,512,256]{2,1,0:T(8,128)S(1)} custom-call(s32[15]{0:T(128)S(1)} %stack.63.index_ref, bf16[256,1024]{1,0:T(8,128)(2,1)} %collective-permute-done.2.refs_0_.refs_2_, bf16[256,1024]{1,0:T(8,128)(2,1)} %collective-permute-done.3.refs_1_.refs_3_, bf16[256,1024]{1,0:T(8,128)(2,1)S(1)} %collective-permute-done.7.refs_2_.refs_4_, ...), custom_call_target="tpu_custom_call" | custom-call | flops 1 | bytes 1 | tf_op jit(solution)/shard_map/pallas_call | solution.py:146
  54.7 0.0 copy-start.7
  54.7 4.2 %collective-permute-done.10.near_ref = bf16[2,512,256]{2,1,0:T(8,128)(2,1)S(1)} collective-permute-done((bf16[2,512,256]{2,1,0:T(8,128)(2,1)S(1)}, bf16[2,512,256]{2,1,0:T(8,128)(2,1)S(1)}, u32[]{:S(2)}, u32[]{:S(2)}) %collective-permute-start.10) | collective-permute-done | bytes 524320 | tf_op jit(solution)/shard_map/ppermute | solution.py:417
  58.9 1.5 %collective-permute-start.11 = (bf16[1,1024,256]{2,1,0:T(8,128)(2,1)S(1)}, bf16[1,1024,256]{2,1,0:T(8,128)(2,1)S(1)}, u32[]{:S(2)}, u32[]{:S(2)}) collective-permute-start(bf16[1,1024,256]{2,1,0:T(8,128)(2,1)S(1)} %shard_map.85), channel_id=1, source_target_pairs={{0,8},{4,12},{8,0},{12,4},{1,9},{5,13},{9,1},{13,5},{2,10},{6,14},... | collective-permute-start | bytes 1572872 | tf_op jit(solution)/shard_map/ppermute | solution.py:417
  60.4 14.2 %shard_map.87 = (bf16[256,512]{1,0:T(8,128)(2,1)S(1)}, bf16[256,512]{1,0:T(8,128)(2,1)S(1)}, bf16[256,512]{1,0:T(8,128)(2,1)S(1)}) custom-call(s32[15]{0:T(128)S(1)} %stack.63.index_ref, f32[3,512,256]{2,1,0:T(8,128)S(1)} %shard_map.83.local_near_ref, f32[3,512,256]{2,1,0:T(8,128)S(1)} %shard_map.86.local_far_ref, ...), custom_call_target="tpu_custom_call" | custom-call | flops 1 | bytes 1 | tf_op jit(solution)/shard_map/pallas_call | solution.py:230
  74.7 2.0 %shard_map.88 = (bf16[256,256]{1,0:T(8,128)(2,1)S(1)}, bf16[256,256]{1,0:T(8,128)(2,1)S(1)}, bf16[256,256]{1,0:T(8,128)(2,1)S(1)}, bf16[256,256]{1,0:T(8,128)(2,1)S(1)}) custom-call(s32[15]{0:T(128)S(1)} %stack.63.index_ref, f32[3,512,256]{2,1,0:T(8,128)S(1)} %shard_map.83.local_near_ref, f32[3,512,256]{2,1,0:T(8,128)S(1)} %shard_map.86.local_far_ref, ...), custom_call_target="tpu_custom_call" | custom-call | flops 1 | bytes 1 | tf_op jit(solution)/shard_map/pallas_call | solution.py:276
  76.7 0.1 collective-permute-start.14
  76.7 0.6 collective-permute-start.12
  77.3 1.3 collective-permute-start.13
  78.7 1.3 collective-permute-start.16
  80.0 4.6 %collective-permute-start.15 = (bf16[256,512]{1,0:T(8,128)(2,1)S(1)}, bf16[256,512]{1,0:T(8,128)(2,1)S(1)}, u32[]{:S(2)}, u32[]{:S(2)}) collective-permute-start(bf16[256,512]{1,0:T(8,128)(2,1)S(1)} %constant_dynamic-update-slice_fusion.2), channel_id=1, source_target_pairs={{0,1},{1,2},{2,3},{4,5},{5,6},{6,7},{8,9},{9,10},{10,11},{12,13},{... | collective-permute-start | bytes 786440 | tf_op jit(solution)/shard_map/ppermute | solution.py:420
  84.5 0.5 collective-permute-done.13
  85.0 0.6 collective-permute-start.23
  85.6 3.5 %collective-permute-done.16 = bf16[256,512]{1,0:T(8,128)(2,1)S(1)} collective-permute-done((bf16[256,512]{1,0:T(8,128)(2,1)S(1)}, bf16[256,512]{1,0:T(8,128)(2,1)S(1)}, u32[]{:S(2)}, u32[]{:S(2)}) %collective-permute-start.16) | collective-permute-done | bytes 262176 | tf_op jit(solution)/shard_map/ppermute | solution.py:420
  89.1 1.2 collective-permute-done.15
  90.3 1.3 collective-permute-start.20
  91.6 5.0 %collective-permute-start.17 = (bf16[256,512]{1,0:T(8,128)(2,1)S(1)}, bf16[256,512]{1,0:T(8,128)(2,1)S(1)}, u32[]{:S(2)}, u32[]{:S(2)}) collective-permute-start(bf16[256,512]{1,0:T(8,128)(2,1)S(1)} %constant_dynamic-update-slice_fusion), channel_id=1, source_target_pairs={{0,1},{1,2},{2,3},{4,5},{5,6},{6,7},{8,9},{9,10},{10,11},{12,13},{... | collective-permute-start | bytes 786440 | tf_op jit(solution)/shard_map/ppermute | solution.py:420
  96.7 3.7 %collective-permute-done.20 = bf16[256,512]{1,0:T(8,128)(2,1)S(1)} collective-permute-done((bf16[256,512]{1,0:T(8,128)(2,1)S(1)}, bf16[256,512]{1,0:T(8,128)(2,1)S(1)}, u32[]{:S(2)}, u32[]{:S(2)}) %collective-permute-start.20) | collective-permute-done | bytes 262176 | tf_op jit(solution)/shard_map/ppermute | solution.py:420
  100.4 1.3 collective-permute-start.21
  101.7 0.7 collective-permute-start.18
  102.4 0.6 collective-permute-start.27
  103.0 1.5 %collective-permute-start.24 = (bf16[256,1024]{1,0:T(8,128)(2,1)S(1)}, bf16[256,1024]{1,0:T(8,128)(2,1)S(1)}, u32[]{:S(2)}, u32[]{:S(2)}) collective-permute-start(bf16[256,1024]{1,0:T(8,128)(2,1)S(1)} %collective-permute-done.23.one), channel_id=1, source_target_pairs={{0,16},{16,0},{1,17},{17,1},{2,18},{18,2},{3,19},{19,3},{4,20},{20... | collective-permute-start | bytes 1572872 | tf_op jit(solution)/shard_map/ppermute | solution.py:474
  104.5 10.1 %collective-permute-done.21.above_2 = bf16[256,1024]{1,0:T(8,128)(2,1)S(1)} collective-permute-done((bf16[256,1024]{1,0:T(8,128)(2,1)S(1)}, bf16[256,1024]{1,0:T(8,128)(2,1)S(1)}, u32[]{:S(2)}, u32[]{:S(2)}) %collective-permute-start.21) | collective-permute-done | bytes 524320 | tf_op jit(solution)/shard_map/ppermute | solution.py:420
  114.7 0.2 collective-permute-done.27.one
  114.9 0.3 collective-permute-done.24.other
  115.2 0.0 collective-permute-start.26
  115.2 1.5 %collective-permute-start.28 = (bf16[256,1024]{1,0:T(8,128)(2,1)S(1)}, bf16[256,1024]{1,0:T(8,128)(2,1)S(1)}, u32[]{:S(2)}, u32[]{:S(2)}) collective-permute-start(bf16[256,1024]{1,0:T(8,128)(2,1)S(1)} %collective-permute-done.27.one), channel_id=1, source_target_pairs={{0,16},{16,0},{1,17},{17,1},{2,18},{18,2},{3,19},{19,3},{4,20},{20... | collective-permute-start | bytes 1572872 | tf_op jit(solution)/shard_map/ppermute | solution.py:474
  116.7 0.1 pad_maximum_fusion.own
  116.8 1.3 collective-permute-start.22
  118.1 0.7 collective-permute-start.19
  118.8 4.7 %shard_map.89 = (f32[256,1024]{1,0:T(8,128)S(1)}, bf16[256,1024]{1,0:T(8,128)(2,1)S(1)}, bf16[1024,1024]{1,0:T(8,128)(2,1)S(1)}) custom-call(s32[15]{0:T(128)S(1)} %stack.63.index_ref, bf16[256,1024]{1,0:T(8,128)(2,1)S(1)} %pad_maximum_fusion.own, bf16[256,1024]{1,0:T(8,128)(2,1)S(1)} %constant_dynamic-update-slice_fusion.4.below_1, ...), custom_call_target="tpu_custom_call" | custom-call | flops 1 | bytes 1 | tf_op jit(solution)/shard_map/pallas_call | solution.py:343
  123.6 5.9 %collective-permute-done.28.other = bf16[256,1024]{1,0:T(8,128)(2,1)S(1)} collective-permute-done((bf16[256,1024]{1,0:T(8,128)(2,1)S(1)}, bf16[256,1024]{1,0:T(8,128)(2,1)S(1)}, u32[]{:S(2)}, u32[]{:S(2)}) %collective-permute-start.28) | collective-permute-done | bytes 524320 | tf_op jit(solution)/shard_map/ppermute | solution.py:474
  129.5 0.5 collective-permute-start.30
  130.0 5.2 %collective-permute-done.22.above = bf16[256,1024]{1,0:T(8,128)(2,1)S(1)} collective-permute-done((bf16[256,1024]{1,0:T(8,128)(2,1)S(1)}, bf16[256,1024]{1,0:T(8,128)(2,1)S(1)}, u32[]{:S(2)}, u32[]{:S(2)}) %collective-permute-start.22) | collective-permute-done | bytes 524320 | tf_op jit(solution)/shard_map/ppermute | solution.py:420
  135.2 3.1 %shard_map.90 = bf16[256,1024]{1,0:T(8,128)(2,1)} custom-call(s32[15]{0:T(128)S(1)} %stack.63.index_ref, bf16[256,1024]{1,0:T(8,128)(2,1)S(1)} %collective-permute-done.19.below, bf16[256,1024]{1,0:T(8,128)(2,1)S(1)} %collective-permute-done.22.above, bf16[1024,1024]{1,0:T(8,128)(2,1)S(1)} %get-tuple-element.61.weight, ...), custom_call_target="tpu_custom_call" | custom-call | flops 1 | bytes 1 | tf_op jit(solution)/shard_map/pallas_call | solution.py:387
  (38 shorter events, 0.2 us)
Async XLA Ops:
  0.0 26.2 %copy-start = (bf16[4096,4]{0,1:T(4,128)(2,1)S(1)}, bf16[4096,4]{0,1:T(4,128)(2,1)}, u32[]{:S(2)}) copy-start(bf16[4096,4]{0,1:T(4,128)(2,1)} %param.10) | copy-start | bytes 98308
  5.6 9.0 %collective-permute-start.1 = (bf16[3,1024,512]{2,1,0:T(8,128)(2,1)}, bf16[3,1024,512]{2,1,0:T(8,128)(2,1)S(1)}, u32[]{:S(2)}, u32[]{:S(2)}) collective-permute-start(bf16[3,1024,512]{2,1,0:T(8,128)(2,1)} %dynamic-slice_bitcast_fusion), channel_id=1, source_target_pairs={{0,4},{4,0},{8,12},{12,8},{1,5},{5,1},{9,13},{13,9},{2,6},{6,2},{1... | collective-permute-start | bytes 9437192 | tf_op jit(solution)/shard_map/ppermute | solution.py:417
  6.1 8.5 %collective-permute-start = (bf16[256,4096]{1,0:T(8,128)(2,1)}, bf16[256,4096]{1,0:T(8,128)(2,1)}, u32[]{:S(2)}, u32[]{:S(2)}) collective-permute-start(bf16[256,4096]{1,0:T(8,128)(2,1)} %refs_0_.5), channel_id=1, source_target_pairs={{0,4},{4,0},{8,12},{12,8},{1,5},{5,1},{9,13},{13,9},{2,6},{6,2},{1... | collective-permute-start | bytes 6291464 | tf_op jit(solution)/shard_map/ppermute | solution.py:417
  6.1 15.7 %collective-permute-start.2 = (bf16[256,1024]{1,0:T(8,128)(2,1)}, bf16[256,1024]{1,0:T(8,128)(2,1)}, u32[]{:S(2)}, u32[]{:S(2)}) collective-permute-start(bf16[256,1024]{1,0:T(8,128)(2,1)} %constant_dynamic-slice_fusion.2), channel_id=1, source_target_pairs={{0,8},{4,12},{8,0},{12,4},{1,9},{5,13},{9,1},{13,5},{2,10},{6,14},... | collective-permute-start | bytes 1572872 | tf_op jit(solution)/shard_map/ppermute | solution.py:417
  14.6 2.8 %copy-start.1 = (bf16[1024,3,1024]{2,0,1:T(8,128)(2,1)S(1)}, bf16[1024,3,1024]{2,0,1:T(8,128)(2,1)}, u32[]{:S(2)}) copy-start(bf16[1024,3,1024]{2,0,1:T(8,128)(2,1)} %param.9) | copy-start | bytes 18874372
  21.8 17.1 %collective-permute-start.3 = (bf16[256,1024]{1,0:T(8,128)(2,1)}, bf16[256,1024]{1,0:T(8,128)(2,1)}, u32[]{:S(2)}, u32[]{:S(2)}) collective-permute-start(bf16[256,1024]{1,0:T(8,128)(2,1)} %collective-permute-done.2.refs_0_.refs_2_), channel_id=1, source_target_pairs={{0,1},{1,0},{2,3},{3,2},{4,5},{5,4},{6,7},{7,6},{8,9},{9,8},{10,11... | collective-permute-start | bytes 1572872 | tf_op jit(solution)/shard_map/ppermute | solution.py:420
  24.7 14.2 %collective-permute-start.4 = (bf16[2,512,256]{2,1,0:T(8,128)(2,1)}, bf16[2,512,256]{2,1,0:T(8,128)(2,1)}, u32[]{:S(2)}, u32[]{:S(2)}) collective-permute-start(bf16[2,512,256]{2,1,0:T(8,128)(2,1)} %shard_map.82), channel_id=1, source_target_pairs={{0,8},{4,12},{8,0},{12,4},{1,9},{5,13},{9,1},{13,5},{2,10},{6,14},... | collective-permute-start | bytes 1572872 | tf_op jit(solution)/shard_map/ppermute | solution.py:417
  28.5 1.2 collective-permute-start.5
  28.6 10.4 %collective-permute-start.7 = (bf16[256,1024]{1,0:T(8,128)(2,1)}, bf16[256,1024]{1,0:T(8,128)(2,1)S(1)}, u32[]{:S(2)}, u32[]{:S(2)}) collective-permute-start(bf16[256,1024]{1,0:T(8,128)(2,1)} %collective-permute-done.2.refs_0_.refs_2_), channel_id=1, source_target_pairs={{0,4},{4,0},{8,12},{12,8},{1,5},{5,1},{9,13},{13,9},{2,6},{6,2},{1... | collective-permute-start | bytes 1572872 | tf_op jit(solution)/shard_map/ppermute | solution.py:417
  29.7 9.2 %collective-permute-start.6 = (f32[8,256]{1,0:T(8,128)S(1)}, f32[8,256]{1,0:T(8,128)S(1)}, u32[]{:S(2)}, u32[]{:S(2)}) collective-permute-start(f32[8,256]{1,0:T(8,128)S(1)} %pad_maximum_fusion.1.rate_near_ref), channel_id=1, source_target_pairs={{0,8},{4,12},{8,0},{12,4},{1,9},{5,13},{9,1},{13,5},{2,10},{6,14},... | collective-permute-start | bytes 24584 | tf_op jit(solution)/shard_map/ppermute | solution.py:417
  31.5 2.8 %copy-start.2 = (bf16[1024,3,1024]{2,0,1:T(8,128)(2,1)S(1)}, bf16[1024,3,1024]{2,0,1:T(8,128)(2,1)}, u32[]{:S(2)}) copy-start(bf16[1024,3,1024]{2,0,1:T(8,128)(2,1)} %param.9) | copy-start | bytes 18874372
  38.9 5.6 %copy-start.3 = (bf16[1024,1024]{1,0:T(8,128)(2,1)S(1)}, bf16[1024,1024]{1,0:T(8,128)(2,1)}, u32[]{:S(2)}) copy-start(bf16[1024,1024]{1,0:T(8,128)(2,1)} %own_w.1) | copy-start | bytes 6291460
  38.9 2.2 %collective-permute-start.8 = (bf16[256,1024]{1,0:T(8,128)(2,1)}, bf16[256,1024]{1,0:T(8,128)(2,1)S(1)}, u32[]{:S(2)}, u32[]{:S(2)}) collective-permute-start(bf16[256,1024]{1,0:T(8,128)(2,1)} %collective-permute-done.3.refs_1_.refs_3_), channel_id=1, source_target_pairs={{0,4},{4,0},{8,12},{12,8},{1,5},{5,1},{9,13},{13,9},{2,6},{6,2},{1... | collective-permute-start | bytes 1572872 | tf_op jit(solution)/shard_map/ppermute | solution.py:417
  44.5 5.7 %collective-permute-start.9 = (bf16[1024,1024]{1,0:T(8,128)(2,1)S(1)}, bf16[1024,1024]{1,0:T(8,128)(2,1)S(1)}, u32[]{:S(2)}, u32[]{:S(2)}) collective-permute-start(bf16[1024,1024]{1,0:T(8,128)(2,1)S(1)} %copy-done.3), channel_id=1, source_target_pairs={{0,4},{4,0},{8,12},{12,8},{1,5},{5,1},{9,13},{13,9},{2,6},{6,2},{1... | collective-permute-start | bytes 6291464 | tf_op jit(solution)/shard_map/ppermute | solution.py:417
  44.7 14.2 %collective-permute-start.10 = (bf16[2,512,256]{2,1,0:T(8,128)(2,1)S(1)}, bf16[2,512,256]{2,1,0:T(8,128)(2,1)S(1)}, u32[]{:S(2)}, u32[]{:S(2)}) collective-permute-start(bf16[2,512,256]{2,1,0:T(8,128)(2,1)S(1)} %shard_map.84), channel_id=1, source_target_pairs={{0,8},{4,12},{8,0},{12,4},{1,9},{5,13},{9,1},{13,5},{2,10},{6,14},... | collective-permute-start | bytes 1572872 | tf_op jit(solution)/shard_map/ppermute | solution.py:417
  50.2 10.2 %copy-start.4 = (bf16[4,256,512]{2,1,0:T(8,128)(2,1)S(1)}, bf16[4,256,512]{2,1,0:T(8,128)(2,1)}, u32[]{:S(2)}) copy-start(bf16[4,256,512]{2,1,0:T(8,128)(2,1)} %gate_ref.1) | copy-start | bytes 3145732
  50.2 10.2 %copy-start.5 = (bf16[4,256,512]{2,1,0:T(8,128)(2,1)S(1)}, bf16[4,256,512]{2,1,0:T(8,128)(2,1)}, u32[]{:S(2)}) copy-start(bf16[4,256,512]{2,1,0:T(8,128)(2,1)} %up_ref.1) | copy-start | bytes 3145732
  50.2 10.2 %copy-start.6 = (bf16[4,256,512]{2,1,0:T(8,128)(2,1)S(1)}, bf16[4,256,512]{2,1,0:T(8,128)(2,1)}, u32[]{:S(2)}) copy-start(bf16[4,256,512]{2,1,0:T(8,128)(2,1)} %down_ref.1) | copy-start | bytes 3145732
  54.7 20.0 %copy-start.7 = (f32[1024]{0:T(1024)S(1)}, f32[1024]{0:T(1024)}, u32[]{:S(2)}) copy-start(f32[1024]{0:T(1024)} %param.14) | copy-start | bytes 12292
  58.9 15.7 %collective-permute-start.11 = (bf16[1,1024,256]{2,1,0:T(8,128)(2,1)S(1)}, bf16[1,1024,256]{2,1,0:T(8,128)(2,1)S(1)}, u32[]{:S(2)}, u32[]{:S(2)}) collective-permute-start(bf16[1,1024,256]{2,1,0:T(8,128)(2,1)S(1)} %shard_map.85), channel_id=1, source_target_pairs={{0,8},{4,12},{8,0},{12,4},{1,9},{5,13},{9,1},{13,5},{2,10},{6,14},... | collective-permute-start | bytes 1572872 | tf_op jit(solution)/shard_map/ppermute | solution.py:417
  76.7 2.0 %collective-permute-start.14 = (bf16[256,256]{1,0:T(8,128)(2,1)S(1)}, bf16[256,256]{1,0:T(8,128)(2,1)S(1)}, u32[]{:S(2)}, u32[]{:S(2)}) collective-permute-start(bf16[256,256]{1,0:T(8,128)(2,1)S(1)} %get-tuple-element.53), channel_id=1, source_target_pairs={{0,4},{4,0},{8,12},{12,8},{1,5},{5,1},{9,13},{13,9},{2,6},{6,2},{1... | collective-permute-start | bytes 393224 | tf_op jit(solution)/shard_map/ppermute | solution.py:417
  76.7 7.8 %collective-permute-start.12 = (bf16[256,256]{1,0:T(8,128)(2,1)S(1)}, bf16[256,256]{1,0:T(8,128)(2,1)S(1)}, u32[]{:S(2)}, u32[]{:S(2)}) collective-permute-start(bf16[256,256]{1,0:T(8,128)(2,1)S(1)} %get-tuple-element.50), channel_id=1, source_target_pairs={{0,8},{4,12},{8,0},{12,4},{1,9},{5,13},{9,1},{13,5},{2,10},{6,14},... | collective-permute-start | bytes 393224 | tf_op jit(solution)/shard_map/ppermute | solution.py:417
  77.3 7.7 %collective-permute-start.13 = (bf16[256,256]{1,0:T(8,128)(2,1)S(1)}, bf16[256,256]{1,0:T(8,128)(2,1)S(1)}, u32[]{:S(2)}, u32[]{:S(2)}) collective-permute-start(bf16[256,256]{1,0:T(8,128)(2,1)S(1)} %get-tuple-element.51), channel_id=1, source_target_pairs={{0,12},{4,8},{8,4},{12,0},{1,13},{5,9},{9,5},{13,1},{2,14},{6,10},... | collective-permute-start | bytes 393224 | tf_op jit(solution)/shard_map/ppermute | solution.py:417
  78.7 10.4 %collective-permute-start.16 = (bf16[256,512]{1,0:T(8,128)(2,1)S(1)}, bf16[256,512]{1,0:T(8,128)(2,1)S(1)}, u32[]{:S(2)}, u32[]{:S(2)}) collective-permute-start(bf16[256,512]{1,0:T(8,128)(2,1)S(1)} %constant_dynamic-update-slice_fusion.2), channel_id=1, source_target_pairs={{1,0},{2,1},{3,2},{5,4},{6,5},{7,6},{9,8},{10,9},{11,10},{13,12},{... | collective-permute-start | bytes 786440 | tf_op jit(solution)/shard_map/ppermute | solution.py:420
  80.0 10.3 %collective-permute-start.15 = (bf16[256,512]{1,0:T(8,128)(2,1)S(1)}, bf16[256,512]{1,0:T(8,128)(2,1)S(1)}, u32[]{:S(2)}, u32[]{:S(2)}) collective-permute-start(bf16[256,512]{1,0:T(8,128)(2,1)S(1)} %constant_dynamic-update-slice_fusion.2), channel_id=1, source_target_pairs={{0,1},{1,2},{2,3},{4,5},{5,6},{6,7},{8,9},{9,10},{10,11},{12,13},{... | collective-permute-start | bytes 786440 | tf_op jit(solution)/shard_map/ppermute | solution.py:420
  85.0 17.4 %collective-permute-start.23 = (bf16[256,1024]{1,0:T(8,128)(2,1)S(1)}, bf16[256,1024]{1,0:T(8,128)(2,1)S(1)}, u32[]{:S(2)}, u32[]{:S(2)}) collective-permute-start(bf16[256,1024]{1,0:T(8,128)(2,1)S(1)} %get-tuple-element.57), channel_id=1, source_target_pairs={{0,8},{4,12},{8,0},{12,4},{1,9},{5,13},{9,1},{13,5},{2,10},{6,14},... | collective-permute-start | bytes 1572872 | tf_op jit(solution)/shard_map/ppermute | solution.py:417
  90.3 10.1 %collective-permute-start.20 = (bf16[256,512]{1,0:T(8,128)(2,1)S(1)}, bf16[256,512]{1,0:T(8,128)(2,1)S(1)}, u32[]{:S(2)}, u32[]{:S(2)}) collective-permute-start(bf16[256,512]{1,0:T(8,128)(2,1)S(1)} %constant_dynamic-update-slice_fusion), channel_id=1, source_target_pairs={{1,0},{2,1},{3,2},{5,4},{6,5},{7,6},{9,8},{10,9},{11,10},{13,12},{... | collective-permute-start | bytes 786440 | tf_op jit(solution)/shard_map/ppermute | solution.py:420
  91.6 10.1 %collective-permute-start.17 = (bf16[256,512]{1,0:T(8,128)(2,1)S(1)}, bf16[256,512]{1,0:T(8,128)(2,1)S(1)}, u32[]{:S(2)}, u32[]{:S(2)}) collective-permute-start(bf16[256,512]{1,0:T(8,128)(2,1)S(1)} %constant_dynamic-update-slice_fusion), channel_id=1, source_target_pairs={{0,1},{1,2},{2,3},{4,5},{5,6},{6,7},{8,9},{9,10},{10,11},{12,13},{... | collective-permute-start | bytes 786440 | tf_op jit(solution)/shard_map/ppermute | solution.py:420
  100.4 14.3 %collective-permute-start.21 = (bf16[256,1024]{1,0:T(8,128)(2,1)S(1)}, bf16[256,1024]{1,0:T(8,128)(2,1)S(1)}, u32[]{:S(2)}, u32[]{:S(2)}) collective-permute-start(bf16[256,1024]{1,0:T(8,128)(2,1)S(1)} %constant_dynamic-update-slice_fusion.6.above_1), channel_id=1, source_target_pairs={{1,0},{2,1},{5,4},{6,5},{9,8},{10,9},{13,12},{14,13},{17,16},{18,1... | collective-permute-start | bytes 1572872 | tf_op jit(solution)/shard_map/ppermute | solution.py:420
  101.7 13.0 %collective-permute-start.18 = (bf16[256,1024]{1,0:T(8,128)(2,1)S(1)}, bf16[256,1024]{1,0:T(8,128)(2,1)S(1)}, u32[]{:S(2)}, u32[]{:S(2)}) collective-permute-start(bf16[256,1024]{1,0:T(8,128)(2,1)S(1)} %constant_dynamic-update-slice_fusion.4.below_1), channel_id=1, source_target_pairs={{1,2},{2,3},{5,6},{6,7},{9,10},{10,11},{13,14},{14,15},{17,18},{18... | collective-permute-start | bytes 1572872 | tf_op jit(solution)/shard_map/ppermute | solution.py:420
  102.4 12.5 %collective-permute-start.27 = (bf16[256,1024]{1,0:T(8,128)(2,1)S(1)}, bf16[256,1024]{1,0:T(8,128)(2,1)S(1)}, u32[]{:S(2)}, u32[]{:S(2)}) collective-permute-start(bf16[256,1024]{1,0:T(8,128)(2,1)S(1)} %get-tuple-element.63), channel_id=1, source_target_pairs={{0,8},{4,12},{8,0},{12,4},{1,9},{5,13},{9,1},{13,5},{2,10},{6,14},... | collective-permute-start | bytes 1572872 | tf_op jit(solution)/shard_map/ppermute | solution.py:417
  103.0 12.1 %collective-permute-start.24 = (bf16[256,1024]{1,0:T(8,128)(2,1)S(1)}, bf16[256,1024]{1,0:T(8,128)(2,1)S(1)}, u32[]{:S(2)}, u32[]{:S(2)}) collective-permute-start(bf16[256,1024]{1,0:T(8,128)(2,1)S(1)} %collective-permute-done.23.one), channel_id=1, source_target_pairs={{0,16},{16,0},{1,17},{17,1},{2,18},{18,2},{3,19},{19,3},{4,20},{20... | collective-permute-start | bytes 1572872 | tf_op jit(solution)/shard_map/ppermute | solution.py:474
  114.7 4.1 %collective-permute-start.25 = (bf16[256,1024]{1,0:T(8,128)(2,1)S(1)}, bf16[256,1024]{1,0:T(8,128)(2,1)S(1)}, u32[]{:S(2)}, u32[]{:S(2)}) collective-permute-start(bf16[256,1024]{1,0:T(8,128)(2,1)S(1)} %collective-permute-done.23.one), channel_id=1, source_target_pairs={{0,4},{4,0},{8,12},{12,8},{1,5},{5,1},{9,13},{13,9},{2,6},{6,2},{1... | collective-permute-start | bytes 1572872 | tf_op jit(solution)/shard_map/ppermute | solution.py:417
  115.2 3.7 %collective-permute-start.26 = (bf16[256,1024]{1,0:T(8,128)(2,1)S(1)}, bf16[256,1024]{1,0:T(8,128)(2,1)S(1)}, u32[]{:S(2)}, u32[]{:S(2)}) collective-permute-start(bf16[256,1024]{1,0:T(8,128)(2,1)S(1)} %collective-permute-done.24.other), channel_id=1, source_target_pairs={{0,4},{4,0},{8,12},{12,8},{1,5},{5,1},{9,13},{13,9},{2,6},{6,2},{1... | collective-permute-start | bytes 1572872 | tf_op jit(solution)/shard_map/ppermute | solution.py:417
  115.2 14.3 %collective-permute-start.28 = (bf16[256,1024]{1,0:T(8,128)(2,1)S(1)}, bf16[256,1024]{1,0:T(8,128)(2,1)S(1)}, u32[]{:S(2)}, u32[]{:S(2)}) collective-permute-start(bf16[256,1024]{1,0:T(8,128)(2,1)S(1)} %collective-permute-done.27.one), channel_id=1, source_target_pairs={{0,16},{16,0},{1,17},{17,1},{2,18},{18,2},{3,19},{19,3},{4,20},{20... | collective-permute-start | bytes 1572872 | tf_op jit(solution)/shard_map/ppermute | solution.py:474
  116.8 18.4 %collective-permute-start.22 = (bf16[256,1024]{1,0:T(8,128)(2,1)S(1)}, bf16[256,1024]{1,0:T(8,128)(2,1)S(1)}, u32[]{:S(2)}, u32[]{:S(2)}) collective-permute-start(bf16[256,1024]{1,0:T(8,128)(2,1)S(1)} %collective-permute-done.21.above_2), channel_id=1, source_target_pairs={{1,0},{5,4},{9,8},{13,12},{17,16},{21,20},{25,24},{29,28}} | collective-permute-start | bytes 1572872 | tf_op jit(solution)/shard_map/ppermute | solution.py:420
  118.1 17.1 %collective-permute-start.19 = (bf16[256,1024]{1,0:T(8,128)(2,1)S(1)}, bf16[256,1024]{1,0:T(8,128)(2,1)S(1)}, u32[]{:S(2)}, u32[]{:S(2)}) collective-permute-start(bf16[256,1024]{1,0:T(8,128)(2,1)S(1)} %collective-permute-done.18.below_2), channel_id=1, source_target_pairs={{2,3},{6,7},{10,11},{14,15},{18,19},{22,23},{26,27},{30,31}} | collective-permute-start | bytes 1572872 | tf_op jit(solution)/shard_map/ppermute | solution.py:420
  129.5 5.7 %collective-permute-start.29 = (bf16[256,1024]{1,0:T(8,128)(2,1)S(1)}, bf16[256,1024]{1,0:T(8,128)(2,1)S(1)}, u32[]{:S(2)}, u32[]{:S(2)}) collective-permute-start(bf16[256,1024]{1,0:T(8,128)(2,1)S(1)} %collective-permute-done.27.one), channel_id=1, source_target_pairs={{0,4},{4,0},{8,12},{12,8},{1,5},{5,1},{9,13},{13,9},{2,6},{6,2},{1... | collective-permute-start | bytes 1572872 | tf_op jit(solution)/shard_map/ppermute | solution.py:417
  129.5 5.7 %collective-permute-start.30 = (bf16[256,1024]{1,0:T(8,128)(2,1)S(1)}, bf16[256,1024]{1,0:T(8,128)(2,1)S(1)}, u32[]{:S(2)}, u32[]{:S(2)}) collective-permute-start(bf16[256,1024]{1,0:T(8,128)(2,1)S(1)} %collective-permute-done.28.other), channel_id=1, source_target_pairs={{0,4},{4,0},{8,12},{12,8},{1,5},{5,1},{9,13},{13,9},{2,6},{6,2},{1... | collective-permute-start | bytes 1572872 | tf_op jit(solution)/shard_map/ppermute | solution.py:417

commit v9 on v8

--- a/solution.py
+++ b/solution.py
@@ -473,9 +473,8 @@
     def swap_groups(array):
         return lax.ppermute(array, "groups", [(0, 1), (1, 0)])
 
-    first_x = across(after(out_first, theirs), 2)
     below_mine, above_mine = both(0, mine, mine)
-    theirs, below_mine, above_mine = lax.optimization_barrier((theirs, below_mine, above_mine))
+    first_x = across(after(out_first, theirs, below_mine, above_mine), 2)
     below_theirs, above_theirs = both(0, theirs, theirs)
     below_1 = jnp.concatenate([below_mine, below_theirs], axis=1)
     above_1 = jnp.concatenate([above_mine, above_theirs], axis=1)

time: 139 us -> 138 us (level)
    ppermute x20, waiting for transfers between devices: 13.2 us -> 19.9 us  [across(): return lax.ppermute(array, 'seq', [(i, i ^ bit) for i in range(4)])]
    ppermute x9, waiting for transfers between devices: 23.6 us -> 16.9 us  [hop(): return lax.ppermute(array, 'head', links)]
  transfers between devices with their start and end apart: 31 -> 31, of which waited for: 13 -> 15; matrix products, arithmetic and copies ran while one was open for 3% -> 3% of each run, Pallas kernels for 26% -> 26%
where the time goes in v9:
time: 138 us
  Pallas kernels  44.8 us (32%)
  waiting for transfers between devices  43.1 us (31%)
  starting transfers between devices  34.3 us (25%)
  local copies, waits for them, and re-layouts  12.7 us (9%)
  matrix products  2.25 us (2%)
    pallas_call x5, Pallas kernels, project(): pl.pallas_call(functools.partial(project_kernel, len(whole), len(pairs)),...  20.7 us
    ppermute x20, waiting for transfers between devices, across(): return lax.ppermute(array, 'seq', [(i, i ^ bit) for i in range(4)])  19.9 us
    ppermute x9, starting transfers between devices, hop(): return lax.ppermute(array, 'head', links)  18.4 us
    ppermute x9, waiting for transfers between devices, hop(): return lax.ppermute(array, 'head', links)  16.9 us
    pallas_call x1, Pallas kernels, update(): pl.pallas_call(update_kernel, out_shape=[out] * 3, grid_spec=pltpu.Prefet...  14.2 us
    ppermute x20, starting transfers between devices, across(): return lax.ppermute(array, 'seq', [(i, i ^ bit) for i in range(4)])  12.8 us
    ppermute x2, waiting for transfers between devices, swap_groups(): return lax.ppermute(array, 'groups', [(0, 1), (1, 0)])  6.25 us
    unnamed x20, local copies, waits for them, and re-layouts  5.67 us
  transfers between devices with their start and end apart: 31, of which 15 were waited for; matrix products, arithmetic and copies ran while one was open for 3% of the time, Pallas kernels for 26%

profile of v9, /device:TPU:0, one launch (start us, length us, event | category | flops | bytes accessed | tf_op | source)
XLA Modules:
  0.0 137.5 jit_solution(16177713403315423093)
XLA Ops:
  0.0 1.9 %constant_dynamic-slice_fusion.2 = bf16[256,1024]{1,0:T(8,128)(2,1)} fusion(bf16[256,4096]{1,0:T(8,128)(2,1)} %refs_0_.5, s32[]{:T(128)S(6)} %select_n.23), kind=kLoop, calls=%fused_computation.15 | loop fusion | bytes 1048580 | tf_op jit(solution)/shard_map/dynamic_slice | solution.py:429
  1.9 3.7 %dynamic-slice_bitcast_fusion = bf16[3,1024,512]{2,1,0:T(8,128)(2,1)} fusion(bf16[1024,3,1024]{2,0,1:T(8,128)(2,1)} %param.9, s32[]{:T(128)S(6)} %select_n.24), kind=kLoop, calls=%fused_computation | loop fusion | bytes 6291460 | tf_op jit(solution)/shard_map/dynamic_slice | solution.py:433
  5.6 0.5 collective-permute-start.1
  6.1 0.1 collective-permute-start
  6.1 2.9 %collective-permute-start.2 = (bf16[256,1024]{1,0:T(8,128)(2,1)}, bf16[256,1024]{1,0:T(8,128)(2,1)}, u32[]{:S(2)}, u32[]{:S(2)}) collective-permute-start(bf16[256,1024]{1,0:T(8,128)(2,1)} %constant_dynamic-slice_fusion.2), channel_id=1, source_target_pairs={{0,8},{4,12},{8,0},{12,4},{1,9},{5,13},{9,1},{13,5},{2,10},{6,14},... | collective-permute-start | bytes 1572872 | tf_op jit(solution)/shard_map/ppermute | solution.py:417
  9.1 0.1 stack.63.index_ref
  9.2 5.5 %collective-permute-done.refs_1_ = bf16[256,4096]{1,0:T(8,128)(2,1)} collective-permute-done((bf16[256,4096]{1,0:T(8,128)(2,1)}, bf16[256,4096]{1,0:T(8,128)(2,1)}, u32[]{:S(2)}, u32[]{:S(2)}) %collective-permute-start) | collective-permute-done | bytes 2097184 | tf_op jit(solution)/shard_map/ppermute | solution.py:417
  14.6 2.8 %copy-done.1 = bf16[1024,3,1024]{2,0,1:T(8,128)(2,1)S(1)} copy-done((bf16[1024,3,1024]{2,0,1:T(8,128)(2,1)S(1)}, bf16[1024,3,1024]{2,0,1:T(8,128)(2,1)}, u32[]{:S(2)}) %copy-start.1) | copy-done | bytes 6291480
  17.4 4.4 %shard_map.82 = bf16[2,512,256]{2,1,0:T(8,128)(2,1)} custom-call(s32[15]{0:T(128)S(1)} %stack.63.index_ref, bf16[256,4096]{1,0:T(8,128)(2,1)} %refs_0_.5, bf16[256,4096]{1,0:T(8,128)(2,1)} %collective-permute-done.refs_1_, bf16[3,1024,1024]{2,1,0:T(8,128)(2,1)S(1)} %bitcast.25, bf16[3,1024,512]{2,1,0:T(8,128)(2,1)S(1)} %collective-permute-done.1.refs_3_.refs_5_.refs_7_), custom_call_target="tpu_custom_call" | custom-call | flops 1 | bytes 1 | tf_op jit(solution)/shard_map/pallas_call | solution.py:146
  21.8 2.9 %collective-permute-start.3 = (bf16[256,1024]{1,0:T(8,128)(2,1)}, bf16[256,1024]{1,0:T(8,128)(2,1)}, u32[]{:S(2)}, u32[]{:S(2)}) collective-permute-start(bf16[256,1024]{1,0:T(8,128)(2,1)} %collective-permute-done.2.refs_0_.refs_2_), channel_id=1, source_target_pairs={{0,1},{1,0},{2,3},{3,2},{4,5},{5,4},{6,7},{7,6},{8,9},{9,8},{10,11... | collective-permute-start | bytes 1572872 | tf_op jit(solution)/shard_map/ppermute | solution.py:420
  24.7 1.5 %collective-permute-start.4 = (bf16[2,512,256]{2,1,0:T(8,128)(2,1)}, bf16[2,512,256]{2,1,0:T(8,128)(2,1)}, u32[]{:S(2)}, u32[]{:S(2)}) collective-permute-start(bf16[2,512,256]{2,1,0:T(8,128)(2,1)} %shard_map.82), channel_id=1, source_target_pairs={{0,8},{4,12},{8,0},{12,4},{1,9},{5,13},{9,1},{13,5},{2,10},{6,14},... | collective-permute-start | bytes 1572872 | tf_op jit(solution)/shard_map/ppermute | solution.py:417
  26.2 2.3 %compare_select_fusion = f32[4,256]{1,0:T(4,128)S(1)} fusion(bf16[256,4096]{1,0:T(8,128)(2,1)} %refs_0_.5, bf16[4096,4]{0,1:T(4,128)(2,1)S(1)} %copy-done), kind=kOutput, calls=%fused_computation.11 | convolution fusion | flops 8394752 | bytes 2134016 | tf_op jit(solution)/shard_map/dot_general | solution.py:445
  28.5 0.1 collective-permute-start.5
  28.6 0.5 collective-permute-start.7
  29.1 0.7 collective-permute-done.5
  29.7 0.5 collective-permute-start.6
  30.3 1.3 constant_dynamic-slice_fusion.1
  31.5 0.0 copy-start.2
  31.5 2.8 %copy-done.2 = bf16[1024,3,1024]{2,0,1:T(8,128)(2,1)S(1)} copy-done((bf16[1024,3,1024]{2,0,1:T(8,128)(2,1)S(1)}, bf16[1024,3,1024]{2,0,1:T(8,128)(2,1)}, u32[]{:S(2)}) %copy-start.2) | copy-done | bytes 6291480
  34.3 4.6 %shard_map.83.local_near_ref = f32[3,512,256]{2,1,0:T(8,128)S(1)} custom-call(s32[15]{0:T(128)S(1)} %stack.63.index_ref, bf16[256,4096]{1,0:T(8,128)(2,1)} %refs_0_.5, bf16[256,4096]{1,0:T(8,128)(2,1)} %collective-permute-done.refs_1_, bf16[3,1024,1024]{2,1,0:T(8,128)(2,1)S(1)} %bitcast.26, ...), custom_call_target="tpu_custom_call" | custom-call | flops 1 | bytes 1 | tf_op jit(solution)/shard_map/pallas_call | solution.py:146
  38.9 0.1 collective-permute-start.8
  39.0 2.1 %collective-permute-done.8.refs_3_.refs_5_ = bf16[256,1024]{1,0:T(8,128)(2,1)S(1)} collective-permute-done((bf16[256,1024]{1,0:T(8,128)(2,1)}, bf16[256,1024]{1,0:T(8,128)(2,1)S(1)}, u32[]{:S(2)}, u32[]{:S(2)}) %collective-permute-start.8) | collective-permute-done | bytes 524320 | tf_op jit(solution)/shard_map/ppermute | solution.py:417
  41.1 3.4 %shard_map.84 = bf16[2,512,256]{2,1,0:T(8,128)(2,1)S(1)} custom-call(s32[15]{0:T(128)S(1)} %stack.63.index_ref, bf16[256,1024]{1,0:T(8,128)(2,1)} %collective-permute-done.2.refs_0_.refs_2_, bf16[256,1024]{1,0:T(8,128)(2,1)} %collective-permute-done.3.refs_1_.refs_3_, bf16[256,1024]{1,0:T(8,128)(2,1)S(1)} %collective-permute-done.7.refs_2_.refs_4_, ...), custom_call_target="tpu_custom_call" | custom-call | flops 1 | bytes 1 | tf_op jit(solution)/shard_map/pallas_call | solution.py:146
  44.5 0.2 collective-permute-start.9
  44.7 1.5 %collective-permute-start.10 = (bf16[2,512,256]{2,1,0:T(8,128)(2,1)S(1)}, bf16[2,512,256]{2,1,0:T(8,128)(2,1)S(1)}, u32[]{:S(2)}, u32[]{:S(2)}) collective-permute-start(bf16[2,512,256]{2,1,0:T(8,128)(2,1)S(1)} %shard_map.84), channel_id=1, source_target_pairs={{0,8},{4,12},{8,0},{12,4},{1,9},{5,13},{9,1},{13,5},{2,10},{6,14},... | collective-permute-start | bytes 1572872 | tf_op jit(solution)/shard_map/ppermute | solution.py:417
  46.2 3.9 %shard_map.85 = bf16[1,1024,256]{2,1,0:T(8,128)(2,1)S(1)} custom-call(s32[15]{0:T(128)S(1)} %stack.63.index_ref, bf16[256,4096]{1,0:T(8,128)(2,1)} %refs_0_.5, bf16[256,4096]{1,0:T(8,128)(2,1)} %collective-permute-done.refs_1_, bf16[256,1024]{1,0:T(8,128)(2,1)} %collective-permute-done.2.refs_0_.refs_2_, ...), custom_call_target="tpu_custom_call" | custom-call | flops 1 | bytes 1 | tf_op jit(solution)/shard_map/pallas_call | solution.py:146
  50.2 0.0 copy-start.4
  50.2 0.0 copy-start.5
  50.2 4.4 %shard_map.86.local_far_ref = f32[3,512,256]{2,1,0:T(8,128)S(1)} custom-call(s32[15]{0:T(128)S(1)} %stack.63.index_ref, bf16[256,1024]{1,0:T(8,128)(2,1)} %collective-permute-done.2.refs_0_.refs_2_, bf16[256,1024]{1,0:T(8,128)(2,1)} %collective-permute-done.3.refs_1_.refs_3_, bf16[256,1024]{1,0:T(8,128)(2,1)S(1)} %collective-permute-done.7.refs_2_.refs_4_, ...), custom_call_target="tpu_custom_call" | custom-call | flops 1 | bytes 1 | tf_op jit(solution)/shard_map/pallas_call | solution.py:146
  54.7 0.0 copy-start.7
  54.7 4.2 %collective-permute-done.10.near_ref = bf16[2,512,256]{2,1,0:T(8,128)(2,1)S(1)} collective-permute-done((bf16[2,512,256]{2,1,0:T(8,128)(2,1)S(1)}, bf16[2,512,256]{2,1,0:T(8,128)(2,1)S(1)}, u32[]{:S(2)}, u32[]{:S(2)}) %collective-permute-start.10) | collective-permute-done | bytes 524320 | tf_op jit(solution)/shard_map/ppermute | solution.py:417
  58.9 1.5 %collective-permute-start.11 = (bf16[1,1024,256]{2,1,0:T(8,128)(2,1)S(1)}, bf16[1,1024,256]{2,1,0:T(8,128)(2,1)S(1)}, u32[]{:S(2)}, u32[]{:S(2)}) collective-permute-start(bf16[1,1024,256]{2,1,0:T(8,128)(2,1)S(1)} %shard_map.85), channel_id=1, source_target_pairs={{0,8},{4,12},{8,0},{12,4},{1,9},{5,13},{9,1},{13,5},{2,10},{6,14},... | collective-permute-start | bytes 1572872 | tf_op jit(solution)/shard_map/ppermute | solution.py:417
  60.4 14.2 %shard_map.87 = (bf16[256,512]{1,0:T(8,128)(2,1)S(1)}, bf16[256,512]{1,0:T(8,128)(2,1)S(1)}, bf16[256,512]{1,0:T(8,128)(2,1)S(1)}) custom-call(s32[15]{0:T(128)S(1)} %stack.63.index_ref, f32[3,512,256]{2,1,0:T(8,128)S(1)} %shard_map.83.local_near_ref, f32[3,512,256]{2,1,0:T(8,128)S(1)} %shard_map.86.local_far_ref, ...), custom_call_target="tpu_custom_call" | custom-call | flops 1 | bytes 1 | tf_op jit(solution)/shard_map/pallas_call | solution.py:230
  74.7 2.0 %shard_map.88 = (bf16[256,256]{1,0:T(8,128)(2,1)S(1)}, bf16[256,256]{1,0:T(8,128)(2,1)S(1)}, bf16[256,256]{1,0:T(8,128)(2,1)S(1)}, bf16[256,256]{1,0:T(8,128)(2,1)S(1)}) custom-call(s32[15]{0:T(128)S(1)} %stack.63.index_ref, f32[3,512,256]{2,1,0:T(8,128)S(1)} %shard_map.83.local_near_ref, f32[3,512,256]{2,1,0:T(8,128)S(1)} %shard_map.86.local_far_ref, ...), custom_call_target="tpu_custom_call" | custom-call | flops 1 | bytes 1 | tf_op jit(solution)/shard_map/pallas_call | solution.py:276
  76.7 0.1 collective-permute-start.12
  76.7 0.6 collective-permute-start.14
  77.3 1.3 collective-permute-start.15
  78.7 1.3 collective-permute-start.19
  80.0 4.6 %collective-permute-start.13 = (bf16[256,512]{1,0:T(8,128)(2,1)S(1)}, bf16[256,512]{1,0:T(8,128)(2,1)S(1)}, u32[]{:S(2)}, u32[]{:S(2)}) collective-permute-start(bf16[256,512]{1,0:T(8,128)(2,1)S(1)} %constant_dynamic-update-slice_fusion), channel_id=1, source_target_pairs={{0,1},{1,2},{2,3},{4,5},{5,6},{6,7},{8,9},{9,10},{10,11},{12,13},{... | collective-permute-start | bytes 786440 | tf_op jit(solution)/shard_map/ppermute | solution.py:420
  84.5 0.5 collective-permute-done.15
  85.0 1.3 collective-permute-start.20
  86.3 2.8 %collective-permute-done.19 = bf16[256,512]{1,0:T(8,128)(2,1)S(1)} collective-permute-done((bf16[256,512]{1,0:T(8,128)(2,1)S(1)}, bf16[256,512]{1,0:T(8,128)(2,1)S(1)}, u32[]{:S(2)}, u32[]{:S(2)}) %collective-permute-start.19) | collective-permute-done | bytes 262176 | tf_op jit(solution)/shard_map/ppermute | solution.py:420
  89.1 1.2 collective-permute-done.13
  90.3 0.5 collective-permute-start.23
  90.8 4.4 %collective-permute-start.16 = (bf16[256,512]{1,0:T(8,128)(2,1)S(1)}, bf16[256,512]{1,0:T(8,128)(2,1)S(1)}, u32[]{:S(2)}, u32[]{:S(2)}) collective-permute-start(bf16[256,512]{1,0:T(8,128)(2,1)S(1)} %constant_dynamic-update-slice_fusion.2), channel_id=1, source_target_pairs={{0,1},{1,2},{2,3},{4,5},{5,6},{6,7},{8,9},{9,10},{10,11},{12,13},{... | collective-permute-start | bytes 786440 | tf_op jit(solution)/shard_map/ppermute | solution.py:420
  95.2 0.5 collective-permute-done.20
  95.7 1.3 collective-permute-start.21
  97.1 2.8 %collective-permute-done.16 = bf16[256,512]{1,0:T(8,128)(2,1)S(1)} collective-permute-done((bf16[256,512]{1,0:T(8,128)(2,1)S(1)}, bf16[256,512]{1,0:T(8,128)(2,1)S(1)}, u32[]{:S(2)}, u32[]{:S(2)}) %collective-permute-start.16) | collective-permute-done | bytes 262176 | tf_op jit(solution)/shard_map/ppermute | solution.py:420
  99.9 0.7 collective-permute-start.17
  100.6 2.8 %collective-permute-done.23.one = bf16[256,1024]{1,0:T(8,128)(2,1)S(1)} collective-permute-done((bf16[256,1024]{1,0:T(8,128)(2,1)S(1)}, bf16[256,1024]{1,0:T(8,128)(2,1)S(1)}, u32[]{:S(2)}, u32[]{:S(2)}) %collective-permute-start.23) | collective-permute-done | bytes 524320 | tf_op jit(solution)/shard_map/ppermute | solution.py:417
  103.3 0.5 collective-permute-start.27
  103.9 1.5 %collective-permute-start.24 = (bf16[256,1024]{1,0:T(8,128)(2,1)S(1)}, bf16[256,1024]{1,0:T(8,128)(2,1)S(1)}, u32[]{:S(2)}, u32[]{:S(2)}) collective-permute-start(bf16[256,1024]{1,0:T(8,128)(2,1)S(1)} %collective-permute-done.23.one), channel_id=1, source_target_pairs={{0,16},{16,0},{1,17},{17,1},{2,18},{18,2},{3,19},{19,3},{4,20},{20... | collective-permute-start | bytes 1572872 | tf_op jit(solution)/shard_map/ppermute | solution.py:474
  105.4 5.9 %collective-permute-done.21.above_2 = bf16[256,1024]{1,0:T(8,128)(2,1)S(1)} collective-permute-done((bf16[256,1024]{1,0:T(8,128)(2,1)S(1)}, bf16[256,1024]{1,0:T(8,128)(2,1)S(1)}, u32[]{:S(2)}, u32[]{:S(2)}) %collective-permute-start.21) | collective-permute-done | bytes 524320 | tf_op jit(solution)/shard_map/ppermute | solution.py:420
  111.3 4.2 %collective-permute-done.27.one = bf16[256,1024]{1,0:T(8,128)(2,1)S(1)} collective-permute-done((bf16[256,1024]{1,0:T(8,128)(2,1)S(1)}, bf16[256,1024]{1,0:T(8,128)(2,1)S(1)}, u32[]{:S(2)}, u32[]{:S(2)}) %collective-permute-start.27) | collective-permute-done | bytes 524320 | tf_op jit(solution)/shard_map/ppermute | solution.py:417
  115.5 0.3 collective-permute-done.24.other
  115.7 1.5 %collective-permute-start.28 = (bf16[256,1024]{1,0:T(8,128)(2,1)S(1)}, bf16[256,1024]{1,0:T(8,128)(2,1)S(1)}, u32[]{:S(2)}, u32[]{:S(2)}) collective-permute-start(bf16[256,1024]{1,0:T(8,128)(2,1)S(1)} %collective-permute-done.27.one), channel_id=1, source_target_pairs={{0,16},{16,0},{1,17},{17,1},{2,18},{18,2},{3,19},{19,3},{4,20},{20... | collective-permute-start | bytes 1572872 | tf_op jit(solution)/shard_map/ppermute | solution.py:474
  117.2 0.1 pad_maximum_fusion.own
  117.3 1.3 collective-permute-start.22
  118.6 0.7 collective-permute-start.18
  119.3 4.7 %shard_map.89 = (f32[256,1024]{1,0:T(8,128)S(1)}, bf16[256,1024]{1,0:T(8,128)(2,1)S(1)}, bf16[1024,1024]{1,0:T(8,128)(2,1)S(1)}) custom-call(s32[15]{0:T(128)S(1)} %stack.63.index_ref, bf16[256,1024]{1,0:T(8,128)(2,1)S(1)} %pad_maximum_fusion.own, bf16[256,1024]{1,0:T(8,128)(2,1)S(1)} %constant_dynamic-update-slice_fusion.4.below_1, ...), custom_call_target="tpu_custom_call" | custom-call | flops 1 | bytes 1 | tf_op jit(solution)/shard_map/pallas_call | solution.py:343
  124.1 6.0 %collective-permute-done.28.other = bf16[256,1024]{1,0:T(8,128)(2,1)S(1)} collective-permute-done((bf16[256,1024]{1,0:T(8,128)(2,1)S(1)}, bf16[256,1024]{1,0:T(8,128)(2,1)S(1)}, u32[]{:S(2)}, u32[]{:S(2)}) %collective-permute-start.28) | collective-permute-done | bytes 524320 | tf_op jit(solution)/shard_map/ppermute | solution.py:474
  130.1 0.5 collective-permute-start.30
  130.6 3.8 %collective-permute-done.22.above = bf16[256,1024]{1,0:T(8,128)(2,1)S(1)} collective-permute-done((bf16[256,1024]{1,0:T(8,128)(2,1)S(1)}, bf16[256,1024]{1,0:T(8,128)(2,1)S(1)}, u32[]{:S(2)}, u32[]{:S(2)}) %collective-permute-start.22) | collective-permute-done | bytes 524320 | tf_op jit(solution)/shard_map/ppermute | solution.py:420
  134.4 3.1 %shard_map.90 = bf16[256,1024]{1,0:T(8,128)(2,1)} custom-call(s32[15]{0:T(128)S(1)} %stack.63.index_ref, bf16[256,1024]{1,0:T(8,128)(2,1)S(1)} %collective-permute-done.18.below, bf16[256,1024]{1,0:T(8,128)(2,1)S(1)} %collective-permute-done.22.above, bf16[1024,1024]{1,0:T(8,128)(2,1)S(1)} %get-tuple-element.55.weight, ...), custom_call_target="tpu_custom_call" | custom-call | flops 1 | bytes 1 | tf_op jit(solution)/shard_map/pallas_call | solution.py:387
  (38 shorter events, 0.2 us)
Async XLA Ops:
  0.0 26.2 %copy-start = (bf16[4096,4]{0,1:T(4,128)(2,1)S(1)}, bf16[4096,4]{0,1:T(4,128)(2,1)}, u32[]{:S(2)}) copy-start(bf16[4096,4]{0,1:T(4,128)(2,1)} %param.10) | copy-start | bytes 98308
  5.6 9.0 %collective-permute-start.1 = (bf16[3,1024,512]{2,1,0:T(8,128)(2,1)}, bf16[3,1024,512]{2,1,0:T(8,128)(2,1)S(1)}, u32[]{:S(2)}, u32[]{:S(2)}) collective-permute-start(bf16[3,1024,512]{2,1,0:T(8,128)(2,1)} %dynamic-slice_bitcast_fusion), channel_id=1, source_target_pairs={{0,4},{4,0},{8,12},{12,8},{1,5},{5,1},{9,13},{13,9},{2,6},{6,2},{1... | collective-permute-start | bytes 9437192 | tf_op jit(solution)/shard_map/ppermute | solution.py:417
  6.1 8.5 %collective-permute-start = (bf16[256,4096]{1,0:T(8,128)(2,1)}, bf16[256,4096]{1,0:T(8,128)(2,1)}, u32[]{:S(2)}, u32[]{:S(2)}) collective-permute-start(bf16[256,4096]{1,0:T(8,128)(2,1)} %refs_0_.5), channel_id=1, source_target_pairs={{0,4},{4,0},{8,12},{12,8},{1,5},{5,1},{9,13},{13,9},{2,6},{6,2},{1... | collective-permute-start | bytes 6291464 | tf_op jit(solution)/shard_map/ppermute | solution.py:417
  6.1 15.7 %collective-permute-start.2 = (bf16[256,1024]{1,0:T(8,128)(2,1)}, bf16[256,1024]{1,0:T(8,128)(2,1)}, u32[]{:S(2)}, u32[]{:S(2)}) collective-permute-start(bf16[256,1024]{1,0:T(8,128)(2,1)} %constant_dynamic-slice_fusion.2), channel_id=1, source_target_pairs={{0,8},{4,12},{8,0},{12,4},{1,9},{5,13},{9,1},{13,5},{2,10},{6,14},... | collective-permute-start | bytes 1572872 | tf_op jit(solution)/shard_map/ppermute | solution.py:417
  14.6 2.8 %copy-start.1 = (bf16[1024,3,1024]{2,0,1:T(8,128)(2,1)S(1)}, bf16[1024,3,1024]{2,0,1:T(8,128)(2,1)}, u32[]{:S(2)}) copy-start(bf16[1024,3,1024]{2,0,1:T(8,128)(2,1)} %param.9) | copy-start | bytes 18874372
  21.8 17.1 %collective-permute-start.3 = (bf16[256,1024]{1,0:T(8,128)(2,1)}, bf16[256,1024]{1,0:T(8,128)(2,1)}, u32[]{:S(2)}, u32[]{:S(2)}) collective-permute-start(bf16[256,1024]{1,0:T(8,128)(2,1)} %collective-permute-done.2.refs_0_.refs_2_), channel_id=1, source_target_pairs={{0,1},{1,0},{2,3},{3,2},{4,5},{5,4},{6,7},{7,6},{8,9},{9,8},{10,11... | collective-permute-start | bytes 1572872 | tf_op jit(solution)/shard_map/ppermute | solution.py:420
  24.7 14.2 %collective-permute-start.4 = (bf16[2,512,256]{2,1,0:T(8,128)(2,1)}, bf16[2,512,256]{2,1,0:T(8,128)(2,1)}, u32[]{:S(2)}, u32[]{:S(2)}) collective-permute-start(bf16[2,512,256]{2,1,0:T(8,128)(2,1)} %shard_map.82), channel_id=1, source_target_pairs={{0,8},{4,12},{8,0},{12,4},{1,9},{5,13},{9,1},{13,5},{2,10},{6,14},... | collective-permute-start | bytes 1572872 | tf_op jit(solution)/shard_map/ppermute | solution.py:417
  28.5 1.2 collective-permute-start.5
  28.6 10.4 %collective-permute-start.7 = (bf16[256,1024]{1,0:T(8,128)(2,1)}, bf16[256,1024]{1,0:T(8,128)(2,1)S(1)}, u32[]{:S(2)}, u32[]{:S(2)}) collective-permute-start(bf16[256,1024]{1,0:T(8,128)(2,1)} %collective-permute-done.2.refs_0_.refs_2_), channel_id=1, source_target_pairs={{0,4},{4,0},{8,12},{12,8},{1,5},{5,1},{9,13},{13,9},{2,6},{6,2},{1... | collective-permute-start | bytes 1572872 | tf_op jit(solution)/shard_map/ppermute | solution.py:417
  29.7 9.2 %collective-permute-start.6 = (f32[8,256]{1,0:T(8,128)S(1)}, f32[8,256]{1,0:T(8,128)S(1)}, u32[]{:S(2)}, u32[]{:S(2)}) collective-permute-start(f32[8,256]{1,0:T(8,128)S(1)} %pad_maximum_fusion.1.rate_near_ref), channel_id=1, source_target_pairs={{0,8},{4,12},{8,0},{12,4},{1,9},{5,13},{9,1},{13,5},{2,10},{6,14},... | collective-permute-start | bytes 24584 | tf_op jit(solution)/shard_map/ppermute | solution.py:417
  31.5 2.8 %copy-start.2 = (bf16[1024,3,1024]{2,0,1:T(8,128)(2,1)S(1)}, bf16[1024,3,1024]{2,0,1:T(8,128)(2,1)}, u32[]{:S(2)}) copy-start(bf16[1024,3,1024]{2,0,1:T(8,128)(2,1)} %param.9) | copy-start | bytes 18874372
  38.9 5.6 %copy-start.3 = (bf16[1024,1024]{1,0:T(8,128)(2,1)S(1)}, bf16[1024,1024]{1,0:T(8,128)(2,1)}, u32[]{:S(2)}) copy-start(bf16[1024,1024]{1,0:T(8,128)(2,1)} %own_w.1) | copy-start | bytes 6291460
  38.9 2.2 %collective-permute-start.8 = (bf16[256,1024]{1,0:T(8,128)(2,1)}, bf16[256,1024]{1,0:T(8,128)(2,1)S(1)}, u32[]{:S(2)}, u32[]{:S(2)}) collective-permute-start(bf16[256,1024]{1,0:T(8,128)(2,1)} %collective-permute-done.3.refs_1_.refs_3_), channel_id=1, source_target_pairs={{0,4},{4,0},{8,12},{12,8},{1,5},{5,1},{9,13},{13,9},{2,6},{6,2},{1... | collective-permute-start | bytes 1572872 | tf_op jit(solution)/shard_map/ppermute | solution.py:417
  44.5 5.7 %collective-permute-start.9 = (bf16[1024,1024]{1,0:T(8,128)(2,1)S(1)}, bf16[1024,1024]{1,0:T(8,128)(2,1)S(1)}, u32[]{:S(2)}, u32[]{:S(2)}) collective-permute-start(bf16[1024,1024]{1,0:T(8,128)(2,1)S(1)} %copy-done.3), channel_id=1, source_target_pairs={{0,4},{4,0},{8,12},{12,8},{1,5},{5,1},{9,13},{13,9},{2,6},{6,2},{1... | collective-permute-start | bytes 6291464 | tf_op jit(solution)/shard_map/ppermute | solution.py:417
  44.7 14.2 %collective-permute-start.10 = (bf16[2,512,256]{2,1,0:T(8,128)(2,1)S(1)}, bf16[2,512,256]{2,1,0:T(8,128)(2,1)S(1)}, u32[]{:S(2)}, u32[]{:S(2)}) collective-permute-start(bf16[2,512,256]{2,1,0:T(8,128)(2,1)S(1)} %shard_map.84), channel_id=1, source_target_pairs={{0,8},{4,12},{8,0},{12,4},{1,9},{5,13},{9,1},{13,5},{2,10},{6,14},... | collective-permute-start | bytes 1572872 | tf_op jit(solution)/shard_map/ppermute | solution.py:417
  50.2 10.2 %copy-start.4 = (bf16[4,256,512]{2,1,0:T(8,128)(2,1)S(1)}, bf16[4,256,512]{2,1,0:T(8,128)(2,1)}, u32[]{:S(2)}) copy-start(bf16[4,256,512]{2,1,0:T(8,128)(2,1)} %gate_ref.1) | copy-start | bytes 3145732
  50.2 10.2 %copy-start.5 = (bf16[4,256,512]{2,1,0:T(8,128)(2,1)S(1)}, bf16[4,256,512]{2,1,0:T(8,128)(2,1)}, u32[]{:S(2)}) copy-start(bf16[4,256,512]{2,1,0:T(8,128)(2,1)} %up_ref.1) | copy-start | bytes 3145732
  50.2 10.2 %copy-start.6 = (bf16[4,256,512]{2,1,0:T(8,128)(2,1)S(1)}, bf16[4,256,512]{2,1,0:T(8,128)(2,1)}, u32[]{:S(2)}) copy-start(bf16[4,256,512]{2,1,0:T(8,128)(2,1)} %down_ref.1) | copy-start | bytes 3145732
  54.7 20.0 %copy-start.7 = (f32[1024]{0:T(1024)S(1)}, f32[1024]{0:T(1024)}, u32[]{:S(2)}) copy-start(f32[1024]{0:T(1024)} %param.14) | copy-start | bytes 12292
  58.9 15.7 %collective-permute-start.11 = (bf16[1,1024,256]{2,1,0:T(8,128)(2,1)S(1)}, bf16[1,1024,256]{2,1,0:T(8,128)(2,1)S(1)}, u32[]{:S(2)}, u32[]{:S(2)}) collective-permute-start(bf16[1,1024,256]{2,1,0:T(8,128)(2,1)S(1)} %shard_map.85), channel_id=1, source_target_pairs={{0,8},{4,12},{8,0},{12,4},{1,9},{5,13},{9,1},{13,5},{2,10},{6,14},... | collective-permute-start | bytes 1572872 | tf_op jit(solution)/shard_map/ppermute | solution.py:417
  76.7 2.0 %collective-permute-start.12 = (bf16[256,256]{1,0:T(8,128)(2,1)S(1)}, bf16[256,256]{1,0:T(8,128)(2,1)S(1)}, u32[]{:S(2)}, u32[]{:S(2)}) collective-permute-start(bf16[256,256]{1,0:T(8,128)(2,1)S(1)} %get-tuple-element.48), channel_id=1, source_target_pairs={{0,4},{4,0},{8,12},{12,8},{1,5},{5,1},{9,13},{13,9},{2,6},{6,2},{1... | collective-permute-start | bytes 393224 | tf_op jit(solution)/shard_map/ppermute | solution.py:417
  76.7 7.8 %collective-permute-start.14 = (bf16[256,256]{1,0:T(8,128)(2,1)S(1)}, bf16[256,256]{1,0:T(8,128)(2,1)S(1)}, u32[]{:S(2)}, u32[]{:S(2)}) collective-permute-start(bf16[256,256]{1,0:T(8,128)(2,1)S(1)} %get-tuple-element.49), channel_id=1, source_target_pairs={{0,8},{4,12},{8,0},{12,4},{1,9},{5,13},{9,1},{13,5},{2,10},{6,14},... | collective-permute-start | bytes 393224 | tf_op jit(solution)/shard_map/ppermute | solution.py:417
  77.3 7.7 %collective-permute-start.15 = (bf16[256,256]{1,0:T(8,128)(2,1)S(1)}, bf16[256,256]{1,0:T(8,128)(2,1)S(1)}, u32[]{:S(2)}, u32[]{:S(2)}) collective-permute-start(bf16[256,256]{1,0:T(8,128)(2,1)S(1)} %get-tuple-element.50), channel_id=1, source_target_pairs={{0,12},{4,8},{8,4},{12,0},{1,13},{5,9},{9,5},{13,1},{2,14},{6,10},... | collective-permute-start | bytes 393224 | tf_op jit(solution)/shard_map/ppermute | solution.py:417
  78.7 10.4 %collective-permute-start.19 = (bf16[256,512]{1,0:T(8,128)(2,1)S(1)}, bf16[256,512]{1,0:T(8,128)(2,1)S(1)}, u32[]{:S(2)}, u32[]{:S(2)}) collective-permute-start(bf16[256,512]{1,0:T(8,128)(2,1)S(1)} %constant_dynamic-update-slice_fusion), channel_id=1, source_target_pairs={{1,0},{2,1},{3,2},{5,4},{6,5},{7,6},{9,8},{10,9},{11,10},{13,12},{... | collective-permute-start | bytes 786440 | tf_op jit(solution)/shard_map/ppermute | solution.py:420
  80.0 10.3 %collective-permute-start.13 = (bf16[256,512]{1,0:T(8,128)(2,1)S(1)}, bf16[256,512]{1,0:T(8,128)(2,1)S(1)}, u32[]{:S(2)}, u32[]{:S(2)}) collective-permute-start(bf16[256,512]{1,0:T(8,128)(2,1)S(1)} %constant_dynamic-update-slice_fusion), channel_id=1, source_target_pairs={{0,1},{1,2},{2,3},{4,5},{5,6},{6,7},{8,9},{9,10},{10,11},{12,13},{... | collective-permute-start | bytes 786440 | tf_op jit(solution)/shard_map/ppermute | solution.py:420
  85.0 10.7 %collective-permute-start.20 = (bf16[256,512]{1,0:T(8,128)(2,1)S(1)}, bf16[256,512]{1,0:T(8,128)(2,1)S(1)}, u32[]{:S(2)}, u32[]{:S(2)}) collective-permute-start(bf16[256,512]{1,0:T(8,128)(2,1)S(1)} %constant_dynamic-update-slice_fusion.2), channel_id=1, source_target_pairs={{1,0},{2,1},{3,2},{5,4},{6,5},{7,6},{9,8},{10,9},{11,10},{13,12},{... | collective-permute-start | bytes 786440 | tf_op jit(solution)/shard_map/ppermute | solution.py:420
  90.3 13.1 %collective-permute-start.23 = (bf16[256,1024]{1,0:T(8,128)(2,1)S(1)}, bf16[256,1024]{1,0:T(8,128)(2,1)S(1)}, u32[]{:S(2)}, u32[]{:S(2)}) collective-permute-start(bf16[256,1024]{1,0:T(8,128)(2,1)S(1)} %get-tuple-element.51), channel_id=1, source_target_pairs={{0,8},{4,12},{8,0},{12,4},{1,9},{5,13},{9,1},{13,5},{2,10},{6,14},... | collective-permute-start | bytes 1572872 | tf_op jit(solution)/shard_map/ppermute | solution.py:417
  90.8 9.0 %collective-permute-start.16 = (bf16[256,512]{1,0:T(8,128)(2,1)S(1)}, bf16[256,512]{1,0:T(8,128)(2,1)S(1)}, u32[]{:S(2)}, u32[]{:S(2)}) collective-permute-start(bf16[256,512]{1,0:T(8,128)(2,1)S(1)} %constant_dynamic-update-slice_fusion.2), channel_id=1, source_target_pairs={{0,1},{1,2},{2,3},{4,5},{5,6},{6,7},{8,9},{9,10},{10,11},{12,13},{... | collective-permute-start | bytes 786440 | tf_op jit(solution)/shard_map/ppermute | solution.py:420
  95.7 15.5 %collective-permute-start.21 = (bf16[256,1024]{1,0:T(8,128)(2,1)S(1)}, bf16[256,1024]{1,0:T(8,128)(2,1)S(1)}, u32[]{:S(2)}, u32[]{:S(2)}) collective-permute-start(bf16[256,1024]{1,0:T(8,128)(2,1)S(1)} %constant_dynamic-update-slice_fusion.6.above_1), channel_id=1, source_target_pairs={{1,0},{2,1},{5,4},{6,5},{9,8},{10,9},{13,12},{14,13},{17,16},{18,1... | collective-permute-start | bytes 1572872 | tf_op jit(solution)/shard_map/ppermute | solution.py:420
  99.9 11.4 %collective-permute-start.17 = (bf16[256,1024]{1,0:T(8,128)(2,1)S(1)}, bf16[256,1024]{1,0:T(8,128)(2,1)S(1)}, u32[]{:S(2)}, u32[]{:S(2)}) collective-permute-start(bf16[256,1024]{1,0:T(8,128)(2,1)S(1)} %constant_dynamic-update-slice_fusion.4.below_1), channel_id=1, source_target_pairs={{1,2},{2,3},{5,6},{6,7},{9,10},{10,11},{13,14},{14,15},{17,18},{18... | collective-permute-start | bytes 1572872 | tf_op jit(solution)/shard_map/ppermute | solution.py:420
  103.3 12.1 %collective-permute-start.27 = (bf16[256,1024]{1,0:T(8,128)(2,1)S(1)}, bf16[256,1024]{1,0:T(8,128)(2,1)S(1)}, u32[]{:S(2)}, u32[]{:S(2)}) collective-permute-start(bf16[256,1024]{1,0:T(8,128)(2,1)S(1)} %get-tuple-element.57), channel_id=1, source_target_pairs={{0,8},{4,12},{8,0},{12,4},{1,9},{5,13},{9,1},{13,5},{2,10},{6,14},... | collective-permute-start | bytes 1572872 | tf_op jit(solution)/shard_map/ppermute | solution.py:417
  103.9 11.8 %collective-permute-start.24 = (bf16[256,1024]{1,0:T(8,128)(2,1)S(1)}, bf16[256,1024]{1,0:T(8,128)(2,1)S(1)}, u32[]{:S(2)}, u32[]{:S(2)}) collective-permute-start(bf16[256,1024]{1,0:T(8,128)(2,1)S(1)} %collective-permute-done.23.one), channel_id=1, source_target_pairs={{0,16},{16,0},{1,17},{17,1},{2,18},{18,2},{3,19},{19,3},{4,20},{20... | collective-permute-start | bytes 1572872 | tf_op jit(solution)/shard_map/ppermute | solution.py:474
  111.3 8.0 %collective-permute-start.25 = (bf16[256,1024]{1,0:T(8,128)(2,1)S(1)}, bf16[256,1024]{1,0:T(8,128)(2,1)S(1)}, u32[]{:S(2)}, u32[]{:S(2)}) collective-permute-start(bf16[256,1024]{1,0:T(8,128)(2,1)S(1)} %collective-permute-done.23.one), channel_id=1, source_target_pairs={{0,4},{4,0},{8,12},{12,8},{1,5},{5,1},{9,13},{13,9},{2,6},{6,2},{1... | collective-permute-start | bytes 1572872 | tf_op jit(solution)/shard_map/ppermute | solution.py:417
  115.7 3.6 %collective-permute-start.26 = (bf16[256,1024]{1,0:T(8,128)(2,1)S(1)}, bf16[256,1024]{1,0:T(8,128)(2,1)S(1)}, u32[]{:S(2)}, u32[]{:S(2)}) collective-permute-start(bf16[256,1024]{1,0:T(8,128)(2,1)S(1)} %collective-permute-done.24.other), channel_id=1, source_target_pairs={{0,4},{4,0},{8,12},{12,8},{1,5},{5,1},{9,13},{13,9},{2,6},{6,2},{1... | collective-permute-start | bytes 1572872 | tf_op jit(solution)/shard_map/ppermute | solution.py:417
  115.7 14.3 %collective-permute-start.28 = (bf16[256,1024]{1,0:T(8,128)(2,1)S(1)}, bf16[256,1024]{1,0:T(8,128)(2,1)S(1)}, u32[]{:S(2)}, u32[]{:S(2)}) collective-permute-start(bf16[256,1024]{1,0:T(8,128)(2,1)S(1)} %collective-permute-done.27.one), channel_id=1, source_target_pairs={{0,16},{16,0},{1,17},{17,1},{2,18},{18,2},{3,19},{19,3},{4,20},{20... | collective-permute-start | bytes 1572872 | tf_op jit(solution)/shard_map/ppermute | solution.py:474
  117.3 17.1 %collective-permute-start.22 = (bf16[256,1024]{1,0:T(8,128)(2,1)S(1)}, bf16[256,1024]{1,0:T(8,128)(2,1)S(1)}, u32[]{:S(2)}, u32[]{:S(2)}) collective-permute-start(bf16[256,1024]{1,0:T(8,128)(2,1)S(1)} %collective-permute-done.21.above_2), channel_id=1, source_target_pairs={{1,0},{5,4},{9,8},{13,12},{17,16},{21,20},{25,24},{29,28}} | collective-permute-start | bytes 1572872 | tf_op jit(solution)/shard_map/ppermute | solution.py:420
  118.6 15.8 %collective-permute-start.18 = (bf16[256,1024]{1,0:T(8,128)(2,1)S(1)}, bf16[256,1024]{1,0:T(8,128)(2,1)S(1)}, u32[]{:S(2)}, u32[]{:S(2)}) collective-permute-start(bf16[256,1024]{1,0:T(8,128)(2,1)S(1)} %collective-permute-done.17.below_2), channel_id=1, source_target_pairs={{2,3},{6,7},{10,11},{14,15},{18,19},{22,23},{26,27},{30,31}} | collective-permute-start | bytes 1572872 | tf_op jit(solution)/shard_map/ppermute | solution.py:420
  130.1 4.4 %collective-permute-start.29 = (bf16[256,1024]{1,0:T(8,128)(2,1)S(1)}, bf16[256,1024]{1,0:T(8,128)(2,1)S(1)}, u32[]{:S(2)}, u32[]{:S(2)}) collective-permute-start(bf16[256,1024]{1,0:T(8,128)(2,1)S(1)} %collective-permute-done.27.one), channel_id=1, source_target_pairs={{0,4},{4,0},{8,12},{12,8},{1,5},{5,1},{9,13},{13,9},{2,6},{6,2},{1... | collective-permute-start | bytes 1572872 | tf_op jit(solution)/shard_map/ppermute | solution.py:417
  130.1 4.4 %collective-permute-start.30 = (bf16[256,1024]{1,0:T(8,128)(2,1)S(1)}, bf16[256,1024]{1,0:T(8,128)(2,1)S(1)}, u32[]{:S(2)}, u32[]{:S(2)}) collective-permute-start(bf16[256,1024]{1,0:T(8,128)(2,1)S(1)} %collective-permute-done.28.other), channel_id=1, source_target_pairs={{0,4},{4,0},{8,12},{12,8},{1,5},{5,1},{9,13},{13,9},{2,6},{6,2},{1... | collective-permute-start | bytes 1572872 | tf_op jit(solution)/shard_map/ppermute | solution.py:417

commit v10 on v9

--- a/solution.py
+++ b/solution.py
@@ -474,13 +474,13 @@
         return lax.ppermute(array, "groups", [(0, 1), (1, 0)])
 
     below_mine, above_mine = both(0, mine, mine)
-    first_x = across(after(out_first, theirs, below_mine, above_mine), 2)
+    first_x = across(after(out_first, theirs), 2)
+    later_x = across(after(out_later, theirs, below_mine, above_mine), 2)
     below_theirs, above_theirs = both(0, theirs, theirs)
     below_1 = jnp.concatenate([below_mine, below_theirs], axis=1)
     above_1 = jnp.concatenate([above_mine, above_theirs], axis=1)
-    first_x, out_later = lax.optimization_barrier((first_x, out_later, below_1, above_1))[:2]
+    first_x = after(first_x, below_1, above_1)
     first_y = swap_groups(first_x)
-    later_x = across(out_later, 2)
     below_2, above_2 = both(1, below_1, above_1)
     first_x_peer, first_y_peer, later_x = (after(array, below_2, above_2) for array in (first_x, first_y, later_x))
     first_x_peer, first_y_peer = across(first_x_peer, 1), across(first_y_peer, 1)

time: 138 us -> 136 us (0.986)
  waiting for transfers between devices: 43.1 us -> 39.9 us
    ppermute x20, waiting for transfers between devices: 19.9 us -> 15.3 us  [across(): return lax.ppermute(array, 'seq', [(i, i ^ bit) for i in range(4)])]
    ppermute x2, waiting for transfers between devices: 6.25 us -> 8.38 us  [swap_groups(): return lax.ppermute(array, 'groups', [(0, 1), (1, 0)])]
  transfers between devices with their start and end apart: 31 -> 31, of which waited for: 15 -> 13; matrix products, arithmetic and copies ran while one was open for 3% -> 3% of each run, Pallas kernels for 26% -> 27%
where the time goes in v10:
time: 136 us
  Pallas kernels  44.8 us (33%)
  waiting for transfers between devices  39.9 us (29%)
  starting transfers between devices  35.5 us (26%)
  local copies, waits for them, and re-layouts  12.7 us (9%)
  matrix products  2.25 us (2%)
    pallas_call x5, Pallas kernels, project(): pl.pallas_call(functools.partial(project_kernel, len(whole), len(pairs)),...  20.7 us
    ppermute x9, starting transfers between devices, hop(): return lax.ppermute(array, 'head', links)  18.6 us
    ppermute x9, waiting for transfers between devices, hop(): return lax.ppermute(array, 'head', links)  16.2 us
    ppermute x20, waiting for transfers between devices, across(): return lax.ppermute(array, 'seq', [(i, i ^ bit) for i in range(4)])  15.3 us
    pallas_call x1, Pallas kernels, update(): pl.pallas_call(update_kernel, out_shape=[out] * 3, grid_spec=pltpu.Prefet...  14.2 us
    ppermute x20, starting transfers between devices, across(): return lax.ppermute(array, 'seq', [(i, i ^ bit) for i in range(4)])  13.9 us
    ppermute x2, waiting for transfers between devices, swap_groups(): return lax.ppermute(array, 'groups', [(0, 1), (1, 0)])  8.38 us
    unnamed x20, local copies, waits for them, and re-layouts  5.67 us
  transfers between devices with their start and end apart: 31, of which 13 were waited for; matrix products, arithmetic and copies ran while one was open for 3% of the time, Pallas kernels for 27%

profile of v10, /device:TPU:0, one launch (start us, length us, event | category | flops | bytes accessed | tf_op | source)
XLA Modules:
  0.0 135.7 jit_solution(1882027237086286586)
XLA Ops:
  0.0 1.9 %constant_dynamic-slice_fusion.2 = bf16[256,1024]{1,0:T(8,128)(2,1)} fusion(bf16[256,4096]{1,0:T(8,128)(2,1)} %refs_0_.5, s32[]{:T(128)S(6)} %select_n.23), kind=kLoop, calls=%fused_computation.15 | loop fusion | bytes 1048580 | tf_op jit(solution)/shard_map/dynamic_slice | solution.py:429
  1.9 3.7 %dynamic-slice_bitcast_fusion = bf16[3,1024,512]{2,1,0:T(8,128)(2,1)} fusion(bf16[1024,3,1024]{2,0,1:T(8,128)(2,1)} %param.9, s32[]{:T(128)S(6)} %select_n.24), kind=kLoop, calls=%fused_computation | loop fusion | bytes 6291460 | tf_op jit(solution)/shard_map/dynamic_slice | solution.py:433
  5.6 0.5 collective-permute-start.1
  6.1 0.1 collective-permute-start
  6.1 2.9 %collective-permute-start.2 = (bf16[256,1024]{1,0:T(8,128)(2,1)}, bf16[256,1024]{1,0:T(8,128)(2,1)}, u32[]{:S(2)}, u32[]{:S(2)}) collective-permute-start(bf16[256,1024]{1,0:T(8,128)(2,1)} %constant_dynamic-slice_fusion.2), channel_id=1, source_target_pairs={{0,8},{4,12},{8,0},{12,4},{1,9},{5,13},{9,1},{13,5},{2,10},{6,14},... | collective-permute-start | bytes 1572872 | tf_op jit(solution)/shard_map/ppermute | solution.py:417
  9.1 0.1 stack.63.index_ref
  9.2 5.5 %collective-permute-done.refs_1_ = bf16[256,4096]{1,0:T(8,128)(2,1)} collective-permute-done((bf16[256,4096]{1,0:T(8,128)(2,1)}, bf16[256,4096]{1,0:T(8,128)(2,1)}, u32[]{:S(2)}, u32[]{:S(2)}) %collective-permute-start) | collective-permute-done | bytes 2097184 | tf_op jit(solution)/shard_map/ppermute | solution.py:417
  14.6 2.8 %copy-done.1 = bf16[1024,3,1024]{2,0,1:T(8,128)(2,1)S(1)} copy-done((bf16[1024,3,1024]{2,0,1:T(8,128)(2,1)S(1)}, bf16[1024,3,1024]{2,0,1:T(8,128)(2,1)}, u32[]{:S(2)}) %copy-start.1) | copy-done | bytes 6291480
  17.4 4.4 %shard_map.82 = bf16[2,512,256]{2,1,0:T(8,128)(2,1)} custom-call(s32[15]{0:T(128)S(1)} %stack.63.index_ref, bf16[256,4096]{1,0:T(8,128)(2,1)} %refs_0_.5, bf16[256,4096]{1,0:T(8,128)(2,1)} %collective-permute-done.refs_1_, bf16[3,1024,1024]{2,1,0:T(8,128)(2,1)S(1)} %bitcast.25, bf16[3,1024,512]{2,1,0:T(8,128)(2,1)S(1)} %collective-permute-done.1.refs_3_.refs_5_.refs_7_), custom_call_target="tpu_custom_call" | custom-call | flops 1 | bytes 1 | tf_op jit(solution)/shard_map/pallas_call | solution.py:146
  21.8 2.9 %collective-permute-start.3 = (bf16[256,1024]{1,0:T(8,128)(2,1)}, bf16[256,1024]{1,0:T(8,128)(2,1)}, u32[]{:S(2)}, u32[]{:S(2)}) collective-permute-start(bf16[256,1024]{1,0:T(8,128)(2,1)} %collective-permute-done.2.refs_0_.refs_2_), channel_id=1, source_target_pairs={{0,1},{1,0},{2,3},{3,2},{4,5},{5,4},{6,7},{7,6},{8,9},{9,8},{10,11... | collective-permute-start | bytes 1572872 | tf_op jit(solution)/shard_map/ppermute | solution.py:420
  24.7 1.5 %collective-permute-start.4 = (bf16[2,512,256]{2,1,0:T(8,128)(2,1)}, bf16[2,512,256]{2,1,0:T(8,128)(2,1)}, u32[]{:S(2)}, u32[]{:S(2)}) collective-permute-start(bf16[2,512,256]{2,1,0:T(8,128)(2,1)} %shard_map.82), channel_id=1, source_target_pairs={{0,8},{4,12},{8,0},{12,4},{1,9},{5,13},{9,1},{13,5},{2,10},{6,14},... | collective-permute-start | bytes 1572872 | tf_op jit(solution)/shard_map/ppermute | solution.py:417
  26.2 2.3 %compare_select_fusion = f32[4,256]{1,0:T(4,128)S(1)} fusion(bf16[256,4096]{1,0:T(8,128)(2,1)} %refs_0_.5, bf16[4096,4]{0,1:T(4,128)(2,1)S(1)} %copy-done), kind=kOutput, calls=%fused_computation.11 | convolution fusion | flops 8394752 | bytes 2134016 | tf_op jit(solution)/shard_map/dot_general | solution.py:445
  28.5 0.1 collective-permute-start.5
  28.6 0.5 collective-permute-start.7
  29.1 0.7 collective-permute-done.5
  29.7 0.5 collective-permute-start.6
  30.3 1.3 constant_dynamic-slice_fusion.1
  31.5 0.0 copy-start.2
  31.5 2.8 %copy-done.2 = bf16[1024,3,1024]{2,0,1:T(8,128)(2,1)S(1)} copy-done((bf16[1024,3,1024]{2,0,1:T(8,128)(2,1)S(1)}, bf16[1024,3,1024]{2,0,1:T(8,128)(2,1)}, u32[]{:S(2)}) %copy-start.2) | copy-done | bytes 6291480
  34.3 4.6 %shard_map.83.local_near_ref = f32[3,512,256]{2,1,0:T(8,128)S(1)} custom-call(s32[15]{0:T(128)S(1)} %stack.63.index_ref, bf16[256,4096]{1,0:T(8,128)(2,1)} %refs_0_.5, bf16[256,4096]{1,0:T(8,128)(2,1)} %collective-permute-done.refs_1_, bf16[3,1024,1024]{2,1,0:T(8,128)(2,1)S(1)} %bitcast.26, ...), custom_call_target="tpu_custom_call" | custom-call | flops 1 | bytes 1 | tf_op jit(solution)/shard_map/pallas_call | solution.py:146
  38.9 0.0 copy-start.3
  38.9 0.1 collective-permute-start.8
  39.0 2.1 %collective-permute-done.8.refs_3_.refs_5_ = bf16[256,1024]{1,0:T(8,128)(2,1)S(1)} collective-permute-done((bf16[256,1024]{1,0:T(8,128)(2,1)}, bf16[256,1024]{1,0:T(8,128)(2,1)S(1)}, u32[]{:S(2)}, u32[]{:S(2)}) %collective-permute-start.8) | collective-permute-done | bytes 524320 | tf_op jit(solution)/shard_map/ppermute | solution.py:417
  41.1 3.4 %shard_map.84 = bf16[2,512,256]{2,1,0:T(8,128)(2,1)S(1)} custom-call(s32[15]{0:T(128)S(1)} %stack.63.index_ref, bf16[256,1024]{1,0:T(8,128)(2,1)} %collective-permute-done.2.refs_0_.refs_2_, bf16[256,1024]{1,0:T(8,128)(2,1)} %collective-permute-done.3.refs_1_.refs_3_, bf16[256,1024]{1,0:T(8,128)(2,1)S(1)} %collective-permute-done.7.refs_2_.refs_4_, ...), custom_call_target="tpu_custom_call" | custom-call | flops 1 | bytes 1 | tf_op jit(solution)/shard_map/pallas_call | solution.py:146
  44.5 0.2 collective-permute-start.9
  44.7 1.5 %collective-permute-start.10 = (bf16[2,512,256]{2,1,0:T(8,128)(2,1)S(1)}, bf16[2,512,256]{2,1,0:T(8,128)(2,1)S(1)}, u32[]{:S(2)}, u32[]{:S(2)}) collective-permute-start(bf16[2,512,256]{2,1,0:T(8,128)(2,1)S(1)} %shard_map.84), channel_id=1, source_target_pairs={{0,8},{4,12},{8,0},{12,4},{1,9},{5,13},{9,1},{13,5},{2,10},{6,14},... | collective-permute-start | bytes 1572872 | tf_op jit(solution)/shard_map/ppermute | solution.py:417
  46.2 3.9 %shard_map.85 = bf16[1,1024,256]{2,1,0:T(8,128)(2,1)S(1)} custom-call(s32[15]{0:T(128)S(1)} %stack.63.index_ref, bf16[256,4096]{1,0:T(8,128)(2,1)} %refs_0_.5, bf16[256,4096]{1,0:T(8,128)(2,1)} %collective-permute-done.refs_1_, bf16[256,1024]{1,0:T(8,128)(2,1)} %collective-permute-done.2.refs_0_.refs_2_, ...), custom_call_target="tpu_custom_call" | custom-call | flops 1 | bytes 1 | tf_op jit(solution)/shard_map/pallas_call | solution.py:146
  50.2 0.0 copy-start.4
  50.2 0.0 copy-start.5
  50.2 0.0 copy-start.6
  50.2 4.4 %shard_map.86.local_far_ref = f32[3,512,256]{2,1,0:T(8,128)S(1)} custom-call(s32[15]{0:T(128)S(1)} %stack.63.index_ref, bf16[256,1024]{1,0:T(8,128)(2,1)} %collective-permute-done.2.refs_0_.refs_2_, bf16[256,1024]{1,0:T(8,128)(2,1)} %collective-permute-done.3.refs_1_.refs_3_, bf16[256,1024]{1,0:T(8,128)(2,1)S(1)} %collective-permute-done.7.refs_2_.refs_4_, ...), custom_call_target="tpu_custom_call" | custom-call | flops 1 | bytes 1 | tf_op jit(solution)/shard_map/pallas_call | solution.py:146
  54.7 0.0 copy-start.7
  54.7 4.2 %collective-permute-done.10.near_ref = bf16[2,512,256]{2,1,0:T(8,128)(2,1)S(1)} collective-permute-done((bf16[2,512,256]{2,1,0:T(8,128)(2,1)S(1)}, bf16[2,512,256]{2,1,0:T(8,128)(2,1)S(1)}, u32[]{:S(2)}, u32[]{:S(2)}) %collective-permute-start.10) | collective-permute-done | bytes 524320 | tf_op jit(solution)/shard_map/ppermute | solution.py:417
  58.9 1.5 %collective-permute-start.11 = (bf16[1,1024,256]{2,1,0:T(8,128)(2,1)S(1)}, bf16[1,1024,256]{2,1,0:T(8,128)(2,1)S(1)}, u32[]{:S(2)}, u32[]{:S(2)}) collective-permute-start(bf16[1,1024,256]{2,1,0:T(8,128)(2,1)S(1)} %shard_map.85), channel_id=1, source_target_pairs={{0,8},{4,12},{8,0},{12,4},{1,9},{5,13},{9,1},{13,5},{2,10},{6,14},... | collective-permute-start | bytes 1572872 | tf_op jit(solution)/shard_map/ppermute | solution.py:417
  60.4 14.2 %shard_map.87 = (bf16[256,512]{1,0:T(8,128)(2,1)S(1)}, bf16[256,512]{1,0:T(8,128)(2,1)S(1)}, bf16[256,512]{1,0:T(8,128)(2,1)S(1)}) custom-call(s32[15]{0:T(128)S(1)} %stack.63.index_ref, f32[3,512,256]{2,1,0:T(8,128)S(1)} %shard_map.83.local_near_ref, f32[3,512,256]{2,1,0:T(8,128)S(1)} %shard_map.86.local_far_ref, ...), custom_call_target="tpu_custom_call" | custom-call | flops 1 | bytes 1 | tf_op jit(solution)/shard_map/pallas_call | solution.py:230
  74.7 2.0 %shard_map.88 = (bf16[256,256]{1,0:T(8,128)(2,1)S(1)}, bf16[256,256]{1,0:T(8,128)(2,1)S(1)}, bf16[256,256]{1,0:T(8,128)(2,1)S(1)}, bf16[256,256]{1,0:T(8,128)(2,1)S(1)}) custom-call(s32[15]{0:T(128)S(1)} %stack.63.index_ref, f32[3,512,256]{2,1,0:T(8,128)S(1)} %shard_map.83.local_near_ref, f32[3,512,256]{2,1,0:T(8,128)S(1)} %shard_map.86.local_far_ref, ...), custom_call_target="tpu_custom_call" | custom-call | flops 1 | bytes 1 | tf_op jit(solution)/shard_map/pallas_call | solution.py:276
  76.7 0.1 collective-permute-start.12
  76.7 0.6 collective-permute-start.14
  77.3 1.3 collective-permute-start.15
  78.7 1.3 collective-permute-start.19
  80.0 4.6 %collective-permute-start.13 = (bf16[256,512]{1,0:T(8,128)(2,1)S(1)}, bf16[256,512]{1,0:T(8,128)(2,1)S(1)}, u32[]{:S(2)}, u32[]{:S(2)}) collective-permute-start(bf16[256,512]{1,0:T(8,128)(2,1)S(1)} %constant_dynamic-update-slice_fusion), channel_id=1, source_target_pairs={{0,1},{1,2},{2,3},{4,5},{5,6},{6,7},{8,9},{9,10},{10,11},{12,13},{... | collective-permute-start | bytes 786440 | tf_op jit(solution)/shard_map/ppermute | solution.py:420
  84.5 0.5 collective-permute-done.15
  85.0 1.3 collective-permute-start.20
  86.3 0.6 collective-permute-start.23
  86.9 4.5 %collective-permute-start.16 = (bf16[256,512]{1,0:T(8,128)(2,1)S(1)}, bf16[256,512]{1,0:T(8,128)(2,1)S(1)}, u32[]{:S(2)}, u32[]{:S(2)}) collective-permute-start(bf16[256,512]{1,0:T(8,128)(2,1)S(1)} %constant_dynamic-update-slice_fusion.2), channel_id=1, source_target_pairs={{0,1},{1,2},{2,3},{4,5},{5,6},{6,7},{8,9},{9,10},{10,11},{12,13},{... | collective-permute-start | bytes 786440 | tf_op jit(solution)/shard_map/ppermute | solution.py:420
  91.5 4.2 %collective-permute-done.20 = bf16[256,512]{1,0:T(8,128)(2,1)S(1)} collective-permute-done((bf16[256,512]{1,0:T(8,128)(2,1)S(1)}, bf16[256,512]{1,0:T(8,128)(2,1)S(1)}, u32[]{:S(2)}, u32[]{:S(2)}) %collective-permute-start.20) | collective-permute-done | bytes 262176 | tf_op jit(solution)/shard_map/ppermute | solution.py:420
  95.7 1.3 collective-permute-start.21
  97.1 0.1 collective-permute-done.16
  97.2 0.7 collective-permute-start.17
  97.9 1.6 %collective-permute-start.27 = (bf16[256,1024]{1,0:T(8,128)(2,1)S(1)}, bf16[256,1024]{1,0:T(8,128)(2,1)S(1)}, u32[]{:S(2)}, u32[]{:S(2)}) collective-permute-start(bf16[256,1024]{1,0:T(8,128)(2,1)S(1)} %get-tuple-element.57), channel_id=1, source_target_pairs={{0,8},{4,12},{8,0},{12,4},{1,9},{5,13},{9,1},{13,5},{2,10},{6,14},... | collective-permute-start | bytes 1572872 | tf_op jit(solution)/shard_map/ppermute | solution.py:417
  99.5 1.6 %collective-permute-done.23.one = bf16[256,1024]{1,0:T(8,128)(2,1)S(1)} collective-permute-done((bf16[256,1024]{1,0:T(8,128)(2,1)S(1)}, bf16[256,1024]{1,0:T(8,128)(2,1)S(1)}, u32[]{:S(2)}, u32[]{:S(2)}) %collective-permute-start.23) | collective-permute-done | bytes 524320 | tf_op jit(solution)/shard_map/ppermute | solution.py:417
  101.1 1.5 %collective-permute-start.24 = (bf16[256,1024]{1,0:T(8,128)(2,1)S(1)}, bf16[256,1024]{1,0:T(8,128)(2,1)S(1)}, u32[]{:S(2)}, u32[]{:S(2)}) collective-permute-start(bf16[256,1024]{1,0:T(8,128)(2,1)S(1)} %collective-permute-done.23.one), channel_id=1, source_target_pairs={{0,16},{16,0},{1,17},{17,1},{2,18},{18,2},{3,19},{19,3},{4,20},{20... | collective-permute-start | bytes 1572872 | tf_op jit(solution)/shard_map/ppermute | solution.py:474
  102.6 8.6 %collective-permute-done.21.above_2 = bf16[256,1024]{1,0:T(8,128)(2,1)S(1)} collective-permute-done((bf16[256,1024]{1,0:T(8,128)(2,1)S(1)}, bf16[256,1024]{1,0:T(8,128)(2,1)S(1)}, u32[]{:S(2)}, u32[]{:S(2)}) %collective-permute-start.21) | collective-permute-done | bytes 524320 | tf_op jit(solution)/shard_map/ppermute | solution.py:420
  111.3 0.8 collective-permute-done.27.one
  112.0 2.4 %collective-permute-done.24.other = bf16[256,1024]{1,0:T(8,128)(2,1)S(1)} collective-permute-done((bf16[256,1024]{1,0:T(8,128)(2,1)S(1)}, bf16[256,1024]{1,0:T(8,128)(2,1)S(1)}, u32[]{:S(2)}, u32[]{:S(2)}) %collective-permute-start.24) | collective-permute-done | bytes 524320 | tf_op jit(solution)/shard_map/ppermute | solution.py:474
  114.4 1.5 %collective-permute-start.28 = (bf16[256,1024]{1,0:T(8,128)(2,1)S(1)}, bf16[256,1024]{1,0:T(8,128)(2,1)S(1)}, u32[]{:S(2)}, u32[]{:S(2)}) collective-permute-start(bf16[256,1024]{1,0:T(8,128)(2,1)S(1)} %collective-permute-done.27.one), channel_id=1, source_target_pairs={{0,16},{16,0},{1,17},{17,1},{2,18},{18,2},{3,19},{19,3},{4,20},{20... | collective-permute-start | bytes 1572872 | tf_op jit(solution)/shard_map/ppermute | solution.py:474
  116.0 0.1 pad_maximum_fusion.own
  116.0 1.3 collective-permute-start.22
  117.3 0.7 collective-permute-start.18
  118.0 4.7 %shard_map.89 = (f32[256,1024]{1,0:T(8,128)S(1)}, bf16[256,1024]{1,0:T(8,128)(2,1)S(1)}, bf16[1024,1024]{1,0:T(8,128)(2,1)S(1)}) custom-call(s32[15]{0:T(128)S(1)} %stack.63.index_ref, bf16[256,1024]{1,0:T(8,128)(2,1)S(1)} %pad_maximum_fusion.own, bf16[256,1024]{1,0:T(8,128)(2,1)S(1)} %constant_dynamic-update-slice_fusion.4.below_1, ...), custom_call_target="tpu_custom_call" | custom-call | flops 1 | bytes 1 | tf_op jit(solution)/shard_map/pallas_call | solution.py:343
  122.8 6.0 %collective-permute-done.28.other = bf16[256,1024]{1,0:T(8,128)(2,1)S(1)} collective-permute-done((bf16[256,1024]{1,0:T(8,128)(2,1)S(1)}, bf16[256,1024]{1,0:T(8,128)(2,1)S(1)}, u32[]{:S(2)}, u32[]{:S(2)}) %collective-permute-start.28) | collective-permute-done | bytes 524320 | tf_op jit(solution)/shard_map/ppermute | solution.py:474
  128.8 0.5 collective-permute-start.30
  129.3 3.3 %collective-permute-done.22.above = bf16[256,1024]{1,0:T(8,128)(2,1)S(1)} collective-permute-done((bf16[256,1024]{1,0:T(8,128)(2,1)S(1)}, bf16[256,1024]{1,0:T(8,128)(2,1)S(1)}, u32[]{:S(2)}, u32[]{:S(2)}) %collective-permute-start.22) | collective-permute-done | bytes 524320 | tf_op jit(solution)/shard_map/ppermute | solution.py:420
  132.6 3.1 %shard_map.90 = bf16[256,1024]{1,0:T(8,128)(2,1)} custom-call(s32[15]{0:T(128)S(1)} %stack.63.index_ref, bf16[256,1024]{1,0:T(8,128)(2,1)S(1)} %collective-permute-done.18.below, bf16[256,1024]{1,0:T(8,128)(2,1)S(1)} %collective-permute-done.22.above, bf16[1024,1024]{1,0:T(8,128)(2,1)S(1)} %get-tuple-element.55.weight, ...), custom_call_target="tpu_custom_call" | custom-call | flops 1 | bytes 1 | tf_op jit(solution)/shard_map/pallas_call | solution.py:387
  (38 shorter events, 0.2 us)
Async XLA Ops:
  0.0 26.2 %copy-start = (bf16[4096,4]{0,1:T(4,128)(2,1)S(1)}, bf16[4096,4]{0,1:T(4,128)(2,1)}, u32[]{:S(2)}) copy-start(bf16[4096,4]{0,1:T(4,128)(2,1)} %param.10) | copy-start | bytes 98308
  5.6 9.0 %collective-permute-start.1 = (bf16[3,1024,512]{2,1,0:T(8,128)(2,1)}, bf16[3,1024,512]{2,1,0:T(8,128)(2,1)S(1)}, u32[]{:S(2)}, u32[]{:S(2)}) collective-permute-start(bf16[3,1024,512]{2,1,0:T(8,128)(2,1)} %dynamic-slice_bitcast_fusion), channel_id=1, source_target_pairs={{0,4},{4,0},{8,12},{12,8},{1,5},{5,1},{9,13},{13,9},{2,6},{6,2},{1... | collective-permute-start | bytes 9437192 | tf_op jit(solution)/shard_map/ppermute | solution.py:417
  6.1 8.5 %collective-permute-start = (bf16[256,4096]{1,0:T(8,128)(2,1)}, bf16[256,4096]{1,0:T(8,128)(2,1)}, u32[]{:S(2)}, u32[]{:S(2)}) collective-permute-start(bf16[256,4096]{1,0:T(8,128)(2,1)} %refs_0_.5), channel_id=1, source_target_pairs={{0,4},{4,0},{8,12},{12,8},{1,5},{5,1},{9,13},{13,9},{2,6},{6,2},{1... | collective-permute-start | bytes 6291464 | tf_op jit(solution)/shard_map/ppermute | solution.py:417
  6.1 15.7 %collective-permute-start.2 = (bf16[256,1024]{1,0:T(8,128)(2,1)}, bf16[256,1024]{1,0:T(8,128)(2,1)}, u32[]{:S(2)}, u32[]{:S(2)}) collective-permute-start(bf16[256,1024]{1,0:T(8,128)(2,1)} %constant_dynamic-slice_fusion.2), channel_id=1, source_target_pairs={{0,8},{4,12},{8,0},{12,4},{1,9},{5,13},{9,1},{13,5},{2,10},{6,14},... | collective-permute-start | bytes 1572872 | tf_op jit(solution)/shard_map/ppermute | solution.py:417
  14.6 2.8 %copy-start.1 = (bf16[1024,3,1024]{2,0,1:T(8,128)(2,1)S(1)}, bf16[1024,3,1024]{2,0,1:T(8,128)(2,1)}, u32[]{:S(2)}) copy-start(bf16[1024,3,1024]{2,0,1:T(8,128)(2,1)} %param.9) | copy-start | bytes 18874372
  21.8 17.1 %collective-permute-start.3 = (bf16[256,1024]{1,0:T(8,128)(2,1)}, bf16[256,1024]{1,0:T(8,128)(2,1)}, u32[]{:S(2)}, u32[]{:S(2)}) collective-permute-start(bf16[256,1024]{1,0:T(8,128)(2,1)} %collective-permute-done.2.refs_0_.refs_2_), channel_id=1, source_target_pairs={{0,1},{1,0},{2,3},{3,2},{4,5},{5,4},{6,7},{7,6},{8,9},{9,8},{10,11... | collective-permute-start | bytes 1572872 | tf_op jit(solution)/shard_map/ppermute | solution.py:420
  24.7 14.2 %collective-permute-start.4 = (bf16[2,512,256]{2,1,0:T(8,128)(2,1)}, bf16[2,512,256]{2,1,0:T(8,128)(2,1)}, u32[]{:S(2)}, u32[]{:S(2)}) collective-permute-start(bf16[2,512,256]{2,1,0:T(8,128)(2,1)} %shard_map.82), channel_id=1, source_target_pairs={{0,8},{4,12},{8,0},{12,4},{1,9},{5,13},{9,1},{13,5},{2,10},{6,14},... | collective-permute-start | bytes 1572872 | tf_op jit(solution)/shard_map/ppermute | solution.py:417
  28.5 1.2 collective-permute-start.5
  28.6 10.4 %collective-permute-start.7 = (bf16[256,1024]{1,0:T(8,128)(2,1)}, bf16[256,1024]{1,0:T(8,128)(2,1)S(1)}, u32[]{:S(2)}, u32[]{:S(2)}) collective-permute-start(bf16[256,1024]{1,0:T(8,128)(2,1)} %collective-permute-done.2.refs_0_.refs_2_), channel_id=1, source_target_pairs={{0,4},{4,0},{8,12},{12,8},{1,5},{5,1},{9,13},{13,9},{2,6},{6,2},{1... | collective-permute-start | bytes 1572872 | tf_op jit(solution)/shard_map/ppermute | solution.py:417
  29.7 9.2 %collective-permute-start.6 = (f32[8,256]{1,0:T(8,128)S(1)}, f32[8,256]{1,0:T(8,128)S(1)}, u32[]{:S(2)}, u32[]{:S(2)}) collective-permute-start(f32[8,256]{1,0:T(8,128)S(1)} %pad_maximum_fusion.1.rate_near_ref), channel_id=1, source_target_pairs={{0,8},{4,12},{8,0},{12,4},{1,9},{5,13},{9,1},{13,5},{2,10},{6,14},... | collective-permute-start | bytes 24584 | tf_op jit(solution)/shard_map/ppermute | solution.py:417
  31.5 2.8 %copy-start.2 = (bf16[1024,3,1024]{2,0,1:T(8,128)(2,1)S(1)}, bf16[1024,3,1024]{2,0,1:T(8,128)(2,1)}, u32[]{:S(2)}) copy-start(bf16[1024,3,1024]{2,0,1:T(8,128)(2,1)} %param.9) | copy-start | bytes 18874372
  38.9 5.6 %copy-start.3 = (bf16[1024,1024]{1,0:T(8,128)(2,1)S(1)}, bf16[1024,1024]{1,0:T(8,128)(2,1)}, u32[]{:S(2)}) copy-start(bf16[1024,1024]{1,0:T(8,128)(2,1)} %own_w.1) | copy-start | bytes 6291460
  38.9 2.2 %collective-permute-start.8 = (bf16[256,1024]{1,0:T(8,128)(2,1)}, bf16[256,1024]{1,0:T(8,128)(2,1)S(1)}, u32[]{:S(2)}, u32[]{:S(2)}) collective-permute-start(bf16[256,1024]{1,0:T(8,128)(2,1)} %collective-permute-done.3.refs_1_.refs_3_), channel_id=1, source_target_pairs={{0,4},{4,0},{8,12},{12,8},{1,5},{5,1},{9,13},{13,9},{2,6},{6,2},{1... | collective-permute-start | bytes 1572872 | tf_op jit(solution)/shard_map/ppermute | solution.py:417
  44.5 5.7 %collective-permute-start.9 = (bf16[1024,1024]{1,0:T(8,128)(2,1)S(1)}, bf16[1024,1024]{1,0:T(8,128)(2,1)S(1)}, u32[]{:S(2)}, u32[]{:S(2)}) collective-permute-start(bf16[1024,1024]{1,0:T(8,128)(2,1)S(1)} %copy-done.3), channel_id=1, source_target_pairs={{0,4},{4,0},{8,12},{12,8},{1,5},{5,1},{9,13},{13,9},{2,6},{6,2},{1... | collective-permute-start | bytes 6291464 | tf_op jit(solution)/shard_map/ppermute | solution.py:417
  44.7 14.2 %collective-permute-start.10 = (bf16[2,512,256]{2,1,0:T(8,128)(2,1)S(1)}, bf16[2,512,256]{2,1,0:T(8,128)(2,1)S(1)}, u32[]{:S(2)}, u32[]{:S(2)}) collective-permute-start(bf16[2,512,256]{2,1,0:T(8,128)(2,1)S(1)} %shard_map.84), channel_id=1, source_target_pairs={{0,8},{4,12},{8,0},{12,4},{1,9},{5,13},{9,1},{13,5},{2,10},{6,14},... | collective-permute-start | bytes 1572872 | tf_op jit(solution)/shard_map/ppermute | solution.py:417
  50.2 10.2 %copy-start.4 = (bf16[4,256,512]{2,1,0:T(8,128)(2,1)S(1)}, bf16[4,256,512]{2,1,0:T(8,128)(2,1)}, u32[]{:S(2)}) copy-start(bf16[4,256,512]{2,1,0:T(8,128)(2,1)} %gate_ref.1) | copy-start | bytes 3145732
  50.2 10.2 %copy-start.5 = (bf16[4,256,512]{2,1,0:T(8,128)(2,1)S(1)}, bf16[4,256,512]{2,1,0:T(8,128)(2,1)}, u32[]{:S(2)}) copy-start(bf16[4,256,512]{2,1,0:T(8,128)(2,1)} %up_ref.1) | copy-start | bytes 3145732
  50.2 10.2 %copy-start.6 = (bf16[4,256,512]{2,1,0:T(8,128)(2,1)S(1)}, bf16[4,256,512]{2,1,0:T(8,128)(2,1)}, u32[]{:S(2)}) copy-start(bf16[4,256,512]{2,1,0:T(8,128)(2,1)} %down_ref.1) | copy-start | bytes 3145732
  54.7 20.0 %copy-start.7 = (f32[1024]{0:T(1024)S(1)}, f32[1024]{0:T(1024)}, u32[]{:S(2)}) copy-start(f32[1024]{0:T(1024)} %param.14) | copy-start | bytes 12292
  58.9 15.7 %collective-permute-start.11 = (bf16[1,1024,256]{2,1,0:T(8,128)(2,1)S(1)}, bf16[1,1024,256]{2,1,0:T(8,128)(2,1)S(1)}, u32[]{:S(2)}, u32[]{:S(2)}) collective-permute-start(bf16[1,1024,256]{2,1,0:T(8,128)(2,1)S(1)} %shard_map.85), channel_id=1, source_target_pairs={{0,8},{4,12},{8,0},{12,4},{1,9},{5,13},{9,1},{13,5},{2,10},{6,14},... | collective-permute-start | bytes 1572872 | tf_op jit(solution)/shard_map/ppermute | solution.py:417
  76.7 2.0 %collective-permute-start.12 = (bf16[256,256]{1,0:T(8,128)(2,1)S(1)}, bf16[256,256]{1,0:T(8,128)(2,1)S(1)}, u32[]{:S(2)}, u32[]{:S(2)}) collective-permute-start(bf16[256,256]{1,0:T(8,128)(2,1)S(1)} %get-tuple-element.48), channel_id=1, source_target_pairs={{0,4},{4,0},{8,12},{12,8},{1,5},{5,1},{9,13},{13,9},{2,6},{6,2},{1... | collective-permute-start | bytes 393224 | tf_op jit(solution)/shard_map/ppermute | solution.py:417
  76.7 7.8 %collective-permute-start.14 = (bf16[256,256]{1,0:T(8,128)(2,1)S(1)}, bf16[256,256]{1,0:T(8,128)(2,1)S(1)}, u32[]{:S(2)}, u32[]{:S(2)}) collective-permute-start(bf16[256,256]{1,0:T(8,128)(2,1)S(1)} %get-tuple-element.49), channel_id=1, source_target_pairs={{0,8},{4,12},{8,0},{12,4},{1,9},{5,13},{9,1},{13,5},{2,10},{6,14},... | collective-permute-start | bytes 393224 | tf_op jit(solution)/shard_map/ppermute | solution.py:417
  77.3 7.7 %collective-permute-start.15 = (bf16[256,256]{1,0:T(8,128)(2,1)S(1)}, bf16[256,256]{1,0:T(8,128)(2,1)S(1)}, u32[]{:S(2)}, u32[]{:S(2)}) collective-permute-start(bf16[256,256]{1,0:T(8,128)(2,1)S(1)} %get-tuple-element.50), channel_id=1, source_target_pairs={{0,12},{4,8},{8,4},{12,0},{1,13},{5,9},{9,5},{13,1},{2,14},{6,10},... | collective-permute-start | bytes 393224 | tf_op jit(solution)/shard_map/ppermute | solution.py:417
  78.7 12.8 %collective-permute-start.19 = (bf16[256,512]{1,0:T(8,128)(2,1)S(1)}, bf16[256,512]{1,0:T(8,128)(2,1)S(1)}, u32[]{:S(2)}, u32[]{:S(2)}) collective-permute-start(bf16[256,512]{1,0:T(8,128)(2,1)S(1)} %constant_dynamic-update-slice_fusion), channel_id=1, source_target_pairs={{1,0},{2,1},{3,2},{5,4},{6,5},{7,6},{9,8},{10,9},{11,10},{13,12},{... | collective-permute-start | bytes 786440 | tf_op jit(solution)/shard_map/ppermute | solution.py:420
  80.0 11.6 %collective-permute-start.13 = (bf16[256,512]{1,0:T(8,128)(2,1)S(1)}, bf16[256,512]{1,0:T(8,128)(2,1)S(1)}, u32[]{:S(2)}, u32[]{:S(2)}) collective-permute-start(bf16[256,512]{1,0:T(8,128)(2,1)S(1)} %constant_dynamic-update-slice_fusion), channel_id=1, source_target_pairs={{0,1},{1,2},{2,3},{4,5},{5,6},{6,7},{8,9},{9,10},{10,11},{12,13},{... | collective-permute-start | bytes 786440 | tf_op jit(solution)/shard_map/ppermute | solution.py:420
  85.0 10.7 %collective-permute-start.20 = (bf16[256,512]{1,0:T(8,128)(2,1)S(1)}, bf16[256,512]{1,0:T(8,128)(2,1)S(1)}, u32[]{:S(2)}, u32[]{:S(2)}) collective-permute-start(bf16[256,512]{1,0:T(8,128)(2,1)S(1)} %constant_dynamic-update-slice_fusion.2), channel_id=1, source_target_pairs={{1,0},{2,1},{3,2},{5,4},{6,5},{7,6},{9,8},{10,9},{11,10},{13,12},{... | collective-permute-start | bytes 786440 | tf_op jit(solution)/shard_map/ppermute | solution.py:420
  86.3 14.8 %collective-permute-start.23 = (bf16[256,1024]{1,0:T(8,128)(2,1)S(1)}, bf16[256,1024]{1,0:T(8,128)(2,1)S(1)}, u32[]{:S(2)}, u32[]{:S(2)}) collective-permute-start(bf16[256,1024]{1,0:T(8,128)(2,1)S(1)} %get-tuple-element.51), channel_id=1, source_target_pairs={{0,8},{4,12},{8,0},{12,4},{1,9},{5,13},{9,1},{13,5},{2,10},{6,14},... | collective-permute-start | bytes 1572872 | tf_op jit(solution)/shard_map/ppermute | solution.py:417
  86.9 10.3 %collective-permute-start.16 = (bf16[256,512]{1,0:T(8,128)(2,1)S(1)}, bf16[256,512]{1,0:T(8,128)(2,1)S(1)}, u32[]{:S(2)}, u32[]{:S(2)}) collective-permute-start(bf16[256,512]{1,0:T(8,128)(2,1)S(1)} %constant_dynamic-update-slice_fusion.2), channel_id=1, source_target_pairs={{0,1},{1,2},{2,3},{4,5},{5,6},{6,7},{8,9},{9,10},{10,11},{12,13},{... | collective-permute-start | bytes 786440 | tf_op jit(solution)/shard_map/ppermute | solution.py:420
  95.7 15.5 %collective-permute-start.21 = (bf16[256,1024]{1,0:T(8,128)(2,1)S(1)}, bf16[256,1024]{1,0:T(8,128)(2,1)S(1)}, u32[]{:S(2)}, u32[]{:S(2)}) collective-permute-start(bf16[256,1024]{1,0:T(8,128)(2,1)S(1)} %constant_dynamic-update-slice_fusion.6.above_1), channel_id=1, source_target_pairs={{1,0},{2,1},{5,4},{6,5},{9,8},{10,9},{13,12},{14,13},{17,16},{18,1... | collective-permute-start | bytes 1572872 | tf_op jit(solution)/shard_map/ppermute | solution.py:420
  97.2 14.0 %collective-permute-start.17 = (bf16[256,1024]{1,0:T(8,128)(2,1)S(1)}, bf16[256,1024]{1,0:T(8,128)(2,1)S(1)}, u32[]{:S(2)}, u32[]{:S(2)}) collective-permute-start(bf16[256,1024]{1,0:T(8,128)(2,1)S(1)} %constant_dynamic-update-slice_fusion.4.below_1), channel_id=1, source_target_pairs={{1,2},{2,3},{5,6},{6,7},{9,10},{10,11},{13,14},{14,15},{17,18},{18... | collective-permute-start | bytes 1572872 | tf_op jit(solution)/shard_map/ppermute | solution.py:420
  97.9 14.1 %collective-permute-start.27 = (bf16[256,1024]{1,0:T(8,128)(2,1)S(1)}, bf16[256,1024]{1,0:T(8,128)(2,1)S(1)}, u32[]{:S(2)}, u32[]{:S(2)}) collective-permute-start(bf16[256,1024]{1,0:T(8,128)(2,1)S(1)} %get-tuple-element.57), channel_id=1, source_target_pairs={{0,8},{4,12},{8,0},{12,4},{1,9},{5,13},{9,1},{13,5},{2,10},{6,14},... | collective-permute-start | bytes 1572872 | tf_op jit(solution)/shard_map/ppermute | solution.py:417
  101.1 13.3 %collective-permute-start.24 = (bf16[256,1024]{1,0:T(8,128)(2,1)S(1)}, bf16[256,1024]{1,0:T(8,128)(2,1)S(1)}, u32[]{:S(2)}, u32[]{:S(2)}) collective-permute-start(bf16[256,1024]{1,0:T(8,128)(2,1)S(1)} %collective-permute-done.23.one), channel_id=1, source_target_pairs={{0,16},{16,0},{1,17},{17,1},{2,18},{18,2},{3,19},{19,3},{4,20},{20... | collective-permute-start | bytes 1572872 | tf_op jit(solution)/shard_map/ppermute | solution.py:474
  112.0 6.0 %collective-permute-start.25 = (bf16[256,1024]{1,0:T(8,128)(2,1)S(1)}, bf16[256,1024]{1,0:T(8,128)(2,1)S(1)}, u32[]{:S(2)}, u32[]{:S(2)}) collective-permute-start(bf16[256,1024]{1,0:T(8,128)(2,1)S(1)} %collective-permute-done.23.one), channel_id=1, source_target_pairs={{0,4},{4,0},{8,12},{12,8},{1,5},{5,1},{9,13},{13,9},{2,6},{6,2},{1... | collective-permute-start | bytes 1572872 | tf_op jit(solution)/shard_map/ppermute | solution.py:417
  114.4 3.6 %collective-permute-start.26 = (bf16[256,1024]{1,0:T(8,128)(2,1)S(1)}, bf16[256,1024]{1,0:T(8,128)(2,1)S(1)}, u32[]{:S(2)}, u32[]{:S(2)}) collective-permute-start(bf16[256,1024]{1,0:T(8,128)(2,1)S(1)} %collective-permute-done.24.other), channel_id=1, source_target_pairs={{0,4},{4,0},{8,12},{12,8},{1,5},{5,1},{9,13},{13,9},{2,6},{6,2},{1... | collective-permute-start | bytes 1572872 | tf_op jit(solution)/shard_map/ppermute | solution.py:417
  114.4 14.3 %collective-permute-start.28 = (bf16[256,1024]{1,0:T(8,128)(2,1)S(1)}, bf16[256,1024]{1,0:T(8,128)(2,1)S(1)}, u32[]{:S(2)}, u32[]{:S(2)}) collective-permute-start(bf16[256,1024]{1,0:T(8,128)(2,1)S(1)} %collective-permute-done.27.one), channel_id=1, source_target_pairs={{0,16},{16,0},{1,17},{17,1},{2,18},{18,2},{3,19},{19,3},{4,20},{20... | collective-permute-start | bytes 1572872 | tf_op jit(solution)/shard_map/ppermute | solution.py:474
  116.0 16.5 %collective-permute-start.22 = (bf16[256,1024]{1,0:T(8,128)(2,1)S(1)}, bf16[256,1024]{1,0:T(8,128)(2,1)S(1)}, u32[]{:S(2)}, u32[]{:S(2)}) collective-permute-start(bf16[256,1024]{1,0:T(8,128)(2,1)S(1)} %collective-permute-done.21.above_2), channel_id=1, source_target_pairs={{1,0},{5,4},{9,8},{13,12},{17,16},{21,20},{25,24},{29,28}} | collective-permute-start | bytes 1572872 | tf_op jit(solution)/shard_map/ppermute | solution.py:420
  117.3 15.2 %collective-permute-start.18 = (bf16[256,1024]{1,0:T(8,128)(2,1)S(1)}, bf16[256,1024]{1,0:T(8,128)(2,1)S(1)}, u32[]{:S(2)}, u32[]{:S(2)}) collective-permute-start(bf16[256,1024]{1,0:T(8,128)(2,1)S(1)} %collective-permute-done.17.below_2), channel_id=1, source_target_pairs={{2,3},{6,7},{10,11},{14,15},{18,19},{22,23},{26,27},{30,31}} | collective-permute-start | bytes 1572872 | tf_op jit(solution)/shard_map/ppermute | solution.py:420
  128.8 3.8 %collective-permute-start.29 = (bf16[256,1024]{1,0:T(8,128)(2,1)S(1)}, bf16[256,1024]{1,0:T(8,128)(2,1)S(1)}, u32[]{:S(2)}, u32[]{:S(2)}) collective-permute-start(bf16[256,1024]{1,0:T(8,128)(2,1)S(1)} %collective-permute-done.27.one), channel_id=1, source_target_pairs={{0,4},{4,0},{8,12},{12,8},{1,5},{5,1},{9,13},{13,9},{2,6},{6,2},{1... | collective-permute-start | bytes 1572872 | tf_op jit(solution)/shard_map/ppermute | solution.py:417
  128.8 3.8 %collective-permute-start.30 = (bf16[256,1024]{1,0:T(8,128)(2,1)S(1)}, bf16[256,1024]{1,0:T(8,128)(2,1)S(1)}, u32[]{:S(2)}, u32[]{:S(2)}) collective-permute-start(bf16[256,1024]{1,0:T(8,128)(2,1)S(1)} %collective-permute-done.28.other), channel_id=1, source_target_pairs={{0,4},{4,0},{8,12},{12,8},{1,5},{5,1},{9,13},{13,9},{2,6},{6,2},{1... | collective-permute-start | bytes 1572872 | tf_op jit(solution)/shard_map/ppermute | solution.py:417

commit v11 on v10

--- a/solution.py
+++ b/solution.py
@@ -167,18 +167,20 @@
     return high, (value - high.astype(F32)).astype(BF16)
 
 
-def update_kernel(index_ref, local_near_ref, local_far_ref, near_ref, far_ref, rate_near_ref,
+def update_kernel(index_ref, local_near_ref, local_far_ref, near_own_ref, near_ref, far_ref, rate_near_ref,
                   rate_far_ref, gate_ref, up_ref, down_ref,
                   gate_out, up_out, down_out, current):
     gate_w, up_w, down_w = gate_ref[0], up_ref[0], down_ref[0]
-    rows = near_ref.shape[1] // 2
+    rows = near_ref.shape[1]
     sums = [None] * 3
     for block in range(4):
-        local_ref, other = (local_near_ref, near_ref) if block < 2 else (local_far_ref, far_ref)
+        local_ref = local_near_ref if block < 2 else local_far_ref
+        other = (near_own_ref, near_ref, far_ref, far_ref)[block]
         here = pl.ds((block % 2) * rows, rows)
-        keys = local_ref[0, here, :] + other[0, here, :].astype(F32)
+        there = here if block >= 2 else pl.ds(0, rows)
+        keys = local_ref[0, here, :] + other[0, there, :].astype(F32)
         keys = rms_scale(keys).astype(BF16)
-        values = (local_ref[1, here, :] + other[1, here, :].astype(F32)).astype(BF16)
+        values = (local_ref[1, here, :] + other[1, there, :].astype(F32)).astype(BF16)
         rate_ref = rate_near_ref if block < 2 else rate_far_ref
         rate = jnp.broadcast_to(rate_ref[pl.ds((block % 2) * 4 + index_ref[HEAD], 1), :], (8, rows)).T[:, :1]
         scaled = (rate * values.astype(F32)).astype(BF16)
@@ -217,9 +219,9 @@
     down_out[...] = (down_w.astype(F32) + current[2]).astype(BF16)
 
 
-def update(index, local_near, local_far, near, far, rates_near, rates_far, fast_gate, fast_up, fast_down):
+def update(index, local_near, local_far, near_own, near, far, rates_near, rates_far, fast_gate, fast_up, fast_down):
     size, hidden = fast_gate.shape[1:]
-    total = 2 * near.shape[1]
+    total = 4 * near.shape[1]
 
     def whole(array):
         zeros = (0,) * array.ndim
@@ -234,8 +236,9 @@
             num_scalar_prefetch=1,
             grid=(1,),
             in_specs=[
-                pl.BlockSpec(near.shape, lambda i, idx: (0, 0, 0)),
                 pl.BlockSpec(far.shape, lambda i, idx: (0, 0, 0)),
+                pl.BlockSpec(far.shape, lambda i, idx: (0, 0, 0)),
+                whole(near_own),
                 whole(near),
                 whole(far),
                 whole(rates_near),
@@ -249,7 +252,7 @@
         ),
         compiler_params=params(),
         cost_estimate=pl.CostEstimate(flops=1, bytes_accessed=1, transcendentals=0),
-    )(index, local_near, local_far, near, far, rates_near, rates_far, fast_gate, fast_up, fast_down)
+    )(index, local_near, local_far, near_own, near, far, rates_near, rates_far, fast_gate, fast_up, fast_down)
 
 
 def read_kernel(index_ref, local_near_ref, local_far_ref, other_ref, gain_ref, gate_ref, up_ref, down_ref, *out_refs):
@@ -449,17 +452,19 @@
 
     handed = after(handed, local_near, got_far, rates_far, out_first, out_later)
     far = [(direct, handed), (direct_peer, across(handed, 1))]
-    send_far = project(index, [], far, weight, given, size, False, 1, 2, BF16)
+    send_far_own = project(index, [], far[:1], weight, given, size, False, 1, 2, BF16)
+    got_near_own = across(send_far_own, 2)
+    send_far = project(index, [], far[1:], weight, after(given, send_far_own), size, False, 1, 2, BF16)
     got_near = across(send_far, 2)
     send_query = project(index, near, far, weight, after(given, send_far), size, False, 0, 1, BF16)
-    out_peer = across(after(out_weight, send_far), 1)
+    out_peer = across(after(out_weight, send_far, got_near_own), 1)
     held = after(given, send_query, out_peer)
     local_far = project(index, [], far, weight, held, size, True, 1, 3, F32)
     send_query = after(send_query, got_near, local_far)
     got_query = across(send_query, 2)
 
     rates = (rates_near, rates_far)
-    fresh = update(index, local_near, local_far, got_near, got_far, *rates, fast_gate, fast_up, fast_down)
+    fresh = update(index, local_near, local_far, got_near_own, got_near, got_far, *rates, fast_gate, fast_up, fast_down)
     normed = read_out(index, local_near, local_far, got_query, out_gain.reshape(4, 1, size), *fresh)
     mine = jnp.concatenate([normed[0], across(normed[1], 1)], axis=1)
     theirs = jnp.concatenate([across(normed[2], 2), across(normed[3], 3)], axis=1)

time: 136 us -> 137 us (level)
    pallas_call x5 -> x6, Pallas kernels: 20.7 us -> 22 us  [project(): pl.pallas_call(functools.partial(project_kernel, len(whole), len(pairs)),...]
    ppermute x20 -> x21, waiting for transfers between devices: 15.3 us -> 14.1 us  [across(): return lax.ppermute(array, 'seq', [(i, i ^ bit) for i in range(4)])]
    ppermute x20 -> x21, starting transfers between devices: 13.9 us -> 14.4 us  [across(): return lax.ppermute(array, 'seq', [(i, i ^ bit) for i in range(4)])]
  transfers between devices with their start and end apart: 31 -> 32, of which waited for: 13 -> 12; matrix products, arithmetic and copies ran while one was open for 3% -> 3% of each run, Pallas kernels for 27% -> 30%
where the time goes in v11:
time: 137 us
  Pallas kernels  46 us (34%)
  waiting for transfers between devices  39.4 us (29%)
  starting transfers between devices  36 us (26%)
  local copies, waits for them, and re-layouts  12.7 us (9%)
  matrix products  2.25 us (2%)
    pallas_call x6, Pallas kernels, project(): pl.pallas_call(functools.partial(project_kernel, len(whole), len(pairs)),...  22 us
    ppermute x9, starting transfers between devices, hop(): return lax.ppermute(array, 'head', links)  18.6 us
    ppermute x9, waiting for transfers between devices, hop(): return lax.ppermute(array, 'head', links)  16.8 us
    ppermute x21, starting transfers between devices, across(): return lax.ppermute(array, 'seq', [(i, i ^ bit) for i in range(4)])  14.4 us
    pallas_call x1, Pallas kernels, update(): pl.pallas_call(update_kernel, out_shape=[out] * 3, grid_spec=pltpu.Prefet...  14.2 us
    ppermute x21, waiting for transfers between devices, across(): return lax.ppermute(array, 'seq', [(i, i ^ bit) for i in range(4)])  14.1 us
    ppermute x2, waiting for transfers between devices, swap_groups(): return lax.ppermute(array, 'groups', [(0, 1), (1, 0)])  8.4 us
    unnamed x20, local copies, waits for them, and re-layouts  5.67 us
  transfers between devices with their start and end apart: 32, of which 12 were waited for; matrix products, arithmetic and copies ran while one was open for 3% of the time, Pallas kernels for 30%

profile of v11, /device:TPU:0, one launch (start us, length us, event | category | flops | bytes accessed | tf_op | source)
XLA Modules:
  0.0 136.7 jit_solution(11473043933763649501)
XLA Ops:
  0.0 1.9 %constant_dynamic-slice_fusion.2 = bf16[256,1024]{1,0:T(8,128)(2,1)} fusion(bf16[256,4096]{1,0:T(8,128)(2,1)} %refs_0_.5, s32[]{:T(128)S(6)} %select_n.23), kind=kLoop, calls=%fused_computation.15 | loop fusion | bytes 1048580 | tf_op jit(solution)/shard_map/dynamic_slice | solution.py:432
  1.9 3.7 %dynamic-slice_bitcast_fusion = bf16[3,1024,512]{2,1,0:T(8,128)(2,1)} fusion(bf16[1024,3,1024]{2,0,1:T(8,128)(2,1)} %param.9, s32[]{:T(128)S(6)} %select_n.24), kind=kLoop, calls=%fused_computation | loop fusion | bytes 6291460 | tf_op jit(solution)/shard_map/dynamic_slice | solution.py:436
  5.6 0.5 collective-permute-start.1
  6.1 0.1 collective-permute-start
  6.1 2.9 %collective-permute-start.2 = (bf16[256,1024]{1,0:T(8,128)(2,1)}, bf16[256,1024]{1,0:T(8,128)(2,1)}, u32[]{:S(2)}, u32[]{:S(2)}) collective-permute-start(bf16[256,1024]{1,0:T(8,128)(2,1)} %constant_dynamic-slice_fusion.2), channel_id=1, source_target_pairs={{0,8},{4,12},{8,0},{12,4},{1,9},{5,13},{9,1},{13,5},{2,10},{6,14},... | collective-permute-start | bytes 1572872 | tf_op jit(solution)/shard_map/ppermute | solution.py:420
  9.1 0.1 stack.63.index_ref
  9.2 5.5 %collective-permute-done.refs_1_ = bf16[256,4096]{1,0:T(8,128)(2,1)} collective-permute-done((bf16[256,4096]{1,0:T(8,128)(2,1)}, bf16[256,4096]{1,0:T(8,128)(2,1)}, u32[]{:S(2)}, u32[]{:S(2)}) %collective-permute-start) | collective-permute-done | bytes 2097184 | tf_op jit(solution)/shard_map/ppermute | solution.py:420
  14.6 2.8 %copy-done.1 = bf16[1024,3,1024]{2,0,1:T(8,128)(2,1)S(1)} copy-done((bf16[1024,3,1024]{2,0,1:T(8,128)(2,1)S(1)}, bf16[1024,3,1024]{2,0,1:T(8,128)(2,1)}, u32[]{:S(2)}) %copy-start.1) | copy-done | bytes 6291480
  17.4 4.4 %shard_map.82 = bf16[2,512,256]{2,1,0:T(8,128)(2,1)} custom-call(s32[15]{0:T(128)S(1)} %stack.63.index_ref, bf16[256,4096]{1,0:T(8,128)(2,1)} %refs_0_.5, bf16[256,4096]{1,0:T(8,128)(2,1)} %collective-permute-done.refs_1_, bf16[3,1024,1024]{2,1,0:T(8,128)(2,1)S(1)} %bitcast.25, bf16[3,1024,512]{2,1,0:T(8,128)(2,1)S(1)} %collective-permute-done.1.refs_3_.refs_7_.refs_5_), custom_call_target="tpu_custom_call" | custom-call | flops 1 | bytes 1 | tf_op jit(solution)/shard_map/pallas_call | solution.py:146
  21.8 2.9 %collective-permute-start.3 = (bf16[256,1024]{1,0:T(8,128)(2,1)}, bf16[256,1024]{1,0:T(8,128)(2,1)}, u32[]{:S(2)}, u32[]{:S(2)}) collective-permute-start(bf16[256,1024]{1,0:T(8,128)(2,1)} %collective-permute-done.2.refs_0_.refs_2_), channel_id=1, source_target_pairs={{0,1},{1,0},{2,3},{3,2},{4,5},{5,4},{6,7},{7,6},{8,9},{9,8},{10,11... | collective-permute-start | bytes 1572872 | tf_op jit(solution)/shard_map/ppermute | solution.py:423
  24.7 1.5 %collective-permute-start.4 = (bf16[2,512,256]{2,1,0:T(8,128)(2,1)}, bf16[2,512,256]{2,1,0:T(8,128)(2,1)}, u32[]{:S(2)}, u32[]{:S(2)}) collective-permute-start(bf16[2,512,256]{2,1,0:T(8,128)(2,1)} %shard_map.82), channel_id=1, source_target_pairs={{0,8},{4,12},{8,0},{12,4},{1,9},{5,13},{9,1},{13,5},{2,10},{6,14},... | collective-permute-start | bytes 1572872 | tf_op jit(solution)/shard_map/ppermute | solution.py:420
  26.2 2.3 %compare_select_fusion = f32[4,256]{1,0:T(4,128)S(1)} fusion(bf16[256,4096]{1,0:T(8,128)(2,1)} %refs_0_.5, bf16[4096,4]{0,1:T(4,128)(2,1)S(1)} %copy-done), kind=kOutput, calls=%fused_computation.11 | convolution fusion | flops 8394752 | bytes 2134016 | tf_op jit(solution)/shard_map/dot_general | solution.py:448
  28.5 0.1 collective-permute-start.5
  28.6 0.5 collective-permute-start.7
  29.1 0.7 collective-permute-done.5
  29.7 0.5 collective-permute-start.6
  30.3 1.3 constant_dynamic-slice_fusion.1
  31.5 0.0 copy-start.2
  31.5 2.8 %copy-done.2 = bf16[1024,3,1024]{2,0,1:T(8,128)(2,1)S(1)} copy-done((bf16[1024,3,1024]{2,0,1:T(8,128)(2,1)S(1)}, bf16[1024,3,1024]{2,0,1:T(8,128)(2,1)}, u32[]{:S(2)}) %copy-start.2) | copy-done | bytes 6291480
  34.3 4.6 %shard_map.83.local_near_ref = f32[3,512,256]{2,1,0:T(8,128)S(1)} custom-call(s32[15]{0:T(128)S(1)} %stack.63.index_ref, bf16[256,4096]{1,0:T(8,128)(2,1)} %refs_0_.5, bf16[256,4096]{1,0:T(8,128)(2,1)} %collective-permute-done.refs_1_, bf16[3,1024,1024]{2,1,0:T(8,128)(2,1)S(1)} %bitcast.26, ...), custom_call_target="tpu_custom_call" | custom-call | flops 1 | bytes 1 | tf_op jit(solution)/shard_map/pallas_call | solution.py:146
  38.9 0.1 collective-permute-start.8
  39.0 2.8 %shard_map.84 = bf16[2,256,256]{2,1,0:T(8,128)(2,1)S(1)} custom-call(s32[15]{0:T(128)S(1)} %stack.63.index_ref, bf16[256,1024]{1,0:T(8,128)(2,1)} %collective-permute-done.2.refs_0_.refs_2_, bf16[256,1024]{1,0:T(8,128)(2,1)} %collective-permute-done.3.refs_1_.refs_3_, bf16[3,1024,1024]{2,1,0:T(8,128)(2,1)S(1)} %bitcast.27, ...), custom_call_target="tpu_custom_call" | custom-call | flops 1 | bytes 1 | tf_op jit(solution)/shard_map/pallas_call | solution.py:146
  41.8 0.0 copy-start.3
  41.8 1.6 %collective-permute-start.9 = (bf16[2,256,256]{2,1,0:T(8,128)(2,1)S(1)}, bf16[2,256,256]{2,1,0:T(8,128)(2,1)S(1)}, u32[]{:S(2)}, u32[]{:S(2)}) collective-permute-start(bf16[2,256,256]{2,1,0:T(8,128)(2,1)S(1)} %shard_map.84), channel_id=1, source_target_pairs={{0,8},{4,12},{8,0},{12,4},{1,9},{5,13},{9,1},{13,5},{2,10},{6,14},... | collective-permute-start | bytes 786440 | tf_op jit(solution)/shard_map/ppermute | solution.py:420
  43.4 1.8 %shard_map.85 = bf16[2,256,256]{2,1,0:T(8,128)(2,1)S(1)} custom-call(s32[15]{0:T(128)S(1)} %stack.63.index_ref, bf16[256,1024]{1,0:T(8,128)(2,1)S(1)} %collective-permute-done.7.refs_0_.refs_4_.refs_2_, bf16[256,1024]{1,0:T(8,128)(2,1)S(1)} %collective-permute-done.8.refs_1_.refs_5_.refs_3_, bf16[3,1024,1024]{2,1,0:T(8,128)(2,1)S(1)} %bitcast.28, ...), custom_call_target="tpu_custom_call" | custom-call | flops 1 | bytes 1 | tf_op jit(solution)/shard_map/pallas_call | solution.py:146
  45.2 5.4 %collective-permute-done.9.near_own_ref = bf16[2,256,256]{2,1,0:T(8,128)(2,1)S(1)} collective-permute-done((bf16[2,256,256]{2,1,0:T(8,128)(2,1)S(1)}, bf16[2,256,256]{2,1,0:T(8,128)(2,1)S(1)}, u32[]{:S(2)}, u32[]{:S(2)}) %collective-permute-start.9) | collective-permute-done | bytes 262176 | tf_op jit(solution)/shard_map/ppermute | solution.py:420
  50.6 1.5 %collective-permute-start.11 = (bf16[2,256,256]{2,1,0:T(8,128)(2,1)S(1)}, bf16[2,256,256]{2,1,0:T(8,128)(2,1)S(1)}, u32[]{:S(2)}, u32[]{:S(2)}) collective-permute-start(bf16[2,256,256]{2,1,0:T(8,128)(2,1)S(1)} %shard_map.85), channel_id=1, source_target_pairs={{0,8},{4,12},{8,0},{12,4},{1,9},{5,13},{9,1},{13,5},{2,10},{6,14},... | collective-permute-start | bytes 786440 | tf_op jit(solution)/shard_map/ppermute | solution.py:420
  52.1 3.9 %shard_map.86 = bf16[1,1024,256]{2,1,0:T(8,128)(2,1)S(1)} custom-call(s32[15]{0:T(128)S(1)} %stack.63.index_ref, bf16[256,4096]{1,0:T(8,128)(2,1)} %refs_0_.5, bf16[256,4096]{1,0:T(8,128)(2,1)} %collective-permute-done.refs_1_, bf16[256,1024]{1,0:T(8,128)(2,1)} %collective-permute-done.2.refs_0_.refs_2_, ...), custom_call_target="tpu_custom_call" | custom-call | flops 1 | bytes 1 | tf_op jit(solution)/shard_map/pallas_call | solution.py:146
  56.1 0.0 copy-start.4
  56.1 0.0 copy-start.5
  56.1 0.0 copy-start.6
  56.1 4.4 %shard_map.87.local_far_ref = f32[3,512,256]{2,1,0:T(8,128)S(1)} custom-call(s32[15]{0:T(128)S(1)} %stack.63.index_ref, bf16[256,1024]{1,0:T(8,128)(2,1)} %collective-permute-done.2.refs_0_.refs_2_, bf16[256,1024]{1,0:T(8,128)(2,1)} %collective-permute-done.3.refs_1_.refs_3_, bf16[256,1024]{1,0:T(8,128)(2,1)S(1)} %collective-permute-done.7.refs_0_.refs_4_.refs_2_, ...), custom_call_target="tpu_custom_call" | custom-call | flops 1 | bytes 1 | tf_op jit(solution)/shard_map/pallas_call | solution.py:146
  60.6 0.0 copy-start.7
  60.6 0.6 collective-permute-start.12
  61.2 14.2 %shard_map.88 = (bf16[256,512]{1,0:T(8,128)(2,1)S(1)}, bf16[256,512]{1,0:T(8,128)(2,1)S(1)}, bf16[256,512]{1,0:T(8,128)(2,1)S(1)}) custom-call(s32[15]{0:T(128)S(1)} %stack.63.index_ref, f32[3,512,256]{2,1,0:T(8,128)S(1)} %shard_map.83.local_near_ref, f32[3,512,256]{2,1,0:T(8,128)S(1)} %shard_map.87.local_far_ref, ...), custom_call_target="tpu_custom_call" | custom-call | flops 1 | bytes 1 | tf_op jit(solution)/shard_map/pallas_call | solution.py:232
  75.4 2.0 %shard_map.89 = (bf16[256,256]{1,0:T(8,128)(2,1)S(1)}, bf16[256,256]{1,0:T(8,128)(2,1)S(1)}, bf16[256,256]{1,0:T(8,128)(2,1)S(1)}, bf16[256,256]{1,0:T(8,128)(2,1)S(1)}) custom-call(s32[15]{0:T(128)S(1)} %stack.63.index_ref, f32[3,512,256]{2,1,0:T(8,128)S(1)} %shard_map.83.local_near_ref, f32[3,512,256]{2,1,0:T(8,128)S(1)} %shard_map.87.local_far_ref, ...), custom_call_target="tpu_custom_call" | custom-call | flops 1 | bytes 1 | tf_op jit(solution)/shard_map/pallas_call | solution.py:279
  77.4 0.1 collective-permute-start.13
  77.5 1.6 %collective-permute-start.15 = (bf16[256,256]{1,0:T(8,128)(2,1)S(1)}, bf16[256,256]{1,0:T(8,128)(2,1)S(1)}, u32[]{:S(2)}, u32[]{:S(2)}) collective-permute-start(bf16[256,256]{1,0:T(8,128)(2,1)S(1)} %get-tuple-element.51), channel_id=1, source_target_pairs={{0,8},{4,12},{8,0},{12,4},{1,9},{5,13},{9,1},{13,5},{2,10},{6,14},... | collective-permute-start | bytes 393224 | tf_op jit(solution)/shard_map/ppermute | solution.py:420
  79.1 0.3 collective-permute-start.16
  79.4 1.3 collective-permute-start.20
  80.7 4.6 %collective-permute-start.14 = (bf16[256,512]{1,0:T(8,128)(2,1)S(1)}, bf16[256,512]{1,0:T(8,128)(2,1)S(1)}, u32[]{:S(2)}, u32[]{:S(2)}) collective-permute-start(bf16[256,512]{1,0:T(8,128)(2,1)S(1)} %constant_dynamic-update-slice_fusion), channel_id=1, source_target_pairs={{0,1},{1,2},{2,3},{4,5},{5,6},{6,7},{8,9},{9,10},{10,11},{12,13},{... | collective-permute-start | bytes 786440 | tf_op jit(solution)/shard_map/ppermute | solution.py:423
  85.3 0.5 collective-permute-done.16
  85.8 1.3 collective-permute-start.21
  87.1 1.6 %collective-permute-start.24 = (bf16[256,1024]{1,0:T(8,128)(2,1)S(1)}, bf16[256,1024]{1,0:T(8,128)(2,1)S(1)}, u32[]{:S(2)}, u32[]{:S(2)}) collective-permute-start(bf16[256,1024]{1,0:T(8,128)(2,1)S(1)} %get-tuple-element.53), channel_id=1, source_target_pairs={{0,8},{4,12},{8,0},{12,4},{1,9},{5,13},{9,1},{13,5},{2,10},{6,14},... | collective-permute-start | bytes 1572872 | tf_op jit(solution)/shard_map/ppermute | solution.py:420
  88.6 4.5 %collective-permute-start.17 = (bf16[256,512]{1,0:T(8,128)(2,1)S(1)}, bf16[256,512]{1,0:T(8,128)(2,1)S(1)}, u32[]{:S(2)}, u32[]{:S(2)}) collective-permute-start(bf16[256,512]{1,0:T(8,128)(2,1)S(1)} %constant_dynamic-update-slice_fusion.2), channel_id=1, source_target_pairs={{0,1},{1,2},{2,3},{4,5},{5,6},{6,7},{8,9},{9,10},{10,11},{12,13},{... | collective-permute-start | bytes 786440 | tf_op jit(solution)/shard_map/ppermute | solution.py:423
  93.3 3.2 %collective-permute-done.21 = bf16[256,512]{1,0:T(8,128)(2,1)S(1)} collective-permute-done((bf16[256,512]{1,0:T(8,128)(2,1)S(1)}, bf16[256,512]{1,0:T(8,128)(2,1)S(1)}, u32[]{:S(2)}, u32[]{:S(2)}) %collective-permute-start.21) | collective-permute-done | bytes 262176 | tf_op jit(solution)/shard_map/ppermute | solution.py:423
  96.5 1.3 collective-permute-start.22
  97.8 1.1 collective-permute-done.17
  98.9 0.7 collective-permute-start.18
  99.6 0.6 collective-permute-start.28
  100.2 1.3 collective-permute-done.24.one
  101.6 1.5 %collective-permute-start.25 = (bf16[256,1024]{1,0:T(8,128)(2,1)S(1)}, bf16[256,1024]{1,0:T(8,128)(2,1)S(1)}, u32[]{:S(2)}, u32[]{:S(2)}) collective-permute-start(bf16[256,1024]{1,0:T(8,128)(2,1)S(1)} %collective-permute-done.24.one), channel_id=1, source_target_pairs={{0,16},{16,0},{1,17},{17,1},{2,18},{18,2},{3,19},{19,3},{4,20},{20... | collective-permute-start | bytes 1572872 | tf_op jit(solution)/shard_map/ppermute | solution.py:479
  103.1 8.9 %collective-permute-done.22.above_2 = bf16[256,1024]{1,0:T(8,128)(2,1)S(1)} collective-permute-done((bf16[256,1024]{1,0:T(8,128)(2,1)S(1)}, bf16[256,1024]{1,0:T(8,128)(2,1)S(1)}, u32[]{:S(2)}, u32[]{:S(2)}) %collective-permute-start.22) | collective-permute-done | bytes 524320 | tf_op jit(solution)/shard_map/ppermute | solution.py:423
  112.0 0.8 collective-permute-done.28.one
  112.8 2.4 %collective-permute-done.25.other = bf16[256,1024]{1,0:T(8,128)(2,1)S(1)} collective-permute-done((bf16[256,1024]{1,0:T(8,128)(2,1)S(1)}, bf16[256,1024]{1,0:T(8,128)(2,1)S(1)}, u32[]{:S(2)}, u32[]{:S(2)}) %collective-permute-start.25) | collective-permute-done | bytes 524320 | tf_op jit(solution)/shard_map/ppermute | solution.py:479
  115.2 1.5 %collective-permute-start.29 = (bf16[256,1024]{1,0:T(8,128)(2,1)S(1)}, bf16[256,1024]{1,0:T(8,128)(2,1)S(1)}, u32[]{:S(2)}, u32[]{:S(2)}) collective-permute-start(bf16[256,1024]{1,0:T(8,128)(2,1)S(1)} %collective-permute-done.28.one), channel_id=1, source_target_pairs={{0,16},{16,0},{1,17},{17,1},{2,18},{18,2},{3,19},{19,3},{4,20},{20... | collective-permute-start | bytes 1572872 | tf_op jit(solution)/shard_map/ppermute | solution.py:479
  116.7 0.1 pad_maximum_fusion.own
  116.8 1.3 collective-permute-start.23
  118.1 0.7 collective-permute-start.19
  118.8 4.7 %shard_map.90 = (f32[256,1024]{1,0:T(8,128)S(1)}, bf16[256,1024]{1,0:T(8,128)(2,1)S(1)}, bf16[1024,1024]{1,0:T(8,128)(2,1)S(1)}) custom-call(s32[15]{0:T(128)S(1)} %stack.63.index_ref, bf16[256,1024]{1,0:T(8,128)(2,1)S(1)} %pad_maximum_fusion.own, bf16[256,1024]{1,0:T(8,128)(2,1)S(1)} %constant_dynamic-update-slice_fusion.4.below_1, ...), custom_call_target="tpu_custom_call" | custom-call | flops 1 | bytes 1 | tf_op jit(solution)/shard_map/pallas_call | solution.py:346
  123.5 6.0 %collective-permute-done.29.other = bf16[256,1024]{1,0:T(8,128)(2,1)S(1)} collective-permute-done((bf16[256,1024]{1,0:T(8,128)(2,1)S(1)}, bf16[256,1024]{1,0:T(8,128)(2,1)S(1)}, u32[]{:S(2)}, u32[]{:S(2)}) %collective-permute-start.29) | collective-permute-done | bytes 524320 | tf_op jit(solution)/shard_map/ppermute | solution.py:479
  129.5 0.5 collective-permute-start.31
  130.0 3.6 %collective-permute-done.23.above = bf16[256,1024]{1,0:T(8,128)(2,1)S(1)} collective-permute-done((bf16[256,1024]{1,0:T(8,128)(2,1)S(1)}, bf16[256,1024]{1,0:T(8,128)(2,1)S(1)}, u32[]{:S(2)}, u32[]{:S(2)}) %collective-permute-start.23) | collective-permute-done | bytes 524320 | tf_op jit(solution)/shard_map/ppermute | solution.py:423
  133.6 3.1 %shard_map.91 = bf16[256,1024]{1,0:T(8,128)(2,1)} custom-call(s32[15]{0:T(128)S(1)} %stack.63.index_ref, bf16[256,1024]{1,0:T(8,128)(2,1)S(1)} %collective-permute-done.19.below, bf16[256,1024]{1,0:T(8,128)(2,1)S(1)} %collective-permute-done.23.above, bf16[1024,1024]{1,0:T(8,128)(2,1)S(1)} %get-tuple-element.57.weight, ...), custom_call_target="tpu_custom_call" | custom-call | flops 1 | bytes 1 | tf_op jit(solution)/shard_map/pallas_call | solution.py:390
  (41 shorter events, 0.2 us)
Async XLA Ops:
  0.0 26.2 %copy-start = (bf16[4096,4]{0,1:T(4,128)(2,1)S(1)}, bf16[4096,4]{0,1:T(4,128)(2,1)}, u32[]{:S(2)}) copy-start(bf16[4096,4]{0,1:T(4,128)(2,1)} %param.10) | copy-start | bytes 98308
  5.6 9.0 %collective-permute-start.1 = (bf16[3,1024,512]{2,1,0:T(8,128)(2,1)}, bf16[3,1024,512]{2,1,0:T(8,128)(2,1)S(1)}, u32[]{:S(2)}, u32[]{:S(2)}) collective-permute-start(bf16[3,1024,512]{2,1,0:T(8,128)(2,1)} %dynamic-slice_bitcast_fusion), channel_id=1, source_target_pairs={{0,4},{4,0},{8,12},{12,8},{1,5},{5,1},{9,13},{13,9},{2,6},{6,2},{1... | collective-permute-start | bytes 9437192 | tf_op jit(solution)/shard_map/ppermute | solution.py:420
  6.1 8.5 %collective-permute-start = (bf16[256,4096]{1,0:T(8,128)(2,1)}, bf16[256,4096]{1,0:T(8,128)(2,1)}, u32[]{:S(2)}, u32[]{:S(2)}) collective-permute-start(bf16[256,4096]{1,0:T(8,128)(2,1)} %refs_0_.5), channel_id=1, source_target_pairs={{0,4},{4,0},{8,12},{12,8},{1,5},{5,1},{9,13},{13,9},{2,6},{6,2},{1... | collective-permute-start | bytes 6291464 | tf_op jit(solution)/shard_map/ppermute | solution.py:420
  6.1 15.7 %collective-permute-start.2 = (bf16[256,1024]{1,0:T(8,128)(2,1)}, bf16[256,1024]{1,0:T(8,128)(2,1)}, u32[]{:S(2)}, u32[]{:S(2)}) collective-permute-start(bf16[256,1024]{1,0:T(8,128)(2,1)} %constant_dynamic-slice_fusion.2), channel_id=1, source_target_pairs={{0,8},{4,12},{8,0},{12,4},{1,9},{5,13},{9,1},{13,5},{2,10},{6,14},... | collective-permute-start | bytes 1572872 | tf_op jit(solution)/shard_map/ppermute | solution.py:420
  14.6 2.8 %copy-start.1 = (bf16[1024,3,1024]{2,0,1:T(8,128)(2,1)S(1)}, bf16[1024,3,1024]{2,0,1:T(8,128)(2,1)}, u32[]{:S(2)}) copy-start(bf16[1024,3,1024]{2,0,1:T(8,128)(2,1)} %param.9) | copy-start | bytes 18874372
  21.8 17.1 %collective-permute-start.3 = (bf16[256,1024]{1,0:T(8,128)(2,1)}, bf16[256,1024]{1,0:T(8,128)(2,1)}, u32[]{:S(2)}, u32[]{:S(2)}) collective-permute-start(bf16[256,1024]{1,0:T(8,128)(2,1)} %collective-permute-done.2.refs_0_.refs_2_), channel_id=1, source_target_pairs={{0,1},{1,0},{2,3},{3,2},{4,5},{5,4},{6,7},{7,6},{8,9},{9,8},{10,11... | collective-permute-start | bytes 1572872 | tf_op jit(solution)/shard_map/ppermute | solution.py:423
  24.7 14.2 %collective-permute-start.4 = (bf16[2,512,256]{2,1,0:T(8,128)(2,1)}, bf16[2,512,256]{2,1,0:T(8,128)(2,1)}, u32[]{:S(2)}, u32[]{:S(2)}) collective-permute-start(bf16[2,512,256]{2,1,0:T(8,128)(2,1)} %shard_map.82), channel_id=1, source_target_pairs={{0,8},{4,12},{8,0},{12,4},{1,9},{5,13},{9,1},{13,5},{2,10},{6,14},... | collective-permute-start | bytes 1572872 | tf_op jit(solution)/shard_map/ppermute | solution.py:420
  28.5 1.2 collective-permute-start.5
  28.6 14.8 %collective-permute-start.7 = (bf16[256,1024]{1,0:T(8,128)(2,1)}, bf16[256,1024]{1,0:T(8,128)(2,1)S(1)}, u32[]{:S(2)}, u32[]{:S(2)}) collective-permute-start(bf16[256,1024]{1,0:T(8,128)(2,1)} %collective-permute-done.2.refs_0_.refs_2_), channel_id=1, source_target_pairs={{0,4},{4,0},{8,12},{12,8},{1,5},{5,1},{9,13},{13,9},{2,6},{6,2},{1... | collective-permute-start | bytes 1572872 | tf_op jit(solution)/shard_map/ppermute | solution.py:420
  29.7 9.2 %collective-permute-start.6 = (f32[8,256]{1,0:T(8,128)S(1)}, f32[8,256]{1,0:T(8,128)S(1)}, u32[]{:S(2)}, u32[]{:S(2)}) collective-permute-start(f32[8,256]{1,0:T(8,128)S(1)} %pad_maximum_fusion.1.rate_near_ref), channel_id=1, source_target_pairs={{0,8},{4,12},{8,0},{12,4},{1,9},{5,13},{9,1},{13,5},{2,10},{6,14},... | collective-permute-start | bytes 24584 | tf_op jit(solution)/shard_map/ppermute | solution.py:420
  31.5 2.8 %copy-start.2 = (bf16[1024,3,1024]{2,0,1:T(8,128)(2,1)S(1)}, bf16[1024,3,1024]{2,0,1:T(8,128)(2,1)}, u32[]{:S(2)}) copy-start(bf16[1024,3,1024]{2,0,1:T(8,128)(2,1)} %param.9) | copy-start | bytes 18874372
  38.9 4.5 %collective-permute-start.8 = (bf16[256,1024]{1,0:T(8,128)(2,1)}, bf16[256,1024]{1,0:T(8,128)(2,1)S(1)}, u32[]{:S(2)}, u32[]{:S(2)}) collective-permute-start(bf16[256,1024]{1,0:T(8,128)(2,1)} %collective-permute-done.3.refs_1_.refs_3_), channel_id=1, source_target_pairs={{0,4},{4,0},{8,12},{12,8},{1,5},{5,1},{9,13},{13,9},{2,6},{6,2},{1... | collective-permute-start | bytes 1572872 | tf_op jit(solution)/shard_map/ppermute | solution.py:420
  41.8 8.8 %copy-start.3 = (bf16[1024,1024]{1,0:T(8,128)(2,1)S(1)}, bf16[1024,1024]{1,0:T(8,128)(2,1)}, u32[]{:S(2)}) copy-start(bf16[1024,1024]{1,0:T(8,128)(2,1)} %own_w.1) | copy-start | bytes 6291460
  41.8 8.8 %collective-permute-start.9 = (bf16[2,256,256]{2,1,0:T(8,128)(2,1)S(1)}, bf16[2,256,256]{2,1,0:T(8,128)(2,1)S(1)}, u32[]{:S(2)}, u32[]{:S(2)}) collective-permute-start(bf16[2,256,256]{2,1,0:T(8,128)(2,1)S(1)} %shard_map.84), channel_id=1, source_target_pairs={{0,8},{4,12},{8,0},{12,4},{1,9},{5,13},{9,1},{13,5},{2,10},{6,14},... | collective-permute-start | bytes 786440 | tf_op jit(solution)/shard_map/ppermute | solution.py:420
  50.6 5.5 %collective-permute-start.10 = (bf16[1024,1024]{1,0:T(8,128)(2,1)S(1)}, bf16[1024,1024]{1,0:T(8,128)(2,1)S(1)}, u32[]{:S(2)}, u32[]{:S(2)}) collective-permute-start(bf16[1024,1024]{1,0:T(8,128)(2,1)S(1)} %copy-done.3), channel_id=1, source_target_pairs={{0,4},{4,0},{8,12},{12,8},{1,5},{5,1},{9,13},{13,9},{2,6},{6,2},{1... | collective-permute-start | bytes 6291464 | tf_op jit(solution)/shard_map/ppermute | solution.py:420
  50.6 10.0 %collective-permute-start.11 = (bf16[2,256,256]{2,1,0:T(8,128)(2,1)S(1)}, bf16[2,256,256]{2,1,0:T(8,128)(2,1)S(1)}, u32[]{:S(2)}, u32[]{:S(2)}) collective-permute-start(bf16[2,256,256]{2,1,0:T(8,128)(2,1)S(1)} %shard_map.85), channel_id=1, source_target_pairs={{0,8},{4,12},{8,0},{12,4},{1,9},{5,13},{9,1},{13,5},{2,10},{6,14},... | collective-permute-start | bytes 786440 | tf_op jit(solution)/shard_map/ppermute | solution.py:420
  56.1 5.1 %copy-start.4 = (bf16[4,256,512]{2,1,0:T(8,128)(2,1)S(1)}, bf16[4,256,512]{2,1,0:T(8,128)(2,1)}, u32[]{:S(2)}) copy-start(bf16[4,256,512]{2,1,0:T(8,128)(2,1)} %gate_ref.1) | copy-start | bytes 3145732
  56.1 5.1 %copy-start.5 = (bf16[4,256,512]{2,1,0:T(8,128)(2,1)S(1)}, bf16[4,256,512]{2,1,0:T(8,128)(2,1)}, u32[]{:S(2)}) copy-start(bf16[4,256,512]{2,1,0:T(8,128)(2,1)} %up_ref.1) | copy-start | bytes 3145732
  56.1 5.1 %copy-start.6 = (bf16[4,256,512]{2,1,0:T(8,128)(2,1)S(1)}, bf16[4,256,512]{2,1,0:T(8,128)(2,1)}, u32[]{:S(2)}) copy-start(bf16[4,256,512]{2,1,0:T(8,128)(2,1)} %down_ref.1) | copy-start | bytes 3145732
  60.6 14.9 %copy-start.7 = (f32[1024]{0:T(1024)S(1)}, f32[1024]{0:T(1024)}, u32[]{:S(2)}) copy-start(f32[1024]{0:T(1024)} %param.14) | copy-start | bytes 12292
  60.6 14.8 %collective-permute-start.12 = (bf16[1,1024,256]{2,1,0:T(8,128)(2,1)S(1)}, bf16[1,1024,256]{2,1,0:T(8,128)(2,1)S(1)}, u32[]{:S(2)}, u32[]{:S(2)}) collective-permute-start(bf16[1,1024,256]{2,1,0:T(8,128)(2,1)S(1)} %shard_map.86), channel_id=1, source_target_pairs={{0,8},{4,12},{8,0},{12,4},{1,9},{5,13},{9,1},{13,5},{2,10},{6,14},... | collective-permute-start | bytes 1572872 | tf_op jit(solution)/shard_map/ppermute | solution.py:420
  77.4 2.0 %collective-permute-start.13 = (bf16[256,256]{1,0:T(8,128)(2,1)S(1)}, bf16[256,256]{1,0:T(8,128)(2,1)S(1)}, u32[]{:S(2)}, u32[]{:S(2)}) collective-permute-start(bf16[256,256]{1,0:T(8,128)(2,1)S(1)} %get-tuple-element.50), channel_id=1, source_target_pairs={{0,4},{4,0},{8,12},{12,8},{1,5},{5,1},{9,13},{13,9},{2,6},{6,2},{1... | collective-permute-start | bytes 393224 | tf_op jit(solution)/shard_map/ppermute | solution.py:420
  77.5 7.8 %collective-permute-start.15 = (bf16[256,256]{1,0:T(8,128)(2,1)S(1)}, bf16[256,256]{1,0:T(8,128)(2,1)S(1)}, u32[]{:S(2)}, u32[]{:S(2)}) collective-permute-start(bf16[256,256]{1,0:T(8,128)(2,1)S(1)} %get-tuple-element.51), channel_id=1, source_target_pairs={{0,8},{4,12},{8,0},{12,4},{1,9},{5,13},{9,1},{13,5},{2,10},{6,14},... | collective-permute-start | bytes 393224 | tf_op jit(solution)/shard_map/ppermute | solution.py:420
  79.1 6.7 %collective-permute-start.16 = (bf16[256,256]{1,0:T(8,128)(2,1)S(1)}, bf16[256,256]{1,0:T(8,128)(2,1)S(1)}, u32[]{:S(2)}, u32[]{:S(2)}) collective-permute-start(bf16[256,256]{1,0:T(8,128)(2,1)S(1)} %get-tuple-element.52), channel_id=1, source_target_pairs={{0,12},{4,8},{8,4},{12,0},{1,13},{5,9},{9,5},{13,1},{2,14},{6,10},... | collective-permute-start | bytes 393224 | tf_op jit(solution)/shard_map/ppermute | solution.py:420
  79.4 13.8 %collective-permute-start.20 = (bf16[256,512]{1,0:T(8,128)(2,1)S(1)}, bf16[256,512]{1,0:T(8,128)(2,1)S(1)}, u32[]{:S(2)}, u32[]{:S(2)}) collective-permute-start(bf16[256,512]{1,0:T(8,128)(2,1)S(1)} %constant_dynamic-update-slice_fusion), channel_id=1, source_target_pairs={{1,0},{2,1},{3,2},{5,4},{6,5},{7,6},{9,8},{10,9},{11,10},{13,12},{... | collective-permute-start | bytes 786440 | tf_op jit(solution)/shard_map/ppermute | solution.py:423
  80.7 12.5 %collective-permute-start.14 = (bf16[256,512]{1,0:T(8,128)(2,1)S(1)}, bf16[256,512]{1,0:T(8,128)(2,1)S(1)}, u32[]{:S(2)}, u32[]{:S(2)}) collective-permute-start(bf16[256,512]{1,0:T(8,128)(2,1)S(1)} %constant_dynamic-update-slice_fusion), channel_id=1, source_target_pairs={{0,1},{1,2},{2,3},{4,5},{5,6},{6,7},{8,9},{9,10},{10,11},{12,13},{... | collective-permute-start | bytes 786440 | tf_op jit(solution)/shard_map/ppermute | solution.py:423
  85.8 10.7 %collective-permute-start.21 = (bf16[256,512]{1,0:T(8,128)(2,1)S(1)}, bf16[256,512]{1,0:T(8,128)(2,1)S(1)}, u32[]{:S(2)}, u32[]{:S(2)}) collective-permute-start(bf16[256,512]{1,0:T(8,128)(2,1)S(1)} %constant_dynamic-update-slice_fusion.2), channel_id=1, source_target_pairs={{1,0},{2,1},{3,2},{5,4},{6,5},{7,6},{9,8},{10,9},{11,10},{13,12},{... | collective-permute-start | bytes 786440 | tf_op jit(solution)/shard_map/ppermute | solution.py:423
  87.1 14.5 %collective-permute-start.24 = (bf16[256,1024]{1,0:T(8,128)(2,1)S(1)}, bf16[256,1024]{1,0:T(8,128)(2,1)S(1)}, u32[]{:S(2)}, u32[]{:S(2)}) collective-permute-start(bf16[256,1024]{1,0:T(8,128)(2,1)S(1)} %get-tuple-element.53), channel_id=1, source_target_pairs={{0,8},{4,12},{8,0},{12,4},{1,9},{5,13},{9,1},{13,5},{2,10},{6,14},... | collective-permute-start | bytes 1572872 | tf_op jit(solution)/shard_map/ppermute | solution.py:420
  88.6 10.3 %collective-permute-start.17 = (bf16[256,512]{1,0:T(8,128)(2,1)S(1)}, bf16[256,512]{1,0:T(8,128)(2,1)S(1)}, u32[]{:S(2)}, u32[]{:S(2)}) collective-permute-start(bf16[256,512]{1,0:T(8,128)(2,1)S(1)} %constant_dynamic-update-slice_fusion.2), channel_id=1, source_target_pairs={{0,1},{1,2},{2,3},{4,5},{5,6},{6,7},{8,9},{9,10},{10,11},{12,13},{... | collective-permute-start | bytes 786440 | tf_op jit(solution)/shard_map/ppermute | solution.py:423
  96.5 15.5 %collective-permute-start.22 = (bf16[256,1024]{1,0:T(8,128)(2,1)S(1)}, bf16[256,1024]{1,0:T(8,128)(2,1)S(1)}, u32[]{:S(2)}, u32[]{:S(2)}) collective-permute-start(bf16[256,1024]{1,0:T(8,128)(2,1)S(1)} %constant_dynamic-update-slice_fusion.6.above_1), channel_id=1, source_target_pairs={{1,0},{2,1},{5,4},{6,5},{9,8},{10,9},{13,12},{14,13},{17,16},{18,1... | collective-permute-start | bytes 1572872 | tf_op jit(solution)/shard_map/ppermute | solution.py:423
  98.9 13.1 %collective-permute-start.18 = (bf16[256,1024]{1,0:T(8,128)(2,1)S(1)}, bf16[256,1024]{1,0:T(8,128)(2,1)S(1)}, u32[]{:S(2)}, u32[]{:S(2)}) collective-permute-start(bf16[256,1024]{1,0:T(8,128)(2,1)S(1)} %constant_dynamic-update-slice_fusion.4.below_1), channel_id=1, source_target_pairs={{1,2},{2,3},{5,6},{6,7},{9,10},{10,11},{13,14},{14,15},{17,18},{18... | collective-permute-start | bytes 1572872 | tf_op jit(solution)/shard_map/ppermute | solution.py:423
  99.6 13.1 %collective-permute-start.28 = (bf16[256,1024]{1,0:T(8,128)(2,1)S(1)}, bf16[256,1024]{1,0:T(8,128)(2,1)S(1)}, u32[]{:S(2)}, u32[]{:S(2)}) collective-permute-start(bf16[256,1024]{1,0:T(8,128)(2,1)S(1)} %get-tuple-element.59), channel_id=1, source_target_pairs={{0,8},{4,12},{8,0},{12,4},{1,9},{5,13},{9,1},{13,5},{2,10},{6,14},... | collective-permute-start | bytes 1572872 | tf_op jit(solution)/shard_map/ppermute | solution.py:420
  101.6 13.6 %collective-permute-start.25 = (bf16[256,1024]{1,0:T(8,128)(2,1)S(1)}, bf16[256,1024]{1,0:T(8,128)(2,1)S(1)}, u32[]{:S(2)}, u32[]{:S(2)}) collective-permute-start(bf16[256,1024]{1,0:T(8,128)(2,1)S(1)} %collective-permute-done.24.one), channel_id=1, source_target_pairs={{0,16},{16,0},{1,17},{17,1},{2,18},{18,2},{3,19},{19,3},{4,20},{20... | collective-permute-start | bytes 1572872 | tf_op jit(solution)/shard_map/ppermute | solution.py:479
  112.8 6.0 %collective-permute-start.26 = (bf16[256,1024]{1,0:T(8,128)(2,1)S(1)}, bf16[256,1024]{1,0:T(8,128)(2,1)S(1)}, u32[]{:S(2)}, u32[]{:S(2)}) collective-permute-start(bf16[256,1024]{1,0:T(8,128)(2,1)S(1)} %collective-permute-done.24.one), channel_id=1, source_target_pairs={{0,4},{4,0},{8,12},{12,8},{1,5},{5,1},{9,13},{13,9},{2,6},{6,2},{1... | collective-permute-start | bytes 1572872 | tf_op jit(solution)/shard_map/ppermute | solution.py:420
  115.2 3.6 %collective-permute-start.27 = (bf16[256,1024]{1,0:T(8,128)(2,1)S(1)}, bf16[256,1024]{1,0:T(8,128)(2,1)S(1)}, u32[]{:S(2)}, u32[]{:S(2)}) collective-permute-start(bf16[256,1024]{1,0:T(8,128)(2,1)S(1)} %collective-permute-done.25.other), channel_id=1, source_target_pairs={{0,4},{4,0},{8,12},{12,8},{1,5},{5,1},{9,13},{13,9},{2,6},{6,2},{1... | collective-permute-start | bytes 1572872 | tf_op jit(solution)/shard_map/ppermute | solution.py:420
  115.2 14.3 %collective-permute-start.29 = (bf16[256,1024]{1,0:T(8,128)(2,1)S(1)}, bf16[256,1024]{1,0:T(8,128)(2,1)S(1)}, u32[]{:S(2)}, u32[]{:S(2)}) collective-permute-start(bf16[256,1024]{1,0:T(8,128)(2,1)S(1)} %collective-permute-done.28.one), channel_id=1, source_target_pairs={{0,16},{16,0},{1,17},{17,1},{2,18},{18,2},{3,19},{19,3},{4,20},{20... | collective-permute-start | bytes 1572872 | tf_op jit(solution)/shard_map/ppermute | solution.py:479
  116.8 16.8 %collective-permute-start.23 = (bf16[256,1024]{1,0:T(8,128)(2,1)S(1)}, bf16[256,1024]{1,0:T(8,128)(2,1)S(1)}, u32[]{:S(2)}, u32[]{:S(2)}) collective-permute-start(bf16[256,1024]{1,0:T(8,128)(2,1)S(1)} %collective-permute-done.22.above_2), channel_id=1, source_target_pairs={{1,0},{5,4},{9,8},{13,12},{17,16},{21,20},{25,24},{29,28}} | collective-permute-start | bytes 1572872 | tf_op jit(solution)/shard_map/ppermute | solution.py:423
  118.1 15.6 %collective-permute-start.19 = (bf16[256,1024]{1,0:T(8,128)(2,1)S(1)}, bf16[256,1024]{1,0:T(8,128)(2,1)S(1)}, u32[]{:S(2)}, u32[]{:S(2)}) collective-permute-start(bf16[256,1024]{1,0:T(8,128)(2,1)S(1)} %collective-permute-done.18.below_2), channel_id=1, source_target_pairs={{2,3},{6,7},{10,11},{14,15},{18,19},{22,23},{26,27},{30,31}} | collective-permute-start | bytes 1572872 | tf_op jit(solution)/shard_map/ppermute | solution.py:423
  129.5 4.1 %collective-permute-start.30 = (bf16[256,1024]{1,0:T(8,128)(2,1)S(1)}, bf16[256,1024]{1,0:T(8,128)(2,1)S(1)}, u32[]{:S(2)}, u32[]{:S(2)}) collective-permute-start(bf16[256,1024]{1,0:T(8,128)(2,1)S(1)} %collective-permute-done.28.one), channel_id=1, source_target_pairs={{0,4},{4,0},{8,12},{12,8},{1,5},{5,1},{9,13},{13,9},{2,6},{6,2},{1... | collective-permute-start | bytes 1572872 | tf_op jit(solution)/shard_map/ppermute | solution.py:420
  129.5 4.1 %collective-permute-start.31 = (bf16[256,1024]{1,0:T(8,128)(2,1)S(1)}, bf16[256,1024]{1,0:T(8,128)(2,1)S(1)}, u32[]{:S(2)}, u32[]{:S(2)}) collective-permute-start(bf16[256,1024]{1,0:T(8,128)(2,1)S(1)} %collective-permute-done.29.other), channel_id=1, source_target_pairs={{0,4},{4,0},{8,12},{12,8},{1,5},{5,1},{9,13},{13,9},{2,6},{6,2},{1... | collective-permute-start | bytes 1572872 | tf_op jit(solution)/shard_map/ppermute | solution.py:420

commit v12 on v10

--- a/solution.py
+++ b/solution.py
@@ -205,7 +205,8 @@
         crosses = [dot_nt(high, low) for high, low in halves]
         grams = [dot_nt(high, high) + (cross + cross.T) for (high, low), cross in zip(halves, crosses)]
         gram_halves = [split(gram) for gram in grams]
-        squares = [dot(high, high) + (dot(high, low) + dot(low, high)) for high, low in gram_halves]
+        crosses = [dot(high, low) for high, low in gram_halves]
+        squares = [dot(high, high) + (cross + cross.T) for (high, low), cross in zip(gram_halves, crosses)]
         polys = [split(quintic_b * gram + quintic_c * square) for gram, square in zip(grams, squares)]
         for i in range(3):
             (poly_high, poly_low), (high, low) = polys[i], halves[i]
@@ -295,7 +296,7 @@
     )(index, local_near, local_far, other, gain, gate, up, down)
 
 
-def mix_kernel(index_ref, own, below_1, above_1, below_2, above_2, own_w, peer_w, one, other, one_peer, other_peer,
+def mix_kernel(index_ref, own, below_1, above_1, below_2, above_2, own_w, peer_w, one, one_peer,
                out_ref, rest_ref, last_ref, held):
     place, seq, last = index_ref[PLACE], index_ref[SEQ], index_ref[LAST]
     size = one.shape[0]
@@ -314,14 +315,14 @@
         for part in range(4):
             head = part if k < 2 else index_ref[PARTS + part]
             column = pl.multiple_of(index_ref[BLOCKS + head] * size, size)
-            if k >= 2 and part >= 2:
-                place_in_rest = (2 * (k - 2) + part - 2) * size
+            if k >= 2 and part >= 1:
+                place_in_rest = (3 * (k - 2) + part - 1) * size
                 rest_ref[:, place_in_rest : place_in_rest + size] = held[owner, :, pl.ds(column, size)]
                 continue
             if k < 2:
                 ref, here = (own_w, peer_w)[k], pl.ds(part * size, size)
             else:
-                ref, here = ((one, other), (one_peer, other_peer))[k - 2][part], pl.ds(0, size)
+                ref, here = (one, one_peer)[k - 2], pl.ds(0, size)
             term = dot(held[owner, :, pl.ds(column, size)], ref[here, :])
             total = term if total is None else total + term
 
@@ -344,16 +345,16 @@
         mix_kernel,
         out_shape=[
             jax.ShapeDtypeStruct((rows, columns), F32),
-            jax.ShapeDtypeStruct((rows, 4 * size), BF16),
+            jax.ShapeDtypeStruct((rows, 6 * size), BF16),
             jax.ShapeDtypeStruct((depth, columns), BF16),
         ],
         grid_spec=pltpu.PrefetchScalarGridSpec(
             num_scalar_prefetch=1,
             grid=(2,),
-            in_specs=[shard] * 5 + [whole] * 2 + [part] * 4,
+            in_specs=[shard] * 5 + [whole] * 2 + [part] * 2,
             out_specs=[
                 pl.BlockSpec((rows, tile), lambda i, idx: (0, i)),
-                pl.BlockSpec((rows, 4 * size), lambda i, idx: (0, 0)),
+                pl.BlockSpec((rows, 6 * size), lambda i, idx: (0, 0)),
                 whole,
             ],
             scratch_shapes=[pltpu.VMEM((4, rows, width), BF16)],
@@ -363,13 +364,14 @@
     )(index, *shards, own, peer, *firsts)
 
 
-def last_kernel(index_ref, below, above, weight, rest, one, other, one_peer, other_peer, before, out_ref, held):
-    size = one.shape[0]
+def last_kernel(index_ref, below, above, weight, rest, *refs):
+    laters, (before, out_ref, held) = refs[:6], refs[6:]
+    size = laters[0].shape[0]
     held[...] = jnp.where(index_ref[PLACE] == 0, above[...], below[...])
     total = before[...] + dot(held[...], weight[...])
-    for i, ref in enumerate((one, other, one_peer, other_peer)):
-        owner = lax.bitwise_xor(index_ref[SEQ], 2 + i // 2)
-        column = pl.multiple_of(index_ref[BLOCKS + index_ref[PARTS + 2 + i % 2]] * size, size)
+    for i, ref in enumerate(laters):
+        owner = lax.bitwise_xor(index_ref[SEQ], 2 + i // 3)
+        column = pl.multiple_of(index_ref[BLOCKS + index_ref[PARTS + 1 + i % 3]] * size, size)
         kept = rest[:, i * size : (i + 1) * size]
         block = jnp.where(owner == index_ref[LAST], held[:, pl.ds(column, size)], kept)
         total += dot(block, ref[...])
@@ -390,7 +392,9 @@
         grid_spec=pltpu.PrefetchScalarGridSpec(
             num_scalar_prefetch=1,
             grid=(2,),
-            in_specs=[shard, shard, pl.BlockSpec((width, tile), lambda i, idx: (0, i)), shard] + [part] * 4 + [slab],
+            in_specs=[shard, shard, pl.BlockSpec((width, tile), lambda i, idx: (0, i)), pl.BlockSpec(rest.shape, lambda i, idx: (0, 0))]
+            + [part] * 6
+            + [slab],
             out_specs=slab,
             scratch_shapes=[pltpu.VMEM((rows, width), BF16)],
         ),
@@ -482,16 +486,17 @@
     first_x = after(first_x, below_1, above_1)
     first_y = swap_groups(first_x)
     below_2, above_2 = both(1, below_1, above_1)
-    first_x_peer, first_y_peer, later_x = (after(array, below_2, above_2) for array in (first_x, first_y, later_x))
-    first_x_peer, first_y_peer = across(first_x_peer, 1), across(first_y_peer, 1)
+    held_x, later_x = (after(array, below_2, above_2) for array in (first_x, later_x))
+    first_x_peer = across(held_x, 1)
     later_y = swap_groups(later_x)
     below_3, above_3 = both(2, below_2, above_2)
 
     shards = [shard, below_1, above_1, below_2, above_2]
-    firsts = [first_x, first_y, first_x_peer, first_y_peer]
+    firsts = [first_x, first_x_peer]
     mixed, rest, weight_last = mix(index, shards, out_weight, out_peer, firsts)
-    later_x, later_y, mixed = lax.optimization_barrier((later_x, later_y, mixed))
-    laters = [later_x, later_y, across(later_x, 1), across(later_y, 1)]
+    first_y, later_x, later_y, mixed = lax.optimization_barrier((first_y, later_x, later_y, mixed))
+    laters = [first_y, later_x, later_y]
+    laters += [across(array, 1) for array in laters]
     return mix_last(index, below_3, above_3, weight_last, rest, laters, mixed)
 
 

time: 136 us -> 139 us (1.022)
  waiting for transfers between devices: 39.9 us -> 45.9 us
  starting transfers between devices: 35.5 us -> 33.1 us
    ppermute x20, waiting for transfers between devices: 15.3 us -> 30.5 us  [across(): return lax.ppermute(array, 'seq', [(i, i ^ bit) for i in range(4)])]
    ppermute x9, waiting for transfers between devices: 16.2 us -> 10.1 us  [hop(): return lax.ppermute(array, 'head', links)]
    ppermute x2, waiting for transfers between devices: 8.38 us -> 5.17 us  [swap_groups(): return lax.ppermute(array, 'groups', [(0, 1), (1, 0)])]
    ppermute x9, starting transfers between devices: 18.6 us -> 17.1 us  [hop(): return lax.ppermute(array, 'head', links)]
  transfers between devices with their start and end apart: 31 -> 31, of which waited for: 13 -> 15; matrix products, arithmetic and copies ran while one was open for 3% -> 3% of each run, Pallas kernels for 27% -> 25%
where the time goes in v12:
time: 139 us; the launch traced here: 138 us
  waiting for transfers between devices  45.9 us (33%)
  Pallas kernels  43.7 us (31%)
  starting transfers between devices  33.1 us (24%)
  local copies, waits for them, and re-layouts  12.7 us (9%)
  matrix products  2.25 us (2%)
    ppermute x20, waiting for transfers between devices, across(): return lax.ppermute(array, 'seq', [(i, i ^ bit) for i in range(4)])  30.5 us
    pallas_call x5, Pallas kernels, project(): pl.pallas_call(functools.partial(project_kernel, len(whole), len(pairs)),...  20.7 us
    ppermute x9, starting transfers between devices, hop(): return lax.ppermute(array, 'head', links)  17.1 us
    pallas_call x1, Pallas kernels, update(): pl.pallas_call(update_kernel, out_shape=[out] * 3, grid_spec=pltpu.Prefet...  13.2 us
    ppermute x20, starting transfers between devices, across(): return lax.ppermute(array, 'seq', [(i, i ^ bit) for i in range(4)])  13 us
    ppermute x9, waiting for transfers between devices, hop(): return lax.ppermute(array, 'head', links)  10.1 us
    unnamed x20, local copies, waits for them, and re-layouts  5.66 us
    ppermute x2, waiting for transfers between devices, swap_groups(): return lax.ppermute(array, 'groups', [(0, 1), (1, 0)])  5.17 us
  transfers between devices with their start and end apart: 31, of which 15 were waited for; matrix products, arithmetic and copies ran while one was open for 3% of the time, Pallas kernels for 25%

profile of v12, /device:TPU:0, one launch (start us, length us, event | category | flops | bytes accessed | tf_op | source)
XLA Modules:
  0.0 138.0 jit_solution(17603870689667163859)
XLA Ops:
  0.0 1.9 %constant_dynamic-slice_fusion.2 = bf16[256,1024]{1,0:T(8,128)(2,1)} fusion(bf16[256,4096]{1,0:T(8,128)(2,1)} %refs_0_.5, s32[]{:T(128)S(6)} %select_n.23), kind=kLoop, calls=%fused_computation.15 | loop fusion | bytes 1048580 | tf_op jit(solution)/shard_map/dynamic_slice | solution.py:433
  1.9 3.7 %dynamic-slice_bitcast_fusion = bf16[3,1024,512]{2,1,0:T(8,128)(2,1)} fusion(bf16[1024,3,1024]{2,0,1:T(8,128)(2,1)} %param.9, s32[]{:T(128)S(6)} %select_n.24), kind=kLoop, calls=%fused_computation | loop fusion | bytes 6291460 | tf_op jit(solution)/shard_map/dynamic_slice | solution.py:437
  5.6 0.5 collective-permute-start.1
  6.1 0.1 collective-permute-start
  6.1 2.9 %collective-permute-start.2 = (bf16[256,1024]{1,0:T(8,128)(2,1)}, bf16[256,1024]{1,0:T(8,128)(2,1)}, u32[]{:S(2)}, u32[]{:S(2)}) collective-permute-start(bf16[256,1024]{1,0:T(8,128)(2,1)} %constant_dynamic-slice_fusion.2), channel_id=1, source_target_pairs={{0,8},{4,12},{8,0},{12,4},{1,9},{5,13},{9,1},{13,5},{2,10},{6,14},... | collective-permute-start | bytes 1572872 | tf_op jit(solution)/shard_map/ppermute | solution.py:421
  9.1 0.1 stack.63.index_ref
  9.2 5.5 %collective-permute-done.refs_1_ = bf16[256,4096]{1,0:T(8,128)(2,1)} collective-permute-done((bf16[256,4096]{1,0:T(8,128)(2,1)}, bf16[256,4096]{1,0:T(8,128)(2,1)}, u32[]{:S(2)}, u32[]{:S(2)}) %collective-permute-start) | collective-permute-done | bytes 2097184 | tf_op jit(solution)/shard_map/ppermute | solution.py:421
  14.6 2.8 %copy-done.1 = bf16[1024,3,1024]{2,0,1:T(8,128)(2,1)S(1)} copy-done((bf16[1024,3,1024]{2,0,1:T(8,128)(2,1)S(1)}, bf16[1024,3,1024]{2,0,1:T(8,128)(2,1)}, u32[]{:S(2)}) %copy-start.1) | copy-done | bytes 6291480
  17.4 4.4 %shard_map.82 = bf16[2,512,256]{2,1,0:T(8,128)(2,1)} custom-call(s32[15]{0:T(128)S(1)} %stack.63.index_ref, bf16[256,4096]{1,0:T(8,128)(2,1)} %refs_0_.5, bf16[256,4096]{1,0:T(8,128)(2,1)} %collective-permute-done.refs_1_, bf16[3,1024,1024]{2,1,0:T(8,128)(2,1)S(1)} %bitcast.25, bf16[3,1024,512]{2,1,0:T(8,128)(2,1)S(1)} %collective-permute-done.1.refs_3_.refs_5_.refs_7_), custom_call_target="tpu_custom_call" | custom-call | flops 1 | bytes 1 | tf_op jit(solution)/shard_map/pallas_call | solution.py:146
  21.8 2.9 %collective-permute-start.3 = (bf16[256,1024]{1,0:T(8,128)(2,1)}, bf16[256,1024]{1,0:T(8,128)(2,1)}, u32[]{:S(2)}, u32[]{:S(2)}) collective-permute-start(bf16[256,1024]{1,0:T(8,128)(2,1)} %collective-permute-done.2.refs_0_.refs_2_), channel_id=1, source_target_pairs={{0,1},{1,0},{2,3},{3,2},{4,5},{5,4},{6,7},{7,6},{8,9},{9,8},{10,11... | collective-permute-start | bytes 1572872 | tf_op jit(solution)/shard_map/ppermute | solution.py:424
  24.7 1.5 %collective-permute-start.4 = (bf16[2,512,256]{2,1,0:T(8,128)(2,1)}, bf16[2,512,256]{2,1,0:T(8,128)(2,1)}, u32[]{:S(2)}, u32[]{:S(2)}) collective-permute-start(bf16[2,512,256]{2,1,0:T(8,128)(2,1)} %shard_map.82), channel_id=1, source_target_pairs={{0,8},{4,12},{8,0},{12,4},{1,9},{5,13},{9,1},{13,5},{2,10},{6,14},... | collective-permute-start | bytes 1572872 | tf_op jit(solution)/shard_map/ppermute | solution.py:421
  26.2 2.3 %compare_select_fusion = f32[4,256]{1,0:T(4,128)S(1)} fusion(bf16[256,4096]{1,0:T(8,128)(2,1)} %refs_0_.5, bf16[4096,4]{0,1:T(4,128)(2,1)S(1)} %copy-done), kind=kOutput, calls=%fused_computation.11 | convolution fusion | flops 8394752 | bytes 2134016 | tf_op jit(solution)/shard_map/dot_general | solution.py:449
  28.5 0.1 collective-permute-start.5
  28.6 0.5 collective-permute-start.7
  29.1 0.7 collective-permute-done.5
  29.7 0.5 collective-permute-start.6
  30.3 1.3 constant_dynamic-slice_fusion.1
  31.5 0.0 copy-start.2
  31.5 2.8 %copy-done.2 = bf16[1024,3,1024]{2,0,1:T(8,128)(2,1)S(1)} copy-done((bf16[1024,3,1024]{2,0,1:T(8,128)(2,1)S(1)}, bf16[1024,3,1024]{2,0,1:T(8,128)(2,1)}, u32[]{:S(2)}) %copy-start.2) | copy-done | bytes 6291480
  34.3 4.6 %shard_map.83.local_near_ref = f32[3,512,256]{2,1,0:T(8,128)S(1)} custom-call(s32[15]{0:T(128)S(1)} %stack.63.index_ref, bf16[256,4096]{1,0:T(8,128)(2,1)} %refs_0_.5, bf16[256,4096]{1,0:T(8,128)(2,1)} %collective-permute-done.refs_1_, bf16[3,1024,1024]{2,1,0:T(8,128)(2,1)S(1)} %bitcast.26, ...), custom_call_target="tpu_custom_call" | custom-call | flops 1 | bytes 1 | tf_op jit(solution)/shard_map/pallas_call | solution.py:146
  38.9 0.0 copy-start.3
  38.9 0.1 collective-permute-start.8
  39.0 2.1 %collective-permute-done.8.refs_3_.refs_5_ = bf16[256,1024]{1,0:T(8,128)(2,1)S(1)} collective-permute-done((bf16[256,1024]{1,0:T(8,128)(2,1)}, bf16[256,1024]{1,0:T(8,128)(2,1)S(1)}, u32[]{:S(2)}, u32[]{:S(2)}) %collective-permute-start.8) | collective-permute-done | bytes 524320 | tf_op jit(solution)/shard_map/ppermute | solution.py:421
  41.1 3.4 %shard_map.84 = bf16[2,512,256]{2,1,0:T(8,128)(2,1)S(1)} custom-call(s32[15]{0:T(128)S(1)} %stack.63.index_ref, bf16[256,1024]{1,0:T(8,128)(2,1)} %collective-permute-done.2.refs_0_.refs_2_, bf16[256,1024]{1,0:T(8,128)(2,1)} %collective-permute-done.3.refs_1_.refs_3_, bf16[256,1024]{1,0:T(8,128)(2,1)S(1)} %collective-permute-done.7.refs_2_.refs_4_, ...), custom_call_target="tpu_custom_call" | custom-call | flops 1 | bytes 1 | tf_op jit(solution)/shard_map/pallas_call | solution.py:146
  44.5 0.2 collective-permute-start.9
  44.7 1.5 %collective-permute-start.10 = (bf16[2,512,256]{2,1,0:T(8,128)(2,1)S(1)}, bf16[2,512,256]{2,1,0:T(8,128)(2,1)S(1)}, u32[]{:S(2)}, u32[]{:S(2)}) collective-permute-start(bf16[2,512,256]{2,1,0:T(8,128)(2,1)S(1)} %shard_map.84), channel_id=1, source_target_pairs={{0,8},{4,12},{8,0},{12,4},{1,9},{5,13},{9,1},{13,5},{2,10},{6,14},... | collective-permute-start | bytes 1572872 | tf_op jit(solution)/shard_map/ppermute | solution.py:421
  46.2 3.9 %shard_map.85 = bf16[1,1024,256]{2,1,0:T(8,128)(2,1)S(1)} custom-call(s32[15]{0:T(128)S(1)} %stack.63.index_ref, bf16[256,4096]{1,0:T(8,128)(2,1)} %refs_0_.5, bf16[256,4096]{1,0:T(8,128)(2,1)} %collective-permute-done.refs_1_, bf16[256,1024]{1,0:T(8,128)(2,1)} %collective-permute-done.2.refs_0_.refs_2_, ...), custom_call_target="tpu_custom_call" | custom-call | flops 1 | bytes 1 | tf_op jit(solution)/shard_map/pallas_call | solution.py:146
  50.2 0.0 copy-start.4
  50.2 4.4 %shard_map.86.local_far_ref = f32[3,512,256]{2,1,0:T(8,128)S(1)} custom-call(s32[15]{0:T(128)S(1)} %stack.63.index_ref, bf16[256,1024]{1,0:T(8,128)(2,1)} %collective-permute-done.2.refs_0_.refs_2_, bf16[256,1024]{1,0:T(8,128)(2,1)} %collective-permute-done.3.refs_1_.refs_3_, bf16[256,1024]{1,0:T(8,128)(2,1)S(1)} %collective-permute-done.7.refs_2_.refs_4_, ...), custom_call_target="tpu_custom_call" | custom-call | flops 1 | bytes 1 | tf_op jit(solution)/shard_map/pallas_call | solution.py:146
  54.7 0.0 copy-start.7
  54.7 4.2 %collective-permute-done.10.near_ref = bf16[2,512,256]{2,1,0:T(8,128)(2,1)S(1)} collective-permute-done((bf16[2,512,256]{2,1,0:T(8,128)(2,1)S(1)}, bf16[2,512,256]{2,1,0:T(8,128)(2,1)S(1)}, u32[]{:S(2)}, u32[]{:S(2)}) %collective-permute-start.10) | collective-permute-done | bytes 524320 | tf_op jit(solution)/shard_map/ppermute | solution.py:421
  58.9 1.5 %collective-permute-start.11 = (bf16[1,1024,256]{2,1,0:T(8,128)(2,1)S(1)}, bf16[1,1024,256]{2,1,0:T(8,128)(2,1)S(1)}, u32[]{:S(2)}, u32[]{:S(2)}) collective-permute-start(bf16[1,1024,256]{2,1,0:T(8,128)(2,1)S(1)} %shard_map.85), channel_id=1, source_target_pairs={{0,8},{4,12},{8,0},{12,4},{1,9},{5,13},{9,1},{13,5},{2,10},{6,14},... | collective-permute-start | bytes 1572872 | tf_op jit(solution)/shard_map/ppermute | solution.py:421
  60.4 13.2 %shard_map.87 = (bf16[256,512]{1,0:T(8,128)(2,1)S(1)}, bf16[256,512]{1,0:T(8,128)(2,1)S(1)}, bf16[256,512]{1,0:T(8,128)(2,1)S(1)}) custom-call(s32[15]{0:T(128)S(1)} %stack.63.index_ref, f32[3,512,256]{2,1,0:T(8,128)S(1)} %shard_map.83.local_near_ref, f32[3,512,256]{2,1,0:T(8,128)S(1)} %shard_map.86.local_far_ref, ...), custom_call_target="tpu_custom_call" | custom-call | flops 1 | bytes 1 | tf_op jit(solution)/shard_map/pallas_call | solution.py:231
  73.7 2.0 %shard_map.88 = (bf16[256,256]{1,0:T(8,128)(2,1)S(1)}, bf16[256,256]{1,0:T(8,128)(2,1)S(1)}, bf16[256,256]{1,0:T(8,128)(2,1)S(1)}, bf16[256,256]{1,0:T(8,128)(2,1)S(1)}) custom-call(s32[15]{0:T(128)S(1)} %stack.63.index_ref, f32[3,512,256]{2,1,0:T(8,128)S(1)} %shard_map.83.local_near_ref, f32[3,512,256]{2,1,0:T(8,128)S(1)} %shard_map.86.local_far_ref, ...), custom_call_target="tpu_custom_call" | custom-call | flops 1 | bytes 1 | tf_op jit(solution)/shard_map/pallas_call | solution.py:277
  75.7 0.1 collective-permute-start.12
  75.8 0.6 collective-permute-start.14
  76.4 1.3 collective-permute-start.15
  77.7 1.3 collective-permute-start.19
  79.0 3.2 %collective-permute-done.14 = bf16[256,256]{1,0:T(8,128)(2,1)S(1)} collective-permute-done((bf16[256,256]{1,0:T(8,128)(2,1)S(1)}, bf16[256,256]{1,0:T(8,128)(2,1)S(1)}, u32[]{:S(2)}, u32[]{:S(2)}) %collective-permute-start.14) | collective-permute-done | bytes 131104 | tf_op jit(solution)/shard_map/ppermute | solution.py:421
  82.2 1.9 %collective-permute-done.15 = bf16[256,256]{1,0:T(8,128)(2,1)S(1)} collective-permute-done((bf16[256,256]{1,0:T(8,128)(2,1)S(1)}, bf16[256,256]{1,0:T(8,128)(2,1)S(1)}, u32[]{:S(2)}, u32[]{:S(2)}) %collective-permute-start.15) | collective-permute-done | bytes 131104 | tf_op jit(solution)/shard_map/ppermute | solution.py:421
  84.1 1.3 collective-permute-start.20
  85.4 4.6 %collective-permute-start.13 = (bf16[256,512]{1,0:T(8,128)(2,1)S(1)}, bf16[256,512]{1,0:T(8,128)(2,1)S(1)}, u32[]{:S(2)}, u32[]{:S(2)}) collective-permute-start(bf16[256,512]{1,0:T(8,128)(2,1)S(1)} %constant_dynamic-update-slice_fusion), channel_id=1, source_target_pairs={{0,1},{1,2},{2,3},{4,5},{5,6},{6,7},{8,9},{9,10},{10,11},{12,13},{... | collective-permute-start | bytes 786440 | tf_op jit(solution)/shard_map/ppermute | solution.py:424
  89.9 3.0 %collective-permute-start.16 = (bf16[256,512]{1,0:T(8,128)(2,1)S(1)}, bf16[256,512]{1,0:T(8,128)(2,1)S(1)}, u32[]{:S(2)}, u32[]{:S(2)}) collective-permute-start(bf16[256,512]{1,0:T(8,128)(2,1)S(1)} %constant_dynamic-update-slice_fusion.2), channel_id=1, source_target_pairs={{0,1},{1,2},{2,3},{4,5},{5,6},{6,7},{8,9},{9,10},{10,11},{12,13},{... | collective-permute-start | bytes 786440 | tf_op jit(solution)/shard_map/ppermute | solution.py:424
  93.0 0.6 collective-permute-start.23
  93.7 1.1 collective-permute-done.20
  94.8 1.3 collective-permute-start.21
  96.1 0.5 collective-permute-done.13
  96.6 5.0 %collective-permute-done.16 = bf16[256,512]{1,0:T(8,128)(2,1)S(1)} collective-permute-done((bf16[256,512]{1,0:T(8,128)(2,1)S(1)}, bf16[256,512]{1,0:T(8,128)(2,1)S(1)}, u32[]{:S(2)}, u32[]{:S(2)}) %collective-permute-start.16) | collective-permute-done | bytes 262176 | tf_op jit(solution)/shard_map/ppermute | solution.py:424
  101.6 0.7 collective-permute-start.17
  102.3 0.6 collective-permute-start.26
  102.9 5.0 %collective-permute-done.23.one = bf16[256,1024]{1,0:T(8,128)(2,1)S(1)} collective-permute-done((bf16[256,1024]{1,0:T(8,128)(2,1)S(1)}, bf16[256,1024]{1,0:T(8,128)(2,1)S(1)}, u32[]{:S(2)}, u32[]{:S(2)}) %collective-permute-start.23) | collective-permute-done | bytes 524320 | tf_op jit(solution)/shard_map/ppermute | solution.py:421
  107.8 1.5 %collective-permute-start.25 = (bf16[256,1024]{1,0:T(8,128)(2,1)S(1)}, bf16[256,1024]{1,0:T(8,128)(2,1)S(1)}, u32[]{:S(2)}, u32[]{:S(2)}) collective-permute-start(bf16[256,1024]{1,0:T(8,128)(2,1)S(1)} %collective-permute-done.23.one), channel_id=1, source_target_pairs={{0,16},{16,0},{1,17},{17,1},{2,18},{18,2},{3,19},{19,3},{4,20},{20... | collective-permute-start | bytes 1572872 | tf_op jit(solution)/shard_map/ppermute | solution.py:478
  109.4 0.9 collective-permute-done.21.above_2
  110.3 7.8 %collective-permute-done.26.refs_1_ = bf16[256,1024]{1,0:T(8,128)(2,1)S(1)} collective-permute-done((bf16[256,1024]{1,0:T(8,128)(2,1)S(1)}, bf16[256,1024]{1,0:T(8,128)(2,1)S(1)}, u32[]{:S(2)}, u32[]{:S(2)}) %collective-permute-start.26) | collective-permute-done | bytes 524320 | tf_op jit(solution)/shard_map/ppermute | solution.py:421
  118.1 1.5 %collective-permute-start.27 = (bf16[256,1024]{1,0:T(8,128)(2,1)S(1)}, bf16[256,1024]{1,0:T(8,128)(2,1)S(1)}, u32[]{:S(2)}, u32[]{:S(2)}) collective-permute-start(bf16[256,1024]{1,0:T(8,128)(2,1)S(1)} %collective-permute-done.26.refs_1_), channel_id=1, source_target_pairs={{0,16},{16,0},{1,17},{17,1},{2,18},{18,2},{3,19},{19,3},{4,20},{20... | collective-permute-start | bytes 1572872 | tf_op jit(solution)/shard_map/ppermute | solution.py:478
  119.6 0.1 pad_maximum_fusion.own
  119.7 1.3 collective-permute-start.22
  121.0 0.7 collective-permute-start.18
  121.7 4.2 %shard_map.89 = (f32[256,1024]{1,0:T(8,128)S(1)}, bf16[256,1536]{1,0:T(8,128)(2,1)S(1)}, bf16[1024,1024]{1,0:T(8,128)(2,1)S(1)}) custom-call(s32[15]{0:T(128)S(1)} %stack.63.index_ref, bf16[256,1024]{1,0:T(8,128)(2,1)S(1)} %pad_maximum_fusion.own, bf16[256,1024]{1,0:T(8,128)(2,1)S(1)} %constant_dynamic-update-slice_fusion.4.below_1, ...), custom_call_target="tpu_custom_call" | custom-call | flops 1 | bytes 1 | tf_op jit(solution)/shard_map/pallas_call | solution.py:344
  126.0 5.2 %collective-permute-done.27.refs_2_ = bf16[256,1024]{1,0:T(8,128)(2,1)S(1)} collective-permute-done((bf16[256,1024]{1,0:T(8,128)(2,1)S(1)}, bf16[256,1024]{1,0:T(8,128)(2,1)S(1)}, u32[]{:S(2)}, u32[]{:S(2)}) %collective-permute-start.27) | collective-permute-done | bytes 524320 | tf_op jit(solution)/shard_map/ppermute | solution.py:478
  131.1 0.5 collective-permute-start.29
  131.6 2.7 %collective-permute-done.22.above = bf16[256,1024]{1,0:T(8,128)(2,1)S(1)} collective-permute-done((bf16[256,1024]{1,0:T(8,128)(2,1)S(1)}, bf16[256,1024]{1,0:T(8,128)(2,1)S(1)}, u32[]{:S(2)}, u32[]{:S(2)}) %collective-permute-start.22) | collective-permute-done | bytes 524320 | tf_op jit(solution)/shard_map/ppermute | solution.py:424
  134.3 0.2 collective-permute-done.30.refs_5_
  134.5 3.5 %shard_map.90 = bf16[256,1024]{1,0:T(8,128)(2,1)} custom-call(s32[15]{0:T(128)S(1)} %stack.63.index_ref, bf16[256,1024]{1,0:T(8,128)(2,1)S(1)} %collective-permute-done.18.below, bf16[256,1024]{1,0:T(8,128)(2,1)S(1)} %collective-permute-done.22.above, bf16[1024,1024]{1,0:T(8,128)(2,1)S(1)} %get-tuple-element.54.weight, ...), custom_call_target="tpu_custom_call" | custom-call | flops 1 | bytes 1 | tf_op jit(solution)/shard_map/pallas_call | solution.py:389
  (38 shorter events, 0.2 us)
Async XLA Ops:
  0.0 26.2 %copy-start = (bf16[4096,4]{0,1:T(4,128)(2,1)S(1)}, bf16[4096,4]{0,1:T(4,128)(2,1)}, u32[]{:S(2)}) copy-start(bf16[4096,4]{0,1:T(4,128)(2,1)} %param.10) | copy-start | bytes 98308
  5.6 9.0 %collective-permute-start.1 = (bf16[3,1024,512]{2,1,0:T(8,128)(2,1)}, bf16[3,1024,512]{2,1,0:T(8,128)(2,1)S(1)}, u32[]{:S(2)}, u32[]{:S(2)}) collective-permute-start(bf16[3,1024,512]{2,1,0:T(8,128)(2,1)} %dynamic-slice_bitcast_fusion), channel_id=1, source_target_pairs={{0,4},{4,0},{8,12},{12,8},{1,5},{5,1},{9,13},{13,9},{2,6},{6,2},{1... | collective-permute-start | bytes 9437192 | tf_op jit(solution)/shard_map/ppermute | solution.py:421
  6.1 8.5 %collective-permute-start = (bf16[256,4096]{1,0:T(8,128)(2,1)}, bf16[256,4096]{1,0:T(8,128)(2,1)}, u32[]{:S(2)}, u32[]{:S(2)}) collective-permute-start(bf16[256,4096]{1,0:T(8,128)(2,1)} %refs_0_.5), channel_id=1, source_target_pairs={{0,4},{4,0},{8,12},{12,8},{1,5},{5,1},{9,13},{13,9},{2,6},{6,2},{1... | collective-permute-start | bytes 6291464 | tf_op jit(solution)/shard_map/ppermute | solution.py:421
  6.1 15.7 %collective-permute-start.2 = (bf16[256,1024]{1,0:T(8,128)(2,1)}, bf16[256,1024]{1,0:T(8,128)(2,1)}, u32[]{:S(2)}, u32[]{:S(2)}) collective-permute-start(bf16[256,1024]{1,0:T(8,128)(2,1)} %constant_dynamic-slice_fusion.2), channel_id=1, source_target_pairs={{0,8},{4,12},{8,0},{12,4},{1,9},{5,13},{9,1},{13,5},{2,10},{6,14},... | collective-permute-start | bytes 1572872 | tf_op jit(solution)/shard_map/ppermute | solution.py:421
  14.6 2.8 %copy-start.1 = (bf16[1024,3,1024]{2,0,1:T(8,128)(2,1)S(1)}, bf16[1024,3,1024]{2,0,1:T(8,128)(2,1)}, u32[]{:S(2)}) copy-start(bf16[1024,3,1024]{2,0,1:T(8,128)(2,1)} %param.9) | copy-start | bytes 18874372
  21.8 17.1 %collective-permute-start.3 = (bf16[256,1024]{1,0:T(8,128)(2,1)}, bf16[256,1024]{1,0:T(8,128)(2,1)}, u32[]{:S(2)}, u32[]{:S(2)}) collective-permute-start(bf16[256,1024]{1,0:T(8,128)(2,1)} %collective-permute-done.2.refs_0_.refs_2_), channel_id=1, source_target_pairs={{0,1},{1,0},{2,3},{3,2},{4,5},{5,4},{6,7},{7,6},{8,9},{9,8},{10,11... | collective-permute-start | bytes 1572872 | tf_op jit(solution)/shard_map/ppermute | solution.py:424
  24.7 14.2 %collective-permute-start.4 = (bf16[2,512,256]{2,1,0:T(8,128)(2,1)}, bf16[2,512,256]{2,1,0:T(8,128)(2,1)}, u32[]{:S(2)}, u32[]{:S(2)}) collective-permute-start(bf16[2,512,256]{2,1,0:T(8,128)(2,1)} %shard_map.82), channel_id=1, source_target_pairs={{0,8},{4,12},{8,0},{12,4},{1,9},{5,13},{9,1},{13,5},{2,10},{6,14},... | collective-permute-start | bytes 1572872 | tf_op jit(solution)/shard_map/ppermute | solution.py:421
  28.5 1.2 collective-permute-start.5
  28.6 10.4 %collective-permute-start.7 = (bf16[256,1024]{1,0:T(8,128)(2,1)}, bf16[256,1024]{1,0:T(8,128)(2,1)S(1)}, u32[]{:S(2)}, u32[]{:S(2)}) collective-permute-start(bf16[256,1024]{1,0:T(8,128)(2,1)} %collective-permute-done.2.refs_0_.refs_2_), channel_id=1, source_target_pairs={{0,4},{4,0},{8,12},{12,8},{1,5},{5,1},{9,13},{13,9},{2,6},{6,2},{1... | collective-permute-start | bytes 1572872 | tf_op jit(solution)/shard_map/ppermute | solution.py:421
  29.7 9.2 %collective-permute-start.6 = (f32[8,256]{1,0:T(8,128)S(1)}, f32[8,256]{1,0:T(8,128)S(1)}, u32[]{:S(2)}, u32[]{:S(2)}) collective-permute-start(f32[8,256]{1,0:T(8,128)S(1)} %pad_maximum_fusion.1.rate_near_ref), channel_id=1, source_target_pairs={{0,8},{4,12},{8,0},{12,4},{1,9},{5,13},{9,1},{13,5},{2,10},{6,14},... | collective-permute-start | bytes 24584 | tf_op jit(solution)/shard_map/ppermute | solution.py:421
  31.5 2.8 %copy-start.2 = (bf16[1024,3,1024]{2,0,1:T(8,128)(2,1)S(1)}, bf16[1024,3,1024]{2,0,1:T(8,128)(2,1)}, u32[]{:S(2)}) copy-start(bf16[1024,3,1024]{2,0,1:T(8,128)(2,1)} %param.9) | copy-start | bytes 18874372
  38.9 5.6 %copy-start.3 = (bf16[1024,1024]{1,0:T(8,128)(2,1)S(1)}, bf16[1024,1024]{1,0:T(8,128)(2,1)}, u32[]{:S(2)}) copy-start(bf16[1024,1024]{1,0:T(8,128)(2,1)} %own_w.1) | copy-start | bytes 6291460
  38.9 2.2 %collective-permute-start.8 = (bf16[256,1024]{1,0:T(8,128)(2,1)}, bf16[256,1024]{1,0:T(8,128)(2,1)S(1)}, u32[]{:S(2)}, u32[]{:S(2)}) collective-permute-start(bf16[256,1024]{1,0:T(8,128)(2,1)} %collective-permute-done.3.refs_1_.refs_3_), channel_id=1, source_target_pairs={{0,4},{4,0},{8,12},{12,8},{1,5},{5,1},{9,13},{13,9},{2,6},{6,2},{1... | collective-permute-start | bytes 1572872 | tf_op jit(solution)/shard_map/ppermute | solution.py:421
  44.5 5.7 %collective-permute-start.9 = (bf16[1024,1024]{1,0:T(8,128)(2,1)S(1)}, bf16[1024,1024]{1,0:T(8,128)(2,1)S(1)}, u32[]{:S(2)}, u32[]{:S(2)}) collective-permute-start(bf16[1024,1024]{1,0:T(8,128)(2,1)S(1)} %copy-done.3), channel_id=1, source_target_pairs={{0,4},{4,0},{8,12},{12,8},{1,5},{5,1},{9,13},{13,9},{2,6},{6,2},{1... | collective-permute-start | bytes 6291464 | tf_op jit(solution)/shard_map/ppermute | solution.py:421
  44.7 14.2 %collective-permute-start.10 = (bf16[2,512,256]{2,1,0:T(8,128)(2,1)S(1)}, bf16[2,512,256]{2,1,0:T(8,128)(2,1)S(1)}, u32[]{:S(2)}, u32[]{:S(2)}) collective-permute-start(bf16[2,512,256]{2,1,0:T(8,128)(2,1)S(1)} %shard_map.84), channel_id=1, source_target_pairs={{0,8},{4,12},{8,0},{12,4},{1,9},{5,13},{9,1},{13,5},{2,10},{6,14},... | collective-permute-start | bytes 1572872 | tf_op jit(solution)/shard_map/ppermute | solution.py:421
  50.2 10.2 %copy-start.4 = (bf16[4,256,512]{2,1,0:T(8,128)(2,1)S(1)}, bf16[4,256,512]{2,1,0:T(8,128)(2,1)}, u32[]{:S(2)}) copy-start(bf16[4,256,512]{2,1,0:T(8,128)(2,1)} %gate_ref.1) | copy-start | bytes 3145732
  50.2 10.2 %copy-start.5 = (bf16[4,256,512]{2,1,0:T(8,128)(2,1)S(1)}, bf16[4,256,512]{2,1,0:T(8,128)(2,1)}, u32[]{:S(2)}) copy-start(bf16[4,256,512]{2,1,0:T(8,128)(2,1)} %up_ref.1) | copy-start | bytes 3145732
  50.2 10.2 %copy-start.6 = (bf16[4,256,512]{2,1,0:T(8,128)(2,1)S(1)}, bf16[4,256,512]{2,1,0:T(8,128)(2,1)}, u32[]{:S(2)}) copy-start(bf16[4,256,512]{2,1,0:T(8,128)(2,1)} %down_ref.1) | copy-start | bytes 3145732
  54.7 19.0 %copy-start.7 = (f32[1024]{0:T(1024)S(1)}, f32[1024]{0:T(1024)}, u32[]{:S(2)}) copy-start(f32[1024]{0:T(1024)} %param.14) | copy-start | bytes 12292
  58.9 14.8 %collective-permute-start.11 = (bf16[1,1024,256]{2,1,0:T(8,128)(2,1)S(1)}, bf16[1,1024,256]{2,1,0:T(8,128)(2,1)S(1)}, u32[]{:S(2)}, u32[]{:S(2)}) collective-permute-start(bf16[1,1024,256]{2,1,0:T(8,128)(2,1)S(1)} %shard_map.85), channel_id=1, source_target_pairs={{0,8},{4,12},{8,0},{12,4},{1,9},{5,13},{9,1},{13,5},{2,10},{6,14},... | collective-permute-start | bytes 1572872 | tf_op jit(solution)/shard_map/ppermute | solution.py:421
  75.7 2.0 %collective-permute-start.12 = (bf16[256,256]{1,0:T(8,128)(2,1)S(1)}, bf16[256,256]{1,0:T(8,128)(2,1)S(1)}, u32[]{:S(2)}, u32[]{:S(2)}) collective-permute-start(bf16[256,256]{1,0:T(8,128)(2,1)S(1)} %get-tuple-element.48), channel_id=1, source_target_pairs={{0,4},{4,0},{8,12},{12,8},{1,5},{5,1},{9,13},{13,9},{2,6},{6,2},{1... | collective-permute-start | bytes 393224 | tf_op jit(solution)/shard_map/ppermute | solution.py:421
  75.8 6.4 %collective-permute-start.14 = (bf16[256,256]{1,0:T(8,128)(2,1)S(1)}, bf16[256,256]{1,0:T(8,128)(2,1)S(1)}, u32[]{:S(2)}, u32[]{:S(2)}) collective-permute-start(bf16[256,256]{1,0:T(8,128)(2,1)S(1)} %get-tuple-element.49), channel_id=1, source_target_pairs={{0,8},{4,12},{8,0},{12,4},{1,9},{5,13},{9,1},{13,5},{2,10},{6,14},... | collective-permute-start | bytes 393224 | tf_op jit(solution)/shard_map/ppermute | solution.py:421
  76.4 7.7 %collective-permute-start.15 = (bf16[256,256]{1,0:T(8,128)(2,1)S(1)}, bf16[256,256]{1,0:T(8,128)(2,1)S(1)}, u32[]{:S(2)}, u32[]{:S(2)}) collective-permute-start(bf16[256,256]{1,0:T(8,128)(2,1)S(1)} %get-tuple-element.50), channel_id=1, source_target_pairs={{0,12},{4,8},{8,4},{12,0},{1,13},{5,9},{9,5},{13,1},{2,14},{6,10},... | collective-permute-start | bytes 393224 | tf_op jit(solution)/shard_map/ppermute | solution.py:421
  77.7 15.9 %collective-permute-start.19 = (bf16[256,512]{1,0:T(8,128)(2,1)S(1)}, bf16[256,512]{1,0:T(8,128)(2,1)S(1)}, u32[]{:S(2)}, u32[]{:S(2)}) collective-permute-start(bf16[256,512]{1,0:T(8,128)(2,1)S(1)} %constant_dynamic-update-slice_fusion), channel_id=1, source_target_pairs={{1,0},{2,1},{3,2},{5,4},{6,5},{7,6},{9,8},{10,9},{11,10},{13,12},{... | collective-permute-start | bytes 786440 | tf_op jit(solution)/shard_map/ppermute | solution.py:424
  84.1 10.7 %collective-permute-start.20 = (bf16[256,512]{1,0:T(8,128)(2,1)S(1)}, bf16[256,512]{1,0:T(8,128)(2,1)S(1)}, u32[]{:S(2)}, u32[]{:S(2)}) collective-permute-start(bf16[256,512]{1,0:T(8,128)(2,1)S(1)} %constant_dynamic-update-slice_fusion.2), channel_id=1, source_target_pairs={{1,0},{2,1},{3,2},{5,4},{6,5},{7,6},{9,8},{10,9},{11,10},{13,12},{... | collective-permute-start | bytes 786440 | tf_op jit(solution)/shard_map/ppermute | solution.py:424
  85.4 11.2 %collective-permute-start.13 = (bf16[256,512]{1,0:T(8,128)(2,1)S(1)}, bf16[256,512]{1,0:T(8,128)(2,1)S(1)}, u32[]{:S(2)}, u32[]{:S(2)}) collective-permute-start(bf16[256,512]{1,0:T(8,128)(2,1)S(1)} %constant_dynamic-update-slice_fusion), channel_id=1, source_target_pairs={{0,1},{1,2},{2,3},{4,5},{5,6},{6,7},{8,9},{9,10},{10,11},{12,13},{... | collective-permute-start | bytes 786440 | tf_op jit(solution)/shard_map/ppermute | solution.py:424
  89.9 11.6 %collective-permute-start.16 = (bf16[256,512]{1,0:T(8,128)(2,1)S(1)}, bf16[256,512]{1,0:T(8,128)(2,1)S(1)}, u32[]{:S(2)}, u32[]{:S(2)}) collective-permute-start(bf16[256,512]{1,0:T(8,128)(2,1)S(1)} %constant_dynamic-update-slice_fusion.2), channel_id=1, source_target_pairs={{0,1},{1,2},{2,3},{4,5},{5,6},{6,7},{8,9},{9,10},{10,11},{12,13},{... | collective-permute-start | bytes 786440 | tf_op jit(solution)/shard_map/ppermute | solution.py:424
  93.0 14.9 %collective-permute-start.23 = (bf16[256,1024]{1,0:T(8,128)(2,1)S(1)}, bf16[256,1024]{1,0:T(8,128)(2,1)S(1)}, u32[]{:S(2)}, u32[]{:S(2)}) collective-permute-start(bf16[256,1024]{1,0:T(8,128)(2,1)S(1)} %get-tuple-element.51), channel_id=1, source_target_pairs={{0,8},{4,12},{8,0},{12,4},{1,9},{5,13},{9,1},{13,5},{2,10},{6,14},... | collective-permute-start | bytes 1572872 | tf_op jit(solution)/shard_map/ppermute | solution.py:421
  94.8 15.5 %collective-permute-start.21 = (bf16[256,1024]{1,0:T(8,128)(2,1)S(1)}, bf16[256,1024]{1,0:T(8,128)(2,1)S(1)}, u32[]{:S(2)}, u32[]{:S(2)}) collective-permute-start(bf16[256,1024]{1,0:T(8,128)(2,1)S(1)} %constant_dynamic-update-slice_fusion.6.above_1), channel_id=1, source_target_pairs={{1,0},{2,1},{5,4},{6,5},{9,8},{10,9},{13,12},{14,13},{17,16},{18,1... | collective-permute-start | bytes 1572872 | tf_op jit(solution)/shard_map/ppermute | solution.py:424
  101.6 8.7 %collective-permute-start.17 = (bf16[256,1024]{1,0:T(8,128)(2,1)S(1)}, bf16[256,1024]{1,0:T(8,128)(2,1)S(1)}, u32[]{:S(2)}, u32[]{:S(2)}) collective-permute-start(bf16[256,1024]{1,0:T(8,128)(2,1)S(1)} %constant_dynamic-update-slice_fusion.4.below_1), channel_id=1, source_target_pairs={{1,2},{2,3},{5,6},{6,7},{9,10},{10,11},{13,14},{14,15},{17,18},{18... | collective-permute-start | bytes 1572872 | tf_op jit(solution)/shard_map/ppermute | solution.py:424
  102.3 15.9 %collective-permute-start.26 = (bf16[256,1024]{1,0:T(8,128)(2,1)S(1)}, bf16[256,1024]{1,0:T(8,128)(2,1)S(1)}, u32[]{:S(2)}, u32[]{:S(2)}) collective-permute-start(bf16[256,1024]{1,0:T(8,128)(2,1)S(1)} %get-tuple-element.56), channel_id=1, source_target_pairs={{0,8},{4,12},{8,0},{12,4},{1,9},{5,13},{9,1},{13,5},{2,10},{6,14},... | collective-permute-start | bytes 1572872 | tf_op jit(solution)/shard_map/ppermute | solution.py:421
  107.8 18.1 %collective-permute-start.25 = (bf16[256,1024]{1,0:T(8,128)(2,1)S(1)}, bf16[256,1024]{1,0:T(8,128)(2,1)S(1)}, u32[]{:S(2)}, u32[]{:S(2)}) collective-permute-start(bf16[256,1024]{1,0:T(8,128)(2,1)S(1)} %collective-permute-done.23.one), channel_id=1, source_target_pairs={{0,16},{16,0},{1,17},{17,1},{2,18},{18,2},{3,19},{19,3},{4,20},{20... | collective-permute-start | bytes 1572872 | tf_op jit(solution)/shard_map/ppermute | solution.py:478
  110.3 11.4 %collective-permute-start.24 = (bf16[256,1024]{1,0:T(8,128)(2,1)S(1)}, bf16[256,1024]{1,0:T(8,128)(2,1)S(1)}, u32[]{:S(2)}, u32[]{:S(2)}) collective-permute-start(bf16[256,1024]{1,0:T(8,128)(2,1)S(1)} %collective-permute-done.23.one), channel_id=1, source_target_pairs={{0,4},{4,0},{8,12},{12,8},{1,5},{5,1},{9,13},{13,9},{2,6},{6,2},{1... | collective-permute-start | bytes 1572872 | tf_op jit(solution)/shard_map/ppermute | solution.py:421
  118.1 13.0 %collective-permute-start.27 = (bf16[256,1024]{1,0:T(8,128)(2,1)S(1)}, bf16[256,1024]{1,0:T(8,128)(2,1)S(1)}, u32[]{:S(2)}, u32[]{:S(2)}) collective-permute-start(bf16[256,1024]{1,0:T(8,128)(2,1)S(1)} %collective-permute-done.26.refs_1_), channel_id=1, source_target_pairs={{0,16},{16,0},{1,17},{17,1},{2,18},{18,2},{3,19},{19,3},{4,20},{20... | collective-permute-start | bytes 1572872 | tf_op jit(solution)/shard_map/ppermute | solution.py:478
  119.7 14.6 %collective-permute-start.22 = (bf16[256,1024]{1,0:T(8,128)(2,1)S(1)}, bf16[256,1024]{1,0:T(8,128)(2,1)S(1)}, u32[]{:S(2)}, u32[]{:S(2)}) collective-permute-start(bf16[256,1024]{1,0:T(8,128)(2,1)S(1)} %collective-permute-done.21.above_2), channel_id=1, source_target_pairs={{1,0},{5,4},{9,8},{13,12},{17,16},{21,20},{25,24},{29,28}} | collective-permute-start | bytes 1572872 | tf_op jit(solution)/shard_map/ppermute | solution.py:424
  121.0 13.3 %collective-permute-start.18 = (bf16[256,1024]{1,0:T(8,128)(2,1)S(1)}, bf16[256,1024]{1,0:T(8,128)(2,1)S(1)}, u32[]{:S(2)}, u32[]{:S(2)}) collective-permute-start(bf16[256,1024]{1,0:T(8,128)(2,1)S(1)} %collective-permute-done.17.below_2), channel_id=1, source_target_pairs={{2,3},{6,7},{10,11},{14,15},{18,19},{22,23},{26,27},{30,31}} | collective-permute-start | bytes 1572872 | tf_op jit(solution)/shard_map/ppermute | solution.py:424
  131.1 3.2 %collective-permute-start.28 = (bf16[256,1024]{1,0:T(8,128)(2,1)S(1)}, bf16[256,1024]{1,0:T(8,128)(2,1)S(1)}, u32[]{:S(2)}, u32[]{:S(2)}) collective-permute-start(bf16[256,1024]{1,0:T(8,128)(2,1)S(1)} %collective-permute-done.25.refs_0_), channel_id=1, source_target_pairs={{0,4},{4,0},{8,12},{12,8},{1,5},{5,1},{9,13},{13,9},{2,6},{6,2},{1... | collective-permute-start | bytes 1572872 | tf_op jit(solution)/shard_map/ppermute | solution.py:421
  131.1 3.2 %collective-permute-start.29 = (bf16[256,1024]{1,0:T(8,128)(2,1)S(1)}, bf16[256,1024]{1,0:T(8,128)(2,1)S(1)}, u32[]{:S(2)}, u32[]{:S(2)}) collective-permute-start(bf16[256,1024]{1,0:T(8,128)(2,1)S(1)} %collective-permute-done.26.refs_1_), channel_id=1, source_target_pairs={{0,4},{4,0},{8,12},{12,8},{1,5},{5,1},{9,13},{13,9},{2,6},{6,2},{1... | collective-permute-start | bytes 1572872 | tf_op jit(solution)/shard_map/ppermute | solution.py:421
  131.6 2.9 %collective-permute-start.30 = (bf16[256,1024]{1,0:T(8,128)(2,1)S(1)}, bf16[256,1024]{1,0:T(8,128)(2,1)S(1)}, u32[]{:S(2)}, u32[]{:S(2)}) collective-permute-start(bf16[256,1024]{1,0:T(8,128)(2,1)S(1)} %collective-permute-done.27.refs_2_), channel_id=1, source_target_pairs={{0,4},{4,0},{8,12},{12,8},{1,5},{5,1},{9,13},{13,9},{2,6},{6,2},{1... | collective-permute-start | bytes 1572872 | tf_op jit(solution)/shard_map/ppermute | solution.py:421

commit v13 on v10

--- a/solution.py
+++ b/solution.py
@@ -205,7 +205,8 @@
         crosses = [dot_nt(high, low) for high, low in halves]
         grams = [dot_nt(high, high) + (cross + cross.T) for (high, low), cross in zip(halves, crosses)]
         gram_halves = [split(gram) for gram in grams]
-        squares = [dot(high, high) + (dot(high, low) + dot(low, high)) for high, low in gram_halves]
+        crosses = [dot(high, low) for high, low in gram_halves]
+        squares = [dot(high, high) + (cross + cross.T) for (high, low), cross in zip(gram_halves, crosses)]
         polys = [split(quintic_b * gram + quintic_c * square) for gram, square in zip(grams, squares)]
         for i in range(3):
             (poly_high, poly_low), (high, low) = polys[i], halves[i]

time: 136 us -> 135 us (level)
  transfers between devices with their start and end apart: 31 -> 31, of which waited for: 13 -> 13; matrix products, arithmetic and copies ran while one was open for 3% -> 3% of each run, Pallas kernels for 27% -> 26%
where the time goes in v13:
time: 135 us
  Pallas kernels  43.8 us (32%)
  waiting for transfers between devices  39.9 us (30%)
  starting transfers between devices  35.6 us (26%)
  local copies, waits for them, and re-layouts  12.7 us (9%)
  matrix products  2.25 us (2%)
    pallas_call x5, Pallas kernels, project(): pl.pallas_call(functools.partial(project_kernel, len(whole), len(pairs)),...  20.7 us
    ppermute x9, starting transfers between devices, hop(): return lax.ppermute(array, 'head', links)  18.6 us
    ppermute x9, waiting for transfers between devices, hop(): return lax.ppermute(array, 'head', links)  16.2 us
    ppermute x20, waiting for transfers between devices, across(): return lax.ppermute(array, 'seq', [(i, i ^ bit) for i in range(4)])  15.3 us
    ppermute x20, starting transfers between devices, across(): return lax.ppermute(array, 'seq', [(i, i ^ bit) for i in range(4)])  13.9 us
    pallas_call x1, Pallas kernels, update(): pl.pallas_call(update_kernel, out_shape=[out] * 3, grid_spec=pltpu.Prefet...  13.2 us
    ppermute x2, waiting for transfers between devices, swap_groups(): return lax.ppermute(array, 'groups', [(0, 1), (1, 0)])  8.38 us
    unnamed x20, local copies, waits for them, and re-layouts  5.67 us
  transfers between devices with their start and end apart: 31, of which 13 were waited for; matrix products, arithmetic and copies ran while one was open for 3% of the time, Pallas kernels for 26%

profile of v13, /device:TPU:0, one launch (start us, length us, event | category | flops | bytes accessed | tf_op | source)
XLA Modules:
  0.0 134.7 jit_solution(6049223317433683040)
XLA Ops:
  0.0 1.9 %constant_dynamic-slice_fusion.2 = bf16[256,1024]{1,0:T(8,128)(2,1)} fusion(bf16[256,4096]{1,0:T(8,128)(2,1)} %refs_0_.5, s32[]{:T(128)S(6)} %select_n.23), kind=kLoop, calls=%fused_computation.15 | loop fusion | bytes 1048580 | tf_op jit(solution)/shard_map/dynamic_slice | solution.py:430
  1.9 3.7 %dynamic-slice_bitcast_fusion = bf16[3,1024,512]{2,1,0:T(8,128)(2,1)} fusion(bf16[1024,3,1024]{2,0,1:T(8,128)(2,1)} %param.9, s32[]{:T(128)S(6)} %select_n.24), kind=kLoop, calls=%fused_computation | loop fusion | bytes 6291460 | tf_op jit(solution)/shard_map/dynamic_slice | solution.py:434
  5.6 0.5 collective-permute-start.1
  6.1 0.1 collective-permute-start
  6.1 2.9 %collective-permute-start.2 = (bf16[256,1024]{1,0:T(8,128)(2,1)}, bf16[256,1024]{1,0:T(8,128)(2,1)}, u32[]{:S(2)}, u32[]{:S(2)}) collective-permute-start(bf16[256,1024]{1,0:T(8,128)(2,1)} %constant_dynamic-slice_fusion.2), channel_id=1, source_target_pairs={{0,8},{4,12},{8,0},{12,4},{1,9},{5,13},{9,1},{13,5},{2,10},{6,14},... | collective-permute-start | bytes 1572872 | tf_op jit(solution)/shard_map/ppermute | solution.py:418
  9.1 0.1 stack.63.index_ref
  9.2 5.5 %collective-permute-done.refs_1_ = bf16[256,4096]{1,0:T(8,128)(2,1)} collective-permute-done((bf16[256,4096]{1,0:T(8,128)(2,1)}, bf16[256,4096]{1,0:T(8,128)(2,1)}, u32[]{:S(2)}, u32[]{:S(2)}) %collective-permute-start) | collective-permute-done | bytes 2097184 | tf_op jit(solution)/shard_map/ppermute | solution.py:418
  14.6 2.8 %copy-done.1 = bf16[1024,3,1024]{2,0,1:T(8,128)(2,1)S(1)} copy-done((bf16[1024,3,1024]{2,0,1:T(8,128)(2,1)S(1)}, bf16[1024,3,1024]{2,0,1:T(8,128)(2,1)}, u32[]{:S(2)}) %copy-start.1) | copy-done | bytes 6291480
  17.4 4.4 %shard_map.82 = bf16[2,512,256]{2,1,0:T(8,128)(2,1)} custom-call(s32[15]{0:T(128)S(1)} %stack.63.index_ref, bf16[256,4096]{1,0:T(8,128)(2,1)} %refs_0_.5, bf16[256,4096]{1,0:T(8,128)(2,1)} %collective-permute-done.refs_1_, bf16[3,1024,1024]{2,1,0:T(8,128)(2,1)S(1)} %bitcast.25, bf16[3,1024,512]{2,1,0:T(8,128)(2,1)S(1)} %collective-permute-done.1.refs_3_.refs_5_.refs_7_), custom_call_target="tpu_custom_call" | custom-call | flops 1 | bytes 1 | tf_op jit(solution)/shard_map/pallas_call | solution.py:146
  21.8 2.9 %collective-permute-start.3 = (bf16[256,1024]{1,0:T(8,128)(2,1)}, bf16[256,1024]{1,0:T(8,128)(2,1)}, u32[]{:S(2)}, u32[]{:S(2)}) collective-permute-start(bf16[256,1024]{1,0:T(8,128)(2,1)} %collective-permute-done.2.refs_0_.refs_2_), channel_id=1, source_target_pairs={{0,1},{1,0},{2,3},{3,2},{4,5},{5,4},{6,7},{7,6},{8,9},{9,8},{10,11... | collective-permute-start | bytes 1572872 | tf_op jit(solution)/shard_map/ppermute | solution.py:421
  24.7 1.5 %collective-permute-start.4 = (bf16[2,512,256]{2,1,0:T(8,128)(2,1)}, bf16[2,512,256]{2,1,0:T(8,128)(2,1)}, u32[]{:S(2)}, u32[]{:S(2)}) collective-permute-start(bf16[2,512,256]{2,1,0:T(8,128)(2,1)} %shard_map.82), channel_id=1, source_target_pairs={{0,8},{4,12},{8,0},{12,4},{1,9},{5,13},{9,1},{13,5},{2,10},{6,14},... | collective-permute-start | bytes 1572872 | tf_op jit(solution)/shard_map/ppermute | solution.py:418
  26.2 2.3 %compare_select_fusion = f32[4,256]{1,0:T(4,128)S(1)} fusion(bf16[256,4096]{1,0:T(8,128)(2,1)} %refs_0_.5, bf16[4096,4]{0,1:T(4,128)(2,1)S(1)} %copy-done), kind=kOutput, calls=%fused_computation.11 | convolution fusion | flops 8394752 | bytes 2134016 | tf_op jit(solution)/shard_map/dot_general | solution.py:446
  28.5 0.1 collective-permute-start.5
  28.6 0.5 collective-permute-start.7
  29.1 0.7 collective-permute-done.5
  29.7 0.5 collective-permute-start.6
  30.3 1.3 constant_dynamic-slice_fusion.1
  31.5 0.0 copy-start.2
  31.5 2.8 %copy-done.2 = bf16[1024,3,1024]{2,0,1:T(8,128)(2,1)S(1)} copy-done((bf16[1024,3,1024]{2,0,1:T(8,128)(2,1)S(1)}, bf16[1024,3,1024]{2,0,1:T(8,128)(2,1)}, u32[]{:S(2)}) %copy-start.2) | copy-done | bytes 6291480
  34.3 4.6 %shard_map.83.local_near_ref = f32[3,512,256]{2,1,0:T(8,128)S(1)} custom-call(s32[15]{0:T(128)S(1)} %stack.63.index_ref, bf16[256,4096]{1,0:T(8,128)(2,1)} %refs_0_.5, bf16[256,4096]{1,0:T(8,128)(2,1)} %collective-permute-done.refs_1_, bf16[3,1024,1024]{2,1,0:T(8,128)(2,1)S(1)} %bitcast.26, ...), custom_call_target="tpu_custom_call" | custom-call | flops 1 | bytes 1 | tf_op jit(solution)/shard_map/pallas_call | solution.py:146
  38.9 0.0 copy-start.3
  38.9 0.1 collective-permute-start.8
  39.0 2.1 %collective-permute-done.8.refs_3_.refs_5_ = bf16[256,1024]{1,0:T(8,128)(2,1)S(1)} collective-permute-done((bf16[256,1024]{1,0:T(8,128)(2,1)}, bf16[256,1024]{1,0:T(8,128)(2,1)S(1)}, u32[]{:S(2)}, u32[]{:S(2)}) %collective-permute-start.8) | collective-permute-done | bytes 524320 | tf_op jit(solution)/shard_map/ppermute | solution.py:418
  41.1 3.4 %shard_map.84 = bf16[2,512,256]{2,1,0:T(8,128)(2,1)S(1)} custom-call(s32[15]{0:T(128)S(1)} %stack.63.index_ref, bf16[256,1024]{1,0:T(8,128)(2,1)} %collective-permute-done.2.refs_0_.refs_2_, bf16[256,1024]{1,0:T(8,128)(2,1)} %collective-permute-done.3.refs_1_.refs_3_, bf16[256,1024]{1,0:T(8,128)(2,1)S(1)} %collective-permute-done.7.refs_2_.refs_4_, ...), custom_call_target="tpu_custom_call" | custom-call | flops 1 | bytes 1 | tf_op jit(solution)/shard_map/pallas_call | solution.py:146
  44.5 0.2 collective-permute-start.9
  44.7 1.5 %collective-permute-start.10 = (bf16[2,512,256]{2,1,0:T(8,128)(2,1)S(1)}, bf16[2,512,256]{2,1,0:T(8,128)(2,1)S(1)}, u32[]{:S(2)}, u32[]{:S(2)}) collective-permute-start(bf16[2,512,256]{2,1,0:T(8,128)(2,1)S(1)} %shard_map.84), channel_id=1, source_target_pairs={{0,8},{4,12},{8,0},{12,4},{1,9},{5,13},{9,1},{13,5},{2,10},{6,14},... | collective-permute-start | bytes 1572872 | tf_op jit(solution)/shard_map/ppermute | solution.py:418
  46.2 3.9 %shard_map.85 = bf16[1,1024,256]{2,1,0:T(8,128)(2,1)S(1)} custom-call(s32[15]{0:T(128)S(1)} %stack.63.index_ref, bf16[256,4096]{1,0:T(8,128)(2,1)} %refs_0_.5, bf16[256,4096]{1,0:T(8,128)(2,1)} %collective-permute-done.refs_1_, bf16[256,1024]{1,0:T(8,128)(2,1)} %collective-permute-done.2.refs_0_.refs_2_, ...), custom_call_target="tpu_custom_call" | custom-call | flops 1 | bytes 1 | tf_op jit(solution)/shard_map/pallas_call | solution.py:146
  50.2 0.0 copy-start.4
  50.2 0.0 copy-start.5
  50.2 0.0 copy-start.6
  50.2 4.4 %shard_map.86.local_far_ref = f32[3,512,256]{2,1,0:T(8,128)S(1)} custom-call(s32[15]{0:T(128)S(1)} %stack.63.index_ref, bf16[256,1024]{1,0:T(8,128)(2,1)} %collective-permute-done.2.refs_0_.refs_2_, bf16[256,1024]{1,0:T(8,128)(2,1)} %collective-permute-done.3.refs_1_.refs_3_, bf16[256,1024]{1,0:T(8,128)(2,1)S(1)} %collective-permute-done.7.refs_2_.refs_4_, ...), custom_call_target="tpu_custom_call" | custom-call | flops 1 | bytes 1 | tf_op jit(solution)/shard_map/pallas_call | solution.py:146
  54.7 0.0 copy-start.7
  54.7 4.2 %collective-permute-done.10.near_ref = bf16[2,512,256]{2,1,0:T(8,128)(2,1)S(1)} collective-permute-done((bf16[2,512,256]{2,1,0:T(8,128)(2,1)S(1)}, bf16[2,512,256]{2,1,0:T(8,128)(2,1)S(1)}, u32[]{:S(2)}, u32[]{:S(2)}) %collective-permute-start.10) | collective-permute-done | bytes 524320 | tf_op jit(solution)/shard_map/ppermute | solution.py:418
  58.9 1.5 %collective-permute-start.11 = (bf16[1,1024,256]{2,1,0:T(8,128)(2,1)S(1)}, bf16[1,1024,256]{2,1,0:T(8,128)(2,1)S(1)}, u32[]{:S(2)}, u32[]{:S(2)}) collective-permute-start(bf16[1,1024,256]{2,1,0:T(8,128)(2,1)S(1)} %shard_map.85), channel_id=1, source_target_pairs={{0,8},{4,12},{8,0},{12,4},{1,9},{5,13},{9,1},{13,5},{2,10},{6,14},... | collective-permute-start | bytes 1572872 | tf_op jit(solution)/shard_map/ppermute | solution.py:418
  60.4 13.2 %shard_map.87 = (bf16[256,512]{1,0:T(8,128)(2,1)S(1)}, bf16[256,512]{1,0:T(8,128)(2,1)S(1)}, bf16[256,512]{1,0:T(8,128)(2,1)S(1)}) custom-call(s32[15]{0:T(128)S(1)} %stack.63.index_ref, f32[3,512,256]{2,1,0:T(8,128)S(1)} %shard_map.83.local_near_ref, f32[3,512,256]{2,1,0:T(8,128)S(1)} %shard_map.86.local_far_ref, ...), custom_call_target="tpu_custom_call" | custom-call | flops 1 | bytes 1 | tf_op jit(solution)/shard_map/pallas_call | solution.py:231
  73.7 2.0 %shard_map.88 = (bf16[256,256]{1,0:T(8,128)(2,1)S(1)}, bf16[256,256]{1,0:T(8,128)(2,1)S(1)}, bf16[256,256]{1,0:T(8,128)(2,1)S(1)}, bf16[256,256]{1,0:T(8,128)(2,1)S(1)}) custom-call(s32[15]{0:T(128)S(1)} %stack.63.index_ref, f32[3,512,256]{2,1,0:T(8,128)S(1)} %shard_map.83.local_near_ref, f32[3,512,256]{2,1,0:T(8,128)S(1)} %shard_map.86.local_far_ref, ...), custom_call_target="tpu_custom_call" | custom-call | flops 1 | bytes 1 | tf_op jit(solution)/shard_map/pallas_call | solution.py:277
  75.7 0.1 collective-permute-start.12
  75.8 0.6 collective-permute-start.14
  76.4 1.3 collective-permute-start.15
  77.7 1.3 collective-permute-start.19
  79.0 4.6 %collective-permute-start.13 = (bf16[256,512]{1,0:T(8,128)(2,1)S(1)}, bf16[256,512]{1,0:T(8,128)(2,1)S(1)}, u32[]{:S(2)}, u32[]{:S(2)}) collective-permute-start(bf16[256,512]{1,0:T(8,128)(2,1)S(1)} %constant_dynamic-update-slice_fusion), channel_id=1, source_target_pairs={{0,1},{1,2},{2,3},{4,5},{5,6},{6,7},{8,9},{9,10},{10,11},{12,13},{... | collective-permute-start | bytes 786440 | tf_op jit(solution)/shard_map/ppermute | solution.py:421
  83.6 0.5 collective-permute-done.15
  84.1 1.3 collective-permute-start.20
  85.4 0.6 collective-permute-start.23
  86.0 4.5 %collective-permute-start.16 = (bf16[256,512]{1,0:T(8,128)(2,1)S(1)}, bf16[256,512]{1,0:T(8,128)(2,1)S(1)}, u32[]{:S(2)}, u32[]{:S(2)}) collective-permute-start(bf16[256,512]{1,0:T(8,128)(2,1)S(1)} %constant_dynamic-update-slice_fusion.2), channel_id=1, source_target_pairs={{0,1},{1,2},{2,3},{4,5},{5,6},{6,7},{8,9},{9,10},{10,11},{12,13},{... | collective-permute-start | bytes 786440 | tf_op jit(solution)/shard_map/ppermute | solution.py:421
  90.6 4.2 %collective-permute-done.20 = bf16[256,512]{1,0:T(8,128)(2,1)S(1)} collective-permute-done((bf16[256,512]{1,0:T(8,128)(2,1)S(1)}, bf16[256,512]{1,0:T(8,128)(2,1)S(1)}, u32[]{:S(2)}, u32[]{:S(2)}) %collective-permute-start.20) | collective-permute-done | bytes 262176 | tf_op jit(solution)/shard_map/ppermute | solution.py:421
  94.8 1.3 collective-permute-start.21
  96.1 0.1 collective-permute-done.16
  96.3 0.7 collective-permute-start.17
  97.0 1.6 %collective-permute-start.27 = (bf16[256,1024]{1,0:T(8,128)(2,1)S(1)}, bf16[256,1024]{1,0:T(8,128)(2,1)S(1)}, u32[]{:S(2)}, u32[]{:S(2)}) collective-permute-start(bf16[256,1024]{1,0:T(8,128)(2,1)S(1)} %get-tuple-element.57), channel_id=1, source_target_pairs={{0,8},{4,12},{8,0},{12,4},{1,9},{5,13},{9,1},{13,5},{2,10},{6,14},... | collective-permute-start | bytes 1572872 | tf_op jit(solution)/shard_map/ppermute | solution.py:418
  98.5 1.6 %collective-permute-done.23.one = bf16[256,1024]{1,0:T(8,128)(2,1)S(1)} collective-permute-done((bf16[256,1024]{1,0:T(8,128)(2,1)S(1)}, bf16[256,1024]{1,0:T(8,128)(2,1)S(1)}, u32[]{:S(2)}, u32[]{:S(2)}) %collective-permute-start.23) | collective-permute-done | bytes 524320 | tf_op jit(solution)/shard_map/ppermute | solution.py:418
  100.1 1.6 %collective-permute-start.24 = (bf16[256,1024]{1,0:T(8,128)(2,1)S(1)}, bf16[256,1024]{1,0:T(8,128)(2,1)S(1)}, u32[]{:S(2)}, u32[]{:S(2)}) collective-permute-start(bf16[256,1024]{1,0:T(8,128)(2,1)S(1)} %collective-permute-done.23.one), channel_id=1, source_target_pairs={{0,16},{16,0},{1,17},{17,1},{2,18},{18,2},{3,19},{19,3},{4,20},{20... | collective-permute-start | bytes 1572872 | tf_op jit(solution)/shard_map/ppermute | solution.py:475
  101.7 8.6 %collective-permute-done.21.above_2 = bf16[256,1024]{1,0:T(8,128)(2,1)S(1)} collective-permute-done((bf16[256,1024]{1,0:T(8,128)(2,1)S(1)}, bf16[256,1024]{1,0:T(8,128)(2,1)S(1)}, u32[]{:S(2)}, u32[]{:S(2)}) %collective-permute-start.21) | collective-permute-done | bytes 524320 | tf_op jit(solution)/shard_map/ppermute | solution.py:421
  110.3 0.8 collective-permute-done.27.one
  111.1 2.4 %collective-permute-done.24.other = bf16[256,1024]{1,0:T(8,128)(2,1)S(1)} collective-permute-done((bf16[256,1024]{1,0:T(8,128)(2,1)S(1)}, bf16[256,1024]{1,0:T(8,128)(2,1)S(1)}, u32[]{:S(2)}, u32[]{:S(2)}) %collective-permute-start.24) | collective-permute-done | bytes 524320 | tf_op jit(solution)/shard_map/ppermute | solution.py:475
  113.5 1.6 %collective-permute-start.28 = (bf16[256,1024]{1,0:T(8,128)(2,1)S(1)}, bf16[256,1024]{1,0:T(8,128)(2,1)S(1)}, u32[]{:S(2)}, u32[]{:S(2)}) collective-permute-start(bf16[256,1024]{1,0:T(8,128)(2,1)S(1)} %collective-permute-done.27.one), channel_id=1, source_target_pairs={{0,16},{16,0},{1,17},{17,1},{2,18},{18,2},{3,19},{19,3},{4,20},{20... | collective-permute-start | bytes 1572872 | tf_op jit(solution)/shard_map/ppermute | solution.py:475
  115.0 0.1 pad_maximum_fusion.own
  115.1 1.3 collective-permute-start.22
  116.4 0.7 collective-permute-start.18
  117.1 4.7 %shard_map.89 = (f32[256,1024]{1,0:T(8,128)S(1)}, bf16[256,1024]{1,0:T(8,128)(2,1)S(1)}, bf16[1024,1024]{1,0:T(8,128)(2,1)S(1)}) custom-call(s32[15]{0:T(128)S(1)} %stack.63.index_ref, bf16[256,1024]{1,0:T(8,128)(2,1)S(1)} %pad_maximum_fusion.own, bf16[256,1024]{1,0:T(8,128)(2,1)S(1)} %constant_dynamic-update-slice_fusion.4.below_1, ...), custom_call_target="tpu_custom_call" | custom-call | flops 1 | bytes 1 | tf_op jit(solution)/shard_map/pallas_call | solution.py:344
  121.8 6.0 %collective-permute-done.28.other = bf16[256,1024]{1,0:T(8,128)(2,1)S(1)} collective-permute-done((bf16[256,1024]{1,0:T(8,128)(2,1)S(1)}, bf16[256,1024]{1,0:T(8,128)(2,1)S(1)}, u32[]{:S(2)}, u32[]{:S(2)}) %collective-permute-start.28) | collective-permute-done | bytes 524320 | tf_op jit(solution)/shard_map/ppermute | solution.py:475
  127.8 0.5 collective-permute-start.30
  128.3 3.3 %collective-permute-done.22.above = bf16[256,1024]{1,0:T(8,128)(2,1)S(1)} collective-permute-done((bf16[256,1024]{1,0:T(8,128)(2,1)S(1)}, bf16[256,1024]{1,0:T(8,128)(2,1)S(1)}, u32[]{:S(2)}, u32[]{:S(2)}) %collective-permute-start.22) | collective-permute-done | bytes 524320 | tf_op jit(solution)/shard_map/ppermute | solution.py:421
  131.6 3.1 %shard_map.90 = bf16[256,1024]{1,0:T(8,128)(2,1)} custom-call(s32[15]{0:T(128)S(1)} %stack.63.index_ref, bf16[256,1024]{1,0:T(8,128)(2,1)S(1)} %collective-permute-done.18.below, bf16[256,1024]{1,0:T(8,128)(2,1)S(1)} %collective-permute-done.22.above, bf16[1024,1024]{1,0:T(8,128)(2,1)S(1)} %get-tuple-element.55.weight, ...), custom_call_target="tpu_custom_call" | custom-call | flops 1 | bytes 1 | tf_op jit(solution)/shard_map/pallas_call | solution.py:388
  (38 shorter events, 0.2 us)
Async XLA Ops:
  0.0 26.2 %copy-start = (bf16[4096,4]{0,1:T(4,128)(2,1)S(1)}, bf16[4096,4]{0,1:T(4,128)(2,1)}, u32[]{:S(2)}) copy-start(bf16[4096,4]{0,1:T(4,128)(2,1)} %param.10) | copy-start | bytes 98308
  5.6 9.0 %collective-permute-start.1 = (bf16[3,1024,512]{2,1,0:T(8,128)(2,1)}, bf16[3,1024,512]{2,1,0:T(8,128)(2,1)S(1)}, u32[]{:S(2)}, u32[]{:S(2)}) collective-permute-start(bf16[3,1024,512]{2,1,0:T(8,128)(2,1)} %dynamic-slice_bitcast_fusion), channel_id=1, source_target_pairs={{0,4},{4,0},{8,12},{12,8},{1,5},{5,1},{9,13},{13,9},{2,6},{6,2},{1... | collective-permute-start | bytes 9437192 | tf_op jit(solution)/shard_map/ppermute | solution.py:418
  6.1 8.5 %collective-permute-start = (bf16[256,4096]{1,0:T(8,128)(2,1)}, bf16[256,4096]{1,0:T(8,128)(2,1)}, u32[]{:S(2)}, u32[]{:S(2)}) collective-permute-start(bf16[256,4096]{1,0:T(8,128)(2,1)} %refs_0_.5), channel_id=1, source_target_pairs={{0,4},{4,0},{8,12},{12,8},{1,5},{5,1},{9,13},{13,9},{2,6},{6,2},{1... | collective-permute-start | bytes 6291464 | tf_op jit(solution)/shard_map/ppermute | solution.py:418
  6.1 15.7 %collective-permute-start.2 = (bf16[256,1024]{1,0:T(8,128)(2,1)}, bf16[256,1024]{1,0:T(8,128)(2,1)}, u32[]{:S(2)}, u32[]{:S(2)}) collective-permute-start(bf16[256,1024]{1,0:T(8,128)(2,1)} %constant_dynamic-slice_fusion.2), channel_id=1, source_target_pairs={{0,8},{4,12},{8,0},{12,4},{1,9},{5,13},{9,1},{13,5},{2,10},{6,14},... | collective-permute-start | bytes 1572872 | tf_op jit(solution)/shard_map/ppermute | solution.py:418
  14.6 2.8 %copy-start.1 = (bf16[1024,3,1024]{2,0,1:T(8,128)(2,1)S(1)}, bf16[1024,3,1024]{2,0,1:T(8,128)(2,1)}, u32[]{:S(2)}) copy-start(bf16[1024,3,1024]{2,0,1:T(8,128)(2,1)} %param.9) | copy-start | bytes 18874372
  21.8 17.1 %collective-permute-start.3 = (bf16[256,1024]{1,0:T(8,128)(2,1)}, bf16[256,1024]{1,0:T(8,128)(2,1)}, u32[]{:S(2)}, u32[]{:S(2)}) collective-permute-start(bf16[256,1024]{1,0:T(8,128)(2,1)} %collective-permute-done.2.refs_0_.refs_2_), channel_id=1, source_target_pairs={{0,1},{1,0},{2,3},{3,2},{4,5},{5,4},{6,7},{7,6},{8,9},{9,8},{10,11... | collective-permute-start | bytes 1572872 | tf_op jit(solution)/shard_map/ppermute | solution.py:421
  24.7 14.2 %collective-permute-start.4 = (bf16[2,512,256]{2,1,0:T(8,128)(2,1)}, bf16[2,512,256]{2,1,0:T(8,128)(2,1)}, u32[]{:S(2)}, u32[]{:S(2)}) collective-permute-start(bf16[2,512,256]{2,1,0:T(8,128)(2,1)} %shard_map.82), channel_id=1, source_target_pairs={{0,8},{4,12},{8,0},{12,4},{1,9},{5,13},{9,1},{13,5},{2,10},{6,14},... | collective-permute-start | bytes 1572872 | tf_op jit(solution)/shard_map/ppermute | solution.py:418
  28.5 1.2 collective-permute-start.5
  28.6 10.4 %collective-permute-start.7 = (bf16[256,1024]{1,0:T(8,128)(2,1)}, bf16[256,1024]{1,0:T(8,128)(2,1)S(1)}, u32[]{:S(2)}, u32[]{:S(2)}) collective-permute-start(bf16[256,1024]{1,0:T(8,128)(2,1)} %collective-permute-done.2.refs_0_.refs_2_), channel_id=1, source_target_pairs={{0,4},{4,0},{8,12},{12,8},{1,5},{5,1},{9,13},{13,9},{2,6},{6,2},{1... | collective-permute-start | bytes 1572872 | tf_op jit(solution)/shard_map/ppermute | solution.py:418
  29.7 9.2 %collective-permute-start.6 = (f32[8,256]{1,0:T(8,128)S(1)}, f32[8,256]{1,0:T(8,128)S(1)}, u32[]{:S(2)}, u32[]{:S(2)}) collective-permute-start(f32[8,256]{1,0:T(8,128)S(1)} %pad_maximum_fusion.1.rate_near_ref), channel_id=1, source_target_pairs={{0,8},{4,12},{8,0},{12,4},{1,9},{5,13},{9,1},{13,5},{2,10},{6,14},... | collective-permute-start | bytes 24584 | tf_op jit(solution)/shard_map/ppermute | solution.py:418
  31.5 2.8 %copy-start.2 = (bf16[1024,3,1024]{2,0,1:T(8,128)(2,1)S(1)}, bf16[1024,3,1024]{2,0,1:T(8,128)(2,1)}, u32[]{:S(2)}) copy-start(bf16[1024,3,1024]{2,0,1:T(8,128)(2,1)} %param.9) | copy-start | bytes 18874372
  38.9 5.6 %copy-start.3 = (bf16[1024,1024]{1,0:T(8,128)(2,1)S(1)}, bf16[1024,1024]{1,0:T(8,128)(2,1)}, u32[]{:S(2)}) copy-start(bf16[1024,1024]{1,0:T(8,128)(2,1)} %own_w.1) | copy-start | bytes 6291460
  38.9 2.2 %collective-permute-start.8 = (bf16[256,1024]{1,0:T(8,128)(2,1)}, bf16[256,1024]{1,0:T(8,128)(2,1)S(1)}, u32[]{:S(2)}, u32[]{:S(2)}) collective-permute-start(bf16[256,1024]{1,0:T(8,128)(2,1)} %collective-permute-done.3.refs_1_.refs_3_), channel_id=1, source_target_pairs={{0,4},{4,0},{8,12},{12,8},{1,5},{5,1},{9,13},{13,9},{2,6},{6,2},{1... | collective-permute-start | bytes 1572872 | tf_op jit(solution)/shard_map/ppermute | solution.py:418
  44.5 5.7 %collective-permute-start.9 = (bf16[1024,1024]{1,0:T(8,128)(2,1)S(1)}, bf16[1024,1024]{1,0:T(8,128)(2,1)S(1)}, u32[]{:S(2)}, u32[]{:S(2)}) collective-permute-start(bf16[1024,1024]{1,0:T(8,128)(2,1)S(1)} %copy-done.3), channel_id=1, source_target_pairs={{0,4},{4,0},{8,12},{12,8},{1,5},{5,1},{9,13},{13,9},{2,6},{6,2},{1... | collective-permute-start | bytes 6291464 | tf_op jit(solution)/shard_map/ppermute | solution.py:418
  44.7 14.2 %collective-permute-start.10 = (bf16[2,512,256]{2,1,0:T(8,128)(2,1)S(1)}, bf16[2,512,256]{2,1,0:T(8,128)(2,1)S(1)}, u32[]{:S(2)}, u32[]{:S(2)}) collective-permute-start(bf16[2,512,256]{2,1,0:T(8,128)(2,1)S(1)} %shard_map.84), channel_id=1, source_target_pairs={{0,8},{4,12},{8,0},{12,4},{1,9},{5,13},{9,1},{13,5},{2,10},{6,14},... | collective-permute-start | bytes 1572872 | tf_op jit(solution)/shard_map/ppermute | solution.py:418
  50.2 10.2 %copy-start.4 = (bf16[4,256,512]{2,1,0:T(8,128)(2,1)S(1)}, bf16[4,256,512]{2,1,0:T(8,128)(2,1)}, u32[]{:S(2)}) copy-start(bf16[4,256,512]{2,1,0:T(8,128)(2,1)} %gate_ref.1) | copy-start | bytes 3145732
  50.2 10.2 %copy-start.5 = (bf16[4,256,512]{2,1,0:T(8,128)(2,1)S(1)}, bf16[4,256,512]{2,1,0:T(8,128)(2,1)}, u32[]{:S(2)}) copy-start(bf16[4,256,512]{2,1,0:T(8,128)(2,1)} %up_ref.1) | copy-start | bytes 3145732
  50.2 10.2 %copy-start.6 = (bf16[4,256,512]{2,1,0:T(8,128)(2,1)S(1)}, bf16[4,256,512]{2,1,0:T(8,128)(2,1)}, u32[]{:S(2)}) copy-start(bf16[4,256,512]{2,1,0:T(8,128)(2,1)} %down_ref.1) | copy-start | bytes 3145732
  54.7 19.0 %copy-start.7 = (f32[1024]{0:T(1024)S(1)}, f32[1024]{0:T(1024)}, u32[]{:S(2)}) copy-start(f32[1024]{0:T(1024)} %param.14) | copy-start | bytes 12292
  58.9 14.8 %collective-permute-start.11 = (bf16[1,1024,256]{2,1,0:T(8,128)(2,1)S(1)}, bf16[1,1024,256]{2,1,0:T(8,128)(2,1)S(1)}, u32[]{:S(2)}, u32[]{:S(2)}) collective-permute-start(bf16[1,1024,256]{2,1,0:T(8,128)(2,1)S(1)} %shard_map.85), channel_id=1, source_target_pairs={{0,8},{4,12},{8,0},{12,4},{1,9},{5,13},{9,1},{13,5},{2,10},{6,14},... | collective-permute-start | bytes 1572872 | tf_op jit(solution)/shard_map/ppermute | solution.py:418
  75.7 2.0 %collective-permute-start.12 = (bf16[256,256]{1,0:T(8,128)(2,1)S(1)}, bf16[256,256]{1,0:T(8,128)(2,1)S(1)}, u32[]{:S(2)}, u32[]{:S(2)}) collective-permute-start(bf16[256,256]{1,0:T(8,128)(2,1)S(1)} %get-tuple-element.48), channel_id=1, source_target_pairs={{0,4},{4,0},{8,12},{12,8},{1,5},{5,1},{9,13},{13,9},{2,6},{6,2},{1... | collective-permute-start | bytes 393224 | tf_op jit(solution)/shard_map/ppermute | solution.py:418
  75.8 7.8 %collective-permute-start.14 = (bf16[256,256]{1,0:T(8,128)(2,1)S(1)}, bf16[256,256]{1,0:T(8,128)(2,1)S(1)}, u32[]{:S(2)}, u32[]{:S(2)}) collective-permute-start(bf16[256,256]{1,0:T(8,128)(2,1)S(1)} %get-tuple-element.49), channel_id=1, source_target_pairs={{0,8},{4,12},{8,0},{12,4},{1,9},{5,13},{9,1},{13,5},{2,10},{6,14},... | collective-permute-start | bytes 393224 | tf_op jit(solution)/shard_map/ppermute | solution.py:418
  76.4 7.7 %collective-permute-start.15 = (bf16[256,256]{1,0:T(8,128)(2,1)S(1)}, bf16[256,256]{1,0:T(8,128)(2,1)S(1)}, u32[]{:S(2)}, u32[]{:S(2)}) collective-permute-start(bf16[256,256]{1,0:T(8,128)(2,1)S(1)} %get-tuple-element.50), channel_id=1, source_target_pairs={{0,12},{4,8},{8,4},{12,0},{1,13},{5,9},{9,5},{13,1},{2,14},{6,10},... | collective-permute-start | bytes 393224 | tf_op jit(solution)/shard_map/ppermute | solution.py:418
  77.7 12.8 %collective-permute-start.19 = (bf16[256,512]{1,0:T(8,128)(2,1)S(1)}, bf16[256,512]{1,0:T(8,128)(2,1)S(1)}, u32[]{:S(2)}, u32[]{:S(2)}) collective-permute-start(bf16[256,512]{1,0:T(8,128)(2,1)S(1)} %constant_dynamic-update-slice_fusion), channel_id=1, source_target_pairs={{1,0},{2,1},{3,2},{5,4},{6,5},{7,6},{9,8},{10,9},{11,10},{13,12},{... | collective-permute-start | bytes 786440 | tf_op jit(solution)/shard_map/ppermute | solution.py:421
  79.0 11.6 %collective-permute-start.13 = (bf16[256,512]{1,0:T(8,128)(2,1)S(1)}, bf16[256,512]{1,0:T(8,128)(2,1)S(1)}, u32[]{:S(2)}, u32[]{:S(2)}) collective-permute-start(bf16[256,512]{1,0:T(8,128)(2,1)S(1)} %constant_dynamic-update-slice_fusion), channel_id=1, source_target_pairs={{0,1},{1,2},{2,3},{4,5},{5,6},{6,7},{8,9},{9,10},{10,11},{12,13},{... | collective-permute-start | bytes 786440 | tf_op jit(solution)/shard_map/ppermute | solution.py:421
  84.1 10.7 %collective-permute-start.20 = (bf16[256,512]{1,0:T(8,128)(2,1)S(1)}, bf16[256,512]{1,0:T(8,128)(2,1)S(1)}, u32[]{:S(2)}, u32[]{:S(2)}) collective-permute-start(bf16[256,512]{1,0:T(8,128)(2,1)S(1)} %constant_dynamic-update-slice_fusion.2), channel_id=1, source_target_pairs={{1,0},{2,1},{3,2},{5,4},{6,5},{7,6},{9,8},{10,9},{11,10},{13,12},{... | collective-permute-start | bytes 786440 | tf_op jit(solution)/shard_map/ppermute | solution.py:421
  85.4 14.8 %collective-permute-start.23 = (bf16[256,1024]{1,0:T(8,128)(2,1)S(1)}, bf16[256,1024]{1,0:T(8,128)(2,1)S(1)}, u32[]{:S(2)}, u32[]{:S(2)}) collective-permute-start(bf16[256,1024]{1,0:T(8,128)(2,1)S(1)} %get-tuple-element.51), channel_id=1, source_target_pairs={{0,8},{4,12},{8,0},{12,4},{1,9},{5,13},{9,1},{13,5},{2,10},{6,14},... | collective-permute-start | bytes 1572872 | tf_op jit(solution)/shard_map/ppermute | solution.py:418
  86.0 10.3 %collective-permute-start.16 = (bf16[256,512]{1,0:T(8,128)(2,1)S(1)}, bf16[256,512]{1,0:T(8,128)(2,1)S(1)}, u32[]{:S(2)}, u32[]{:S(2)}) collective-permute-start(bf16[256,512]{1,0:T(8,128)(2,1)S(1)} %constant_dynamic-update-slice_fusion.2), channel_id=1, source_target_pairs={{0,1},{1,2},{2,3},{4,5},{5,6},{6,7},{8,9},{9,10},{10,11},{12,13},{... | collective-permute-start | bytes 786440 | tf_op jit(solution)/shard_map/ppermute | solution.py:421
  94.8 15.5 %collective-permute-start.21 = (bf16[256,1024]{1,0:T(8,128)(2,1)S(1)}, bf16[256,1024]{1,0:T(8,128)(2,1)S(1)}, u32[]{:S(2)}, u32[]{:S(2)}) collective-permute-start(bf16[256,1024]{1,0:T(8,128)(2,1)S(1)} %constant_dynamic-update-slice_fusion.6.above_1), channel_id=1, source_target_pairs={{1,0},{2,1},{5,4},{6,5},{9,8},{10,9},{13,12},{14,13},{17,16},{18,1... | collective-permute-start | bytes 1572872 | tf_op jit(solution)/shard_map/ppermute | solution.py:421
  96.3 14.0 %collective-permute-start.17 = (bf16[256,1024]{1,0:T(8,128)(2,1)S(1)}, bf16[256,1024]{1,0:T(8,128)(2,1)S(1)}, u32[]{:S(2)}, u32[]{:S(2)}) collective-permute-start(bf16[256,1024]{1,0:T(8,128)(2,1)S(1)} %constant_dynamic-update-slice_fusion.4.below_1), channel_id=1, source_target_pairs={{1,2},{2,3},{5,6},{6,7},{9,10},{10,11},{13,14},{14,15},{17,18},{18... | collective-permute-start | bytes 1572872 | tf_op jit(solution)/shard_map/ppermute | solution.py:421
  97.0 14.1 %collective-permute-start.27 = (bf16[256,1024]{1,0:T(8,128)(2,1)S(1)}, bf16[256,1024]{1,0:T(8,128)(2,1)S(1)}, u32[]{:S(2)}, u32[]{:S(2)}) collective-permute-start(bf16[256,1024]{1,0:T(8,128)(2,1)S(1)} %get-tuple-element.57), channel_id=1, source_target_pairs={{0,8},{4,12},{8,0},{12,4},{1,9},{5,13},{9,1},{13,5},{2,10},{6,14},... | collective-permute-start | bytes 1572872 | tf_op jit(solution)/shard_map/ppermute | solution.py:418
  100.1 13.3 %collective-permute-start.24 = (bf16[256,1024]{1,0:T(8,128)(2,1)S(1)}, bf16[256,1024]{1,0:T(8,128)(2,1)S(1)}, u32[]{:S(2)}, u32[]{:S(2)}) collective-permute-start(bf16[256,1024]{1,0:T(8,128)(2,1)S(1)} %collective-permute-done.23.one), channel_id=1, source_target_pairs={{0,16},{16,0},{1,17},{17,1},{2,18},{18,2},{3,19},{19,3},{4,20},{20... | collective-permute-start | bytes 1572872 | tf_op jit(solution)/shard_map/ppermute | solution.py:475
  111.1 6.0 %collective-permute-start.25 = (bf16[256,1024]{1,0:T(8,128)(2,1)S(1)}, bf16[256,1024]{1,0:T(8,128)(2,1)S(1)}, u32[]{:S(2)}, u32[]{:S(2)}) collective-permute-start(bf16[256,1024]{1,0:T(8,128)(2,1)S(1)} %collective-permute-done.23.one), channel_id=1, source_target_pairs={{0,4},{4,0},{8,12},{12,8},{1,5},{5,1},{9,13},{13,9},{2,6},{6,2},{1... | collective-permute-start | bytes 1572872 | tf_op jit(solution)/shard_map/ppermute | solution.py:418
  113.5 3.6 %collective-permute-start.26 = (bf16[256,1024]{1,0:T(8,128)(2,1)S(1)}, bf16[256,1024]{1,0:T(8,128)(2,1)S(1)}, u32[]{:S(2)}, u32[]{:S(2)}) collective-permute-start(bf16[256,1024]{1,0:T(8,128)(2,1)S(1)} %collective-permute-done.24.other), channel_id=1, source_target_pairs={{0,4},{4,0},{8,12},{12,8},{1,5},{5,1},{9,13},{13,9},{2,6},{6,2},{1... | collective-permute-start | bytes 1572872 | tf_op jit(solution)/shard_map/ppermute | solution.py:418
  113.5 14.3 %collective-permute-start.28 = (bf16[256,1024]{1,0:T(8,128)(2,1)S(1)}, bf16[256,1024]{1,0:T(8,128)(2,1)S(1)}, u32[]{:S(2)}, u32[]{:S(2)}) collective-permute-start(bf16[256,1024]{1,0:T(8,128)(2,1)S(1)} %collective-permute-done.27.one), channel_id=1, source_target_pairs={{0,16},{16,0},{1,17},{17,1},{2,18},{18,2},{3,19},{19,3},{4,20},{20... | collective-permute-start | bytes 1572872 | tf_op jit(solution)/shard_map/ppermute | solution.py:475
  115.1 16.5 %collective-permute-start.22 = (bf16[256,1024]{1,0:T(8,128)(2,1)S(1)}, bf16[256,1024]{1,0:T(8,128)(2,1)S(1)}, u32[]{:S(2)}, u32[]{:S(2)}) collective-permute-start(bf16[256,1024]{1,0:T(8,128)(2,1)S(1)} %collective-permute-done.21.above_2), channel_id=1, source_target_pairs={{1,0},{5,4},{9,8},{13,12},{17,16},{21,20},{25,24},{29,28}} | collective-permute-start | bytes 1572872 | tf_op jit(solution)/shard_map/ppermute | solution.py:421
  116.4 15.2 %collective-permute-start.18 = (bf16[256,1024]{1,0:T(8,128)(2,1)S(1)}, bf16[256,1024]{1,0:T(8,128)(2,1)S(1)}, u32[]{:S(2)}, u32[]{:S(2)}) collective-permute-start(bf16[256,1024]{1,0:T(8,128)(2,1)S(1)} %collective-permute-done.17.below_2), channel_id=1, source_target_pairs={{2,3},{6,7},{10,11},{14,15},{18,19},{22,23},{26,27},{30,31}} | collective-permute-start | bytes 1572872 | tf_op jit(solution)/shard_map/ppermute | solution.py:421
  127.8 3.8 %collective-permute-start.29 = (bf16[256,1024]{1,0:T(8,128)(2,1)S(1)}, bf16[256,1024]{1,0:T(8,128)(2,1)S(1)}, u32[]{:S(2)}, u32[]{:S(2)}) collective-permute-start(bf16[256,1024]{1,0:T(8,128)(2,1)S(1)} %collective-permute-done.27.one), channel_id=1, source_target_pairs={{0,4},{4,0},{8,12},{12,8},{1,5},{5,1},{9,13},{13,9},{2,6},{6,2},{1... | collective-permute-start | bytes 1572872 | tf_op jit(solution)/shard_map/ppermute | solution.py:418
  127.8 3.8 %collective-permute-start.30 = (bf16[256,1024]{1,0:T(8,128)(2,1)S(1)}, bf16[256,1024]{1,0:T(8,128)(2,1)S(1)}, u32[]{:S(2)}, u32[]{:S(2)}) collective-permute-start(bf16[256,1024]{1,0:T(8,128)(2,1)S(1)} %collective-permute-done.28.other), channel_id=1, source_target_pairs={{0,4},{4,0},{8,12},{12,8},{1,5},{5,1},{9,13},{13,9},{2,6},{6,2},{1... | collective-permute-start | bytes 1572872 | tf_op jit(solution)/shard_map/ppermute | solution.py:418

commit v14 on v13

--- a/solution.py
+++ b/solution.py
@@ -162,6 +162,10 @@
     )(index, *whole, *[block for pair in pairs for block in pair], weight, given)
 
 
+def half_tanh(value):
+    return 0.5 + 0.5 * jnp.tanh(0.5 * value)
+
+
 def split(value):
     high = value.astype(BF16)
     return high, (value - high.astype(F32)).astype(BF16)
@@ -185,7 +189,7 @@
         gate = dot(keys, gate_w)
         up = dot(keys, up_w)
         back = dot(scaled, down_w)
-        sigma = jax.nn.sigmoid(gate)
+        sigma = half_tanh(gate)
         active = gate * sigma
         hidden = (active * up).astype(BF16)
         dgate = (back * up * (sigma * (1.0 + gate * (1.0 - sigma)))).astype(BF16)
@@ -263,7 +267,7 @@
         queries = rms_scale(local_ref[0, here, :] + other_ref[0, there, :].astype(F32)).astype(BF16)
         gate = dot(queries, gate_w)
         up = dot(queries, up_w)
-        hidden = (gate * jax.nn.sigmoid(gate) * up).astype(BF16)
+        hidden = (gate * half_tanh(gate) * up).astype(BF16)
         read = dot_nt(hidden, down_w)
         out_ref[...] = (rms_scale(read) * gain_ref[0]).astype(BF16)
 

time: 135 us -> 135 us (level)
  no operation moved by 1% of the time
where the time goes in v14:
time: 135 us
  Pallas kernels  43.8 us (32%)
  waiting for transfers between devices  39.9 us (30%)
  starting transfers between devices  35.6 us (26%)
  local copies, waits for them, and re-layouts  12.7 us (9%)
  matrix products  2.25 us (2%)
    pallas_call x5, Pallas kernels, project(): pl.pallas_call(functools.partial(project_kernel, len(whole), len(pairs)),...  20.7 us
    ppermute x9, starting transfers between devices, hop(): return lax.ppermute(array, 'head', links)  18.6 us
    ppermute x9, waiting for transfers between devices, hop(): return lax.ppermute(array, 'head', links)  16.2 us
    ppermute x20, waiting for transfers between devices, across(): return lax.ppermute(array, 'seq', [(i, i ^ bit) for i in range(4)])  15.3 us
    ppermute x20, starting transfers between devices, across(): return lax.ppermute(array, 'seq', [(i, i ^ bit) for i in range(4)])  13.9 us
    pallas_call x1, Pallas kernels, update(): pl.pallas_call(update_kernel, out_shape=[out] * 3, grid_spec=pltpu.Prefet...  13.3 us
    ppermute x2, waiting for transfers between devices, swap_groups(): return lax.ppermute(array, 'groups', [(0, 1), (1, 0)])  8.37 us
    unnamed x20, local copies, waits for them, and re-layouts  5.67 us
  transfers between devices with their start and end apart: 31, of which 13 were waited for; matrix products, arithmetic and copies ran while one was open for 3% of the time, Pallas kernels for 26%

profile of v14, /device:TPU:0, one launch (start us, length us, event | category | flops | bytes accessed | tf_op | source)
XLA Modules:
  0.0 134.7 jit_solution(5897312719862739355)
XLA Ops:
  0.0 1.9 %constant_dynamic-slice_fusion.2 = bf16[256,1024]{1,0:T(8,128)(2,1)} fusion(bf16[256,4096]{1,0:T(8,128)(2,1)} %refs_0_.5, s32[]{:T(128)S(6)} %select_n.23), kind=kLoop, calls=%fused_computation.15 | loop fusion | bytes 1048580 | tf_op jit(solution)/shard_map/dynamic_slice | solution.py:434
  1.9 3.7 %dynamic-slice_bitcast_fusion = bf16[3,1024,512]{2,1,0:T(8,128)(2,1)} fusion(bf16[1024,3,1024]{2,0,1:T(8,128)(2,1)} %param.9, s32[]{:T(128)S(6)} %select_n.24), kind=kLoop, calls=%fused_computation | loop fusion | bytes 6291460 | tf_op jit(solution)/shard_map/dynamic_slice | solution.py:438
  5.6 0.5 collective-permute-start.1
  6.1 0.1 collective-permute-start
  6.1 2.9 %collective-permute-start.2 = (bf16[256,1024]{1,0:T(8,128)(2,1)}, bf16[256,1024]{1,0:T(8,128)(2,1)}, u32[]{:S(2)}, u32[]{:S(2)}) collective-permute-start(bf16[256,1024]{1,0:T(8,128)(2,1)} %constant_dynamic-slice_fusion.2), channel_id=1, source_target_pairs={{0,8},{4,12},{8,0},{12,4},{1,9},{5,13},{9,1},{13,5},{2,10},{6,14},... | collective-permute-start | bytes 1572872 | tf_op jit(solution)/shard_map/ppermute | solution.py:422
  9.1 0.1 stack.63.index_ref
  9.2 5.5 %collective-permute-done.refs_1_ = bf16[256,4096]{1,0:T(8,128)(2,1)} collective-permute-done((bf16[256,4096]{1,0:T(8,128)(2,1)}, bf16[256,4096]{1,0:T(8,128)(2,1)}, u32[]{:S(2)}, u32[]{:S(2)}) %collective-permute-start) | collective-permute-done | bytes 2097184 | tf_op jit(solution)/shard_map/ppermute | solution.py:422
  14.6 2.8 %copy-done.1 = bf16[1024,3,1024]{2,0,1:T(8,128)(2,1)S(1)} copy-done((bf16[1024,3,1024]{2,0,1:T(8,128)(2,1)S(1)}, bf16[1024,3,1024]{2,0,1:T(8,128)(2,1)}, u32[]{:S(2)}) %copy-start.1) | copy-done | bytes 6291480
  17.4 4.4 %shard_map.82 = bf16[2,512,256]{2,1,0:T(8,128)(2,1)} custom-call(s32[15]{0:T(128)S(1)} %stack.63.index_ref, bf16[256,4096]{1,0:T(8,128)(2,1)} %refs_0_.5, bf16[256,4096]{1,0:T(8,128)(2,1)} %collective-permute-done.refs_1_, bf16[3,1024,1024]{2,1,0:T(8,128)(2,1)S(1)} %bitcast.25, bf16[3,1024,512]{2,1,0:T(8,128)(2,1)S(1)} %collective-permute-done.1.refs_3_.refs_5_.refs_7_), custom_call_target="tpu_custom_call" | custom-call | flops 1 | bytes 1 | tf_op jit(solution)/shard_map/pallas_call | solution.py:146
  21.8 2.9 %collective-permute-start.3 = (bf16[256,1024]{1,0:T(8,128)(2,1)}, bf16[256,1024]{1,0:T(8,128)(2,1)}, u32[]{:S(2)}, u32[]{:S(2)}) collective-permute-start(bf16[256,1024]{1,0:T(8,128)(2,1)} %collective-permute-done.2.refs_0_.refs_2_), channel_id=1, source_target_pairs={{0,1},{1,0},{2,3},{3,2},{4,5},{5,4},{6,7},{7,6},{8,9},{9,8},{10,11... | collective-permute-start | bytes 1572872 | tf_op jit(solution)/shard_map/ppermute | solution.py:425
  24.7 1.5 %collective-permute-start.4 = (bf16[2,512,256]{2,1,0:T(8,128)(2,1)}, bf16[2,512,256]{2,1,0:T(8,128)(2,1)}, u32[]{:S(2)}, u32[]{:S(2)}) collective-permute-start(bf16[2,512,256]{2,1,0:T(8,128)(2,1)} %shard_map.82), channel_id=1, source_target_pairs={{0,8},{4,12},{8,0},{12,4},{1,9},{5,13},{9,1},{13,5},{2,10},{6,14},... | collective-permute-start | bytes 1572872 | tf_op jit(solution)/shard_map/ppermute | solution.py:422
  26.2 2.3 %compare_select_fusion = f32[4,256]{1,0:T(4,128)S(1)} fusion(bf16[256,4096]{1,0:T(8,128)(2,1)} %refs_0_.5, bf16[4096,4]{0,1:T(4,128)(2,1)S(1)} %copy-done), kind=kOutput, calls=%fused_computation.11 | convolution fusion | flops 8394752 | bytes 2134016 | tf_op jit(solution)/shard_map/dot_general | solution.py:450
  28.5 0.1 collective-permute-start.5
  28.6 0.5 collective-permute-start.7
  29.1 0.7 collective-permute-done.5
  29.7 0.5 collective-permute-start.6
  30.3 1.3 constant_dynamic-slice_fusion.1
  31.5 0.0 copy-start.2
  31.5 2.8 %copy-done.2 = bf16[1024,3,1024]{2,0,1:T(8,128)(2,1)S(1)} copy-done((bf16[1024,3,1024]{2,0,1:T(8,128)(2,1)S(1)}, bf16[1024,3,1024]{2,0,1:T(8,128)(2,1)}, u32[]{:S(2)}) %copy-start.2) | copy-done | bytes 6291480
  34.3 4.6 %shard_map.83.local_near_ref = f32[3,512,256]{2,1,0:T(8,128)S(1)} custom-call(s32[15]{0:T(128)S(1)} %stack.63.index_ref, bf16[256,4096]{1,0:T(8,128)(2,1)} %refs_0_.5, bf16[256,4096]{1,0:T(8,128)(2,1)} %collective-permute-done.refs_1_, bf16[3,1024,1024]{2,1,0:T(8,128)(2,1)S(1)} %bitcast.26, ...), custom_call_target="tpu_custom_call" | custom-call | flops 1 | bytes 1 | tf_op jit(solution)/shard_map/pallas_call | solution.py:146
  38.9 0.0 copy-start.3
  38.9 0.1 collective-permute-start.8
  39.0 2.1 %collective-permute-done.8.refs_3_.refs_5_ = bf16[256,1024]{1,0:T(8,128)(2,1)S(1)} collective-permute-done((bf16[256,1024]{1,0:T(8,128)(2,1)}, bf16[256,1024]{1,0:T(8,128)(2,1)S(1)}, u32[]{:S(2)}, u32[]{:S(2)}) %collective-permute-start.8) | collective-permute-done | bytes 524320 | tf_op jit(solution)/shard_map/ppermute | solution.py:422
  41.1 3.4 %shard_map.84 = bf16[2,512,256]{2,1,0:T(8,128)(2,1)S(1)} custom-call(s32[15]{0:T(128)S(1)} %stack.63.index_ref, bf16[256,1024]{1,0:T(8,128)(2,1)} %collective-permute-done.2.refs_0_.refs_2_, bf16[256,1024]{1,0:T(8,128)(2,1)} %collective-permute-done.3.refs_1_.refs_3_, bf16[256,1024]{1,0:T(8,128)(2,1)S(1)} %collective-permute-done.7.refs_2_.refs_4_, ...), custom_call_target="tpu_custom_call" | custom-call | flops 1 | bytes 1 | tf_op jit(solution)/shard_map/pallas_call | solution.py:146
  44.5 0.2 collective-permute-start.9
  44.7 1.5 %collective-permute-start.10 = (bf16[2,512,256]{2,1,0:T(8,128)(2,1)S(1)}, bf16[2,512,256]{2,1,0:T(8,128)(2,1)S(1)}, u32[]{:S(2)}, u32[]{:S(2)}) collective-permute-start(bf16[2,512,256]{2,1,0:T(8,128)(2,1)S(1)} %shard_map.84), channel_id=1, source_target_pairs={{0,8},{4,12},{8,0},{12,4},{1,9},{5,13},{9,1},{13,5},{2,10},{6,14},... | collective-permute-start | bytes 1572872 | tf_op jit(solution)/shard_map/ppermute | solution.py:422
  46.2 3.9 %shard_map.85 = bf16[1,1024,256]{2,1,0:T(8,128)(2,1)S(1)} custom-call(s32[15]{0:T(128)S(1)} %stack.63.index_ref, bf16[256,4096]{1,0:T(8,128)(2,1)} %refs_0_.5, bf16[256,4096]{1,0:T(8,128)(2,1)} %collective-permute-done.refs_1_, bf16[256,1024]{1,0:T(8,128)(2,1)} %collective-permute-done.2.refs_0_.refs_2_, ...), custom_call_target="tpu_custom_call" | custom-call | flops 1 | bytes 1 | tf_op jit(solution)/shard_map/pallas_call | solution.py:146
  50.2 0.0 copy-start.4
  50.2 0.0 copy-start.5
  50.2 0.0 copy-start.6
  50.2 4.4 %shard_map.86.local_far_ref = f32[3,512,256]{2,1,0:T(8,128)S(1)} custom-call(s32[15]{0:T(128)S(1)} %stack.63.index_ref, bf16[256,1024]{1,0:T(8,128)(2,1)} %collective-permute-done.2.refs_0_.refs_2_, bf16[256,1024]{1,0:T(8,128)(2,1)} %collective-permute-done.3.refs_1_.refs_3_, bf16[256,1024]{1,0:T(8,128)(2,1)S(1)} %collective-permute-done.7.refs_2_.refs_4_, ...), custom_call_target="tpu_custom_call" | custom-call | flops 1 | bytes 1 | tf_op jit(solution)/shard_map/pallas_call | solution.py:146
  54.7 0.0 copy-start.7
  54.7 4.2 %collective-permute-done.10.near_ref = bf16[2,512,256]{2,1,0:T(8,128)(2,1)S(1)} collective-permute-done((bf16[2,512,256]{2,1,0:T(8,128)(2,1)S(1)}, bf16[2,512,256]{2,1,0:T(8,128)(2,1)S(1)}, u32[]{:S(2)}, u32[]{:S(2)}) %collective-permute-start.10) | collective-permute-done | bytes 524320 | tf_op jit(solution)/shard_map/ppermute | solution.py:422
  58.9 1.5 %collective-permute-start.11 = (bf16[1,1024,256]{2,1,0:T(8,128)(2,1)S(1)}, bf16[1,1024,256]{2,1,0:T(8,128)(2,1)S(1)}, u32[]{:S(2)}, u32[]{:S(2)}) collective-permute-start(bf16[1,1024,256]{2,1,0:T(8,128)(2,1)S(1)} %shard_map.85), channel_id=1, source_target_pairs={{0,8},{4,12},{8,0},{12,4},{1,9},{5,13},{9,1},{13,5},{2,10},{6,14},... | collective-permute-start | bytes 1572872 | tf_op jit(solution)/shard_map/ppermute | solution.py:422
  60.4 13.3 %shard_map.87 = (bf16[256,512]{1,0:T(8,128)(2,1)S(1)}, bf16[256,512]{1,0:T(8,128)(2,1)S(1)}, bf16[256,512]{1,0:T(8,128)(2,1)S(1)}) custom-call(s32[15]{0:T(128)S(1)} %stack.63.index_ref, f32[3,512,256]{2,1,0:T(8,128)S(1)} %shard_map.83.local_near_ref, f32[3,512,256]{2,1,0:T(8,128)S(1)} %shard_map.86.local_far_ref, ...), custom_call_target="tpu_custom_call" | custom-call | flops 1 | bytes 1 | tf_op jit(solution)/shard_map/pallas_call | solution.py:235
  73.7 2.0 %shard_map.88 = (bf16[256,256]{1,0:T(8,128)(2,1)S(1)}, bf16[256,256]{1,0:T(8,128)(2,1)S(1)}, bf16[256,256]{1,0:T(8,128)(2,1)S(1)}, bf16[256,256]{1,0:T(8,128)(2,1)S(1)}) custom-call(s32[15]{0:T(128)S(1)} %stack.63.index_ref, f32[3,512,256]{2,1,0:T(8,128)S(1)} %shard_map.83.local_near_ref, f32[3,512,256]{2,1,0:T(8,128)S(1)} %shard_map.86.local_far_ref, ...), custom_call_target="tpu_custom_call" | custom-call | flops 1 | bytes 1 | tf_op jit(solution)/shard_map/pallas_call | solution.py:281
  75.7 0.1 collective-permute-start.12
  75.8 0.6 collective-permute-start.14
  76.4 1.3 collective-permute-start.15
  77.7 1.3 collective-permute-start.19
  79.0 4.6 %collective-permute-start.13 = (bf16[256,512]{1,0:T(8,128)(2,1)S(1)}, bf16[256,512]{1,0:T(8,128)(2,1)S(1)}, u32[]{:S(2)}, u32[]{:S(2)}) collective-permute-start(bf16[256,512]{1,0:T(8,128)(2,1)S(1)} %constant_dynamic-update-slice_fusion), channel_id=1, source_target_pairs={{0,1},{1,2},{2,3},{4,5},{5,6},{6,7},{8,9},{9,10},{10,11},{12,13},{... | collective-permute-start | bytes 786440 | tf_op jit(solution)/shard_map/ppermute | solution.py:425
  83.6 0.5 collective-permute-done.15
  84.1 1.3 collective-permute-start.20
  85.4 0.6 collective-permute-start.23
  86.0 4.5 %collective-permute-start.16 = (bf16[256,512]{1,0:T(8,128)(2,1)S(1)}, bf16[256,512]{1,0:T(8,128)(2,1)S(1)}, u32[]{:S(2)}, u32[]{:S(2)}) collective-permute-start(bf16[256,512]{1,0:T(8,128)(2,1)S(1)} %constant_dynamic-update-slice_fusion.2), channel_id=1, source_target_pairs={{0,1},{1,2},{2,3},{4,5},{5,6},{6,7},{8,9},{9,10},{10,11},{12,13},{... | collective-permute-start | bytes 786440 | tf_op jit(solution)/shard_map/ppermute | solution.py:425
  90.6 4.2 %collective-permute-done.20 = bf16[256,512]{1,0:T(8,128)(2,1)S(1)} collective-permute-done((bf16[256,512]{1,0:T(8,128)(2,1)S(1)}, bf16[256,512]{1,0:T(8,128)(2,1)S(1)}, u32[]{:S(2)}, u32[]{:S(2)}) %collective-permute-start.20) | collective-permute-done | bytes 262176 | tf_op jit(solution)/shard_map/ppermute | solution.py:425
  94.8 1.3 collective-permute-start.21
  96.1 0.1 collective-permute-done.16
  96.3 0.7 collective-permute-start.17
  97.0 1.6 %collective-permute-start.27 = (bf16[256,1024]{1,0:T(8,128)(2,1)S(1)}, bf16[256,1024]{1,0:T(8,128)(2,1)S(1)}, u32[]{:S(2)}, u32[]{:S(2)}) collective-permute-start(bf16[256,1024]{1,0:T(8,128)(2,1)S(1)} %get-tuple-element.57), channel_id=1, source_target_pairs={{0,8},{4,12},{8,0},{12,4},{1,9},{5,13},{9,1},{13,5},{2,10},{6,14},... | collective-permute-start | bytes 1572872 | tf_op jit(solution)/shard_map/ppermute | solution.py:422
  98.5 1.6 %collective-permute-done.23.one = bf16[256,1024]{1,0:T(8,128)(2,1)S(1)} collective-permute-done((bf16[256,1024]{1,0:T(8,128)(2,1)S(1)}, bf16[256,1024]{1,0:T(8,128)(2,1)S(1)}, u32[]{:S(2)}, u32[]{:S(2)}) %collective-permute-start.23) | collective-permute-done | bytes 524320 | tf_op jit(solution)/shard_map/ppermute | solution.py:422
  100.1 1.5 %collective-permute-start.24 = (bf16[256,1024]{1,0:T(8,128)(2,1)S(1)}, bf16[256,1024]{1,0:T(8,128)(2,1)S(1)}, u32[]{:S(2)}, u32[]{:S(2)}) collective-permute-start(bf16[256,1024]{1,0:T(8,128)(2,1)S(1)} %collective-permute-done.23.one), channel_id=1, source_target_pairs={{0,16},{16,0},{1,17},{17,1},{2,18},{18,2},{3,19},{19,3},{4,20},{20... | collective-permute-start | bytes 1572872 | tf_op jit(solution)/shard_map/ppermute | solution.py:479
  101.7 8.6 %collective-permute-done.21.above_2 = bf16[256,1024]{1,0:T(8,128)(2,1)S(1)} collective-permute-done((bf16[256,1024]{1,0:T(8,128)(2,1)S(1)}, bf16[256,1024]{1,0:T(8,128)(2,1)S(1)}, u32[]{:S(2)}, u32[]{:S(2)}) %collective-permute-start.21) | collective-permute-done | bytes 524320 | tf_op jit(solution)/shard_map/ppermute | solution.py:425
  110.3 0.8 collective-permute-done.27.one
  111.1 2.4 %collective-permute-done.24.other = bf16[256,1024]{1,0:T(8,128)(2,1)S(1)} collective-permute-done((bf16[256,1024]{1,0:T(8,128)(2,1)S(1)}, bf16[256,1024]{1,0:T(8,128)(2,1)S(1)}, u32[]{:S(2)}, u32[]{:S(2)}) %collective-permute-start.24) | collective-permute-done | bytes 524320 | tf_op jit(solution)/shard_map/ppermute | solution.py:479
  113.5 1.5 %collective-permute-start.28 = (bf16[256,1024]{1,0:T(8,128)(2,1)S(1)}, bf16[256,1024]{1,0:T(8,128)(2,1)S(1)}, u32[]{:S(2)}, u32[]{:S(2)}) collective-permute-start(bf16[256,1024]{1,0:T(8,128)(2,1)S(1)} %collective-permute-done.27.one), channel_id=1, source_target_pairs={{0,16},{16,0},{1,17},{17,1},{2,18},{18,2},{3,19},{19,3},{4,20},{20... | collective-permute-start | bytes 1572872 | tf_op jit(solution)/shard_map/ppermute | solution.py:479
  115.0 0.1 pad_maximum_fusion.own
  115.1 1.3 collective-permute-start.22
  116.4 0.7 collective-permute-start.18
  117.1 4.7 %shard_map.89 = (f32[256,1024]{1,0:T(8,128)S(1)}, bf16[256,1024]{1,0:T(8,128)(2,1)S(1)}, bf16[1024,1024]{1,0:T(8,128)(2,1)S(1)}) custom-call(s32[15]{0:T(128)S(1)} %stack.63.index_ref, bf16[256,1024]{1,0:T(8,128)(2,1)S(1)} %pad_maximum_fusion.own, bf16[256,1024]{1,0:T(8,128)(2,1)S(1)} %constant_dynamic-update-slice_fusion.4.below_1, ...), custom_call_target="tpu_custom_call" | custom-call | flops 1 | bytes 1 | tf_op jit(solution)/shard_map/pallas_call | solution.py:348
  121.8 6.0 %collective-permute-done.28.other = bf16[256,1024]{1,0:T(8,128)(2,1)S(1)} collective-permute-done((bf16[256,1024]{1,0:T(8,128)(2,1)S(1)}, bf16[256,1024]{1,0:T(8,128)(2,1)S(1)}, u32[]{:S(2)}, u32[]{:S(2)}) %collective-permute-start.28) | collective-permute-done | bytes 524320 | tf_op jit(solution)/shard_map/ppermute | solution.py:479
  127.8 0.5 collective-permute-start.30
  128.3 3.3 %collective-permute-done.22.above = bf16[256,1024]{1,0:T(8,128)(2,1)S(1)} collective-permute-done((bf16[256,1024]{1,0:T(8,128)(2,1)S(1)}, bf16[256,1024]{1,0:T(8,128)(2,1)S(1)}, u32[]{:S(2)}, u32[]{:S(2)}) %collective-permute-start.22) | collective-permute-done | bytes 524320 | tf_op jit(solution)/shard_map/ppermute | solution.py:425
  131.6 3.1 %shard_map.90 = bf16[256,1024]{1,0:T(8,128)(2,1)} custom-call(s32[15]{0:T(128)S(1)} %stack.63.index_ref, bf16[256,1024]{1,0:T(8,128)(2,1)S(1)} %collective-permute-done.18.below, bf16[256,1024]{1,0:T(8,128)(2,1)S(1)} %collective-permute-done.22.above, bf16[1024,1024]{1,0:T(8,128)(2,1)S(1)} %get-tuple-element.55.weight, ...), custom_call_target="tpu_custom_call" | custom-call | flops 1 | bytes 1 | tf_op jit(solution)/shard_map/pallas_call | solution.py:392
  (38 shorter events, 0.2 us)
Async XLA Ops:
  0.0 26.2 %copy-start = (bf16[4096,4]{0,1:T(4,128)(2,1)S(1)}, bf16[4096,4]{0,1:T(4,128)(2,1)}, u32[]{:S(2)}) copy-start(bf16[4096,4]{0,1:T(4,128)(2,1)} %param.10) | copy-start | bytes 98308
  5.6 9.0 %collective-permute-start.1 = (bf16[3,1024,512]{2,1,0:T(8,128)(2,1)}, bf16[3,1024,512]{2,1,0:T(8,128)(2,1)S(1)}, u32[]{:S(2)}, u32[]{:S(2)}) collective-permute-start(bf16[3,1024,512]{2,1,0:T(8,128)(2,1)} %dynamic-slice_bitcast_fusion), channel_id=1, source_target_pairs={{0,4},{4,0},{8,12},{12,8},{1,5},{5,1},{9,13},{13,9},{2,6},{6,2},{1... | collective-permute-start | bytes 9437192 | tf_op jit(solution)/shard_map/ppermute | solution.py:422
  6.1 8.5 %collective-permute-start = (bf16[256,4096]{1,0:T(8,128)(2,1)}, bf16[256,4096]{1,0:T(8,128)(2,1)}, u32[]{:S(2)}, u32[]{:S(2)}) collective-permute-start(bf16[256,4096]{1,0:T(8,128)(2,1)} %refs_0_.5), channel_id=1, source_target_pairs={{0,4},{4,0},{8,12},{12,8},{1,5},{5,1},{9,13},{13,9},{2,6},{6,2},{1... | collective-permute-start | bytes 6291464 | tf_op jit(solution)/shard_map/ppermute | solution.py:422
  6.1 15.7 %collective-permute-start.2 = (bf16[256,1024]{1,0:T(8,128)(2,1)}, bf16[256,1024]{1,0:T(8,128)(2,1)}, u32[]{:S(2)}, u32[]{:S(2)}) collective-permute-start(bf16[256,1024]{1,0:T(8,128)(2,1)} %constant_dynamic-slice_fusion.2), channel_id=1, source_target_pairs={{0,8},{4,12},{8,0},{12,4},{1,9},{5,13},{9,1},{13,5},{2,10},{6,14},... | collective-permute-start | bytes 1572872 | tf_op jit(solution)/shard_map/ppermute | solution.py:422
  14.6 2.8 %copy-start.1 = (bf16[1024,3,1024]{2,0,1:T(8,128)(2,1)S(1)}, bf16[1024,3,1024]{2,0,1:T(8,128)(2,1)}, u32[]{:S(2)}) copy-start(bf16[1024,3,1024]{2,0,1:T(8,128)(2,1)} %param.9) | copy-start | bytes 18874372
  21.8 17.1 %collective-permute-start.3 = (bf16[256,1024]{1,0:T(8,128)(2,1)}, bf16[256,1024]{1,0:T(8,128)(2,1)}, u32[]{:S(2)}, u32[]{:S(2)}) collective-permute-start(bf16[256,1024]{1,0:T(8,128)(2,1)} %collective-permute-done.2.refs_0_.refs_2_), channel_id=1, source_target_pairs={{0,1},{1,0},{2,3},{3,2},{4,5},{5,4},{6,7},{7,6},{8,9},{9,8},{10,11... | collective-permute-start | bytes 1572872 | tf_op jit(solution)/shard_map/ppermute | solution.py:425
  24.7 14.2 %collective-permute-start.4 = (bf16[2,512,256]{2,1,0:T(8,128)(2,1)}, bf16[2,512,256]{2,1,0:T(8,128)(2,1)}, u32[]{:S(2)}, u32[]{:S(2)}) collective-permute-start(bf16[2,512,256]{2,1,0:T(8,128)(2,1)} %shard_map.82), channel_id=1, source_target_pairs={{0,8},{4,12},{8,0},{12,4},{1,9},{5,13},{9,1},{13,5},{2,10},{6,14},... | collective-permute-start | bytes 1572872 | tf_op jit(solution)/shard_map/ppermute | solution.py:422
  28.5 1.2 collective-permute-start.5
  28.6 10.4 %collective-permute-start.7 = (bf16[256,1024]{1,0:T(8,128)(2,1)}, bf16[256,1024]{1,0:T(8,128)(2,1)S(1)}, u32[]{:S(2)}, u32[]{:S(2)}) collective-permute-start(bf16[256,1024]{1,0:T(8,128)(2,1)} %collective-permute-done.2.refs_0_.refs_2_), channel_id=1, source_target_pairs={{0,4},{4,0},{8,12},{12,8},{1,5},{5,1},{9,13},{13,9},{2,6},{6,2},{1... | collective-permute-start | bytes 1572872 | tf_op jit(solution)/shard_map/ppermute | solution.py:422
  29.7 9.2 %collective-permute-start.6 = (f32[8,256]{1,0:T(8,128)S(1)}, f32[8,256]{1,0:T(8,128)S(1)}, u32[]{:S(2)}, u32[]{:S(2)}) collective-permute-start(f32[8,256]{1,0:T(8,128)S(1)} %pad_maximum_fusion.1.rate_near_ref), channel_id=1, source_target_pairs={{0,8},{4,12},{8,0},{12,4},{1,9},{5,13},{9,1},{13,5},{2,10},{6,14},... | collective-permute-start | bytes 24584 | tf_op jit(solution)/shard_map/ppermute | solution.py:422
  31.5 2.8 %copy-start.2 = (bf16[1024,3,1024]{2,0,1:T(8,128)(2,1)S(1)}, bf16[1024,3,1024]{2,0,1:T(8,128)(2,1)}, u32[]{:S(2)}) copy-start(bf16[1024,3,1024]{2,0,1:T(8,128)(2,1)} %param.9) | copy-start | bytes 18874372
  38.9 5.6 %copy-start.3 = (bf16[1024,1024]{1,0:T(8,128)(2,1)S(1)}, bf16[1024,1024]{1,0:T(8,128)(2,1)}, u32[]{:S(2)}) copy-start(bf16[1024,1024]{1,0:T(8,128)(2,1)} %own_w.1) | copy-start | bytes 6291460
  38.9 2.2 %collective-permute-start.8 = (bf16[256,1024]{1,0:T(8,128)(2,1)}, bf16[256,1024]{1,0:T(8,128)(2,1)S(1)}, u32[]{:S(2)}, u32[]{:S(2)}) collective-permute-start(bf16[256,1024]{1,0:T(8,128)(2,1)} %collective-permute-done.3.refs_1_.refs_3_), channel_id=1, source_target_pairs={{0,4},{4,0},{8,12},{12,8},{1,5},{5,1},{9,13},{13,9},{2,6},{6,2},{1... | collective-permute-start | bytes 1572872 | tf_op jit(solution)/shard_map/ppermute | solution.py:422
  44.5 5.7 %collective-permute-start.9 = (bf16[1024,1024]{1,0:T(8,128)(2,1)S(1)}, bf16[1024,1024]{1,0:T(8,128)(2,1)S(1)}, u32[]{:S(2)}, u32[]{:S(2)}) collective-permute-start(bf16[1024,1024]{1,0:T(8,128)(2,1)S(1)} %copy-done.3), channel_id=1, source_target_pairs={{0,4},{4,0},{8,12},{12,8},{1,5},{5,1},{9,13},{13,9},{2,6},{6,2},{1... | collective-permute-start | bytes 6291464 | tf_op jit(solution)/shard_map/ppermute | solution.py:422
  44.7 14.2 %collective-permute-start.10 = (bf16[2,512,256]{2,1,0:T(8,128)(2,1)S(1)}, bf16[2,512,256]{2,1,0:T(8,128)(2,1)S(1)}, u32[]{:S(2)}, u32[]{:S(2)}) collective-permute-start(bf16[2,512,256]{2,1,0:T(8,128)(2,1)S(1)} %shard_map.84), channel_id=1, source_target_pairs={{0,8},{4,12},{8,0},{12,4},{1,9},{5,13},{9,1},{13,5},{2,10},{6,14},... | collective-permute-start | bytes 1572872 | tf_op jit(solution)/shard_map/ppermute | solution.py:422
  50.2 10.2 %copy-start.4 = (bf16[4,256,512]{2,1,0:T(8,128)(2,1)S(1)}, bf16[4,256,512]{2,1,0:T(8,128)(2,1)}, u32[]{:S(2)}) copy-start(bf16[4,256,512]{2,1,0:T(8,128)(2,1)} %gate_ref.1) | copy-start | bytes 3145732
  50.2 10.2 %copy-start.5 = (bf16[4,256,512]{2,1,0:T(8,128)(2,1)S(1)}, bf16[4,256,512]{2,1,0:T(8,128)(2,1)}, u32[]{:S(2)}) copy-start(bf16[4,256,512]{2,1,0:T(8,128)(2,1)} %up_ref.1) | copy-start | bytes 3145732
  50.2 10.2 %copy-start.6 = (bf16[4,256,512]{2,1,0:T(8,128)(2,1)S(1)}, bf16[4,256,512]{2,1,0:T(8,128)(2,1)}, u32[]{:S(2)}) copy-start(bf16[4,256,512]{2,1,0:T(8,128)(2,1)} %down_ref.1) | copy-start | bytes 3145732
  54.7 19.0 %copy-start.7 = (f32[1024]{0:T(1024)S(1)}, f32[1024]{0:T(1024)}, u32[]{:S(2)}) copy-start(f32[1024]{0:T(1024)} %param.14) | copy-start | bytes 12292
  58.9 14.8 %collective-permute-start.11 = (bf16[1,1024,256]{2,1,0:T(8,128)(2,1)S(1)}, bf16[1,1024,256]{2,1,0:T(8,128)(2,1)S(1)}, u32[]{:S(2)}, u32[]{:S(2)}) collective-permute-start(bf16[1,1024,256]{2,1,0:T(8,128)(2,1)S(1)} %shard_map.85), channel_id=1, source_target_pairs={{0,8},{4,12},{8,0},{12,4},{1,9},{5,13},{9,1},{13,5},{2,10},{6,14},... | collective-permute-start | bytes 1572872 | tf_op jit(solution)/shard_map/ppermute | solution.py:422
  75.7 2.0 %collective-permute-start.12 = (bf16[256,256]{1,0:T(8,128)(2,1)S(1)}, bf16[256,256]{1,0:T(8,128)(2,1)S(1)}, u32[]{:S(2)}, u32[]{:S(2)}) collective-permute-start(bf16[256,256]{1,0:T(8,128)(2,1)S(1)} %get-tuple-element.48), channel_id=1, source_target_pairs={{0,4},{4,0},{8,12},{12,8},{1,5},{5,1},{9,13},{13,9},{2,6},{6,2},{1... | collective-permute-start | bytes 393224 | tf_op jit(solution)/shard_map/ppermute | solution.py:422
  75.8 7.8 %collective-permute-start.14 = (bf16[256,256]{1,0:T(8,128)(2,1)S(1)}, bf16[256,256]{1,0:T(8,128)(2,1)S(1)}, u32[]{:S(2)}, u32[]{:S(2)}) collective-permute-start(bf16[256,256]{1,0:T(8,128)(2,1)S(1)} %get-tuple-element.49), channel_id=1, source_target_pairs={{0,8},{4,12},{8,0},{12,4},{1,9},{5,13},{9,1},{13,5},{2,10},{6,14},... | collective-permute-start | bytes 393224 | tf_op jit(solution)/shard_map/ppermute | solution.py:422
  76.4 7.7 %collective-permute-start.15 = (bf16[256,256]{1,0:T(8,128)(2,1)S(1)}, bf16[256,256]{1,0:T(8,128)(2,1)S(1)}, u32[]{:S(2)}, u32[]{:S(2)}) collective-permute-start(bf16[256,256]{1,0:T(8,128)(2,1)S(1)} %get-tuple-element.50), channel_id=1, source_target_pairs={{0,12},{4,8},{8,4},{12,0},{1,13},{5,9},{9,5},{13,1},{2,14},{6,10},... | collective-permute-start | bytes 393224 | tf_op jit(solution)/shard_map/ppermute | solution.py:422
  77.7 12.8 %collective-permute-start.19 = (bf16[256,512]{1,0:T(8,128)(2,1)S(1)}, bf16[256,512]{1,0:T(8,128)(2,1)S(1)}, u32[]{:S(2)}, u32[]{:S(2)}) collective-permute-start(bf16[256,512]{1,0:T(8,128)(2,1)S(1)} %constant_dynamic-update-slice_fusion), channel_id=1, source_target_pairs={{1,0},{2,1},{3,2},{5,4},{6,5},{7,6},{9,8},{10,9},{11,10},{13,12},{... | collective-permute-start | bytes 786440 | tf_op jit(solution)/shard_map/ppermute | solution.py:425
  79.0 11.6 %collective-permute-start.13 = (bf16[256,512]{1,0:T(8,128)(2,1)S(1)}, bf16[256,512]{1,0:T(8,128)(2,1)S(1)}, u32[]{:S(2)}, u32[]{:S(2)}) collective-permute-start(bf16[256,512]{1,0:T(8,128)(2,1)S(1)} %constant_dynamic-update-slice_fusion), channel_id=1, source_target_pairs={{0,1},{1,2},{2,3},{4,5},{5,6},{6,7},{8,9},{9,10},{10,11},{12,13},{... | collective-permute-start | bytes 786440 | tf_op jit(solution)/shard_map/ppermute | solution.py:425
  84.1 10.7 %collective-permute-start.20 = (bf16[256,512]{1,0:T(8,128)(2,1)S(1)}, bf16[256,512]{1,0:T(8,128)(2,1)S(1)}, u32[]{:S(2)}, u32[]{:S(2)}) collective-permute-start(bf16[256,512]{1,0:T(8,128)(2,1)S(1)} %constant_dynamic-update-slice_fusion.2), channel_id=1, source_target_pairs={{1,0},{2,1},{3,2},{5,4},{6,5},{7,6},{9,8},{10,9},{11,10},{13,12},{... | collective-permute-start | bytes 786440 | tf_op jit(solution)/shard_map/ppermute | solution.py:425
  85.4 14.8 %collective-permute-start.23 = (bf16[256,1024]{1,0:T(8,128)(2,1)S(1)}, bf16[256,1024]{1,0:T(8,128)(2,1)S(1)}, u32[]{:S(2)}, u32[]{:S(2)}) collective-permute-start(bf16[256,1024]{1,0:T(8,128)(2,1)S(1)} %get-tuple-element.51), channel_id=1, source_target_pairs={{0,8},{4,12},{8,0},{12,4},{1,9},{5,13},{9,1},{13,5},{2,10},{6,14},... | collective-permute-start | bytes 1572872 | tf_op jit(solution)/shard_map/ppermute | solution.py:422
  86.0 10.3 %collective-permute-start.16 = (bf16[256,512]{1,0:T(8,128)(2,1)S(1)}, bf16[256,512]{1,0:T(8,128)(2,1)S(1)}, u32[]{:S(2)}, u32[]{:S(2)}) collective-permute-start(bf16[256,512]{1,0:T(8,128)(2,1)S(1)} %constant_dynamic-update-slice_fusion.2), channel_id=1, source_target_pairs={{0,1},{1,2},{2,3},{4,5},{5,6},{6,7},{8,9},{9,10},{10,11},{12,13},{... | collective-permute-start | bytes 786440 | tf_op jit(solution)/shard_map/ppermute | solution.py:425
  94.8 15.5 %collective-permute-start.21 = (bf16[256,1024]{1,0:T(8,128)(2,1)S(1)}, bf16[256,1024]{1,0:T(8,128)(2,1)S(1)}, u32[]{:S(2)}, u32[]{:S(2)}) collective-permute-start(bf16[256,1024]{1,0:T(8,128)(2,1)S(1)} %constant_dynamic-update-slice_fusion.6.above_1), channel_id=1, source_target_pairs={{1,0},{2,1},{5,4},{6,5},{9,8},{10,9},{13,12},{14,13},{17,16},{18,1... | collective-permute-start | bytes 1572872 | tf_op jit(solution)/shard_map/ppermute | solution.py:425
  96.3 14.0 %collective-permute-start.17 = (bf16[256,1024]{1,0:T(8,128)(2,1)S(1)}, bf16[256,1024]{1,0:T(8,128)(2,1)S(1)}, u32[]{:S(2)}, u32[]{:S(2)}) collective-permute-start(bf16[256,1024]{1,0:T(8,128)(2,1)S(1)} %constant_dynamic-update-slice_fusion.4.below_1), channel_id=1, source_target_pairs={{1,2},{2,3},{5,6},{6,7},{9,10},{10,11},{13,14},{14,15},{17,18},{18... | collective-permute-start | bytes 1572872 | tf_op jit(solution)/shard_map/ppermute | solution.py:425
  97.0 14.1 %collective-permute-start.27 = (bf16[256,1024]{1,0:T(8,128)(2,1)S(1)}, bf16[256,1024]{1,0:T(8,128)(2,1)S(1)}, u32[]{:S(2)}, u32[]{:S(2)}) collective-permute-start(bf16[256,1024]{1,0:T(8,128)(2,1)S(1)} %get-tuple-element.57), channel_id=1, source_target_pairs={{0,8},{4,12},{8,0},{12,4},{1,9},{5,13},{9,1},{13,5},{2,10},{6,14},... | collective-permute-start | bytes 1572872 | tf_op jit(solution)/shard_map/ppermute | solution.py:422
  100.1 13.3 %collective-permute-start.24 = (bf16[256,1024]{1,0:T(8,128)(2,1)S(1)}, bf16[256,1024]{1,0:T(8,128)(2,1)S(1)}, u32[]{:S(2)}, u32[]{:S(2)}) collective-permute-start(bf16[256,1024]{1,0:T(8,128)(2,1)S(1)} %collective-permute-done.23.one), channel_id=1, source_target_pairs={{0,16},{16,0},{1,17},{17,1},{2,18},{18,2},{3,19},{19,3},{4,20},{20... | collective-permute-start | bytes 1572872 | tf_op jit(solution)/shard_map/ppermute | solution.py:479
  111.1 6.0 %collective-permute-start.25 = (bf16[256,1024]{1,0:T(8,128)(2,1)S(1)}, bf16[256,1024]{1,0:T(8,128)(2,1)S(1)}, u32[]{:S(2)}, u32[]{:S(2)}) collective-permute-start(bf16[256,1024]{1,0:T(8,128)(2,1)S(1)} %collective-permute-done.23.one), channel_id=1, source_target_pairs={{0,4},{4,0},{8,12},{12,8},{1,5},{5,1},{9,13},{13,9},{2,6},{6,2},{1... | collective-permute-start | bytes 1572872 | tf_op jit(solution)/shard_map/ppermute | solution.py:422
  113.5 3.6 %collective-permute-start.26 = (bf16[256,1024]{1,0:T(8,128)(2,1)S(1)}, bf16[256,1024]{1,0:T(8,128)(2,1)S(1)}, u32[]{:S(2)}, u32[]{:S(2)}) collective-permute-start(bf16[256,1024]{1,0:T(8,128)(2,1)S(1)} %collective-permute-done.24.other), channel_id=1, source_target_pairs={{0,4},{4,0},{8,12},{12,8},{1,5},{5,1},{9,13},{13,9},{2,6},{6,2},{1... | collective-permute-start | bytes 1572872 | tf_op jit(solution)/shard_map/ppermute | solution.py:422
  113.5 14.3 %collective-permute-start.28 = (bf16[256,1024]{1,0:T(8,128)(2,1)S(1)}, bf16[256,1024]{1,0:T(8,128)(2,1)S(1)}, u32[]{:S(2)}, u32[]{:S(2)}) collective-permute-start(bf16[256,1024]{1,0:T(8,128)(2,1)S(1)} %collective-permute-done.27.one), channel_id=1, source_target_pairs={{0,16},{16,0},{1,17},{17,1},{2,18},{18,2},{3,19},{19,3},{4,20},{20... | collective-permute-start | bytes 1572872 | tf_op jit(solution)/shard_map/ppermute | solution.py:479
  115.1 16.5 %collective-permute-start.22 = (bf16[256,1024]{1,0:T(8,128)(2,1)S(1)}, bf16[256,1024]{1,0:T(8,128)(2,1)S(1)}, u32[]{:S(2)}, u32[]{:S(2)}) collective-permute-start(bf16[256,1024]{1,0:T(8,128)(2,1)S(1)} %collective-permute-done.21.above_2), channel_id=1, source_target_pairs={{1,0},{5,4},{9,8},{13,12},{17,16},{21,20},{25,24},{29,28}} | collective-permute-start | bytes 1572872 | tf_op jit(solution)/shard_map/ppermute | solution.py:425
  116.4 15.2 %collective-permute-start.18 = (bf16[256,1024]{1,0:T(8,128)(2,1)S(1)}, bf16[256,1024]{1,0:T(8,128)(2,1)S(1)}, u32[]{:S(2)}, u32[]{:S(2)}) collective-permute-start(bf16[256,1024]{1,0:T(8,128)(2,1)S(1)} %collective-permute-done.17.below_2), channel_id=1, source_target_pairs={{2,3},{6,7},{10,11},{14,15},{18,19},{22,23},{26,27},{30,31}} | collective-permute-start | bytes 1572872 | tf_op jit(solution)/shard_map/ppermute | solution.py:425
  127.8 3.8 %collective-permute-start.29 = (bf16[256,1024]{1,0:T(8,128)(2,1)S(1)}, bf16[256,1024]{1,0:T(8,128)(2,1)S(1)}, u32[]{:S(2)}, u32[]{:S(2)}) collective-permute-start(bf16[256,1024]{1,0:T(8,128)(2,1)S(1)} %collective-permute-done.27.one), channel_id=1, source_target_pairs={{0,4},{4,0},{8,12},{12,8},{1,5},{5,1},{9,13},{13,9},{2,6},{6,2},{1... | collective-permute-start | bytes 1572872 | tf_op jit(solution)/shard_map/ppermute | solution.py:422
  127.8 3.8 %collective-permute-start.30 = (bf16[256,1024]{1,0:T(8,128)(2,1)S(1)}, bf16[256,1024]{1,0:T(8,128)(2,1)S(1)}, u32[]{:S(2)}, u32[]{:S(2)}) collective-permute-start(bf16[256,1024]{1,0:T(8,128)(2,1)S(1)} %collective-permute-done.28.other), channel_id=1, source_target_pairs={{0,4},{4,0},{8,12},{12,8},{1,5},{5,1},{9,13},{13,9},{2,6},{6,2},{1... | collective-permute-start | bytes 1572872 | tf_op jit(solution)/shard_map/ppermute | solution.py:422

commit v15 on v14

--- a/solution.py
+++ b/solution.py
@@ -385,7 +385,7 @@
     rows, width = below.shape
     columns = weight.shape[1]
     size = laters[0].shape[0]
-    tile = columns // 2
+    tile = columns
     slab = pl.BlockSpec((rows, tile), lambda i, idx: (0, i))
     shard = pl.BlockSpec((rows, width), lambda i, idx: (0, 0))
     part = pl.BlockSpec((size, tile), lambda i, idx: (0, i))
@@ -394,7 +394,7 @@
         out_shape=jax.ShapeDtypeStruct((rows, columns), BF16),
         grid_spec=pltpu.PrefetchScalarGridSpec(
             num_scalar_prefetch=1,
-            grid=(2,),
+            grid=(1,),
             in_specs=[shard, shard, pl.BlockSpec((width, tile), lambda i, idx: (0, i)), shard] + [part] * 4 + [slab],
             out_specs=slab,
             scratch_shapes=[pltpu.VMEM((rows, width), BF16)],

time: 135 us -> 135 us (level)
  no operation moved by 1% of the time
where the time goes in v15:
time: 135 us; the launch traced here: 134 us
  Pallas kernels  43.4 us (32%)
  waiting for transfers between devices  39.9 us (30%)
  starting transfers between devices  35.6 us (26%)
  local copies, waits for them, and re-layouts  12.7 us (9%)
  matrix products  2.25 us (2%)
    pallas_call x5, Pallas kernels, project(): pl.pallas_call(functools.partial(project_kernel, len(whole), len(pairs)),...  20.7 us
    ppermute x9, starting transfers between devices, hop(): return lax.ppermute(array, 'head', links)  18.6 us
    ppermute x9, waiting for transfers between devices, hop(): return lax.ppermute(array, 'head', links)  16.2 us
    ppermute x20, waiting for transfers between devices, across(): return lax.ppermute(array, 'seq', [(i, i ^ bit) for i in range(4)])  15.3 us
    ppermute x20, starting transfers between devices, across(): return lax.ppermute(array, 'seq', [(i, i ^ bit) for i in range(4)])  13.9 us
    pallas_call x1, Pallas kernels, update(): pl.pallas_call(update_kernel, out_shape=[out] * 3, grid_spec=pltpu.Prefet...  13.3 us
    ppermute x2, waiting for transfers between devices, swap_groups(): return lax.ppermute(array, 'groups', [(0, 1), (1, 0)])  8.37 us
    unnamed x20, local copies, waits for them, and re-layouts  5.67 us
  transfers between devices with their start and end apart: 31, of which 13 were waited for; matrix products, arithmetic and copies ran while one was open for 3% of the time, Pallas kernels for 26%

profile of v15, /device:TPU:0, one launch (start us, length us, event | category | flops | bytes accessed | tf_op | source)
XLA Modules:
  0.0 134.2 jit_solution(17330613941678842461)
XLA Ops:
  0.0 1.9 %constant_dynamic-slice_fusion.2 = bf16[256,1024]{1,0:T(8,128)(2,1)} fusion(bf16[256,4096]{1,0:T(8,128)(2,1)} %refs_0_.5, s32[]{:T(128)S(6)} %select_n.23), kind=kLoop, calls=%fused_computation.15 | loop fusion | bytes 1048580 | tf_op jit(solution)/shard_map/dynamic_slice | solution.py:434
  1.9 3.7 %dynamic-slice_bitcast_fusion = bf16[3,1024,512]{2,1,0:T(8,128)(2,1)} fusion(bf16[1024,3,1024]{2,0,1:T(8,128)(2,1)} %param.9, s32[]{:T(128)S(6)} %select_n.24), kind=kLoop, calls=%fused_computation | loop fusion | bytes 6291460 | tf_op jit(solution)/shard_map/dynamic_slice | solution.py:438
  5.6 0.5 collective-permute-start.1
  6.1 0.1 collective-permute-start
  6.1 2.9 %collective-permute-start.2 = (bf16[256,1024]{1,0:T(8,128)(2,1)}, bf16[256,1024]{1,0:T(8,128)(2,1)}, u32[]{:S(2)}, u32[]{:S(2)}) collective-permute-start(bf16[256,1024]{1,0:T(8,128)(2,1)} %constant_dynamic-slice_fusion.2), channel_id=1, source_target_pairs={{0,8},{4,12},{8,0},{12,4},{1,9},{5,13},{9,1},{13,5},{2,10},{6,14},... | collective-permute-start | bytes 1572872 | tf_op jit(solution)/shard_map/ppermute | solution.py:422
  9.1 0.1 stack.63.index_ref
  9.2 5.5 %collective-permute-done.refs_1_ = bf16[256,4096]{1,0:T(8,128)(2,1)} collective-permute-done((bf16[256,4096]{1,0:T(8,128)(2,1)}, bf16[256,4096]{1,0:T(8,128)(2,1)}, u32[]{:S(2)}, u32[]{:S(2)}) %collective-permute-start) | collective-permute-done | bytes 2097184 | tf_op jit(solution)/shard_map/ppermute | solution.py:422
  14.6 2.8 %copy-done.1 = bf16[1024,3,1024]{2,0,1:T(8,128)(2,1)S(1)} copy-done((bf16[1024,3,1024]{2,0,1:T(8,128)(2,1)S(1)}, bf16[1024,3,1024]{2,0,1:T(8,128)(2,1)}, u32[]{:S(2)}) %copy-start.1) | copy-done | bytes 6291480
  17.4 4.4 %shard_map.82 = bf16[2,512,256]{2,1,0:T(8,128)(2,1)} custom-call(s32[15]{0:T(128)S(1)} %stack.63.index_ref, bf16[256,4096]{1,0:T(8,128)(2,1)} %refs_0_.5, bf16[256,4096]{1,0:T(8,128)(2,1)} %collective-permute-done.refs_1_, bf16[3,1024,1024]{2,1,0:T(8,128)(2,1)S(1)} %bitcast.25, bf16[3,1024,512]{2,1,0:T(8,128)(2,1)S(1)} %collective-permute-done.1.refs_3_.refs_5_.refs_7_), custom_call_target="tpu_custom_call" | custom-call | flops 1 | bytes 1 | tf_op jit(solution)/shard_map/pallas_call | solution.py:146
  21.8 2.9 %collective-permute-start.3 = (bf16[256,1024]{1,0:T(8,128)(2,1)}, bf16[256,1024]{1,0:T(8,128)(2,1)}, u32[]{:S(2)}, u32[]{:S(2)}) collective-permute-start(bf16[256,1024]{1,0:T(8,128)(2,1)} %collective-permute-done.2.refs_0_.refs_2_), channel_id=1, source_target_pairs={{0,1},{1,0},{2,3},{3,2},{4,5},{5,4},{6,7},{7,6},{8,9},{9,8},{10,11... | collective-permute-start | bytes 1572872 | tf_op jit(solution)/shard_map/ppermute | solution.py:425
  24.7 1.5 %collective-permute-start.4 = (bf16[2,512,256]{2,1,0:T(8,128)(2,1)}, bf16[2,512,256]{2,1,0:T(8,128)(2,1)}, u32[]{:S(2)}, u32[]{:S(2)}) collective-permute-start(bf16[2,512,256]{2,1,0:T(8,128)(2,1)} %shard_map.82), channel_id=1, source_target_pairs={{0,8},{4,12},{8,0},{12,4},{1,9},{5,13},{9,1},{13,5},{2,10},{6,14},... | collective-permute-start | bytes 1572872 | tf_op jit(solution)/shard_map/ppermute | solution.py:422
  26.2 2.3 %compare_select_fusion = f32[4,256]{1,0:T(4,128)S(1)} fusion(bf16[256,4096]{1,0:T(8,128)(2,1)} %refs_0_.5, bf16[4096,4]{0,1:T(4,128)(2,1)S(1)} %copy-done), kind=kOutput, calls=%fused_computation.11 | convolution fusion | flops 8394752 | bytes 2134016 | tf_op jit(solution)/shard_map/dot_general | solution.py:450
  28.5 0.1 collective-permute-start.5
  28.6 0.5 collective-permute-start.7
  29.1 0.7 collective-permute-done.5
  29.7 0.5 collective-permute-start.6
  30.3 1.3 constant_dynamic-slice_fusion.1
  31.5 0.0 copy-start.2
  31.5 2.8 %copy-done.2 = bf16[1024,3,1024]{2,0,1:T(8,128)(2,1)S(1)} copy-done((bf16[1024,3,1024]{2,0,1:T(8,128)(2,1)S(1)}, bf16[1024,3,1024]{2,0,1:T(8,128)(2,1)}, u32[]{:S(2)}) %copy-start.2) | copy-done | bytes 6291480
  34.3 4.6 %shard_map.83.local_near_ref = f32[3,512,256]{2,1,0:T(8,128)S(1)} custom-call(s32[15]{0:T(128)S(1)} %stack.63.index_ref, bf16[256,4096]{1,0:T(8,128)(2,1)} %refs_0_.5, bf16[256,4096]{1,0:T(8,128)(2,1)} %collective-permute-done.refs_1_, bf16[3,1024,1024]{2,1,0:T(8,128)(2,1)S(1)} %bitcast.26, ...), custom_call_target="tpu_custom_call" | custom-call | flops 1 | bytes 1 | tf_op jit(solution)/shard_map/pallas_call | solution.py:146
  38.9 0.0 copy-start.3
  38.9 0.1 collective-permute-start.8
  39.0 2.1 %collective-permute-done.8.refs_3_.refs_5_ = bf16[256,1024]{1,0:T(8,128)(2,1)S(1)} collective-permute-done((bf16[256,1024]{1,0:T(8,128)(2,1)}, bf16[256,1024]{1,0:T(8,128)(2,1)S(1)}, u32[]{:S(2)}, u32[]{:S(2)}) %collective-permute-start.8) | collective-permute-done | bytes 524320 | tf_op jit(solution)/shard_map/ppermute | solution.py:422
  41.1 3.4 %shard_map.84 = bf16[2,512,256]{2,1,0:T(8,128)(2,1)S(1)} custom-call(s32[15]{0:T(128)S(1)} %stack.63.index_ref, bf16[256,1024]{1,0:T(8,128)(2,1)} %collective-permute-done.2.refs_0_.refs_2_, bf16[256,1024]{1,0:T(8,128)(2,1)} %collective-permute-done.3.refs_1_.refs_3_, bf16[256,1024]{1,0:T(8,128)(2,1)S(1)} %collective-permute-done.7.refs_2_.refs_4_, ...), custom_call_target="tpu_custom_call" | custom-call | flops 1 | bytes 1 | tf_op jit(solution)/shard_map/pallas_call | solution.py:146
  44.5 0.2 collective-permute-start.9
  44.7 1.5 %collective-permute-start.10 = (bf16[2,512,256]{2,1,0:T(8,128)(2,1)S(1)}, bf16[2,512,256]{2,1,0:T(8,128)(2,1)S(1)}, u32[]{:S(2)}, u32[]{:S(2)}) collective-permute-start(bf16[2,512,256]{2,1,0:T(8,128)(2,1)S(1)} %shard_map.84), channel_id=1, source_target_pairs={{0,8},{4,12},{8,0},{12,4},{1,9},{5,13},{9,1},{13,5},{2,10},{6,14},... | collective-permute-start | bytes 1572872 | tf_op jit(solution)/shard_map/ppermute | solution.py:422
  46.2 3.9 %shard_map.85 = bf16[1,1024,256]{2,1,0:T(8,128)(2,1)S(1)} custom-call(s32[15]{0:T(128)S(1)} %stack.63.index_ref, bf16[256,4096]{1,0:T(8,128)(2,1)} %refs_0_.5, bf16[256,4096]{1,0:T(8,128)(2,1)} %collective-permute-done.refs_1_, bf16[256,1024]{1,0:T(8,128)(2,1)} %collective-permute-done.2.refs_0_.refs_2_, ...), custom_call_target="tpu_custom_call" | custom-call | flops 1 | bytes 1 | tf_op jit(solution)/shard_map/pallas_call | solution.py:146
  50.2 0.0 copy-start.4
  50.2 0.0 copy-start.5
  50.2 0.0 copy-start.6
  50.2 4.4 %shard_map.86.local_far_ref = f32[3,512,256]{2,1,0:T(8,128)S(1)} custom-call(s32[15]{0:T(128)S(1)} %stack.63.index_ref, bf16[256,1024]{1,0:T(8,128)(2,1)} %collective-permute-done.2.refs_0_.refs_2_, bf16[256,1024]{1,0:T(8,128)(2,1)} %collective-permute-done.3.refs_1_.refs_3_, bf16[256,1024]{1,0:T(8,128)(2,1)S(1)} %collective-permute-done.7.refs_2_.refs_4_, ...), custom_call_target="tpu_custom_call" | custom-call | flops 1 | bytes 1 | tf_op jit(solution)/shard_map/pallas_call | solution.py:146
  54.7 0.0 copy-start.7
  54.7 4.2 %collective-permute-done.10.near_ref = bf16[2,512,256]{2,1,0:T(8,128)(2,1)S(1)} collective-permute-done((bf16[2,512,256]{2,1,0:T(8,128)(2,1)S(1)}, bf16[2,512,256]{2,1,0:T(8,128)(2,1)S(1)}, u32[]{:S(2)}, u32[]{:S(2)}) %collective-permute-start.10) | collective-permute-done | bytes 524320 | tf_op jit(solution)/shard_map/ppermute | solution.py:422
  58.9 1.5 %collective-permute-start.11 = (bf16[1,1024,256]{2,1,0:T(8,128)(2,1)S(1)}, bf16[1,1024,256]{2,1,0:T(8,128)(2,1)S(1)}, u32[]{:S(2)}, u32[]{:S(2)}) collective-permute-start(bf16[1,1024,256]{2,1,0:T(8,128)(2,1)S(1)} %shard_map.85), channel_id=1, source_target_pairs={{0,8},{4,12},{8,0},{12,4},{1,9},{5,13},{9,1},{13,5},{2,10},{6,14},... | collective-permute-start | bytes 1572872 | tf_op jit(solution)/shard_map/ppermute | solution.py:422
  60.4 13.3 %shard_map.87 = (bf16[256,512]{1,0:T(8,128)(2,1)S(1)}, bf16[256,512]{1,0:T(8,128)(2,1)S(1)}, bf16[256,512]{1,0:T(8,128)(2,1)S(1)}) custom-call(s32[15]{0:T(128)S(1)} %stack.63.index_ref, f32[3,512,256]{2,1,0:T(8,128)S(1)} %shard_map.83.local_near_ref, f32[3,512,256]{2,1,0:T(8,128)S(1)} %shard_map.86.local_far_ref, ...), custom_call_target="tpu_custom_call" | custom-call | flops 1 | bytes 1 | tf_op jit(solution)/shard_map/pallas_call | solution.py:235
  73.7 2.0 %shard_map.88 = (bf16[256,256]{1,0:T(8,128)(2,1)S(1)}, bf16[256,256]{1,0:T(8,128)(2,1)S(1)}, bf16[256,256]{1,0:T(8,128)(2,1)S(1)}, bf16[256,256]{1,0:T(8,128)(2,1)S(1)}) custom-call(s32[15]{0:T(128)S(1)} %stack.63.index_ref, f32[3,512,256]{2,1,0:T(8,128)S(1)} %shard_map.83.local_near_ref, f32[3,512,256]{2,1,0:T(8,128)S(1)} %shard_map.86.local_far_ref, ...), custom_call_target="tpu_custom_call" | custom-call | flops 1 | bytes 1 | tf_op jit(solution)/shard_map/pallas_call | solution.py:281
  75.7 0.1 collective-permute-start.12
  75.8 0.6 collective-permute-start.14
  76.4 1.3 collective-permute-start.15
  77.7 1.3 collective-permute-start.19
  79.0 4.6 %collective-permute-start.13 = (bf16[256,512]{1,0:T(8,128)(2,1)S(1)}, bf16[256,512]{1,0:T(8,128)(2,1)S(1)}, u32[]{:S(2)}, u32[]{:S(2)}) collective-permute-start(bf16[256,512]{1,0:T(8,128)(2,1)S(1)} %constant_dynamic-update-slice_fusion), channel_id=1, source_target_pairs={{0,1},{1,2},{2,3},{4,5},{5,6},{6,7},{8,9},{9,10},{10,11},{12,13},{... | collective-permute-start | bytes 786440 | tf_op jit(solution)/shard_map/ppermute | solution.py:425
  83.6 0.5 collective-permute-done.15
  84.1 1.3 collective-permute-start.20
  85.4 0.6 collective-permute-start.23
  86.0 4.5 %collective-permute-start.16 = (bf16[256,512]{1,0:T(8,128)(2,1)S(1)}, bf16[256,512]{1,0:T(8,128)(2,1)S(1)}, u32[]{:S(2)}, u32[]{:S(2)}) collective-permute-start(bf16[256,512]{1,0:T(8,128)(2,1)S(1)} %constant_dynamic-update-slice_fusion.2), channel_id=1, source_target_pairs={{0,1},{1,2},{2,3},{4,5},{5,6},{6,7},{8,9},{9,10},{10,11},{12,13},{... | collective-permute-start | bytes 786440 | tf_op jit(solution)/shard_map/ppermute | solution.py:425
  90.6 4.2 %collective-permute-done.20 = bf16[256,512]{1,0:T(8,128)(2,1)S(1)} collective-permute-done((bf16[256,512]{1,0:T(8,128)(2,1)S(1)}, bf16[256,512]{1,0:T(8,128)(2,1)S(1)}, u32[]{:S(2)}, u32[]{:S(2)}) %collective-permute-start.20) | collective-permute-done | bytes 262176 | tf_op jit(solution)/shard_map/ppermute | solution.py:425
  94.8 1.3 collective-permute-start.21
  96.1 0.1 collective-permute-done.16
  96.3 0.7 collective-permute-start.17
  97.0 1.6 %collective-permute-start.27 = (bf16[256,1024]{1,0:T(8,128)(2,1)S(1)}, bf16[256,1024]{1,0:T(8,128)(2,1)S(1)}, u32[]{:S(2)}, u32[]{:S(2)}) collective-permute-start(bf16[256,1024]{1,0:T(8,128)(2,1)S(1)} %get-tuple-element.57), channel_id=1, source_target_pairs={{0,8},{4,12},{8,0},{12,4},{1,9},{5,13},{9,1},{13,5},{2,10},{6,14},... | collective-permute-start | bytes 1572872 | tf_op jit(solution)/shard_map/ppermute | solution.py:422
  98.5 1.6 %collective-permute-done.23.one = bf16[256,1024]{1,0:T(8,128)(2,1)S(1)} collective-permute-done((bf16[256,1024]{1,0:T(8,128)(2,1)S(1)}, bf16[256,1024]{1,0:T(8,128)(2,1)S(1)}, u32[]{:S(2)}, u32[]{:S(2)}) %collective-permute-start.23) | collective-permute-done | bytes 524320 | tf_op jit(solution)/shard_map/ppermute | solution.py:422
  100.1 1.5 %collective-permute-start.24 = (bf16[256,1024]{1,0:T(8,128)(2,1)S(1)}, bf16[256,1024]{1,0:T(8,128)(2,1)S(1)}, u32[]{:S(2)}, u32[]{:S(2)}) collective-permute-start(bf16[256,1024]{1,0:T(8,128)(2,1)S(1)} %collective-permute-done.23.one), channel_id=1, source_target_pairs={{0,16},{16,0},{1,17},{17,1},{2,18},{18,2},{3,19},{19,3},{4,20},{20... | collective-permute-start | bytes 1572872 | tf_op jit(solution)/shard_map/ppermute | solution.py:479
  101.7 8.6 %collective-permute-done.21.above_2 = bf16[256,1024]{1,0:T(8,128)(2,1)S(1)} collective-permute-done((bf16[256,1024]{1,0:T(8,128)(2,1)S(1)}, bf16[256,1024]{1,0:T(8,128)(2,1)S(1)}, u32[]{:S(2)}, u32[]{:S(2)}) %collective-permute-start.21) | collective-permute-done | bytes 524320 | tf_op jit(solution)/shard_map/ppermute | solution.py:425
  110.3 0.8 collective-permute-done.27.one
  111.1 2.4 %collective-permute-done.24.other = bf16[256,1024]{1,0:T(8,128)(2,1)S(1)} collective-permute-done((bf16[256,1024]{1,0:T(8,128)(2,1)S(1)}, bf16[256,1024]{1,0:T(8,128)(2,1)S(1)}, u32[]{:S(2)}, u32[]{:S(2)}) %collective-permute-start.24) | collective-permute-done | bytes 524320 | tf_op jit(solution)/shard_map/ppermute | solution.py:479
  113.5 1.5 %collective-permute-start.28 = (bf16[256,1024]{1,0:T(8,128)(2,1)S(1)}, bf16[256,1024]{1,0:T(8,128)(2,1)S(1)}, u32[]{:S(2)}, u32[]{:S(2)}) collective-permute-start(bf16[256,1024]{1,0:T(8,128)(2,1)S(1)} %collective-permute-done.27.one), channel_id=1, source_target_pairs={{0,16},{16,0},{1,17},{17,1},{2,18},{18,2},{3,19},{19,3},{4,20},{20... | collective-permute-start | bytes 1572872 | tf_op jit(solution)/shard_map/ppermute | solution.py:479
  115.0 0.1 pad_maximum_fusion.own
  115.1 1.3 collective-permute-start.22
  116.4 0.7 collective-permute-start.18
  117.1 4.7 %shard_map.89 = (f32[256,1024]{1,0:T(8,128)S(1)}, bf16[256,1024]{1,0:T(8,128)(2,1)S(1)}, bf16[1024,1024]{1,0:T(8,128)(2,1)S(1)}) custom-call(s32[15]{0:T(128)S(1)} %stack.63.index_ref, bf16[256,1024]{1,0:T(8,128)(2,1)S(1)} %pad_maximum_fusion.own, bf16[256,1024]{1,0:T(8,128)(2,1)S(1)} %constant_dynamic-update-slice_fusion.4.below_1, ...), custom_call_target="tpu_custom_call" | custom-call | flops 1 | bytes 1 | tf_op jit(solution)/shard_map/pallas_call | solution.py:348
  121.8 6.0 %collective-permute-done.28.other = bf16[256,1024]{1,0:T(8,128)(2,1)S(1)} collective-permute-done((bf16[256,1024]{1,0:T(8,128)(2,1)S(1)}, bf16[256,1024]{1,0:T(8,128)(2,1)S(1)}, u32[]{:S(2)}, u32[]{:S(2)}) %collective-permute-start.28) | collective-permute-done | bytes 524320 | tf_op jit(solution)/shard_map/ppermute | solution.py:479
  127.8 0.5 collective-permute-start.30
  128.3 3.3 %collective-permute-done.22.above = bf16[256,1024]{1,0:T(8,128)(2,1)S(1)} collective-permute-done((bf16[256,1024]{1,0:T(8,128)(2,1)S(1)}, bf16[256,1024]{1,0:T(8,128)(2,1)S(1)}, u32[]{:S(2)}, u32[]{:S(2)}) %collective-permute-start.22) | collective-permute-done | bytes 524320 | tf_op jit(solution)/shard_map/ppermute | solution.py:425
  131.6 2.6 %shard_map.90 = bf16[256,1024]{1,0:T(8,128)(2,1)} custom-call(s32[15]{0:T(128)S(1)} %stack.63.index_ref, bf16[256,1024]{1,0:T(8,128)(2,1)S(1)} %collective-permute-done.18.below, bf16[256,1024]{1,0:T(8,128)(2,1)S(1)} %collective-permute-done.22.above, bf16[1024,1024]{1,0:T(8,128)(2,1)S(1)} %get-tuple-element.55.weight, ...), custom_call_target="tpu_custom_call" | custom-call | flops 1 | bytes 1 | tf_op jit(solution)/shard_map/pallas_call | solution.py:392
  (38 shorter events, 0.2 us)
Async XLA Ops:
  0.0 26.2 %copy-start = (bf16[4096,4]{0,1:T(4,128)(2,1)S(1)}, bf16[4096,4]{0,1:T(4,128)(2,1)}, u32[]{:S(2)}) copy-start(bf16[4096,4]{0,1:T(4,128)(2,1)} %param.10) | copy-start | bytes 98308
  5.6 9.0 %collective-permute-start.1 = (bf16[3,1024,512]{2,1,0:T(8,128)(2,1)}, bf16[3,1024,512]{2,1,0:T(8,128)(2,1)S(1)}, u32[]{:S(2)}, u32[]{:S(2)}) collective-permute-start(bf16[3,1024,512]{2,1,0:T(8,128)(2,1)} %dynamic-slice_bitcast_fusion), channel_id=1, source_target_pairs={{0,4},{4,0},{8,12},{12,8},{1,5},{5,1},{9,13},{13,9},{2,6},{6,2},{1... | collective-permute-start | bytes 9437192 | tf_op jit(solution)/shard_map/ppermute | solution.py:422
  6.1 8.5 %collective-permute-start = (bf16[256,4096]{1,0:T(8,128)(2,1)}, bf16[256,4096]{1,0:T(8,128)(2,1)}, u32[]{:S(2)}, u32[]{:S(2)}) collective-permute-start(bf16[256,4096]{1,0:T(8,128)(2,1)} %refs_0_.5), channel_id=1, source_target_pairs={{0,4},{4,0},{8,12},{12,8},{1,5},{5,1},{9,13},{13,9},{2,6},{6,2},{1... | collective-permute-start | bytes 6291464 | tf_op jit(solution)/shard_map/ppermute | solution.py:422
  6.1 15.7 %collective-permute-start.2 = (bf16[256,1024]{1,0:T(8,128)(2,1)}, bf16[256,1024]{1,0:T(8,128)(2,1)}, u32[]{:S(2)}, u32[]{:S(2)}) collective-permute-start(bf16[256,1024]{1,0:T(8,128)(2,1)} %constant_dynamic-slice_fusion.2), channel_id=1, source_target_pairs={{0,8},{4,12},{8,0},{12,4},{1,9},{5,13},{9,1},{13,5},{2,10},{6,14},... | collective-permute-start | bytes 1572872 | tf_op jit(solution)/shard_map/ppermute | solution.py:422
  14.6 2.8 %copy-start.1 = (bf16[1024,3,1024]{2,0,1:T(8,128)(2,1)S(1)}, bf16[1024,3,1024]{2,0,1:T(8,128)(2,1)}, u32[]{:S(2)}) copy-start(bf16[1024,3,1024]{2,0,1:T(8,128)(2,1)} %param.9) | copy-start | bytes 18874372
  21.8 17.1 %collective-permute-start.3 = (bf16[256,1024]{1,0:T(8,128)(2,1)}, bf16[256,1024]{1,0:T(8,128)(2,1)}, u32[]{:S(2)}, u32[]{:S(2)}) collective-permute-start(bf16[256,1024]{1,0:T(8,128)(2,1)} %collective-permute-done.2.refs_0_.refs_2_), channel_id=1, source_target_pairs={{0,1},{1,0},{2,3},{3,2},{4,5},{5,4},{6,7},{7,6},{8,9},{9,8},{10,11... | collective-permute-start | bytes 1572872 | tf_op jit(solution)/shard_map/ppermute | solution.py:425
  24.7 14.2 %collective-permute-start.4 = (bf16[2,512,256]{2,1,0:T(8,128)(2,1)}, bf16[2,512,256]{2,1,0:T(8,128)(2,1)}, u32[]{:S(2)}, u32[]{:S(2)}) collective-permute-start(bf16[2,512,256]{2,1,0:T(8,128)(2,1)} %shard_map.82), channel_id=1, source_target_pairs={{0,8},{4,12},{8,0},{12,4},{1,9},{5,13},{9,1},{13,5},{2,10},{6,14},... | collective-permute-start | bytes 1572872 | tf_op jit(solution)/shard_map/ppermute | solution.py:422
  28.5 1.2 collective-permute-start.5
  28.6 10.4 %collective-permute-start.7 = (bf16[256,1024]{1,0:T(8,128)(2,1)}, bf16[256,1024]{1,0:T(8,128)(2,1)S(1)}, u32[]{:S(2)}, u32[]{:S(2)}) collective-permute-start(bf16[256,1024]{1,0:T(8,128)(2,1)} %collective-permute-done.2.refs_0_.refs_2_), channel_id=1, source_target_pairs={{0,4},{4,0},{8,12},{12,8},{1,5},{5,1},{9,13},{13,9},{2,6},{6,2},{1... | collective-permute-start | bytes 1572872 | tf_op jit(solution)/shard_map/ppermute | solution.py:422
  29.7 9.2 %collective-permute-start.6 = (f32[8,256]{1,0:T(8,128)S(1)}, f32[8,256]{1,0:T(8,128)S(1)}, u32[]{:S(2)}, u32[]{:S(2)}) collective-permute-start(f32[8,256]{1,0:T(8,128)S(1)} %pad_maximum_fusion.1.rate_near_ref), channel_id=1, source_target_pairs={{0,8},{4,12},{8,0},{12,4},{1,9},{5,13},{9,1},{13,5},{2,10},{6,14},... | collective-permute-start | bytes 24584 | tf_op jit(solution)/shard_map/ppermute | solution.py:422
  31.5 2.8 %copy-start.2 = (bf16[1024,3,1024]{2,0,1:T(8,128)(2,1)S(1)}, bf16[1024,3,1024]{2,0,1:T(8,128)(2,1)}, u32[]{:S(2)}) copy-start(bf16[1024,3,1024]{2,0,1:T(8,128)(2,1)} %param.9) | copy-start | bytes 18874372
  38.9 5.6 %copy-start.3 = (bf16[1024,1024]{1,0:T(8,128)(2,1)S(1)}, bf16[1024,1024]{1,0:T(8,128)(2,1)}, u32[]{:S(2)}) copy-start(bf16[1024,1024]{1,0:T(8,128)(2,1)} %own_w.1) | copy-start | bytes 6291460
  38.9 2.2 %collective-permute-start.8 = (bf16[256,1024]{1,0:T(8,128)(2,1)}, bf16[256,1024]{1,0:T(8,128)(2,1)S(1)}, u32[]{:S(2)}, u32[]{:S(2)}) collective-permute-start(bf16[256,1024]{1,0:T(8,128)(2,1)} %collective-permute-done.3.refs_1_.refs_3_), channel_id=1, source_target_pairs={{0,4},{4,0},{8,12},{12,8},{1,5},{5,1},{9,13},{13,9},{2,6},{6,2},{1... | collective-permute-start | bytes 1572872 | tf_op jit(solution)/shard_map/ppermute | solution.py:422
  44.5 5.7 %collective-permute-start.9 = (bf16[1024,1024]{1,0:T(8,128)(2,1)S(1)}, bf16[1024,1024]{1,0:T(8,128)(2,1)S(1)}, u32[]{:S(2)}, u32[]{:S(2)}) collective-permute-start(bf16[1024,1024]{1,0:T(8,128)(2,1)S(1)} %copy-done.3), channel_id=1, source_target_pairs={{0,4},{4,0},{8,12},{12,8},{1,5},{5,1},{9,13},{13,9},{2,6},{6,2},{1... | collective-permute-start | bytes 6291464 | tf_op jit(solution)/shard_map/ppermute | solution.py:422
  44.7 14.2 %collective-permute-start.10 = (bf16[2,512,256]{2,1,0:T(8,128)(2,1)S(1)}, bf16[2,512,256]{2,1,0:T(8,128)(2,1)S(1)}, u32[]{:S(2)}, u32[]{:S(2)}) collective-permute-start(bf16[2,512,256]{2,1,0:T(8,128)(2,1)S(1)} %shard_map.84), channel_id=1, source_target_pairs={{0,8},{4,12},{8,0},{12,4},{1,9},{5,13},{9,1},{13,5},{2,10},{6,14},... | collective-permute-start | bytes 1572872 | tf_op jit(solution)/shard_map/ppermute | solution.py:422
  50.2 10.2 %copy-start.4 = (bf16[4,256,512]{2,1,0:T(8,128)(2,1)S(1)}, bf16[4,256,512]{2,1,0:T(8,128)(2,1)}, u32[]{:S(2)}) copy-start(bf16[4,256,512]{2,1,0:T(8,128)(2,1)} %gate_ref.1) | copy-start | bytes 3145732
  50.2 10.2 %copy-start.5 = (bf16[4,256,512]{2,1,0:T(8,128)(2,1)S(1)}, bf16[4,256,512]{2,1,0:T(8,128)(2,1)}, u32[]{:S(2)}) copy-start(bf16[4,256,512]{2,1,0:T(8,128)(2,1)} %up_ref.1) | copy-start | bytes 3145732
  50.2 10.2 %copy-start.6 = (bf16[4,256,512]{2,1,0:T(8,128)(2,1)S(1)}, bf16[4,256,512]{2,1,0:T(8,128)(2,1)}, u32[]{:S(2)}) copy-start(bf16[4,256,512]{2,1,0:T(8,128)(2,1)} %down_ref.1) | copy-start | bytes 3145732
  54.7 19.0 %copy-start.7 = (f32[1024]{0:T(1024)S(1)}, f32[1024]{0:T(1024)}, u32[]{:S(2)}) copy-start(f32[1024]{0:T(1024)} %param.14) | copy-start | bytes 12292
  58.9 14.8 %collective-permute-start.11 = (bf16[1,1024,256]{2,1,0:T(8,128)(2,1)S(1)}, bf16[1,1024,256]{2,1,0:T(8,128)(2,1)S(1)}, u32[]{:S(2)}, u32[]{:S(2)}) collective-permute-start(bf16[1,1024,256]{2,1,0:T(8,128)(2,1)S(1)} %shard_map.85), channel_id=1, source_target_pairs={{0,8},{4,12},{8,0},{12,4},{1,9},{5,13},{9,1},{13,5},{2,10},{6,14},... | collective-permute-start | bytes 1572872 | tf_op jit(solution)/shard_map/ppermute | solution.py:422
  75.7 2.0 %collective-permute-start.12 = (bf16[256,256]{1,0:T(8,128)(2,1)S(1)}, bf16[256,256]{1,0:T(8,128)(2,1)S(1)}, u32[]{:S(2)}, u32[]{:S(2)}) collective-permute-start(bf16[256,256]{1,0:T(8,128)(2,1)S(1)} %get-tuple-element.48), channel_id=1, source_target_pairs={{0,4},{4,0},{8,12},{12,8},{1,5},{5,1},{9,13},{13,9},{2,6},{6,2},{1... | collective-permute-start | bytes 393224 | tf_op jit(solution)/shard_map/ppermute | solution.py:422
  75.8 7.8 %collective-permute-start.14 = (bf16[256,256]{1,0:T(8,128)(2,1)S(1)}, bf16[256,256]{1,0:T(8,128)(2,1)S(1)}, u32[]{:S(2)}, u32[]{:S(2)}) collective-permute-start(bf16[256,256]{1,0:T(8,128)(2,1)S(1)} %get-tuple-element.49), channel_id=1, source_target_pairs={{0,8},{4,12},{8,0},{12,4},{1,9},{5,13},{9,1},{13,5},{2,10},{6,14},... | collective-permute-start | bytes 393224 | tf_op jit(solution)/shard_map/ppermute | solution.py:422
  76.4 7.7 %collective-permute-start.15 = (bf16[256,256]{1,0:T(8,128)(2,1)S(1)}, bf16[256,256]{1,0:T(8,128)(2,1)S(1)}, u32[]{:S(2)}, u32[]{:S(2)}) collective-permute-start(bf16[256,256]{1,0:T(8,128)(2,1)S(1)} %get-tuple-element.50), channel_id=1, source_target_pairs={{0,12},{4,8},{8,4},{12,0},{1,13},{5,9},{9,5},{13,1},{2,14},{6,10},... | collective-permute-start | bytes 393224 | tf_op jit(solution)/shard_map/ppermute | solution.py:422
  77.7 12.8 %collective-permute-start.19 = (bf16[256,512]{1,0:T(8,128)(2,1)S(1)}, bf16[256,512]{1,0:T(8,128)(2,1)S(1)}, u32[]{:S(2)}, u32[]{:S(2)}) collective-permute-start(bf16[256,512]{1,0:T(8,128)(2,1)S(1)} %constant_dynamic-update-slice_fusion), channel_id=1, source_target_pairs={{1,0},{2,1},{3,2},{5,4},{6,5},{7,6},{9,8},{10,9},{11,10},{13,12},{... | collective-permute-start | bytes 786440 | tf_op jit(solution)/shard_map/ppermute | solution.py:425
  79.0 11.6 %collective-permute-start.13 = (bf16[256,512]{1,0:T(8,128)(2,1)S(1)}, bf16[256,512]{1,0:T(8,128)(2,1)S(1)}, u32[]{:S(2)}, u32[]{:S(2)}) collective-permute-start(bf16[256,512]{1,0:T(8,128)(2,1)S(1)} %constant_dynamic-update-slice_fusion), channel_id=1, source_target_pairs={{0,1},{1,2},{2,3},{4,5},{5,6},{6,7},{8,9},{9,10},{10,11},{12,13},{... | collective-permute-start | bytes 786440 | tf_op jit(solution)/shard_map/ppermute | solution.py:425
  84.1 10.7 %collective-permute-start.20 = (bf16[256,512]{1,0:T(8,128)(2,1)S(1)}, bf16[256,512]{1,0:T(8,128)(2,1)S(1)}, u32[]{:S(2)}, u32[]{:S(2)}) collective-permute-start(bf16[256,512]{1,0:T(8,128)(2,1)S(1)} %constant_dynamic-update-slice_fusion.2), channel_id=1, source_target_pairs={{1,0},{2,1},{3,2},{5,4},{6,5},{7,6},{9,8},{10,9},{11,10},{13,12},{... | collective-permute-start | bytes 786440 | tf_op jit(solution)/shard_map/ppermute | solution.py:425
  85.4 14.8 %collective-permute-start.23 = (bf16[256,1024]{1,0:T(8,128)(2,1)S(1)}, bf16[256,1024]{1,0:T(8,128)(2,1)S(1)}, u32[]{:S(2)}, u32[]{:S(2)}) collective-permute-start(bf16[256,1024]{1,0:T(8,128)(2,1)S(1)} %get-tuple-element.51), channel_id=1, source_target_pairs={{0,8},{4,12},{8,0},{12,4},{1,9},{5,13},{9,1},{13,5},{2,10},{6,14},... | collective-permute-start | bytes 1572872 | tf_op jit(solution)/shard_map/ppermute | solution.py:422
  86.0 10.3 %collective-permute-start.16 = (bf16[256,512]{1,0:T(8,128)(2,1)S(1)}, bf16[256,512]{1,0:T(8,128)(2,1)S(1)}, u32[]{:S(2)}, u32[]{:S(2)}) collective-permute-start(bf16[256,512]{1,0:T(8,128)(2,1)S(1)} %constant_dynamic-update-slice_fusion.2), channel_id=1, source_target_pairs={{0,1},{1,2},{2,3},{4,5},{5,6},{6,7},{8,9},{9,10},{10,11},{12,13},{... | collective-permute-start | bytes 786440 | tf_op jit(solution)/shard_map/ppermute | solution.py:425
  94.8 15.5 %collective-permute-start.21 = (bf16[256,1024]{1,0:T(8,128)(2,1)S(1)}, bf16[256,1024]{1,0:T(8,128)(2,1)S(1)}, u32[]{:S(2)}, u32[]{:S(2)}) collective-permute-start(bf16[256,1024]{1,0:T(8,128)(2,1)S(1)} %constant_dynamic-update-slice_fusion.6.above_1), channel_id=1, source_target_pairs={{1,0},{2,1},{5,4},{6,5},{9,8},{10,9},{13,12},{14,13},{17,16},{18,1... | collective-permute-start | bytes 1572872 | tf_op jit(solution)/shard_map/ppermute | solution.py:425
  96.3 14.0 %collective-permute-start.17 = (bf16[256,1024]{1,0:T(8,128)(2,1)S(1)}, bf16[256,1024]{1,0:T(8,128)(2,1)S(1)}, u32[]{:S(2)}, u32[]{:S(2)}) collective-permute-start(bf16[256,1024]{1,0:T(8,128)(2,1)S(1)} %constant_dynamic-update-slice_fusion.4.below_1), channel_id=1, source_target_pairs={{1,2},{2,3},{5,6},{6,7},{9,10},{10,11},{13,14},{14,15},{17,18},{18... | collective-permute-start | bytes 1572872 | tf_op jit(solution)/shard_map/ppermute | solution.py:425
  97.0 14.1 %collective-permute-start.27 = (bf16[256,1024]{1,0:T(8,128)(2,1)S(1)}, bf16[256,1024]{1,0:T(8,128)(2,1)S(1)}, u32[]{:S(2)}, u32[]{:S(2)}) collective-permute-start(bf16[256,1024]{1,0:T(8,128)(2,1)S(1)} %get-tuple-element.57), channel_id=1, source_target_pairs={{0,8},{4,12},{8,0},{12,4},{1,9},{5,13},{9,1},{13,5},{2,10},{6,14},... | collective-permute-start | bytes 1572872 | tf_op jit(solution)/shard_map/ppermute | solution.py:422
  100.1 13.3 %collective-permute-start.24 = (bf16[256,1024]{1,0:T(8,128)(2,1)S(1)}, bf16[256,1024]{1,0:T(8,128)(2,1)S(1)}, u32[]{:S(2)}, u32[]{:S(2)}) collective-permute-start(bf16[256,1024]{1,0:T(8,128)(2,1)S(1)} %collective-permute-done.23.one), channel_id=1, source_target_pairs={{0,16},{16,0},{1,17},{17,1},{2,18},{18,2},{3,19},{19,3},{4,20},{20... | collective-permute-start | bytes 1572872 | tf_op jit(solution)/shard_map/ppermute | solution.py:479
  111.1 6.0 %collective-permute-start.25 = (bf16[256,1024]{1,0:T(8,128)(2,1)S(1)}, bf16[256,1024]{1,0:T(8,128)(2,1)S(1)}, u32[]{:S(2)}, u32[]{:S(2)}) collective-permute-start(bf16[256,1024]{1,0:T(8,128)(2,1)S(1)} %collective-permute-done.23.one), channel_id=1, source_target_pairs={{0,4},{4,0},{8,12},{12,8},{1,5},{5,1},{9,13},{13,9},{2,6},{6,2},{1... | collective-permute-start | bytes 1572872 | tf_op jit(solution)/shard_map/ppermute | solution.py:422
  113.5 3.6 %collective-permute-start.26 = (bf16[256,1024]{1,0:T(8,128)(2,1)S(1)}, bf16[256,1024]{1,0:T(8,128)(2,1)S(1)}, u32[]{:S(2)}, u32[]{:S(2)}) collective-permute-start(bf16[256,1024]{1,0:T(8,128)(2,1)S(1)} %collective-permute-done.24.other), channel_id=1, source_target_pairs={{0,4},{4,0},{8,12},{12,8},{1,5},{5,1},{9,13},{13,9},{2,6},{6,2},{1... | collective-permute-start | bytes 1572872 | tf_op jit(solution)/shard_map/ppermute | solution.py:422
  113.5 14.3 %collective-permute-start.28 = (bf16[256,1024]{1,0:T(8,128)(2,1)S(1)}, bf16[256,1024]{1,0:T(8,128)(2,1)S(1)}, u32[]{:S(2)}, u32[]{:S(2)}) collective-permute-start(bf16[256,1024]{1,0:T(8,128)(2,1)S(1)} %collective-permute-done.27.one), channel_id=1, source_target_pairs={{0,16},{16,0},{1,17},{17,1},{2,18},{18,2},{3,19},{19,3},{4,20},{20... | collective-permute-start | bytes 1572872 | tf_op jit(solution)/shard_map/ppermute | solution.py:479
  115.1 16.5 %collective-permute-start.22 = (bf16[256,1024]{1,0:T(8,128)(2,1)S(1)}, bf16[256,1024]{1,0:T(8,128)(2,1)S(1)}, u32[]{:S(2)}, u32[]{:S(2)}) collective-permute-start(bf16[256,1024]{1,0:T(8,128)(2,1)S(1)} %collective-permute-done.21.above_2), channel_id=1, source_target_pairs={{1,0},{5,4},{9,8},{13,12},{17,16},{21,20},{25,24},{29,28}} | collective-permute-start | bytes 1572872 | tf_op jit(solution)/shard_map/ppermute | solution.py:425
  116.4 15.2 %collective-permute-start.18 = (bf16[256,1024]{1,0:T(8,128)(2,1)S(1)}, bf16[256,1024]{1,0:T(8,128)(2,1)S(1)}, u32[]{:S(2)}, u32[]{:S(2)}) collective-permute-start(bf16[256,1024]{1,0:T(8,128)(2,1)S(1)} %collective-permute-done.17.below_2), channel_id=1, source_target_pairs={{2,3},{6,7},{10,11},{14,15},{18,19},{22,23},{26,27},{30,31}} | collective-permute-start | bytes 1572872 | tf_op jit(solution)/shard_map/ppermute | solution.py:425
  127.8 3.8 %collective-permute-start.29 = (bf16[256,1024]{1,0:T(8,128)(2,1)S(1)}, bf16[256,1024]{1,0:T(8,128)(2,1)S(1)}, u32[]{:S(2)}, u32[]{:S(2)}) collective-permute-start(bf16[256,1024]{1,0:T(8,128)(2,1)S(1)} %collective-permute-done.27.one), channel_id=1, source_target_pairs={{0,4},{4,0},{8,12},{12,8},{1,5},{5,1},{9,13},{13,9},{2,6},{6,2},{1... | collective-permute-start | bytes 1572872 | tf_op jit(solution)/shard_map/ppermute | solution.py:422
  127.8 3.8 %collective-permute-start.30 = (bf16[256,1024]{1,0:T(8,128)(2,1)S(1)}, bf16[256,1024]{1,0:T(8,128)(2,1)S(1)}, u32[]{:S(2)}, u32[]{:S(2)}) collective-permute-start(bf16[256,1024]{1,0:T(8,128)(2,1)S(1)} %collective-permute-done.28.other), channel_id=1, source_target_pairs={{0,4},{4,0},{8,12},{12,8},{1,5},{5,1},{9,13},{13,9},{2,6},{6,2},{1... | collective-permute-start | bytes 1572872 | tf_op jit(solution)/shard_map/ppermute | solution.py:422

commit v16 on v15

--- a/solution.py
+++ b/solution.py
@@ -111,20 +111,22 @@
 CHIP, CORE, HEAD, PLACE, SEQ, LAST, PARTS, BLOCKS, ORDER = 0, 1, 2, 3, 4, 5, 6, 10, 14
 
 
-def project_kernel(wholes, pairs, index_ref, *refs):
-    keep_ref, given_ref, out_ref = refs[-3:]
-    depth = keep_ref.shape[1]
+def project_kernel(wholes, pairs, count, index_ref, *refs):
+    keep_refs, given_refs, out_ref = refs[-2 * count - 1 : -count - 1], refs[-count - 1 : -1], refs[-1]
+    depth = keep_refs[0].shape[1]
     core = index_ref[CORE]
     mine = pl.ds(pl.multiple_of(core * depth, depth), depth)
     others = pl.ds(pl.multiple_of((1 - core) * depth, depth), depth)
     rows = refs[0].shape[0]
 
-    def store(block, total):
-        out_ref[0, block * rows : (block + 1) * rows, :] = total.astype(out_ref.dtype)
+    def store(block, first, second):
+        for i in range(count):
+            total = dot(first, keep_refs[i][0]) + dot(second, given_refs[i][0])
+            out_ref[i, block * rows : (block + 1) * rows, :] = total.astype(out_ref.dtype)
 
     for block in range(wholes):
         ref = refs[block]
-        store(block, dot(ref[:, mine], keep_ref[0]) + dot(ref[:, others], given_ref[0]))
+        store(block, ref[:, mine], ref[:, others])
     for swapped in range(2 if pairs else 0):
 
         @pl.when(index_ref[ORDER] == swapped)
@@ -132,7 +134,7 @@
             for pair in range(pairs):
                 first = refs[wholes + 2 * pair + swapped]
                 second = refs[wholes + 2 * pair + 1 - swapped]
-                store(wholes + pair, dot(first[...], keep_ref[0]) + dot(second[...], given_ref[0]))
+                store(wholes + pair, first[...], second[...])
 
 
 def project(index, whole, pairs, weight, given, size, own, start, count, dtype):
@@ -144,22 +146,26 @@
         return idx[CHIP] if own else 1 - idx[CHIP]
 
     return pl.pallas_call(
-        functools.partial(project_kernel, len(whole), len(pairs)),
+        functools.partial(project_kernel, len(whole), len(pairs), count),
         out_shape=jax.ShapeDtypeStruct((count, number * rows, size), dtype),
         grid_spec=pltpu.PrefetchScalarGridSpec(
             num_scalar_prefetch=1,
-            grid=(count,),
+            grid=(1,),
             in_specs=[pl.BlockSpec((rows, 2 * depth), lambda i, idx: (0, idx[CHIP]))] * len(whole)
             + [pl.BlockSpec((rows, depth), lambda i, idx: (0, 0))] * (2 * len(pairs))
             + [
-                pl.BlockSpec((1, depth, size), lambda i, idx: ((start + i) % 3, 0, 2 * idx[CORE] + which(idx))),
-                pl.BlockSpec((1, depth, size), lambda i, idx: ((start + i) % 3, 0, which(idx))),
+                pl.BlockSpec((1, depth, size), lambda i, idx, c=c: ((start + c) % 3, 0, 2 * idx[CORE] + which(idx)))
+                for c in range(count)
+            ]
+            + [
+                pl.BlockSpec((1, depth, size), lambda i, idx, c=c: ((start + c) % 3, 0, which(idx)))
+                for c in range(count)
             ],
-            out_specs=pl.BlockSpec((1, number * rows, size), lambda i, idx: (i, 0, 0)),
+            out_specs=pl.BlockSpec((count, number * rows, size), lambda i, idx: (0, 0, 0)),
         ),
         compiler_params=params(),
         cost_estimate=pl.CostEstimate(flops=1, bytes_accessed=1, transcendentals=0),
-    )(index, *whole, *[block for pair in pairs for block in pair], weight, given)
+    )(index, *whole, *[block for pair in pairs for block in pair], *[weight] * count, *[given] * count)
 
 
 def half_tanh(value):

time: 135 us -> 134 us (level)
  Pallas kernels: 43.4 us -> 41.4 us
    pallas_call x5, Pallas kernels: 20.7 us -> 18.7 us  [project(): pl.pallas_call(functools.partial(project_kernel, len(whole), len(pairs),...]
  transfers between devices with their start and end apart: 31 -> 31, of which waited for: 13 -> 14; matrix products, arithmetic and copies ran while one was open for 3% -> 3% of each run, Pallas kernels for 26% -> 25%
where the time goes in v16:
time: 134 us; the launch traced here: 133 us
  Pallas kernels  41.4 us (31%)
  waiting for transfers between devices  41.2 us (31%)
  starting transfers between devices  35.5 us (26%)
  local copies, waits for them, and re-layouts  12.7 us (9%)
  matrix products  2.25 us (2%)
    pallas_call x5, Pallas kernels, project(): pl.pallas_call(functools.partial(project_kernel, len(whole), len(pairs),...  18.7 us
    ppermute x9, starting transfers between devices, hop(): return lax.ppermute(array, 'head', links)  18.6 us
    ppermute x20, waiting for transfers between devices, across(): return lax.ppermute(array, 'seq', [(i, i ^ bit) for i in range(4)])  16.6 us
    ppermute x9, waiting for transfers between devices, hop(): return lax.ppermute(array, 'head', links)  16.2 us
    ppermute x20, starting transfers between devices, across(): return lax.ppermute(array, 'seq', [(i, i ^ bit) for i in range(4)])  13.9 us
    pallas_call x1, Pallas kernels, update(): pl.pallas_call(update_kernel, out_shape=[out] * 3, grid_spec=pltpu.Prefet...  13.3 us
    ppermute x2, waiting for transfers between devices, swap_groups(): return lax.ppermute(array, 'groups', [(0, 1), (1, 0)])  8.4 us
    unnamed x20, local copies, waits for them, and re-layouts  5.66 us
  transfers between devices with their start and end apart: 31, of which 14 were waited for; matrix products, arithmetic and copies ran while one was open for 3% of the time, Pallas kernels for 25%

profile of v16, /device:TPU:0, one launch (start us, length us, event | category | flops | bytes accessed | tf_op | source)
XLA Modules:
  0.0 133.5 jit_solution(12405199199502092229)
XLA Ops:
  0.0 1.9 %constant_dynamic-slice_fusion.2 = bf16[256,1024]{1,0:T(8,128)(2,1)} fusion(bf16[256,4096]{1,0:T(8,128)(2,1)} %refs_0_.5, s32[]{:T(128)S(6)} %select_n.23), kind=kLoop, calls=%fused_computation.15 | loop fusion | bytes 1048580 | tf_op jit(solution)/shard_map/dynamic_slice | solution.py:440
  1.9 3.7 %dynamic-slice_bitcast_fusion = bf16[3,1024,512]{2,1,0:T(8,128)(2,1)} fusion(bf16[1024,3,1024]{2,0,1:T(8,128)(2,1)} %param.9, s32[]{:T(128)S(6)} %select_n.24), kind=kLoop, calls=%fused_computation | loop fusion | bytes 6291460 | tf_op jit(solution)/shard_map/dynamic_slice | solution.py:444
  5.6 0.5 collective-permute-start.1
  6.1 0.1 collective-permute-start
  6.1 2.9 %collective-permute-start.2 = (bf16[256,1024]{1,0:T(8,128)(2,1)}, bf16[256,1024]{1,0:T(8,128)(2,1)}, u32[]{:S(2)}, u32[]{:S(2)}) collective-permute-start(bf16[256,1024]{1,0:T(8,128)(2,1)} %constant_dynamic-slice_fusion.2), channel_id=1, source_target_pairs={{0,8},{4,12},{8,0},{12,4},{1,9},{5,13},{9,1},{13,5},{2,10},{6,14},... | collective-permute-start | bytes 1572872 | tf_op jit(solution)/shard_map/ppermute | solution.py:428
  9.1 0.1 stack.63.index_ref
  9.2 5.5 %collective-permute-done.refs_1_ = bf16[256,4096]{1,0:T(8,128)(2,1)} collective-permute-done((bf16[256,4096]{1,0:T(8,128)(2,1)}, bf16[256,4096]{1,0:T(8,128)(2,1)}, u32[]{:S(2)}, u32[]{:S(2)}) %collective-permute-start) | collective-permute-done | bytes 2097184 | tf_op jit(solution)/shard_map/ppermute | solution.py:428
  14.6 2.8 %copy-done.1 = bf16[1024,3,1024]{2,0,1:T(8,128)(2,1)S(1)} copy-done((bf16[1024,3,1024]{2,0,1:T(8,128)(2,1)S(1)}, bf16[1024,3,1024]{2,0,1:T(8,128)(2,1)}, u32[]{:S(2)}) %copy-start.1) | copy-done | bytes 6291480
  17.4 4.1 %shard_map.82 = bf16[2,512,256]{2,1,0:T(8,128)(2,1)} custom-call(s32[15]{0:T(128)S(1)} %stack.63.index_ref, bf16[256,4096]{1,0:T(8,128)(2,1)} %refs_0_.5, bf16[256,4096]{1,0:T(8,128)(2,1)} %collective-permute-done.refs_1_, bf16[3,1024,1024]{2,1,0:T(8,128)(2,1)S(1)} %bitcast.25, bf16[3,1024,1024]{2,1,0:T(8,128)(2,1)S(1)} %bitcast.26, ...), custom_call_target="tpu_custom_call" | custom-call | flops 1 | bytes 1 | tf_op jit(solution)/shard_map/pallas_call | solution.py:148
  21.5 2.9 %collective-permute-start.3 = (bf16[256,1024]{1,0:T(8,128)(2,1)}, bf16[256,1024]{1,0:T(8,128)(2,1)}, u32[]{:S(2)}, u32[]{:S(2)}) collective-permute-start(bf16[256,1024]{1,0:T(8,128)(2,1)} %collective-permute-done.2.refs_0_.refs_2_), channel_id=1, source_target_pairs={{0,1},{1,0},{2,3},{3,2},{4,5},{5,4},{6,7},{7,6},{8,9},{9,8},{10,11... | collective-permute-start | bytes 1572872 | tf_op jit(solution)/shard_map/ppermute | solution.py:431
  24.4 1.5 %collective-permute-start.4 = (bf16[2,512,256]{2,1,0:T(8,128)(2,1)}, bf16[2,512,256]{2,1,0:T(8,128)(2,1)}, u32[]{:S(2)}, u32[]{:S(2)}) collective-permute-start(bf16[2,512,256]{2,1,0:T(8,128)(2,1)} %shard_map.82), channel_id=1, source_target_pairs={{0,8},{4,12},{8,0},{12,4},{1,9},{5,13},{9,1},{13,5},{2,10},{6,14},... | collective-permute-start | bytes 1572872 | tf_op jit(solution)/shard_map/ppermute | solution.py:428
  25.9 2.3 %compare_select_fusion = f32[4,256]{1,0:T(4,128)S(1)} fusion(bf16[256,4096]{1,0:T(8,128)(2,1)} %refs_0_.5, bf16[4096,4]{0,1:T(4,128)(2,1)S(1)} %copy-done), kind=kOutput, calls=%fused_computation.11 | convolution fusion | flops 8394752 | bytes 2134016 | tf_op jit(solution)/shard_map/dot_general | solution.py:456
  28.2 0.1 collective-permute-start.5
  28.3 0.5 collective-permute-start.7
  28.8 0.7 collective-permute-done.5
  29.4 0.5 collective-permute-start.6
  30.0 1.3 constant_dynamic-slice_fusion.1
  31.2 0.0 copy-start.2
  31.2 2.8 %copy-done.2 = bf16[1024,3,1024]{2,0,1:T(8,128)(2,1)S(1)} copy-done((bf16[1024,3,1024]{2,0,1:T(8,128)(2,1)S(1)}, bf16[1024,3,1024]{2,0,1:T(8,128)(2,1)}, u32[]{:S(2)}) %copy-start.2) | copy-done | bytes 6291480
  34.0 3.9 %shard_map.83.local_near_ref = f32[3,512,256]{2,1,0:T(8,128)S(1)} custom-call(s32[15]{0:T(128)S(1)} %stack.63.index_ref, bf16[256,4096]{1,0:T(8,128)(2,1)} %refs_0_.5, bf16[256,4096]{1,0:T(8,128)(2,1)} %collective-permute-done.refs_1_, bf16[3,1024,1024]{2,1,0:T(8,128)(2,1)S(1)} %bitcast.27, bf16[3,1024,1024]{2,1,0:T(8,128)(2,1)S(1)} %bitcast.28, ...), custom_call_target="tpu_custom_call" | custom-call | flops 1 | bytes 1 | tf_op jit(solution)/shard_map/pallas_call | solution.py:148
  37.9 0.6 collective-permute-done.6.rate_far_ref
  38.5 0.1 collective-permute-start.8
  38.6 2.1 %collective-permute-done.8.refs_3_.refs_5_ = bf16[256,1024]{1,0:T(8,128)(2,1)S(1)} collective-permute-done((bf16[256,1024]{1,0:T(8,128)(2,1)}, bf16[256,1024]{1,0:T(8,128)(2,1)S(1)}, u32[]{:S(2)}, u32[]{:S(2)}) %collective-permute-start.8) | collective-permute-done | bytes 524320 | tf_op jit(solution)/shard_map/ppermute | solution.py:428
  40.7 3.0 %shard_map.84 = bf16[2,512,256]{2,1,0:T(8,128)(2,1)S(1)} custom-call(s32[15]{0:T(128)S(1)} %stack.63.index_ref, bf16[256,1024]{1,0:T(8,128)(2,1)} %collective-permute-done.2.refs_0_.refs_2_, bf16[256,1024]{1,0:T(8,128)(2,1)} %collective-permute-done.3.refs_1_.refs_3_, bf16[256,1024]{1,0:T(8,128)(2,1)S(1)} %collective-permute-done.7.refs_2_.refs_4_, ...), custom_call_target="tpu_custom_call" | custom-call | flops 1 | bytes 1 | tf_op jit(solution)/shard_map/pallas_call | solution.py:148
  43.7 0.2 collective-permute-start.9
  43.9 1.5 %collective-permute-start.10 = (bf16[2,512,256]{2,1,0:T(8,128)(2,1)S(1)}, bf16[2,512,256]{2,1,0:T(8,128)(2,1)S(1)}, u32[]{:S(2)}, u32[]{:S(2)}) collective-permute-start(bf16[2,512,256]{2,1,0:T(8,128)(2,1)S(1)} %shard_map.84), channel_id=1, source_target_pairs={{0,8},{4,12},{8,0},{12,4},{1,9},{5,13},{9,1},{13,5},{2,10},{6,14},... | collective-permute-start | bytes 1572872 | tf_op jit(solution)/shard_map/ppermute | solution.py:428
  45.4 3.8 %shard_map.85 = bf16[1,1024,256]{2,1,0:T(8,128)(2,1)S(1)} custom-call(s32[15]{0:T(128)S(1)} %stack.63.index_ref, bf16[256,4096]{1,0:T(8,128)(2,1)} %refs_0_.5, bf16[256,4096]{1,0:T(8,128)(2,1)} %collective-permute-done.refs_1_, bf16[256,1024]{1,0:T(8,128)(2,1)} %collective-permute-done.2.refs_0_.refs_2_, ...), custom_call_target="tpu_custom_call" | custom-call | flops 1 | bytes 1 | tf_op jit(solution)/shard_map/pallas_call | solution.py:148
  49.2 0.0 copy-start.4
  49.2 0.0 copy-start.5
  49.2 0.0 copy-start.6
  49.3 4.0 %shard_map.86.local_far_ref = f32[3,512,256]{2,1,0:T(8,128)S(1)} custom-call(s32[15]{0:T(128)S(1)} %stack.63.index_ref, bf16[256,1024]{1,0:T(8,128)(2,1)} %collective-permute-done.2.refs_0_.refs_2_, bf16[256,1024]{1,0:T(8,128)(2,1)} %collective-permute-done.3.refs_1_.refs_3_, bf16[256,1024]{1,0:T(8,128)(2,1)S(1)} %collective-permute-done.7.refs_2_.refs_4_, ...), custom_call_target="tpu_custom_call" | custom-call | flops 1 | bytes 1 | tf_op jit(solution)/shard_map/pallas_call | solution.py:148
  53.3 0.0 copy-start.7
  53.3 4.9 %collective-permute-done.10.near_ref = bf16[2,512,256]{2,1,0:T(8,128)(2,1)S(1)} collective-permute-done((bf16[2,512,256]{2,1,0:T(8,128)(2,1)S(1)}, bf16[2,512,256]{2,1,0:T(8,128)(2,1)S(1)}, u32[]{:S(2)}, u32[]{:S(2)}) %collective-permute-start.10) | collective-permute-done | bytes 524320 | tf_op jit(solution)/shard_map/ppermute | solution.py:428
  58.1 1.5 %collective-permute-start.11 = (bf16[1,1024,256]{2,1,0:T(8,128)(2,1)S(1)}, bf16[1,1024,256]{2,1,0:T(8,128)(2,1)S(1)}, u32[]{:S(2)}, u32[]{:S(2)}) collective-permute-start(bf16[1,1024,256]{2,1,0:T(8,128)(2,1)S(1)} %shard_map.85), channel_id=1, source_target_pairs={{0,8},{4,12},{8,0},{12,4},{1,9},{5,13},{9,1},{13,5},{2,10},{6,14},... | collective-permute-start | bytes 1572872 | tf_op jit(solution)/shard_map/ppermute | solution.py:428
  59.6 13.3 %shard_map.87 = (bf16[256,512]{1,0:T(8,128)(2,1)S(1)}, bf16[256,512]{1,0:T(8,128)(2,1)S(1)}, bf16[256,512]{1,0:T(8,128)(2,1)S(1)}) custom-call(s32[15]{0:T(128)S(1)} %stack.63.index_ref, f32[3,512,256]{2,1,0:T(8,128)S(1)} %shard_map.83.local_near_ref, f32[3,512,256]{2,1,0:T(8,128)S(1)} %shard_map.86.local_far_ref, ...), custom_call_target="tpu_custom_call" | custom-call | flops 1 | bytes 1 | tf_op jit(solution)/shard_map/pallas_call | solution.py:241
  72.9 2.0 %shard_map.88 = (bf16[256,256]{1,0:T(8,128)(2,1)S(1)}, bf16[256,256]{1,0:T(8,128)(2,1)S(1)}, bf16[256,256]{1,0:T(8,128)(2,1)S(1)}, bf16[256,256]{1,0:T(8,128)(2,1)S(1)}) custom-call(s32[15]{0:T(128)S(1)} %stack.63.index_ref, f32[3,512,256]{2,1,0:T(8,128)S(1)} %shard_map.83.local_near_ref, f32[3,512,256]{2,1,0:T(8,128)S(1)} %shard_map.86.local_far_ref, ...), custom_call_target="tpu_custom_call" | custom-call | flops 1 | bytes 1 | tf_op jit(solution)/shard_map/pallas_call | solution.py:287
  74.9 0.1 collective-permute-start.12
  75.0 0.6 collective-permute-start.14
  75.6 1.3 collective-permute-start.15
  76.9 1.3 collective-permute-start.19
  78.2 4.6 %collective-permute-start.13 = (bf16[256,512]{1,0:T(8,128)(2,1)S(1)}, bf16[256,512]{1,0:T(8,128)(2,1)S(1)}, u32[]{:S(2)}, u32[]{:S(2)}) collective-permute-start(bf16[256,512]{1,0:T(8,128)(2,1)S(1)} %constant_dynamic-update-slice_fusion), channel_id=1, source_target_pairs={{0,1},{1,2},{2,3},{4,5},{5,6},{6,7},{8,9},{9,10},{10,11},{12,13},{... | collective-permute-start | bytes 786440 | tf_op jit(solution)/shard_map/ppermute | solution.py:431
  82.8 0.5 collective-permute-done.15
  83.3 1.3 collective-permute-start.20
  84.6 0.6 collective-permute-start.23
  85.2 4.5 %collective-permute-start.16 = (bf16[256,512]{1,0:T(8,128)(2,1)S(1)}, bf16[256,512]{1,0:T(8,128)(2,1)S(1)}, u32[]{:S(2)}, u32[]{:S(2)}) collective-permute-start(bf16[256,512]{1,0:T(8,128)(2,1)S(1)} %constant_dynamic-update-slice_fusion.2), channel_id=1, source_target_pairs={{0,1},{1,2},{2,3},{4,5},{5,6},{6,7},{8,9},{9,10},{10,11},{12,13},{... | collective-permute-start | bytes 786440 | tf_op jit(solution)/shard_map/ppermute | solution.py:431
  89.8 4.2 %collective-permute-done.20 = bf16[256,512]{1,0:T(8,128)(2,1)S(1)} collective-permute-done((bf16[256,512]{1,0:T(8,128)(2,1)S(1)}, bf16[256,512]{1,0:T(8,128)(2,1)S(1)}, u32[]{:S(2)}, u32[]{:S(2)}) %collective-permute-start.20) | collective-permute-done | bytes 262176 | tf_op jit(solution)/shard_map/ppermute | solution.py:431
  94.0 1.3 collective-permute-start.21
  95.3 0.1 collective-permute-done.16
  95.5 0.7 collective-permute-start.17
  96.2 1.6 %collective-permute-start.27 = (bf16[256,1024]{1,0:T(8,128)(2,1)S(1)}, bf16[256,1024]{1,0:T(8,128)(2,1)S(1)}, u32[]{:S(2)}, u32[]{:S(2)}) collective-permute-start(bf16[256,1024]{1,0:T(8,128)(2,1)S(1)} %get-tuple-element.57), channel_id=1, source_target_pairs={{0,8},{4,12},{8,0},{12,4},{1,9},{5,13},{9,1},{13,5},{2,10},{6,14},... | collective-permute-start | bytes 1572872 | tf_op jit(solution)/shard_map/ppermute | solution.py:428
  97.7 1.6 %collective-permute-done.23.one = bf16[256,1024]{1,0:T(8,128)(2,1)S(1)} collective-permute-done((bf16[256,1024]{1,0:T(8,128)(2,1)S(1)}, bf16[256,1024]{1,0:T(8,128)(2,1)S(1)}, u32[]{:S(2)}, u32[]{:S(2)}) %collective-permute-start.23) | collective-permute-done | bytes 524320 | tf_op jit(solution)/shard_map/ppermute | solution.py:428
  99.4 1.5 %collective-permute-start.24 = (bf16[256,1024]{1,0:T(8,128)(2,1)S(1)}, bf16[256,1024]{1,0:T(8,128)(2,1)S(1)}, u32[]{:S(2)}, u32[]{:S(2)}) collective-permute-start(bf16[256,1024]{1,0:T(8,128)(2,1)S(1)} %collective-permute-done.23.one), channel_id=1, source_target_pairs={{0,16},{16,0},{1,17},{17,1},{2,18},{18,2},{3,19},{19,3},{4,20},{20... | collective-permute-start | bytes 1572872 | tf_op jit(solution)/shard_map/ppermute | solution.py:485
  100.9 8.6 %collective-permute-done.21.above_2 = bf16[256,1024]{1,0:T(8,128)(2,1)S(1)} collective-permute-done((bf16[256,1024]{1,0:T(8,128)(2,1)S(1)}, bf16[256,1024]{1,0:T(8,128)(2,1)S(1)}, u32[]{:S(2)}, u32[]{:S(2)}) %collective-permute-start.21) | collective-permute-done | bytes 524320 | tf_op jit(solution)/shard_map/ppermute | solution.py:431
  109.5 0.8 collective-permute-done.27.one
  110.3 2.4 %collective-permute-done.24.other = bf16[256,1024]{1,0:T(8,128)(2,1)S(1)} collective-permute-done((bf16[256,1024]{1,0:T(8,128)(2,1)S(1)}, bf16[256,1024]{1,0:T(8,128)(2,1)S(1)}, u32[]{:S(2)}, u32[]{:S(2)}) %collective-permute-start.24) | collective-permute-done | bytes 524320 | tf_op jit(solution)/shard_map/ppermute | solution.py:485
  112.7 1.5 %collective-permute-start.28 = (bf16[256,1024]{1,0:T(8,128)(2,1)S(1)}, bf16[256,1024]{1,0:T(8,128)(2,1)S(1)}, u32[]{:S(2)}, u32[]{:S(2)}) collective-permute-start(bf16[256,1024]{1,0:T(8,128)(2,1)S(1)} %collective-permute-done.27.one), channel_id=1, source_target_pairs={{0,16},{16,0},{1,17},{17,1},{2,18},{18,2},{3,19},{19,3},{4,20},{20... | collective-permute-start | bytes 1572872 | tf_op jit(solution)/shard_map/ppermute | solution.py:485
  114.2 0.1 pad_maximum_fusion.own
  114.3 1.3 collective-permute-start.22
  115.6 0.7 collective-permute-start.18
  116.3 4.7 %shard_map.89 = (f32[256,1024]{1,0:T(8,128)S(1)}, bf16[256,1024]{1,0:T(8,128)(2,1)S(1)}, bf16[1024,1024]{1,0:T(8,128)(2,1)S(1)}) custom-call(s32[15]{0:T(128)S(1)} %stack.63.index_ref, bf16[256,1024]{1,0:T(8,128)(2,1)S(1)} %pad_maximum_fusion.own, bf16[256,1024]{1,0:T(8,128)(2,1)S(1)} %constant_dynamic-update-slice_fusion.4.below_1, ...), custom_call_target="tpu_custom_call" | custom-call | flops 1 | bytes 1 | tf_op jit(solution)/shard_map/pallas_call | solution.py:354
  121.0 6.0 %collective-permute-done.28.other = bf16[256,1024]{1,0:T(8,128)(2,1)S(1)} collective-permute-done((bf16[256,1024]{1,0:T(8,128)(2,1)S(1)}, bf16[256,1024]{1,0:T(8,128)(2,1)S(1)}, u32[]{:S(2)}, u32[]{:S(2)}) %collective-permute-start.28) | collective-permute-done | bytes 524320 | tf_op jit(solution)/shard_map/ppermute | solution.py:485
  127.0 0.5 collective-permute-start.30
  127.5 3.3 %collective-permute-done.22.above = bf16[256,1024]{1,0:T(8,128)(2,1)S(1)} collective-permute-done((bf16[256,1024]{1,0:T(8,128)(2,1)S(1)}, bf16[256,1024]{1,0:T(8,128)(2,1)S(1)}, u32[]{:S(2)}, u32[]{:S(2)}) %collective-permute-start.22) | collective-permute-done | bytes 524320 | tf_op jit(solution)/shard_map/ppermute | solution.py:431
  130.8 2.6 %shard_map.90 = bf16[256,1024]{1,0:T(8,128)(2,1)} custom-call(s32[15]{0:T(128)S(1)} %stack.63.index_ref, bf16[256,1024]{1,0:T(8,128)(2,1)S(1)} %collective-permute-done.18.below, bf16[256,1024]{1,0:T(8,128)(2,1)S(1)} %collective-permute-done.22.above, bf16[1024,1024]{1,0:T(8,128)(2,1)S(1)} %get-tuple-element.55.weight, ...), custom_call_target="tpu_custom_call" | custom-call | flops 1 | bytes 1 | tf_op jit(solution)/shard_map/pallas_call | solution.py:398
  (38 shorter events, 0.2 us)
Async XLA Ops:
  0.0 25.9 %copy-start = (bf16[4096,4]{0,1:T(4,128)(2,1)S(1)}, bf16[4096,4]{0,1:T(4,128)(2,1)}, u32[]{:S(2)}) copy-start(bf16[4096,4]{0,1:T(4,128)(2,1)} %param.10) | copy-start | bytes 98308
  5.6 9.0 %collective-permute-start.1 = (bf16[3,1024,512]{2,1,0:T(8,128)(2,1)}, bf16[3,1024,512]{2,1,0:T(8,128)(2,1)S(1)}, u32[]{:S(2)}, u32[]{:S(2)}) collective-permute-start(bf16[3,1024,512]{2,1,0:T(8,128)(2,1)} %dynamic-slice_bitcast_fusion), channel_id=1, source_target_pairs={{0,4},{4,0},{8,12},{12,8},{1,5},{5,1},{9,13},{13,9},{2,6},{6,2},{1... | collective-permute-start | bytes 9437192 | tf_op jit(solution)/shard_map/ppermute | solution.py:428
  6.1 8.5 %collective-permute-start = (bf16[256,4096]{1,0:T(8,128)(2,1)}, bf16[256,4096]{1,0:T(8,128)(2,1)}, u32[]{:S(2)}, u32[]{:S(2)}) collective-permute-start(bf16[256,4096]{1,0:T(8,128)(2,1)} %refs_0_.5), channel_id=1, source_target_pairs={{0,4},{4,0},{8,12},{12,8},{1,5},{5,1},{9,13},{13,9},{2,6},{6,2},{1... | collective-permute-start | bytes 6291464 | tf_op jit(solution)/shard_map/ppermute | solution.py:428
  6.1 15.4 %collective-permute-start.2 = (bf16[256,1024]{1,0:T(8,128)(2,1)}, bf16[256,1024]{1,0:T(8,128)(2,1)}, u32[]{:S(2)}, u32[]{:S(2)}) collective-permute-start(bf16[256,1024]{1,0:T(8,128)(2,1)} %constant_dynamic-slice_fusion.2), channel_id=1, source_target_pairs={{0,8},{4,12},{8,0},{12,4},{1,9},{5,13},{9,1},{13,5},{2,10},{6,14},... | collective-permute-start | bytes 1572872 | tf_op jit(solution)/shard_map/ppermute | solution.py:428
  14.6 2.8 %copy-start.1 = (bf16[1024,3,1024]{2,0,1:T(8,128)(2,1)S(1)}, bf16[1024,3,1024]{2,0,1:T(8,128)(2,1)}, u32[]{:S(2)}) copy-start(bf16[1024,3,1024]{2,0,1:T(8,128)(2,1)} %param.9) | copy-start | bytes 18874372
  21.5 17.0 %collective-permute-start.3 = (bf16[256,1024]{1,0:T(8,128)(2,1)}, bf16[256,1024]{1,0:T(8,128)(2,1)}, u32[]{:S(2)}, u32[]{:S(2)}) collective-permute-start(bf16[256,1024]{1,0:T(8,128)(2,1)} %collective-permute-done.2.refs_0_.refs_2_), channel_id=1, source_target_pairs={{0,1},{1,0},{2,3},{3,2},{4,5},{5,4},{6,7},{7,6},{8,9},{9,8},{10,11... | collective-permute-start | bytes 1572872 | tf_op jit(solution)/shard_map/ppermute | solution.py:431
  24.4 14.1 %collective-permute-start.4 = (bf16[2,512,256]{2,1,0:T(8,128)(2,1)}, bf16[2,512,256]{2,1,0:T(8,128)(2,1)}, u32[]{:S(2)}, u32[]{:S(2)}) collective-permute-start(bf16[2,512,256]{2,1,0:T(8,128)(2,1)} %shard_map.82), channel_id=1, source_target_pairs={{0,8},{4,12},{8,0},{12,4},{1,9},{5,13},{9,1},{13,5},{2,10},{6,14},... | collective-permute-start | bytes 1572872 | tf_op jit(solution)/shard_map/ppermute | solution.py:428
  28.2 1.2 collective-permute-start.5
  28.3 10.3 %collective-permute-start.7 = (bf16[256,1024]{1,0:T(8,128)(2,1)}, bf16[256,1024]{1,0:T(8,128)(2,1)S(1)}, u32[]{:S(2)}, u32[]{:S(2)}) collective-permute-start(bf16[256,1024]{1,0:T(8,128)(2,1)} %collective-permute-done.2.refs_0_.refs_2_), channel_id=1, source_target_pairs={{0,4},{4,0},{8,12},{12,8},{1,5},{5,1},{9,13},{13,9},{2,6},{6,2},{1... | collective-permute-start | bytes 1572872 | tf_op jit(solution)/shard_map/ppermute | solution.py:428
  29.4 9.1 %collective-permute-start.6 = (f32[8,256]{1,0:T(8,128)S(1)}, f32[8,256]{1,0:T(8,128)S(1)}, u32[]{:S(2)}, u32[]{:S(2)}) collective-permute-start(f32[8,256]{1,0:T(8,128)S(1)} %pad_maximum_fusion.1.rate_near_ref), channel_id=1, source_target_pairs={{0,8},{4,12},{8,0},{12,4},{1,9},{5,13},{9,1},{13,5},{2,10},{6,14},... | collective-permute-start | bytes 24584 | tf_op jit(solution)/shard_map/ppermute | solution.py:428
  31.2 2.8 %copy-start.2 = (bf16[1024,3,1024]{2,0,1:T(8,128)(2,1)S(1)}, bf16[1024,3,1024]{2,0,1:T(8,128)(2,1)}, u32[]{:S(2)}) copy-start(bf16[1024,3,1024]{2,0,1:T(8,128)(2,1)} %param.9) | copy-start | bytes 18874372
  38.5 5.2 %copy-start.3 = (bf16[1024,1024]{1,0:T(8,128)(2,1)S(1)}, bf16[1024,1024]{1,0:T(8,128)(2,1)}, u32[]{:S(2)}) copy-start(bf16[1024,1024]{1,0:T(8,128)(2,1)} %own_w.1) | copy-start | bytes 6291460
  38.5 2.2 %collective-permute-start.8 = (bf16[256,1024]{1,0:T(8,128)(2,1)}, bf16[256,1024]{1,0:T(8,128)(2,1)S(1)}, u32[]{:S(2)}, u32[]{:S(2)}) collective-permute-start(bf16[256,1024]{1,0:T(8,128)(2,1)} %collective-permute-done.3.refs_1_.refs_3_), channel_id=1, source_target_pairs={{0,4},{4,0},{8,12},{12,8},{1,5},{5,1},{9,13},{13,9},{2,6},{6,2},{1... | collective-permute-start | bytes 1572872 | tf_op jit(solution)/shard_map/ppermute | solution.py:428
  43.7 5.5 %collective-permute-start.9 = (bf16[1024,1024]{1,0:T(8,128)(2,1)S(1)}, bf16[1024,1024]{1,0:T(8,128)(2,1)S(1)}, u32[]{:S(2)}, u32[]{:S(2)}) collective-permute-start(bf16[1024,1024]{1,0:T(8,128)(2,1)S(1)} %copy-done.3), channel_id=1, source_target_pairs={{0,4},{4,0},{8,12},{12,8},{1,5},{5,1},{9,13},{13,9},{2,6},{6,2},{1... | collective-permute-start | bytes 6291464 | tf_op jit(solution)/shard_map/ppermute | solution.py:428
  43.9 14.2 %collective-permute-start.10 = (bf16[2,512,256]{2,1,0:T(8,128)(2,1)S(1)}, bf16[2,512,256]{2,1,0:T(8,128)(2,1)S(1)}, u32[]{:S(2)}, u32[]{:S(2)}) collective-permute-start(bf16[2,512,256]{2,1,0:T(8,128)(2,1)S(1)} %shard_map.84), channel_id=1, source_target_pairs={{0,8},{4,12},{8,0},{12,4},{1,9},{5,13},{9,1},{13,5},{2,10},{6,14},... | collective-permute-start | bytes 1572872 | tf_op jit(solution)/shard_map/ppermute | solution.py:428
  49.2 10.4 %copy-start.4 = (bf16[4,256,512]{2,1,0:T(8,128)(2,1)S(1)}, bf16[4,256,512]{2,1,0:T(8,128)(2,1)}, u32[]{:S(2)}) copy-start(bf16[4,256,512]{2,1,0:T(8,128)(2,1)} %gate_ref.1) | copy-start | bytes 3145732
  49.2 10.4 %copy-start.5 = (bf16[4,256,512]{2,1,0:T(8,128)(2,1)S(1)}, bf16[4,256,512]{2,1,0:T(8,128)(2,1)}, u32[]{:S(2)}) copy-start(bf16[4,256,512]{2,1,0:T(8,128)(2,1)} %up_ref.1) | copy-start | bytes 3145732
  49.2 10.4 %copy-start.6 = (bf16[4,256,512]{2,1,0:T(8,128)(2,1)S(1)}, bf16[4,256,512]{2,1,0:T(8,128)(2,1)}, u32[]{:S(2)}) copy-start(bf16[4,256,512]{2,1,0:T(8,128)(2,1)} %down_ref.1) | copy-start | bytes 3145732
  53.3 19.7 %copy-start.7 = (f32[1024]{0:T(1024)S(1)}, f32[1024]{0:T(1024)}, u32[]{:S(2)}) copy-start(f32[1024]{0:T(1024)} %param.14) | copy-start | bytes 12292
  58.1 14.8 %collective-permute-start.11 = (bf16[1,1024,256]{2,1,0:T(8,128)(2,1)S(1)}, bf16[1,1024,256]{2,1,0:T(8,128)(2,1)S(1)}, u32[]{:S(2)}, u32[]{:S(2)}) collective-permute-start(bf16[1,1024,256]{2,1,0:T(8,128)(2,1)S(1)} %shard_map.85), channel_id=1, source_target_pairs={{0,8},{4,12},{8,0},{12,4},{1,9},{5,13},{9,1},{13,5},{2,10},{6,14},... | collective-permute-start | bytes 1572872 | tf_op jit(solution)/shard_map/ppermute | solution.py:428
  74.9 2.0 %collective-permute-start.12 = (bf16[256,256]{1,0:T(8,128)(2,1)S(1)}, bf16[256,256]{1,0:T(8,128)(2,1)S(1)}, u32[]{:S(2)}, u32[]{:S(2)}) collective-permute-start(bf16[256,256]{1,0:T(8,128)(2,1)S(1)} %get-tuple-element.48), channel_id=1, source_target_pairs={{0,4},{4,0},{8,12},{12,8},{1,5},{5,1},{9,13},{13,9},{2,6},{6,2},{1... | collective-permute-start | bytes 393224 | tf_op jit(solution)/shard_map/ppermute | solution.py:428
  75.0 7.8 %collective-permute-start.14 = (bf16[256,256]{1,0:T(8,128)(2,1)S(1)}, bf16[256,256]{1,0:T(8,128)(2,1)S(1)}, u32[]{:S(2)}, u32[]{:S(2)}) collective-permute-start(bf16[256,256]{1,0:T(8,128)(2,1)S(1)} %get-tuple-element.49), channel_id=1, source_target_pairs={{0,8},{4,12},{8,0},{12,4},{1,9},{5,13},{9,1},{13,5},{2,10},{6,14},... | collective-permute-start | bytes 393224 | tf_op jit(solution)/shard_map/ppermute | solution.py:428
  75.6 7.7 %collective-permute-start.15 = (bf16[256,256]{1,0:T(8,128)(2,1)S(1)}, bf16[256,256]{1,0:T(8,128)(2,1)S(1)}, u32[]{:S(2)}, u32[]{:S(2)}) collective-permute-start(bf16[256,256]{1,0:T(8,128)(2,1)S(1)} %get-tuple-element.50), channel_id=1, source_target_pairs={{0,12},{4,8},{8,4},{12,0},{1,13},{5,9},{9,5},{13,1},{2,14},{6,10},... | collective-permute-start | bytes 393224 | tf_op jit(solution)/shard_map/ppermute | solution.py:428
  76.9 12.8 %collective-permute-start.19 = (bf16[256,512]{1,0:T(8,128)(2,1)S(1)}, bf16[256,512]{1,0:T(8,128)(2,1)S(1)}, u32[]{:S(2)}, u32[]{:S(2)}) collective-permute-start(bf16[256,512]{1,0:T(8,128)(2,1)S(1)} %constant_dynamic-update-slice_fusion), channel_id=1, source_target_pairs={{1,0},{2,1},{3,2},{5,4},{6,5},{7,6},{9,8},{10,9},{11,10},{13,12},{... | collective-permute-start | bytes 786440 | tf_op jit(solution)/shard_map/ppermute | solution.py:431
  78.2 11.6 %collective-permute-start.13 = (bf16[256,512]{1,0:T(8,128)(2,1)S(1)}, bf16[256,512]{1,0:T(8,128)(2,1)S(1)}, u32[]{:S(2)}, u32[]{:S(2)}) collective-permute-start(bf16[256,512]{1,0:T(8,128)(2,1)S(1)} %constant_dynamic-update-slice_fusion), channel_id=1, source_target_pairs={{0,1},{1,2},{2,3},{4,5},{5,6},{6,7},{8,9},{9,10},{10,11},{12,13},{... | collective-permute-start | bytes 786440 | tf_op jit(solution)/shard_map/ppermute | solution.py:431
  83.3 10.7 %collective-permute-start.20 = (bf16[256,512]{1,0:T(8,128)(2,1)S(1)}, bf16[256,512]{1,0:T(8,128)(2,1)S(1)}, u32[]{:S(2)}, u32[]{:S(2)}) collective-permute-start(bf16[256,512]{1,0:T(8,128)(2,1)S(1)} %constant_dynamic-update-slice_fusion.2), channel_id=1, source_target_pairs={{1,0},{2,1},{3,2},{5,4},{6,5},{7,6},{9,8},{10,9},{11,10},{13,12},{... | collective-permute-start | bytes 786440 | tf_op jit(solution)/shard_map/ppermute | solution.py:431
  84.6 14.8 %collective-permute-start.23 = (bf16[256,1024]{1,0:T(8,128)(2,1)S(1)}, bf16[256,1024]{1,0:T(8,128)(2,1)S(1)}, u32[]{:S(2)}, u32[]{:S(2)}) collective-permute-start(bf16[256,1024]{1,0:T(8,128)(2,1)S(1)} %get-tuple-element.51), channel_id=1, source_target_pairs={{0,8},{4,12},{8,0},{12,4},{1,9},{5,13},{9,1},{13,5},{2,10},{6,14},... | collective-permute-start | bytes 1572872 | tf_op jit(solution)/shard_map/ppermute | solution.py:428
  85.2 10.3 %collective-permute-start.16 = (bf16[256,512]{1,0:T(8,128)(2,1)S(1)}, bf16[256,512]{1,0:T(8,128)(2,1)S(1)}, u32[]{:S(2)}, u32[]{:S(2)}) collective-permute-start(bf16[256,512]{1,0:T(8,128)(2,1)S(1)} %constant_dynamic-update-slice_fusion.2), channel_id=1, source_target_pairs={{0,1},{1,2},{2,3},{4,5},{5,6},{6,7},{8,9},{9,10},{10,11},{12,13},{... | collective-permute-start | bytes 786440 | tf_op jit(solution)/shard_map/ppermute | solution.py:431
  94.0 15.5 %collective-permute-start.21 = (bf16[256,1024]{1,0:T(8,128)(2,1)S(1)}, bf16[256,1024]{1,0:T(8,128)(2,1)S(1)}, u32[]{:S(2)}, u32[]{:S(2)}) collective-permute-start(bf16[256,1024]{1,0:T(8,128)(2,1)S(1)} %constant_dynamic-update-slice_fusion.6.above_1), channel_id=1, source_target_pairs={{1,0},{2,1},{5,4},{6,5},{9,8},{10,9},{13,12},{14,13},{17,16},{18,1... | collective-permute-start | bytes 1572872 | tf_op jit(solution)/shard_map/ppermute | solution.py:431
  95.5 14.0 %collective-permute-start.17 = (bf16[256,1024]{1,0:T(8,128)(2,1)S(1)}, bf16[256,1024]{1,0:T(8,128)(2,1)S(1)}, u32[]{:S(2)}, u32[]{:S(2)}) collective-permute-start(bf16[256,1024]{1,0:T(8,128)(2,1)S(1)} %constant_dynamic-update-slice_fusion.4.below_1), channel_id=1, source_target_pairs={{1,2},{2,3},{5,6},{6,7},{9,10},{10,11},{13,14},{14,15},{17,18},{18... | collective-permute-start | bytes 1572872 | tf_op jit(solution)/shard_map/ppermute | solution.py:431
  96.2 14.1 %collective-permute-start.27 = (bf16[256,1024]{1,0:T(8,128)(2,1)S(1)}, bf16[256,1024]{1,0:T(8,128)(2,1)S(1)}, u32[]{:S(2)}, u32[]{:S(2)}) collective-permute-start(bf16[256,1024]{1,0:T(8,128)(2,1)S(1)} %get-tuple-element.57), channel_id=1, source_target_pairs={{0,8},{4,12},{8,0},{12,4},{1,9},{5,13},{9,1},{13,5},{2,10},{6,14},... | collective-permute-start | bytes 1572872 | tf_op jit(solution)/shard_map/ppermute | solution.py:428
  99.4 13.3 %collective-permute-start.24 = (bf16[256,1024]{1,0:T(8,128)(2,1)S(1)}, bf16[256,1024]{1,0:T(8,128)(2,1)S(1)}, u32[]{:S(2)}, u32[]{:S(2)}) collective-permute-start(bf16[256,1024]{1,0:T(8,128)(2,1)S(1)} %collective-permute-done.23.one), channel_id=1, source_target_pairs={{0,16},{16,0},{1,17},{17,1},{2,18},{18,2},{3,19},{19,3},{4,20},{20... | collective-permute-start | bytes 1572872 | tf_op jit(solution)/shard_map/ppermute | solution.py:485
  110.3 6.0 %collective-permute-start.25 = (bf16[256,1024]{1,0:T(8,128)(2,1)S(1)}, bf16[256,1024]{1,0:T(8,128)(2,1)S(1)}, u32[]{:S(2)}, u32[]{:S(2)}) collective-permute-start(bf16[256,1024]{1,0:T(8,128)(2,1)S(1)} %collective-permute-done.23.one), channel_id=1, source_target_pairs={{0,4},{4,0},{8,12},{12,8},{1,5},{5,1},{9,13},{13,9},{2,6},{6,2},{1... | collective-permute-start | bytes 1572872 | tf_op jit(solution)/shard_map/ppermute | solution.py:428
  112.7 3.6 %collective-permute-start.26 = (bf16[256,1024]{1,0:T(8,128)(2,1)S(1)}, bf16[256,1024]{1,0:T(8,128)(2,1)S(1)}, u32[]{:S(2)}, u32[]{:S(2)}) collective-permute-start(bf16[256,1024]{1,0:T(8,128)(2,1)S(1)} %collective-permute-done.24.other), channel_id=1, source_target_pairs={{0,4},{4,0},{8,12},{12,8},{1,5},{5,1},{9,13},{13,9},{2,6},{6,2},{1... | collective-permute-start | bytes 1572872 | tf_op jit(solution)/shard_map/ppermute | solution.py:428
  112.7 14.3 %collective-permute-start.28 = (bf16[256,1024]{1,0:T(8,128)(2,1)S(1)}, bf16[256,1024]{1,0:T(8,128)(2,1)S(1)}, u32[]{:S(2)}, u32[]{:S(2)}) collective-permute-start(bf16[256,1024]{1,0:T(8,128)(2,1)S(1)} %collective-permute-done.27.one), channel_id=1, source_target_pairs={{0,16},{16,0},{1,17},{17,1},{2,18},{18,2},{3,19},{19,3},{4,20},{20... | collective-permute-start | bytes 1572872 | tf_op jit(solution)/shard_map/ppermute | solution.py:485
  114.3 16.5 %collective-permute-start.22 = (bf16[256,1024]{1,0:T(8,128)(2,1)S(1)}, bf16[256,1024]{1,0:T(8,128)(2,1)S(1)}, u32[]{:S(2)}, u32[]{:S(2)}) collective-permute-start(bf16[256,1024]{1,0:T(8,128)(2,1)S(1)} %collective-permute-done.21.above_2), channel_id=1, source_target_pairs={{1,0},{5,4},{9,8},{13,12},{17,16},{21,20},{25,24},{29,28}} | collective-permute-start | bytes 1572872 | tf_op jit(solution)/shard_map/ppermute | solution.py:431
  115.6 15.3 %collective-permute-start.18 = (bf16[256,1024]{1,0:T(8,128)(2,1)S(1)}, bf16[256,1024]{1,0:T(8,128)(2,1)S(1)}, u32[]{:S(2)}, u32[]{:S(2)}) collective-permute-start(bf16[256,1024]{1,0:T(8,128)(2,1)S(1)} %collective-permute-done.17.below_2), channel_id=1, source_target_pairs={{2,3},{6,7},{10,11},{14,15},{18,19},{22,23},{26,27},{30,31}} | collective-permute-start | bytes 1572872 | tf_op jit(solution)/shard_map/ppermute | solution.py:431
  127.0 3.8 %collective-permute-start.29 = (bf16[256,1024]{1,0:T(8,128)(2,1)S(1)}, bf16[256,1024]{1,0:T(8,128)(2,1)S(1)}, u32[]{:S(2)}, u32[]{:S(2)}) collective-permute-start(bf16[256,1024]{1,0:T(8,128)(2,1)S(1)} %collective-permute-done.27.one), channel_id=1, source_target_pairs={{0,4},{4,0},{8,12},{12,8},{1,5},{5,1},{9,13},{13,9},{2,6},{6,2},{1... | collective-permute-start | bytes 1572872 | tf_op jit(solution)/shard_map/ppermute | solution.py:428
  127.0 3.8 %collective-permute-start.30 = (bf16[256,1024]{1,0:T(8,128)(2,1)S(1)}, bf16[256,1024]{1,0:T(8,128)(2,1)S(1)}, u32[]{:S(2)}, u32[]{:S(2)}) collective-permute-start(bf16[256,1024]{1,0:T(8,128)(2,1)S(1)} %collective-permute-done.28.other), channel_id=1, source_target_pairs={{0,4},{4,0},{8,12},{12,8},{1,5},{5,1},{9,13},{13,9},{2,6},{6,2},{1... | collective-permute-start | bytes 1572872 | tf_op jit(solution)/shard_map/ppermute | solution.py:428

commit v17 on v16

--- a/solution.py
+++ b/solution.py
@@ -208,7 +208,7 @@
         norm = jnp.sqrt(jnp.sum(value * value))
         current[i] = value / (norm + 1e-07)
 
-    @pl.loop(0, NSI)
+    @pl.loop(0, NSI, unroll=True)
     def _(step):
         values = [current[i] for i in range(3)]
         halves = [split(value) for value in values]

time: 134 us -> 133 us (level)
  no operation moved by 1% of the time
where the time goes in v17:
time: 133 us
  waiting for transfers between devices  41.2 us (31%)
  Pallas kernels  40.5 us (30%)
  starting transfers between devices  35.7 us (27%)
  local copies, waits for them, and re-layouts  12.7 us (10%)
  matrix products  2.25 us (2%)
    ppermute x9, starting transfers between devices, hop(): return lax.ppermute(array, 'head', links)  18.8 us
    pallas_call x5, Pallas kernels, project(): pl.pallas_call(functools.partial(project_kernel, len(whole), len(pairs),...  18.7 us
    ppermute x20, waiting for transfers between devices, across(): return lax.ppermute(array, 'seq', [(i, i ^ bit) for i in range(4)])  16.6 us
    ppermute x9, waiting for transfers between devices, hop(): return lax.ppermute(array, 'head', links)  16.2 us
    ppermute x20, starting transfers between devices, across(): return lax.ppermute(array, 'seq', [(i, i ^ bit) for i in range(4)])  13.9 us
    pallas_call x1, Pallas kernels, update(): pl.pallas_call(update_kernel, out_shape=[out] * 3, grid_spec=pltpu.Prefet...  12.4 us
    ppermute x2, waiting for transfers between devices, swap_groups(): return lax.ppermute(array, 'groups', [(0, 1), (1, 0)])  8.39 us
    unnamed x20, local copies, waits for them, and re-layouts  5.66 us
  transfers between devices with their start and end apart: 31, of which 14 were waited for; matrix products, arithmetic and copies ran while one was open for 3% of the time, Pallas kernels for 25%

profile of v17, /device:TPU:0, one launch (start us, length us, event | category | flops | bytes accessed | tf_op | source)
XLA Modules:
  0.0 132.8 jit_solution(7220154108048121019)
XLA Ops:
  0.0 1.9 %constant_dynamic-slice_fusion.2 = bf16[256,1024]{1,0:T(8,128)(2,1)} fusion(bf16[256,4096]{1,0:T(8,128)(2,1)} %refs_0_.5, s32[]{:T(128)S(6)} %select_n.23), kind=kLoop, calls=%fused_computation.15 | loop fusion | bytes 1048580 | tf_op jit(solution)/shard_map/dynamic_slice | solution.py:440
  1.9 3.7 %dynamic-slice_bitcast_fusion = bf16[3,1024,512]{2,1,0:T(8,128)(2,1)} fusion(bf16[1024,3,1024]{2,0,1:T(8,128)(2,1)} %param.9, s32[]{:T(128)S(6)} %select_n.24), kind=kLoop, calls=%fused_computation | loop fusion | bytes 6291460 | tf_op jit(solution)/shard_map/dynamic_slice | solution.py:444
  5.6 0.5 collective-permute-start.1
  6.1 0.1 collective-permute-start
  6.1 2.9 %collective-permute-start.2 = (bf16[256,1024]{1,0:T(8,128)(2,1)}, bf16[256,1024]{1,0:T(8,128)(2,1)}, u32[]{:S(2)}, u32[]{:S(2)}) collective-permute-start(bf16[256,1024]{1,0:T(8,128)(2,1)} %constant_dynamic-slice_fusion.2), channel_id=1, source_target_pairs={{0,8},{4,12},{8,0},{12,4},{1,9},{5,13},{9,1},{13,5},{2,10},{6,14},... | collective-permute-start | bytes 1572872 | tf_op jit(solution)/shard_map/ppermute | solution.py:428
  9.1 0.1 stack.63.index_ref
  9.2 5.5 %collective-permute-done.refs_1_ = bf16[256,4096]{1,0:T(8,128)(2,1)} collective-permute-done((bf16[256,4096]{1,0:T(8,128)(2,1)}, bf16[256,4096]{1,0:T(8,128)(2,1)}, u32[]{:S(2)}, u32[]{:S(2)}) %collective-permute-start) | collective-permute-done | bytes 2097184 | tf_op jit(solution)/shard_map/ppermute | solution.py:428
  14.6 2.8 %copy-done.1 = bf16[1024,3,1024]{2,0,1:T(8,128)(2,1)S(1)} copy-done((bf16[1024,3,1024]{2,0,1:T(8,128)(2,1)S(1)}, bf16[1024,3,1024]{2,0,1:T(8,128)(2,1)}, u32[]{:S(2)}) %copy-start.1) | copy-done | bytes 6291480
  17.4 4.1 %shard_map.82 = bf16[2,512,256]{2,1,0:T(8,128)(2,1)} custom-call(s32[15]{0:T(128)S(1)} %stack.63.index_ref, bf16[256,4096]{1,0:T(8,128)(2,1)} %refs_0_.5, bf16[256,4096]{1,0:T(8,128)(2,1)} %collective-permute-done.refs_1_, bf16[3,1024,1024]{2,1,0:T(8,128)(2,1)S(1)} %bitcast.25, bf16[3,1024,1024]{2,1,0:T(8,128)(2,1)S(1)} %bitcast.26, ...), custom_call_target="tpu_custom_call" | custom-call | flops 1 | bytes 1 | tf_op jit(solution)/shard_map/pallas_call | solution.py:148
  21.5 2.9 %collective-permute-start.3 = (bf16[256,1024]{1,0:T(8,128)(2,1)}, bf16[256,1024]{1,0:T(8,128)(2,1)}, u32[]{:S(2)}, u32[]{:S(2)}) collective-permute-start(bf16[256,1024]{1,0:T(8,128)(2,1)} %collective-permute-done.2.refs_0_.refs_2_), channel_id=1, source_target_pairs={{0,1},{1,0},{2,3},{3,2},{4,5},{5,4},{6,7},{7,6},{8,9},{9,8},{10,11... | collective-permute-start | bytes 1572872 | tf_op jit(solution)/shard_map/ppermute | solution.py:431
  24.4 1.5 %collective-permute-start.4 = (bf16[2,512,256]{2,1,0:T(8,128)(2,1)}, bf16[2,512,256]{2,1,0:T(8,128)(2,1)}, u32[]{:S(2)}, u32[]{:S(2)}) collective-permute-start(bf16[2,512,256]{2,1,0:T(8,128)(2,1)} %shard_map.82), channel_id=1, source_target_pairs={{0,8},{4,12},{8,0},{12,4},{1,9},{5,13},{9,1},{13,5},{2,10},{6,14},... | collective-permute-start | bytes 1572872 | tf_op jit(solution)/shard_map/ppermute | solution.py:428
  25.9 2.3 %compare_select_fusion = f32[4,256]{1,0:T(4,128)S(1)} fusion(bf16[256,4096]{1,0:T(8,128)(2,1)} %refs_0_.5, bf16[4096,4]{0,1:T(4,128)(2,1)S(1)} %copy-done), kind=kOutput, calls=%fused_computation.11 | convolution fusion | flops 8394752 | bytes 2134016 | tf_op jit(solution)/shard_map/dot_general | solution.py:456
  28.2 0.1 collective-permute-start.5
  28.3 0.5 collective-permute-start.7
  28.8 0.7 collective-permute-done.5
  29.4 0.5 collective-permute-start.6
  30.0 1.3 constant_dynamic-slice_fusion.1
  31.2 0.0 copy-start.2
  31.2 2.8 %copy-done.2 = bf16[1024,3,1024]{2,0,1:T(8,128)(2,1)S(1)} copy-done((bf16[1024,3,1024]{2,0,1:T(8,128)(2,1)S(1)}, bf16[1024,3,1024]{2,0,1:T(8,128)(2,1)}, u32[]{:S(2)}) %copy-start.2) | copy-done | bytes 6291480
  34.0 3.9 %shard_map.83.local_near_ref = f32[3,512,256]{2,1,0:T(8,128)S(1)} custom-call(s32[15]{0:T(128)S(1)} %stack.63.index_ref, bf16[256,4096]{1,0:T(8,128)(2,1)} %refs_0_.5, bf16[256,4096]{1,0:T(8,128)(2,1)} %collective-permute-done.refs_1_, bf16[3,1024,1024]{2,1,0:T(8,128)(2,1)S(1)} %bitcast.27, bf16[3,1024,1024]{2,1,0:T(8,128)(2,1)S(1)} %bitcast.28, ...), custom_call_target="tpu_custom_call" | custom-call | flops 1 | bytes 1 | tf_op jit(solution)/shard_map/pallas_call | solution.py:148
  37.9 0.6 collective-permute-done.6.rate_far_ref
  38.5 0.1 collective-permute-start.8
  38.6 2.1 %collective-permute-done.8.refs_3_.refs_5_ = bf16[256,1024]{1,0:T(8,128)(2,1)S(1)} collective-permute-done((bf16[256,1024]{1,0:T(8,128)(2,1)}, bf16[256,1024]{1,0:T(8,128)(2,1)S(1)}, u32[]{:S(2)}, u32[]{:S(2)}) %collective-permute-start.8) | collective-permute-done | bytes 524320 | tf_op jit(solution)/shard_map/ppermute | solution.py:428
  40.7 3.0 %shard_map.84 = bf16[2,512,256]{2,1,0:T(8,128)(2,1)S(1)} custom-call(s32[15]{0:T(128)S(1)} %stack.63.index_ref, bf16[256,1024]{1,0:T(8,128)(2,1)} %collective-permute-done.2.refs_0_.refs_2_, bf16[256,1024]{1,0:T(8,128)(2,1)} %collective-permute-done.3.refs_1_.refs_3_, bf16[256,1024]{1,0:T(8,128)(2,1)S(1)} %collective-permute-done.7.refs_2_.refs_4_, ...), custom_call_target="tpu_custom_call" | custom-call | flops 1 | bytes 1 | tf_op jit(solution)/shard_map/pallas_call | solution.py:148
  43.7 0.2 collective-permute-start.9
  43.9 1.5 %collective-permute-start.10 = (bf16[2,512,256]{2,1,0:T(8,128)(2,1)S(1)}, bf16[2,512,256]{2,1,0:T(8,128)(2,1)S(1)}, u32[]{:S(2)}, u32[]{:S(2)}) collective-permute-start(bf16[2,512,256]{2,1,0:T(8,128)(2,1)S(1)} %shard_map.84), channel_id=1, source_target_pairs={{0,8},{4,12},{8,0},{12,4},{1,9},{5,13},{9,1},{13,5},{2,10},{6,14},... | collective-permute-start | bytes 1572872 | tf_op jit(solution)/shard_map/ppermute | solution.py:428
  45.4 3.8 %shard_map.85 = bf16[1,1024,256]{2,1,0:T(8,128)(2,1)S(1)} custom-call(s32[15]{0:T(128)S(1)} %stack.63.index_ref, bf16[256,4096]{1,0:T(8,128)(2,1)} %refs_0_.5, bf16[256,4096]{1,0:T(8,128)(2,1)} %collective-permute-done.refs_1_, bf16[256,1024]{1,0:T(8,128)(2,1)} %collective-permute-done.2.refs_0_.refs_2_, ...), custom_call_target="tpu_custom_call" | custom-call | flops 1 | bytes 1 | tf_op jit(solution)/shard_map/pallas_call | solution.py:148
  49.2 0.0 copy-start.4
  49.2 0.0 copy-start.5
  49.2 0.0 copy-start.6
  49.3 4.0 %shard_map.86.local_far_ref = f32[3,512,256]{2,1,0:T(8,128)S(1)} custom-call(s32[15]{0:T(128)S(1)} %stack.63.index_ref, bf16[256,1024]{1,0:T(8,128)(2,1)} %collective-permute-done.2.refs_0_.refs_2_, bf16[256,1024]{1,0:T(8,128)(2,1)} %collective-permute-done.3.refs_1_.refs_3_, bf16[256,1024]{1,0:T(8,128)(2,1)S(1)} %collective-permute-done.7.refs_2_.refs_4_, ...), custom_call_target="tpu_custom_call" | custom-call | flops 1 | bytes 1 | tf_op jit(solution)/shard_map/pallas_call | solution.py:148
  53.3 0.0 copy-start.7
  53.3 4.9 %collective-permute-done.10.near_ref = bf16[2,512,256]{2,1,0:T(8,128)(2,1)S(1)} collective-permute-done((bf16[2,512,256]{2,1,0:T(8,128)(2,1)S(1)}, bf16[2,512,256]{2,1,0:T(8,128)(2,1)S(1)}, u32[]{:S(2)}, u32[]{:S(2)}) %collective-permute-start.10) | collective-permute-done | bytes 524320 | tf_op jit(solution)/shard_map/ppermute | solution.py:428
  58.1 1.5 %collective-permute-start.11 = (bf16[1,1024,256]{2,1,0:T(8,128)(2,1)S(1)}, bf16[1,1024,256]{2,1,0:T(8,128)(2,1)S(1)}, u32[]{:S(2)}, u32[]{:S(2)}) collective-permute-start(bf16[1,1024,256]{2,1,0:T(8,128)(2,1)S(1)} %shard_map.85), channel_id=1, source_target_pairs={{0,8},{4,12},{8,0},{12,4},{1,9},{5,13},{9,1},{13,5},{2,10},{6,14},... | collective-permute-start | bytes 1572872 | tf_op jit(solution)/shard_map/ppermute | solution.py:428
  59.6 12.4 %shard_map.87 = (bf16[256,512]{1,0:T(8,128)(2,1)S(1)}, bf16[256,512]{1,0:T(8,128)(2,1)S(1)}, bf16[256,512]{1,0:T(8,128)(2,1)S(1)}) custom-call(s32[15]{0:T(128)S(1)} %stack.63.index_ref, f32[3,512,256]{2,1,0:T(8,128)S(1)} %shard_map.83.local_near_ref, f32[3,512,256]{2,1,0:T(8,128)S(1)} %shard_map.86.local_far_ref, ...), custom_call_target="tpu_custom_call" | custom-call | flops 1 | bytes 1 | tf_op jit(solution)/shard_map/pallas_call | solution.py:241
  72.1 2.0 %shard_map.88 = (bf16[256,256]{1,0:T(8,128)(2,1)S(1)}, bf16[256,256]{1,0:T(8,128)(2,1)S(1)}, bf16[256,256]{1,0:T(8,128)(2,1)S(1)}, bf16[256,256]{1,0:T(8,128)(2,1)S(1)}) custom-call(s32[15]{0:T(128)S(1)} %stack.63.index_ref, f32[3,512,256]{2,1,0:T(8,128)S(1)} %shard_map.83.local_near_ref, f32[3,512,256]{2,1,0:T(8,128)S(1)} %shard_map.86.local_far_ref, ...), custom_call_target="tpu_custom_call" | custom-call | flops 1 | bytes 1 | tf_op jit(solution)/shard_map/pallas_call | solution.py:287
  74.1 0.1 collective-permute-start.12
  74.1 1.0 collective-permute-start.14
  75.2 0.8 collective-permute-start.15
  76.1 1.3 collective-permute-start.19
  77.4 4.6 %collective-permute-start.13 = (bf16[256,512]{1,0:T(8,128)(2,1)S(1)}, bf16[256,512]{1,0:T(8,128)(2,1)S(1)}, u32[]{:S(2)}, u32[]{:S(2)}) collective-permute-start(bf16[256,512]{1,0:T(8,128)(2,1)S(1)} %constant_dynamic-update-slice_fusion), channel_id=1, source_target_pairs={{0,1},{1,2},{2,3},{4,5},{5,6},{6,7},{8,9},{9,10},{10,11},{12,13},{... | collective-permute-start | bytes 786440 | tf_op jit(solution)/shard_map/ppermute | solution.py:431
  82.0 0.5 collective-permute-done.15
  82.4 1.5 %collective-permute-start.20 = (bf16[256,512]{1,0:T(8,128)(2,1)S(1)}, bf16[256,512]{1,0:T(8,128)(2,1)S(1)}, u32[]{:S(2)}, u32[]{:S(2)}) collective-permute-start(bf16[256,512]{1,0:T(8,128)(2,1)S(1)} %constant_dynamic-update-slice_fusion.2), channel_id=1, source_target_pairs={{1,0},{2,1},{3,2},{5,4},{6,5},{7,6},{9,8},{10,9},{11,10},{13,12},{... | collective-permute-start | bytes 786440 | tf_op jit(solution)/shard_map/ppermute | solution.py:431
  83.9 1.0 collective-permute-start.23
  85.0 4.5 %collective-permute-start.16 = (bf16[256,512]{1,0:T(8,128)(2,1)S(1)}, bf16[256,512]{1,0:T(8,128)(2,1)S(1)}, u32[]{:S(2)}, u32[]{:S(2)}) collective-permute-start(bf16[256,512]{1,0:T(8,128)(2,1)S(1)} %constant_dynamic-update-slice_fusion.2), channel_id=1, source_target_pairs={{0,1},{1,2},{2,3},{4,5},{5,6},{6,7},{8,9},{9,10},{10,11},{12,13},{... | collective-permute-start | bytes 786440 | tf_op jit(solution)/shard_map/ppermute | solution.py:431
  89.6 3.7 %collective-permute-done.20 = bf16[256,512]{1,0:T(8,128)(2,1)S(1)} collective-permute-done((bf16[256,512]{1,0:T(8,128)(2,1)S(1)}, bf16[256,512]{1,0:T(8,128)(2,1)S(1)}, u32[]{:S(2)}, u32[]{:S(2)}) %collective-permute-start.20) | collective-permute-done | bytes 262176 | tf_op jit(solution)/shard_map/ppermute | solution.py:431
  93.4 1.3 collective-permute-start.21
  94.7 0.6 collective-permute-done.16
  95.3 0.7 collective-permute-start.17
  96.0 1.1 collective-permute-start.27
  97.1 1.6 %collective-permute-done.23.one = bf16[256,1024]{1,0:T(8,128)(2,1)S(1)} collective-permute-done((bf16[256,1024]{1,0:T(8,128)(2,1)S(1)}, bf16[256,1024]{1,0:T(8,128)(2,1)S(1)}, u32[]{:S(2)}, u32[]{:S(2)}) %collective-permute-start.23) | collective-permute-done | bytes 524320 | tf_op jit(solution)/shard_map/ppermute | solution.py:428
  98.7 1.5 %collective-permute-start.24 = (bf16[256,1024]{1,0:T(8,128)(2,1)S(1)}, bf16[256,1024]{1,0:T(8,128)(2,1)S(1)}, u32[]{:S(2)}, u32[]{:S(2)}) collective-permute-start(bf16[256,1024]{1,0:T(8,128)(2,1)S(1)} %collective-permute-done.23.one), channel_id=1, source_target_pairs={{0,16},{16,0},{1,17},{17,1},{2,18},{18,2},{3,19},{19,3},{4,20},{20... | collective-permute-start | bytes 1572872 | tf_op jit(solution)/shard_map/ppermute | solution.py:485
  100.2 8.6 %collective-permute-done.21.above_2 = bf16[256,1024]{1,0:T(8,128)(2,1)S(1)} collective-permute-done((bf16[256,1024]{1,0:T(8,128)(2,1)S(1)}, bf16[256,1024]{1,0:T(8,128)(2,1)S(1)}, u32[]{:S(2)}, u32[]{:S(2)}) %collective-permute-start.21) | collective-permute-done | bytes 524320 | tf_op jit(solution)/shard_map/ppermute | solution.py:431
  108.9 0.8 collective-permute-done.27.one
  109.7 2.4 %collective-permute-done.24.other = bf16[256,1024]{1,0:T(8,128)(2,1)S(1)} collective-permute-done((bf16[256,1024]{1,0:T(8,128)(2,1)S(1)}, bf16[256,1024]{1,0:T(8,128)(2,1)S(1)}, u32[]{:S(2)}, u32[]{:S(2)}) %collective-permute-start.24) | collective-permute-done | bytes 524320 | tf_op jit(solution)/shard_map/ppermute | solution.py:485
  112.0 1.5 %collective-permute-start.28 = (bf16[256,1024]{1,0:T(8,128)(2,1)S(1)}, bf16[256,1024]{1,0:T(8,128)(2,1)S(1)}, u32[]{:S(2)}, u32[]{:S(2)}) collective-permute-start(bf16[256,1024]{1,0:T(8,128)(2,1)S(1)} %collective-permute-done.27.one), channel_id=1, source_target_pairs={{0,16},{16,0},{1,17},{17,1},{2,18},{18,2},{3,19},{19,3},{4,20},{20... | collective-permute-start | bytes 1572872 | tf_op jit(solution)/shard_map/ppermute | solution.py:485
  113.6 0.1 pad_maximum_fusion.own
  113.6 1.3 collective-permute-start.22
  114.9 0.7 collective-permute-start.18
  115.7 4.7 %shard_map.89 = (f32[256,1024]{1,0:T(8,128)S(1)}, bf16[256,1024]{1,0:T(8,128)(2,1)S(1)}, bf16[1024,1024]{1,0:T(8,128)(2,1)S(1)}) custom-call(s32[15]{0:T(128)S(1)} %stack.63.index_ref, bf16[256,1024]{1,0:T(8,128)(2,1)S(1)} %pad_maximum_fusion.own, bf16[256,1024]{1,0:T(8,128)(2,1)S(1)} %constant_dynamic-update-slice_fusion.4.below_1, ...), custom_call_target="tpu_custom_call" | custom-call | flops 1 | bytes 1 | tf_op jit(solution)/shard_map/pallas_call | solution.py:354
  120.4 6.0 %collective-permute-done.28.other = bf16[256,1024]{1,0:T(8,128)(2,1)S(1)} collective-permute-done((bf16[256,1024]{1,0:T(8,128)(2,1)S(1)}, bf16[256,1024]{1,0:T(8,128)(2,1)S(1)}, u32[]{:S(2)}, u32[]{:S(2)}) %collective-permute-start.28) | collective-permute-done | bytes 524320 | tf_op jit(solution)/shard_map/ppermute | solution.py:485
  126.4 0.5 collective-permute-start.30
  126.9 3.3 %collective-permute-done.22.above = bf16[256,1024]{1,0:T(8,128)(2,1)S(1)} collective-permute-done((bf16[256,1024]{1,0:T(8,128)(2,1)S(1)}, bf16[256,1024]{1,0:T(8,128)(2,1)S(1)}, u32[]{:S(2)}, u32[]{:S(2)}) %collective-permute-start.22) | collective-permute-done | bytes 524320 | tf_op jit(solution)/shard_map/ppermute | solution.py:431
  130.2 2.6 %shard_map.90 = bf16[256,1024]{1,0:T(8,128)(2,1)} custom-call(s32[15]{0:T(128)S(1)} %stack.63.index_ref, bf16[256,1024]{1,0:T(8,128)(2,1)S(1)} %collective-permute-done.18.below, bf16[256,1024]{1,0:T(8,128)(2,1)S(1)} %collective-permute-done.22.above, bf16[1024,1024]{1,0:T(8,128)(2,1)S(1)} %get-tuple-element.55.weight, ...), custom_call_target="tpu_custom_call" | custom-call | flops 1 | bytes 1 | tf_op jit(solution)/shard_map/pallas_call | solution.py:398
  (38 shorter events, 0.2 us)
Async XLA Ops:
  0.0 25.9 %copy-start = (bf16[4096,4]{0,1:T(4,128)(2,1)S(1)}, bf16[4096,4]{0,1:T(4,128)(2,1)}, u32[]{:S(2)}) copy-start(bf16[4096,4]{0,1:T(4,128)(2,1)} %param.10) | copy-start | bytes 98308
  5.6 9.0 %collective-permute-start.1 = (bf16[3,1024,512]{2,1,0:T(8,128)(2,1)}, bf16[3,1024,512]{2,1,0:T(8,128)(2,1)S(1)}, u32[]{:S(2)}, u32[]{:S(2)}) collective-permute-start(bf16[3,1024,512]{2,1,0:T(8,128)(2,1)} %dynamic-slice_bitcast_fusion), channel_id=1, source_target_pairs={{0,4},{4,0},{8,12},{12,8},{1,5},{5,1},{9,13},{13,9},{2,6},{6,2},{1... | collective-permute-start | bytes 9437192 | tf_op jit(solution)/shard_map/ppermute | solution.py:428
  6.1 8.5 %collective-permute-start = (bf16[256,4096]{1,0:T(8,128)(2,1)}, bf16[256,4096]{1,0:T(8,128)(2,1)}, u32[]{:S(2)}, u32[]{:S(2)}) collective-permute-start(bf16[256,4096]{1,0:T(8,128)(2,1)} %refs_0_.5), channel_id=1, source_target_pairs={{0,4},{4,0},{8,12},{12,8},{1,5},{5,1},{9,13},{13,9},{2,6},{6,2},{1... | collective-permute-start | bytes 6291464 | tf_op jit(solution)/shard_map/ppermute | solution.py:428
  6.1 15.4 %collective-permute-start.2 = (bf16[256,1024]{1,0:T(8,128)(2,1)}, bf16[256,1024]{1,0:T(8,128)(2,1)}, u32[]{:S(2)}, u32[]{:S(2)}) collective-permute-start(bf16[256,1024]{1,0:T(8,128)(2,1)} %constant_dynamic-slice_fusion.2), channel_id=1, source_target_pairs={{0,8},{4,12},{8,0},{12,4},{1,9},{5,13},{9,1},{13,5},{2,10},{6,14},... | collective-permute-start | bytes 1572872 | tf_op jit(solution)/shard_map/ppermute | solution.py:428
  14.6 2.8 %copy-start.1 = (bf16[1024,3,1024]{2,0,1:T(8,128)(2,1)S(1)}, bf16[1024,3,1024]{2,0,1:T(8,128)(2,1)}, u32[]{:S(2)}) copy-start(bf16[1024,3,1024]{2,0,1:T(8,128)(2,1)} %param.9) | copy-start | bytes 18874372
  21.5 17.0 %collective-permute-start.3 = (bf16[256,1024]{1,0:T(8,128)(2,1)}, bf16[256,1024]{1,0:T(8,128)(2,1)}, u32[]{:S(2)}, u32[]{:S(2)}) collective-permute-start(bf16[256,1024]{1,0:T(8,128)(2,1)} %collective-permute-done.2.refs_0_.refs_2_), channel_id=1, source_target_pairs={{0,1},{1,0},{2,3},{3,2},{4,5},{5,4},{6,7},{7,6},{8,9},{9,8},{10,11... | collective-permute-start | bytes 1572872 | tf_op jit(solution)/shard_map/ppermute | solution.py:431
  24.4 14.1 %collective-permute-start.4 = (bf16[2,512,256]{2,1,0:T(8,128)(2,1)}, bf16[2,512,256]{2,1,0:T(8,128)(2,1)}, u32[]{:S(2)}, u32[]{:S(2)}) collective-permute-start(bf16[2,512,256]{2,1,0:T(8,128)(2,1)} %shard_map.82), channel_id=1, source_target_pairs={{0,8},{4,12},{8,0},{12,4},{1,9},{5,13},{9,1},{13,5},{2,10},{6,14},... | collective-permute-start | bytes 1572872 | tf_op jit(solution)/shard_map/ppermute | solution.py:428
  28.2 1.2 collective-permute-start.5
  28.3 10.3 %collective-permute-start.7 = (bf16[256,1024]{1,0:T(8,128)(2,1)}, bf16[256,1024]{1,0:T(8,128)(2,1)S(1)}, u32[]{:S(2)}, u32[]{:S(2)}) collective-permute-start(bf16[256,1024]{1,0:T(8,128)(2,1)} %collective-permute-done.2.refs_0_.refs_2_), channel_id=1, source_target_pairs={{0,4},{4,0},{8,12},{12,8},{1,5},{5,1},{9,13},{13,9},{2,6},{6,2},{1... | collective-permute-start | bytes 1572872 | tf_op jit(solution)/shard_map/ppermute | solution.py:428
  29.4 9.1 %collective-permute-start.6 = (f32[8,256]{1,0:T(8,128)S(1)}, f32[8,256]{1,0:T(8,128)S(1)}, u32[]{:S(2)}, u32[]{:S(2)}) collective-permute-start(f32[8,256]{1,0:T(8,128)S(1)} %pad_maximum_fusion.1.rate_near_ref), channel_id=1, source_target_pairs={{0,8},{4,12},{8,0},{12,4},{1,9},{5,13},{9,1},{13,5},{2,10},{6,14},... | collective-permute-start | bytes 24584 | tf_op jit(solution)/shard_map/ppermute | solution.py:428
  31.2 2.8 %copy-start.2 = (bf16[1024,3,1024]{2,0,1:T(8,128)(2,1)S(1)}, bf16[1024,3,1024]{2,0,1:T(8,128)(2,1)}, u32[]{:S(2)}) copy-start(bf16[1024,3,1024]{2,0,1:T(8,128)(2,1)} %param.9) | copy-start | bytes 18874372
  38.5 5.2 %copy-start.3 = (bf16[1024,1024]{1,0:T(8,128)(2,1)S(1)}, bf16[1024,1024]{1,0:T(8,128)(2,1)}, u32[]{:S(2)}) copy-start(bf16[1024,1024]{1,0:T(8,128)(2,1)} %own_w.1) | copy-start | bytes 6291460
  38.5 2.2 %collective-permute-start.8 = (bf16[256,1024]{1,0:T(8,128)(2,1)}, bf16[256,1024]{1,0:T(8,128)(2,1)S(1)}, u32[]{:S(2)}, u32[]{:S(2)}) collective-permute-start(bf16[256,1024]{1,0:T(8,128)(2,1)} %collective-permute-done.3.refs_1_.refs_3_), channel_id=1, source_target_pairs={{0,4},{4,0},{8,12},{12,8},{1,5},{5,1},{9,13},{13,9},{2,6},{6,2},{1... | collective-permute-start | bytes 1572872 | tf_op jit(solution)/shard_map/ppermute | solution.py:428
  43.7 5.5 %collective-permute-start.9 = (bf16[1024,1024]{1,0:T(8,128)(2,1)S(1)}, bf16[1024,1024]{1,0:T(8,128)(2,1)S(1)}, u32[]{:S(2)}, u32[]{:S(2)}) collective-permute-start(bf16[1024,1024]{1,0:T(8,128)(2,1)S(1)} %copy-done.3), channel_id=1, source_target_pairs={{0,4},{4,0},{8,12},{12,8},{1,5},{5,1},{9,13},{13,9},{2,6},{6,2},{1... | collective-permute-start | bytes 6291464 | tf_op jit(solution)/shard_map/ppermute | solution.py:428
  43.9 14.2 %collective-permute-start.10 = (bf16[2,512,256]{2,1,0:T(8,128)(2,1)S(1)}, bf16[2,512,256]{2,1,0:T(8,128)(2,1)S(1)}, u32[]{:S(2)}, u32[]{:S(2)}) collective-permute-start(bf16[2,512,256]{2,1,0:T(8,128)(2,1)S(1)} %shard_map.84), channel_id=1, source_target_pairs={{0,8},{4,12},{8,0},{12,4},{1,9},{5,13},{9,1},{13,5},{2,10},{6,14},... | collective-permute-start | bytes 1572872 | tf_op jit(solution)/shard_map/ppermute | solution.py:428
  49.2 10.4 %copy-start.4 = (bf16[4,256,512]{2,1,0:T(8,128)(2,1)S(1)}, bf16[4,256,512]{2,1,0:T(8,128)(2,1)}, u32[]{:S(2)}) copy-start(bf16[4,256,512]{2,1,0:T(8,128)(2,1)} %gate_ref.1) | copy-start | bytes 3145732
  49.2 10.4 %copy-start.5 = (bf16[4,256,512]{2,1,0:T(8,128)(2,1)S(1)}, bf16[4,256,512]{2,1,0:T(8,128)(2,1)}, u32[]{:S(2)}) copy-start(bf16[4,256,512]{2,1,0:T(8,128)(2,1)} %up_ref.1) | copy-start | bytes 3145732
  49.2 10.4 %copy-start.6 = (bf16[4,256,512]{2,1,0:T(8,128)(2,1)S(1)}, bf16[4,256,512]{2,1,0:T(8,128)(2,1)}, u32[]{:S(2)}) copy-start(bf16[4,256,512]{2,1,0:T(8,128)(2,1)} %down_ref.1) | copy-start | bytes 3145732
  53.3 18.8 %copy-start.7 = (f32[1024]{0:T(1024)S(1)}, f32[1024]{0:T(1024)}, u32[]{:S(2)}) copy-start(f32[1024]{0:T(1024)} %param.14) | copy-start | bytes 12292
  58.1 13.9 %collective-permute-start.11 = (bf16[1,1024,256]{2,1,0:T(8,128)(2,1)S(1)}, bf16[1,1024,256]{2,1,0:T(8,128)(2,1)S(1)}, u32[]{:S(2)}, u32[]{:S(2)}) collective-permute-start(bf16[1,1024,256]{2,1,0:T(8,128)(2,1)S(1)} %shard_map.85), channel_id=1, source_target_pairs={{0,8},{4,12},{8,0},{12,4},{1,9},{5,13},{9,1},{13,5},{2,10},{6,14},... | collective-permute-start | bytes 1572872 | tf_op jit(solution)/shard_map/ppermute | solution.py:428
  74.1 2.0 %collective-permute-start.12 = (bf16[256,256]{1,0:T(8,128)(2,1)S(1)}, bf16[256,256]{1,0:T(8,128)(2,1)S(1)}, u32[]{:S(2)}, u32[]{:S(2)}) collective-permute-start(bf16[256,256]{1,0:T(8,128)(2,1)S(1)} %get-tuple-element.48), channel_id=1, source_target_pairs={{0,4},{4,0},{8,12},{12,8},{1,5},{5,1},{9,13},{13,9},{2,6},{6,2},{1... | collective-permute-start | bytes 393224 | tf_op jit(solution)/shard_map/ppermute | solution.py:428
  74.1 7.8 %collective-permute-start.14 = (bf16[256,256]{1,0:T(8,128)(2,1)S(1)}, bf16[256,256]{1,0:T(8,128)(2,1)S(1)}, u32[]{:S(2)}, u32[]{:S(2)}) collective-permute-start(bf16[256,256]{1,0:T(8,128)(2,1)S(1)} %get-tuple-element.49), channel_id=1, source_target_pairs={{0,8},{4,12},{8,0},{12,4},{1,9},{5,13},{9,1},{13,5},{2,10},{6,14},... | collective-permute-start | bytes 393224 | tf_op jit(solution)/shard_map/ppermute | solution.py:428
  75.2 7.2 %collective-permute-start.15 = (bf16[256,256]{1,0:T(8,128)(2,1)S(1)}, bf16[256,256]{1,0:T(8,128)(2,1)S(1)}, u32[]{:S(2)}, u32[]{:S(2)}) collective-permute-start(bf16[256,256]{1,0:T(8,128)(2,1)S(1)} %get-tuple-element.50), channel_id=1, source_target_pairs={{0,12},{4,8},{8,4},{12,0},{1,13},{5,9},{9,5},{13,1},{2,14},{6,10},... | collective-permute-start | bytes 393224 | tf_op jit(solution)/shard_map/ppermute | solution.py:428
  76.1 13.5 %collective-permute-start.19 = (bf16[256,512]{1,0:T(8,128)(2,1)S(1)}, bf16[256,512]{1,0:T(8,128)(2,1)S(1)}, u32[]{:S(2)}, u32[]{:S(2)}) collective-permute-start(bf16[256,512]{1,0:T(8,128)(2,1)S(1)} %constant_dynamic-update-slice_fusion), channel_id=1, source_target_pairs={{1,0},{2,1},{3,2},{5,4},{6,5},{7,6},{9,8},{10,9},{11,10},{13,12},{... | collective-permute-start | bytes 786440 | tf_op jit(solution)/shard_map/ppermute | solution.py:431
  77.4 12.2 %collective-permute-start.13 = (bf16[256,512]{1,0:T(8,128)(2,1)S(1)}, bf16[256,512]{1,0:T(8,128)(2,1)S(1)}, u32[]{:S(2)}, u32[]{:S(2)}) collective-permute-start(bf16[256,512]{1,0:T(8,128)(2,1)S(1)} %constant_dynamic-update-slice_fusion), channel_id=1, source_target_pairs={{0,1},{1,2},{2,3},{4,5},{5,6},{6,7},{8,9},{9,10},{10,11},{12,13},{... | collective-permute-start | bytes 786440 | tf_op jit(solution)/shard_map/ppermute | solution.py:431
  82.4 10.9 %collective-permute-start.20 = (bf16[256,512]{1,0:T(8,128)(2,1)S(1)}, bf16[256,512]{1,0:T(8,128)(2,1)S(1)}, u32[]{:S(2)}, u32[]{:S(2)}) collective-permute-start(bf16[256,512]{1,0:T(8,128)(2,1)S(1)} %constant_dynamic-update-slice_fusion.2), channel_id=1, source_target_pairs={{1,0},{2,1},{3,2},{5,4},{6,5},{7,6},{9,8},{10,9},{11,10},{13,12},{... | collective-permute-start | bytes 786440 | tf_op jit(solution)/shard_map/ppermute | solution.py:431
  83.9 14.8 %collective-permute-start.23 = (bf16[256,1024]{1,0:T(8,128)(2,1)S(1)}, bf16[256,1024]{1,0:T(8,128)(2,1)S(1)}, u32[]{:S(2)}, u32[]{:S(2)}) collective-permute-start(bf16[256,1024]{1,0:T(8,128)(2,1)S(1)} %get-tuple-element.51), channel_id=1, source_target_pairs={{0,8},{4,12},{8,0},{12,4},{1,9},{5,13},{9,1},{13,5},{2,10},{6,14},... | collective-permute-start | bytes 1572872 | tf_op jit(solution)/shard_map/ppermute | solution.py:428
  85.0 10.3 %collective-permute-start.16 = (bf16[256,512]{1,0:T(8,128)(2,1)S(1)}, bf16[256,512]{1,0:T(8,128)(2,1)S(1)}, u32[]{:S(2)}, u32[]{:S(2)}) collective-permute-start(bf16[256,512]{1,0:T(8,128)(2,1)S(1)} %constant_dynamic-update-slice_fusion.2), channel_id=1, source_target_pairs={{0,1},{1,2},{2,3},{4,5},{5,6},{6,7},{8,9},{9,10},{10,11},{12,13},{... | collective-permute-start | bytes 786440 | tf_op jit(solution)/shard_map/ppermute | solution.py:431
  93.4 15.5 %collective-permute-start.21 = (bf16[256,1024]{1,0:T(8,128)(2,1)S(1)}, bf16[256,1024]{1,0:T(8,128)(2,1)S(1)}, u32[]{:S(2)}, u32[]{:S(2)}) collective-permute-start(bf16[256,1024]{1,0:T(8,128)(2,1)S(1)} %constant_dynamic-update-slice_fusion.6.above_1), channel_id=1, source_target_pairs={{1,0},{2,1},{5,4},{6,5},{9,8},{10,9},{13,12},{14,13},{17,16},{18,1... | collective-permute-start | bytes 1572872 | tf_op jit(solution)/shard_map/ppermute | solution.py:431
  95.3 13.6 %collective-permute-start.17 = (bf16[256,1024]{1,0:T(8,128)(2,1)S(1)}, bf16[256,1024]{1,0:T(8,128)(2,1)S(1)}, u32[]{:S(2)}, u32[]{:S(2)}) collective-permute-start(bf16[256,1024]{1,0:T(8,128)(2,1)S(1)} %constant_dynamic-update-slice_fusion.4.below_1), channel_id=1, source_target_pairs={{1,2},{2,3},{5,6},{6,7},{9,10},{10,11},{13,14},{14,15},{17,18},{18... | collective-permute-start | bytes 1572872 | tf_op jit(solution)/shard_map/ppermute | solution.py:431
  96.0 13.7 %collective-permute-start.27 = (bf16[256,1024]{1,0:T(8,128)(2,1)S(1)}, bf16[256,1024]{1,0:T(8,128)(2,1)S(1)}, u32[]{:S(2)}, u32[]{:S(2)}) collective-permute-start(bf16[256,1024]{1,0:T(8,128)(2,1)S(1)} %get-tuple-element.57), channel_id=1, source_target_pairs={{0,8},{4,12},{8,0},{12,4},{1,9},{5,13},{9,1},{13,5},{2,10},{6,14},... | collective-permute-start | bytes 1572872 | tf_op jit(solution)/shard_map/ppermute | solution.py:428
  98.7 13.3 %collective-permute-start.24 = (bf16[256,1024]{1,0:T(8,128)(2,1)S(1)}, bf16[256,1024]{1,0:T(8,128)(2,1)S(1)}, u32[]{:S(2)}, u32[]{:S(2)}) collective-permute-start(bf16[256,1024]{1,0:T(8,128)(2,1)S(1)} %collective-permute-done.23.one), channel_id=1, source_target_pairs={{0,16},{16,0},{1,17},{17,1},{2,18},{18,2},{3,19},{19,3},{4,20},{20... | collective-permute-start | bytes 1572872 | tf_op jit(solution)/shard_map/ppermute | solution.py:485
  109.6 6.0 %collective-permute-start.25 = (bf16[256,1024]{1,0:T(8,128)(2,1)S(1)}, bf16[256,1024]{1,0:T(8,128)(2,1)S(1)}, u32[]{:S(2)}, u32[]{:S(2)}) collective-permute-start(bf16[256,1024]{1,0:T(8,128)(2,1)S(1)} %collective-permute-done.23.one), channel_id=1, source_target_pairs={{0,4},{4,0},{8,12},{12,8},{1,5},{5,1},{9,13},{13,9},{2,6},{6,2},{1... | collective-permute-start | bytes 1572872 | tf_op jit(solution)/shard_map/ppermute | solution.py:428
  112.0 3.6 %collective-permute-start.26 = (bf16[256,1024]{1,0:T(8,128)(2,1)S(1)}, bf16[256,1024]{1,0:T(8,128)(2,1)S(1)}, u32[]{:S(2)}, u32[]{:S(2)}) collective-permute-start(bf16[256,1024]{1,0:T(8,128)(2,1)S(1)} %collective-permute-done.24.other), channel_id=1, source_target_pairs={{0,4},{4,0},{8,12},{12,8},{1,5},{5,1},{9,13},{13,9},{2,6},{6,2},{1... | collective-permute-start | bytes 1572872 | tf_op jit(solution)/shard_map/ppermute | solution.py:428
  112.0 14.3 %collective-permute-start.28 = (bf16[256,1024]{1,0:T(8,128)(2,1)S(1)}, bf16[256,1024]{1,0:T(8,128)(2,1)S(1)}, u32[]{:S(2)}, u32[]{:S(2)}) collective-permute-start(bf16[256,1024]{1,0:T(8,128)(2,1)S(1)} %collective-permute-done.27.one), channel_id=1, source_target_pairs={{0,16},{16,0},{1,17},{17,1},{2,18},{18,2},{3,19},{19,3},{4,20},{20... | collective-permute-start | bytes 1572872 | tf_op jit(solution)/shard_map/ppermute | solution.py:485
  113.6 16.5 %collective-permute-start.22 = (bf16[256,1024]{1,0:T(8,128)(2,1)S(1)}, bf16[256,1024]{1,0:T(8,128)(2,1)S(1)}, u32[]{:S(2)}, u32[]{:S(2)}) collective-permute-start(bf16[256,1024]{1,0:T(8,128)(2,1)S(1)} %collective-permute-done.21.above_2), channel_id=1, source_target_pairs={{1,0},{5,4},{9,8},{13,12},{17,16},{21,20},{25,24},{29,28}} | collective-permute-start | bytes 1572872 | tf_op jit(solution)/shard_map/ppermute | solution.py:431
  114.9 15.3 %collective-permute-start.18 = (bf16[256,1024]{1,0:T(8,128)(2,1)S(1)}, bf16[256,1024]{1,0:T(8,128)(2,1)S(1)}, u32[]{:S(2)}, u32[]{:S(2)}) collective-permute-start(bf16[256,1024]{1,0:T(8,128)(2,1)S(1)} %collective-permute-done.17.below_2), channel_id=1, source_target_pairs={{2,3},{6,7},{10,11},{14,15},{18,19},{22,23},{26,27},{30,31}} | collective-permute-start | bytes 1572872 | tf_op jit(solution)/shard_map/ppermute | solution.py:431
  126.4 3.8 %collective-permute-start.29 = (bf16[256,1024]{1,0:T(8,128)(2,1)S(1)}, bf16[256,1024]{1,0:T(8,128)(2,1)S(1)}, u32[]{:S(2)}, u32[]{:S(2)}) collective-permute-start(bf16[256,1024]{1,0:T(8,128)(2,1)S(1)} %collective-permute-done.27.one), channel_id=1, source_target_pairs={{0,4},{4,0},{8,12},{12,8},{1,5},{5,1},{9,13},{13,9},{2,6},{6,2},{1... | collective-permute-start | bytes 1572872 | tf_op jit(solution)/shard_map/ppermute | solution.py:428
  126.4 3.8 %collective-permute-start.30 = (bf16[256,1024]{1,0:T(8,128)(2,1)S(1)}, bf16[256,1024]{1,0:T(8,128)(2,1)S(1)}, u32[]{:S(2)}, u32[]{:S(2)}) collective-permute-start(bf16[256,1024]{1,0:T(8,128)(2,1)S(1)} %collective-permute-done.28.other), channel_id=1, source_target_pairs={{0,4},{4,0},{8,12},{12,8},{1,5},{5,1},{9,13},{13,9},{2,6},{6,2},{1... | collective-permute-start | bytes 1572872 | tf_op jit(solution)/shard_map/ppermute | solution.py:428
